TPU v7x, 32 devices: a whole 2x2x4 slice. The times are simulated.
32 devices in a mesh: copy: 16 (over z, y, core), tok: 2 (over x).
Axes of the slice: x: 2, y: 2, z: 4, core: 2. Of those that a mesh axis runs over, the one named last changes fastest.
Arguments:
- noisy: bfloat16 [16, 256, 768], P('copy', 'tok'), may hold values from -6 to 6
- single: bfloat16 [256, 768], P('tok'), may hold values from -6 to 6
- pair: bfloat16 [256, 256, 128], P('tok', 'copy'), may hold values from -6 to 6
- restype: int32 [256], P('tok'), may hold values from 0 to 31
- chain: int32 [256], replicated, may hold values from 0 to 5, never falling along the last dimension, each value on 1 to 128 neighbouring positions
- keymask: int32 [256], replicated, may hold values from 0 to 1, as said below
- restype_table: bfloat16 [32, 768], replicated, may hold values from -3 to 3
- norm_gain: float32 [768], replicated, may hold values from 0.25 to 1.75
- pair_gain: float32 [128], replicated, may hold values from 0.25 to 1.75
- trans_gain: float32 [768], replicated, may hold values from 0.25 to 1.75
- w_query: bfloat16 [768, 768], replicated, may hold values from -0.21875 to 0.21875
- w_key: bfloat16 [768, 768], replicated, may hold values from -0.21875 to 0.21875
- w_value: bfloat16 [768, 768], replicated, may hold values from -0.21875 to 0.21875
- w_out: bfloat16 [768, 768], replicated, may hold values from -0.21875 to 0.21875
- w_pair: bfloat16 [128, 8], replicated, may hold values from -0.5 to 0.5
- chain_weight: float32 [6, 8], replicated, may hold values from -80 to 240
- w_hidden_gate: bfloat16 [768, 1536], replicated, may hold values from -0.21875 to 0.21875
- w_hidden_up: bfloat16 [768, 1536], replicated, may hold values from -0.21875 to 0.21875
- w_down: bfloat16 [1536, 768], replicated, may hold values from -0.15625 to 0.15625
- cotangent: bfloat16 [16, 256, 768], P('copy', 'tok'), may hold values from -6 to 6
Outputs:
- grad_noisy: bfloat16 [16, 256, 768], P('copy', 'tok')
- grad_single: float32 [256, 768], P('tok', 'copy')
- grad_pair: bfloat16 [256, 256, 128], P('tok', 'copy')
- grad_query: float32 [768, 768], P('tok', 'copy')
- grad_key: float32 [768, 768], P('tok', 'copy')
- grad_value: float32 [768, 768], P('tok', 'copy')
- grad_out: float32 [768, 768], P('tok', 'copy')
- grad_pair_weight: float32 [128, 8], replicated
Inputs may be any that keep to these rules, and one draw needn't show every extreme that they name: `keymask`: 1 on the first positions of the crop and 0 after them, with at least 128 ones. chain numbers never fall along the crop.
All inputs are finite; a program needn't handle non-finite values.
Results may differ from a plain program's by a relative error of at most 0.03.
Values may be sent and summed in bfloat16 or wider, within the bound.
No kernel may reach another device: no remote copies, remote signals or barrier semaphores. Data moves between devices by JAX's collectives and lax.ppermute only.
A program may use at most 128 MiB of HBM per device.

v0:
```python
import jax
import jax.numpy as jnp
from jax import lax
from jax.sharding import PartitionSpec as P

epsilon = 1e-05
highest_precision = lax.Precision.HIGHEST


def layer_forward(values, scales):
    average = jnp.mean(values, axis=-1, keepdims=True)
    centred = values - average
    inverse = lax.rsqrt(jnp.mean(centred * centred, axis=-1, keepdims=True) + epsilon)
    normed = centred * inverse
    return (normed * scales, normed, inverse)


def layer_backward(upstream, scales, normed, inverse):
    scaled = upstream * scales
    first_moment = jnp.mean(scaled, axis=-1, keepdims=True)
    second_moment = jnp.mean(scaled * normed, axis=-1, keepdims=True)
    return inverse * (scaled - first_moment - normed * second_moment)


def matmul(left, right):
    return jnp.dot(left, right, preferred_element_type=jnp.float32)


def per_device(
    noisy,
    single,
    pair,
    restype,
    chain,
    keymask,
    restype_table,
    norm_gain,
    pair_gain,
    trans_gain,
    w_query,
    w_key,
    w_value,
    w_out,
    w_pair,
    chain_weight,
    w_hidden_gate,
    w_hidden_up,
    w_down,
    cotangent,
):
    copy_count, tok_rows, model_width = noisy.shape
    head_count = w_pair.shape[1]
    head_width = model_width // head_count
    key_count = chain.shape[0]
    scale = head_width ** (-0.5)
    first_row = lax.axis_index("tok") * tok_rows
    flat_count = copy_count * tok_rows
    res_onehot = (
        restype[:, None] == jnp.arange(restype_table.shape[0], dtype=jnp.int32)[None, :]
    ).astype(jnp.bfloat16)
    condition = single.astype(jnp.float32) + matmul(res_onehot, restype_table)
    noisy_f = noisy.astype(jnp.float32)
    normed_scaled, noisy_hat, noisy_inverse = layer_forward(noisy_f, norm_gain)
    inputs_x = (normed_scaled + condition[None]).astype(jnp.bfloat16)
    flat_x = inputs_x.reshape(flat_count, model_width)
    query = matmul(flat_x, w_query).astype(jnp.bfloat16).reshape(copy_count, tok_rows, model_width)
    key_local = (
        matmul(flat_x, w_key).astype(jnp.bfloat16).reshape(copy_count, tok_rows, model_width)
    )
    value_local = (
        matmul(flat_x, w_value).astype(jnp.bfloat16).reshape(copy_count, tok_rows, model_width)
    )
    key_full, value_full = (
        lax.all_gather(key_local, "tok", axis=1, tiled=True),
        lax.all_gather(value_local, "tok", axis=1, tiled=True),
    )
    pair_scaled, pair_hat, pair_inverse = layer_forward(pair.astype(jnp.float32), pair_gain)
    pair_rounded = pair_scaled.astype(jnp.bfloat16)
    bias_local = jnp.einsum(
        "ijc,ch->hij", pair_rounded, w_pair, preferred_element_type=jnp.float32
    ).astype(jnp.bfloat16)
    bias_rows = lax.all_gather(bias_local, "copy", axis=2, tiled=True)
    chain_rows = lax.dynamic_slice_in_dim(chain, first_row, tok_rows)
    chain_onehot = (
        chain[:, None] == jnp.arange(chain_weight.shape[0], dtype=jnp.int32)[None, :]
    ).astype(jnp.float32)
    key_weight = jnp.dot(chain_onehot, chain_weight, precision=highest_precision)
    same_chain = (chain_rows[:, None] == chain[None, :]).astype(jnp.float32)
    extra = bias_rows.astype(jnp.float32) + same_chain[None, :, :] * key_weight.T[:, None, :]
    valid = (keymask > 0)[None, None, None, :]
    query_heads = query.reshape(copy_count, tok_rows, head_count, head_width)
    key_heads = key_full.reshape(copy_count, key_count, head_count, head_width)
    value_heads = value_full.reshape(copy_count, key_count, head_count, head_width)
    logits = (
        jnp.einsum("cihd,cjhd->chij", query_heads, key_heads, preferred_element_type=jnp.float32)
        * scale
        + extra[None]
    )
    logits = jnp.where(valid, logits, -1e30)
    highest = jnp.max(logits, axis=-1, keepdims=True)
    exponent = jnp.exp(logits - highest)
    total_mass = jnp.sum(exponent, axis=-1, keepdims=True)
    weights = exponent / total_mass
    weights_b = weights.astype(jnp.bfloat16)
    attended = jnp.einsum(
        "chij,cjhd->cihd", weights_b, value_heads, preferred_element_type=jnp.float32
    ).astype(jnp.bfloat16)
    flat_att = attended.reshape(flat_count, model_width)
    residual = noisy_f.reshape(flat_count, model_width) + matmul(flat_att, w_out)
    trans_scaled, trans_hat, trans_inverse = layer_forward(residual, trans_gain)
    trans_in = trans_scaled.astype(jnp.bfloat16)
    gate = matmul(trans_in, w_hidden_gate)
    up_part = matmul(trans_in, w_hidden_up)
    sigmoid_gate = jax.nn.sigmoid(gate)
    upstream = cotangent.reshape(flat_count, model_width)
    d_hidden = matmul(upstream, w_down.T)
    d_gate = (d_hidden * up_part * sigmoid_gate * (1.0 + gate * (1.0 - sigmoid_gate))).astype(
        jnp.bfloat16
    )
    d_up = (d_hidden * gate * sigmoid_gate).astype(jnp.bfloat16)
    d_trans = matmul(d_gate, w_hidden_gate.T) + matmul(d_up, w_hidden_up.T)
    d_res = upstream.astype(jnp.float32) + layer_backward(
        d_trans, trans_gain, trans_hat, trans_inverse
    )
    d_res_b = d_res.astype(jnp.bfloat16)
    out_term = jnp.einsum("rd,re->de", flat_att, d_res_b, preferred_element_type=jnp.float32)
    d_att = matmul(d_res_b, w_out.T).astype(jnp.bfloat16).reshape(copy_count, tok_rows, model_width)
    d_att_heads = d_att.reshape(copy_count, tok_rows, head_count, head_width)
    d_weights = jnp.einsum(
        "cihd,cjhd->chij", d_att_heads, value_heads, preferred_element_type=jnp.float32
    )
    delta = jnp.sum(weights * d_weights, axis=-1, keepdims=True)
    d_logits = weights * (d_weights - delta)
    d_logits_b = d_logits.astype(jnp.bfloat16)
    d_query = (
        (
            jnp.einsum("chij,cjhd->cihd", d_logits_b, key_heads, preferred_element_type=jnp.float32)
            * scale
        )
        .astype(jnp.bfloat16)
        .reshape(flat_count, model_width)
    )
    bias_grad_rows = jnp.sum(d_logits, axis=0)
    count = tok_rows * lax.axis_size("tok")
    key_part = (
        jnp.einsum("chij,cihd->jchd", d_logits_b, query_heads, preferred_element_type=jnp.float32)
        * scale
    )
    value_part = jnp.einsum(
        "chij,cihd->jchd", weights_b, d_att_heads, preferred_element_type=jnp.float32
    )
    key_sums = lax.psum_scatter(
        jnp.concatenate(
            [
                key_part.reshape(count, copy_count, model_width),
                value_part.reshape(count, copy_count, model_width),
            ],
            axis=2,
        ).astype(jnp.bfloat16),
        "tok",
        scatter_dimension=0,
        tiled=True,
    ).astype(jnp.float32)
    d_key = (
        jnp.transpose(key_sums[:, :, :model_width], (1, 0, 2))
        .astype(jnp.bfloat16)
        .reshape(flat_count, model_width)
    )
    d_value = (
        jnp.transpose(key_sums[:, :, model_width:], (1, 0, 2))
        .astype(jnp.bfloat16)
        .reshape(flat_count, model_width)
    )
    d_inputs = matmul(d_query, w_query.T) + matmul(d_key, w_key.T) + matmul(d_value, w_value.T)
    grad_noisy = (
        (
            d_res
            + layer_backward(
                d_inputs,
                norm_gain,
                noisy_hat.reshape(flat_count, model_width),
                noisy_inverse.reshape(flat_count, 1),
            )
        )
        .astype(jnp.bfloat16)
        .reshape(copy_count, tok_rows, model_width)
    )
    grad_single = lax.psum_scatter(
        jnp.sum(d_inputs.reshape(copy_count, tok_rows, model_width), axis=0).astype(jnp.bfloat16),
        "copy",
        scatter_dimension=1,
        tiled=True,
    ).astype(jnp.float32)
    bias_grad = lax.psum_scatter(
        bias_grad_rows.astype(jnp.bfloat16), "copy", scatter_dimension=2, tiled=True
    ).astype(jnp.float32)
    d_pair_scaled = jnp.einsum(
        "hij,ch->ijc", bias_grad, w_pair.astype(jnp.float32), precision=highest_precision
    )
    grad_pair = layer_backward(d_pair_scaled, pair_gain, pair_hat, pair_inverse).astype(
        jnp.bfloat16
    )
    pair_weight_term = jnp.einsum(
        "ijc,hij->ch", pair_rounded.astype(jnp.float32), bias_grad, precision=highest_precision
    )
    grad_pair_weight = lax.psum(pair_weight_term, ("copy", "tok"))
    stacked = jnp.stack(
        [
            jnp.einsum("rd,re->de", flat_x, d_query, preferred_element_type=jnp.float32),
            jnp.einsum("rd,re->de", flat_x, d_key, preferred_element_type=jnp.float32),
            jnp.einsum("rd,re->de", flat_x, d_value, preferred_element_type=jnp.float32),
            out_term,
        ]
    )
    partial_sum = lax.psum_scatter(
        stacked.astype(jnp.bfloat16), "copy", scatter_dimension=2, tiled=True
    )
    reduced = lax.psum_scatter(partial_sum, "tok", scatter_dimension=1, tiled=True).astype(
        jnp.float32
    )
    return (
        grad_noisy,
        grad_single,
        grad_pair,
        reduced[0],
        reduced[1],
        reduced[2],
        reduced[3],
        grad_pair_weight,
    )


def solution(mesh):
    placed = (
        P("copy", "tok", None),
        P("tok", None),
        P("tok", "copy", None),
        P("tok"),
        P(),
        P(),
        P(),
        P(),
        P(),
        P(),
        P(),
        P(),
        P(),
        P(),
        P(),
        P(),
        P(),
        P(),
        P(),
        P("copy", "tok", None),
    )
    return jax.shard_map(
        per_device,
        mesh=mesh,
        in_specs=placed,
        out_specs=(
            P("copy", "tok", None),
            P("tok", "copy"),
            P("tok", "copy", None),
            P("tok", "copy"),
            P("tok", "copy"),
            P("tok", "copy"),
            P("tok", "copy"),
            P(),
        ),
        check_vma=False,
    )
```

profile of v0, /device:TPU:2, one launch (start us, length us, event | category | flops | bytes accessed | tf_op | source)
XLA Modules:
  0.0 381.6 jit_solution(12268986313362583396)
XLA Ops:
  7.2 0.8 broadcast_compare_fusion
  8.1 1.0 convert_reduce_fusion.1
  9.1 1.1 fusion.46
  10.3 0.8 dynamic_slice.3
  11.0 0.9 convolution_bitcast_fusion
  11.9 1.5 compare_convert_fusion
  13.4 1.3 fusion.24
  14.7 1.6 convolution_convert_fusion.6
  16.3 7.3 %all-gather.1 = bf16[256,768]{1,0:T(8,128)(2,1)S(1)} all-gather(bf16[128,768]{1,0:T(8,128)(2,1)S(1)} %convolution_convert_fusion.6), channel_id=3, replica_groups=mesh['copy'=16,'tok'=2] {'tok'}, dimensions={0}, use_global_device_ids=true | all-gather | bytes 589824 | tf_op jit(solution)/shard_map/all_gather | solution.py:74
  23.8 1.7 convolution_convert_fusion.7
  25.6 0.8 copy.77
  26.4 1.6 convolution_convert_fusion.8
  28.0 6.4 %all-gather = bf16[256,768]{1,0:T(8,128)(2,1)S(1)} all-gather(bf16[128,768]{1,0:T(8,128)(2,1)S(1)} %convolution_convert_fusion.8), channel_id=2, replica_groups=mesh['copy'=16,'tok'=2] {'tok'}, dimensions={0}, use_global_device_ids=true | all-gather | bytes 589824 | tf_op jit(solution)/shard_map/all_gather | solution.py:75
  34.4 0.9 copy.76
  35.4 1.5 copy.79
  37.4 24.5 %all_gather.11 = bf16[8,128,256]{1,0,2:T(8,128)(2,1)} all-gather(bf16[8,128,16]{1,0,2:T(8,128)(2,1)S(1)} %fusion.25), channel_id=1, replica_groups=mesh['copy'=16,'tok'=2] {'copy'}, dimensions={2}, use_global_device_ids=true | all-gather | bytes 557056 | tf_op jit(solution)/shard_map/all_gather | solution.py:82
  61.9 2.1 copy.81
  64.0 1.5 fusion.11
  65.5 1.0 copy-done.8
  66.6 1.2 fusion.75
  67.8 4.3 %convolution_convert_fusion.9 = bf16[8,96,128]{2,1,0:T(8,128)(2,1)} fusion(bf16[256,8,96]{0,2,1:T(8,128)(2,1)S(1)} %bitcast.173, f32[8,128]{1,0:T(8,128)S(1)} %get-tuple-element.52, f32[8,128,256]{2,1,0:T(8,128)} %copy-done.8), kind=kOutput, calls=%fused_computation.46 | convolution fusion | flops 51217664 | bytes 1642496 | tf_op jit(solution)/shard_map/chij,cjhd->cihd/dot_general | solution.py:105
  72.0 1.9 fusion.76
  74.2 2.7 fusion.54
  77.0 1.4 fusion.70
  78.4 4.2 %fusion.20 = f32[128,768]{1,0:T(8,128)} fusion(bf16[768,1536]{1,0:T(8,128)(2,1)S(1)} %copy-done, f32[128,1536]{1,0:T(8,128)} %fusion.54, bf16[768,1536]{1,0:T(8,128)(2,1)} %param.37, f32[128,1536]{1,0:T(8,128)} %fusion.70, f32[128,768]{1,0:T(8,128)S(1)} %get-tuple-element.55, f32[768]{0:T(1024)S(1)} %copy-done.20, f32[128]{0:T(128)S(1)} %add_rsqrt_fusion.1, ...), kind=kOutput, calls=%fused_computation.37 | convolution fusion | flops 606339072 | bytes 7081984 | tf_op jit(solution)/shard_map/dot_general | solution.py:26
  82.5 3.2 fusion.72
  85.9 1.0 copy-done.4
  87.0 0.5 convolution_convert_fusion.5
  87.7 3.6 convolution_convert_fusion.4
  91.3 0.5 multiply_reduce_fusion
  92.2 0.6 copy-done.13
  93.0 1.2 copy.96
  94.3 1.1 copy.83
  96.4 1.5 fusion.5
  97.9 10.0 %reduce-scatter.13.cloned.1.call-done = bf16[128,1536]{1,0:T(8,128)(2,1)} async-done(((bf16[256,1536]{1,0:T(8,128)(2,1)}), bf16[128,1536]{1,0:T(8,128)(2,1)}) %reduce-scatter.13.cloned.1.call-update) | async-done | bytes 393232
  108.0 1.2 copy.97
  109.2 0.5 fusion.6
  110.2 0.8 copy-done.3
  111.0 2.5 pad_maximum_fusion
  113.4 8.5 %copy.84 = bf16[4,768,768]{1,0,2:T(4,128)(2,1)} copy(bf16[4,768,768]{2,1,0:T(8,128)(2,1)} %pad_maximum_fusion) | data formatting | bytes 9437184 | tf_op jit(solution)/shard_map/stack | solution.py:207
  122.0 0.6 copy-done.24
  122.6 0.6 dynamic-slice
  123.8 0.5 fusion.77
  124.4 45.1 %reduce-scatter.11.cloned.1.call-done = bf16[8,128,16]{1,0,2:T(8,128)(2,1)} async-done(((bf16[8,128,256]{1,0,2:T(8,128)(2,1)}), bf16[8,128,16]{1,0,2:T(8,128)(2,1)}) %reduce-scatter.11.cloned.1.call-update) | async-done | bytes 32784 | tf_op jit(solution)/shard_map/reduce_scatter | solution.py:194
  169.5 2.2 fusion.71
  171.6 0.5 convolution_add_fusion.1
  173.0 0.6 multiply_reduce_fusion.3
  173.7 0.9 fusion.73
  174.6 0.8 copy.92
  175.4 113.8 %all-reduce.3.cloned.1.call-done = bf16[4,768,768]{1,0,2:T(4,128)(2,1)} async-done(((bf16[4,768,768]{1,0,2:T(4,128)(2,1)}), bf16[4,768,768]{1,0,2:T(4,128)(2,1)}) %all-reduce.3.cloned.1.call-update) | async-done | bytes 4718608
  289.2 1.1 constant_dynamic-slice_fusion
  290.3 10.1 %copy.94 = bf16[4,768,48]{0,2,1:T(8,128)(2,1)} copy(bf16[4,768,48]{1,0,2:T(4,128)(2,1)S(1)} %constant_dynamic-slice_fusion) | data formatting | bytes 589824
  300.4 11.8 %reshape.316 = bf16[768,192]{1,0:T(8,128)(2,1)} reshape(bf16[768,48,4]{2,1,0:T(8,128)(2,1)} %bitcast.157) | data formatting | bytes 589824
  312.5 1.2 copy.87
  314.1 40.6 %psum.7 = f32[128,8]{0,1:T(8,128)} all-reduce(f32[128,8]{0,1:T(8,128)S(1)} %convolution_bitcast_fusion.1), channel_id=1, replica_groups=mesh['copy'=16,'tok'=2] {'copy','tok'}, use_global_device_ids=true, to_apply=%region_20.21 | all-reduce | flops 1024 | bytes 8192 | tf_op jit(solution)/shard_map/psum | solution.py:206
  354.7 0.8 copy.93
  355.5 0.7 copy.86
  356.2 3.0 reduce-scatter.17.cloned.1.call-done
  359.2 7.1 %reshape.317 = bf16[384,48,4]{2,1,0:T(8,128)(2,1)} reshape(bf16[384,192]{1,0:T(8,128)(2,1)} %reduce-scatter.17.cloned.1.call-done) | data formatting | bytes 294912
  366.3 6.0 %copy.95 = bf16[4,384,48]{1,0,2:T(4,128)(2,1)S(1)} copy(bf16[4,384,48]{0,2,1:T(8,128)(2,1)} %bitcast.158) | data formatting | bytes 294912
  372.5 0.6 copy.106
  373.1 0.6 copy.107
  373.8 0.6 copy.108
  374.4 0.6 copy.109
  (83 shorter events, 5.4 us)
Async XLA Ops:
  7.2 69.8 %copy-start = (bf16[768,1536]{1,0:T(8,128)(2,1)S(1)}, bf16[768,1536]{1,0:T(8,128)(2,1)}, u32[]{:S(2)}) copy-start(bf16[768,1536]{1,0:T(8,128)(2,1)} %param.36) | copy-start | bytes 7077892
  7.2 100.8 %reduce-scatter.13.cloned.1.call-start = ((), (), s32[]{:S(2)}) async-start(), calls=%async_computation.5 | async-start | bytes 1179648
  23.8 40.2 %copy-start.10 = (bf16[256,768]{0,1:T(8,128)(2,1)}, bf16[256,768]{0,1:T(8,128)(2,1)S(1)}, u32[]{:S(2)}) copy-start(bf16[256,768]{0,1:T(8,128)(2,1)S(1)} %copy.78) | copy-start | bytes 1179652
  35.4 1.8 copy-start.22
  35.4 1.8 copy-start.23
  65.5 1.0 copy-start.8
  66.6 1.2 copy-start.17
  72.0 2.2 copy-start.12
  74.2 2.7 copy-start.20
  82.5 3.2 copy-start.16
  85.7 1.3 copy-start.4
  87.7 3.6 copy-start.9
  87.7 3.6 copy-start.18
  91.8 0.9 copy-start.13
  94.2 1.4 copy-start.11
  94.3 1.7 copy-start.15
  94.3 75.2 %reduce-scatter.11.cloned.1.call-start = ((), (), s32[]{:S(2)}) async-start(), calls=%async_computation.4 | async-start | bytes 557056 | tf_op jit(solution)/shard_map/reduce_scatter | solution.py:194
  95.4 193.8 %all-reduce.3.cloned.1.call-start = ((), (), s32[]{:S(2)}) async-start(), calls=%async_computation.8 | async-start | bytes 9437184
  109.7 1.3 copy-start.3
  121.9 0.7 copy-start.24
  121.9 1.9 copy-start.5
  122.0 232.7 %reduce-scatter.15.cloned.1.call-start = ((), (), s32[]{:S(2)}) async-start(), calls=%async_computation.6 | async-start | bytes 208896
  124.4 47.3 %copy-start.6 = (bf16[768,768]{1,0:T(8,128)(2,1)S(1)}, bf16[768,768]{1,0:T(8,128)(2,1)}, u32[]{:S(2)}) copy-start(bf16[768,768]{1,0:T(8,128)(2,1)} %param.31) | copy-start | bytes 3538948
  171.6 0.9 copy-start.2
  171.6 1.4 copy-start.7
  171.6 1.4 copy-start.19
  175.4 183.8 %reduce-scatter.17.cloned.1.call-start = ((), (), s32[]{:S(2)}) async-start(), calls=%async_computation.7 | async-start | bytes 589824
  300.4 11.8 %copy-start.14 = (f32[128,16,128]{0,2,1:T(8,128)S(1)}, f32[128,16,128]{0,2,1:T(8,128)}, u32[]{:S(2)}) copy-start(f32[128,16,128]{0,2,1:T(8,128)} %get-tuple-element.60) | copy-start | bytes 3145732
  312.2 1.5 copy-start.21
  366.3 8.8 %copy-start.1 = (bf16[768,1536]{1,0:T(8,128)(2,1)S(1)}, bf16[768,1536]{1,0:T(8,128)(2,1)}, u32[]{:S(2)}) copy-start(bf16[768,1536]{1,0:T(8,128)(2,1)} %param.36) | copy-start | bytes 7077892
Sparse Core Ops, SparseCore 0:
  94.4 13.5 reduce-scatter.12
  112.5 56.9 reduce-scatter.10
  173.1 116.0 all-reduce.2
  292.6 53.3 reduce-scatter.14
  348.1 11.0 reduce-scatter.16
where the time goes:
time: 385 us; the launch traced here: 382 us
  waiting for transfers between devices  172 us (45%)
  blocking collectives  78.9 us (20%)
  local copies, waits for them, and re-layouts  66.2 us (17%)
  matrix products  38.9 us (10%)
  between operations  14.9 us (4%)
  other arithmetic  10.4 us (3%)
    unnamed x9, waiting for transfers between devices  127 us
    unnamed x67, local copies, waits for them, and re-layouts  51.4 us
    reduce_scatter x1, waiting for transfers between devices, per_device(): lax.psum_scatter(bias_grad_rows.astype(jnp.bfloat16), 'copy', scatter_dim...  45.1 us
    psum x1, blocking collectives, per_device(): grad_pair_weight = lax.psum(pair_weight_term, ('copy', 'tok'))  40.6 us
    all_gather x1, blocking collectives, per_device(): bias_rows = lax.all_gather(bias_local, 'copy', axis=2, tiled=True)  24.5 us
    dot_general x13, matrix products, matmul(): return jnp.dot(left, right, preferred_element_type=jnp.float32)  21.9 us
    another operation x1, local copies, waits for them, and re-layouts, per_device(): jnp.stack([jnp.einsum('rd,re->de', flat_x, d_query, preferred_element_typ...  8.53 us
  transfers between devices with their start and end apart: 5, of which 4 were waited for; matrix products, arithmetic and copies ran while one was open for 13% of the time, Pallas kernels for 0%

commit v1 on v0

v1 whole, which is shorter than its diff:
```python
import jax
import jax.numpy as jnp
from jax import lax
from jax.sharding import PartitionSpec as P

epsilon = 1e-05
f32 = jnp.float32
bf16 = jnp.bfloat16


def layer_forward(values, scales):
    average = jnp.mean(values, axis=-1, keepdims=True)
    centred = values - average
    inverse = lax.rsqrt(jnp.mean(centred * centred, axis=-1, keepdims=True) + epsilon)
    normed = centred * inverse
    return (normed * scales, normed, inverse)


def layer_backward(upstream, scales, normed, inverse):
    scaled = upstream * scales
    first_moment = jnp.mean(scaled, axis=-1, keepdims=True)
    second_moment = jnp.mean(scaled * normed, axis=-1, keepdims=True)
    return inverse * (scaled - first_moment - normed * second_moment)


def mm(left, right, dims=((1,), (0,))):
    return lax.dot_general(left, right, (dims, ((), ())), preferred_element_type=f32)


def swap(value, axis, mask):
    size = lax.axis_size(axis)
    return lax.ppermute(value, axis, [(i, i ^ mask) for i in range(size)])


def gather_tok(value):
    size = lax.axis_size("tok")
    return jnp.stack([value] + [swap(value, "tok", r) for r in range(1, size)])


def scatter_copy(parts):
    size = lax.axis_size("copy")
    me = lax.axis_index("copy")
    mask = 1
    while mask < size:
        bit = (me // mask) % 2
        pairs = parts.reshape((parts.shape[0] // 2, 2) + parts.shape[1:])
        kept = lax.dynamic_index_in_dim(pairs, bit, 1, keepdims=False)
        sent = lax.dynamic_index_in_dim(pairs, 1 - bit, 1, keepdims=False)
        got = swap(sent, "copy", mask)
        parts = (kept.astype(f32) + got.astype(f32)).astype(bf16)
        mask *= 2
    return parts[0]


def gather_copy(value):
    size = lax.axis_size("copy")
    me = lax.axis_index("copy")
    held = value[None]
    mask = size // 2
    while mask:
        got = swap(held, "copy", mask)
        bit = (me // mask) % 2
        held = jnp.where(
            bit == 0, jnp.stack([held, got], axis=1), jnp.stack([got, held], axis=1)
        )
        held = held.reshape((-1,) + value.shape)
        mask //= 2
    return held


def per_device(
    noisy,
    single,
    pair,
    restype,
    chain,
    keymask,
    restype_table,
    norm_gain,
    pair_gain,
    trans_gain,
    w_query,
    w_key,
    w_value,
    w_out,
    w_pair,
    chain_weight,
    w_hidden_gate,
    w_hidden_up,
    w_down,
    cotangent,
):
    copies = lax.axis_size("copy")
    toks = lax.axis_size("tok")
    me_tok = lax.axis_index("tok")
    _, rows, width = noisy.shape
    cols = pair.shape[1]
    channels = pair.shape[2]
    heads = w_pair.shape[1]
    head_width = width // heads
    own_heads = heads // toks
    own_width = own_heads * head_width
    tokens = rows * toks
    scale = head_width ** (-0.5)
    blocks = [me_tok ^ r for r in range(toks)]

    pair_scaled, pair_hat, pair_inverse = layer_forward(pair.astype(f32), pair_gain)
    pair_rounded = pair_scaled.astype(bf16)
    bias_local = jnp.einsum(
        "ijc,ch->hji", pair_rounded, w_pair, preferred_element_type=f32
    ).astype(bf16)
    bias_split = bias_local.reshape(toks, own_heads, cols, rows)
    bias_parts = []
    for r in range(toks):
        piece = lax.dynamic_index_in_dim(bias_split, blocks[r], 0, keepdims=False)
        bias_parts.append(piece if r == 0 else swap(piece, "tok", r))
    bias_mine = jnp.concatenate(bias_parts, axis=-1)
    bias_all = gather_copy(bias_mine)
    bias = jnp.transpose(bias_all, (1, 0, 2, 3)).reshape(own_heads, tokens, tokens)

    res_onehot = (
        restype[:, None] == jnp.arange(restype_table.shape[0], dtype=jnp.int32)[None, :]
    ).astype(bf16)
    condition = single.astype(f32) + mm(res_onehot, restype_table)
    noisy_f = noisy[0].astype(f32)
    normed_scaled, noisy_hat, noisy_inverse = layer_forward(noisy_f, norm_gain)
    x_own = (normed_scaled + condition).astype(bf16)
    x = gather_tok(x_own).reshape(tokens, width)

    def columns(weight):
        return lax.dynamic_slice_in_dim(weight, me_tok * own_width, own_width, axis=1)

    wq, wk, wv = columns(w_query), columns(w_key), columns(w_value)
    query = mm(wq, x, ((0,), (1,))).astype(bf16).reshape(own_heads, head_width, tokens)
    key = mm(wk, x, ((0,), (1,))).astype(bf16).reshape(own_heads, head_width, tokens)
    value = mm(wv, x, ((0,), (1,))).astype(bf16).reshape(own_heads, head_width, tokens)

    def token_order(array, axis):
        return jnp.concatenate(
            [
                lax.dynamic_slice_in_dim(array, b * rows, rows, axis=axis)
                for b in blocks
            ],
            axis=axis,
        )

    chain_rel = token_order(chain, 0)
    mask_rel = token_order(keymask, 0)
    chain_onehot = (
        chain_rel[:, None] == jnp.arange(chain_weight.shape[0], dtype=jnp.int32)[None, :]
    ).astype(f32)
    key_weight = jnp.dot(
        chain_onehot,
        lax.dynamic_slice_in_dim(chain_weight, me_tok * own_heads, own_heads, axis=1),
        precision=lax.Precision.HIGHEST,
    )
    same_chain = (chain_rel[:, None] == chain_rel[None, :]).astype(f32)
    extra = (
        token_order(bias, 1).astype(f32)
        + same_chain[None] * key_weight.T[:, :, None]
    )
    logits = (
        jnp.einsum("hdj,hdi->hji", key, query, preferred_element_type=f32) * scale + extra
    )
    logits = jnp.where((mask_rel > 0)[None, :, None], logits, -1e30)
    highest = jnp.max(logits, axis=1, keepdims=True)
    exponent = jnp.exp(logits - highest)
    weights = exponent / jnp.sum(exponent, axis=1, keepdims=True)
    weights_b = weights.astype(bf16)
    att = jnp.einsum("hdj,hji->hdi", value, weights_b, preferred_element_type=f32).astype(
        bf16
    )
    att = att.reshape(own_width, toks, rows)
    attended = []
    for r in range(toks):
        piece = att[:, r]
        attended.append(piece if r == 0 else swap(piece, "tok", r))

    projected = 0.0
    for r in range(toks):
        w_rows = lax.dynamic_slice_in_dim(w_out, blocks[r] * own_width, own_width, axis=0)
        projected = projected + mm(attended[r], w_rows, ((0,), (0,)))
    residual = noisy_f + projected
    trans_scaled, trans_hat, trans_inverse = layer_forward(residual, trans_gain)
    trans_in = trans_scaled.astype(bf16)
    gate = mm(trans_in, w_hidden_gate)
    up_part = mm(trans_in, w_hidden_up)
    sigmoid_gate = jax.nn.sigmoid(gate)
    upstream = cotangent[0]
    d_hidden = mm(upstream, w_down, ((1,), (1,)))
    d_gate = (
        d_hidden * up_part * sigmoid_gate * (1.0 + gate * (1.0 - sigmoid_gate))
    ).astype(bf16)
    d_up = (d_hidden * gate * sigmoid_gate).astype(bf16)
    d_trans = mm(d_gate, w_hidden_gate, ((1,), (1,))) + mm(
        d_up, w_hidden_up, ((1,), (1,))
    )
    d_res = upstream.astype(f32) + layer_backward(
        d_trans, trans_gain, trans_hat, trans_inverse
    )
    d_res_all = gather_tok(d_res.astype(bf16)).reshape(tokens, width)

    w_out_rows = lax.dynamic_slice_in_dim(w_out, me_tok * own_width, own_width, axis=0)
    d_att = mm(w_out_rows, d_res_all, ((1,), (1,))).astype(bf16)
    out_grad = mm(d_res_all, att.reshape(own_width, tokens), ((0,), (1,)))
    d_att = d_att.reshape(own_heads, head_width, tokens)
    d_weights = jnp.einsum("hdj,hdi->hji", value, d_att, preferred_element_type=f32)
    delta = jnp.sum(weights * d_weights, axis=1, keepdims=True)
    d_logits = weights * (d_weights - delta)
    d_logits_b = d_logits.astype(bf16)
    d_query = (
        jnp.einsum("hdj,hji->hdi", key, d_logits_b, preferred_element_type=f32) * scale
    )
    d_key = (
        jnp.einsum("hdi,hji->hdj", query, d_logits_b, preferred_element_type=f32) * scale
    )
    d_value = jnp.einsum("hdi,hji->hdj", d_att, weights_b, preferred_element_type=f32)
    d_query, d_key, d_value = [
        part.astype(bf16).reshape(own_width, tokens) for part in (d_query, d_key, d_value)
    ]

    d_bias = token_order(d_logits_b, 1).reshape(own_heads, copies, cols, tokens)
    bias_grad_mine = scatter_copy(jnp.transpose(d_bias, (1, 0, 2, 3)))
    bias_grad_mine = bias_grad_mine.reshape(own_heads, cols, toks, rows)
    received = []
    for r in range(toks):
        piece = bias_grad_mine[:, :, r]
        received.append(piece if r == 0 else swap(piece, "tok", r))
    received = jnp.stack(received)
    bias_grad = jnp.concatenate(
        [lax.dynamic_index_in_dim(received, me_tok ^ a, 0, keepdims=False) for a in range(toks)]
    )
    d_pair_scaled = jnp.einsum("hji,ch->ijc", bias_grad, w_pair, preferred_element_type=f32)
    grad_pair = layer_backward(d_pair_scaled, pair_gain, pair_hat, pair_inverse).astype(bf16)
    pair_weight_term = jnp.einsum(
        "ijc,hji->ch", pair_rounded, bias_grad, preferred_element_type=f32
    )
    mask = 1
    while mask < copies:
        pair_weight_term = pair_weight_term + swap(pair_weight_term, "copy", mask)
        mask *= 2
    mask = 1
    while mask < toks:
        pair_weight_term = pair_weight_term + swap(pair_weight_term, "tok", mask)
        mask *= 2

    d_inputs = mm(wq, d_query) + mm(wk, d_key) + mm(wv, d_value)
    d_inputs = d_inputs.reshape(width, toks, rows)
    total = d_inputs[:, 0]
    for r in range(1, toks):
        total = total + swap(d_inputs[:, r].astype(bf16), "tok", r).astype(f32)
    grad_noisy = (
        d_res + layer_backward(total.T, norm_gain, noisy_hat, noisy_inverse)
    ).astype(bf16)[None]
    grad_single = scatter_copy(total.astype(bf16).reshape(copies, width // copies, rows))
    grad_single = grad_single.T.astype(f32)

    group = copies // toks
    piece_cols = width // copies
    piece_rows = width // toks
    wide = jnp.stack([mm(part, x) for part in (d_query, d_key, d_value)]).astype(bf16)
    wide = wide.reshape(3, group, piece_cols, toks, piece_rows)
    wide = jnp.transpose(wide, (3, 1, 0, 2, 4)).reshape(copies, 3, piece_cols, piece_rows)
    narrow = out_grad.astype(bf16).reshape(copies, 1, piece_cols, own_width)
    mine = scatter_copy(jnp.concatenate([wide, narrow], axis=1))
    pairs = []
    for c in range(copies):
        for t in range(toks):
            pairs.append((c * toks + t, (t * group + c % group) * toks + c // group))
    moved = lax.ppermute(mine[:3], ("copy", "tok"), pairs)
    finals = [jnp.transpose(part).astype(f32) for part in (moved[0], moved[1], moved[2], mine[3])]
    return (
        grad_noisy,
        grad_single,
        grad_pair,
        finals[0],
        finals[1],
        finals[2],
        finals[3],
        pair_weight_term,
    )


def solution(mesh):
    placed = (
        P("copy", "tok", None),
        P("tok", None),
        P("tok", "copy", None),
        P("tok"),
    ) + (P(),) * 15 + (P("copy", "tok", None),)
    return jax.shard_map(
        per_device,
        mesh=mesh,
        in_specs=placed,
        out_specs=(
            P("copy", "tok", None),
            P("tok", "copy"),
            P("tok", "copy", None),
            P("tok", "copy"),
            P("tok", "copy"),
            P("tok", "copy"),
            P("tok", "copy"),
            P(),
        ),
        check_vma=False,
    )
```

time: 385 us -> 154 us (0.40)
  waiting for transfers between devices: 172 us -> 45.4 us
  blocking collectives: 78.9 us -> 0 us
  local copies, waits for them, and re-layouts: 66.2 us -> 14.1 us
  starting transfers between devices: 0.39 us -> 34.6 us
  between operations: 14.9 us -> 1.8 us
  other arithmetic: 10.4 us -> 20.5 us
    unnamed x9 -> x0, waiting for transfers between devices: 127 us -> none
    ppermute x0 -> x28, waiting for transfers between devices: none -> 45.4 us  [the longest x27 41.7 us: swap(): return lax.ppermute(value, axis, [(i, i ^ mask) for i in range(size)])]
    unnamed x67 -> x113, local copies, waits for them, and re-layouts: 51.4 us -> 6.09 us
    reduce_scatter x1 -> x0, waiting for transfers between devices: 45.1 us -> none  [per_device(): lax.psum_scatter(bias_grad_rows.astype(jnp.bfloat16), 'copy', scatter_dim...]
    psum x1 -> x0, blocking collectives: 40.6 us -> none  [per_device(): grad_pair_weight = lax.psum(pair_weight_term, ('copy', 'tok'))]
    all_gather x3 -> x0, blocking collectives: 38.2 us -> none  [the longest x1 24.5 us: per_device(): bias_rows = lax.all_gather(bias_local, 'copy', axis=2, tiled=True)]
    ppermute x0 -> x28, starting transfers between devices: none -> 34.6 us  [the longest x27 30.5 us: swap(): return lax.ppermute(value, axis, [(i, i ^ mask) for i in range(size)])]
    another operation x1, local copies, waits for them, and re-layouts: 8.53 us -> 0.02 us  [per_device(): bias_grad_mine = bias_grad_mine.reshape(own_heads, cols, toks, rows)]
  transfers between devices with their start and end apart: 5 -> 28, of which waited for: 4 -> 17; matrix products, arithmetic and copies ran while one was open for 13% -> 21% of each run, Pallas kernels for 0% -> 0%
where the time goes in v1:
time: 154 us; the launch traced here: 152 us
  waiting for transfers between devices  45.4 us (29%)
  matrix products  35.6 us (23%)
  starting transfers between devices  34.6 us (22%)
  other arithmetic  20.5 us (13%)
  local copies, waits for them, and re-layouts  14.1 us (9%)
  between operations  1.8 us (1%)
    ppermute x27, waiting for transfers between devices, swap(): return lax.ppermute(value, axis, [(i, i ^ mask) for i in range(size)])  41.7 us
    ppermute x27, starting transfers between devices, swap(): return lax.ppermute(value, axis, [(i, i ^ mask) for i in range(size)])  30.5 us
    dot_general x18, matrix products, mm(): lax.dot_general(left, right, (dims, ((), ())), preferred_element_type=f32)  23.6 us
    unnamed x113, local copies, waits for them, and re-layouts  6.09 us
    convert_element_type x11, other arithmetic, scatter_copy(): parts = (kept.astype(f32) + got.astype(f32)).astype(bf16)  4.86 us
    ppermute x1, starting transfers between devices, per_device(): moved = lax.ppermute(mine[:3], ('copy', 'tok'), pairs)  4.07 us
    ppermute x1, waiting for transfers between devices, per_device(): moved = lax.ppermute(mine[:3], ('copy', 'tok'), pairs)  3.72 us
  transfers between devices with their start and end apart: 28, of which 17 were waited for; matrix products, arithmetic and copies ran while one was open for 21% of the time, Pallas kernels for 0%

profile of v1, /device:TPU:2, one launch (start us, length us, event | category | flops | bytes accessed | tf_op | source)
XLA Modules:
  0.0 152.1 jit_solution(11475946982370922619)
XLA Ops:
  0.7 1.2 convert_reduce_fusion.1
  1.9 1.1 fusion.63
  3.0 2.0 %fusion.27 = bf16[128,768]{1,0:T(8,128)(2,1)} fusion(bf16[32,768]{1,0:T(8,128)(2,1)} %param.26, bf16[1,128,768]{2,1,0:T(8,128)(2,1)} %param.20, bf16[128,768]{1,0:T(8,128)(2,1)} %param.21, f32[768]{0:T(1024)} %param.27, f32[128]{0:T(128)S(1)} %add_rsqrt_fusion.2, f32[128]{0:T(128)S(1)} %broadcast_multiply_fusion.8, s32[128]{0:T(128)} %param.23), kind=kOutput, calls=%fused_computation.50 | convolution fusion | flops 7081984 | bytes 643584 | tf_op jit(solution)/shard_map/dot_general | solution.py:27
  6.2 2.1 %collective-permute-start.1 = (bf16[4,16,128]{2,1,0:T(8,128)(2,1)S(1)}, bf16[4,16,128]{2,1,0:T(8,128)(2,1)S(1)}, u32[]{:S(2)}, u32[]{:S(2)}) collective-permute-start(bf16[4,16,128]{2,1,0:T(8,128)(2,1)S(1)} %bitcast.370), channel_id=1, source_target_pairs={{0,1},{1,0},{2,3},{3,2},{4,5},{5,4},{6,7},{7,6},{8,9},{9,8},{10,11... | collective-permute-start | bytes 49160 | tf_op jit(solution)/shard_map/ppermute | solution.py:32
  8.4 0.8 compare_convert_fusion
  9.2 3.4 %fusion.73 = f32[128,1536]{1,0:T(8,128)} fusion(bf16[1536,768]{1,0:T(8,128)(2,1)} %param.38, bf16[1,128,768]{2,1,0:T(8,128)(2,1)S(1)} %copy-done.22), kind=kOutput, calls=%fused_computation.134 | convolution fusion | flops 301989888 | bytes 3342336 | tf_op jit(solution)/shard_map/dot_general | solution.py:27
  13.0 2.6 %collective-permute-start.2 = (bf16[1,4,16,256]{3,2,1,0:T(8,128)(2,1)S(1)}, bf16[1,4,16,256]{3,2,1,0:T(8,128)(2,1)S(1)}, u32[]{:S(2)}, u32[]{:S(2)}) collective-permute-start(bf16[1,4,16,256]{3,2,1,0:T(8,128)(2,1)S(1)} %get-tuple-element.70), channel_id=1, source_target_pairs={{0,16},{2,18},{4,20},{6,22},{8,24},{10,26},{12,28},{14,30},{16,0},... | collective-permute-start | bytes 98312 | tf_op jit(solution)/shard_map/ppermute | solution.py:32
  15.8 2.1 %collective-permute-done.2 = bf16[1,4,16,256]{3,2,1,0:T(8,128)(2,1)S(1)} collective-permute-done((bf16[1,4,16,256]{3,2,1,0:T(8,128)(2,1)S(1)}, bf16[1,4,16,256]{3,2,1,0:T(8,128)(2,1)S(1)}, u32[]{:S(2)}, u32[]{:S(2)}) %collective-permute-start.2) | collective-permute-done | bytes 32800 | tf_op jit(solution)/shard_map/ppermute | solution.py:32
  17.9 1.6 %collective-permute-start.3 = (bf16[2,4,16,256]{3,2,1,0:T(8,128)(2,1)S(1)}, bf16[2,4,16,256]{3,2,1,0:T(8,128)(2,1)S(1)}, u32[]{:S(2)}, u32[]{:S(2)}) collective-permute-start(bf16[2,4,16,256]{3,2,1,0:T(8,128)(2,1)S(1)} %maximum_select_fusion.4), channel_id=1, source_target_pairs={{0,8},{2,10},{4,12},{6,14},{8,0},{10,2},{12,4},{14,6},{16,24},{18,... | collective-permute-start | bytes 196616 | tf_op jit(solution)/shard_map/ppermute | solution.py:32
  19.5 2.7 %collective-permute-done.3 = bf16[2,4,16,256]{3,2,1,0:T(8,128)(2,1)S(1)} collective-permute-done((bf16[2,4,16,256]{3,2,1,0:T(8,128)(2,1)S(1)}, bf16[2,4,16,256]{3,2,1,0:T(8,128)(2,1)S(1)}, u32[]{:S(2)}, u32[]{:S(2)}) %collective-permute-start.3) | collective-permute-done | bytes 65568 | tf_op jit(solution)/shard_map/ppermute | solution.py:32
  22.2 1.6 %collective-permute-start.4 = (bf16[4,4,16,256]{3,2,1,0:T(8,128)(2,1)S(1)}, bf16[4,4,16,256]{3,2,1,0:T(8,128)(2,1)S(1)}, u32[]{:S(2)}, u32[]{:S(2)}) collective-permute-start(bf16[4,4,16,256]{3,2,1,0:T(8,128)(2,1)S(1)} %bitcast.349), channel_id=1, source_target_pairs={{0,4},{2,6},{4,0},{6,2},{8,12},{10,14},{12,8},{14,10},{16,20},{18,... | collective-permute-start | bytes 393224 | tf_op jit(solution)/shard_map/ppermute | solution.py:32
  23.8 1.1 pad_maximum_fusion.1
  25.3 2.0 %collective-permute-done.4 = bf16[4,4,16,256]{3,2,1,0:T(8,128)(2,1)S(1)} collective-permute-done((bf16[4,4,16,256]{3,2,1,0:T(8,128)(2,1)S(1)}, bf16[4,4,16,256]{3,2,1,0:T(8,128)(2,1)S(1)}, u32[]{:S(2)}, u32[]{:S(2)}) %collective-permute-start.4) | collective-permute-done | bytes 131104 | tf_op jit(solution)/shard_map/ppermute | solution.py:32
  27.4 1.1 convolution_convert_fusion.8
  28.4 1.1 convolution_convert_fusion.9
  29.7 0.8 constant_dynamic-slice_fusion.7
  30.5 2.8 %fusion.116 = (f32[4,256]{1,0:T(4,128)S(1)}, f32[4,256,256]{2,1,0:T(8,128)}) fusion(bf16[4,96,256]{2,1,0:T(8,128)(2,1)} %bitcast.345, bf16[4,96,256]{2,1,0:T(8,128)(2,1)S(1)} %bitcast.341, bf16[4,128,256]{2,1,0:T(8,128)(2,1)} %get-tuple-element.59, bf16[4,128,256]{2,1,0:T(8,128)(2,1)} %get-tuple-element.58, f32[4,256]{1,0:T(4,128)S(1)} %fusion.76, ...), kind=kOutput, calls=%fused_computation.238 | convolution fusion | flops 53215488 | bytes 2236672 | tf_op jit(solution)/shard_map/sub | solution.py:167
  33.4 2.8 %convolution_convert_fusion.5 = bf16[4,96,256]{2,1,0:T(8,128)(2,1)} fusion(bf16[4,96,256]{2,1,0:T(8,128)(2,1)} %bitcast.358, f32[4,256]{1,0:T(4,128)S(1)} %get-tuple-element.77, bf16[4,96,256]{2,1,0:T(8,128)(2,1)} %bitcast.346, bf16[4,96,256]{2,1,0:T(8,128)(2,1)S(1)} %bitcast.342, bf16[4,128,256]{2,1,0:T(8,128)(2,1)} %get-tuple-element.59, ...), kind=kOutput, calls=%fused_computation.52 | convolution fusion | flops 103908608 | bytes 1581312 | tf_op jit(solution)/shard_map/hdj,hji->hdi/dot_general | solution.py:170
  36.2 1.0 reshape.425
  37.8 1.4 fusion.43
  39.2 3.6 %collective-permute-done.6 = bf16[384,128]{1,0:T(8,128)(2,1)S(1)} collective-permute-done((bf16[384,128]{1,0:T(8,128)(2,1)S(1)}, bf16[384,128]{1,0:T(8,128)(2,1)S(1)}, u32[]{:S(2)}, u32[]{:S(2)}) %collective-permute-start.6) | collective-permute-done | bytes 98336 | tf_op jit(solution)/shard_map/ppermute | solution.py:32
  43.9 1.4 fusion.108
  45.3 4.3 %fusion.21 = f32[128,768]{1,0:T(8,128)} fusion(bf16[768,1536]{1,0:T(8,128)(2,1)S(1)} %copy-done, f32[128,1536]{1,0:T(8,128)} %fusion.73, bf16[768,1536]{1,0:T(8,128)(2,1)} %param.37, f32[128,1536]{1,0:T(8,128)} %fusion.108, f32[128,768]{1,0:T(8,128)} %copy-done.2, f32[768]{0:T(1024)S(1)} %copy-done.40, f32[128]{0:T(128)S(1)} %add_rsqrt_fusion.1, ...), kind=kOutput, calls=%fused_computation.43 | convolution fusion | flops 606339072 | bytes 7081984 | tf_op jit(solution)/shard_map/dot_general | solution.py:27
  49.6 3.3 %fusion.110 = (f32[128]{0:T(128)S(1)}, f32[128]{0:T(128)S(1)}, f32[128,768]{1,0:T(8,128)S(1)}) fusion(f32[128]{0:T(128)S(1)} %add_rsqrt_fusion.1, f32[128,768]{1,0:T(8,128)} %copy-done.2, f32[128]{0:T(128)S(1)} %broadcast_multiply_fusion.7, f32[768]{0:T(1024)S(1)} %copy-done.40, f32[128,768]{1,0:T(8,128)} %fusion.21, bf16[768,1536]{1,0:T(8,128)(2,1)} %param.37, ...), kind=kOutput, calls=%fused_computation.232 | convolution fusion | flops 303857408 | bytes 5116928 | tf_op jit(solution)/shard_map/dot_general | solution.py:27
  53.0 1.0 fusion.111
  54.2 0.9 copy.108
  55.1 5.4 %collective-permute-done.7 = bf16[128,768]{1,0:T(8,128)(2,1)} collective-permute-done((bf16[128,768]{1,0:T(8,128)(2,1)S(1)}, bf16[128,768]{1,0:T(8,128)(2,1)}, u32[]{:S(2)}, u32[]{:S(2)}) %collective-permute-start.7) | collective-permute-done | bytes 196640 | tf_op jit(solution)/shard_map/ppermute | solution.py:32
  60.5 1.0 pad_maximum_fusion.2
  61.5 0.7 copy-done.8
  62.2 2.1 %convolution_convert_fusion.6 = bf16[384,256]{1,0:T(8,128)(2,1)} fusion(bf16[256,768]{1,0:T(8,128)(2,1)S(1)} %bitcast.318, bf16[768,768]{1,0:T(8,128)(2,1)} %param.33, s32[]{:T(128)S(6)} %select_n.234), kind=kOutput, calls=%fused_computation.55 | convolution fusion | flops 151093248 | bytes 1179652 | tf_op jit(solution)/shard_map/dot_general | solution.py:27
  64.4 2.7 %convolution_convert_fusion.4 = bf16[4,96,256]{2,1,0:T(8,128)(2,1)} fusion(bf16[4,96,256]{2,1,0:T(8,128)(2,1)} %bitcast.360, f32[4,256]{1,0:T(4,128)} %copy-done.41, bf16[4,96,256]{2,1,0:T(8,128)(2,1)S(1)} %bitcast.347, bf16[4,96,256]{2,1,0:T(8,128)(2,1)S(1)} %bitcast.343, bf16[4,128,256]{2,1,0:T(8,128)(2,1)} %get-tuple-element.59, ...), kind=kOutput, calls=%fused_computation.51 | convolution fusion | flops 103908608 | bytes 1581312 | tf_op jit(solution)/shard_map/hdi,hji->hdj/dot_general | solution.py:217
  67.0 1.9 %multiply_reduce_fusion = (f32[4,256]{1,0:T(4,128)S(1)}, f32[4,256,256]{2,1,0:T(8,128)S(1)}) fusion(f32[4,256,256]{2,1,0:T(8,128)} %get-tuple-element.78, f32[4,256]{1,0:T(4,128)} %copy-done.41, bf16[4,96,256]{2,1,0:T(8,128)(2,1)} %bitcast.359, bf16[4,96,256]{2,1,0:T(8,128)(2,1)} %bitcast.361), kind=kOutput, calls=%fused_computation.68 | convolution fusion | flops 51117056 | bytes 2498560 | tf_op jit(solution)/shard_map/hdj,hdi->hji/dot_general | solution.py:207
  71.0 0.7 dynamic-slice_bitcast_fusion.2
  74.8 0.8 copy-done.17
  77.0 1.2 fusion.23
  78.5 4.5 %collective-permute-done.8 = bf16[768,128]{0,1:T(8,128)(2,1)S(1)} collective-permute-done((bf16[768,128]{0,1:T(8,128)(2,1)S(1)}, bf16[768,128]{0,1:T(8,128)(2,1)S(1)}, u32[]{:S(2)}, u32[]{:S(2)}) %collective-permute-start.8) | collective-permute-done | bytes 196640 | tf_op jit(solution)/shard_map/ppermute | solution.py:32
  83.3 0.7 fusion.107
  84.1 1.7 %copy.102 = bf16[768,128]{1,0:T(8,128)(2,1)} copy(bf16[768,128]{0,1:T(8,128)(2,1)} %get-tuple-element.54) | data formatting | bytes 393216 | tf_op jit(solution)/shard_map/convert_element_type | solution.py:255
  85.8 1.0 dynamic-slice_bitcast_fusion.4
  86.8 2.2 %fusion.71 = bf16[1,128,768]{2,1,0:T(8,128)(2,1)} fusion(f32[128,768]{1,0:T(8,128)} %get-tuple-element.53, bf16[1,128,768]{2,1,0:T(8,128)(2,1)} %param.20, f32[128]{0:T(128)S(1)} %broadcast_multiply_fusion.3, f32[128]{0:T(128)S(1)} %broadcast_multiply_fusion.4, f32[768]{0:T(1024)S(1)} %copy-done.35, f32[128]{0:T(128)S(1)} %copy-done.44, ...), kind=kLoop, calls=%fused_computation.131 | loop fusion | flops 1179648 | bytes 1381376 | tf_op jit(solution)/shard_map/broadcast_in_dim | solution.py:252
  89.0 1.0 fusion.41
  90.1 1.6 %collective-permute-start.10 = (bf16[4,48,128]{2,1,0:T(8,128)(2,1)S(1)}, bf16[4,48,128]{2,1,0:T(8,128)(2,1)S(1)}, u32[]{:S(2)}, u32[]{:S(2)}) collective-permute-start(bf16[4,48,128]{2,1,0:T(8,128)(2,1)S(1)} %dynamic-slice_bitcast_fusion.6), channel_id=1, source_target_pairs={{0,4},{2,6},{4,0},{6,2},{8,12},{10,14},{12,8},{14,10},{16,20},{18,... | collective-permute-start | bytes 147464 | tf_op jit(solution)/shard_map/ppermute | solution.py:32
  92.2 2.0 %collective-permute-done.10 = bf16[4,48,128]{2,1,0:T(8,128)(2,1)S(1)} collective-permute-done((bf16[4,48,128]{2,1,0:T(8,128)(2,1)S(1)}, bf16[4,48,128]{2,1,0:T(8,128)(2,1)S(1)}, u32[]{:S(2)}, u32[]{:S(2)}) %collective-permute-start.10) | collective-permute-done | bytes 49184 | tf_op jit(solution)/shard_map/ppermute | solution.py:32
  94.3 3.1 %collective-permute-done.14 = bf16[4,4,16,256]{3,2,1,0:T(8,128)(2,1)S(1)} collective-permute-done((bf16[4,4,16,256]{3,2,1,0:T(8,128)(2,1)S(1)}, bf16[4,4,16,256]{3,2,1,0:T(8,128)(2,1)S(1)}, u32[]{:S(2)}, u32[]{:S(2)}) %collective-permute-start.14) | collective-permute-done | bytes 131104 | tf_op jit(solution)/shard_map/ppermute | solution.py:32
  97.4 1.6 %collective-permute-start.15 = (bf16[2,4,16,256]{3,2,1,0:T(8,128)(2,1)S(1)}, bf16[2,4,16,256]{3,2,1,0:T(8,128)(2,1)S(1)}, u32[]{:S(2)}, u32[]{:S(2)}) collective-permute-start(bf16[2,4,16,256]{3,2,1,0:T(8,128)(2,1)S(1)} %dynamic-slice_bitcast_fusion.5), channel_id=1, source_target_pairs={{0,8},{2,10},{4,12},{6,14},{8,0},{10,2},{12,4},{14,6},{16,24},{18,... | collective-permute-start | bytes 196616 | tf_op jit(solution)/shard_map/ppermute | solution.py:32
  99.5 2.2 %collective-permute-done.15 = bf16[2,4,16,256]{3,2,1,0:T(8,128)(2,1)S(1)} collective-permute-done((bf16[2,4,16,256]{3,2,1,0:T(8,128)(2,1)S(1)}, bf16[2,4,16,256]{3,2,1,0:T(8,128)(2,1)S(1)}, u32[]{:S(2)}, u32[]{:S(2)}) %collective-permute-start.15) | collective-permute-done | bytes 65568 | tf_op jit(solution)/shard_map/ppermute | solution.py:32
  101.8 2.9 %collective-permute-start.16 = (bf16[1,4,16,256]{3,2,1,0:T(8,128)(2,1)S(1)}, bf16[1,4,16,256]{3,2,1,0:T(8,128)(2,1)S(1)}, u32[]{:S(2)}, u32[]{:S(2)}) collective-permute-start(bf16[1,4,16,256]{3,2,1,0:T(8,128)(2,1)S(1)} %constant_dynamic-slice_fusion.1), channel_id=1, source_target_pairs={{0,16},{2,18},{4,20},{6,22},{8,24},{10,26},{12,28},{14,30},{16,0},... | collective-permute-start | bytes 98312 | tf_op jit(solution)/shard_map/ppermute | solution.py:32
  105.3 1.4 collective-permute-done.16
  107.4 0.7 constant_dynamic-slice_fusion.4
  108.1 2.8 %collective-permute-start.12 = (bf16[1,48,128]{2,1,0:T(8,128)(2,1)S(1)}, bf16[1,48,128]{2,1,0:T(8,128)(2,1)S(1)}, u32[]{:S(2)}, u32[]{:S(2)}) collective-permute-start(bf16[1,48,128]{2,1,0:T(8,128)(2,1)S(1)} %constant_dynamic-slice_fusion.4), channel_id=1, source_target_pairs={{0,16},{2,18},{4,20},{6,22},{8,24},{10,26},{12,28},{14,30},{16,0},... | collective-permute-start | bytes 36872 | tf_op jit(solution)/shard_map/ppermute | solution.py:32
  111.0 1.8 %fusion.4 = bf16[8,4,48,384]{3,2,1,0:T(8,128)(2,1)S(1)} fusion(bf16[8,4,48,384]{3,2,1,0:T(8,128)(2,1)} %collective-permute-done.18, s32[]{:T(128)S(6)} %select_n.264, bf16[8,2,3,48,384]{4,3,2,1,0:T(8,128)(2,1)} %bitcast.302, bf16[8,2,1,48,384]{4,3,2,1,0:T(8,128)(2,1)S(1)} %bitcast.315), kind=kLoop, calls=%fused_computation.10 | loop fusion | flops 2949120 | bytes 4718596 | tf_op jit(solution)/shard_map/convert_element_type | solution.py:50
  112.9 1.4 collective-permute-start.19
  117.0 7.7 %collective-permute-done.24 = f32[128,8]{0,1:T(8,128)S(1)} collective-permute-done((f32[128,8]{0,1:T(8,128)S(1)}, f32[128,8]{0,1:T(8,128)S(1)}, u32[]{:S(2)}, u32[]{:S(2)}) %collective-permute-start.24) | collective-permute-done | bytes 4128 | tf_op jit(solution)/shard_map/ppermute | solution.py:32
  124.7 1.8 %collective-permute-start.25 = (f32[128,8]{0,1:T(8,128)S(1)}, f32[128,8]{0,1:T(8,128)S(1)}, u32[]{:S(2)}, u32[]{:S(2)}) collective-permute-start(f32[128,8]{0,1:T(8,128)S(1)} %add.289), channel_id=1, source_target_pairs={{0,8},{2,10},{4,12},{6,14},{8,0},{10,2},{12,4},{14,6},{16,24},{18,... | collective-permute-start | bytes 12296 | tf_op jit(solution)/shard_map/ppermute | solution.py:32
  127.0 1.3 collective-permute-done.25
  128.3 2.2 %collective-permute-start.26 = (f32[128,8]{0,1:T(8,128)S(1)}, f32[128,8]{0,1:T(8,128)S(1)}, u32[]{:S(2)}, u32[]{:S(2)}) collective-permute-start(f32[128,8]{0,1:T(8,128)S(1)} %add.290), channel_id=1, source_target_pairs={{0,16},{2,18},{4,20},{6,22},{8,24},{10,26},{12,28},{14,30},{16,0},... | collective-permute-start | bytes 12296 | tf_op jit(solution)/shard_map/ppermute | solution.py:32
  130.5 2.4 %collective-permute-done.26 = f32[128,8]{0,1:T(8,128)S(1)} collective-permute-done((f32[128,8]{0,1:T(8,128)S(1)}, f32[128,8]{0,1:T(8,128)S(1)}, u32[]{:S(2)}, u32[]{:S(2)}) %collective-permute-start.26) | collective-permute-done | bytes 4128 | tf_op jit(solution)/shard_map/ppermute | solution.py:32
  133.5 1.6 %collective-permute-start.27 = (f32[128,8]{0,1:T(8,128)}, f32[128,8]{0,1:T(8,128)}, u32[]{:S(2)}, u32[]{:S(2)}) collective-permute-start(f32[128,8]{0,1:T(8,128)} %add.291), channel_id=1, source_target_pairs={{0,1},{1,0},{2,3},{3,2},{4,5},{5,4},{6,7},{7,6},{8,9},{9,8},{10,11... | collective-permute-start | bytes 12296 | tf_op jit(solution)/shard_map/ppermute | solution.py:32
  135.3 3.1 %collective-permute-start.21 = (bf16[1,4,48,384]{3,2,1,0:T(8,128)(2,1)S(1)}, bf16[1,4,48,384]{3,2,1,0:T(8,128)(2,1)}, u32[]{:S(2)}, u32[]{:S(2)}) collective-permute-start(bf16[1,4,48,384]{3,2,1,0:T(8,128)(2,1)S(1)} %constant_dynamic-slice_fusion), channel_id=1, source_target_pairs={{0,16},{2,18},{4,20},{6,22},{8,24},{10,26},{12,28},{14,30},{16,0},... | collective-permute-start | bytes 442376 | tf_op jit(solution)/shard_map/ppermute | solution.py:32
  138.7 1.2 copy.113
  139.9 1.3 add.292
  141.9 1.0 add_convert_fusion
  142.9 4.1 %collective-permute-start.22 = (bf16[3,48,384]{2,1,0:T(8,128)(2,1)S(1)}, bf16[3,48,384]{2,1,0:T(8,128)(2,1)S(1)}, u32[]{:S(2)}, u32[]{:S(2)}) collective-permute-start(bf16[3,48,384]{2,1,0:T(8,128)(2,1)S(1)} %slice_bitcast_fusion.1), channel_id=1, source_target_pairs={{0,0},{1,16},{2,2},{3,18},{4,4},{5,20},{6,6},{7,22},{8,8},{9,24},{... | collective-permute-start | bytes 331784 | tf_op jit(solution)/shard_map/ppermute | solution.py:270
  147.6 3.7 %collective-permute-done.22 = bf16[3,48,384]{2,1,0:T(8,128)(2,1)S(1)} collective-permute-done((bf16[3,48,384]{2,1,0:T(8,128)(2,1)S(1)}, bf16[3,48,384]{2,1,0:T(8,128)(2,1)S(1)}, u32[]{:S(2)}, u32[]{:S(2)}) %collective-permute-start.22) | collective-permute-done | bytes 110624 | tf_op jit(solution)/shard_map/ppermute | solution.py:270
  (222 shorter events, 20.0 us)
Async XLA Ops:
  0.6 43.3 %copy-start = (bf16[768,1536]{1,0:T(8,128)(2,1)S(1)}, bf16[768,1536]{1,0:T(8,128)(2,1)}, u32[]{:S(2)}) copy-start(bf16[768,1536]{1,0:T(8,128)(2,1)} %param.36) | copy-start | bytes 7077892
  0.6 4.4 %copy-start.30 = (bf16[128,16,128]{2,1,0:T(8,128)(2,1)S(1)}, bf16[128,16,128]{2,1,0:T(8,128)(2,1)}, u32[]{:S(2)}) copy-start(bf16[128,16,128]{2,1,0:T(8,128)(2,1)} %param.22) | copy-start | bytes 1572868
  1.9 3.2 %copy-start.38 = (f32[128]{0:T(128)}, f32[128]{0:T(128)S(1)}, u32[]{:S(2)}) copy-start(f32[128]{0:T(128)S(1)} %broadcast_multiply_fusion.8) | copy-start | bytes 1540
  3.0 2.0 %copy-start.43 = (f32[128]{0:T(128)}, f32[128]{0:T(128)S(1)}, u32[]{:S(2)}) copy-start(f32[128]{0:T(128)S(1)} %add_rsqrt_fusion.2) | copy-start | bytes 1540
  5.0 18.8 %collective-permute-start = (bf16[128,768]{1,0:T(8,128)(2,1)}, bf16[128,768]{1,0:T(8,128)(2,1)}, u32[]{:S(2)}, u32[]{:S(2)}) collective-permute-start(bf16[128,768]{1,0:T(8,128)(2,1)} %fusion.27), channel_id=1, source_target_pairs={{0,1},{1,0},{2,3},{3,2},{4,5},{5,4},{6,7},{7,6},{8,9},{9,8},{10,11... | collective-permute-start | bytes 589832 | tf_op jit(solution)/shard_map/ppermute | solution.py:32
  5.5 2.7 %copy-start.45 = (s32[256]{0:T(256)S(1)}, s32[256]{0:T(256)}, u32[]{:S(2)}) copy-start(s32[256]{0:T(256)} %param.25) | copy-start | bytes 3076
  5.6 2.7 %copy-start.46 = (s32[256]{0:T(256)S(1)}, s32[256]{0:T(256)}, u32[]{:S(2)}) copy-start(s32[256]{0:T(256)} %param.24) | copy-start | bytes 3076
  5.7 3.5 %copy-start.22 = (bf16[1,128,768]{2,1,0:T(8,128)(2,1)S(1)}, bf16[1,128,768]{2,1,0:T(8,128)(2,1)}, u32[]{:S(2)}) copy-start(bf16[1,128,768]{2,1,0:T(8,128)(2,1)} %param.39) | copy-start | bytes 589828
  5.7 110.8 %copy-start.33 = (f32[128,16]{0,1:T(8,128)}, f32[128,16]{0,1:T(8,128)S(1)}, u32[]{:S(2)}) copy-start(f32[128,16]{0,1:T(8,128)S(1)} %broadcast_multiply_fusion.2) | copy-start | bytes 24580
  5.9 110.7 %copy-start.36 = (f32[128,16]{0,1:T(8,128)}, f32[128,16]{0,1:T(8,128)S(1)}, u32[]{:S(2)}) copy-start(f32[128,16]{0,1:T(8,128)S(1)} %add_rsqrt_fusion) | copy-start | bytes 24580
  6.2 6.7 %collective-permute-start.1 = (bf16[4,16,128]{2,1,0:T(8,128)(2,1)S(1)}, bf16[4,16,128]{2,1,0:T(8,128)(2,1)S(1)}, u32[]{:S(2)}, u32[]{:S(2)}) collective-permute-start(bf16[4,16,128]{2,1,0:T(8,128)(2,1)S(1)} %bitcast.370), channel_id=1, source_target_pairs={{0,1},{1,0},{2,3},{3,2},{4,5},{5,4},{6,7},{7,6},{8,9},{9,8},{10,11... | collective-permute-start | bytes 49160 | tf_op jit(solution)/shard_map/ppermute | solution.py:32
  9.2 3.5 %copy-start.47 = (f32[6,8]{1,0:T(8,128)S(1)}, f32[6,8]{1,0:T(8,128)}, u32[]{:S(2)}) copy-start(f32[6,8]{1,0:T(8,128)} %param.35) | copy-start | bytes 580
  12.9 20.5 %copy-start.53 = (f32[4,256]{1,0:T(4,128)}, f32[4,256]{1,0:T(4,128)S(1)}, u32[]{:S(2)}) copy-start(f32[4,256]{1,0:T(4,128)S(1)} %fusion.76) | copy-start | bytes 12292
  13.0 4.9 %collective-permute-start.2 = (bf16[1,4,16,256]{3,2,1,0:T(8,128)(2,1)S(1)}, bf16[1,4,16,256]{3,2,1,0:T(8,128)(2,1)S(1)}, u32[]{:S(2)}, u32[]{:S(2)}) collective-permute-start(bf16[1,4,16,256]{3,2,1,0:T(8,128)(2,1)S(1)} %get-tuple-element.70), channel_id=1, source_target_pairs={{0,16},{2,18},{4,20},{6,22},{8,24},{10,26},{12,28},{14,30},{16,0},... | collective-permute-start | bytes 98312 | tf_op jit(solution)/shard_map/ppermute | solution.py:32
  15.6 17.7 %copy-start.52 = (pred[256]{0:T(512)(128)(4,1)}, pred[256]{0:T(512)(128)(4,1)S(1)}, u32[]{:S(2)}) copy-start(pred[256]{0:T(512)(128)(4,1)S(1)} %add_compare_fusion) | copy-start | bytes 772
  15.7 9.1 %copy-start.19 = (bf16[768,768]{1,0:T(8,128)(2,1)S(1)}, bf16[768,768]{1,0:T(8,128)(2,1)}, u32[]{:S(2)}) copy-start(bf16[768,768]{1,0:T(8,128)(2,1)} %param.30) | copy-start | bytes 3538948
  17.9 4.3 %collective-permute-start.3 = (bf16[2,4,16,256]{3,2,1,0:T(8,128)(2,1)S(1)}, bf16[2,4,16,256]{3,2,1,0:T(8,128)(2,1)S(1)}, u32[]{:S(2)}, u32[]{:S(2)}) collective-permute-start(bf16[2,4,16,256]{3,2,1,0:T(8,128)(2,1)S(1)} %maximum_select_fusion.4), channel_id=1, source_target_pairs={{0,8},{2,10},{4,12},{6,14},{8,0},{10,2},{12,4},{14,6},{16,24},{18,... | collective-permute-start | bytes 196616 | tf_op jit(solution)/shard_map/ppermute | solution.py:32
  22.2 5.0 %collective-permute-start.4 = (bf16[4,4,16,256]{3,2,1,0:T(8,128)(2,1)S(1)}, bf16[4,4,16,256]{3,2,1,0:T(8,128)(2,1)S(1)}, u32[]{:S(2)}, u32[]{:S(2)}) collective-permute-start(bf16[4,4,16,256]{3,2,1,0:T(8,128)(2,1)S(1)} %bitcast.349), channel_id=1, source_target_pairs={{0,4},{2,6},{4,0},{6,2},{8,12},{10,14},{12,8},{14,10},{16,20},{18,... | collective-permute-start | bytes 393224 | tf_op jit(solution)/shard_map/ppermute | solution.py:32
  24.9 2.5 %copy-start.14 = (bf16[768,768]{1,0:T(8,128)(2,1)S(1)}, bf16[768,768]{1,0:T(8,128)(2,1)}, u32[]{:S(2)}) copy-start(bf16[768,768]{1,0:T(8,128)(2,1)} %param.31) | copy-start | bytes 3538948
  25.3 8.1 %copy-start.27 = (bf16[384,256]{1,0:T(8,128)(2,1)}, bf16[384,256]{1,0:T(8,128)(2,1)S(1)}, u32[]{:S(2)}) copy-start(bf16[384,256]{1,0:T(8,128)(2,1)S(1)} %convolution_convert_fusion.7) | copy-start | bytes 589828
  25.3 3.2 %copy-start.16 = (bf16[768,768]{1,0:T(8,128)(2,1)S(1)}, bf16[768,768]{1,0:T(8,128)(2,1)}, u32[]{:S(2)}) copy-start(bf16[768,768]{1,0:T(8,128)(2,1)} %param.32) | copy-start | bytes 3538948
  27.3 2.2 %collective-permute-start.5 = (bf16[8,4,16,256]{3,2,1,0:T(8,128)(2,1)S(1)}, bf16[8,4,16,256]{3,2,1,0:T(8,128)(2,1)S(1)}, u32[]{:S(2)}, u32[]{:S(2)}) collective-permute-start(bf16[8,4,16,256]{3,2,1,0:T(8,128)(2,1)S(1)} %bitcast.333), channel_id=1, source_target_pairs={{0,2},{2,0},{4,6},{6,4},{8,10},{10,8},{12,14},{14,12},{16,18},{18,... | collective-permute-start | bytes 786440 | tf_op jit(solution)/shard_map/ppermute | solution.py:32
  33.4 2.8 %copy-start.41 = (f32[4,256]{1,0:T(4,128)}, f32[4,256]{1,0:T(4,128)S(1)}, u32[]{:S(2)}) copy-start(f32[4,256]{1,0:T(4,128)S(1)} %get-tuple-element.77) | copy-start | bytes 12292
  37.2 5.6 %copy-start.6 = (bf16[1,128,768]{2,1,0:T(8,128)(2,1)S(1)}, bf16[1,128,768]{2,1,0:T(8,128)(2,1)}, u32[]{:S(2)}) copy-start(bf16[1,128,768]{2,1,0:T(8,128)(2,1)} %param.20) | copy-start | bytes 589828
  37.2 5.6 %copy-start.10 = (bf16[768,768]{1,0:T(8,128)(2,1)S(1)}, bf16[768,768]{1,0:T(8,128)(2,1)}, u32[]{:S(2)}) copy-start(bf16[768,768]{1,0:T(8,128)(2,1)} %param.33) | copy-start | bytes 3538948
  37.5 5.3 %collective-permute-start.6 = (bf16[384,128]{1,0:T(8,128)(2,1)S(1)}, bf16[384,128]{1,0:T(8,128)(2,1)S(1)}, u32[]{:S(2)}, u32[]{:S(2)}) collective-permute-start(bf16[384,128]{1,0:T(8,128)(2,1)S(1)} %bitcast.364), channel_id=1, source_target_pairs={{0,1},{1,0},{2,3},{3,2},{4,5},{5,4},{6,7},{7,6},{8,9},{9,8},{10,11... | collective-permute-start | bytes 294920 | tf_op jit(solution)/shard_map/ppermute | solution.py:32
  39.1 4.8 %copy-start.40 = (f32[768]{0:T(1024)S(1)}, f32[768]{0:T(1024)}, u32[]{:S(2)}) copy-start(f32[768]{0:T(1024)} %param.29) | copy-start | bytes 9220
  49.6 3.3 %copy-start.3 = (f32[128,768]{1,0:T(8,128)S(1)}, f32[128,768]{1,0:T(8,128)}, u32[]{:S(2)}) copy-start(f32[128,768]{1,0:T(8,128)} %copy-done.2) | copy-start | bytes 1179652
  49.6 3.3 %copy-start.23 = (bf16[1,128,768]{2,1,0:T(8,128)(2,1)S(1)}, bf16[1,128,768]{2,1,0:T(8,128)(2,1)}, u32[]{:S(2)}) copy-start(bf16[1,128,768]{2,1,0:T(8,128)(2,1)} %param.39) | copy-start | bytes 589828
  53.9 6.6 %collective-permute-start.7 = (bf16[128,768]{1,0:T(8,128)(2,1)S(1)}, bf16[128,768]{1,0:T(8,128)(2,1)}, u32[]{:S(2)}, u32[]{:S(2)}) collective-permute-start(bf16[128,768]{1,0:T(8,128)(2,1)S(1)} %get-tuple-element.52), channel_id=1, source_target_pairs={{0,1},{1,0},{2,3},{3,2},{4,5},{5,4},{6,7},{7,6},{8,9},{9,8},{10,11... | collective-permute-start | bytes 589832 | tf_op jit(solution)/shard_map/ppermute | solution.py:32
  55.1 9.2 %copy-start.28 = (bf16[384,256]{1,0:T(8,128)(2,1)S(1)}, bf16[384,256]{1,0:T(8,128)(2,1)}, u32[]{:S(2)}) copy-start(bf16[384,256]{1,0:T(8,128)(2,1)} %copy-done.27) | copy-start | bytes 589828
  55.1 9.2 %copy-start.29 = (bf16[384,256]{1,0:T(8,128)(2,1)S(1)}, bf16[384,256]{1,0:T(8,128)(2,1)}, u32[]{:S(2)}) copy-start(bf16[384,256]{1,0:T(8,128)(2,1)} %convolution_convert_fusion.8) | copy-start | bytes 589828
  61.5 2.8 %copy-start.31 = (bf16[4,128,256]{2,1,0:T(8,128)(2,1)S(1)}, bf16[4,128,256]{2,1,0:T(8,128)(2,1)}, u32[]{:S(2)}) copy-start(bf16[4,128,256]{2,1,0:T(8,128)(2,1)} %get-tuple-element.58) | copy-start | bytes 786436
  71.7 17.3 %collective-permute-start.13 = (bf16[8,4,16,256]{3,2,1,0:T(8,128)(2,1)}, bf16[8,4,16,256]{3,2,1,0:T(8,128)(2,1)}, u32[]{:S(2)}, u32[]{:S(2)}) collective-permute-start(bf16[8,4,16,256]{3,2,1,0:T(8,128)(2,1)} %dynamic-slice_bitcast_fusion.2), channel_id=1, source_target_pairs={{0,2},{2,0},{4,6},{6,4},{8,10},{10,8},{12,14},{14,12},{16,18},{18,... | collective-permute-start | bytes 786440 | tf_op jit(solution)/shard_map/ppermute | solution.py:32
  76.0 7.3 %copy-start.5 = (f32[768,256]{0,1:T(8,128)}, f32[768,256]{0,1:T(8,128)S(1)}, u32[]{:S(2)}) copy-start(f32[768,256]{0,1:T(8,128)S(1)} %convolution_add_fusion) | copy-start | bytes 2359300
  76.1 7.0 %collective-permute-start.8 = (bf16[768,128]{0,1:T(8,128)(2,1)S(1)}, bf16[768,128]{0,1:T(8,128)(2,1)S(1)}, u32[]{:S(2)}, u32[]{:S(2)}) collective-permute-start(bf16[768,128]{0,1:T(8,128)(2,1)S(1)} %fusion.70), channel_id=1, source_target_pairs={{0,1},{1,0},{2,3},{3,2},{4,5},{5,4},{6,7},{7,6},{8,9},{9,8},{10,11... | collective-permute-start | bytes 589832 | tf_op jit(solution)/shard_map/ppermute | solution.py:32
  76.9 6.2 %copy-start.7 = (bf16[1,128,768]{2,1,0:T(8,128)(2,1)S(1)}, bf16[1,128,768]{2,1,0:T(8,128)(2,1)}, u32[]{:S(2)}) copy-start(bf16[1,128,768]{2,1,0:T(8,128)(2,1)} %param.20) | copy-start | bytes 589828
  76.9 6.2 %copy-start.35 = (f32[768]{0:T(1024)S(1)}, f32[768]{0:T(1024)}, u32[]{:S(2)}) copy-start(f32[768]{0:T(1024)} %param.27) | copy-start | bytes 9220
  76.9 6.1 %copy-start.39 = (f32[128]{0:T(128)S(1)}, f32[128]{0:T(128)}, u32[]{:S(2)}) copy-start(f32[128]{0:T(128)} %copy-done.38) | copy-start | bytes 1540
  76.9 6.1 %copy-start.44 = (f32[128]{0:T(128)S(1)}, f32[128]{0:T(128)}, u32[]{:S(2)}) copy-start(f32[128]{0:T(128)} %copy-done.43) | copy-start | bytes 1540
  78.5 32.5 %collective-permute-start.18 = (bf16[8,4,48,384]{3,2,1,0:T(8,128)(2,1)}, bf16[8,4,48,384]{3,2,1,0:T(8,128)(2,1)}, u32[]{:S(2)}, u32[]{:S(2)}) collective-permute-start(bf16[8,4,48,384]{3,2,1,0:T(8,128)(2,1)} %fusion.23), channel_id=1, source_target_pairs={{0,2},{2,0},{4,6},{6,4},{8,10},{10,8},{12,14},{14,12},{16,18},{18,... | collective-permute-start | bytes 3538952 | tf_op jit(solution)/shard_map/ppermute | solution.py:32
  85.8 3.2 %copy-start.12 = (bf16[4,16,16,256]{3,2,0,1:T(8,128)(2,1)S(1)}, bf16[4,16,16,256]{3,2,0,1:T(8,128)(2,1)}, u32[]{:S(2)}) copy-start(bf16[4,16,16,256]{3,2,0,1:T(8,128)(2,1)} %copy-done.11) | copy-start | bytes 1572868
  85.8 4.2 %copy-start.26 = (bf16[768,128]{1,0:T(8,128)(2,1)S(1)}, bf16[768,128]{1,0:T(8,128)(2,1)}, u32[]{:S(2)}) copy-start(bf16[768,128]{1,0:T(8,128)(2,1)} %copy.102) | copy-start | bytes 589828
  86.8 3.2 %collective-permute-start.9 = (bf16[8,48,128]{2,1,0:T(8,128)(2,1)S(1)}, bf16[8,48,128]{2,1,0:T(8,128)(2,1)S(1)}, u32[]{:S(2)}, u32[]{:S(2)}) collective-permute-start(bf16[8,48,128]{2,1,0:T(8,128)(2,1)S(1)} %dynamic-slice_bitcast_fusion.4), channel_id=1, source_target_pairs={{0,2},{2,0},{4,6},{6,4},{8,10},{10,8},{12,14},{14,12},{16,18},{18,... | collective-permute-start | bytes 294920 | tf_op jit(solution)/shard_map/ppermute | solution.py:32
  90.1 4.2 %collective-permute-start.10 = (bf16[4,48,128]{2,1,0:T(8,128)(2,1)S(1)}, bf16[4,48,128]{2,1,0:T(8,128)(2,1)S(1)}, u32[]{:S(2)}, u32[]{:S(2)}) collective-permute-start(bf16[4,48,128]{2,1,0:T(8,128)(2,1)S(1)} %dynamic-slice_bitcast_fusion.6), channel_id=1, source_target_pairs={{0,4},{2,6},{4,0},{6,2},{8,12},{10,14},{12,8},{14,10},{16,20},{18,... | collective-permute-start | bytes 147464 | tf_op jit(solution)/shard_map/ppermute | solution.py:32
  91.7 5.7 %collective-permute-start.14 = (bf16[4,4,16,256]{3,2,1,0:T(8,128)(2,1)S(1)}, bf16[4,4,16,256]{3,2,1,0:T(8,128)(2,1)S(1)}, u32[]{:S(2)}, u32[]{:S(2)}) collective-permute-start(bf16[4,4,16,256]{3,2,1,0:T(8,128)(2,1)S(1)} %dynamic-slice_bitcast_fusion.3), channel_id=1, source_target_pairs={{0,4},{2,6},{4,0},{6,2},{8,12},{10,14},{12,8},{14,10},{16,20},{18,... | collective-permute-start | bytes 393224 | tf_op jit(solution)/shard_map/ppermute | solution.py:32
  97.4 4.3 %collective-permute-start.15 = (bf16[2,4,16,256]{3,2,1,0:T(8,128)(2,1)S(1)}, bf16[2,4,16,256]{3,2,1,0:T(8,128)(2,1)S(1)}, u32[]{:S(2)}, u32[]{:S(2)}) collective-permute-start(bf16[2,4,16,256]{3,2,1,0:T(8,128)(2,1)S(1)} %dynamic-slice_bitcast_fusion.5), channel_id=1, source_target_pairs={{0,8},{2,10},{4,12},{6,14},{8,0},{10,2},{12,4},{14,6},{16,24},{18,... | collective-permute-start | bytes 196616 | tf_op jit(solution)/shard_map/ppermute | solution.py:32
  99.1 5.6 %collective-permute-start.11 = (bf16[2,48,128]{2,1,0:T(8,128)(2,1)S(1)}, bf16[2,48,128]{2,1,0:T(8,128)(2,1)S(1)}, u32[]{:S(2)}, u32[]{:S(2)}) collective-permute-start(bf16[2,48,128]{2,1,0:T(8,128)(2,1)S(1)} %dynamic-slice_bitcast_fusion.7), channel_id=1, source_target_pairs={{0,8},{2,10},{4,12},{6,14},{8,0},{10,2},{12,4},{14,6},{16,24},{18,... | collective-permute-start | bytes 73736 | tf_op jit(solution)/shard_map/ppermute | solution.py:32
  101.8 4.9 %collective-permute-start.16 = (bf16[1,4,16,256]{3,2,1,0:T(8,128)(2,1)S(1)}, bf16[1,4,16,256]{3,2,1,0:T(8,128)(2,1)S(1)}, u32[]{:S(2)}, u32[]{:S(2)}) collective-permute-start(bf16[1,4,16,256]{3,2,1,0:T(8,128)(2,1)S(1)} %constant_dynamic-slice_fusion.1), channel_id=1, source_target_pairs={{0,16},{2,18},{4,20},{6,22},{8,24},{10,26},{12,28},{14,30},{16,0},... | collective-permute-start | bytes 98312 | tf_op jit(solution)/shard_map/ppermute | solution.py:32
  106.8 4.1 %collective-permute-start.17 = (bf16[4,16,128]{2,1,0:T(8,128)(2,1)S(1)}, bf16[4,16,128]{2,1,0:T(8,128)(2,1)S(1)}, u32[]{:S(2)}, u32[]{:S(2)}) collective-permute-start(bf16[4,16,128]{2,1,0:T(8,128)(2,1)S(1)} %bitcast.369), channel_id=1, source_target_pairs={{0,1},{1,0},{2,3},{3,2},{4,5},{5,4},{6,7},{7,6},{8,9},{9,8},{10,11... | collective-permute-start | bytes 49160 | tf_op jit(solution)/shard_map/ppermute | solution.py:32
  108.1 6.6 %collective-permute-start.12 = (bf16[1,48,128]{2,1,0:T(8,128)(2,1)S(1)}, bf16[1,48,128]{2,1,0:T(8,128)(2,1)S(1)}, u32[]{:S(2)}, u32[]{:S(2)}) collective-permute-start(bf16[1,48,128]{2,1,0:T(8,128)(2,1)S(1)} %constant_dynamic-slice_fusion.4), channel_id=1, source_target_pairs={{0,16},{2,18},{4,20},{6,22},{8,24},{10,26},{12,28},{14,30},{16,0},... | collective-permute-start | bytes 36872 | tf_op jit(solution)/shard_map/ppermute | solution.py:32
  112.8 3.7 %copy-start.49 = (bf16[128,8]{0,1:T(8,128)(2,1)S(1)}, bf16[128,8]{0,1:T(8,128)(2,1)}, u32[]{:S(2)}) copy-start(bf16[128,8]{0,1:T(8,128)(2,1)} %param.34) | copy-start | bytes 6148
  112.9 13.6 %collective-permute-start.19 = (bf16[4,4,48,384]{3,2,1,0:T(8,128)(2,1)S(1)}, bf16[4,4,48,384]{3,2,1,0:T(8,128)(2,1)S(1)}, u32[]{:S(2)}, u32[]{:S(2)}) collective-permute-start(bf16[4,4,48,384]{3,2,1,0:T(8,128)(2,1)S(1)} %dynamic-slice_bitcast_fusion), channel_id=1, source_target_pairs={{0,4},{2,6},{4,0},{6,2},{8,12},{10,14},{12,8},{14,10},{16,20},{18,... | collective-permute-start | bytes 1769480 | tf_op jit(solution)/shard_map/ppermute | solution.py:32
  114.6 1.2 collective-permute-start.23
  115.8 8.9 %collective-permute-start.24 = (f32[128,8]{0,1:T(8,128)S(1)}, f32[128,8]{0,1:T(8,128)S(1)}, u32[]{:S(2)}, u32[]{:S(2)}) collective-permute-start(f32[128,8]{0,1:T(8,128)S(1)} %add.288), channel_id=1, source_target_pairs={{0,4},{2,6},{4,0},{6,2},{8,12},{10,14},{12,8},{14,10},{16,20},{18,... | collective-permute-start | bytes 12296 | tf_op jit(solution)/shard_map/ppermute | solution.py:32
  124.7 3.6 %collective-permute-start.25 = (f32[128,8]{0,1:T(8,128)S(1)}, f32[128,8]{0,1:T(8,128)S(1)}, u32[]{:S(2)}, u32[]{:S(2)}) collective-permute-start(f32[128,8]{0,1:T(8,128)S(1)} %add.289), channel_id=1, source_target_pairs={{0,8},{2,10},{4,12},{6,14},{8,0},{10,2},{12,4},{14,6},{16,24},{18,... | collective-permute-start | bytes 12296 | tf_op jit(solution)/shard_map/ppermute | solution.py:32
  126.7 11.7 %copy-start.34 = (f32[128,16]{0,1:T(8,128)S(1)}, f32[128,16]{0,1:T(8,128)}, u32[]{:S(2)}) copy-start(f32[128,16]{0,1:T(8,128)} %copy-done.33) | copy-start | bytes 24580
  126.7 11.7 %copy-start.37 = (f32[128,16]{0,1:T(8,128)S(1)}, f32[128,16]{0,1:T(8,128)}, u32[]{:S(2)}) copy-start(f32[128,16]{0,1:T(8,128)} %copy-done.36) | copy-start | bytes 24580
  126.7 8.4 %collective-permute-start.20 = (bf16[2,4,48,384]{3,2,1,0:T(8,128)(2,1)S(1)}, bf16[2,4,48,384]{3,2,1,0:T(8,128)(2,1)S(1)}, u32[]{:S(2)}, u32[]{:S(2)}) collective-permute-start(bf16[2,4,48,384]{3,2,1,0:T(8,128)(2,1)S(1)} %dynamic-slice_bitcast_fusion.1), channel_id=1, source_target_pairs={{0,8},{2,10},{4,12},{6,14},{8,0},{10,2},{12,4},{14,6},{16,24},{18,... | collective-permute-start | bytes 884744 | tf_op jit(solution)/shard_map/ppermute | solution.py:32
  128.3 4.6 %collective-permute-start.26 = (f32[128,8]{0,1:T(8,128)S(1)}, f32[128,8]{0,1:T(8,128)S(1)}, u32[]{:S(2)}, u32[]{:S(2)}) collective-permute-start(f32[128,8]{0,1:T(8,128)S(1)} %add.290), channel_id=1, source_target_pairs={{0,16},{2,18},{4,20},{6,22},{8,24},{10,26},{12,28},{14,30},{16,0},... | collective-permute-start | bytes 12296 | tf_op jit(solution)/shard_map/ppermute | solution.py:32
  133.5 6.4 %collective-permute-start.27 = (f32[128,8]{0,1:T(8,128)}, f32[128,8]{0,1:T(8,128)}, u32[]{:S(2)}, u32[]{:S(2)}) collective-permute-start(f32[128,8]{0,1:T(8,128)} %add.291), channel_id=1, source_target_pairs={{0,1},{1,0},{2,3},{3,2},{4,5},{5,4},{6,7},{7,6},{8,9},{9,8},{10,11... | collective-permute-start | bytes 12296 | tf_op jit(solution)/shard_map/ppermute | solution.py:32
  135.2 3.1 %copy-start.18 = (bf16[2,4,48,384]{3,2,1,0:T(8,128)(2,1)}, bf16[2,4,48,384]{3,2,1,0:T(8,128)(2,1)S(1)}, u32[]{:S(2)}) copy-start(bf16[2,4,48,384]{3,2,1,0:T(8,128)(2,1)S(1)} %fusion.39) | copy-start | bytes 884740
  135.3 6.6 %collective-permute-start.21 = (bf16[1,4,48,384]{3,2,1,0:T(8,128)(2,1)S(1)}, bf16[1,4,48,384]{3,2,1,0:T(8,128)(2,1)}, u32[]{:S(2)}, u32[]{:S(2)}) collective-permute-start(bf16[1,4,48,384]{3,2,1,0:T(8,128)(2,1)S(1)} %constant_dynamic-slice_fusion), channel_id=1, source_target_pairs={{0,16},{2,18},{4,20},{6,22},{8,24},{10,26},{12,28},{14,30},{16,0},... | collective-permute-start | bytes 442376 | tf_op jit(solution)/shard_map/ppermute | solution.py:32
  142.9 8.4 %collective-permute-start.22 = (bf16[3,48,384]{2,1,0:T(8,128)(2,1)S(1)}, bf16[3,48,384]{2,1,0:T(8,128)(2,1)S(1)}, u32[]{:S(2)}, u32[]{:S(2)}) collective-permute-start(bf16[3,48,384]{2,1,0:T(8,128)(2,1)S(1)} %slice_bitcast_fusion.1), channel_id=1, source_target_pairs={{0,0},{1,16},{2,2},{3,18},{4,4},{5,20},{6,6},{7,22},{8,8},{9,24},{... | collective-permute-start | bytes 331784 | tf_op jit(solution)/shard_map/ppermute | solution.py:270
  (18 other events, 22.1 us)

commit v2 on v1

v2 whole, which is shorter than its diff:
```python
import functools

import jax
import jax.numpy as jnp
from jax import lax
from jax.experimental import pallas as pl
from jax.experimental.pallas import tpu as pltpu
from jax.sharding import PartitionSpec as P

epsilon = 1e-05
f32 = jnp.float32
bf16 = jnp.bfloat16
VMEM, SMEM, ANY = pltpu.VMEM, pltpu.SMEM, pl.ANY
MIB = 1 << 20


def layer_forward(values, scales):
    average = jnp.mean(values, axis=-1, keepdims=True)
    centred = values - average
    inverse = lax.rsqrt(jnp.mean(centred * centred, axis=-1, keepdims=True) + epsilon)
    normed = centred * inverse
    return (normed * scales, normed, inverse)


def layer_backward(upstream, scales, normed, inverse):
    scaled = upstream * scales
    first_moment = jnp.mean(scaled, axis=-1, keepdims=True)
    second_moment = jnp.mean(scaled * normed, axis=-1, keepdims=True)
    return inverse * (scaled - first_moment - normed * second_moment)


NN = ((1,), (0,))
NT = ((1,), (1,))
TN = ((0,), (0,))


def mm(left, right, dims=NN):
    return lax.dot_general(left, right, (dims, ((), ())), preferred_element_type=f32)


def call(body, name, inputs, outs, scratch=(), flops=0, limit=32):
    arrays, specs, moved = [], [], 0
    for item in inputs:
        array, space = item if isinstance(item, tuple) else (item, VMEM)
        arrays.append(array)
        specs.append(pl.BlockSpec(memory_space=space))
        moved += array.size * array.dtype.itemsize
    for shape, kind in outs:
        size = jnp.dtype(kind).itemsize
        for extent in shape:
            size *= extent
        moved += size
    results = pl.pallas_call(
        body,
        name=name,
        out_shape=[jax.ShapeDtypeStruct(shape, kind) for shape, kind in outs],
        in_specs=specs,
        out_specs=[pl.BlockSpec(memory_space=VMEM)] * len(outs),
        scratch_shapes=list(scratch),
        compiler_params=pltpu.CompilerParams(vmem_limit_bytes=limit * MIB),
        cost_estimate=pl.CostEstimate(flops=flops, bytes_accessed=moved, transcendentals=0),
    )(*arrays)
    return results


def low_bits(index, size):
    return jnp.bitwise_and(index, size - 1)


def pair_weight_rows(w_pair, head_count, cols):
    rows = head_count * cols
    shift = cols.bit_length() - 1
    head = lax.shift_right_logical(
        lax.broadcasted_iota(jnp.int32, (rows, head_count), 0), jnp.int32(shift)
    )
    pick = (head == lax.broadcasted_iota(jnp.int32, (rows, head_count), 1)).astype(f32)
    spread = mm(pick.astype(bf16), w_pair, NT)
    row_col = low_bits(lax.broadcasted_iota(jnp.int32, spread.shape, 0), cols)
    return spread, row_col


def enter_kernel(toks, cols, ids, noisy, single, restype, table, gain, pair, pair_gain, w_pair, *rest):
    x_out, bias_outs = rest[0], rest[1 : 1 + toks]
    rounded, bias = rest[1 + toks :]
    t = ids[0]
    rows = noisy.shape[0]
    pair_scaled, _, _ = layer_forward(pair[...].astype(f32), pair_gain[...])
    rounded[...] = pair_scaled.astype(bf16).astype(f32)
    head_count = w_pair.shape[1]
    spread, row_col = pair_weight_rows(w_pair[...], head_count, cols)
    total = jnp.zeros((head_count * cols, rows), f32)
    for j in range(cols):
        column = rounded[pl.ds(j, rows, stride=cols), :].astype(bf16)
        total = total + mm(jnp.where(row_col == j, spread, 0.0).astype(bf16), column, NT)
    bias[...] = total
    part = head_count // toks * cols
    for r in range(toks):
        start = pl.multiple_of(jnp.bitwise_xor(t, r) * part, part)
        bias_outs[r][...] = bias[pl.ds(start, part), :].astype(bf16)

    normed_scaled, _, _ = layer_forward(noisy[...].astype(f32), gain[...])
    types = table.shape[0]
    onehot = (lax.broadcasted_iota(jnp.int32, (types, rows), 0) == restype[...]).astype(f32)
    condition = single[...].astype(f32) + mm(onehot.astype(bf16), table[...], TN)
    x_out[...] = (normed_scaled + condition).astype(bf16)


def own_slice(weight, t, own_width):
    if weight.shape[1] == own_width:
        return weight
    return weight.at[:, pl.ds(pl.multiple_of(t * own_width, own_width), own_width)]


def project_kernel(toks, own_width, ids, *rest):
    parts = rest[:toks]
    weights = rest[toks : toks + 3]
    x_out, outs = rest[toks + 3], rest[toks + 4 : toks + 7]
    held, sem = rest[toks + 7 :]
    t = ids[0]
    copies = []
    for k in range(3):
        copy = pltpu.make_async_copy(
            own_slice(weights[k], t, own_width), held.at[k], sem.at[k]
        )
        copy.start()
        copies.append(copy)
    rows = parts[0].shape[0]
    for r in range(toks):
        start = pl.multiple_of(jnp.bitwise_xor(t, r) * rows, rows)
        x_out[pl.ds(start, rows), :] = parts[r][...]
    x = x_out[...]
    for k in range(3):
        copies[k].wait()
        outs[k][...] = jnp.transpose(mm(x, held[k])).astype(bf16)


def attention_kernel(copies, toks, near, cols, head_width, ids, query, key, value, *rest):
    biases = rest[:near]
    chain, keymask, chain_weight = rest[near : near + 3]
    weights_out, att_out = rest[near + 3 : near + 5]
    pieces = rest[near + 5 : near + 5 + toks]
    bias = rest[near + 5 + toks]
    t, c = ids[0], ids[1]
    far = copies // near
    z, yc = c // near, low_bits(c, near)
    own_heads = weights_out.shape[0]
    tokens = query.shape[1]
    rows = tokens // toks
    for m in range(near):
        for rz in range(far):
            start = (jnp.bitwise_xor(z, rz) * near + jnp.bitwise_xor(yc, m)) * cols
            start = pl.multiple_of(start, cols)
            for rt in range(toks):
                a = jnp.bitwise_xor(t, rt)
                for h in range(own_heads):
                    bias[h, a, pl.ds(start, cols), :] = biases[m][
                        rz * toks + rt, h * cols : (h + 1) * cols, :
                    ]
    chain_row = chain[...]
    keep_row = keymask[...].astype(f32)
    line = lax.broadcasted_iota(jnp.int32, (128, tokens), 0)
    facts = jnp.where(line == 0, chain_row.astype(f32), 0.0) + jnp.where(line == 1, keep_row, 0.0)
    for h in range(own_heads):
        weight_row = jnp.zeros((1, tokens), f32)
        for m in range(chain_weight.shape[0]):
            weight_row = jnp.where(chain_row == m, chain_weight[m, t * own_heads + h], weight_row)
        facts = jnp.where(line == 2 + h, weight_row, facts)
    facts = jnp.transpose(facts)
    same = facts[:, 0:1] == chain_row.astype(f32)
    keep = facts[:, 1:2] > 0.0
    scale = head_width ** (-0.5)
    attended = []
    for h in range(own_heads):
        span = slice(h * head_width, (h + 1) * head_width)
        logits = mm(key[span, :], query[span, :], TN) * scale
        extra = jnp.concatenate([bias[h, a] for a in range(toks)], axis=1).astype(f32)
        logits = logits + (extra + jnp.where(same, facts[:, 2 + h : 3 + h], 0.0))
        logits = jnp.where(keep, logits, -1e30)
        exponent = jnp.exp(logits - jnp.max(logits, axis=0, keepdims=True))
        weights = exponent / jnp.sum(exponent, axis=0, keepdims=True)
        weights_b = weights.astype(bf16)
        weights_out[h] = weights_b
        attended.append(mm(value[span, :], weights_b))
    att_out[...] = jnp.transpose(jnp.concatenate(attended, axis=0)).astype(bf16)
    for r in range(toks):
        start = pl.multiple_of(jnp.bitwise_xor(t, r) * rows, rows)
        pieces[r][...] = att_out[pl.ds(start, rows), :]


def down_kernel(upstream, w_down, d_hidden):
    d_hidden[...] = mm(upstream[...], w_down[...], NT)


def hidden_kernel(toks, chunk, ids, noisy, upstream, d_hidden, gain, *rest):
    parts = rest[:toks]
    w_out, w_gate, w_up = rest[toks : toks + 3]
    d_res_out, d_res_b_out = rest[toks + 3 : toks + 5]
    held_out, held_gate, held_up, sem = rest[toks + 5 :]
    t = ids[0]
    hidden = w_gate.shape[1]
    first = pltpu.make_async_copy(w_out, held_out, sem.at[0])
    first.start()
    copies = []
    for k in range(hidden // chunk):
        span = pl.ds(k * chunk, chunk)
        pair = [
            pltpu.make_async_copy(w.at[:, span], held.at[:, span], sem.at[1 + 2 * k + n])
            for n, (w, held) in enumerate(((w_gate, held_gate), (w_up, held_up)))
        ]
        for copy in pair:
            copy.start()
        copies.append(pair)
    residual = noisy[...].astype(f32)
    first.wait()
    own_width = parts[0].shape[1]
    for r in range(toks):
        start = pl.multiple_of(jnp.bitwise_xor(t, r) * own_width, own_width)
        residual = residual + mm(parts[r][...], held_out[pl.ds(start, own_width), :])
    trans_scaled, trans_hat, trans_inverse = layer_forward(residual, gain[...])
    trans_in = trans_scaled.astype(bf16)
    d_trans = jnp.zeros(residual.shape, f32)
    for k in range(hidden // chunk):
        for copy in copies[k]:
            copy.wait()
        span = slice(k * chunk, (k + 1) * chunk)
        gate = mm(trans_in, held_gate[:, span])
        up = mm(trans_in, held_up[:, span])
        incoming = d_hidden[:, span]
        sigmoid = jax.nn.sigmoid(gate)
        d_up = (incoming * gate * sigmoid).astype(bf16)
        d_gate = (incoming * up * sigmoid * (1.0 + gate * (1.0 - sigmoid))).astype(bf16)
        d_trans = d_trans + mm(d_gate, held_gate[:, span], NT) + mm(d_up, held_up[:, span], NT)
    d_res = upstream[...].astype(f32) + layer_backward(
        d_trans, gain[...], trans_hat, trans_inverse
    )
    d_res_out[...] = d_res
    d_res_b_out[...] = d_res.astype(bf16)


def backward_kernel(copies, toks, near, cols, head_width, ids, query, key, value, weights, *rest):
    parts = rest[:toks]
    w_out = rest[toks]
    d_res_out, d_query, d_key, d_value = rest[toks + 1 : toks + 5]
    d_bias = rest[toks + 5 : toks + 5 + near]
    d_logits, held, sem = rest[toks + 5 + near :]
    t, c = ids[0], ids[1]
    far = copies // near
    yc = low_bits(c, near)
    own_width, tokens = query.shape
    rows = tokens // toks
    start = pl.multiple_of(t * own_width, own_width)
    copy = pltpu.make_async_copy(w_out.at[pl.ds(start, own_width), :], held, sem.at[0])
    copy.start()
    for r in range(toks):
        start = pl.multiple_of(jnp.bitwise_xor(t, r) * rows, rows)
        d_res_out[pl.ds(start, rows), :] = parts[r][...]
    copy.wait()
    d_att = mm(held[...], d_res_out[...], NT).astype(bf16)
    scale = head_width ** (-0.5)
    for h in range(weights.shape[0]):
        span = slice(h * head_width, (h + 1) * head_width)
        d_att_h = d_att[span, :]
        weights_b = weights[h]
        d_weights = mm(value[span, :], d_att_h, TN)
        weights_f = weights_b.astype(f32)
        delta = jnp.sum(weights_f * d_weights, axis=0, keepdims=True)
        d_logits_b = (weights_f * (d_weights - delta)).astype(bf16)
        d_logits[h] = d_logits_b
        d_query[span, :] = (mm(key[span, :], d_logits_b) * scale).astype(bf16)
        d_key[span, :] = (mm(query[span, :], d_logits_b, NT) * scale).astype(bf16)
        d_value[span, :] = mm(d_att_h, weights_b, NT).astype(bf16)
    for m in range(near):
        for z in range(far):
            start = pl.multiple_of((z * near + jnp.bitwise_xor(yc, m)) * cols, cols)
            for h in range(weights.shape[0]):
                d_bias[m][z, h * cols : (h + 1) * cols, :] = d_logits[h, pl.ds(start, cols), :]


def gradient_kernel(copies, toks, ids, x, att, d_res, d_query, d_key, d_value, *rest):
    weights = rest[:3]
    kept, sent, d_own = rest[3:6]
    d_others = rest[6 : 5 + toks]
    wide, narrow, d_inputs, held, sem = rest[5 + toks :]
    t, c = ids[0], ids[1]
    own_width, tokens = d_query.shape
    rows = tokens // toks
    width = x.shape[1]
    group = copies // toks
    transfers = []
    for k in range(3):
        copy = pltpu.make_async_copy(
            own_slice(weights[k], t, own_width), held.at[k], sem.at[k]
        )
        copy.start()
        transfers.append(copy)
    for k, part in enumerate((d_query, d_key, d_value)):
        wide[k] = mm(part[...], x[...])
    narrow[...] = mm(d_res[...], att[...], TN)
    cut, depth = width // copies, width // toks
    near = low_bits(c, 2)
    for side, out in ((near, kept), (1 - near, sent)):
        for q in range(copies // 2):
            h = 2 * q // group
            first = pl.multiple_of((2 * q - h * group + side) * cut, 8)
            for k in range(3):
                out[q, k] = wide[k, pl.ds(first, cut), h * depth : (h + 1) * depth].astype(bf16)
            first = pl.multiple_of((2 * q + side) * cut, 8)
            out[q, 3] = narrow[pl.ds(first, cut), :].astype(bf16)
    total = None
    for k, part in enumerate((d_query, d_key, d_value)):
        transfers[k].wait()
        term = mm(held[k], part[...])
        total = term if total is None else total + term
    for a in range(toks):
        d_inputs[a] = total[:, a * rows : (a + 1) * rows]
    d_own[...] = d_inputs[t]
    for r in range(1, toks):
        d_others[r - 1][...] = d_inputs[jnp.bitwise_xor(t, r)].astype(bf16)


def halve_kernel(divide, ids, kept, got, kept_out, sent_out):
    bit = low_bits(ids[1] // divide, 2)
    for q in range(kept_out.shape[0]):
        for side, out in ((bit, kept_out), (1 - bit, sent_out)):
            out[q] = (kept[2 * q + side].astype(f32) + got[2 * q + side].astype(f32)).astype(bf16)


def spread_kernel(near, ids, kept, got, *outs):
    z = ids[1] // near
    for r, out in enumerate(outs):
        k = jnp.bitwise_xor(z, r)
        out[...] = (kept[k].astype(f32) + got[k].astype(f32)).astype(bf16)


def collect_kernel(count, *refs):
    parts, (moved, final, flat) = refs[:count], refs[count:]
    for k in range(4):
        total = parts[0][k].astype(f32)
        for part in parts[1:]:
            total = total + part[k].astype(f32)
        if k < 3:
            moved[k] = total.astype(bf16)
        else:
            flat[...] = jnp.zeros(flat.shape, f32)
            flat[: total.shape[0], : total.shape[1]] = total
            final[...] = jnp.transpose(flat[...])[: total.shape[1], : total.shape[0]]


def finish_kernel(moved, kept_single, got_single, first, second, third, single, flat):
    cut = moved.shape[1]
    flat[...] = jnp.zeros(flat.shape, f32)
    for k, out in enumerate((first, second, third)):
        flat[:cut, : moved.shape[2]] = moved[k].astype(f32)
        out[...] = jnp.transpose(flat[...])[: moved.shape[2], :cut]
    rows = single.shape[0]
    flat[:cut, :rows] = kept_single[...].astype(f32) + got_single[...].astype(f32)
    single[...] = jnp.transpose(flat[...])[:rows, :cut]


def exit_kernel(copies, toks, ids, noisy, gain, d_res, d_own, *rest):
    others = rest[: toks - 1]
    grad_noisy, kept, sent, total_ref = rest[toks - 1 :]
    total = d_own[...]
    for part in others:
        total = total + part[...].astype(f32)
    total_ref[...] = total
    _, noisy_hat, noisy_inverse = layer_forward(noisy[...].astype(f32), gain[...])
    grad_noisy[...] = (
        d_res[...] + layer_backward(jnp.transpose(total), gain[...], noisy_hat, noisy_inverse)
    ).astype(bf16)
    cut = total.shape[0] // copies
    bit = low_bits(ids[1] // 2, 2)
    for q in range(copies // 4):
        for low in range(2):
            for side, out in ((bit, kept), (1 - bit, sent)):
                start = pl.multiple_of((q * 4 + side * 2 + low) * cut, 8)
                out[q, low] = total_ref[pl.ds(start, cut), :].astype(bf16)


def single_spread_kernel(near, ids, kept, got, *outs):
    z = ids[1] // near
    for r, out in enumerate(outs):
        k = jnp.bitwise_xor(z, r)
        out[...] = (kept[k].astype(f32) + got[k].astype(f32)).astype(bf16)


def single_collect_kernel(count, ids, *refs):
    parts, (kept, sent) = refs[:count], refs[count:]
    bit = low_bits(ids[1], 2)
    for side, out in ((bit, kept), (1 - bit, sent)):
        total = parts[0][side].astype(f32)
        for part in parts[1:]:
            total = total + part[side].astype(f32)
        out[...] = total.astype(bf16)


def bias_sum_kernel(near, toks, ids, *refs):
    parts, outs, total = refs[:near], refs[near:-1], refs[-1]
    t, z = ids[0], ids[1] // near
    rows = outs[0].shape[1]
    for k in range(parts[0].shape[0]):
        whole = parts[0][k].astype(f32)
        for part in parts[1:]:
            whole = whole + part[k].astype(f32)
        for a in range(toks):
            total[k, a] = whole[:, a * rows : (a + 1) * rows].astype(bf16)
    for n, out in enumerate(outs):
        rz, rt = n // toks, n % toks
        out[...] = total[jnp.bitwise_xor(z, rz), jnp.bitwise_xor(t, rt)]


def pair_kernel(toks, cols, count, ids, pair, gain, w_pair, *refs):
    parts = refs[:count]
    grad_pair, weight_grad, rounded, grads, spread_out = refs[count:]
    t = ids[0]
    head_count = w_pair.shape[1]
    part_rows = parts[0].shape[0]
    rows = parts[0].shape[1]
    for rt in range(toks):
        total = parts[rt][...].astype(f32)
        for rz in range(1, count // toks):
            total = total + parts[rz * toks + rt][...].astype(f32)
        start = pl.multiple_of(jnp.bitwise_xor(t, rt) * part_rows, part_rows)
        grads[pl.ds(start, part_rows), :] = total
    pair_scaled, pair_hat, pair_inverse = layer_forward(pair[...].astype(f32), gain[...])
    rounded[...] = pair_scaled.astype(bf16).astype(f32)
    spread, row_col = pair_weight_rows(w_pair[...], head_count, cols)
    grad = grads[...]
    grad_b = grad.astype(bf16)
    turned = jnp.transpose(grad).astype(bf16)
    sums = jnp.zeros(spread.shape, f32)
    for j in range(cols):
        here = row_col == j
        column = rounded[pl.ds(j, rows, stride=cols), :].astype(bf16)
        sums = sums + jnp.where(here, mm(grad_b, column), 0.0)
        spread_out[pl.ds(j, rows, stride=cols), :] = mm(
            turned, jnp.where(here, spread, 0.0).astype(bf16)
        )
    grad_pair[...] = layer_backward(
        spread_out[...], gain[...], pair_hat, pair_inverse
    ).astype(bf16)
    for h in range(head_count):
        weight_grad[h : h + 1, :] = jnp.sum(
            sums[h * cols : (h + 1) * cols, :], axis=0, keepdims=True
        )


def xor_tree(parts):
    while len(parts) > 1:
        parts = [parts[k] + parts[k + 1] for k in range(0, len(parts), 2)]
    return parts[0]


def swap_copy(value, mask):
    size = lax.axis_size("copy")
    return lax.ppermute(value, "copy", [(i, i ^ mask) for i in range(size)])


def swap_tok(value, mask):
    size = lax.axis_size("tok")
    return lax.ppermute(value, "tok", [(i, i ^ mask) for i in range(size)])


def swap_both(value, mask_copy, mask_tok):
    size, toks = lax.axis_size("copy"), lax.axis_size("tok")
    pairs = [
        (c * toks + t, (c ^ mask_copy) * toks + (t ^ mask_tok))
        for c in range(size)
        for t in range(toks)
    ]
    return lax.ppermute(value, ("copy", "tok"), pairs)


def per_device(
    noisy,
    single,
    pair,
    restype,
    chain,
    keymask,
    restype_table,
    norm_gain,
    pair_gain,
    trans_gain,
    w_query,
    w_key,
    w_value,
    w_out,
    w_pair,
    chain_weight,
    w_hidden_gate,
    w_hidden_up,
    w_down,
    cotangent,
):
    copies = lax.axis_size("copy")
    toks = lax.axis_size("tok")
    _, rows, width = noisy.shape
    cols = pair.shape[1]
    channels = pair.shape[2]
    heads = w_pair.shape[1]
    head_width = width // heads
    own_heads = heads // toks
    own_width = own_heads * head_width
    tokens = rows * toks
    hidden = w_down.shape[0]
    near = 4
    far = copies // near
    cut = width // copies
    ids = jnp.stack([lax.axis_index("tok"), lax.axis_index("copy")]).astype(jnp.int32)
    where_am_i = (ids, SMEM)
    noisy2 = noisy.reshape(rows, width)
    upstream = cotangent.reshape(rows, width)
    pair2 = pair.reshape(rows * cols, channels)
    norm_gain2 = norm_gain.reshape(1, width)
    trans_gain2 = trans_gain.reshape(1, width)
    pair_gain2 = pair_gain.reshape(1, channels)

    entered = call(
        functools.partial(enter_kernel, toks, cols),
        "enter",
        [where_am_i, noisy2, single, restype.reshape(1, rows), restype_table, norm_gain2]
        + [pair2, pair_gain2, w_pair],
        [((rows, width), bf16)] + [((own_heads * cols, rows), bf16)] * toks,
        [VMEM((rows * cols, channels), f32), VMEM((heads * cols, rows), f32)],
        flops=2 * heads * cols * rows * channels * cols,
    )
    x_own, bias_parts = entered[0], entered[1:]
    first = []
    for rz in range(far):
        for rt in range(toks):
            part = bias_parts[rt]
            first.append(part if rz + rt == 0 else swap_both(part, rz * near, rt))
    x_parts = [x_own] + [swap_tok(x_own, r) for r in range(1, toks)]
    bias_first = jnp.stack(first)
    biases = [bias_first] + [swap_copy(bias_first, m) for m in range(1, near)]

    weights3 = [w_query, w_key, w_value]
    if own_width % 128:
        weights3 = [
            lax.dynamic_slice_in_dim(w, ids[0] * own_width, own_width, axis=1) for w in weights3
        ]
    weights3 = [(w, ANY) for w in weights3]
    x, query, key, value = call(
        functools.partial(project_kernel, toks, own_width),
        "project",
        [where_am_i] + x_parts + weights3,
        [((tokens, width), bf16)] + [((own_width, tokens), bf16)] * 3,
        [VMEM((3, width, own_width), bf16), pltpu.SemaphoreType.DMA((3,))],
        flops=6 * tokens * width * own_width,
    )
    done = call(
        functools.partial(attention_kernel, copies, toks, near, cols, head_width),
        "attention",
        [where_am_i, query, key, value]
        + biases
        + [chain.reshape(1, tokens), keymask.reshape(1, tokens), (chain_weight, SMEM)],
        [((own_heads, tokens, tokens), bf16), ((tokens, own_width), bf16)]
        + [((rows, own_width), bf16)] * toks,
        [VMEM((own_heads, toks, tokens, rows), bf16)],
        flops=4 * tokens * tokens * own_width,
    )
    weights, att, pieces = done[0], done[1], done[2:]
    att_parts = [pieces[0]] + [swap_tok(pieces[r], r) for r in range(1, toks)]

    (d_hidden,) = call(
        down_kernel,
        "down",
        [upstream, w_down],
        [((rows, hidden), f32)],
        flops=2 * rows * hidden * width,
    )
    chunk = hidden // 3
    d_res, d_res_b = call(
        functools.partial(hidden_kernel, toks, chunk),
        "hidden",
        [where_am_i, noisy2, upstream, d_hidden, trans_gain2]
        + att_parts
        + [(w_out, ANY), (w_hidden_gate, ANY), (w_hidden_up, ANY)],
        [((rows, width), f32), ((rows, width), bf16)],
        [
            VMEM((width, width), bf16),
            VMEM((width, hidden), bf16),
            VMEM((width, hidden), bf16),
            pltpu.SemaphoreType.DMA((7,)),
        ],
        flops=2 * rows * width * (width + 4 * hidden),
    )
    d_res_parts = [d_res_b] + [swap_tok(d_res_b, r) for r in range(1, toks)]

    back = call(
        functools.partial(backward_kernel, copies, toks, near, cols, head_width),
        "backward",
        [where_am_i, query, key, value, weights] + d_res_parts + [(w_out, ANY)],
        [((tokens, width), bf16)]
        + [((own_width, tokens), bf16)] * 3
        + [((far, own_heads * cols, tokens), bf16)] * near,
        [
            VMEM((own_heads, tokens, tokens), bf16),
            VMEM((own_width, width), bf16),
            pltpu.SemaphoreType.DMA((1,)),
        ],
        flops=8 * tokens * tokens * own_width + 2 * tokens * width * own_width,
    )
    d_res_all, d_query, d_key, d_value = back[:4]
    d_bias = [back[4]] + [swap_copy(back[4 + m], m) for m in range(1, near)]

    found = call(
        functools.partial(gradient_kernel, copies, toks),
        "gradient",
        [where_am_i, x, att, d_res_all, d_query, d_key, d_value] + weights3,
        [((copies // 2, 4, cut, own_width), bf16)] * 2
        + [((width, rows), f32)]
        + [((width, rows), bf16)] * (toks - 1),
        [
            VMEM((3, own_width, width), f32),
            VMEM((width, own_width), f32),
            VMEM((toks, width, rows), f32),
            VMEM((3, width, own_width), bf16),
            pltpu.SemaphoreType.DMA((3,)),
        ],
        flops=14 * tokens * width * own_width,
    )
    kept, sent, d_own = found[:3]
    d_others = [swap_tok(found[2 + r], r) for r in range(1, toks)]
    got = swap_copy(sent, 1)

    bias_out = call(
        functools.partial(bias_sum_kernel, near, toks),
        "bias_sum",
        [where_am_i] + d_bias,
        [((own_heads * cols, rows), bf16)] * (far * toks),
        [VMEM((far, toks, own_heads * cols, rows), bf16)],
    )
    bias_in = []
    for rz in range(far):
        for rt in range(toks):
            part = bias_out[rz * toks + rt]
            bias_in.append(part if rz + rt == 0 else swap_both(part, rz * near, rt))

    kept2, sent2 = call(
        functools.partial(halve_kernel, 2),
        "halve",
        [where_am_i, kept, got],
        [((copies // 4, 4, cut, own_width), bf16)] * 2,
    )
    got2 = swap_copy(sent2, 2)
    grad_noisy, kept_s, sent_s = call(
        functools.partial(exit_kernel, copies, toks),
        "exit",
        [where_am_i, noisy2, norm_gain2, d_res, d_own] + d_others,
        [((rows, width), bf16)] + [((far, 2, cut, rows), bf16)] * 2,
        [VMEM((width, rows), f32)],
    )
    got_s = swap_copy(sent_s, 2)
    grad_pair, weight_grad = call(
        functools.partial(pair_kernel, toks, cols, far * toks),
        "pair",
        [where_am_i, pair2, pair_gain2, w_pair] + bias_in,
        [((rows * cols, channels), bf16), ((heads, channels), f32)],
        [
            VMEM((rows * cols, channels), f32),
            VMEM((heads * cols, rows), f32),
            VMEM((rows * cols, channels), f32),
        ],
        flops=4 * heads * cols * rows * channels * cols,
    )
    terms = []
    for rz in range(far):
        for rt in range(toks):
            terms.append(
                weight_grad if rz + rt == 0 else swap_both(weight_grad, rz * near, rt)
            )
    far_sum = xor_tree(terms)

    spread = call(
        functools.partial(spread_kernel, near),
        "spread",
        [where_am_i, kept2, got2],
        [((4, cut, own_width), bf16)] * far,
    )
    arrived = [spread[0]] + [swap_copy(spread[r], r * near) for r in range(1, far)]
    spread_s = call(
        functools.partial(single_spread_kernel, near),
        "single_spread",
        [where_am_i, kept_s, got_s],
        [((2, cut, rows), bf16)] * far,
    )
    arrived_s = [spread_s[0]] + [swap_copy(spread_s[r], r * near) for r in range(1, far)]
    whole_sum = xor_tree([far_sum] + [swap_copy(far_sum, m) for m in range(1, near)])

    moved, grad_out = call(
        functools.partial(collect_kernel, far),
        "collect",
        arrived,
        [((3, cut, own_width), bf16), ((own_width, cut), f32)],
        [VMEM((128, max(own_width, 128)), f32)],
    )
    last_kept, last_sent = call(
        functools.partial(single_collect_kernel, far),
        "single_collect",
        [where_am_i] + arrived_s,
        [((cut, rows), bf16)] * 2,
    )
    last_got = swap_copy(last_sent, 1)
    group = copies // toks
    pairs = []
    for c in range(copies):
        for t in range(toks):
            pairs.append((c * toks + t, (t * group + c % group) * toks + c // group))
    moved = lax.ppermute(moved, ("copy", "tok"), pairs)
    grad_query, grad_key, grad_value, grad_single = call(
        finish_kernel,
        "finish",
        [moved, last_kept, last_got],
        [((own_width, cut), f32)] * 3 + [((rows, cut), f32)],
        [VMEM((128, max(own_width, rows, 128)), f32)],
    )
    return (
        grad_noisy[None],
        grad_single,
        grad_pair.reshape(rows, cols, channels),
        grad_query,
        grad_key,
        grad_value,
        grad_out,
        whole_sum.T,
    )


def solution(mesh):
    placed = (
        P("copy", "tok", None),
        P("tok", None),
        P("tok", "copy", None),
        P("tok"),
    ) + (P(),) * 15 + (P("copy", "tok", None),)
    return jax.shard_map(
        per_device,
        mesh=mesh,
        in_specs=placed,
        out_specs=(
            P("copy", "tok", None),
            P("tok", "copy"),
            P("tok", "copy", None),
            P("tok", "copy"),
            P("tok", "copy"),
            P("tok", "copy"),
            P("tok", "copy"),
            P(),
        ),
        check_vma=False,
    )
```

time: 154 us -> 150 us (0.974)
  matrix products: 35.6 us -> 0 us
  Pallas kernels: 0 us -> 27.6 us
  starting transfers between devices: 34.6 us -> 59.1 us
  other arithmetic: 20.5 us -> 0.68 us
  local copies, waits for them, and re-layouts: 14.1 us -> 15.7 us
    dot_general x27 -> x0, matrix products: 32.8 us -> none  [the longest x18 23.6 us: mm(): lax.dot_general(left, right, (dims, ((), ())), preferred_element_type=f32)]
    pallas_call x0 -> x16, Pallas kernels: none -> 27.6 us  [call(): pl.pallas_call(body, name=name, out_shape=[jax.ShapeDtypeStruct(shape, ki...]
    ppermute x28 -> x45, starting transfers between devices: 34.6 us -> 59.1 us  [the longest x21 32.3 us: swap_both(): return lax.ppermute(value, ('copy', 'tok'), pairs)]
    convert_element_type x19 -> x0, other arithmetic: 9.8 us -> none  [the longest x11 4.86 us: scatter_copy(): parts = (kept.astype(f32) + got.astype(f32)).astype(bf16)]
    unnamed x113 -> x63, local copies, waits for them, and re-layouts: 6.09 us -> 14.9 us
    reduce_sum x6 -> x0, other arithmetic: 2.95 us -> none  [the longest x3 1.46 us: layer_forward(): jnp.mean(centred * centred, axis=-1, keepdims=True) + epsilon]
    sub x1 -> x0, matrix products: 2.84 us -> none  [per_device(): exponent = jnp.exp(logits - highest)]
    squeeze x11 -> x0, local copies, waits for them, and re-layouts: 2.59 us -> none  [scatter_copy(): sent = lax.dynamic_index_in_dim(pairs, 1 - bit, 1, keepdims=False)]
  transfers between devices with their start and end apart: 28 -> 45, of which waited for: 17 -> 19; matrix products, arithmetic and copies ran while one was open for 21% -> 1% of each run, Pallas kernels for 0% -> 7%
where the time goes in v2:
time: 150 us; the launch traced here: 149 us
  starting transfers between devices  59.1 us (39%)
  waiting for transfers between devices  44.5 us (30%)
  Pallas kernels  27.6 us (18%)
  local copies, waits for them, and re-layouts  15.7 us (10%)
    ppermute x21, starting transfers between devices, swap_both(): return lax.ppermute(value, ('copy', 'tok'), pairs)  32.3 us
    pallas_call x16, Pallas kernels, call(): pl.pallas_call(body, name=name, out_shape=[jax.ShapeDtypeStruct(shape, ki...  27.6 us
    ppermute x19, waiting for transfers between devices, swap_copy(): return lax.ppermute(value, 'copy', [(i, i ^ mask) for i in range(size)])  17.5 us
    ppermute x19, starting transfers between devices, swap_copy(): return lax.ppermute(value, 'copy', [(i, i ^ mask) for i in range(size)])  15.8 us
    unnamed x63, local copies, waits for them, and re-layouts  14.9 us
    ppermute x21, waiting for transfers between devices, swap_both(): return lax.ppermute(value, ('copy', 'tok'), pairs)  11.8 us
    ppermute x4, waiting for transfers between devices, swap_tok(): return lax.ppermute(value, 'tok', [(i, i ^ mask) for i in range(size)])  11 us
    ppermute x4, starting transfers between devices, swap_tok(): return lax.ppermute(value, 'tok', [(i, i ^ mask) for i in range(size)])  6.03 us
  transfers between devices with their start and end apart: 45, of which 19 were waited for; matrix products, arithmetic and copies ran while one was open for 1% of the time, Pallas kernels for 7%

profile of v2, /device:TPU:2, one launch (start us, length us, event | category | flops | bytes accessed | tf_op | source)
XLA Modules:
  0.0 148.6 jit_solution(15455795678962140757)
XLA Ops:
  0.6 0.8 reshape.47.gain
  1.4 0.8 copy.28.w_pair
  2.3 1.0 copy-done.9
  3.4 0.9 copy-done.11
  4.3 0.9 copy-done.16
  5.2 0.8 copy-done.17
  7.3 1.8 %enter.1 = (bf16[128,768]{1,0:T(8,128)(2,1)S(1)}, bf16[64,128]{1,0:T(8,128)(2,1)S(1)}, bf16[64,128]{1,0:T(8,128)(2,1)S(1)}) custom-call(s32[2]{0:T(128)S(1)} %pad_add_fusion.ids, bf16[128,768]{1,0:T(8,128)(2,1)S(1)} %bitcast.31, bf16[128,768]{1,0:T(8,128)(2,1)S(1)} %copy-done.16, s32[1,128]{1,0:T(1,128)S(1)} %bitcast.40, bf16[32,768]{1,0:T(8,128)(2,1)S(1)} %copy-done.17, ...), custom_call_target="tpu_custom_call" | custom-call | flops 67108864 | bytes 1202184 | tf_op jit(solution)/shard_map/enter/pallas_call | solution.py:53
  9.2 3.7 %collective-permute-start.6 = (bf16[64,128]{1,0:T(8,128)(2,1)S(1)}, bf16[64,128]{1,0:T(8,128)(2,1)S(1)}, u32[]{:S(2)}, u32[]{:S(2)}) collective-permute-start(bf16[64,128]{1,0:T(8,128)(2,1)S(1)} %get-tuple-element.68), channel_id=1, source_target_pairs={{0,24},{1,25},{2,26},{3,27},{4,28},{5,29},{6,30},{7,31},{8,16},{9,... | collective-permute-start | bytes 49160 | tf_op jit(solution)/shard_map/ppermute | solution.py:471
  12.8 0.8 collective-permute-start.2
  13.6 3.6 %collective-permute-start.7 = (bf16[64,128]{1,0:T(8,128)(2,1)S(1)}, bf16[64,128]{1,0:T(8,128)(2,1)S(1)}, u32[]{:S(2)}, u32[]{:S(2)}) collective-permute-start(bf16[64,128]{1,0:T(8,128)(2,1)S(1)} %get-tuple-element.69), channel_id=1, source_target_pairs={{0,25},{1,24},{2,27},{3,26},{4,29},{5,28},{6,31},{7,30},{8,17},{9,... | collective-permute-start | bytes 49160 | tf_op jit(solution)/shard_map/ppermute | solution.py:471
  17.2 1.5 %collective-permute-start.1 = (bf16[64,128]{1,0:T(8,128)(2,1)S(1)}, bf16[64,128]{1,0:T(8,128)(2,1)S(1)}, u32[]{:S(2)}, u32[]{:S(2)}) collective-permute-start(bf16[64,128]{1,0:T(8,128)(2,1)S(1)} %get-tuple-element.69), channel_id=1, source_target_pairs={{0,1},{1,0},{2,3},{3,2},{4,5},{5,4},{6,7},{7,6},{8,9},{9,8},{10,11... | collective-permute-start | bytes 49160 | tf_op jit(solution)/shard_map/ppermute | solution.py:471
  18.7 2.2 %collective-permute-done.1 = bf16[64,128]{1,0:T(8,128)(2,1)S(1)} collective-permute-done((bf16[64,128]{1,0:T(8,128)(2,1)S(1)}, bf16[64,128]{1,0:T(8,128)(2,1)S(1)}, u32[]{:S(2)}, u32[]{:S(2)}) %collective-permute-start.1) | collective-permute-done | bytes 16416 | tf_op jit(solution)/shard_map/ppermute | solution.py:471
  21.0 1.5 %collective-permute-start.3 = (bf16[64,128]{1,0:T(8,128)(2,1)S(1)}, bf16[64,128]{1,0:T(8,128)(2,1)S(1)}, u32[]{:S(2)}, u32[]{:S(2)}) collective-permute-start(bf16[64,128]{1,0:T(8,128)(2,1)S(1)} %get-tuple-element.69), channel_id=1, source_target_pairs={{0,9},{1,8},{2,11},{3,10},{4,13},{5,12},{6,15},{7,14},{8,1},{9,0},... | collective-permute-start | bytes 49160 | tf_op jit(solution)/shard_map/ppermute | solution.py:471
  22.5 3.3 %collective-permute-done.3 = bf16[64,128]{1,0:T(8,128)(2,1)S(1)} collective-permute-done((bf16[64,128]{1,0:T(8,128)(2,1)S(1)}, bf16[64,128]{1,0:T(8,128)(2,1)S(1)}, u32[]{:S(2)}, u32[]{:S(2)}) %collective-permute-start.3) | collective-permute-done | bytes 16416 | tf_op jit(solution)/shard_map/ppermute | solution.py:471
  25.8 1.5 collective-permute-start
  27.4 1.6 %collective-permute-start.9 = (bf16[8,64,128]{2,1,0:T(8,128)(2,1)S(1)}, bf16[8,64,128]{2,1,0:T(8,128)(2,1)S(1)}, u32[]{:S(2)}, u32[]{:S(2)}) collective-permute-start(bf16[8,64,128]{2,1,0:T(8,128)(2,1)S(1)} %constant_dynamic-update-slice_fusion.rest_0_), channel_id=1, source_target_pairs={{0,4},{2,6},{4,0},{6,2},{8,12},{10,14},{12,8},{14,10},{16,20},{18,... | collective-permute-start | bytes 393224 | tf_op jit(solution)/shard_map/ppermute | solution.py:456
  29.3 2.1 %collective-permute-done.rest_1_ = bf16[128,768]{1,0:T(8,128)(2,1)S(1)} collective-permute-done((bf16[128,768]{1,0:T(8,128)(2,1)S(1)}, bf16[128,768]{1,0:T(8,128)(2,1)S(1)}, u32[]{:S(2)}, u32[]{:S(2)}) %collective-permute-start) | collective-permute-done | bytes 196640 | tf_op jit(solution)/shard_map/ppermute | solution.py:461
  31.4 1.3 copy-done.2
  32.7 1.3 copy-done.4
  34.0 2.1 %project.1 = (bf16[256,768]{1,0:T(8,128)(2,1)S(1)}, bf16[384,256]{1,0:T(8,128)(2,1)S(1)}, bf16[384,256]{1,0:T(8,128)(2,1)S(1)}, bf16[384,256]{1,0:T(8,128)(2,1)S(1)}) custom-call(s32[2]{0:T(128)S(1)} %pad_add_fusion.ids, bf16[128,768]{1,0:T(8,128)(2,1)S(1)} %get-tuple-element.64.rest_0_, bf16[128,768]{1,0:T(8,128)(2,1)S(1)} %collective-permute-done.rest_1_, ...), custom_call_target="tpu_custom_call" | custom-call | flops 452984832 | bytes 4915208 | tf_op jit(solution)/shard_map/project/pallas_call | solution.py:53
  36.2 2.3 %attention.1 = (bf16[4,256,256]{2,1,0:T(8,128)(2,1)S(1)}, bf16[256,384]{1,0:T(8,128)(2,1)S(1)}, bf16[128,384]{1,0:T(8,128)(2,1)S(1)}, bf16[128,384]{1,0:T(8,128)(2,1)S(1)}) custom-call(s32[2]{0:T(128)S(1)} %pad_add_fusion.ids, bf16[384,256]{1,0:T(8,128)(2,1)S(1)} %get-tuple-element.65.query, bf16[384,256]{1,0:T(8,128)(2,1)S(1)} %get-tuple-element.66.key, ...), custom_call_target="tpu_custom_call" | custom-call | flops 100663296 | bytes 2033864 | tf_op jit(solution)/shard_map/attention/pallas_call | solution.py:53
  38.6 1.5 %collective-permute-start.11 = (bf16[128,384]{1,0:T(8,128)(2,1)S(1)}, bf16[128,384]{1,0:T(8,128)(2,1)S(1)}, u32[]{:S(2)}, u32[]{:S(2)}) collective-permute-start(bf16[128,384]{1,0:T(8,128)(2,1)S(1)} %get-tuple-element.71), channel_id=1, source_target_pairs={{0,1},{1,0},{2,3},{3,2},{4,5},{5,4},{6,7},{7,6},{8,9},{9,8},{10,11... | collective-permute-start | bytes 294920 | tf_op jit(solution)/shard_map/ppermute | solution.py:461
  40.1 0.9 copy-done.14
  41.0 0.9 down.1.d_hidden
  41.9 1.3 collective-permute-done.11.rest_1_
  43.3 0.9 copy-done.12
  44.2 0.9 copy-done.15
  45.1 4.7 %hidden.1 = (f32[128,768]{1,0:T(8,128)S(1)}, bf16[128,768]{1,0:T(8,128)(2,1)S(1)}) custom-call(s32[2]{0:T(128)S(1)} %pad_add_fusion.ids, bf16[128,768]{1,0:T(8,128)(2,1)S(1)} %bitcast.32, bf16[128,768]{1,0:T(8,128)(2,1)S(1)} %bitcast.35, f32[128,1536]{1,0:T(8,128)S(1)} %down.1.d_hidden, f32[1,768]{1,0:T(1,128)S(1)} %reshape.49.gain, ...), custom_call_target="tpu_custom_call" | custom-call | flops 1358954496 | bytes 7867400 | tf_op jit(solution)/shard_map/hidden/pallas_call | solution.py:53
  49.8 1.5 %collective-permute-start.12 = (bf16[128,768]{1,0:T(8,128)(2,1)S(1)}, bf16[128,768]{1,0:T(8,128)(2,1)S(1)}, u32[]{:S(2)}, u32[]{:S(2)}) collective-permute-start(bf16[128,768]{1,0:T(8,128)(2,1)S(1)} %get-tuple-element.76.rest_0_), channel_id=1, source_target_pairs={{0,1},{1,0},{2,3},{3,2},{4,5},{5,4},{6,7},{7,6},{8,9},{9,8},{10,11... | collective-permute-start | bytes 589832 | tf_op jit(solution)/shard_map/ppermute | solution.py:461
  51.4 4.2 %collective-permute-done.12.rest_1_ = bf16[128,768]{1,0:T(8,128)(2,1)S(1)} collective-permute-done((bf16[128,768]{1,0:T(8,128)(2,1)S(1)}, bf16[128,768]{1,0:T(8,128)(2,1)S(1)}, u32[]{:S(2)}, u32[]{:S(2)}) %collective-permute-start.12) | collective-permute-done | bytes 196640 | tf_op jit(solution)/shard_map/ppermute | solution.py:461
  55.6 2.7 %backward.1 = (bf16[256,768]{1,0:T(8,128)(2,1)S(1)}, bf16[384,256]{1,0:T(8,128)(2,1)S(1)}, bf16[384,256]{1,0:T(8,128)(2,1)S(1)}, bf16[384,256]{1,0:T(8,128)(2,1)...) custom-call(s32[2]{0:T(128)S(1)} %pad_add_fusion.ids, ...), custom_call_target="tpu_custom_call" | custom-call | flops 352321536 | bytes 4194312 | tf_op jit(solution)/shard_map/backward/pallas_call | solution.py:53
  58.2 4.0 %gradient.1 = (bf16[8,4,48,384]{3,2,1,0:T(8,128)(2,1)S(1)}, bf16[8,4,48,384]{3,2,1,0:T(8,128)(2,1)S(1)}, f32[768,128]{1,0:T(8,128)S(1)}, bf16[768,128]{1,0:T(8,128)(2,1)S(1)}) custom-call(s32[2]{0:T(128)S(1)} %pad_add_fusion.ids, bf16[256,768]{1,0:T(8,128)(2,1)S(1)} %get-tuple-element.73.x, bf16[256,384]{1,0:T(8,128)(2,1)S(1)} %get-tuple-element.74.att, ...), custom_call_target="tpu_custom_call" | custom-call | flops 1056964608 | bytes 8060936 | tf_op jit(solution)/shard_map/gradient/pallas_call | solution.py:53
  62.3 2.8 %collective-permute-done.14.got = bf16[8,4,48,384]{3,2,1,0:T(8,128)(2,1)S(1)} collective-permute-done((bf16[8,4,48,384]{3,2,1,0:T(8,128)(2,1)S(1)}, bf16[8,4,48,384]{3,2,1,0:T(8,128)(2,1)S(1)}, u32[]{:S(2)}, u32[]{:S(2)}) %collective-permute-start.14) | collective-permute-done | bytes 1179680 | tf_op jit(solution)/shard_map/ppermute | solution.py:456
  65.1 0.8 halve.1
  66.0 1.6 %collective-permute-start.15 = (bf16[4,4,48,384]{3,2,1,0:T(8,128)(2,1)S(1)}, bf16[4,4,48,384]{3,2,1,0:T(8,128)(2,1)S(1)}, u32[]{:S(2)}, u32[]{:S(2)}) collective-permute-start(bf16[4,4,48,384]{3,2,1,0:T(8,128)(2,1)S(1)} %get-tuple-element.87), channel_id=1, source_target_pairs={{0,4},{2,6},{4,0},{6,2},{8,12},{10,14},{12,8},{14,10},{16,20},{18,... | collective-permute-start | bytes 1769480 | tf_op jit(solution)/shard_map/ppermute | solution.py:456
  67.6 1.5 collective-permute-start.13
  69.6 1.3 collective-permute-start.27
  70.9 3.3 %collective-permute-done.13.rest_0_ = bf16[768,128]{1,0:T(8,128)(2,1)S(1)} collective-permute-done((bf16[768,128]{1,0:T(8,128)(2,1)S(1)}, bf16[768,128]{1,0:T(8,128)(2,1)S(1)}, u32[]{:S(2)}, u32[]{:S(2)}) %collective-permute-start.13) | collective-permute-done | bytes 196640 | tf_op jit(solution)/shard_map/ppermute | solution.py:461
  74.2 1.8 %exit.1 = (bf16[128,768]{1,0:T(8,128)(2,1)}, bf16[4,2,48,128]{3,2,1,0:T(8,128)(2,1)S(1)}, bf16[4,2,48,128]{3,2,1,0:T(8,128)(2,1)S(1)}) custom-call(s32[2]{0:T(128)S(1)} %pad_add_fusion.ids, bf16[128,768]{1,0:T(8,128)(2,1)S(1)} %bitcast.33, f32[1,768]{1,0:T(1,128)S(1)} %reshape.47.gain, f32[128,768]{1,0:T(8,128)S(1)} %get-tuple-element.72.d_res, ...), custom_call_target="tpu_custom_call" | custom-call | bytes 1575944 | tf_op jit(solution)/shard_map/exit/pallas_call | solution.py:53
  76.6 8.5 %collective-permute-done.26.refs_2_ = bf16[4,64,256]{2,1,0:T(8,128)(2,1)S(1)} collective-permute-done((bf16[4,64,256]{2,1,0:T(8,128)(2,1)S(1)}, bf16[4,64,256]{2,1,0:T(8,128)(2,1)S(1)}, u32[]{:S(2)}, u32[]{:S(2)}) %collective-permute-start.26) | collective-permute-done | bytes 131104 | tf_op jit(solution)/shard_map/ppermute | solution.py:456
  85.1 1.8 %collective-permute-done.27.refs_3_ = bf16[4,64,256]{2,1,0:T(8,128)(2,1)S(1)} collective-permute-done((bf16[4,64,256]{2,1,0:T(8,128)(2,1)S(1)}, bf16[4,64,256]{2,1,0:T(8,128)(2,1)S(1)}, u32[]{:S(2)}, u32[]{:S(2)}) %collective-permute-start.27) | collective-permute-done | bytes 131104 | tf_op jit(solution)/shard_map/ppermute | solution.py:456
  87.5 1.5 %collective-permute-start.28 = (bf16[64,128]{1,0:T(8,128)(2,1)S(1)}, bf16[64,128]{1,0:T(8,128)(2,1)S(1)}, u32[]{:S(2)}, u32[]{:S(2)}) collective-permute-start(bf16[64,128]{1,0:T(8,128)(2,1)S(1)} %get-tuple-element.107), channel_id=1, source_target_pairs={{0,1},{1,0},{2,3},{3,2},{4,5},{5,4},{6,7},{7,6},{8,9},{9,8},{10,11... | collective-permute-start | bytes 49160 | tf_op jit(solution)/shard_map/ppermute | solution.py:471
  89.7 1.3 collective-permute-start.30
  91.3 3.8 %collective-permute-start.31 = (bf16[64,128]{1,0:T(8,128)(2,1)S(1)}, bf16[64,128]{1,0:T(8,128)(2,1)S(1)}, u32[]{:S(2)}, u32[]{:S(2)}) collective-permute-start(bf16[64,128]{1,0:T(8,128)(2,1)S(1)} %get-tuple-element.110), channel_id=1, source_target_pairs={{0,16},{1,17},{2,18},{3,19},{4,20},{5,21},{6,22},{7,23},{8,24},{9,... | collective-permute-start | bytes 49160 | tf_op jit(solution)/shard_map/ppermute | solution.py:471
  95.1 1.5 %collective-permute-start.32 = (bf16[64,128]{1,0:T(8,128)(2,1)S(1)}, bf16[64,128]{1,0:T(8,128)(2,1)S(1)}, u32[]{:S(2)}, u32[]{:S(2)}) collective-permute-start(bf16[64,128]{1,0:T(8,128)(2,1)S(1)} %get-tuple-element.111), channel_id=1, source_target_pairs={{0,17},{1,16},{2,19},{3,18},{4,21},{5,20},{6,23},{7,22},{8,25},{9,... | collective-permute-start | bytes 49160 | tf_op jit(solution)/shard_map/ppermute | solution.py:471
  96.6 1.4 collective-permute-start.33
  98.0 2.4 %collective-permute-start.34 = (bf16[64,128]{1,0:T(8,128)(2,1)S(1)}, bf16[64,128]{1,0:T(8,128)(2,1)S(1)}, u32[]{:S(2)}, u32[]{:S(2)}) collective-permute-start(bf16[64,128]{1,0:T(8,128)(2,1)S(1)} %get-tuple-element.113), channel_id=1, source_target_pairs={{0,25},{1,24},{2,27},{3,26},{4,29},{5,28},{6,31},{7,30},{8,17},{9,... | collective-permute-start | bytes 49160 | tf_op jit(solution)/shard_map/ppermute | solution.py:471
  101.0 1.1 collective-permute-done.33.refs_6_
  102.2 2.3 %collective-permute-done.34.refs_7_ = bf16[64,128]{1,0:T(8,128)(2,1)S(1)} collective-permute-done((bf16[64,128]{1,0:T(8,128)(2,1)S(1)}, bf16[64,128]{1,0:T(8,128)(2,1)S(1)}, u32[]{:S(2)}, u32[]{:S(2)}) %collective-permute-start.34) | collective-permute-done | bytes 16416 | tf_op jit(solution)/shard_map/ppermute | solution.py:471
  104.4 3.6 %pair.1 = (bf16[2048,128]{1,0:T(8,128)(2,1)}, f32[8,128]{1,0:T(8,128)S(1)}) custom-call(s32[2]{0:T(128)S(1)} %pad_add_fusion.ids, bf16[2048,128]{1,0:T(8,128)(2,1)S(1)} %bitcast.30, f32[1,128]{1,0:T(1,128)S(1)} %bitcast.37, bf16[128,8]{1,0:T(8,128)(2,1)S(1)} %copy.28.w_pair, bf16[64,128]{1,0:T(8,128)(2,1)S(1)} %get-tuple-element.106.refs_0_, ...), custom_call_target="tpu_custom_call" | custom-call | flops 134217728 | bytes 1186312 | tf_op jit(solution)/shard_map/pair/pallas_call | solution.py:53
  108.0 2.4 %collective-permute-start.41 = (f32[8,128]{1,0:T(8,128)S(1)}, f32[8,128]{1,0:T(8,128)S(1)}, u32[]{:S(2)}, u32[]{:S(2)}) collective-permute-start(f32[8,128]{1,0:T(8,128)S(1)} %get-tuple-element.119), channel_id=1, source_target_pairs={{0,25},{1,24},{2,27},{3,26},{4,29},{5,28},{6,31},{7,30},{8,17},{9,... | collective-permute-start | bytes 12296 | tf_op jit(solution)/shard_map/ppermute | solution.py:471
  110.4 2.4 %collective-permute-start.40 = (f32[8,128]{1,0:T(8,128)S(1)}, f32[8,128]{1,0:T(8,128)S(1)}, u32[]{:S(2)}, u32[]{:S(2)}) collective-permute-start(f32[8,128]{1,0:T(8,128)S(1)} %get-tuple-element.119), channel_id=1, source_target_pairs={{0,24},{1,25},{2,26},{3,27},{4,28},{5,29},{6,30},{7,31},{8,16},{9,... | collective-permute-start | bytes 12296 | tf_op jit(solution)/shard_map/ppermute | solution.py:471
  112.8 1.5 %collective-permute-done.41 = f32[8,128]{1,0:T(8,128)S(1)} collective-permute-done((f32[8,128]{1,0:T(8,128)S(1)}, f32[8,128]{1,0:T(8,128)S(1)}, u32[]{:S(2)}, u32[]{:S(2)}) %collective-permute-start.41) | collective-permute-done | bytes 4128 | tf_op jit(solution)/shard_map/ppermute | solution.py:471
  114.3 1.3 collective-permute-start.38
  115.8 1.5 %collective-permute-start.37 = (f32[8,128]{1,0:T(8,128)S(1)}, f32[8,128]{1,0:T(8,128)S(1)}, u32[]{:S(2)}, u32[]{:S(2)}) collective-permute-start(f32[8,128]{1,0:T(8,128)S(1)} %get-tuple-element.119), channel_id=1, source_target_pairs={{0,9},{1,8},{2,11},{3,10},{4,13},{5,12},{6,15},{7,14},{8,1},{9,0},... | collective-permute-start | bytes 12296 | tf_op jit(solution)/shard_map/ppermute | solution.py:471
  117.3 0.9 collective-permute-done.39
  120.0 2.5 %collective-permute-start.22 = (bf16[2,48,128]{2,1,0:T(8,128)(2,1)S(1)}, bf16[2,48,128]{2,1,0:T(8,128)(2,1)S(1)}, u32[]{:S(2)}, u32[]{:S(2)}) collective-permute-start(bf16[2,48,128]{2,1,0:T(8,128)(2,1)S(1)} %get-tuple-element.97), channel_id=1, source_target_pairs={{0,16},{2,18},{4,20},{6,22},{8,24},{10,26},{12,28},{14,30},{16,0},... | collective-permute-start | bytes 73736 | tf_op jit(solution)/shard_map/ppermute | solution.py:456
  122.5 1.5 collective-permute-start.23
  124.0 2.9 %collective-permute-start.17 = (bf16[4,48,384]{2,1,0:T(8,128)(2,1)S(1)}, bf16[4,48,384]{2,1,0:T(8,128)(2,1)S(1)}, u32[]{:S(2)}, u32[]{:S(2)}) collective-permute-start(bf16[4,48,384]{2,1,0:T(8,128)(2,1)S(1)} %get-tuple-element.90), channel_id=1, source_target_pairs={{0,16},{2,18},{4,20},{6,22},{8,24},{10,26},{12,28},{14,30},{16,0},... | collective-permute-start | bytes 442376 | tf_op jit(solution)/shard_map/ppermute | solution.py:456
  126.9 1.5 collective-permute-start.18
  128.5 1.3 collective-permute-start.43
  130.9 3.8 %collective-permute-done.17.refs_2_ = bf16[4,48,384]{2,1,0:T(8,128)(2,1)S(1)} collective-permute-done((bf16[4,48,384]{2,1,0:T(8,128)(2,1)S(1)}, bf16[4,48,384]{2,1,0:T(8,128)(2,1)S(1)}, u32[]{:S(2)}, u32[]{:S(2)}) %collective-permute-start.17) | collective-permute-done | bytes 147488 | tf_op jit(solution)/shard_map/ppermute | solution.py:456
  134.9 4.9 %collective-permute-start.19 = (bf16[3,48,384]{2,1,0:T(8,128)(2,1)S(1)}, bf16[3,48,384]{2,1,0:T(8,128)(2,1)S(1)}, u32[]{:S(2)}, u32[]{:S(2)}) collective-permute-start(bf16[3,48,384]{2,1,0:T(8,128)(2,1)S(1)} %get-tuple-element.92), channel_id=1, source_target_pairs={{0,0},{1,16},{2,2},{3,18},{4,4},{5,20},{6,6},{7,22},{8,8},{9,24},{... | collective-permute-start | bytes 331784 | tf_op jit(solution)/shard_map/ppermute | solution.py:711
  141.2 4.3 %collective-permute-done.19.moved = bf16[3,48,384]{2,1,0:T(8,128)(2,1)S(1)} collective-permute-done((bf16[3,48,384]{2,1,0:T(8,128)(2,1)S(1)}, bf16[3,48,384]{2,1,0:T(8,128)(2,1)S(1)}, u32[]{:S(2)}, u32[]{:S(2)}) %collective-permute-start.19) | collective-permute-done | bytes 110624 | tf_op jit(solution)/shard_map/ppermute | solution.py:711
  (111 shorter events, 13.0 us)
Async XLA Ops:
  0.6 30.8 %copy-start.1 = (bf16[768,768]{1,0:T(8,128)(2,1)S(1)}, bf16[768,768]{1,0:T(8,128)(2,1)}, u32[]{:S(2)}) copy-start(bf16[768,768]{1,0:T(8,128)(2,1)} %rest_0_.1) | copy-start | bytes 3538948
  2.3 1.0 copy-start.9
  9.2 18.1 %collective-permute-start.6 = (bf16[64,128]{1,0:T(8,128)(2,1)S(1)}, bf16[64,128]{1,0:T(8,128)(2,1)S(1)}, u32[]{:S(2)}, u32[]{:S(2)}) collective-permute-start(bf16[64,128]{1,0:T(8,128)(2,1)S(1)} %get-tuple-element.68), channel_id=1, source_target_pairs={{0,24},{1,25},{2,26},{3,27},{4,28},{5,29},{6,30},{7,31},{8,16},{9,... | collective-permute-start | bytes 49160 | tf_op jit(solution)/shard_map/ppermute | solution.py:471
  12.8 14.4 %collective-permute-start.4 = (bf16[64,128]{1,0:T(8,128)(2,1)S(1)}, bf16[64,128]{1,0:T(8,128)(2,1)S(1)}, u32[]{:S(2)}, u32[]{:S(2)}) collective-permute-start(bf16[64,128]{1,0:T(8,128)(2,1)S(1)} %get-tuple-element.68), channel_id=1, source_target_pairs={{0,16},{1,17},{2,18},{3,19},{4,20},{5,21},{6,22},{7,23},{8,24},{9,... | collective-permute-start | bytes 49160 | tf_op jit(solution)/shard_map/ppermute | solution.py:471
  12.8 8.1 %collective-permute-start.2 = (bf16[64,128]{1,0:T(8,128)(2,1)S(1)}, bf16[64,128]{1,0:T(8,128)(2,1)S(1)}, u32[]{:S(2)}, u32[]{:S(2)}) collective-permute-start(bf16[64,128]{1,0:T(8,128)(2,1)S(1)} %get-tuple-element.68), channel_id=1, source_target_pairs={{0,8},{1,9},{2,10},{3,11},{4,12},{5,13},{6,14},{7,15},{8,0},{9,1},... | collective-permute-start | bytes 49160 | tf_op jit(solution)/shard_map/ppermute | solution.py:471
  13.6 13.7 %collective-permute-start.7 = (bf16[64,128]{1,0:T(8,128)(2,1)S(1)}, bf16[64,128]{1,0:T(8,128)(2,1)S(1)}, u32[]{:S(2)}, u32[]{:S(2)}) collective-permute-start(bf16[64,128]{1,0:T(8,128)(2,1)S(1)} %get-tuple-element.69), channel_id=1, source_target_pairs={{0,25},{1,24},{2,27},{3,26},{4,29},{5,28},{6,31},{7,30},{8,17},{9,... | collective-permute-start | bytes 49160 | tf_op jit(solution)/shard_map/ppermute | solution.py:471
  17.2 3.7 %collective-permute-start.1 = (bf16[64,128]{1,0:T(8,128)(2,1)S(1)}, bf16[64,128]{1,0:T(8,128)(2,1)S(1)}, u32[]{:S(2)}, u32[]{:S(2)}) collective-permute-start(bf16[64,128]{1,0:T(8,128)(2,1)S(1)} %get-tuple-element.69), channel_id=1, source_target_pairs={{0,1},{1,0},{2,3},{3,2},{4,5},{5,4},{6,7},{7,6},{8,9},{9,8},{10,11... | collective-permute-start | bytes 49160 | tf_op jit(solution)/shard_map/ppermute | solution.py:471
  20.9 6.3 %collective-permute-start.5 = (bf16[64,128]{1,0:T(8,128)(2,1)S(1)}, bf16[64,128]{1,0:T(8,128)(2,1)S(1)}, u32[]{:S(2)}, u32[]{:S(2)}) collective-permute-start(bf16[64,128]{1,0:T(8,128)(2,1)S(1)} %get-tuple-element.69), channel_id=1, source_target_pairs={{0,17},{1,16},{2,19},{3,18},{4,21},{5,20},{6,23},{7,22},{8,25},{9,... | collective-permute-start | bytes 49160 | tf_op jit(solution)/shard_map/ppermute | solution.py:471
  21.0 4.8 %collective-permute-start.3 = (bf16[64,128]{1,0:T(8,128)(2,1)S(1)}, bf16[64,128]{1,0:T(8,128)(2,1)S(1)}, u32[]{:S(2)}, u32[]{:S(2)}) collective-permute-start(bf16[64,128]{1,0:T(8,128)(2,1)S(1)} %get-tuple-element.69), channel_id=1, source_target_pairs={{0,9},{1,8},{2,11},{3,10},{4,13},{5,12},{6,15},{7,14},{8,1},{9,0},... | collective-permute-start | bytes 49160 | tf_op jit(solution)/shard_map/ppermute | solution.py:471
  25.8 5.7 %collective-permute-start = (bf16[128,768]{1,0:T(8,128)(2,1)S(1)}, bf16[128,768]{1,0:T(8,128)(2,1)S(1)}, u32[]{:S(2)}, u32[]{:S(2)}) collective-permute-start(bf16[128,768]{1,0:T(8,128)(2,1)S(1)} %get-tuple-element.64.rest_0_), channel_id=1, source_target_pairs={{0,1},{1,0},{2,3},{3,2},{4,5},{5,4},{6,7},{7,6},{8,9},{9,8},{10,11... | collective-permute-start | bytes 589832 | tf_op jit(solution)/shard_map/ppermute | solution.py:461
  27.3 8.9 %copy-start.18 = (f32[6,8]{1,0:T(8,128)S(1)}, f32[6,8]{1,0:T(8,128)}, u32[]{:S(2)}) copy-start(f32[6,8]{1,0:T(8,128)} %rest_6_.1) | copy-start | bytes 580
  27.3 8.8 %copy-start.21 = (s32[256]{0:T(256)S(1)}, s32[256]{0:T(256)}, u32[]{:S(2)}) copy-start(s32[256]{0:T(256)} %param.24) | copy-start | bytes 3076
  27.3 8.8 %copy-start.22 = (s32[256]{0:T(256)S(1)}, s32[256]{0:T(256)}, u32[]{:S(2)}) copy-start(s32[256]{0:T(256)} %param.25) | copy-start | bytes 3076
  27.3 12.7 %copy-start.24 = (f32[768]{0:T(1024)S(1)}, f32[768]{0:T(1024)}, u32[]{:S(2)}) copy-start(f32[768]{0:T(1024)} %param.29) | copy-start | bytes 9220
  27.4 8.8 %collective-permute-start.10 = (bf16[8,64,128]{2,1,0:T(8,128)(2,1)S(1)}, bf16[8,64,128]{2,1,0:T(8,128)(2,1)S(1)}, u32[]{:S(2)}, u32[]{:S(2)}) collective-permute-start(bf16[8,64,128]{2,1,0:T(8,128)(2,1)S(1)} %constant_dynamic-update-slice_fusion.rest_0_), channel_id=1, source_target_pairs={{0,6},{2,4},{4,2},{6,0},{8,14},{10,12},{12,10},{14,8},{16,22},{18,... | collective-permute-start | bytes 393224 | tf_op jit(solution)/shard_map/ppermute | solution.py:456
  27.4 8.7 %collective-permute-start.9 = (bf16[8,64,128]{2,1,0:T(8,128)(2,1)S(1)}, bf16[8,64,128]{2,1,0:T(8,128)(2,1)S(1)}, u32[]{:S(2)}, u32[]{:S(2)}) collective-permute-start(bf16[8,64,128]{2,1,0:T(8,128)(2,1)S(1)} %constant_dynamic-update-slice_fusion.rest_0_), channel_id=1, source_target_pairs={{0,4},{2,6},{4,0},{6,2},{8,12},{10,14},{12,8},{14,10},{16,20},{18,... | collective-permute-start | bytes 393224 | tf_op jit(solution)/shard_map/ppermute | solution.py:456
  29.0 7.1 %collective-permute-start.8 = (bf16[8,64,128]{2,1,0:T(8,128)(2,1)S(1)}, bf16[8,64,128]{2,1,0:T(8,128)(2,1)S(1)}, u32[]{:S(2)}, u32[]{:S(2)}) collective-permute-start(bf16[8,64,128]{2,1,0:T(8,128)(2,1)S(1)} %constant_dynamic-update-slice_fusion.rest_0_), channel_id=1, source_target_pairs={{0,2},{2,0},{4,6},{6,4},{8,10},{10,8},{12,14},{14,12},{16,18},{18,... | collective-permute-start | bytes 393224 | tf_op jit(solution)/shard_map/ppermute | solution.py:456
  31.4 1.3 copy-start.2
  32.7 1.3 copy-start.4
  34.0 6.1 %copy-start.8 = (bf16[1536,768]{1,0:T(8,128)(2,1)S(1)}, bf16[1536,768]{1,0:T(8,128)(2,1)}, u32[]{:S(2)}) copy-start(bf16[1536,768]{1,0:T(8,128)(2,1)} %w_down.1) | copy-start | bytes 7077892
  34.0 9.3 %copy-start.7 = (bf16[768,1536]{1,0:T(8,128)(2,1)S(1)}, bf16[768,1536]{1,0:T(8,128)(2,1)}, u32[]{:S(2)}) copy-start(bf16[768,1536]{1,0:T(8,128)(2,1)} %rest_4_.3) | copy-start | bytes 7077892
  36.2 7.1 %copy-start.6 = (bf16[768,1536]{1,0:T(8,128)(2,1)S(1)}, bf16[768,1536]{1,0:T(8,128)(2,1)}, u32[]{:S(2)}) copy-start(bf16[768,1536]{1,0:T(8,128)(2,1)} %rest_3_.3) | copy-start | bytes 7077892
  38.6 4.7 %collective-permute-start.11 = (bf16[128,384]{1,0:T(8,128)(2,1)S(1)}, bf16[128,384]{1,0:T(8,128)(2,1)S(1)}, u32[]{:S(2)}, u32[]{:S(2)}) collective-permute-start(bf16[128,384]{1,0:T(8,128)(2,1)S(1)} %get-tuple-element.71), channel_id=1, source_target_pairs={{0,1},{1,0},{2,3},{3,2},{4,5},{5,4},{6,7},{7,6},{8,9},{9,8},{10,11... | collective-permute-start | bytes 294920 | tf_op jit(solution)/shard_map/ppermute | solution.py:461
  40.1 0.9 copy-start.14
  41.0 2.2 %copy-start = (bf16[768,768]{1,0:T(8,128)(2,1)S(1)}, bf16[768,768]{1,0:T(8,128)(2,1)}, u32[]{:S(2)}) copy-start(bf16[768,768]{1,0:T(8,128)(2,1)} %rest_2_.6) | copy-start | bytes 3538948
  43.2 0.9 copy-start.12
  49.8 5.7 %collective-permute-start.12 = (bf16[128,768]{1,0:T(8,128)(2,1)S(1)}, bf16[128,768]{1,0:T(8,128)(2,1)S(1)}, u32[]{:S(2)}, u32[]{:S(2)}) collective-permute-start(bf16[128,768]{1,0:T(8,128)(2,1)S(1)} %get-tuple-element.76.rest_0_), channel_id=1, source_target_pairs={{0,1},{1,0},{2,3},{3,2},{4,5},{5,4},{6,7},{7,6},{8,9},{9,8},{10,11... | collective-permute-start | bytes 589832 | tf_op jit(solution)/shard_map/ppermute | solution.py:461
  55.6 2.7 %copy-start.3 = (bf16[768,768]{1,0:T(8,128)(2,1)S(1)}, bf16[768,768]{1,0:T(8,128)(2,1)}, u32[]{:S(2)}) copy-start(bf16[768,768]{1,0:T(8,128)(2,1)} %rest_1_.1) | copy-start | bytes 3538948
  55.6 2.7 %copy-start.5 = (bf16[768,768]{1,0:T(8,128)(2,1)S(1)}, bf16[768,768]{1,0:T(8,128)(2,1)}, u32[]{:S(2)}) copy-start(bf16[768,768]{1,0:T(8,128)(2,1)} %rest_2_.7) | copy-start | bytes 3538948
  62.2 2.9 %collective-permute-start.14 = (bf16[8,4,48,384]{3,2,1,0:T(8,128)(2,1)S(1)}, bf16[8,4,48,384]{3,2,1,0:T(8,128)(2,1)S(1)}, u32[]{:S(2)}, u32[]{:S(2)}) collective-permute-start(bf16[8,4,48,384]{3,2,1,0:T(8,128)(2,1)S(1)} %get-tuple-element.85), channel_id=1, source_target_pairs={{0,2},{2,0},{4,6},{6,4},{8,10},{10,8},{12,14},{14,12},{16,18},{18,... | collective-permute-start | bytes 3538952 | tf_op jit(solution)/shard_map/ppermute | solution.py:456
  65.1 9.1 %copy-start.13 = (bf16[1,128,768]{2,1,0:T(8,128)(2,1)S(1)}, bf16[1,128,768]{2,1,0:T(8,128)(2,1)}, u32[]{:S(2)}) copy-start(bf16[1,128,768]{2,1,0:T(8,128)(2,1)} %param.20) | copy-start | bytes 589828
  66.0 38.4 %copy-start.10 = (bf16[128,16,128]{2,1,0:T(8,128)(2,1)S(1)}, bf16[128,16,128]{2,1,0:T(8,128)(2,1)}, u32[]{:S(2)}) copy-start(bf16[128,16,128]{2,1,0:T(8,128)(2,1)} %param.22) | copy-start | bytes 1572868
  66.0 38.4 %copy-start.20 = (f32[128]{0:T(128)S(1)}, f32[128]{0:T(128)}, u32[]{:S(2)}) copy-start(f32[128]{0:T(128)} %param.28) | copy-start | bytes 1540
  66.0 52.8 %collective-permute-start.15 = (bf16[4,4,48,384]{3,2,1,0:T(8,128)(2,1)S(1)}, bf16[4,4,48,384]{3,2,1,0:T(8,128)(2,1)S(1)}, u32[]{:S(2)}, u32[]{:S(2)}) collective-permute-start(bf16[4,4,48,384]{3,2,1,0:T(8,128)(2,1)S(1)} %get-tuple-element.87), channel_id=1, source_target_pairs={{0,4},{2,6},{4,0},{6,2},{8,12},{10,14},{12,8},{14,10},{16,20},{18,... | collective-permute-start | bytes 1769480 | tf_op jit(solution)/shard_map/ppermute | solution.py:456
  67.6 6.7 %collective-permute-start.13 = (bf16[768,128]{1,0:T(8,128)(2,1)S(1)}, bf16[768,128]{1,0:T(8,128)(2,1)S(1)}, u32[]{:S(2)}, u32[]{:S(2)}) collective-permute-start(bf16[768,128]{1,0:T(8,128)(2,1)S(1)} %get-tuple-element.82), channel_id=1, source_target_pairs={{0,1},{1,0},{2,3},{3,2},{4,5},{5,4},{6,7},{7,6},{8,9},{9,8},{10,11... | collective-permute-start | bytes 589832 | tf_op jit(solution)/shard_map/ppermute | solution.py:461
  69.1 7.5 %collective-permute-start.25 = (bf16[4,64,256]{2,1,0:T(8,128)(2,1)S(1)}, bf16[4,64,256]{2,1,0:T(8,128)(2,1)S(1)}, u32[]{:S(2)}, u32[]{:S(2)}) collective-permute-start(bf16[4,64,256]{2,1,0:T(8,128)(2,1)S(1)} %get-tuple-element.103), channel_id=1, source_target_pairs={{0,2},{2,0},{4,6},{6,4},{8,10},{10,8},{12,14},{14,12},{16,18},{18,... | collective-permute-start | bytes 393224 | tf_op jit(solution)/shard_map/ppermute | solution.py:456
  69.1 16.0 %collective-permute-start.26 = (bf16[4,64,256]{2,1,0:T(8,128)(2,1)S(1)}, bf16[4,64,256]{2,1,0:T(8,128)(2,1)S(1)}, u32[]{:S(2)}, u32[]{:S(2)}) collective-permute-start(bf16[4,64,256]{2,1,0:T(8,128)(2,1)S(1)} %get-tuple-element.104), channel_id=1, source_target_pairs={{0,4},{2,6},{4,0},{6,2},{8,12},{10,14},{12,8},{14,10},{16,20},{18,... | collective-permute-start | bytes 393224 | tf_op jit(solution)/shard_map/ppermute | solution.py:456
  69.6 17.3 %collective-permute-start.27 = (bf16[4,64,256]{2,1,0:T(8,128)(2,1)S(1)}, bf16[4,64,256]{2,1,0:T(8,128)(2,1)S(1)}, u32[]{:S(2)}, u32[]{:S(2)}) collective-permute-start(bf16[4,64,256]{2,1,0:T(8,128)(2,1)S(1)} %get-tuple-element.105), channel_id=1, source_target_pairs={{0,6},{2,4},{4,2},{6,0},{8,14},{10,12},{12,10},{14,8},{16,22},{18,... | collective-permute-start | bytes 393224 | tf_op jit(solution)/shard_map/ppermute | solution.py:456
  76.0 21.9 %collective-permute-start.20 = (bf16[4,2,48,128]{3,2,1,0:T(8,128)(2,1)S(1)}, bf16[4,2,48,128]{3,2,1,0:T(8,128)(2,1)S(1)}, u32[]{:S(2)}, u32[]{:S(2)}) collective-permute-start(bf16[4,2,48,128]{3,2,1,0:T(8,128)(2,1)S(1)} %get-tuple-element.94), channel_id=1, source_target_pairs={{0,4},{2,6},{4,0},{6,2},{8,12},{10,14},{12,8},{14,10},{16,20},{18,... | collective-permute-start | bytes 294920 | tf_op jit(solution)/shard_map/ppermute | solution.py:456
  87.5 3.8 %collective-permute-start.28 = (bf16[64,128]{1,0:T(8,128)(2,1)S(1)}, bf16[64,128]{1,0:T(8,128)(2,1)S(1)}, u32[]{:S(2)}, u32[]{:S(2)}) collective-permute-start(bf16[64,128]{1,0:T(8,128)(2,1)S(1)} %get-tuple-element.107), channel_id=1, source_target_pairs={{0,1},{1,0},{2,3},{3,2},{4,5},{5,4},{6,7},{7,6},{8,9},{9,8},{10,11... | collective-permute-start | bytes 49160 | tf_op jit(solution)/shard_map/ppermute | solution.py:471
  89.1 6.0 %collective-permute-start.29 = (bf16[64,128]{1,0:T(8,128)(2,1)S(1)}, bf16[64,128]{1,0:T(8,128)(2,1)S(1)}, u32[]{:S(2)}, u32[]{:S(2)}) collective-permute-start(bf16[64,128]{1,0:T(8,128)(2,1)S(1)} %get-tuple-element.108), channel_id=1, source_target_pairs={{0,8},{1,9},{2,10},{3,11},{4,12},{5,13},{6,14},{7,15},{8,0},{9,1},... | collective-permute-start | bytes 49160 | tf_op jit(solution)/shard_map/ppermute | solution.py:471
  89.7 6.9 %collective-permute-start.30 = (bf16[64,128]{1,0:T(8,128)(2,1)S(1)}, bf16[64,128]{1,0:T(8,128)(2,1)S(1)}, u32[]{:S(2)}, u32[]{:S(2)}) collective-permute-start(bf16[64,128]{1,0:T(8,128)(2,1)S(1)} %get-tuple-element.109), channel_id=1, source_target_pairs={{0,9},{1,8},{2,11},{3,10},{4,13},{5,12},{6,15},{7,14},{8,1},{9,0},... | collective-permute-start | bytes 49160 | tf_op jit(solution)/shard_map/ppermute | solution.py:471
  91.3 9.6 %collective-permute-start.31 = (bf16[64,128]{1,0:T(8,128)(2,1)S(1)}, bf16[64,128]{1,0:T(8,128)(2,1)S(1)}, u32[]{:S(2)}, u32[]{:S(2)}) collective-permute-start(bf16[64,128]{1,0:T(8,128)(2,1)S(1)} %get-tuple-element.110), channel_id=1, source_target_pairs={{0,16},{1,17},{2,18},{3,19},{4,20},{5,21},{6,22},{7,23},{8,24},{9,... | collective-permute-start | bytes 49160 | tf_op jit(solution)/shard_map/ppermute | solution.py:471
  95.1 5.9 %collective-permute-start.32 = (bf16[64,128]{1,0:T(8,128)(2,1)S(1)}, bf16[64,128]{1,0:T(8,128)(2,1)S(1)}, u32[]{:S(2)}, u32[]{:S(2)}) collective-permute-start(bf16[64,128]{1,0:T(8,128)(2,1)S(1)} %get-tuple-element.111), channel_id=1, source_target_pairs={{0,17},{1,16},{2,19},{3,18},{4,21},{5,20},{6,23},{7,22},{8,25},{9,... | collective-permute-start | bytes 49160 | tf_op jit(solution)/shard_map/ppermute | solution.py:471
  96.6 5.6 %collective-permute-start.33 = (bf16[64,128]{1,0:T(8,128)(2,1)S(1)}, bf16[64,128]{1,0:T(8,128)(2,1)S(1)}, u32[]{:S(2)}, u32[]{:S(2)}) collective-permute-start(bf16[64,128]{1,0:T(8,128)(2,1)S(1)} %get-tuple-element.112), channel_id=1, source_target_pairs={{0,24},{1,25},{2,26},{3,27},{4,28},{5,29},{6,30},{7,31},{8,16},{9,... | collective-permute-start | bytes 49160 | tf_op jit(solution)/shard_map/ppermute | solution.py:471
  98.0 6.4 %collective-permute-start.34 = (bf16[64,128]{1,0:T(8,128)(2,1)S(1)}, bf16[64,128]{1,0:T(8,128)(2,1)S(1)}, u32[]{:S(2)}, u32[]{:S(2)}) collective-permute-start(bf16[64,128]{1,0:T(8,128)(2,1)S(1)} %get-tuple-element.113), channel_id=1, source_target_pairs={{0,25},{1,24},{2,27},{3,26},{4,29},{5,28},{6,31},{7,30},{8,17},{9,... | collective-permute-start | bytes 49160 | tf_op jit(solution)/shard_map/ppermute | solution.py:471
  100.9 26.0 %collective-permute-start.21 = (bf16[2,48,128]{2,1,0:T(8,128)(2,1)S(1)}, bf16[2,48,128]{2,1,0:T(8,128)(2,1)S(1)}, u32[]{:S(2)}, u32[]{:S(2)}) collective-permute-start(bf16[2,48,128]{2,1,0:T(8,128)(2,1)S(1)} %get-tuple-element.96), channel_id=1, source_target_pairs={{0,8},{2,10},{4,12},{6,14},{8,0},{10,2},{12,4},{14,6},{16,24},{18,... | collective-permute-start | bytes 73736 | tf_op jit(solution)/shard_map/ppermute | solution.py:456
  108.0 6.3 %collective-permute-start.41 = (f32[8,128]{1,0:T(8,128)S(1)}, f32[8,128]{1,0:T(8,128)S(1)}, u32[]{:S(2)}, u32[]{:S(2)}) collective-permute-start(f32[8,128]{1,0:T(8,128)S(1)} %get-tuple-element.119), channel_id=1, source_target_pairs={{0,25},{1,24},{2,27},{3,26},{4,29},{5,28},{6,31},{7,30},{8,17},{9,... | collective-permute-start | bytes 12296 | tf_op jit(solution)/shard_map/ppermute | solution.py:471
  110.4 5.4 %collective-permute-start.40 = (f32[8,128]{1,0:T(8,128)S(1)}, f32[8,128]{1,0:T(8,128)S(1)}, u32[]{:S(2)}, u32[]{:S(2)}) collective-permute-start(f32[8,128]{1,0:T(8,128)S(1)} %get-tuple-element.119), channel_id=1, source_target_pairs={{0,24},{1,25},{2,26},{3,27},{4,28},{5,29},{6,30},{7,31},{8,16},{9,... | collective-permute-start | bytes 12296 | tf_op jit(solution)/shard_map/ppermute | solution.py:471
  112.8 5.4 %collective-permute-start.39 = (f32[8,128]{1,0:T(8,128)S(1)}, f32[8,128]{1,0:T(8,128)S(1)}, u32[]{:S(2)}, u32[]{:S(2)}) collective-permute-start(f32[8,128]{1,0:T(8,128)S(1)} %get-tuple-element.119), channel_id=1, source_target_pairs={{0,17},{1,16},{2,19},{3,18},{4,21},{5,20},{6,23},{7,22},{8,25},{9,... | collective-permute-start | bytes 12296 | tf_op jit(solution)/shard_map/ppermute | solution.py:471
  114.3 5.7 %collective-permute-start.38 = (f32[8,128]{1,0:T(8,128)S(1)}, f32[8,128]{1,0:T(8,128)S(1)}, u32[]{:S(2)}, u32[]{:S(2)}) collective-permute-start(f32[8,128]{1,0:T(8,128)S(1)} %get-tuple-element.119), channel_id=1, source_target_pairs={{0,16},{1,17},{2,18},{3,19},{4,20},{5,21},{6,22},{7,23},{8,24},{9,... | collective-permute-start | bytes 12296 | tf_op jit(solution)/shard_map/ppermute | solution.py:471
  115.8 6.7 %collective-permute-start.37 = (f32[8,128]{1,0:T(8,128)S(1)}, f32[8,128]{1,0:T(8,128)S(1)}, u32[]{:S(2)}, u32[]{:S(2)}) collective-permute-start(f32[8,128]{1,0:T(8,128)S(1)} %get-tuple-element.119), channel_id=1, source_target_pairs={{0,9},{1,8},{2,11},{3,10},{4,13},{5,12},{6,15},{7,14},{8,1},{9,0},... | collective-permute-start | bytes 12296 | tf_op jit(solution)/shard_map/ppermute | solution.py:471
  118.2 5.8 %collective-permute-start.36 = (f32[8,128]{1,0:T(8,128)S(1)}, f32[8,128]{1,0:T(8,128)S(1)}, u32[]{:S(2)}, u32[]{:S(2)}) collective-permute-start(f32[8,128]{1,0:T(8,128)S(1)} %get-tuple-element.119), channel_id=1, source_target_pairs={{0,8},{1,9},{2,10},{3,11},{4,12},{5,13},{6,14},{7,15},{8,0},{9,1},... | collective-permute-start | bytes 12296 | tf_op jit(solution)/shard_map/ppermute | solution.py:471
  118.8 5.1 %collective-permute-start.35 = (f32[8,128]{1,0:T(8,128)S(1)}, f32[8,128]{1,0:T(8,128)S(1)}, u32[]{:S(2)}, u32[]{:S(2)}) collective-permute-start(f32[8,128]{1,0:T(8,128)S(1)} %get-tuple-element.119), channel_id=1, source_target_pairs={{0,1},{1,0},{2,3},{3,2},{4,5},{5,4},{6,7},{7,6},{8,9},{9,8},{10,11... | collective-permute-start | bytes 12296 | tf_op jit(solution)/shard_map/ppermute | solution.py:471
  120.0 8.5 %collective-permute-start.22 = (bf16[2,48,128]{2,1,0:T(8,128)(2,1)S(1)}, bf16[2,48,128]{2,1,0:T(8,128)(2,1)S(1)}, u32[]{:S(2)}, u32[]{:S(2)}) collective-permute-start(bf16[2,48,128]{2,1,0:T(8,128)(2,1)S(1)} %get-tuple-element.97), channel_id=1, source_target_pairs={{0,16},{2,18},{4,20},{6,22},{8,24},{10,26},{12,28},{14,30},{16,0},... | collective-permute-start | bytes 73736 | tf_op jit(solution)/shard_map/ppermute | solution.py:456
  122.5 6.0 %collective-permute-start.23 = (bf16[2,48,128]{2,1,0:T(8,128)(2,1)S(1)}, bf16[2,48,128]{2,1,0:T(8,128)(2,1)S(1)}, u32[]{:S(2)}, u32[]{:S(2)}) collective-permute-start(bf16[2,48,128]{2,1,0:T(8,128)(2,1)S(1)} %get-tuple-element.98), channel_id=1, source_target_pairs={{0,24},{2,26},{4,28},{6,30},{8,16},{10,18},{12,20},{14,22},{16,8},... | collective-permute-start | bytes 73736 | tf_op jit(solution)/shard_map/ppermute | solution.py:456
  124.0 6.3 %collective-permute-start.16 = (bf16[4,48,384]{2,1,0:T(8,128)(2,1)S(1)}, bf16[4,48,384]{2,1,0:T(8,128)(2,1)S(1)}, u32[]{:S(2)}, u32[]{:S(2)}) collective-permute-start(bf16[4,48,384]{2,1,0:T(8,128)(2,1)S(1)} %get-tuple-element.89), channel_id=1, source_target_pairs={{0,8},{2,10},{4,12},{6,14},{8,0},{10,2},{12,4},{14,6},{16,24},{18,... | collective-permute-start | bytes 442376 | tf_op jit(solution)/shard_map/ppermute | solution.py:456
  124.0 10.7 %collective-permute-start.17 = (bf16[4,48,384]{2,1,0:T(8,128)(2,1)S(1)}, bf16[4,48,384]{2,1,0:T(8,128)(2,1)S(1)}, u32[]{:S(2)}, u32[]{:S(2)}) collective-permute-start(bf16[4,48,384]{2,1,0:T(8,128)(2,1)S(1)} %get-tuple-element.90), channel_id=1, source_target_pairs={{0,16},{2,18},{4,20},{6,22},{8,24},{10,26},{12,28},{14,30},{16,0},... | collective-permute-start | bytes 442376 | tf_op jit(solution)/shard_map/ppermute | solution.py:456
  126.9 7.8 %collective-permute-start.18 = (bf16[4,48,384]{2,1,0:T(8,128)(2,1)S(1)}, bf16[4,48,384]{2,1,0:T(8,128)(2,1)S(1)}, u32[]{:S(2)}, u32[]{:S(2)}) collective-permute-start(bf16[4,48,384]{2,1,0:T(8,128)(2,1)S(1)} %get-tuple-element.91), channel_id=1, source_target_pairs={{0,24},{2,26},{4,28},{6,30},{8,16},{10,18},{12,20},{14,22},{16,8},... | collective-permute-start | bytes 442376 | tf_op jit(solution)/shard_map/ppermute | solution.py:456
  128.5 11.4 %collective-permute-start.44 = (f32[8,128]{1,0:T(8,128)S(1)}, f32[8,128]{1,0:T(8,128)S(1)}, u32[]{:S(2)}, u32[]{:S(2)}) collective-permute-start(f32[8,128]{1,0:T(8,128)S(1)} %add_add_fusion), channel_id=1, source_target_pairs={{0,6},{2,4},{4,2},{6,0},{8,14},{10,12},{12,10},{14,8},{16,22},{18,... | collective-permute-start | bytes 12296 | tf_op jit(solution)/shard_map/ppermute | solution.py:456
  128.5 11.4 %collective-permute-start.43 = (f32[8,128]{1,0:T(8,128)S(1)}, f32[8,128]{1,0:T(8,128)S(1)}, u32[]{:S(2)}, u32[]{:S(2)}) collective-permute-start(f32[8,128]{1,0:T(8,128)S(1)} %add_add_fusion), channel_id=1, source_target_pairs={{0,4},{2,6},{4,0},{6,2},{8,12},{10,14},{12,8},{14,10},{16,20},{18,... | collective-permute-start | bytes 12296 | tf_op jit(solution)/shard_map/ppermute | solution.py:456
  130.2 9.6 %collective-permute-start.42 = (f32[8,128]{1,0:T(8,128)S(1)}, f32[8,128]{1,0:T(8,128)S(1)}, u32[]{:S(2)}, u32[]{:S(2)}) collective-permute-start(f32[8,128]{1,0:T(8,128)S(1)} %add_add_fusion), channel_id=1, source_target_pairs={{0,2},{2,0},{4,6},{6,4},{8,10},{10,8},{12,14},{14,12},{16,18},{18,... | collective-permute-start | bytes 12296 | tf_op jit(solution)/shard_map/ppermute | solution.py:456
  134.7 6.5 %collective-permute-start.24 = (bf16[48,128]{1,0:T(8,128)(2,1)S(1)}, bf16[48,128]{1,0:T(8,128)(2,1)S(1)}, u32[]{:S(2)}, u32[]{:S(2)}) collective-permute-start(bf16[48,128]{1,0:T(8,128)(2,1)S(1)} %get-tuple-element.100), channel_id=1, source_target_pairs={{0,2},{2,0},{4,6},{6,4},{8,10},{10,8},{12,14},{14,12},{16,18},{18,... | collective-permute-start | bytes 36872 | tf_op jit(solution)/shard_map/ppermute | solution.py:456
  134.9 10.6 %collective-permute-start.19 = (bf16[3,48,384]{2,1,0:T(8,128)(2,1)S(1)}, bf16[3,48,384]{2,1,0:T(8,128)(2,1)S(1)}, u32[]{:S(2)}, u32[]{:S(2)}) collective-permute-start(bf16[3,48,384]{2,1,0:T(8,128)(2,1)S(1)} %get-tuple-element.92), channel_id=1, source_target_pairs={{0,0},{1,16},{2,2},{3,18},{4,4},{5,20},{6,6},{7,22},{8,8},{9,24},{... | collective-permute-start | bytes 331784 | tf_op jit(solution)/shard_map/ppermute | solution.py:711
  (6 other events, 4.9 us)

commit v3 on v2

v3 whole, which is shorter than its diff:
```python
import functools

import jax
import jax.numpy as jnp
from jax import lax
from jax.experimental import pallas as pl
from jax.experimental.pallas import tpu as pltpu
from jax.sharding import PartitionSpec as P

epsilon = 1e-05
f32 = jnp.float32
bf16 = jnp.bfloat16
VMEM, SMEM, ANY = pltpu.VMEM, pltpu.SMEM, pl.ANY
MIB = 1 << 20


def layer_forward(values, scales):
    average = jnp.mean(values, axis=-1, keepdims=True)
    centred = values - average
    inverse = lax.rsqrt(jnp.mean(centred * centred, axis=-1, keepdims=True) + epsilon)
    normed = centred * inverse
    return (normed * scales, normed, inverse)


def layer_backward(upstream, scales, normed, inverse):
    scaled = upstream * scales
    first_moment = jnp.mean(scaled, axis=-1, keepdims=True)
    second_moment = jnp.mean(scaled * normed, axis=-1, keepdims=True)
    return inverse * (scaled - first_moment - normed * second_moment)


NN = ((1,), (0,))
NT = ((1,), (1,))
TN = ((0,), (0,))


def mm(left, right, dims=NN):
    return lax.dot_general(left, right, (dims, ((), ())), preferred_element_type=f32)


def call(body, name, inputs, outs, scratch=(), flops=0, limit=32):
    arrays, specs, moved, fetched = [], [], 0, []
    for item in inputs:
        array, space = item if isinstance(item, tuple) else (item, VMEM)
        if space == "fetch":
            fetched.append(len(arrays))
            space = pltpu.HBM
        arrays.append(array)
        specs.append(pl.BlockSpec(memory_space=space))
        moved += array.size * array.dtype.itemsize
    for shape, kind in outs:
        size = jnp.dtype(kind).itemsize
        for extent in shape:
            size *= extent
        moved += size
    extra = [VMEM(arrays[k].shape, arrays[k].dtype) for k in fetched]
    if fetched:
        extra.append(pltpu.SemaphoreType.DMA((len(fetched),)))

    def whole(*refs):
        refs = list(refs)
        if fetched:
            held, sem = refs[-1 - len(fetched) : -1], refs[-1]
            refs = refs[: -1 - len(fetched)]
            transfers = []
            for n, k in enumerate(fetched):
                transfer = pltpu.make_async_copy(refs[k], held[n], sem.at[n])
                transfer.start()
                transfers.append(transfer)
                refs[k] = held[n]
            for transfer in transfers:
                transfer.wait()
        body(*refs)

    return pl.pallas_call(
        whole,
        name=name,
        out_shape=[jax.ShapeDtypeStruct(shape, kind) for shape, kind in outs],
        in_specs=specs,
        out_specs=[pl.BlockSpec(memory_space=VMEM)] * len(outs),
        scratch_shapes=list(scratch) + extra,
        compiler_params=pltpu.CompilerParams(vmem_limit_bytes=limit * MIB),
        cost_estimate=pl.CostEstimate(flops=flops, bytes_accessed=moved, transcendentals=0),
    )(*arrays)


def low_bits(index, size):
    return jnp.bitwise_and(index, size - 1)


def pair_weight_rows(w_pair, head_count, cols):
    rows = head_count * cols
    shift = cols.bit_length() - 1
    head = lax.shift_right_logical(
        lax.broadcasted_iota(jnp.int32, (rows, head_count), 0), jnp.int32(shift)
    )
    pick = (head == lax.broadcasted_iota(jnp.int32, (rows, head_count), 1)).astype(f32)
    spread = mm(pick.astype(bf16), w_pair)
    row_col = low_bits(lax.broadcasted_iota(jnp.int32, spread.shape, 0), cols)
    return spread, row_col


def enter_kernel(toks, cols, noisy, single, restype, table, gain, pair, pair_gain, w_pair, *rest):
    x_out, bias_out, rounded = rest
    rows = noisy.shape[0]
    pair_scaled, _, _ = layer_forward(pair[...].astype(f32), pair_gain[...])
    rounded[...] = pair_scaled.astype(bf16).astype(f32)
    head_count = w_pair.shape[0]
    spread, row_col = pair_weight_rows(w_pair[...], head_count, cols)
    total = jnp.zeros((head_count * cols, rows), f32)
    for j in range(cols):
        column = rounded[pl.ds(j, rows, stride=cols), :].astype(bf16)
        total = total + mm(jnp.where(row_col == j, spread, 0.0).astype(bf16), column, NT)
    bias = total.astype(bf16)
    part = bias_out.shape[1]
    for n in range(bias_out.shape[0]):
        t = n % toks
        bias_out[n] = bias[t * part : (t + 1) * part, :]

    normed_scaled, _, _ = layer_forward(noisy[...].astype(f32), gain[...])
    types = table.shape[0]
    onehot = (lax.broadcasted_iota(jnp.int32, (types, rows), 0) == restype[...]).astype(f32)
    condition = single[...].astype(f32) + mm(onehot.astype(bf16), table[...], TN)
    x_out[...] = (normed_scaled + condition).astype(bf16)


def own_slice(weight, t, own_width):
    if weight.shape[1] == own_width:
        return weight
    return weight.at[:, pl.ds(pl.multiple_of(t * own_width, own_width), own_width)]


def project_kernel(toks, own_width, ids, *rest):
    parts = rest[:toks]
    weights = rest[toks : toks + 3]
    x_out, outs = rest[toks + 3], rest[toks + 4 : toks + 7]
    held, sem = rest[toks + 7 :]
    t = ids[0]
    copies = []
    for k in range(3):
        copy = pltpu.make_async_copy(
            own_slice(weights[k], t, own_width), held.at[k], sem.at[k]
        )
        copy.start()
        copies.append(copy)
    rows = parts[0].shape[0]
    for r in range(toks):
        start = pl.multiple_of(jnp.bitwise_xor(t, r) * rows, rows)
        x_out[pl.ds(start, rows), :] = parts[r][...]
    x = x_out[...]
    for k in range(3):
        copies[k].wait()
        outs[k][...] = jnp.transpose(mm(x, held[k])).astype(bf16)


def attention_kernel(copies, toks, cols, head_width, ids, query, key, value, bias, *rest):
    chain, keymask, chain_weight, weights_out, att_out = rest[:5]
    pieces = rest[5 : 5 + toks]
    t = ids[0]
    own_heads = weights_out.shape[0]
    tokens = query.shape[1]
    rows = tokens // toks
    chain_row = chain[...]
    keep_row = keymask[...].astype(f32)
    line = lax.broadcasted_iota(jnp.int32, (128, tokens), 0)
    facts = jnp.where(line == 0, chain_row.astype(f32), 0.0) + jnp.where(line == 1, keep_row, 0.0)
    for h in range(own_heads):
        weight_row = jnp.zeros((1, tokens), f32)
        for m in range(chain_weight.shape[0]):
            weight_row = jnp.where(chain_row == m, chain_weight[m, t * own_heads + h], weight_row)
        facts = jnp.where(line == 2 + h, weight_row, facts)
    facts = jnp.transpose(facts)
    same = facts[:, 0:1] == chain_row.astype(f32)
    keep = facts[:, 1:2] > 0.0
    scale = head_width ** (-0.5)
    attended = []
    for h in range(own_heads):
        span = slice(h * head_width, (h + 1) * head_width)
        logits = mm(key[span, :], query[span, :], TN) * scale
        line = slice(h * cols, (h + 1) * cols)
        extra = jnp.concatenate(
            [
                jnp.concatenate([bias[c * toks + a, line, :] for c in range(copies)], axis=0)
                for a in range(toks)
            ],
            axis=1,
        ).astype(f32)
        logits = logits + (extra + jnp.where(same, facts[:, 2 + h : 3 + h], 0.0))
        logits = jnp.where(keep, logits, -1e30)
        exponent = jnp.exp(logits - jnp.max(logits, axis=0, keepdims=True))
        weights = exponent / jnp.sum(exponent, axis=0, keepdims=True)
        weights_b = weights.astype(bf16)
        weights_out[h] = weights_b
        attended.append(mm(value[span, :], weights_b))
    att_out[...] = jnp.transpose(jnp.concatenate(attended, axis=0)).astype(bf16)
    for r in range(toks):
        start = pl.multiple_of(jnp.bitwise_xor(t, r) * rows, rows)
        pieces[r][...] = att_out[pl.ds(start, rows), :]


def down_kernel(upstream, w_down, d_hidden):
    d_hidden[...] = mm(upstream[...], w_down[...], NT)


def hidden_kernel(toks, chunk, ids, noisy, upstream, d_hidden, gain, *rest):
    parts = rest[:toks]
    w_out, w_gate, w_up = rest[toks : toks + 3]
    d_res_out, d_res_b_out = rest[toks + 3 : toks + 5]
    d_att_outs = rest[toks + 5 : 2 * toks + 5]
    held_out, held_gate, held_up, sem = rest[2 * toks + 5 :]
    t = ids[0]
    hidden = w_gate.shape[1]
    first = pltpu.make_async_copy(w_out, held_out, sem.at[0])
    first.start()
    copies = []
    for k in range(hidden // chunk):
        span = pl.ds(k * chunk, chunk)
        pair = [
            pltpu.make_async_copy(w.at[:, span], held.at[:, span], sem.at[1 + 2 * k + n])
            for n, (w, held) in enumerate(((w_gate, held_gate), (w_up, held_up)))
        ]
        for copy in pair:
            copy.start()
        copies.append(pair)
    residual = noisy[...].astype(f32)
    first.wait()
    own_width = parts[0].shape[1]
    for r in range(toks):
        start = pl.multiple_of(jnp.bitwise_xor(t, r) * own_width, own_width)
        residual = residual + mm(parts[r][...], held_out[pl.ds(start, own_width), :])
    trans_scaled, trans_hat, trans_inverse = layer_forward(residual, gain[...])
    trans_in = trans_scaled.astype(bf16)
    d_trans = jnp.zeros(residual.shape, f32)
    for k in range(hidden // chunk):
        for copy in copies[k]:
            copy.wait()
        span = slice(k * chunk, (k + 1) * chunk)
        gate = mm(trans_in, held_gate[:, span])
        up = mm(trans_in, held_up[:, span])
        incoming = d_hidden[:, span]
        sigmoid = jax.nn.sigmoid(gate)
        d_up = (incoming * gate * sigmoid).astype(bf16)
        d_gate = (incoming * up * sigmoid * (1.0 + gate * (1.0 - sigmoid))).astype(bf16)
        d_trans = d_trans + mm(d_gate, held_gate[:, span], NT) + mm(d_up, held_up[:, span], NT)
    d_res = upstream[...].astype(f32) + layer_backward(
        d_trans, gain[...], trans_hat, trans_inverse
    )
    d_res_out[...] = d_res
    d_res_b = d_res.astype(bf16)
    d_res_b_out[...] = d_res_b
    for r in range(toks):
        start = pl.multiple_of(jnp.bitwise_xor(t, r) * own_width, own_width)
        d_att_outs[r][...] = mm(held_out[pl.ds(start, own_width), :], d_res_b, NT).astype(bf16)


def backward_kernel(copies, toks, cols, head_width, ids, query, key, value, weights, *rest):
    parts = rest[:toks]
    d_query, d_key, d_value, d_bias, blocks = rest[toks:]
    t = ids[0]
    rows = query.shape[1] // toks
    for r in range(toks):
        blocks[jnp.bitwise_xor(t, r)] = parts[r][...]
    d_att = jnp.concatenate([blocks[a] for a in range(toks)], axis=1)
    scale = head_width ** (-0.5)
    for h in range(weights.shape[0]):
        span = slice(h * head_width, (h + 1) * head_width)
        d_att_h = d_att[span, :]
        weights_b = weights[h]
        d_weights = mm(value[span, :], d_att_h, TN)
        weights_f = weights_b.astype(f32)
        delta = jnp.sum(weights_f * d_weights, axis=0, keepdims=True)
        d_logits_b = (weights_f * (d_weights - delta)).astype(bf16)
        for c in range(copies):
            for a in range(toks):
                d_bias[c * toks + a, h * cols : (h + 1) * cols, :] = d_logits_b[
                    c * cols : (c + 1) * cols, a * rows : (a + 1) * rows
                ]
        d_query[span, :] = (mm(key[span, :], d_logits_b) * scale).astype(bf16)
        d_key[span, :] = (mm(query[span, :], d_logits_b, NT) * scale).astype(bf16)
        d_value[span, :] = mm(d_att_h, weights_b, NT).astype(bf16)


def gradient_kernel(copies, toks, ids, x, att, d_query, d_key, d_value, *rest):
    d_res_parts = rest[:toks]
    weights = rest[toks : toks + 3]
    kept, sent, d_own = rest[toks + 3 : toks + 6]
    d_others = rest[toks + 6 : 2 * toks + 5]
    d_res, wide, narrow, d_inputs, held, sem = rest[2 * toks + 5 :]
    t, c = ids[0], ids[1]
    own_width, tokens = d_query.shape
    rows = tokens // toks
    width = x.shape[1]
    group = copies // toks
    transfers = []
    for k in range(3):
        copy = pltpu.make_async_copy(
            own_slice(weights[k], t, own_width), held.at[k], sem.at[k]
        )
        copy.start()
        transfers.append(copy)
    for r in range(toks):
        start = pl.multiple_of(jnp.bitwise_xor(t, r) * rows, rows)
        d_res[pl.ds(start, rows), :] = d_res_parts[r][...]
    for k, part in enumerate((d_query, d_key, d_value)):
        wide[k] = mm(part[...], x[...])
    narrow[...] = mm(d_res[...], att[...], TN)
    cut, depth = width // copies, width // toks
    near = low_bits(c, 2)
    for side, out in ((near, kept), (1 - near, sent)):
        for q in range(copies // 2):
            h = 2 * q // group
            first = pl.multiple_of((2 * q - h * group + side) * cut, 8)
            for k in range(3):
                out[q, k, :, :depth] = wide[
                    k, pl.ds(first, cut), h * depth : (h + 1) * depth
                ].astype(bf16)
            first = pl.multiple_of((2 * q + side) * cut, 8)
            out[q, 3, :, :own_width] = narrow[pl.ds(first, cut), :].astype(bf16)
            if out.shape[3] > own_width:
                out[q, :, :, own_width:] = jnp.zeros(
                    (4, cut, out.shape[3] - own_width), bf16
                )
    total = None
    for k, part in enumerate((d_query, d_key, d_value)):
        transfers[k].wait()
        term = mm(held[k], part[...])
        total = term if total is None else total + term
    for a in range(toks):
        d_inputs[a] = total[:, a * rows : (a + 1) * rows]
    d_own[...] = d_inputs[t]
    for r in range(1, toks):
        d_others[r - 1][...] = d_inputs[jnp.bitwise_xor(t, r)].astype(bf16)


def halve_kernel(toks, copies, ids, kept, got, d_own, *rest):
    others = rest[: toks - 1]
    kept_out, sent_out, total_ref = rest[toks - 1 :]
    total = d_own[...]
    for part in others:
        total = total + part[...].astype(f32)
    total_ref[...] = total
    bit = low_bits(ids[1] // 2, 2)
    rows = total.shape[1]
    cut = total.shape[0] // copies
    per = kept_out.shape[3] // rows
    for q in range(kept_out.shape[0]):
        for side, out in ((bit, kept_out), (1 - bit, sent_out)):
            k = 2 * q + side
            out[q, :4] = (kept[k].astype(f32) + got[k].astype(f32)).astype(bf16)
            if per > 2:
                out[q, 4, :, 2 * rows :] = jnp.zeros((cut, out.shape[3] - 2 * rows), bf16)
            for low in range(2):
                start = pl.multiple_of((q * 4 + side * 2 + low) * cut, 8)
                lane = low % per * rows
                out[q, 4 + low // per, :, lane : lane + rows] = total_ref[
                    pl.ds(start, cut), :
                ].astype(bf16)


def spread_kernel(near, ids, kept, got, *outs):
    z = ids[1] // near
    for r, out in enumerate(outs):
        k = jnp.bitwise_xor(z, r)
        out[...] = (kept[k].astype(f32) + got[k].astype(f32)).astype(bf16)


def collect_kernel(count, ids, *refs):
    parts, (moved, final, kept, sent, halves) = refs[:count], refs[count:]

    def total(k):
        whole = parts[0][k].astype(f32)
        for part in parts[1:]:
            whole = whole + part[k].astype(f32)
        return whole

    for k in range(3):
        moved[k] = total(k).astype(bf16)
    final[...] = total(3)[:, : final.shape[1]]
    rows = kept.shape[1]
    per = parts[0].shape[2] // rows
    for low in range(2):
        lane = low % per * rows
        halves[low] = total(4 + low // per)[:, lane : lane + rows].astype(bf16)
    bit = low_bits(ids[1], 2)
    kept[...] = halves[bit]
    sent[...] = halves[1 - bit]


def finish_kernel(moved, kept_single, got_single, first, second, third, single):
    for k, out in enumerate((first, second, third)):
        out[...] = moved[k][:, : out.shape[1]].astype(f32)
    single[...] = kept_single[...].astype(f32) + got_single[...].astype(f32)


def exit_kernel(toks, noisy, gain, d_res, d_own, *rest):
    others, (grad_noisy,) = rest[: toks - 1], rest[toks - 1 :]
    total = d_own[...]
    for part in others:
        total = total + part[...].astype(f32)
    _, noisy_hat, noisy_inverse = layer_forward(noisy[...].astype(f32), gain[...])
    grad_noisy[...] = (
        d_res[...] + layer_backward(jnp.transpose(total), gain[...], noisy_hat, noisy_inverse)
    ).astype(bf16)


def pair_kernel(toks, cols, pair, gain, w_pair, parts, grad_pair, weight_grad, *scratch):
    rounded, spread_out = scratch
    head_count = w_pair.shape[0]
    rows = parts.shape[2]
    sums = []
    for t in range(toks):
        total = parts[t].astype(f32)
        for n in range(t + toks, parts.shape[0], toks):
            total = total + parts[n].astype(f32)
        sums.append(total)
    grad = jnp.concatenate(sums, axis=0)
    pair_scaled, pair_hat, pair_inverse = layer_forward(pair[...].astype(f32), gain[...])
    rounded[...] = pair_scaled.astype(bf16).astype(f32)
    spread, row_col = pair_weight_rows(w_pair[...], head_count, cols)
    grad_b = grad.astype(bf16)
    turned = jnp.transpose(grad).astype(bf16)
    sums = jnp.zeros(spread.shape, f32)
    for j in range(cols):
        here = row_col == j
        column = rounded[pl.ds(j, rows, stride=cols), :].astype(bf16)
        sums = sums + jnp.where(here, mm(grad_b, column), 0.0)
        spread_out[pl.ds(j, rows, stride=cols), :] = mm(
            turned, jnp.where(here, spread, 0.0).astype(bf16)
        )
    grad_pair[...] = layer_backward(
        spread_out[...], gain[...], pair_hat, pair_inverse
    ).astype(bf16)
    for h in range(head_count):
        line = jnp.sum(sums[h * cols : (h + 1) * cols, :], axis=0, keepdims=True)
        for n in range(weight_grad.shape[0]):
            weight_grad[n, h : h + 1, :] = line


def swap_copy(value, mask):
    size = lax.axis_size("copy")
    return lax.ppermute(value, "copy", [(i, i ^ mask) for i in range(size)])


def swap_tok(value, mask):
    size = lax.axis_size("tok")
    return lax.ppermute(value, "tok", [(i, i ^ mask) for i in range(size)])


def exchange(value):
    return lax.all_to_all(value, ("copy", "tok"), 0, 0)


def per_device(
    noisy,
    single,
    pair,
    restype,
    chain,
    keymask,
    restype_table,
    norm_gain,
    pair_gain,
    trans_gain,
    w_query,
    w_key,
    w_value,
    w_out,
    w_pair,
    chain_weight,
    w_hidden_gate,
    w_hidden_up,
    w_down,
    cotangent,
):
    copies = lax.axis_size("copy")
    toks = lax.axis_size("tok")
    _, rows, width = noisy.shape
    cols = pair.shape[1]
    channels = pair.shape[2]
    heads = w_pair.shape[1]
    head_width = width // heads
    own_heads = heads // toks
    own_width = own_heads * head_width
    tokens = rows * toks
    hidden = w_down.shape[0]
    near = 4
    far = copies // near
    cut = width // copies
    lanes = max(own_width, rows)
    devices = copies * toks
    ids = jnp.stack([lax.axis_index("tok"), lax.axis_index("copy")]).astype(jnp.int32)
    where_am_i = (ids, SMEM)
    noisy2 = (noisy.reshape(rows, width), "fetch")
    upstream = (cotangent.reshape(rows, width), "fetch")
    pair2 = (pair.reshape(rows * cols, channels), "fetch")
    norm_gain2 = (norm_gain.reshape(1, width), "fetch")
    trans_gain2 = (trans_gain.reshape(1, width), "fetch")
    pair_gain2 = (pair_gain.reshape(1, channels), "fetch")
    w_pair2 = (w_pair.T, "fetch")

    x_own, bias_out = call(
        functools.partial(enter_kernel, toks, cols),
        "enter",
        [noisy2, (single, "fetch"), (restype.reshape(1, rows), "fetch"), (restype_table, "fetch")]
        + [norm_gain2, pair2, pair_gain2, w_pair2],
        [((rows, width), bf16), ((devices, own_heads * cols, rows), bf16)],
        [VMEM((rows * cols, channels), f32)],
        flops=2 * heads * cols * rows * channels * cols,
    )
    x_parts = [x_own] + [swap_tok(x_own, r) for r in range(1, toks)]
    bias = exchange(bias_out)

    weights3 = [w_query, w_key, w_value]
    if own_width % 128:
        weights3 = [
            lax.dynamic_slice_in_dim(w, ids[0] * own_width, own_width, axis=1) for w in weights3
        ]
    x, query, key, value = call(
        functools.partial(project_kernel, toks, own_width),
        "project",
        [where_am_i] + x_parts + [(w, pltpu.HBM) for w in weights3],
        [((tokens, width), bf16)] + [((own_width, tokens), bf16)] * 3,
        [VMEM((3, width, own_width), bf16), pltpu.SemaphoreType.DMA((3,))],
        flops=6 * tokens * width * own_width,
    )
    done = call(
        functools.partial(attention_kernel, copies, toks, cols, head_width),
        "attention",
        [where_am_i, query, key, value, bias]
        + [(chain.reshape(1, tokens), "fetch"), (keymask.reshape(1, tokens), "fetch")]
        + [(chain_weight, SMEM)],
        [((own_heads, tokens, tokens), bf16), ((tokens, own_width), bf16)]
        + [((rows, own_width), bf16)] * toks,
        flops=4 * tokens * tokens * own_width,
    )
    weights, att, pieces = done[0], done[1], done[2:]
    att_parts = [pieces[0]] + [swap_tok(pieces[r], r) for r in range(1, toks)]

    (d_hidden,) = call(
        down_kernel,
        "down",
        [upstream, (w_down, "fetch")],
        [((rows, hidden), f32)],
        flops=2 * rows * hidden * width,
    )
    chunk = hidden // 3
    after = call(
        functools.partial(hidden_kernel, toks, chunk),
        "hidden",
        [where_am_i, noisy2, upstream, d_hidden, trans_gain2]
        + att_parts
        + [(w_out, ANY), (w_hidden_gate, ANY), (w_hidden_up, ANY)],
        [((rows, width), f32), ((rows, width), bf16)] + [((own_width, rows), bf16)] * toks,
        [
            VMEM((width, width), bf16),
            VMEM((width, hidden), bf16),
            VMEM((width, hidden), bf16),
            pltpu.SemaphoreType.DMA((7,)),
        ],
        flops=2 * rows * width * (2 * width + 4 * hidden),
    )
    d_res, d_res_b, d_att = after[0], after[1], after[2:]
    d_att_parts = [d_att[0]] + [swap_tok(d_att[r], r) for r in range(1, toks)]
    d_res_parts = [d_res_b] + [swap_tok(d_res_b, r) for r in range(1, toks)]

    d_query, d_key, d_value, d_bias = call(
        functools.partial(backward_kernel, copies, toks, cols, head_width),
        "backward",
        [where_am_i, query, key, value, weights] + d_att_parts,
        [((own_width, tokens), bf16)] * 3 + [((devices, own_heads * cols, rows), bf16)],
        [VMEM((toks, own_width, rows), bf16)],
        flops=8 * tokens * tokens * own_width,
    )
    found = call(
        functools.partial(gradient_kernel, copies, toks),
        "gradient",
        [where_am_i, x, att, d_query, d_key, d_value]
        + d_res_parts
        + [(w, ANY) for w in weights3],
        [((copies // 2, 4, cut, lanes), bf16)] * 2
        + [((width, rows), f32)]
        + [((width, rows), bf16)] * (toks - 1),
        [
            VMEM((tokens, width), bf16),
            VMEM((3, own_width, width), f32),
            VMEM((width, own_width), f32),
            VMEM((toks, width, rows), f32),
            VMEM((3, width, own_width), bf16),
            pltpu.SemaphoreType.DMA((3,)),
        ],
        flops=14 * tokens * width * own_width,
    )
    kept, sent, d_own = found[:3]
    d_others = [swap_tok(found[2 + r], r) for r in range(1, toks)]
    got = swap_copy(sent, 1)

    slots = 4 + (1 if lanes >= 2 * rows else 2)
    kept, sent = call(
        functools.partial(halve_kernel, toks, copies),
        "halve",
        [where_am_i, kept, got, d_own] + d_others,
        [((far, slots, cut, lanes), bf16)] * 2,
        [VMEM((width, rows), f32)],
    )
    got = swap_copy(sent, 2)
    d_bias = exchange(d_bias)
    (grad_noisy,) = call(
        functools.partial(exit_kernel, toks),
        "exit",
        [noisy2, norm_gain2, d_res, d_own] + d_others,
        [((rows, width), bf16)],
    )
    grad_pair, weight_grad = call(
        functools.partial(pair_kernel, toks, cols),
        "pair",
        [pair2, pair_gain2, w_pair2, d_bias],
        [((rows * cols, channels), bf16), ((devices, heads, channels), f32)],
        [VMEM((rows * cols, channels), f32)] * 2,
        flops=4 * heads * cols * rows * channels * cols,
    )
    weight_grad = jnp.sum(exchange(weight_grad), axis=0)

    spread = call(
        functools.partial(spread_kernel, near),
        "spread",
        [where_am_i, kept, got],
        [((slots, cut, lanes), bf16)] * far,
    )
    arrived = [spread[0]] + [swap_copy(spread[r], r * near) for r in range(1, far)]
    moved, grad_out, last_kept, last_sent = call(
        functools.partial(collect_kernel, far),
        "collect",
        [where_am_i] + arrived,
        [((3, cut, lanes), bf16), ((cut, own_width), f32)] + [((cut, rows), bf16)] * 2,
        [VMEM((2, cut, rows), bf16)],
    )
    last_got = swap_copy(last_sent, 1)
    group = copies // toks
    pairs = []
    for c in range(copies):
        for t in range(toks):
            pairs.append((c * toks + t, (t * group + c % group) * toks + c // group))
    moved = lax.ppermute(moved, ("copy", "tok"), pairs)
    grad_query, grad_key, grad_value, grad_single = call(
        finish_kernel,
        "finish",
        [moved, last_kept, last_got],
        [((cut, own_width), f32)] * 3 + [((cut, rows), f32)],
    )
    return (
        grad_noisy[None],
        grad_single.T,
        grad_pair.reshape(rows, cols, channels),
        grad_query.T,
        grad_key.T,
        grad_value.T,
        grad_out.T,
        weight_grad.T,
    )


def solution(mesh):
    placed = (
        P("copy", "tok", None),
        P("tok", None),
        P("tok", "copy", None),
        P("tok"),
    ) + (P(),) * 15 + (P("copy", "tok", None),)
    return jax.shard_map(
        per_device,
        mesh=mesh,
        in_specs=placed,
        out_specs=(
            P("copy", "tok", None),
            P("tok", "copy"),
            P("tok", "copy", None),
            P("tok", "copy"),
            P("tok", "copy"),
            P("tok", "copy"),
            P("tok", "copy"),
            P(),
        ),
        check_vma=False,
    )
```

time: 150 us -> 143 us (0.953)
  starting transfers between devices: 59.1 us -> 38.7 us
  local copies, waits for them, and re-layouts: 15.7 us -> 21.8 us
  Pallas kernels: 27.6 us -> 31.5 us
  waiting for transfers between devices: 44.5 us -> 47.5 us
    ppermute x21 -> x0, starting transfers between devices: 32.3 us -> none  [swap_both(): return lax.ppermute(value, ('copy', 'tok'), pairs)]
    all_to_all x0 -> x3, starting transfers between devices: none -> 19.1 us  [exchange(): return lax.all_to_all(value, ('copy', 'tok'), 0, 0)]
    ppermute x4 -> x5, waiting for transfers between devices: 11 us -> 26.1 us  [swap_tok(): return lax.ppermute(value, 'tok', [(i, i ^ mask) for i in range(size)])]
    ppermute x21 -> x0, waiting for transfers between devices: 11.8 us -> none  [swap_both(): return lax.ppermute(value, ('copy', 'tok'), pairs)]
    ppermute x19 -> x6, starting transfers between devices: 15.8 us -> 6.26 us  [swap_copy(): return lax.ppermute(value, 'copy', [(i, i ^ mask) for i in range(size)])]
    unnamed x63 -> x84, local copies, waits for them, and re-layouts: 14.9 us -> 20.4 us
    pallas_call x16 -> x13, Pallas kernels: 27.6 us -> 31.5 us  [call(): pl.pallas_call(whole, name=name, out_shape=[jax.ShapeDtypeStruct(shape, k...]
    ppermute x1, waiting for transfers between devices: 4.29 us -> 0.49 us  [per_device(): moved = lax.ppermute(moved, ('copy', 'tok'), pairs)]
  transfers between devices with their start and end apart: 45 -> 15, of which waited for: 19 -> 6; matrix products, arithmetic and copies ran while one was open for 1% -> 1% of each run, Pallas kernels for 7% -> 11%
where the time goes in v3:
time: 143 us; the launch traced here: 141 us
  waiting for transfers between devices  47.5 us (33%)
  starting transfers between devices  38.7 us (27%)
  Pallas kernels  31.5 us (22%)
  local copies, waits for them, and re-layouts  21.8 us (15%)
    pallas_call x13, Pallas kernels, call(): pl.pallas_call(whole, name=name, out_shape=[jax.ShapeDtypeStruct(shape, k...  31.5 us
    ppermute x5, waiting for transfers between devices, swap_tok(): return lax.ppermute(value, 'tok', [(i, i ^ mask) for i in range(size)])  26.1 us
    ppermute x6, waiting for transfers between devices, swap_copy(): return lax.ppermute(value, 'copy', [(i, i ^ mask) for i in range(size)])  20.9 us
    unnamed x84, local copies, waits for them, and re-layouts  20.4 us
    all_to_all x3, starting transfers between devices, exchange(): return lax.all_to_all(value, ('copy', 'tok'), 0, 0)  19.1 us
    ppermute x1, starting transfers between devices, per_device(): moved = lax.ppermute(moved, ('copy', 'tok'), pairs)  8.35 us
    ppermute x6, starting transfers between devices, swap_copy(): return lax.ppermute(value, 'copy', [(i, i ^ mask) for i in range(size)])  6.26 us
    ppermute x5, starting transfers between devices, swap_tok(): return lax.ppermute(value, 'tok', [(i, i ^ mask) for i in range(size)])  4.9 us
  transfers between devices with their start and end apart: 15, of which 6 were waited for; matrix products, arithmetic and copies ran while one was open for 1% of the time, Pallas kernels for 11%

profile of v3, /device:TPU:2, one launch (start us, length us, event | category | flops | bytes accessed | tf_op | source)
XLA Modules:
  0.0 141.2 jit_solution(9023423823527719293)
XLA Ops:
  0.6 0.8 reshape.47.refs_4_.refs_1_
  1.4 1.0 copy-done.8
  2.5 0.9 copy-done.10
  3.4 0.9 copy-done.32
  4.3 0.8 copy-done.33
  5.1 0.7 copy-done.34
  5.8 0.7 copy-done.37
  6.5 0.7 copy-done.41
  7.1 2.7 %enter.1 = (bf16[128,768]{1,0:T(8,128)(2,1)S(1)}, bf16[32,64,128]{2,1,0:T(8,128)(2,1)}) custom-call(bf16[128,768]{1,0:T(8,128)(2,1)S(1)} %bitcast.20, bf16[128,768]{1,0:T(8,128)(2,1)S(1)} %copy-done.32, s32[1,128]{1,0:T(1,128)S(1)} %bitcast.31, bf16[32,768]{1,0:T(8,128)(2,1)S(1)} %copy-done.33, f32[1,768]{1,0:T(1,128)S(1)} %reshape.47.refs_4_.refs_1_, ...), custom_call_target="tpu_custom_call" | custom-call | flops 67108864 | bytes 1693696 | tf_op jit(solution)/shard_map/enter/pallas_call | solution.py:75
  9.9 6.2 %all-to-all-start = ((bf16[32,64,128]{2,1,0:T(8,128)(2,1)}), bf16[32,64,128]{2,1,0:T(8,128)(2,1)}, u32[]{:S(2)}, u32[]{:S(2)}) async-start(bf16[32,64,128]{2,1,0:T(8,128)(2,1)} %get-tuple-element.50), calls=%async_computation | async-start | bytes 1048576 | tf_op jit(solution)/shard_map/all_to_all | solution.py:450
  16.1 0.4 collective-permute-start
  16.5 0.1 pad_add_fusion.refs_0_
  16.6 9.9 %collective-permute-done.refs_2_ = bf16[128,768]{1,0:T(8,128)(2,1)S(1)} collective-permute-done((bf16[128,768]{1,0:T(8,128)(2,1)S(1)}, bf16[128,768]{1,0:T(8,128)(2,1)S(1)}, u32[]{:S(2)}, u32[]{:S(2)}) %collective-permute-start) | collective-permute-done | bytes 196640 | tf_op jit(solution)/shard_map/ppermute | solution.py:446
  26.4 0.7 copy-done.30
  27.1 1.3 copy-done.1
  28.4 1.3 copy-done.3
  29.7 0.9 copy-done.29
  30.6 0.9 copy-done.31
  31.5 2.1 %project.1 = (bf16[256,768]{1,0:T(8,128)(2,1)S(1)}, bf16[384,256]{1,0:T(8,128)(2,1)S(1)}, bf16[384,256]{1,0:T(8,128)(2,1)S(1)}, bf16[384,256]{1,0:T(8,128)(2,1)S(1)}) custom-call(s32[2]{0:T(128)S(1)} %pad_add_fusion.refs_0_, bf16[128,768]{1,0:T(8,128)(2,1)S(1)} %copy-done.29, bf16[128,768]{1,0:T(8,128)(2,1)S(1)} %copy-done.31, bf16[768,768]{1,0:T(8,128)(2,1)S(1)} %copy-done, ...), custom_call_target="tpu_custom_call" | custom-call | flops 452984832 | bytes 4915208 | tf_op jit(solution)/shard_map/project/pallas_call | solution.py:75
  33.7 0.0 copy-start.14
  33.7 0.7 copy-done.14
  34.3 0.7 copy-done.17
  35.0 0.7 copy-done.20
  35.7 0.7 copy-done.26
  36.5 0.0 copy-start.15
  36.5 0.9 copy-done.15
  37.4 0.9 copy-done.18
  38.3 0.9 copy-done.21
  39.3 0.7 copy-done.40
  39.9 2.8 %attention.1 = (bf16[4,256,256]{2,1,0:T(8,128)(2,1)S(1)}, bf16[256,384]{1,0:T(8,128)(2,1)S(1)}, bf16[128,384]{1,0:T(8,128)(2,1)S(1)}, bf16[128,384]{1,0:T(8,128)(2,1)S(1)}) custom-call(s32[2]{0:T(128)S(1)} %pad_add_fusion.refs_0_, bf16[384,256]{1,0:T(8,128)(2,1)S(1)} %copy-done.15, bf16[384,256]{1,0:T(8,128)(2,1)S(1)} %copy-done.18, ...), custom_call_target="tpu_custom_call" | custom-call | flops 100663296 | bytes 2033864 | tf_op jit(solution)/shard_map/attention/pallas_call | solution.py:75
  42.8 1.9 %collective-permute-start.1 = (bf16[128,384]{1,0:T(8,128)(2,1)S(1)}, bf16[128,384]{1,0:T(8,128)(2,1)S(1)}, u32[]{:S(2)}, u32[]{:S(2)}) collective-permute-start(bf16[128,384]{1,0:T(8,128)(2,1)S(1)} %get-tuple-element.52), channel_id=1, source_target_pairs={{0,1},{1,0},{2,3},{3,2},{4,5},{5,4},{6,7},{7,6},{8,9},{9,8},{10,11... | collective-permute-start | bytes 294920 | tf_op jit(solution)/shard_map/ppermute | solution.py:446
  44.7 0.7 reshape.49.refs_4_
  45.4 1.7 %copy-done.7 = bf16[1536,768]{1,0:T(8,128)(2,1)S(1)} copy-done((bf16[1536,768]{1,0:T(8,128)(2,1)S(1)}, bf16[1536,768]{1,0:T(8,128)(2,1)}, u32[]{:S(2)}) %copy-start.7) | copy-done | bytes 2359320
  47.1 1.3 down.1.refs_3_
  48.4 0.3 copy-done.5
  48.7 1.3 copy-done.13
  50.0 6.0 %hidden.1 = (f32[128,768]{1,0:T(8,128)S(1)}, bf16[128,768]{1,0:T(8,128)(2,1)S(1)}, bf16[384,128]{1,0:T(8,128)(2,1)S(1)}, bf16[384,128]{1,0:T(8,128)(2,1)S(1)}) custom-call(s32[2]{0:T(128)S(1)} %pad_add_fusion.refs_0_, bf16[128,768]{1,0:T(8,128)(2,1)S(1)} %bitcast.21, bf16[128,768]{1,0:T(8,128)(2,1)S(1)} %bitcast.24, f32[128,1536]{1,0:T(8,128)S(1)} %down.1.refs_3_, ...), custom_call_target="tpu_custom_call" | custom-call | flops 1509949440 | bytes 8064008 | tf_op jit(solution)/shard_map/hidden/pallas_call | solution.py:75
  56.0 0.0 copy-start.2
  56.0 0.7 collective-permute-start.3
  56.7 1.4 %collective-permute-start.2 = (bf16[384,128]{1,0:T(8,128)(2,1)S(1)}, bf16[384,128]{1,0:T(8,128)(2,1)S(1)}, u32[]{:S(2)}, u32[]{:S(2)}) collective-permute-start(bf16[384,128]{1,0:T(8,128)(2,1)S(1)} %get-tuple-element.58), channel_id=1, source_target_pairs={{0,1},{1,0},{2,3},{3,2},{4,5},{5,4},{6,7},{7,6},{8,9},{9,8},{10,11... | collective-permute-start | bytes 294920 | tf_op jit(solution)/shard_map/ppermute | solution.py:446
  58.1 6.3 %collective-permute-done.2.refs_6_ = bf16[384,128]{1,0:T(8,128)(2,1)S(1)} collective-permute-done((bf16[384,128]{1,0:T(8,128)(2,1)S(1)}, bf16[384,128]{1,0:T(8,128)(2,1)S(1)}, u32[]{:S(2)}, u32[]{:S(2)}) %collective-permute-start.2) | collective-permute-done | bytes 98336 | tf_op jit(solution)/shard_map/ppermute | solution.py:446
  64.5 2.7 %backward.1 = (bf16[384,256]{1,0:T(8,128)(2,1)S(1)}, bf16[384,256]{1,0:T(8,128)(2,1)S(1)}, bf16[384,256]{1,0:T(8,128)(2,1)S(1)}, bf16[32,64,128]{2,1,0:T(8,128)(2,1)}) custom-call(s32[2]{0:T(128)S(1)} %pad_add_fusion.refs_0_, bf16[384,256]{1,0:T(8,128)(2,1)S(1)} %copy-done.16, bf16[384,256]{1,0:T(8,128)(2,1)S(1)} %copy-done.19, ...), custom_call_target="tpu_custom_call" | custom-call | flops 201326592 | bytes 2424840 | tf_op jit(solution)/shard_map/backward/pallas_call | solution.py:75
  67.1 4.4 %gradient.1 = (bf16[8,4,48,384]{3,2,1,0:T(8,128)(2,1)S(1)}, bf16[8,4,48,384]{3,2,1,0:T(8,128)(2,1)}, f32[768,128]{1,0:T(8,128)S(1)}, bf16[768,128]{1,0:T(8,128)(2,1)S(1)}) custom-call(s32[2]{0:T(128)S(1)} %pad_add_fusion.refs_0_, bf16[256,768]{1,0:T(8,128)(2,1)S(1)} %copy-done.27, bf16[256,384]{1,0:T(8,128)(2,1)S(1)} %get-tuple-element.55.refs_2_, ...), custom_call_target="tpu_custom_call" | custom-call | flops 1056964608 | bytes 8060936 | tf_op jit(solution)/shard_map/gradient/pallas_call | solution.py:75
  71.5 0.1 collective-permute-start.5
  71.6 6.5 %all-to-all-start.1 = ((bf16[32,64,128]{2,1,0:T(8,128)(2,1)}), bf16[32,64,128]{2,1,0:T(8,128)(2,1)S(1)}, u32[]{:S(2)}, u32[]{:S(2)}) async-start(bf16[32,64,128]{2,1,0:T(8,128)(2,1)} %get-tuple-element.77), calls=%async_computation.1 | async-start | bytes 1048576 | tf_op jit(solution)/shard_map/all_to_all | solution.py:450
  78.1 0.5 collective-permute-start.4
  78.6 9.9 %collective-permute-done.4.refs_4_ = bf16[768,128]{1,0:T(8,128)(2,1)S(1)} collective-permute-done((bf16[768,128]{1,0:T(8,128)(2,1)S(1)}, bf16[768,128]{1,0:T(8,128)(2,1)S(1)}, u32[]{:S(2)}, u32[]{:S(2)}) %collective-permute-start.4) | collective-permute-done | bytes 196640 | tf_op jit(solution)/shard_map/ppermute | solution.py:446
  88.6 1.8 %halve.1 = (bf16[4,5,48,384]{3,2,1,0:T(8,128)(2,1)S(1)}, bf16[4,5,48,384]{3,2,1,0:T(8,128)(2,1)S(1)}) custom-call(s32[2]{0:T(128)S(1)} %pad_add_fusion.refs_0_, bf16[8,4,48,384]{3,2,1,0:T(8,128)(2,1)S(1)} %get-tuple-element.65.refs_1_, bf16[8,4,48,384]{3,2,1,0:T(8,128)(2,1)} %collective-permute-done.5.refs_2_, f32[768,128]{1,0:T(8,128)S(1)} %get-tuple-element.63.refs_3_, ...), custom_call_target="tpu_custom_call" | custom-call | bytes 4423688 | tf_op jit(solution)/shard_map/halve/pallas_call | solution.py:75
  90.3 1.7 %collective-permute-start.6 = (bf16[4,5,48,384]{3,2,1,0:T(8,128)(2,1)S(1)}, bf16[4,5,48,384]{3,2,1,0:T(8,128)(2,1)S(1)}, u32[]{:S(2)}, u32[]{:S(2)}) collective-permute-start(bf16[4,5,48,384]{3,2,1,0:T(8,128)(2,1)S(1)} %get-tuple-element.68), channel_id=1, source_target_pairs={{0,4},{2,6},{4,0},{6,2},{8,12},{10,14},{12,8},{14,10},{16,20},{18,... | collective-permute-start | bytes 2211848 | tf_op jit(solution)/shard_map/ppermute | solution.py:441
  92.1 16.8 %collective-permute-done.6.refs_2_ = bf16[4,5,48,384]{3,2,1,0:T(8,128)(2,1)S(1)} collective-permute-done((bf16[4,5,48,384]{3,2,1,0:T(8,128)(2,1)S(1)}, bf16[4,5,48,384]{3,2,1,0:T(8,128)(2,1)S(1)}, u32[]{:S(2)}, u32[]{:S(2)}) %collective-permute-start.6) | collective-permute-done | bytes 737312 | tf_op jit(solution)/shard_map/ppermute | solution.py:441
  108.8 1.4 spread.1
  110.2 1.6 %collective-permute-start.7 = (bf16[5,48,384]{2,1,0:T(8,128)(2,1)}, bf16[5,48,384]{2,1,0:T(8,128)(2,1)S(1)}, u32[]{:S(2)}, u32[]{:S(2)}) collective-permute-start(bf16[5,48,384]{2,1,0:T(8,128)(2,1)} %get-tuple-element.70), channel_id=1, source_target_pairs={{0,8},{2,10},{4,12},{6,14},{8,0},{10,2},{12,4},{14,6},{16,24},{18,... | collective-permute-start | bytes 552968 | tf_op jit(solution)/shard_map/ppermute | solution.py:441
  111.8 2.5 %collective-permute-start.8 = (bf16[5,48,384]{2,1,0:T(8,128)(2,1)}, bf16[5,48,384]{2,1,0:T(8,128)(2,1)S(1)}, u32[]{:S(2)}, u32[]{:S(2)}) collective-permute-start(bf16[5,48,384]{2,1,0:T(8,128)(2,1)} %get-tuple-element.71), channel_id=1, source_target_pairs={{0,16},{2,18},{4,20},{6,22},{8,24},{10,26},{12,28},{14,30},{16,0},... | collective-permute-start | bytes 552968 | tf_op jit(solution)/shard_map/ppermute | solution.py:441
  114.3 0.3 collective-permute-start.9
  114.6 3.0 %pair.1 = (bf16[2048,128]{1,0:T(8,128)(2,1)}, f32[32,8,128]{2,1,0:T(8,128)}) custom-call(bf16[2048,128]{1,0:T(8,128)(2,1)S(1)} %bitcast.19, f32[1,128]{1,0:T(1,128)S(1)} %bitcast.28, bf16[8,128]{1,0:T(8,128)(2,1)S(1)} %bitcast.26, bf16[32,64,128]{2,1,0:T(8,128)(2,1)S(1)} %all-to-all-done.1.refs_3_), custom_call_target="tpu_custom_call" | custom-call | flops 134217728 | bytes 1706496 | tf_op jit(solution)/shard_map/pair/pallas_call | solution.py:75
  117.6 6.4 %all-to-all-start.2 = ((f32[32,8,128]{2,1,0:T(8,128)}), f32[32,8,128]{2,1,0:T(8,128)S(1)}, u32[]{:S(2)}, u32[]{:S(2)}) async-start(f32[32,8,128]{2,1,0:T(8,128)} %get-tuple-element.83), calls=%async_computation.2 | async-start | bytes 262144 | tf_op jit(solution)/shard_map/all_to_all | solution.py:450
  124.0 4.1 %collective-permute-done.8.refs_3_ = bf16[5,48,384]{2,1,0:T(8,128)(2,1)S(1)} collective-permute-done((bf16[5,48,384]{2,1,0:T(8,128)(2,1)}, bf16[5,48,384]{2,1,0:T(8,128)(2,1)S(1)}, u32[]{:S(2)}, u32[]{:S(2)}) %collective-permute-start.8) | collective-permute-done | bytes 184352 | tf_op jit(solution)/shard_map/ppermute | solution.py:441
  128.2 1.3 collect.1
  129.4 8.4 %collective-permute-start.10 = (bf16[3,48,384]{2,1,0:T(8,128)(2,1)S(1)}, bf16[3,48,384]{2,1,0:T(8,128)(2,1)S(1)}, u32[]{:S(2)}, u32[]{:S(2)}) collective-permute-start(bf16[3,48,384]{2,1,0:T(8,128)(2,1)S(1)} %get-tuple-element.73), channel_id=1, source_target_pairs={{0,0},{1,16},{2,2},{3,18},{4,4},{5,20},{6,6},{7,22},{8,8},{9,24},{... | collective-permute-start | bytes 331784 | tf_op jit(solution)/shard_map/ppermute | solution.py:643
  137.8 0.1 collective-permute-start.11
  137.9 1.5 %exit.1 = bf16[128,768]{1,0:T(8,128)(2,1)} custom-call(bf16[128,768]{1,0:T(8,128)(2,1)S(1)} %bitcast.22, f32[1,768]{1,0:T(1,128)S(1)} %reshape.47.refs_4_.refs_1_, f32[128,768]{1,0:T(8,128)S(1)} %copy-done.25, f32[768,128]{1,0:T(8,128)S(1)} %get-tuple-element.63.refs_3_, bf16[768,128]{1,0:T(8,128)(2,1)S(1)} %collective-permute-done.4.refs_4_), custom_call_target="tpu_custom_call" | custom-call | bytes 1379328 | tf_op jit(solution)/shard_map/exit/pallas_call | solution.py:75
  139.4 0.6 reduce_sum.9
  140.0 0.5 collective-permute-done.10.refs_0_
  140.5 0.7 finish.1
  (67 shorter events, 0.1 us)
Async XLA Ops:
  0.6 26.5 %copy-start = (bf16[768,768]{1,0:T(8,128)(2,1)S(1)}, bf16[768,768]{1,0:T(8,128)(2,1)}, u32[]{:S(2)}) copy-start(bf16[768,768]{1,0:T(8,128)(2,1)} %refs_8_.3) | copy-start | bytes 3538948
  1.4 1.0 copy-start.8
  2.5 0.9 copy-start.10
  3.4 0.9 copy-start.32
  4.3 0.8 copy-start.33
  5.1 0.7 copy-start.34
  5.8 0.7 copy-start.37
  6.5 0.7 copy-start.41
  9.9 6.7 %copy-start.28 = (bf16[128,768]{1,0:T(8,128)(2,1)}, bf16[128,768]{1,0:T(8,128)(2,1)S(1)}, u32[]{:S(2)}) copy-start(bf16[128,768]{1,0:T(8,128)(2,1)S(1)} %get-tuple-element.46.refs_1_) | copy-start | bytes 589828
  9.9 26.6 %all-to-all-start = ((bf16[32,64,128]{2,1,0:T(8,128)(2,1)}), bf16[32,64,128]{2,1,0:T(8,128)(2,1)}, u32[]{:S(2)}, u32[]{:S(2)}) async-start(bf16[32,64,128]{2,1,0:T(8,128)(2,1)} %get-tuple-element.50), calls=%async_computation | async-start | bytes 1048576 | tf_op jit(solution)/shard_map/all_to_all | solution.py:450
  16.1 10.4 %collective-permute-start = (bf16[128,768]{1,0:T(8,128)(2,1)S(1)}, bf16[128,768]{1,0:T(8,128)(2,1)S(1)}, u32[]{:S(2)}, u32[]{:S(2)}) collective-permute-start(bf16[128,768]{1,0:T(8,128)(2,1)S(1)} %get-tuple-element.46.refs_1_), channel_id=1, source_target_pairs={{0,1},{1,0},{2,3},{3,2},{4,5},{5,4},{6,7},{7,6},{8,9},{9,8},{10,11... | collective-permute-start | bytes 589832 | tf_op jit(solution)/shard_map/ppermute | solution.py:446
  26.4 0.7 copy-start.30
  27.1 1.3 copy-start.1
  28.4 1.3 copy-start.3
  29.7 0.9 copy-start.29
  30.6 0.9 copy-start.31
  31.5 5.0 %copy-start.36 = (f32[6,8]{1,0:T(8,128)S(1)}, f32[6,8]{1,0:T(8,128)}, u32[]{:S(2)}) copy-start(f32[6,8]{1,0:T(8,128)} %refs_7_.2) | copy-start | bytes 580
  31.5 5.0 %copy-start.39 = (s32[256]{0:T(256)S(1)}, s32[256]{0:T(256)}, u32[]{:S(2)}) copy-start(s32[256]{0:T(256)} %param.24) | copy-start | bytes 3076
  31.5 16.8 %copy-start.6 = (bf16[768,1536]{1,0:T(8,128)(2,1)S(1)}, bf16[768,1536]{1,0:T(8,128)(2,1)}, u32[]{:S(2)}) copy-start(bf16[768,1536]{1,0:T(8,128)(2,1)} %refs_9_.2) | copy-start | bytes 7077892
  33.7 0.7 copy-start.14
  34.3 0.7 copy-start.17
  35.0 0.7 copy-start.20
  35.7 0.7 copy-start.26
  36.5 0.9 copy-start.15
  37.4 0.9 copy-start.18
  38.3 0.9 copy-start.21
  39.3 0.7 copy-start.40
  39.9 5.4 %copy-start.23 = (bf16[1,128,768]{2,1,0:T(8,128)(2,1)S(1)}, bf16[1,128,768]{2,1,0:T(8,128)(2,1)}, u32[]{:S(2)}) copy-start(bf16[1,128,768]{2,1,0:T(8,128)(2,1)} %param.39) | copy-start | bytes 589828
  42.8 5.6 %collective-permute-start.1 = (bf16[128,384]{1,0:T(8,128)(2,1)S(1)}, bf16[128,384]{1,0:T(8,128)(2,1)S(1)}, u32[]{:S(2)}, u32[]{:S(2)}) collective-permute-start(bf16[128,384]{1,0:T(8,128)(2,1)S(1)} %get-tuple-element.52), channel_id=1, source_target_pairs={{0,1},{1,0},{2,3},{3,2},{4,5},{5,4},{6,7},{7,6},{8,9},{9,8},{10,11... | collective-permute-start | bytes 294920 | tf_op jit(solution)/shard_map/ppermute | solution.py:446
  45.4 1.7 %copy-start.7 = (bf16[1536,768]{1,0:T(8,128)(2,1)S(1)}, bf16[1536,768]{1,0:T(8,128)(2,1)}, u32[]{:S(2)}) copy-start(bf16[1536,768]{1,0:T(8,128)(2,1)} %refs_1_.2) | copy-start | bytes 7077892
  47.1 1.7 %copy-start.5 = (bf16[768,1536]{1,0:T(8,128)(2,1)S(1)}, bf16[768,1536]{1,0:T(8,128)(2,1)}, u32[]{:S(2)}) copy-start(bf16[768,1536]{1,0:T(8,128)(2,1)} %refs_8_.2) | copy-start | bytes 7077892
  47.1 1.7 %copy-start.11 = (bf16[1,128,768]{2,1,0:T(8,128)(2,1)S(1)}, bf16[1,128,768]{2,1,0:T(8,128)(2,1)}, u32[]{:S(2)}) copy-start(bf16[1,128,768]{2,1,0:T(8,128)(2,1)} %param.20) | copy-start | bytes 589828
  48.7 1.3 copy-start.13
  50.0 14.5 %copy-start.16 = (bf16[384,256]{1,0:T(8,128)(2,1)S(1)}, bf16[384,256]{1,0:T(8,128)(2,1)}, u32[]{:S(2)}) copy-start(bf16[384,256]{1,0:T(8,128)(2,1)} %copy-done.14) | copy-start | bytes 589828
  50.0 14.5 %copy-start.19 = (bf16[384,256]{1,0:T(8,128)(2,1)S(1)}, bf16[384,256]{1,0:T(8,128)(2,1)}, u32[]{:S(2)}) copy-start(bf16[384,256]{1,0:T(8,128)(2,1)} %copy-done.17) | copy-start | bytes 589828
  50.0 14.5 %copy-start.22 = (bf16[384,256]{1,0:T(8,128)(2,1)S(1)}, bf16[384,256]{1,0:T(8,128)(2,1)}, u32[]{:S(2)}) copy-start(bf16[384,256]{1,0:T(8,128)(2,1)} %copy-done.20) | copy-start | bytes 589828
  50.0 17.1 %copy-start.4 = (bf16[768,768]{1,0:T(8,128)(2,1)S(1)}, bf16[768,768]{1,0:T(8,128)(2,1)}, u32[]{:S(2)}) copy-start(bf16[768,768]{1,0:T(8,128)(2,1)} %refs_10_.1) | copy-start | bytes 3538948
  50.0 17.1 %copy-start.27 = (bf16[256,768]{1,0:T(8,128)(2,1)S(1)}, bf16[256,768]{1,0:T(8,128)(2,1)}, u32[]{:S(2)}) copy-start(bf16[256,768]{1,0:T(8,128)(2,1)} %copy-done.26) | copy-start | bytes 1179652
  56.0 15.5 %copy-start.24 = (f32[128,768]{1,0:T(8,128)}, f32[128,768]{1,0:T(8,128)S(1)}, u32[]{:S(2)}) copy-start(f32[128,768]{1,0:T(8,128)S(1)} %get-tuple-element.53.refs_2_) | copy-start | bytes 1179652
  56.0 11.1 %copy-start.2 = (bf16[768,768]{1,0:T(8,128)(2,1)S(1)}, bf16[768,768]{1,0:T(8,128)(2,1)}, u32[]{:S(2)}) copy-start(bf16[768,768]{1,0:T(8,128)(2,1)} %refs_9_.3) | copy-start | bytes 3538948
  56.0 11.1 %collective-permute-start.3 = (bf16[128,768]{1,0:T(8,128)(2,1)S(1)}, bf16[128,768]{1,0:T(8,128)(2,1)S(1)}, u32[]{:S(2)}, u32[]{:S(2)}) collective-permute-start(bf16[128,768]{1,0:T(8,128)(2,1)S(1)} %get-tuple-element.62.refs_6_), channel_id=1, source_target_pairs={{0,1},{1,0},{2,3},{3,2},{4,5},{5,4},{6,7},{7,6},{8,9},{9,8},{10,11... | collective-permute-start | bytes 589832 | tf_op jit(solution)/shard_map/ppermute | solution.py:446
  56.7 7.8 %collective-permute-start.2 = (bf16[384,128]{1,0:T(8,128)(2,1)S(1)}, bf16[384,128]{1,0:T(8,128)(2,1)S(1)}, u32[]{:S(2)}, u32[]{:S(2)}) collective-permute-start(bf16[384,128]{1,0:T(8,128)(2,1)S(1)} %get-tuple-element.58), channel_id=1, source_target_pairs={{0,1},{1,0},{2,3},{3,2},{4,5},{5,4},{6,7},{7,6},{8,9},{9,8},{10,11... | collective-permute-start | bytes 294920 | tf_op jit(solution)/shard_map/ppermute | solution.py:446
  71.5 17.0 %collective-permute-start.5 = (bf16[8,4,48,384]{3,2,1,0:T(8,128)(2,1)}, bf16[8,4,48,384]{3,2,1,0:T(8,128)(2,1)}, u32[]{:S(2)}, u32[]{:S(2)}) collective-permute-start(bf16[8,4,48,384]{3,2,1,0:T(8,128)(2,1)} %get-tuple-element.66), channel_id=1, source_target_pairs={{0,2},{2,0},{4,6},{6,4},{8,10},{10,8},{12,14},{14,12},{16,18},{18,... | collective-permute-start | bytes 3538952 | tf_op jit(solution)/shard_map/ppermute | solution.py:441
  71.6 43.0 %all-to-all-start.1 = ((bf16[32,64,128]{2,1,0:T(8,128)(2,1)}), bf16[32,64,128]{2,1,0:T(8,128)(2,1)S(1)}, u32[]{:S(2)}, u32[]{:S(2)}) async-start(bf16[32,64,128]{2,1,0:T(8,128)(2,1)} %get-tuple-element.77), calls=%async_computation.1 | async-start | bytes 1048576 | tf_op jit(solution)/shard_map/all_to_all | solution.py:450
  78.1 10.4 %collective-permute-start.4 = (bf16[768,128]{1,0:T(8,128)(2,1)S(1)}, bf16[768,128]{1,0:T(8,128)(2,1)S(1)}, u32[]{:S(2)}, u32[]{:S(2)}) collective-permute-start(bf16[768,128]{1,0:T(8,128)(2,1)S(1)} %get-tuple-element.64), channel_id=1, source_target_pairs={{0,1},{1,0},{2,3},{3,2},{4,5},{5,4},{6,7},{7,6},{8,9},{9,8},{10,11... | collective-permute-start | bytes 589832 | tf_op jit(solution)/shard_map/ppermute | solution.py:446
  90.3 24.3 %copy-start.9 = (bf16[128,16,128]{2,1,0:T(8,128)(2,1)S(1)}, bf16[128,16,128]{2,1,0:T(8,128)(2,1)}, u32[]{:S(2)}) copy-start(bf16[128,16,128]{2,1,0:T(8,128)(2,1)} %param.22) | copy-start | bytes 1572868
  90.3 24.3 %copy-start.35 = (bf16[128,8]{0,1:T(8,128)(2,1)S(1)}, bf16[128,8]{0,1:T(8,128)(2,1)}, u32[]{:S(2)}) copy-start(bf16[128,8]{0,1:T(8,128)(2,1)} %param.34) | copy-start | bytes 6148
  90.3 24.3 %copy-start.38 = (f32[128]{0:T(128)S(1)}, f32[128]{0:T(128)}, u32[]{:S(2)}) copy-start(f32[128]{0:T(128)} %param.28) | copy-start | bytes 1540
  90.3 18.5 %collective-permute-start.6 = (bf16[4,5,48,384]{3,2,1,0:T(8,128)(2,1)S(1)}, bf16[4,5,48,384]{3,2,1,0:T(8,128)(2,1)S(1)}, u32[]{:S(2)}, u32[]{:S(2)}) collective-permute-start(bf16[4,5,48,384]{3,2,1,0:T(8,128)(2,1)S(1)} %get-tuple-element.68), channel_id=1, source_target_pairs={{0,4},{2,6},{4,0},{6,2},{8,12},{10,14},{12,8},{14,10},{16,20},{18,... | collective-permute-start | bytes 2211848 | tf_op jit(solution)/shard_map/ppermute | solution.py:441
  110.2 27.7 %copy-start.12 = (bf16[1,128,768]{2,1,0:T(8,128)(2,1)S(1)}, bf16[1,128,768]{2,1,0:T(8,128)(2,1)}, u32[]{:S(2)}) copy-start(bf16[1,128,768]{2,1,0:T(8,128)(2,1)} %param.20) | copy-start | bytes 589828
  110.2 27.7 %copy-start.25 = (f32[128,768]{1,0:T(8,128)S(1)}, f32[128,768]{1,0:T(8,128)}, u32[]{:S(2)}) copy-start(f32[128,768]{1,0:T(8,128)} %copy-done.24) | copy-start | bytes 1179652
  110.2 13.8 %collective-permute-start.7 = (bf16[5,48,384]{2,1,0:T(8,128)(2,1)}, bf16[5,48,384]{2,1,0:T(8,128)(2,1)S(1)}, u32[]{:S(2)}, u32[]{:S(2)}) collective-permute-start(bf16[5,48,384]{2,1,0:T(8,128)(2,1)} %get-tuple-element.70), channel_id=1, source_target_pairs={{0,8},{2,10},{4,12},{6,14},{8,0},{10,2},{12,4},{14,6},{16,24},{18,... | collective-permute-start | bytes 552968 | tf_op jit(solution)/shard_map/ppermute | solution.py:441
  111.8 16.4 %collective-permute-start.8 = (bf16[5,48,384]{2,1,0:T(8,128)(2,1)}, bf16[5,48,384]{2,1,0:T(8,128)(2,1)S(1)}, u32[]{:S(2)}, u32[]{:S(2)}) collective-permute-start(bf16[5,48,384]{2,1,0:T(8,128)(2,1)} %get-tuple-element.71), channel_id=1, source_target_pairs={{0,16},{2,18},{4,20},{6,22},{8,24},{10,26},{12,28},{14,30},{16,0},... | collective-permute-start | bytes 552968 | tf_op jit(solution)/shard_map/ppermute | solution.py:441
  114.3 13.9 %collective-permute-start.9 = (bf16[5,48,384]{2,1,0:T(8,128)(2,1)S(1)}, bf16[5,48,384]{2,1,0:T(8,128)(2,1)S(1)}, u32[]{:S(2)}, u32[]{:S(2)}) collective-permute-start(bf16[5,48,384]{2,1,0:T(8,128)(2,1)S(1)} %get-tuple-element.72), channel_id=1, source_target_pairs={{0,24},{2,26},{4,28},{6,30},{8,16},{10,18},{12,20},{14,22},{16,8},... | collective-permute-start | bytes 552968 | tf_op jit(solution)/shard_map/ppermute | solution.py:441
  117.6 21.8 %all-to-all-start.2 = ((f32[32,8,128]{2,1,0:T(8,128)}), f32[32,8,128]{2,1,0:T(8,128)S(1)}, u32[]{:S(2)}, u32[]{:S(2)}) async-start(f32[32,8,128]{2,1,0:T(8,128)} %get-tuple-element.83), calls=%async_computation.2 | async-start | bytes 262144 | tf_op jit(solution)/shard_map/all_to_all | solution.py:450
  129.4 11.1 %collective-permute-start.10 = (bf16[3,48,384]{2,1,0:T(8,128)(2,1)S(1)}, bf16[3,48,384]{2,1,0:T(8,128)(2,1)S(1)}, u32[]{:S(2)}, u32[]{:S(2)}) collective-permute-start(bf16[3,48,384]{2,1,0:T(8,128)(2,1)S(1)} %get-tuple-element.73), channel_id=1, source_target_pairs={{0,0},{1,16},{2,2},{3,18},{4,4},{5,20},{6,6},{7,22},{8,8},{9,24},{... | collective-permute-start | bytes 331784 | tf_op jit(solution)/shard_map/ppermute | solution.py:643
  137.8 2.2 %collective-permute-start.11 = (bf16[48,128]{1,0:T(8,128)(2,1)S(1)}, bf16[48,128]{1,0:T(8,128)(2,1)S(1)}, u32[]{:S(2)}, u32[]{:S(2)}) collective-permute-start(bf16[48,128]{1,0:T(8,128)(2,1)S(1)} %get-tuple-element.75), channel_id=1, source_target_pairs={{0,2},{2,0},{4,6},{6,4},{8,10},{10,8},{12,14},{14,12},{16,18},{18,... | collective-permute-start | bytes 36872 | tf_op jit(solution)/shard_map/ppermute | solution.py:441

commit v4 on v3

v4 whole, which is shorter than its diff:
```python
import functools

import jax
import jax.numpy as jnp
from jax import lax
from jax.experimental import pallas as pl
from jax.experimental.pallas import tpu as pltpu
from jax.sharding import PartitionSpec as P

epsilon = 1e-05
f32 = jnp.float32
bf16 = jnp.bfloat16
VMEM, SMEM, ANY = pltpu.VMEM, pltpu.SMEM, pl.ANY
MIB = 1 << 20


def layer_forward(values, scales):
    average = jnp.mean(values, axis=-1, keepdims=True)
    centred = values - average
    inverse = lax.rsqrt(jnp.mean(centred * centred, axis=-1, keepdims=True) + epsilon)
    normed = centred * inverse
    return (normed * scales, normed, inverse)


def layer_backward(upstream, scales, normed, inverse):
    scaled = upstream * scales
    first_moment = jnp.mean(scaled, axis=-1, keepdims=True)
    second_moment = jnp.mean(scaled * normed, axis=-1, keepdims=True)
    return inverse * (scaled - first_moment - normed * second_moment)


NN = ((1,), (0,))
NT = ((1,), (1,))
TN = ((0,), (0,))


def mm(left, right, dims=NN):
    return lax.dot_general(left, right, (dims, ((), ())), preferred_element_type=f32)


def call(body, name, inputs, outs, scratch=(), flops=0, limit=16):
    arrays, specs, moved, fetched = [], [], 0, []
    for item in inputs:
        array, space = item if isinstance(item, tuple) else (item, VMEM)
        if space == "fetch":
            fetched.append(len(arrays))
            space = pltpu.HBM
        arrays.append(array)
        specs.append(pl.BlockSpec(memory_space=space))
        moved += array.size * array.dtype.itemsize
    for shape, kind in outs:
        size = jnp.dtype(kind).itemsize
        for extent in shape:
            size *= extent
        moved += size
    extra = [VMEM(arrays[k].shape, arrays[k].dtype) for k in fetched]
    if fetched:
        extra.append(pltpu.SemaphoreType.DMA((len(fetched),)))

    def whole(*refs):
        refs = list(refs)
        if fetched:
            held, sem = refs[-1 - len(fetched) : -1], refs[-1]
            refs = refs[: -1 - len(fetched)]
            transfers = []
            for n, k in enumerate(fetched):
                transfer = pltpu.make_async_copy(refs[k], held[n], sem.at[n])
                transfer.start()
                transfers.append(transfer)
                refs[k] = held[n]
            for transfer in transfers:
                transfer.wait()
        body(*refs)

    return pl.pallas_call(
        whole,
        name=name,
        out_shape=[jax.ShapeDtypeStruct(shape, kind) for shape, kind in outs],
        in_specs=specs,
        out_specs=[pl.BlockSpec(memory_space=VMEM)] * len(outs),
        scratch_shapes=list(scratch) + extra,
        compiler_params=pltpu.CompilerParams(vmem_limit_bytes=limit * MIB),
        cost_estimate=pl.CostEstimate(flops=flops, bytes_accessed=moved, transcendentals=0),
    )(*arrays)


def low_bits(index, size):
    return jnp.bitwise_and(index, size - 1)


def pair_weight_rows(w_pair, head_count, cols):
    rows = head_count * cols
    shift = cols.bit_length() - 1
    head = lax.shift_right_logical(
        lax.broadcasted_iota(jnp.int32, (rows, head_count), 0), jnp.int32(shift)
    )
    pick = (head == lax.broadcasted_iota(jnp.int32, (rows, head_count), 1)).astype(f32)
    spread = mm(pick.astype(bf16), w_pair)
    row_col = low_bits(lax.broadcasted_iota(jnp.int32, spread.shape, 0), cols)
    return spread, row_col


def enter_kernel(noisy, single, restype, table, gain, x_out):
    rows = noisy.shape[0]
    normed_scaled, _, _ = layer_forward(noisy[...].astype(f32), gain[...])
    types = table.shape[0]
    onehot = (lax.broadcasted_iota(jnp.int32, (types, rows), 0) == restype[...]).astype(f32)
    condition = single[...].astype(f32) + mm(onehot.astype(bf16), table[...], TN)
    x_out[...] = (normed_scaled + condition).astype(bf16)


def bias_kernel(toks, cols, pair, pair_gain, w_pair, bias_out, rounded):
    rows = bias_out.shape[2]
    pair_scaled, _, _ = layer_forward(pair[...].astype(f32), pair_gain[...])
    rounded[...] = pair_scaled.astype(bf16).astype(f32)
    head_count = w_pair.shape[0]
    spread, row_col = pair_weight_rows(w_pair[...], head_count, cols)
    total = jnp.zeros((head_count * cols, rows), f32)
    for j in range(cols):
        column = rounded[pl.ds(j, rows, stride=cols), :].astype(bf16)
        total = total + mm(jnp.where(row_col == j, spread, 0.0).astype(bf16), column, NT)
    bias = total.astype(bf16)
    part = bias_out.shape[1]
    for n in range(bias_out.shape[0]):
        t = n % toks
        bias_out[n] = bias[t * part : (t + 1) * part, :]


def own_slice(weight, t, own_width):
    if weight.shape[1] == own_width:
        return weight
    return weight.at[:, pl.ds(pl.multiple_of(t * own_width, own_width), own_width)]


def stage_kernel(own_heads, ids, chain, keymask, chain_weight, *rest):
    weights, (slices, facts_out, chain_out, sem) = rest[:3], rest[3:]
    t = ids[0]
    own_width = slices.shape[2]
    transfers = []
    for k in range(3):
        transfer = pltpu.make_async_copy(
            own_slice(weights[k], t, own_width), slices.at[k], sem.at[k]
        )
        transfer.start()
        transfers.append(transfer)
    chain_row = chain[...]
    tokens = chain_row.shape[1]
    keep_row = keymask[...].astype(f32)
    line = lax.broadcasted_iota(jnp.int32, (128, tokens), 0)
    facts = jnp.where(line == 0, chain_row.astype(f32), 0.0) + jnp.where(line == 1, keep_row, 0.0)
    for h in range(own_heads):
        weight_row = jnp.zeros((1, tokens), f32)
        for m in range(chain_weight.shape[0]):
            weight_row = jnp.where(chain_row == m, chain_weight[m, t * own_heads + h], weight_row)
        facts = jnp.where(line == 2 + h, weight_row, facts)
    facts_out[...] = jnp.transpose(facts)
    chain_out[...] = chain_row.astype(f32)
    for transfer in transfers:
        transfer.wait()


def project_kernel(toks, ids, slices, *rest):
    parts = rest[:toks]
    x_out, outs = rest[toks], rest[toks + 1 :]
    t = ids[0]
    rows = parts[0].shape[0]
    for r in range(toks):
        start = pl.multiple_of(jnp.bitwise_xor(t, r) * rows, rows)
        x_out[pl.ds(start, rows), :] = parts[r][...]
    x = x_out[...]
    for k in range(3):
        outs[k][...] = jnp.transpose(mm(x, slices[k])).astype(bf16)


def attention_kernel(copies, toks, cols, head_width, ids, query, key, value, own, other, *rest):
    facts, chain, weights_out, att_out = rest[:4]
    pieces, bias = rest[4 : 4 + toks], rest[4 + toks]
    t = ids[0]
    core = low_bits(ids[1], 2)
    bias[core] = own[...]
    bias[1 - core] = other[...]
    own_heads = weights_out.shape[0]
    tokens = query.shape[1]
    rows = tokens // toks
    same = facts[:, 0:1] == chain[...]
    keep = facts[:, 1:2] > 0.0
    scale = head_width ** (-0.5)
    attended = []
    for h in range(own_heads):
        span = slice(h * head_width, (h + 1) * head_width)
        logits = mm(key[span, :], query[span, :], TN) * scale
        line = slice(h * cols, (h + 1) * cols)
        extra = jnp.concatenate(
            [
                jnp.concatenate(
                    [bias[c % 2, c // 2 * toks + a, line, :] for c in range(copies)], axis=0
                )
                for a in range(toks)
            ],
            axis=1,
        ).astype(f32)
        logits = logits + (extra + jnp.where(same, facts[:, 2 + h : 3 + h], 0.0))
        logits = jnp.where(keep, logits, -1e30)
        exponent = jnp.exp(logits - jnp.max(logits, axis=0, keepdims=True))
        weights = exponent / jnp.sum(exponent, axis=0, keepdims=True)
        weights_b = weights.astype(bf16)
        weights_out[h] = weights_b
        attended.append(mm(value[span, :], weights_b))
    att_out[...] = jnp.transpose(jnp.concatenate(attended, axis=0)).astype(bf16)
    for r in range(toks):
        start = pl.multiple_of(jnp.bitwise_xor(t, r) * rows, rows)
        pieces[r][...] = att_out[pl.ds(start, rows), :]


def down_kernel(upstream, w_down, noisy, gain, d_hidden, upstream_out, noisy_out, gain_out):
    d_hidden[...] = mm(upstream[...], w_down[...], NT)
    upstream_out[...] = upstream[...]
    noisy_out[...] = noisy[...]
    gain_out[...] = gain[...]


def hidden_kernel(toks, chunk, ids, noisy, upstream, d_hidden, gain, *rest):
    parts = rest[:toks]
    w_out, w_gate, w_up = rest[toks : toks + 3]
    d_res_out, d_res_b_out = rest[toks + 3 : toks + 5]
    d_att_outs = rest[toks + 5 : 2 * toks + 5]
    held_out, held_gate, held_up, sem = rest[2 * toks + 5 :]
    t = ids[0]
    hidden = w_gate.shape[1]
    first = pltpu.make_async_copy(w_out, held_out, sem.at[0])
    first.start()
    copies = []
    for k in range(hidden // chunk):
        span = pl.ds(k * chunk, chunk)
        pair = [
            pltpu.make_async_copy(w.at[:, span], held.at[:, span], sem.at[1 + 2 * k + n])
            for n, (w, held) in enumerate(((w_gate, held_gate), (w_up, held_up)))
        ]
        for copy in pair:
            copy.start()
        copies.append(pair)
    residual = noisy[...].astype(f32)
    first.wait()
    own_width = parts[0].shape[1]
    for r in range(toks):
        start = pl.multiple_of(jnp.bitwise_xor(t, r) * own_width, own_width)
        residual = residual + mm(parts[r][...], held_out[pl.ds(start, own_width), :])
    trans_scaled, trans_hat, trans_inverse = layer_forward(residual, gain[...])
    trans_in = trans_scaled.astype(bf16)
    d_trans = jnp.zeros(residual.shape, f32)
    for k in range(hidden // chunk):
        for copy in copies[k]:
            copy.wait()
        span = slice(k * chunk, (k + 1) * chunk)
        gate = mm(trans_in, held_gate[:, span])
        up = mm(trans_in, held_up[:, span])
        incoming = d_hidden[:, span]
        sigmoid = jax.nn.sigmoid(gate)
        d_up = (incoming * gate * sigmoid).astype(bf16)
        d_gate = (incoming * up * sigmoid * (1.0 + gate * (1.0 - sigmoid))).astype(bf16)
        d_trans = d_trans + mm(d_gate, held_gate[:, span], NT) + mm(d_up, held_up[:, span], NT)
    d_res = upstream[...].astype(f32) + layer_backward(
        d_trans, gain[...], trans_hat, trans_inverse
    )
    d_res_out[...] = d_res
    d_res_b = d_res.astype(bf16)
    d_res_b_out[...] = d_res_b
    for r in range(toks):
        start = pl.multiple_of(jnp.bitwise_xor(t, r) * own_width, own_width)
        d_att_outs[r][...] = mm(held_out[pl.ds(start, own_width), :], d_res_b, NT).astype(bf16)


def backward_kernel(copies, toks, cols, head_width, ids, query, key, value, weights, *rest):
    parts = rest[:toks]
    d_query, d_key, d_value, bias_kept, bias_sent, blocks, d_logits = rest[toks:]
    t = ids[0]
    core = low_bits(ids[1], 2)
    for r in range(toks):
        blocks[jnp.bitwise_xor(t, r)] = parts[r][...]
    d_att = jnp.concatenate([blocks[a] for a in range(toks)], axis=1)
    scale = head_width ** (-0.5)
    for h in range(weights.shape[0]):
        span = slice(h * head_width, (h + 1) * head_width)
        d_att_h = d_att[span, :]
        weights_b = weights[h]
        d_weights = mm(value[span, :], d_att_h, TN)
        weights_f = weights_b.astype(f32)
        delta = jnp.sum(weights_f * d_weights, axis=0, keepdims=True)
        d_logits_b = (weights_f * (d_weights - delta)).astype(bf16)
        d_logits[...] = d_logits_b
        for q in range(copies // 2):
            for side, out in ((core, bias_kept), (1 - core, bias_sent)):
                start = pl.multiple_of((2 * q + side) * cols, cols)
                out[q, h * cols : (h + 1) * cols, :] = d_logits[pl.ds(start, cols), :]
        d_query[span, :] = (mm(key[span, :], d_logits_b) * scale).astype(bf16)
        d_key[span, :] = (mm(query[span, :], d_logits_b, NT) * scale).astype(bf16)
        d_value[span, :] = mm(d_att_h, weights_b, NT).astype(bf16)


def cut_wide(copies, toks, core, slot, grad, kept, sent):
    group = copies // toks
    cut, depth = grad.shape[1] // copies, grad.shape[1] // toks
    for side, out in ((core, kept), (1 - core, sent)):
        for q in range(copies // 2):
            h = 2 * q // group
            first = pl.multiple_of((2 * q - h * group + side) * cut, 8)
            out[q, slot] = grad[pl.ds(first, cut), h * depth : (h + 1) * depth].astype(bf16)


def first_kernel(copies, toks, ids, x, att, d_value, *rest):
    d_res_parts, (kept, sent, d_res, wide, narrow) = rest[:toks], rest[toks:]
    t, core = ids[0], low_bits(ids[1], 2)
    rows = d_res_parts[0].shape[0]
    for r in range(toks):
        start = pl.multiple_of(jnp.bitwise_xor(t, r) * rows, rows)
        d_res[pl.ds(start, rows), :] = d_res_parts[r][...]
    wide[...] = mm(d_value[...], x[...])
    cut_wide(copies, toks, core, 0, wide, kept, sent)
    narrow[...] = mm(d_res[...], att[...], TN)
    cut = narrow.shape[0] // copies
    for side, out in ((core, kept), (1 - core, sent)):
        for q in range(copies // 2):
            first = pl.multiple_of((2 * q + side) * cut, 8)
            out[q, 1] = narrow[pl.ds(first, cut), :].astype(bf16)


def second_kernel(copies, toks, ids, slices, x, d_query, d_key, d_value, *rest):
    kept, sent, d_own = rest[:3]
    d_others, (wide, d_inputs) = rest[3 : 2 + toks], rest[2 + toks :]
    t, core = ids[0], low_bits(ids[1], 2)
    rows = d_own.shape[1]
    for k, part in enumerate((d_query, d_key)):
        wide[...] = mm(part[...], x[...])
        cut_wide(copies, toks, core, k, wide, kept, sent)
    total = mm(slices[0], d_query[...]) + mm(slices[1], d_key[...])
    total = total + mm(slices[2], d_value[...])
    for a in range(toks):
        d_inputs[a] = total[:, a * rows : (a + 1) * rows]
    d_own[...] = d_inputs[t]
    for r in range(1, toks):
        d_others[r - 1][...] = d_inputs[jnp.bitwise_xor(t, r)].astype(bf16)


def halve_kernel(divide, count, ids, *refs):
    ins, outs = refs[: 2 * count], refs[2 * count :]
    bit = low_bits(ids[1] // divide, 2)
    for n in range(count):
        kept, got = ins[2 * n : 2 * n + 2]
        for q in range(kept.shape[0] // 2):
            for side, out in ((bit, outs[2 * n]), (1 - bit, outs[2 * n + 1])):
                k = 2 * q + side
                out[q] = (kept[k].astype(f32) + got[k].astype(f32)).astype(bf16)


def halve_single_kernel(toks, copies, ids, kept, got, d_own, *rest):
    others = rest[: toks - 1]
    kept_out, sent_out, single_kept, single_sent, total_ref = rest[toks - 1 :]
    total = d_own[...]
    for part in others:
        total = total + part[...].astype(f32)
    total_ref[...] = total
    bit = low_bits(ids[1] // 2, 2)
    cut = total.shape[0] // copies
    for q in range(kept_out.shape[0]):
        for side, out, single in ((bit, kept_out, single_kept), (1 - bit, sent_out, single_sent)):
            k = 2 * q + side
            out[q] = (kept[k].astype(f32) + got[k].astype(f32)).astype(bf16)
            for low in range(2):
                start = pl.multiple_of((q * 4 + side * 2 + low) * cut, 8)
                single[q, low] = total_ref[pl.ds(start, cut), :].astype(bf16)


def last_first_kernel(toks, ids, kept, got, bias_kept, bias_got, moved, final, *rest):
    pieces, blocks = rest[:toks], rest[toks]
    moved[...] = (kept[0, 0].astype(f32) + got[0, 0].astype(f32)).astype(bf16)
    final[...] = kept[0, 1].astype(f32) + got[0, 1].astype(f32)
    total = bias_kept[0].astype(f32) + bias_got[0].astype(f32)
    rows = blocks.shape[2]
    for a in range(toks):
        blocks[a] = total[:, a * rows : (a + 1) * rows].astype(bf16)
    for r in range(toks):
        pieces[r][...] = blocks[jnp.bitwise_xor(ids[0], r)]


def last_second_kernel(ids, kept, got, single_kept, single_got, moved, kept_out, sent_out, halves):
    moved[...] = (kept[0].astype(f32) + got[0].astype(f32)).astype(bf16)
    halves[...] = (single_kept[0].astype(f32) + single_got[0].astype(f32)).astype(bf16)
    core = low_bits(ids[1], 2)
    kept_out[...] = halves[core]
    sent_out[...] = halves[1 - core]


def finish_kernel(moved_a, moved_b, kept_single, got_single, first, second, third, single):
    first[...] = moved_b[0].astype(f32)
    second[...] = moved_b[1].astype(f32)
    third[...] = moved_a[...].astype(f32)
    single[...] = kept_single[...].astype(f32) + got_single[...].astype(f32)


def exit_kernel(toks, noisy, gain, d_res, d_own, *rest):
    others, (grad_noisy,) = rest[: toks - 1], rest[toks - 1 :]
    total = d_own[...]
    for part in others:
        total = total + part[...].astype(f32)
    _, noisy_hat, noisy_inverse = layer_forward(noisy[...].astype(f32), gain[...])
    grad_noisy[...] = (
        d_res[...] + layer_backward(jnp.transpose(total), gain[...], noisy_hat, noisy_inverse)
    ).astype(bf16)


def pair_kernel(toks, cols, ids, pair, gain, w_pair, *rest):
    parts, (grad_pair, weight_grad, rounded, spread_out, grads) = rest[:toks], rest[toks:]
    head_count = w_pair.shape[0]
    part_rows, rows = parts[0].shape
    for r in range(toks):
        start = pl.multiple_of(jnp.bitwise_xor(ids[0], r) * part_rows, part_rows)
        grads[pl.ds(start, part_rows), :] = parts[r][...].astype(f32)
    grad = grads[...]
    pair_scaled, pair_hat, pair_inverse = layer_forward(pair[...].astype(f32), gain[...])
    rounded[...] = pair_scaled.astype(bf16).astype(f32)
    spread, row_col = pair_weight_rows(w_pair[...], head_count, cols)
    grad_b = grad.astype(bf16)
    turned = jnp.transpose(grad).astype(bf16)
    sums = jnp.zeros(spread.shape, f32)
    for j in range(cols):
        here = row_col == j
        column = rounded[pl.ds(j, rows, stride=cols), :].astype(bf16)
        sums = sums + jnp.where(here, mm(grad_b, column), 0.0)
        spread_out[pl.ds(j, rows, stride=cols), :] = mm(
            turned, jnp.where(here, spread, 0.0).astype(bf16)
        )
    grad_pair[...] = layer_backward(
        spread_out[...], gain[...], pair_hat, pair_inverse
    ).astype(bf16)
    for h in range(head_count):
        line = jnp.sum(sums[h * cols : (h + 1) * cols, :], axis=0, keepdims=True)
        for n in range(weight_grad.shape[0]):
            weight_grad[n, h : h + 1, :] = line


def swap_copy(value, mask):
    size = lax.axis_size("copy")
    return lax.ppermute(value, "copy", [(i, i ^ mask) for i in range(size)])


def swap_tok(value, mask):
    size = lax.axis_size("tok")
    return lax.ppermute(value, "tok", [(i, i ^ mask) for i in range(size)])


def exchange(value, groups=None):
    return lax.all_to_all(value, ("copy", "tok"), 0, 0, axis_index_groups=groups)


def after(value, *earlier):
    return lax.optimization_barrier((value,) + earlier)[0]


def per_device(
    noisy,
    single,
    pair,
    restype,
    chain,
    keymask,
    restype_table,
    norm_gain,
    pair_gain,
    trans_gain,
    w_query,
    w_key,
    w_value,
    w_out,
    w_pair,
    chain_weight,
    w_hidden_gate,
    w_hidden_up,
    w_down,
    cotangent,
):
    copies = lax.axis_size("copy")
    toks = lax.axis_size("tok")
    _, rows, width = noisy.shape
    cols = pair.shape[1]
    channels = pair.shape[2]
    heads = w_pair.shape[1]
    head_width = width // heads
    own_heads = heads // toks
    own_width = own_heads * head_width
    tokens = rows * toks
    hidden = w_down.shape[0]
    cut = width // copies
    devices = copies * toks
    ids = jnp.stack([lax.axis_index("tok"), lax.axis_index("copy")]).astype(jnp.int32)
    where_am_i = (ids, SMEM)
    noisy2 = noisy.reshape(rows, width)
    pair2 = pair.reshape(rows * cols, channels)
    pair_gain2 = pair_gain.reshape(1, channels)
    norm_gain2 = norm_gain.reshape(1, width)

    (x_own,) = call(
        enter_kernel,
        "enter",
        [(array, "fetch") for array in (noisy2, single, restype.reshape(1, rows), restype_table)]
        + [(norm_gain2, "fetch")],
        [((rows, width), bf16)],
        limit=60,
    )
    x_parts = [x_own] + [swap_tok(x_own, r) for r in range(1, toks)]
    (bias_out,) = call(
        functools.partial(bias_kernel, toks, cols),
        "bias",
        [(pair2, "fetch"), (pair_gain2, "fetch"), (w_pair.T, "fetch")],
        [((devices // 2, own_heads * cols, rows), bf16)],
        [VMEM((rows * cols, channels), f32)],
        flops=2 * heads * cols * rows * channels * cols,
        limit=60,
    )
    groups = [
        [(2 * k + core) * toks + t for k in range(copies // 2) for t in range(toks)]
        for core in range(2)
    ]
    bias_own = exchange(after(bias_out, *x_parts[1:]), groups)
    bias_other = swap_copy(bias_own, 1)

    weights3 = [w_query, w_key, w_value]
    if own_width % 128:
        weights3 = [
            lax.dynamic_slice_in_dim(w, ids[0] * own_width, own_width, axis=1) for w in weights3
        ]
    slices, facts, chain_row = call(
        functools.partial(stage_kernel, own_heads),
        "stage",
        [where_am_i, chain.reshape(1, tokens), keymask.reshape(1, tokens), (chain_weight, SMEM)]
        + [(w, ANY) for w in weights3],
        [((3, width, own_width), bf16), ((tokens, 128), f32), ((1, tokens), f32)],
        [pltpu.SemaphoreType.DMA((3,))],
    )
    x, query, key, value = call(
        functools.partial(project_kernel, toks),
        "project",
        [where_am_i, slices] + x_parts,
        [((tokens, width), bf16)] + [((own_width, tokens), bf16)] * 3,
        flops=6 * tokens * width * own_width,
    )
    done = call(
        functools.partial(attention_kernel, copies, toks, cols, head_width),
        "attention",
        [where_am_i, query, key, value, bias_own, bias_other, facts, chain_row],
        [((own_heads, tokens, tokens), bf16), ((tokens, own_width), bf16)]
        + [((rows, own_width), bf16)] * toks,
        [VMEM((2, devices // 2, own_heads * cols, rows), bf16)],
        flops=4 * tokens * tokens * own_width,
        limit=32,
    )
    weights, att, pieces = done[0], done[1], done[2:]
    att_parts = [pieces[0]] + [swap_tok(pieces[r], r) for r in range(1, toks)]

    d_hidden, upstream, noisy3, trans_gain2 = call(
        down_kernel,
        "down",
        [cotangent.reshape(rows, width), w_down, noisy2, trans_gain.reshape(1, width)],
        [((rows, hidden), f32), ((rows, width), bf16), ((rows, width), bf16), ((1, width), f32)],
        flops=2 * rows * hidden * width,
    )
    chunk = hidden // 3
    results = call(
        functools.partial(hidden_kernel, toks, chunk),
        "hidden",
        [where_am_i, noisy3, upstream, d_hidden, trans_gain2]
        + att_parts
        + [(w_out, ANY), (w_hidden_gate, ANY), (w_hidden_up, ANY)],
        [((rows, width), f32), ((rows, width), bf16)] + [((own_width, rows), bf16)] * toks,
        [
            VMEM((width, width), bf16),
            VMEM((width, hidden), bf16),
            VMEM((width, hidden), bf16),
            pltpu.SemaphoreType.DMA((7,)),
        ],
        flops=2 * rows * width * (2 * width + 4 * hidden),
    )
    d_res, d_res_b, d_att = results[0], results[1], results[2:]
    d_att_parts = [d_att[0]] + [swap_tok(d_att[r], r) for r in range(1, toks)]
    d_res_b = after(d_res_b, *d_att_parts[1:])
    d_res_parts = [d_res_b] + [swap_tok(d_res_b, r) for r in range(1, toks)]

    bias_shape = (copies // 2, own_heads * cols, tokens)
    d_query, d_key, d_value, bias_kept, bias_sent = call(
        functools.partial(backward_kernel, copies, toks, cols, head_width),
        "backward",
        [where_am_i, query, key, value, weights] + d_att_parts,
        [((own_width, tokens), bf16)] * 3 + [(bias_shape, bf16)] * 2,
        [VMEM((toks, own_width, rows), bf16), VMEM((tokens, tokens), bf16)],
        flops=8 * tokens * tokens * own_width,
        limit=32,
    )
    bias_got = swap_copy(bias_sent, 1)

    part_shape = (copies // 2, 2, cut, own_width)
    kept, sent = call(
        functools.partial(first_kernel, copies, toks),
        "first",
        [where_am_i, x, att, d_value] + d_res_parts,
        [(part_shape, bf16)] * 2,
        [
            VMEM((tokens, width), bf16),
            VMEM((own_width, width), f32),
            VMEM((width, own_width), f32),
        ],
        flops=4 * tokens * width * own_width,
    )
    got = swap_copy(sent, 1)

    found = call(
        functools.partial(second_kernel, copies, toks),
        "second",
        [where_am_i, slices, x, d_query, d_key, d_value],
        [(part_shape, bf16)] * 2
        + [((width, rows), f32)]
        + [((width, rows), bf16)] * (toks - 1),
        [VMEM((own_width, width), f32), VMEM((toks, width, rows), f32)],
        flops=10 * tokens * width * own_width,
    )
    kept_b, sent_b, d_own = found[:3]
    d_others = [swap_tok(found[2 + r], r) for r in range(1, toks)]
    got_b = swap_copy(sent_b, 1)

    def halve(name, mask, pairs):
        outs = []
        for pair_kept, _ in pairs:
            outs += [((pair_kept.shape[0] // 2,) + pair_kept.shape[1:], bf16)] * 2
        flat = [array for one in pairs for array in one]
        results = call(
            functools.partial(halve_kernel, mask, len(pairs)), name, [where_am_i] + flat, outs
        )
        return [
            (results[2 * n], swap_copy(results[2 * n + 1], mask)) for n in range(len(pairs))
        ]

    chain_a = halve("halve_a2", 2, [(kept, got), (bias_kept, bias_got)])
    part_shape = (copies // 4, 2, cut, own_width)
    single_shape = (copies // 4, 2, cut, rows)
    kept_b, sent_b, single_kept, single_sent = call(
        functools.partial(halve_single_kernel, toks, copies),
        "halve_b2",
        [where_am_i, kept_b, got_b, d_own] + d_others,
        [(part_shape, bf16)] * 2 + [(single_shape, bf16)] * 2,
        [VMEM((width, rows), f32)],
    )
    chain_b = [(kept_b, swap_copy(sent_b, 2)), (single_kept, swap_copy(single_sent, 2))]
    (grad_noisy,) = call(
        functools.partial(exit_kernel, toks),
        "exit",
        [noisy3, norm_gain2, d_res, d_own] + d_others,
        [((rows, width), bf16)],
    )
    mask = 4
    while mask < copies:
        chain_a = halve("halve_a%d" % mask, mask, chain_a)
        chain_b = halve("halve_b%d" % mask, mask, chain_b)
        mask *= 2

    group = copies // toks
    swaps = []
    for c in range(copies):
        for t in range(toks):
            swaps.append((c * toks + t, (t * group + c % group) * toks + c // group))

    done = call(
        functools.partial(last_first_kernel, toks),
        "last_a",
        [where_am_i] + [array for one in chain_a for array in one],
        [((cut, own_width), bf16), ((cut, own_width), f32)]
        + [((own_heads * cols, rows), bf16)] * toks,
        [VMEM((toks, own_heads * cols, rows), bf16)],
    )
    moved_a, grad_out, bias_parts = done[0], done[1], done[2:]
    bias_parts = [bias_parts[0]] + [swap_tok(bias_parts[r], r) for r in range(1, toks)]
    moved_a = lax.ppermute(moved_a, ("copy", "tok"), swaps)
    grad_pair, weight_grad = call(
        functools.partial(pair_kernel, toks, cols),
        "pair",
        [where_am_i, pair2, pair_gain2, w_pair.T] + bias_parts,
        [((rows * cols, channels), bf16), ((devices, heads, channels), f32)],
        [VMEM((rows * cols, channels), f32)] * 2 + [VMEM((heads * cols, rows), f32)],
        flops=4 * heads * cols * rows * channels * cols,
    )
    weight_grad = jnp.sum(exchange(weight_grad), axis=0)

    moved_b, last_kept, last_sent = call(
        last_second_kernel,
        "last_b",
        [where_am_i] + [array for one in chain_b for array in one],
        [((2, cut, own_width), bf16)] + [((cut, rows), bf16)] * 2,
        [VMEM((2, cut, rows), bf16)],
    )
    last_got = swap_copy(last_sent, 1)
    moved_b = lax.ppermute(moved_b, ("copy", "tok"), swaps)
    grad_query, grad_key, grad_value, grad_single = call(
        finish_kernel,
        "finish",
        [moved_a, moved_b, last_kept, last_got],
        [((cut, own_width), f32)] * 3 + [((cut, rows), f32)],
    )
    return (
        grad_noisy[None],
        grad_single.T,
        grad_pair.reshape(rows, cols, channels),
        grad_query.T,
        grad_key.T,
        grad_value.T,
        grad_out.T,
        weight_grad.T,
    )


def solution(mesh):
    placed = (
        P("copy", "tok", None),
        P("tok", None),
        P("tok", "copy", None),
        P("tok"),
    ) + (P(),) * 15 + (P("copy", "tok", None),)
    return jax.shard_map(
        per_device,
        mesh=mesh,
        in_specs=placed,
        out_specs=(
            P("copy", "tok", None),
            P("tok", "copy"),
            P("tok", "copy", None),
            P("tok", "copy"),
            P("tok", "copy"),
            P("tok", "copy"),
            P("tok", "copy"),
            P(),
        ),
        check_vma=False,
    )
```

time: 143 us -> 127 us (0.89)
  local copies, waits for them, and re-layouts: 21.8 us -> 3.98 us
  blocking collectives: 0 us -> 15.3 us
  starting transfers between devices: 38.7 us -> 31.3 us
  waiting for transfers between devices: 47.5 us -> 41.1 us
    unnamed x84 -> x36, local copies, waits for them, and re-layouts: 20.4 us -> 2.61 us
    all_to_all x3 -> x1, starting transfers between devices: 19.1 us -> 3.12 us  [exchange(): lax.all_to_all(value, ('copy', 'tok'), 0, 0, axis_index_groups=groups)]
    all_to_all x0 -> x1, blocking collectives: none -> 15.3 us  [exchange(): lax.all_to_all(value, ('copy', 'tok'), 0, 0, axis_index_groups=groups)]
    ppermute x6 -> x17, starting transfers between devices: 6.26 us -> 15.1 us  [swap_copy(): return lax.ppermute(value, 'copy', [(i, i ^ mask) for i in range(size)])]
    ppermute x5 -> x6, waiting for transfers between devices: 26.1 us -> 20.7 us  [swap_tok(): return lax.ppermute(value, 'tok', [(i, i ^ mask) for i in range(size)])]
    ppermute x6 -> x17, waiting for transfers between devices: 20.9 us -> 19.2 us  [swap_copy(): return lax.ppermute(value, 'copy', [(i, i ^ mask) for i in range(size)])]
    pallas_call x13 -> x21, Pallas kernels: 31.5 us -> 32.5 us  [call(): pl.pallas_call(whole, name=name, out_shape=[jax.ShapeDtypeStruct(shape, k...]
    ppermute x1 -> x2, starting transfers between devices: 8.35 us -> 7.64 us  [the longest x1 5.16 us: per_device(): moved_a = lax.ppermute(moved_a, ('copy', 'tok'), swaps)]
  transfers between devices with their start and end apart: 15 -> 26, of which waited for: 6 -> 14; matrix products, arithmetic and copies ran while one was open for 1% -> 0% of each run, Pallas kernels for 11% -> 17%
where the time goes in v4:
time: 127 us; the launch traced here: 126 us
  waiting for transfers between devices  41.1 us (32%)
  Pallas kernels  32.5 us (26%)
  starting transfers between devices  31.3 us (25%)
  blocking collectives  15.3 us (12%)
  local copies, waits for them, and re-layouts  3.98 us (3%)
    pallas_call x21, Pallas kernels, call(): pl.pallas_call(whole, name=name, out_shape=[jax.ShapeDtypeStruct(shape, k...  32.5 us
    ppermute x6, waiting for transfers between devices, swap_tok(): return lax.ppermute(value, 'tok', [(i, i ^ mask) for i in range(size)])  20.7 us
    ppermute x17, waiting for transfers between devices, swap_copy(): return lax.ppermute(value, 'copy', [(i, i ^ mask) for i in range(size)])  19.2 us
    all_to_all x1, blocking collectives, exchange(): lax.all_to_all(value, ('copy', 'tok'), 0, 0, axis_index_groups=groups)  15.3 us
    ppermute x17, starting transfers between devices, swap_copy(): return lax.ppermute(value, 'copy', [(i, i ^ mask) for i in range(size)])  15.1 us
    ppermute x6, starting transfers between devices, swap_tok(): return lax.ppermute(value, 'tok', [(i, i ^ mask) for i in range(size)])  5.47 us
    ppermute x1, starting transfers between devices, per_device(): moved_a = lax.ppermute(moved_a, ('copy', 'tok'), swaps)  5.16 us
    all_to_all x1, starting transfers between devices, exchange(): lax.all_to_all(value, ('copy', 'tok'), 0, 0, axis_index_groups=groups)  3.12 us
  transfers between devices with their start and end apart: 26, of which 14 were waited for; matrix products, arithmetic and copies ran while one was open for 0% of the time, Pallas kernels for 17%

profile of v4, /device:TPU:2, one launch (start us, length us, event | category | flops | bytes accessed | tf_op | source)
XLA Modules:
  0.0 125.9 jit_solution(13488873738589858021)
XLA Ops:
  0.7 1.4 %reshape.49.refs_4_.refs_1_ = f32[1,768]{1,0:T(1,128)} reshape(f32[768]{0:T(1024)} %param.27) | data formatting | bytes 6144 | tf_op jit(solution)/shard_map/reshape | solution.py:499
  2.0 2.0 %enter.1.refs_2_ = bf16[128,768]{1,0:T(8,128)(2,1)} custom-call(bf16[128,768]{1,0:T(8,128)(2,1)} %bitcast.20, bf16[128,768]{1,0:T(8,128)(2,1)} %refs_1_.3, s32[1,128]{1,0:T(1,128)} %bitcast.31, bf16[32,768]{1,0:T(8,128)(2,1)} %refs_3_.3, f32[1,768]{1,0:T(1,128)} %reshape.49.refs_4_.refs_1_), custom_call_target="tpu_custom_call" | custom-call | bytes 642560 | tf_op jit(solution)/shard_map/enter/pallas_call | solution.py:75
  4.1 2.9 %bias.1 = bf16[16,64,128]{2,1,0:T(8,128)(2,1)} custom-call(bf16[2048,128]{1,0:T(8,128)(2,1)} %bitcast.18, f32[1,128]{1,0:T(1,128)} %bitcast.25, bf16[8,128]{1,0:T(8,128)(2,1)} %bitcast.23), custom_call_target="tpu_custom_call" | custom-call | flops 67108864 | bytes 788992 | tf_op jit(solution)/shard_map/bias/pallas_call | solution.py:75
  7.1 3.9 %collective-permute-done.refs_3_ = bf16[128,768]{1,0:T(8,128)(2,1)S(1)} collective-permute-done((bf16[128,768]{1,0:T(8,128)(2,1)}, bf16[128,768]{1,0:T(8,128)(2,1)S(1)}, u32[]{:S(2)}, u32[]{:S(2)}) %collective-permute-start) | collective-permute-done | bytes 196640 | tf_op jit(solution)/shard_map/ppermute | solution.py:448
  11.0 15.3 %all_to_all.10.refs_4_ = bf16[16,64,128]{2,1,0:T(8,128)(2,1)S(1)} all-to-all(bf16[16,64,128]{2,1,0:T(8,128)(2,1)} %bias.1), channel_id=1, replica_groups={{0,1,4,5,8,9,12,13,16,17,20,21,24,25,28,29},{2,3,6,7,10,11,14,15,18,19,..., dimensions={0} | all-to-all | bytes 524288 | tf_op jit(solution)/shard_map/all_to_all | solution.py:452
  26.3 0.1 pad_add_fusion.refs_0_
  26.4 1.3 %copy-done.5 = bf16[768,768]{1,0:T(8,128)(2,1)S(1)} copy-done((bf16[768,768]{1,0:T(8,128)(2,1)S(1)}, bf16[768,768]{1,0:T(8,128)(2,1)}, u32[]{:S(2)}) %copy-start.5) | copy-done | bytes 1179672
  27.7 1.3 %copy-done.6 = bf16[768,768]{1,0:T(8,128)(2,1)S(1)} copy-done((bf16[768,768]{1,0:T(8,128)(2,1)S(1)}, bf16[768,768]{1,0:T(8,128)(2,1)}, u32[]{:S(2)}) %copy-start.6) | copy-done | bytes 1179672
  28.9 1.0 stage.1
  30.0 1.4 %project.1 = (bf16[256,768]{1,0:T(8,128)(2,1)S(1)}, bf16[384,256]{1,0:T(8,128)(2,1)S(1)}, bf16[384,256]{1,0:T(8,128)(2,1)S(1)}, bf16[384,256]{1,0:T(8,128)(2,1)S(1)}) custom-call(s32[2]{0:T(128)S(1)} %pad_add_fusion.refs_0_, bf16[3,768,384]{2,1,0:T(8,128)(2,1)S(1)} %get-tuple-element.81.refs_1_, bf16[128,768]{1,0:T(8,128)(2,1)S(1)} %copy-done.9, ...), custom_call_target="tpu_custom_call" | custom-call | flops 452984832 | bytes 3145736 | tf_op jit(solution)/shard_map/project/pallas_call | solution.py:75
  31.4 2.1 %attention.1 = (bf16[4,256,256]{2,1,0:T(8,128)(2,1)S(1)}, bf16[256,384]{1,0:T(8,128)(2,1)S(1)}, bf16[128,384]{1,0:T(8,128)(2,1)S(1)}, bf16[128,384]{1,0:T(8,128)(2,1)S(1)}) custom-call(s32[2]{0:T(128)S(1)} %pad_add_fusion.refs_0_, bf16[384,256]{1,0:T(8,128)(2,1)S(1)} %get-tuple-element.82.refs_1_, bf16[384,256]{1,0:T(8,128)(2,1)S(1)} %get-tuple-element.83.refs_2_, ...), custom_call_target="tpu_custom_call" | custom-call | flops 100663296 | bytes 2163720 | tf_op jit(solution)/shard_map/attention/pallas_call | solution.py:75
  33.6 1.1 collective-permute-start.2
  34.7 0.9 down.1
  35.6 3.2 %collective-permute-done.2.refs_6_ = bf16[128,384]{1,0:T(8,128)(2,1)S(1)} collective-permute-done((bf16[128,384]{1,0:T(8,128)(2,1)S(1)}, bf16[128,384]{1,0:T(8,128)(2,1)S(1)}, u32[]{:S(2)}, u32[]{:S(2)}) %collective-permute-start.2) | collective-permute-done | bytes 98336 | tf_op jit(solution)/shard_map/ppermute | solution.py:448
  38.8 5.6 %hidden.1 = (f32[128,768]{1,0:T(8,128)S(1)}, bf16[128,768]{1,0:T(8,128)(2,1)S(1)}, bf16[384,128]{1,0:T(8,128)(2,1)S(1)}, bf16[384,128]{1,0:T(8,128)(2,1)S(1)}) custom-call(s32[2]{0:T(128)S(1)} %pad_add_fusion.refs_0_, bf16[128,768]{1,0:T(8,128)(2,1)S(1)} %get-tuple-element.77.refs_1_.refs_0_, bf16[128,768]{1,0:T(8,128)(2,1)S(1)} %get-tuple-element.78.refs_2_, ...), custom_call_target="tpu_custom_call" | custom-call | flops 1509949440 | bytes 8064008 | tf_op jit(solution)/shard_map/hidden/pallas_call | solution.py:75
  44.5 1.1 collective-permute-start.3
  45.6 3.5 %collective-permute-done.3.refs_6_ = bf16[384,128]{1,0:T(8,128)(2,1)S(1)} collective-permute-done((bf16[384,128]{1,0:T(8,128)(2,1)S(1)}, bf16[384,128]{1,0:T(8,128)(2,1)S(1)}, u32[]{:S(2)}, u32[]{:S(2)}) %collective-permute-start.3) | collective-permute-done | bytes 98336 | tf_op jit(solution)/shard_map/ppermute | solution.py:448
  49.1 1.1 collective-permute-start.5
  50.2 2.0 %backward.1 = (bf16[384,256]{1,0:T(8,128)(2,1)S(1)}, bf16[384,256]{1,0:T(8,128)(2,1)S(1)}, bf16[384,256]{1,0:T(8,128)(2,1)S(1)}, bf16[8,64,256]{2,1,0:T(8,128)(2,1)S(1)}, bf16[8,64,256]{2,1,0:T(8,128)(2,1)S(1)}) custom-call(s32[2]{0:T(128)S(1)} %pad_add_fusion.refs_0_, bf16[384,256]{1,0:T(8,128)(2,1)S(1)} %get-tuple-element.82.refs_1_, ...), custom_call_target="tpu_custom_call" | custom-call | flops 201326592 | bytes 2424840 | tf_op jit(solution)/shard_map/backward/pallas_call | solution.py:75
  52.2 2.6 %collective-permute-done.5.refs_5_ = bf16[128,768]{1,0:T(8,128)(2,1)S(1)} collective-permute-done((bf16[128,768]{1,0:T(8,128)(2,1)S(1)}, bf16[128,768]{1,0:T(8,128)(2,1)S(1)}, u32[]{:S(2)}, u32[]{:S(2)}) %collective-permute-start.5) | collective-permute-done | bytes 196640 | tf_op jit(solution)/shard_map/ppermute | solution.py:448
  54.8 1.4 %first.1 = (bf16[8,2,48,384]{3,2,1,0:T(8,128)(2,1)S(1)}, bf16[8,2,48,384]{3,2,1,0:T(8,128)(2,1)S(1)}) custom-call(s32[2]{0:T(128)S(1)} %pad_add_fusion.refs_0_, bf16[256,768]{1,0:T(8,128)(2,1)S(1)} %get-tuple-element.91.refs_2_.refs_1_, bf16[256,384]{1,0:T(8,128)(2,1)S(1)} %get-tuple-element.100.refs_2_, ...), custom_call_target="tpu_custom_call" | custom-call | flops 301989888 | bytes 2359304 | tf_op jit(solution)/shard_map/first/pallas_call | solution.py:75
  56.2 0.1 collective-permute-start.6
  56.3 2.0 %second.1 = (bf16[8,2,48,384]{3,2,1,0:T(8,128)(2,1)S(1)}, bf16[8,2,48,384]{3,2,1,0:T(8,128)(2,1)S(1)}, f32[768,128]{1,0:T(8,128)S(1)}, bf16[768,128]{1,0:T(8,128)(2,1)S(1)}) custom-call(s32[2]{0:T(128)S(1)} %pad_add_fusion.refs_0_, bf16[3,768,384]{2,1,0:T(8,128)(2,1)S(1)} %get-tuple-element.81.refs_1_, ...), custom_call_target="tpu_custom_call" | custom-call | flops 754974720 | bytes 4521992 | tf_op jit(solution)/shard_map/second/pallas_call | solution.py:75
  58.3 0.6 collective-permute-start.15
  58.9 0.1 collective-permute-start.7
  59.0 1.9 %collective-permute-done.7.refs_4_ = bf16[8,64,256]{2,1,0:T(8,128)(2,1)S(1)} collective-permute-done((bf16[8,64,256]{2,1,0:T(8,128)(2,1)S(1)}, bf16[8,64,256]{2,1,0:T(8,128)(2,1)S(1)}, u32[]{:S(2)}, u32[]{:S(2)}) %collective-permute-start.7) | collective-permute-done | bytes 262176 | tf_op jit(solution)/shard_map/ppermute | solution.py:443
  60.9 0.8 halve_a2.1
  61.6 0.6 collective-permute-start.8
  62.3 1.5 %collective-permute-start.4 = (bf16[768,128]{1,0:T(8,128)(2,1)S(1)}, bf16[768,128]{1,0:T(8,128)(2,1)S(1)}, u32[]{:S(2)}, u32[]{:S(2)}) collective-permute-start(bf16[768,128]{1,0:T(8,128)(2,1)S(1)} %get-tuple-element.99), channel_id=1, source_target_pairs={{0,1},{1,0},{2,3},{3,2},{4,5},{5,4},{6,7},{7,6},{8,9},{9,8},{10,11... | collective-permute-start | bytes 589832 | tf_op jit(solution)/shard_map/ppermute | solution.py:448
  63.7 1.1 collective-permute-start.9
  64.8 4.3 %collective-permute-done.4.refs_4_ = bf16[768,128]{1,0:T(8,128)(2,1)S(1)} collective-permute-done((bf16[768,128]{1,0:T(8,128)(2,1)S(1)}, bf16[768,128]{1,0:T(8,128)(2,1)S(1)}, u32[]{:S(2)}, u32[]{:S(2)}) %collective-permute-start.4) | collective-permute-done | bytes 196640 | tf_op jit(solution)/shard_map/ppermute | solution.py:448
  69.2 0.8 halve_b2.1
  69.9 1.6 %collective-permute-start.16 = (bf16[4,2,48,384]{3,2,1,0:T(8,128)(2,1)S(1)}, bf16[4,2,48,384]{3,2,1,0:T(8,128)(2,1)S(1)}, u32[]{:S(2)}, u32[]{:S(2)}) collective-permute-start(bf16[4,2,48,384]{3,2,1,0:T(8,128)(2,1)S(1)} %get-tuple-element.123), channel_id=1, source_target_pairs={{0,4},{2,6},{4,0},{6,2},{8,12},{10,14},{12,8},{14,10},{16,20},{18,... | collective-permute-start | bytes 884744 | tf_op jit(solution)/shard_map/ppermute | solution.py:443
  71.5 2.9 %collective-permute-done.9.refs_4_ = bf16[4,64,256]{2,1,0:T(8,128)(2,1)S(1)} collective-permute-done((bf16[4,64,256]{2,1,0:T(8,128)(2,1)S(1)}, bf16[4,64,256]{2,1,0:T(8,128)(2,1)S(1)}, u32[]{:S(2)}, u32[]{:S(2)}) %collective-permute-start.9) | collective-permute-done | bytes 131104 | tf_op jit(solution)/shard_map/ppermute | solution.py:443
  74.4 0.7 halve_a4.1
  75.0 0.8 collective-permute-start.10
  75.8 1.3 %collective-permute-start.11 = (bf16[2,64,256]{2,1,0:T(8,128)(2,1)S(1)}, bf16[2,64,256]{2,1,0:T(8,128)(2,1)S(1)}, u32[]{:S(2)}, u32[]{:S(2)}) collective-permute-start(bf16[2,64,256]{2,1,0:T(8,128)(2,1)S(1)} %get-tuple-element.114), channel_id=1, source_target_pairs={{0,8},{2,10},{4,12},{6,14},{8,0},{10,2},{12,4},{14,6},{16,24},{18,... | collective-permute-start | bytes 196616 | tf_op jit(solution)/shard_map/ppermute | solution.py:443
  77.1 0.5 collective-permute-start.17
  77.6 3.6 %collective-permute-done.11.refs_4_ = bf16[2,64,256]{2,1,0:T(8,128)(2,1)S(1)} collective-permute-done((bf16[2,64,256]{2,1,0:T(8,128)(2,1)S(1)}, bf16[2,64,256]{2,1,0:T(8,128)(2,1)S(1)}, u32[]{:S(2)}, u32[]{:S(2)}) %collective-permute-start.11) | collective-permute-done | bytes 65568 | tf_op jit(solution)/shard_map/ppermute | solution.py:443
  81.3 0.6 halve_a8.1
  81.9 0.9 collective-permute-start.12
  82.8 2.1 %collective-permute-start.13 = (bf16[1,64,256]{2,1,0:T(8,128)(2,1)S(1)}, bf16[1,64,256]{2,1,0:T(8,128)(2,1)S(1)}, u32[]{:S(2)}, u32[]{:S(2)}) collective-permute-start(bf16[1,64,256]{2,1,0:T(8,128)(2,1)S(1)} %get-tuple-element.118), channel_id=1, source_target_pairs={{0,16},{2,18},{4,20},{6,22},{8,24},{10,26},{12,28},{14,30},{16,0},... | collective-permute-start | bytes 98312 | tf_op jit(solution)/shard_map/ppermute | solution.py:443
  84.9 0.6 halve_b4.1
  85.5 0.8 collective-permute-start.18
  86.3 2.3 %collective-permute-done.13.refs_4_ = bf16[1,64,256]{2,1,0:T(8,128)(2,1)S(1)} collective-permute-done((bf16[1,64,256]{2,1,0:T(8,128)(2,1)S(1)}, bf16[1,64,256]{2,1,0:T(8,128)(2,1)S(1)}, u32[]{:S(2)}, u32[]{:S(2)}) %collective-permute-start.13) | collective-permute-done | bytes 32800 | tf_op jit(solution)/shard_map/ppermute | solution.py:443
  88.6 1.2 last_a.1
  89.8 0.6 collective-permute-start.24
  90.4 3.2 %collective-permute-done.24.refs_5_ = bf16[64,128]{1,0:T(8,128)(2,1)S(1)} collective-permute-done((bf16[64,128]{1,0:T(8,128)(2,1)S(1)}, bf16[64,128]{1,0:T(8,128)(2,1)S(1)}, u32[]{:S(2)}, u32[]{:S(2)}) %collective-permute-start.24) | collective-permute-done | bytes 16416 | tf_op jit(solution)/shard_map/ppermute | solution.py:448
  93.6 3.4 %pair.1 = (bf16[2048,128]{1,0:T(8,128)(2,1)}, f32[32,8,128]{2,1,0:T(8,128)}) custom-call(s32[2]{0:T(128)S(1)} %pad_add_fusion.refs_0_, bf16[2048,128]{1,0:T(8,128)(2,1)S(1)} %bitcast.19, f32[1,128]{1,0:T(1,128)S(1)} %bitcast.26, bf16[8,128]{1,0:T(8,128)(2,1)S(1)} %bitcast.24, bf16[64,128]{1,0:T(8,128)(2,1)S(1)} %get-tuple-element.138.refs_4_, ...), custom_call_target="tpu_custom_call" | custom-call | flops 134217728 | bytes 1214984 | tf_op jit(solution)/shard_map/pair/pallas_call | solution.py:75
  97.0 3.1 %all-to-all-start.1 = ((f32[32,8,128]{2,1,0:T(8,128)}), f32[32,8,128]{2,1,0:T(8,128)S(1)}, u32[]{:S(2)}, u32[]{:S(2)}) async-start(f32[32,8,128]{2,1,0:T(8,128)} %get-tuple-element.145), calls=%async_computation.1 | async-start | bytes 262144 | tf_op jit(solution)/shard_map/all_to_all | solution.py:452
  100.1 1.5 %collective-permute-start.19 = (bf16[2,2,48,128]{3,2,1,0:T(8,128)(2,1)S(1)}, bf16[2,2,48,128]{3,2,1,0:T(8,128)(2,1)S(1)}, u32[]{:S(2)}, u32[]{:S(2)}) collective-permute-start(bf16[2,2,48,128]{3,2,1,0:T(8,128)(2,1)S(1)} %get-tuple-element.129), channel_id=1, source_target_pairs={{0,8},{2,10},{4,12},{6,14},{8,0},{10,2},{12,4},{14,6},{16,24},{18,... | collective-permute-start | bytes 147464 | tf_op jit(solution)/shard_map/ppermute | solution.py:443
  101.7 3.6 %collective-permute-done.19.refs_4_ = bf16[2,2,48,128]{3,2,1,0:T(8,128)(2,1)S(1)} collective-permute-done((bf16[2,2,48,128]{3,2,1,0:T(8,128)(2,1)S(1)}, bf16[2,2,48,128]{3,2,1,0:T(8,128)(2,1)S(1)}, u32[]{:S(2)}, u32[]{:S(2)}) %collective-permute-start.19) | collective-permute-done | bytes 49184 | tf_op jit(solution)/shard_map/ppermute | solution.py:443
  105.3 0.6 halve_b8.1
  105.9 3.1 %collective-permute-start.20 = (bf16[1,2,48,384]{3,2,1,0:T(8,128)(2,1)S(1)}, bf16[1,2,48,384]{3,2,1,0:T(8,128)(2,1)S(1)}, u32[]{:S(2)}, u32[]{:S(2)}) collective-permute-start(bf16[1,2,48,384]{3,2,1,0:T(8,128)(2,1)S(1)} %get-tuple-element.131), channel_id=1, source_target_pairs={{0,16},{2,18},{4,20},{6,22},{8,24},{10,26},{12,28},{14,30},{16,0},... | collective-permute-start | bytes 221192 | tf_op jit(solution)/shard_map/ppermute | solution.py:443
  108.9 0.1 collective-permute-start.21
  109.0 4.8 %collective-permute-done.21.refs_4_ = bf16[1,2,48,128]{3,2,1,0:T(8,128)(2,1)S(1)} collective-permute-done((bf16[1,2,48,128]{3,2,1,0:T(8,128)(2,1)S(1)}, bf16[1,2,48,128]{3,2,1,0:T(8,128)(2,1)S(1)}, u32[]{:S(2)}, u32[]{:S(2)}) %collective-permute-start.21) | collective-permute-done | bytes 24608 | tf_op jit(solution)/shard_map/ppermute | solution.py:443
  113.9 0.6 last_b.1
  114.5 2.5 %collective-permute-start.22 = (bf16[2,48,384]{2,1,0:T(8,128)(2,1)S(1)}, bf16[2,48,384]{2,1,0:T(8,128)(2,1)S(1)}, u32[]{:S(2)}, u32[]{:S(2)}) collective-permute-start(bf16[2,48,384]{2,1,0:T(8,128)(2,1)S(1)} %get-tuple-element.134), channel_id=1, source_target_pairs={{0,0},{1,16},{2,2},{3,18},{4,4},{5,20},{6,6},{7,22},{8,8},{9,24},{... | collective-permute-start | bytes 221192 | tf_op jit(solution)/shard_map/ppermute | solution.py:698
  116.9 5.2 %collective-permute-start.14 = (bf16[48,384]{1,0:T(8,128)(2,1)S(1)}, bf16[48,384]{1,0:T(8,128)(2,1)S(1)}, u32[]{:S(2)}, u32[]{:S(2)}) collective-permute-start(bf16[48,384]{1,0:T(8,128)(2,1)S(1)} %get-tuple-element.119), channel_id=1, source_target_pairs={{0,0},{1,16},{2,2},{3,18},{4,4},{5,20},{6,6},{7,22},{8,8},{9,24},{... | collective-permute-start | bytes 110600 | tf_op jit(solution)/shard_map/ppermute | solution.py:679
  122.2 1.2 exit.1
  123.4 0.4 collective-permute-done.22.refs_1_
  123.8 0.8 collective-permute-done.14.refs_0_
  124.6 0.7 finish.1
  125.3 0.6 reduce_sum.9
  (50 shorter events, 0.3 us)
Async XLA Ops:
  0.6 25.7 %copy-start.15 = (s32[256]{0:T(256)S(1)}, s32[256]{0:T(256)}, u32[]{:S(2)}) copy-start(s32[256]{0:T(256)} %param.24) | copy-start | bytes 3076
  0.6 25.7 %copy-start.16 = (s32[256]{0:T(256)S(1)}, s32[256]{0:T(256)}, u32[]{:S(2)}) copy-start(s32[256]{0:T(256)} %param.25) | copy-start | bytes 3076
  0.7 25.7 %copy-start.4 = (bf16[768,768]{1,0:T(8,128)(2,1)S(1)}, bf16[768,768]{1,0:T(8,128)(2,1)}, u32[]{:S(2)}) copy-start(bf16[768,768]{1,0:T(8,128)(2,1)} %refs_4_.1) | copy-start | bytes 3538948
  0.7 25.7 %copy-start.13 = (f32[6,8]{1,0:T(8,128)S(1)}, f32[6,8]{1,0:T(8,128)}, u32[]{:S(2)}) copy-start(f32[6,8]{1,0:T(8,128)} %refs_3_.2) | copy-start | bytes 580
  4.1 6.9 %collective-permute-start = (bf16[128,768]{1,0:T(8,128)(2,1)}, bf16[128,768]{1,0:T(8,128)(2,1)S(1)}, u32[]{:S(2)}, u32[]{:S(2)}) collective-permute-start(bf16[128,768]{1,0:T(8,128)(2,1)} %enter.1.refs_2_), channel_id=1, source_target_pairs={{0,1},{1,0},{2,3},{3,2},{4,5},{5,4},{6,7},{7,6},{8,9},{9,8},{10,11... | collective-permute-start | bytes 589832 | tf_op jit(solution)/shard_map/ppermute | solution.py:448
  26.3 5.1 %collective-permute-start.1 = (bf16[16,64,128]{2,1,0:T(8,128)(2,1)S(1)}, bf16[16,64,128]{2,1,0:T(8,128)(2,1)S(1)}, u32[]{:S(2)}, u32[]{:S(2)}) collective-permute-start(bf16[16,64,128]{2,1,0:T(8,128)(2,1)S(1)} %all_to_all.10.refs_4_), channel_id=1, source_target_pairs={{0,2},{2,0},{4,6},{6,4},{8,10},{10,8},{12,14},{14,12},{16,18},{18,... | collective-permute-start | bytes 786440 | tf_op jit(solution)/shard_map/ppermute | solution.py:443
  26.4 1.3 %copy-start.5 = (bf16[768,768]{1,0:T(8,128)(2,1)S(1)}, bf16[768,768]{1,0:T(8,128)(2,1)}, u32[]{:S(2)}) copy-start(bf16[768,768]{1,0:T(8,128)(2,1)} %refs_5_.1) | copy-start | bytes 3538948
  27.7 1.3 %copy-start.6 = (bf16[768,768]{1,0:T(8,128)(2,1)S(1)}, bf16[768,768]{1,0:T(8,128)(2,1)}, u32[]{:S(2)}) copy-start(bf16[768,768]{1,0:T(8,128)(2,1)} %refs_6_.1) | copy-start | bytes 3538948
  28.9 1.0 copy-start.9
  28.9 5.8 %copy-start.2 = (bf16[1536,768]{1,0:T(8,128)(2,1)S(1)}, bf16[1536,768]{1,0:T(8,128)(2,1)}, u32[]{:S(2)}) copy-start(bf16[1536,768]{1,0:T(8,128)(2,1)} %refs_1_.2) | copy-start | bytes 7077892
  28.9 5.8 %copy-start.10 = (bf16[1,128,768]{2,1,0:T(8,128)(2,1)S(1)}, bf16[1,128,768]{2,1,0:T(8,128)(2,1)}, u32[]{:S(2)}) copy-start(bf16[1,128,768]{2,1,0:T(8,128)(2,1)} %param.39) | copy-start | bytes 589828
  29.9 4.8 %copy-start.17 = (f32[768]{0:T(1024)S(1)}, f32[768]{0:T(1024)}, u32[]{:S(2)}) copy-start(f32[768]{0:T(1024)} %param.29) | copy-start | bytes 9220
  29.9 4.8 %copy-start.8 = (bf16[1,128,768]{2,1,0:T(8,128)(2,1)S(1)}, bf16[1,128,768]{2,1,0:T(8,128)(2,1)}, u32[]{:S(2)}) copy-start(bf16[1,128,768]{2,1,0:T(8,128)(2,1)} %param.20) | copy-start | bytes 589828
  30.0 8.9 %copy-start.1 = (bf16[768,1536]{1,0:T(8,128)(2,1)S(1)}, bf16[768,1536]{1,0:T(8,128)(2,1)}, u32[]{:S(2)}) copy-start(bf16[768,1536]{1,0:T(8,128)(2,1)} %refs_9_.1) | copy-start | bytes 7077892
  31.4 7.4 %copy-start = (bf16[768,1536]{1,0:T(8,128)(2,1)S(1)}, bf16[768,1536]{1,0:T(8,128)(2,1)}, u32[]{:S(2)}) copy-start(bf16[768,1536]{1,0:T(8,128)(2,1)} %refs_8_.1) | copy-start | bytes 7077892
  31.4 7.4 %copy-start.7 = (bf16[768,768]{1,0:T(8,128)(2,1)S(1)}, bf16[768,768]{1,0:T(8,128)(2,1)}, u32[]{:S(2)}) copy-start(bf16[768,768]{1,0:T(8,128)(2,1)} %refs_7_.1) | copy-start | bytes 3538948
  33.6 5.3 %collective-permute-start.2 = (bf16[128,384]{1,0:T(8,128)(2,1)S(1)}, bf16[128,384]{1,0:T(8,128)(2,1)S(1)}, u32[]{:S(2)}, u32[]{:S(2)}) collective-permute-start(bf16[128,384]{1,0:T(8,128)(2,1)S(1)} %get-tuple-element.89), channel_id=1, source_target_pairs={{0,1},{1,0},{2,3},{3,2},{4,5},{5,4},{6,7},{7,6},{8,9},{9,8},{10,11... | collective-permute-start | bytes 294920 | tf_op jit(solution)/shard_map/ppermute | solution.py:448
  44.5 4.7 %collective-permute-start.3 = (bf16[384,128]{1,0:T(8,128)(2,1)S(1)}, bf16[384,128]{1,0:T(8,128)(2,1)S(1)}, u32[]{:S(2)}, u32[]{:S(2)}) collective-permute-start(bf16[384,128]{1,0:T(8,128)(2,1)S(1)} %get-tuple-element.94), channel_id=1, source_target_pairs={{0,1},{1,0},{2,3},{3,2},{4,5},{5,4},{6,7},{7,6},{8,9},{9,8},{10,11... | collective-permute-start | bytes 294920 | tf_op jit(solution)/shard_map/ppermute | solution.py:448
  49.1 5.7 %collective-permute-start.5 = (bf16[128,768]{1,0:T(8,128)(2,1)S(1)}, bf16[128,768]{1,0:T(8,128)(2,1)S(1)}, u32[]{:S(2)}, u32[]{:S(2)}) collective-permute-start(bf16[128,768]{1,0:T(8,128)(2,1)S(1)} %get-tuple-element.102.refs_4_), channel_id=1, source_target_pairs={{0,1},{1,0},{2,3},{3,2},{4,5},{5,4},{6,7},{7,6},{8,9},{9,8},{10,11... | collective-permute-start | bytes 589832 | tf_op jit(solution)/shard_map/ppermute | solution.py:448
  56.2 4.7 %collective-permute-start.6 = (bf16[8,2,48,384]{3,2,1,0:T(8,128)(2,1)S(1)}, bf16[8,2,48,384]{3,2,1,0:T(8,128)(2,1)S(1)}, u32[]{:S(2)}, u32[]{:S(2)}) collective-permute-start(bf16[8,2,48,384]{3,2,1,0:T(8,128)(2,1)S(1)} %get-tuple-element.104), channel_id=1, source_target_pairs={{0,2},{2,0},{4,6},{6,4},{8,10},{10,8},{12,14},{14,12},{16,18},{18,... | collective-permute-start | bytes 1769480 | tf_op jit(solution)/shard_map/ppermute | solution.py:443
  58.3 10.8 %collective-permute-start.15 = (bf16[8,2,48,384]{3,2,1,0:T(8,128)(2,1)S(1)}, bf16[8,2,48,384]{3,2,1,0:T(8,128)(2,1)S(1)}, u32[]{:S(2)}, u32[]{:S(2)}) collective-permute-start(bf16[8,2,48,384]{3,2,1,0:T(8,128)(2,1)S(1)} %get-tuple-element.121), channel_id=1, source_target_pairs={{0,2},{2,0},{4,6},{6,4},{8,10},{10,8},{12,14},{14,12},{16,18},{18,... | collective-permute-start | bytes 1769480 | tf_op jit(solution)/shard_map/ppermute | solution.py:443
  58.9 2.0 %collective-permute-start.7 = (bf16[8,64,256]{2,1,0:T(8,128)(2,1)S(1)}, bf16[8,64,256]{2,1,0:T(8,128)(2,1)S(1)}, u32[]{:S(2)}, u32[]{:S(2)}) collective-permute-start(bf16[8,64,256]{2,1,0:T(8,128)(2,1)S(1)} %get-tuple-element.106), channel_id=1, source_target_pairs={{0,2},{2,0},{4,6},{6,4},{8,10},{10,8},{12,14},{14,12},{16,18},{18,... | collective-permute-start | bytes 786440 | tf_op jit(solution)/shard_map/ppermute | solution.py:443
  61.6 12.7 %collective-permute-start.8 = (bf16[4,2,48,384]{3,2,1,0:T(8,128)(2,1)S(1)}, bf16[4,2,48,384]{3,2,1,0:T(8,128)(2,1)S(1)}, u32[]{:S(2)}, u32[]{:S(2)}) collective-permute-start(bf16[4,2,48,384]{3,2,1,0:T(8,128)(2,1)S(1)} %get-tuple-element.108), channel_id=1, source_target_pairs={{0,4},{2,6},{4,0},{6,2},{8,12},{10,14},{12,8},{14,10},{16,20},{18,... | collective-permute-start | bytes 884744 | tf_op jit(solution)/shard_map/ppermute | solution.py:443
  62.3 6.9 %collective-permute-start.4 = (bf16[768,128]{1,0:T(8,128)(2,1)S(1)}, bf16[768,128]{1,0:T(8,128)(2,1)S(1)}, u32[]{:S(2)}, u32[]{:S(2)}) collective-permute-start(bf16[768,128]{1,0:T(8,128)(2,1)S(1)} %get-tuple-element.99), channel_id=1, source_target_pairs={{0,1},{1,0},{2,3},{3,2},{4,5},{5,4},{6,7},{7,6},{8,9},{9,8},{10,11... | collective-permute-start | bytes 589832 | tf_op jit(solution)/shard_map/ppermute | solution.py:448
  63.7 10.6 %collective-permute-start.9 = (bf16[4,64,256]{2,1,0:T(8,128)(2,1)S(1)}, bf16[4,64,256]{2,1,0:T(8,128)(2,1)S(1)}, u32[]{:S(2)}, u32[]{:S(2)}) collective-permute-start(bf16[4,64,256]{2,1,0:T(8,128)(2,1)S(1)} %get-tuple-element.110), channel_id=1, source_target_pairs={{0,4},{2,6},{4,0},{6,2},{8,12},{10,14},{12,8},{14,10},{16,20},{18,... | collective-permute-start | bytes 393224 | tf_op jit(solution)/shard_map/ppermute | solution.py:443
  69.1 24.4 %copy-start.3 = (bf16[128,16,128]{2,1,0:T(8,128)(2,1)S(1)}, bf16[128,16,128]{2,1,0:T(8,128)(2,1)}, u32[]{:S(2)}) copy-start(bf16[128,16,128]{2,1,0:T(8,128)(2,1)} %param.22) | copy-start | bytes 1572868
  69.1 24.4 %copy-start.12 = (bf16[128,8]{0,1:T(8,128)(2,1)S(1)}, bf16[128,8]{0,1:T(8,128)(2,1)}, u32[]{:S(2)}) copy-start(bf16[128,8]{0,1:T(8,128)(2,1)} %param.34) | copy-start | bytes 6148
  69.1 24.4 %copy-start.14 = (f32[128]{0:T(128)S(1)}, f32[128]{0:T(128)}, u32[]{:S(2)}) copy-start(f32[128]{0:T(128)} %param.28) | copy-start | bytes 1540
  69.9 14.9 %collective-permute-start.16 = (bf16[4,2,48,384]{3,2,1,0:T(8,128)(2,1)S(1)}, bf16[4,2,48,384]{3,2,1,0:T(8,128)(2,1)S(1)}, u32[]{:S(2)}, u32[]{:S(2)}) collective-permute-start(bf16[4,2,48,384]{3,2,1,0:T(8,128)(2,1)S(1)} %get-tuple-element.123), channel_id=1, source_target_pairs={{0,4},{2,6},{4,0},{6,2},{8,12},{10,14},{12,8},{14,10},{16,20},{18,... | collective-permute-start | bytes 884744 | tf_op jit(solution)/shard_map/ppermute | solution.py:443
  74.4 47.8 %copy-start.11 = (f32[1,768]{1,0:T(1,128)S(1)}, f32[1,768]{1,0:T(1,128)}, u32[]{:S(2)}) copy-start(f32[1,768]{1,0:T(1,128)} %reshape.49.refs_4_.refs_1_) | copy-start | bytes 9220
  75.0 6.2 %collective-permute-start.10 = (bf16[2,2,48,384]{3,2,1,0:T(8,128)(2,1)S(1)}, bf16[2,2,48,384]{3,2,1,0:T(8,128)(2,1)S(1)}, u32[]{:S(2)}, u32[]{:S(2)}) collective-permute-start(bf16[2,2,48,384]{3,2,1,0:T(8,128)(2,1)S(1)} %get-tuple-element.112), channel_id=1, source_target_pairs={{0,8},{2,10},{4,12},{6,14},{8,0},{10,2},{12,4},{14,6},{16,24},{18,... | collective-permute-start | bytes 442376 | tf_op jit(solution)/shard_map/ppermute | solution.py:443
  75.8 5.5 %collective-permute-start.11 = (bf16[2,64,256]{2,1,0:T(8,128)(2,1)S(1)}, bf16[2,64,256]{2,1,0:T(8,128)(2,1)S(1)}, u32[]{:S(2)}, u32[]{:S(2)}) collective-permute-start(bf16[2,64,256]{2,1,0:T(8,128)(2,1)S(1)} %get-tuple-element.114), channel_id=1, source_target_pairs={{0,8},{2,10},{4,12},{6,14},{8,0},{10,2},{12,4},{14,6},{16,24},{18,... | collective-permute-start | bytes 196616 | tf_op jit(solution)/shard_map/ppermute | solution.py:443
  77.1 7.7 %collective-permute-start.17 = (bf16[4,2,48,128]{3,2,1,0:T(8,128)(2,1)S(1)}, bf16[4,2,48,128]{3,2,1,0:T(8,128)(2,1)S(1)}, u32[]{:S(2)}, u32[]{:S(2)}) collective-permute-start(bf16[4,2,48,128]{3,2,1,0:T(8,128)(2,1)S(1)} %get-tuple-element.125), channel_id=1, source_target_pairs={{0,4},{2,6},{4,0},{6,2},{8,12},{10,14},{12,8},{14,10},{16,20},{18,... | collective-permute-start | bytes 294920 | tf_op jit(solution)/shard_map/ppermute | solution.py:443
  81.9 6.7 %collective-permute-start.12 = (bf16[1,2,48,384]{3,2,1,0:T(8,128)(2,1)S(1)}, bf16[1,2,48,384]{3,2,1,0:T(8,128)(2,1)S(1)}, u32[]{:S(2)}, u32[]{:S(2)}) collective-permute-start(bf16[1,2,48,384]{3,2,1,0:T(8,128)(2,1)S(1)} %get-tuple-element.116), channel_id=1, source_target_pairs={{0,16},{2,18},{4,20},{6,22},{8,24},{10,26},{12,28},{14,30},{16,0},... | collective-permute-start | bytes 221192 | tf_op jit(solution)/shard_map/ppermute | solution.py:443
  82.8 5.8 %collective-permute-start.13 = (bf16[1,64,256]{2,1,0:T(8,128)(2,1)S(1)}, bf16[1,64,256]{2,1,0:T(8,128)(2,1)S(1)}, u32[]{:S(2)}, u32[]{:S(2)}) collective-permute-start(bf16[1,64,256]{2,1,0:T(8,128)(2,1)S(1)} %get-tuple-element.118), channel_id=1, source_target_pairs={{0,16},{2,18},{4,20},{6,22},{8,24},{10,26},{12,28},{14,30},{16,0},... | collective-permute-start | bytes 98312 | tf_op jit(solution)/shard_map/ppermute | solution.py:443
  85.5 19.8 %collective-permute-start.18 = (bf16[2,2,48,384]{3,2,1,0:T(8,128)(2,1)S(1)}, bf16[2,2,48,384]{3,2,1,0:T(8,128)(2,1)S(1)}, u32[]{:S(2)}, u32[]{:S(2)}) collective-permute-start(bf16[2,2,48,384]{3,2,1,0:T(8,128)(2,1)S(1)} %get-tuple-element.127), channel_id=1, source_target_pairs={{0,8},{2,10},{4,12},{6,14},{8,0},{10,2},{12,4},{14,6},{16,24},{18,... | collective-permute-start | bytes 442376 | tf_op jit(solution)/shard_map/ppermute | solution.py:443
  89.8 3.7 %collective-permute-start.24 = (bf16[64,128]{1,0:T(8,128)(2,1)S(1)}, bf16[64,128]{1,0:T(8,128)(2,1)S(1)}, u32[]{:S(2)}, u32[]{:S(2)}) collective-permute-start(bf16[64,128]{1,0:T(8,128)(2,1)S(1)} %get-tuple-element.139), channel_id=1, source_target_pairs={{0,1},{1,0},{2,3},{3,2},{4,5},{5,4},{6,7},{7,6},{8,9},{9,8},{10,11... | collective-permute-start | bytes 49160 | tf_op jit(solution)/shard_map/ppermute | solution.py:448
  97.0 28.3 %all-to-all-start.1 = ((f32[32,8,128]{2,1,0:T(8,128)}), f32[32,8,128]{2,1,0:T(8,128)S(1)}, u32[]{:S(2)}, u32[]{:S(2)}) async-start(f32[32,8,128]{2,1,0:T(8,128)} %get-tuple-element.145), calls=%async_computation.1 | async-start | bytes 262144 | tf_op jit(solution)/shard_map/all_to_all | solution.py:452
  100.1 5.1 %collective-permute-start.19 = (bf16[2,2,48,128]{3,2,1,0:T(8,128)(2,1)S(1)}, bf16[2,2,48,128]{3,2,1,0:T(8,128)(2,1)S(1)}, u32[]{:S(2)}, u32[]{:S(2)}) collective-permute-start(bf16[2,2,48,128]{3,2,1,0:T(8,128)(2,1)S(1)} %get-tuple-element.129), channel_id=1, source_target_pairs={{0,8},{2,10},{4,12},{6,14},{8,0},{10,2},{12,4},{14,6},{16,24},{18,... | collective-permute-start | bytes 147464 | tf_op jit(solution)/shard_map/ppermute | solution.py:443
  105.9 8.0 %collective-permute-start.20 = (bf16[1,2,48,384]{3,2,1,0:T(8,128)(2,1)S(1)}, bf16[1,2,48,384]{3,2,1,0:T(8,128)(2,1)S(1)}, u32[]{:S(2)}, u32[]{:S(2)}) collective-permute-start(bf16[1,2,48,384]{3,2,1,0:T(8,128)(2,1)S(1)} %get-tuple-element.131), channel_id=1, source_target_pairs={{0,16},{2,18},{4,20},{6,22},{8,24},{10,26},{12,28},{14,30},{16,0},... | collective-permute-start | bytes 221192 | tf_op jit(solution)/shard_map/ppermute | solution.py:443
  108.9 4.9 %collective-permute-start.21 = (bf16[1,2,48,128]{3,2,1,0:T(8,128)(2,1)S(1)}, bf16[1,2,48,128]{3,2,1,0:T(8,128)(2,1)S(1)}, u32[]{:S(2)}, u32[]{:S(2)}) collective-permute-start(bf16[1,2,48,128]{3,2,1,0:T(8,128)(2,1)S(1)} %get-tuple-element.133), channel_id=1, source_target_pairs={{0,16},{2,18},{4,20},{6,22},{8,24},{10,26},{12,28},{14,30},{16,0},... | collective-permute-start | bytes 73736 | tf_op jit(solution)/shard_map/ppermute | solution.py:443
  114.5 9.4 %collective-permute-start.22 = (bf16[2,48,384]{2,1,0:T(8,128)(2,1)S(1)}, bf16[2,48,384]{2,1,0:T(8,128)(2,1)S(1)}, u32[]{:S(2)}, u32[]{:S(2)}) collective-permute-start(bf16[2,48,384]{2,1,0:T(8,128)(2,1)S(1)} %get-tuple-element.134), channel_id=1, source_target_pairs={{0,0},{1,16},{2,2},{3,18},{4,4},{5,20},{6,6},{7,22},{8,8},{9,24},{... | collective-permute-start | bytes 221192 | tf_op jit(solution)/shard_map/ppermute | solution.py:698
  116.9 7.7 %collective-permute-start.14 = (bf16[48,384]{1,0:T(8,128)(2,1)S(1)}, bf16[48,384]{1,0:T(8,128)(2,1)S(1)}, u32[]{:S(2)}, u32[]{:S(2)}) collective-permute-start(bf16[48,384]{1,0:T(8,128)(2,1)S(1)} %get-tuple-element.119), channel_id=1, source_target_pairs={{0,0},{1,16},{2,2},{3,18},{4,4},{5,20},{6,6},{7,22},{8,8},{9,24},{... | collective-permute-start | bytes 110600 | tf_op jit(solution)/shard_map/ppermute | solution.py:679
  122.1 1.3 %collective-permute-start.23 = (bf16[48,128]{1,0:T(8,128)(2,1)S(1)}, bf16[48,128]{1,0:T(8,128)(2,1)S(1)}, u32[]{:S(2)}, u32[]{:S(2)}) collective-permute-start(bf16[48,128]{1,0:T(8,128)(2,1)S(1)} %get-tuple-element.136), channel_id=1, source_target_pairs={{0,2},{2,0},{4,6},{6,4},{8,10},{10,8},{12,14},{14,12},{16,18},{18,... | collective-permute-start | bytes 36872 | tf_op jit(solution)/shard_map/ppermute | solution.py:443

commit v5 on v4

--- a/solution.py
+++ b/solution.py
@@ -100,17 +100,10 @@
     return spread, row_col
 
 
-def enter_kernel(noisy, single, restype, table, gain, x_out):
+def enter_kernel(toks, cols, ids, noisy, single, restype, table, gain, pair, pair_gain, *rest):
+    w_pair, x_out, bias_outs = rest[0], rest[1], rest[2 : 2 + toks]
+    rounded, bias = rest[2 + toks :]
     rows = noisy.shape[0]
-    normed_scaled, _, _ = layer_forward(noisy[...].astype(f32), gain[...])
-    types = table.shape[0]
-    onehot = (lax.broadcasted_iota(jnp.int32, (types, rows), 0) == restype[...]).astype(f32)
-    condition = single[...].astype(f32) + mm(onehot.astype(bf16), table[...], TN)
-    x_out[...] = (normed_scaled + condition).astype(bf16)
-
-
-def bias_kernel(toks, cols, pair, pair_gain, w_pair, bias_out, rounded):
-    rows = bias_out.shape[2]
     pair_scaled, _, _ = layer_forward(pair[...].astype(f32), pair_gain[...])
     rounded[...] = pair_scaled.astype(bf16).astype(f32)
     head_count = w_pair.shape[0]
@@ -119,11 +112,16 @@
     for j in range(cols):
         column = rounded[pl.ds(j, rows, stride=cols), :].astype(bf16)
         total = total + mm(jnp.where(row_col == j, spread, 0.0).astype(bf16), column, NT)
-    bias = total.astype(bf16)
-    part = bias_out.shape[1]
-    for n in range(bias_out.shape[0]):
-        t = n % toks
-        bias_out[n] = bias[t * part : (t + 1) * part, :]
+    bias[...] = total
+    part = bias_outs[0].shape[0]
+    for r in range(toks):
+        start = pl.multiple_of(jnp.bitwise_xor(ids[0], r) * part, part)
+        bias_outs[r][...] = bias[pl.ds(start, part), :].astype(bf16)
+    normed_scaled, _, _ = layer_forward(noisy[...].astype(f32), gain[...])
+    types = table.shape[0]
+    onehot = (lax.broadcasted_iota(jnp.int32, (types, rows), 0) == restype[...]).astype(f32)
+    condition = single[...].astype(f32) + mm(onehot.astype(bf16), table[...], TN)
+    x_out[...] = (normed_scaled + condition).astype(bf16)
 
 
 def own_slice(weight, t, own_width):
@@ -176,9 +174,17 @@
     facts, chain, weights_out, att_out = rest[:4]
     pieces, bias = rest[4 : 4 + toks], rest[4 + toks]
     t = ids[0]
-    core = low_bits(ids[1], 2)
-    bias[core] = own[...]
-    bias[1 - core] = other[...]
+    core, pair_index = low_bits(ids[1], 2), ids[1] // 2
+    half = copies // 2
+    for p in range(half):
+        k = 0
+        for b in range(half.bit_length() - 1):
+            k += (p >> b & 1) * (half >> 1 >> b)
+        k = jnp.bitwise_xor(pair_index, k)
+        for r in range(toks):
+            a = jnp.bitwise_xor(t, r)
+            bias[core, k, a] = own[p * toks + r]
+            bias[1 - core, k, a] = other[p * toks + r]
     own_heads = weights_out.shape[0]
     tokens = query.shape[1]
     rows = tokens // toks
@@ -193,7 +199,7 @@
         extra = jnp.concatenate(
             [
                 jnp.concatenate(
-                    [bias[c % 2, c // 2 * toks + a, line, :] for c in range(copies)], axis=0
+                    [bias[c % 2, c // 2, a, line, :] for c in range(copies)], axis=0
                 )
                 for a in range(toks)
             ],
@@ -221,26 +227,12 @@
 
 def hidden_kernel(toks, chunk, ids, noisy, upstream, d_hidden, gain, *rest):
     parts = rest[:toks]
-    w_out, w_gate, w_up = rest[toks : toks + 3]
+    held_out, held_gate, held_up = rest[toks : toks + 3]
     d_res_out, d_res_b_out = rest[toks + 3 : toks + 5]
-    d_att_outs = rest[toks + 5 : 2 * toks + 5]
-    held_out, held_gate, held_up, sem = rest[2 * toks + 5 :]
+    d_att_outs = rest[toks + 5 :]
     t = ids[0]
-    hidden = w_gate.shape[1]
-    first = pltpu.make_async_copy(w_out, held_out, sem.at[0])
-    first.start()
-    copies = []
-    for k in range(hidden // chunk):
-        span = pl.ds(k * chunk, chunk)
-        pair = [
-            pltpu.make_async_copy(w.at[:, span], held.at[:, span], sem.at[1 + 2 * k + n])
-            for n, (w, held) in enumerate(((w_gate, held_gate), (w_up, held_up)))
-        ]
-        for copy in pair:
-            copy.start()
-        copies.append(pair)
+    hidden = held_gate.shape[1]
     residual = noisy[...].astype(f32)
-    first.wait()
     own_width = parts[0].shape[1]
     for r in range(toks):
         start = pl.multiple_of(jnp.bitwise_xor(t, r) * own_width, own_width)
@@ -249,8 +241,6 @@
     trans_in = trans_scaled.astype(bf16)
     d_trans = jnp.zeros(residual.shape, f32)
     for k in range(hidden // chunk):
-        for copy in copies[k]:
-            copy.wait()
         span = slice(k * chunk, (k + 1) * chunk)
         gate = mm(trans_in, held_gate[:, span])
         up = mm(trans_in, held_up[:, span])
@@ -297,43 +287,59 @@
         d_value[span, :] = mm(d_att_h, weights_b, NT).astype(bf16)
 
 
-def cut_wide(copies, toks, core, slot, grad, kept, sent):
+def tile_count(rows, lanes):
+    return -(-rows // 16) * -(-lanes // 128)
+
+
+def put(out, q, base, value):
+    rows, lanes = value.shape
+    for i in range(0, rows, 16):
+        for j in range(0, lanes, 128):
+            part = value[i : i + 16, j : j + 128]
+            if part.shape != (16, 128):
+                out[q, base] = jnp.zeros((16, 128), out.dtype)
+            out[q, base, : part.shape[0], : part.shape[1]] = part
+            base += 1
+
+
+def take(tiles, base, rows, lanes):
+    across = -(-lanes // 128)
+    lines = []
+    for i in range(-(-rows // 16)):
+        line = [tiles[base + i * across + j] for j in range(across)]
+        lines.append(jnp.concatenate(line, axis=1) if across > 1 else line[0])
+    whole = jnp.concatenate(lines, axis=0) if len(lines) > 1 else lines[0]
+    return whole[:rows, :lanes]
+
+
+def cut_wide(copies, toks, core, base, grad, kept, sent):
     group = copies // toks
     cut, depth = grad.shape[1] // copies, grad.shape[1] // toks
     for side, out in ((core, kept), (1 - core, sent)):
         for q in range(copies // 2):
             h = 2 * q // group
             first = pl.multiple_of((2 * q - h * group + side) * cut, 8)
-            out[q, slot] = grad[pl.ds(first, cut), h * depth : (h + 1) * depth].astype(bf16)
-
-
-def first_kernel(copies, toks, ids, x, att, d_value, *rest):
-    d_res_parts, (kept, sent, d_res, wide, narrow) = rest[:toks], rest[toks:]
+            part = grad[pl.ds(first, cut), h * depth : (h + 1) * depth]
+            put(out, q, base, part.astype(bf16))
+
+
+def first_kernel(copies, toks, ids, slices, x, d_query, d_key, d_value, *rest):
+    kept, sent, d_own = rest[:3]
+    d_others, (wide, d_inputs, total_ref) = rest[3 : 2 + toks], rest[2 + toks :]
     t, core = ids[0], low_bits(ids[1], 2)
-    rows = d_res_parts[0].shape[0]
-    for r in range(toks):
-        start = pl.multiple_of(jnp.bitwise_xor(t, r) * rows, rows)
-        d_res[pl.ds(start, rows), :] = d_res_parts[r][...]
-    wide[...] = mm(d_value[...], x[...])
-    cut_wide(copies, toks, core, 0, wide, kept, sent)
-    narrow[...] = mm(d_res[...], att[...], TN)
-    cut = narrow.shape[0] // copies
+    rows = d_own.shape[1]
+    cut = x.shape[1] // copies
+    count = tile_count(cut, d_query.shape[0])
+    for k, part in enumerate((d_query, d_key)):
+        wide[...] = mm(part[...], x[...])
+        cut_wide(copies, toks, core, k * count, wide, kept, sent)
+    total = mm(slices[0], d_query[...]) + mm(slices[1], d_key[...])
+    total = total + mm(slices[2], d_value[...])
+    total_ref[...] = total
     for side, out in ((core, kept), (1 - core, sent)):
         for q in range(copies // 2):
-            first = pl.multiple_of((2 * q + side) * cut, 8)
-            out[q, 1] = narrow[pl.ds(first, cut), :].astype(bf16)
-
-
-def second_kernel(copies, toks, ids, slices, x, d_query, d_key, d_value, *rest):
-    kept, sent, d_own = rest[:3]
-    d_others, (wide, d_inputs) = rest[3 : 2 + toks], rest[2 + toks :]
-    t, core = ids[0], low_bits(ids[1], 2)
-    rows = d_own.shape[1]
-    for k, part in enumerate((d_query, d_key)):
-        wide[...] = mm(part[...], x[...])
-        cut_wide(copies, toks, core, k, wide, kept, sent)
-    total = mm(slices[0], d_query[...]) + mm(slices[1], d_key[...])
-    total = total + mm(slices[2], d_value[...])
+            start = pl.multiple_of((2 * q + side) * cut, 8)
+            put(out, q, 2 * count, total_ref[pl.ds(start, cut), :].astype(bf16))
     for a in range(toks):
         d_inputs[a] = total[:, a * rows : (a + 1) * rows]
     d_own[...] = d_inputs[t]
@@ -341,40 +347,35 @@
         d_others[r - 1][...] = d_inputs[jnp.bitwise_xor(t, r)].astype(bf16)
 
 
-def halve_kernel(divide, count, ids, *refs):
-    ins, outs = refs[: 2 * count], refs[2 * count :]
-    bit = low_bits(ids[1] // divide, 2)
-    for n in range(count):
-        kept, got = ins[2 * n : 2 * n + 2]
-        for q in range(kept.shape[0] // 2):
-            for side, out in ((bit, outs[2 * n]), (1 - bit, outs[2 * n + 1])):
-                k = 2 * q + side
-                out[q] = (kept[k].astype(f32) + got[k].astype(f32)).astype(bf16)
-
-
-def halve_single_kernel(toks, copies, ids, kept, got, d_own, *rest):
-    others = rest[: toks - 1]
-    kept_out, sent_out, single_kept, single_sent, total_ref = rest[toks - 1 :]
-    total = d_own[...]
-    for part in others:
-        total = total + part[...].astype(f32)
-    total_ref[...] = total
-    bit = low_bits(ids[1] // 2, 2)
-    cut = total.shape[0] // copies
+def second_kernel(copies, toks, ids, x, att, d_value, *rest):
+    d_res_parts, (kept, sent, d_res, wide, narrow) = rest[:toks], rest[toks:]
+    t, core = ids[0], low_bits(ids[1], 2)
+    rows = d_res_parts[0].shape[0]
+    wide[...] = mm(d_value[...], x[...])
+    cut_wide(copies, toks, core, 0, wide, kept, sent)
+    for r in range(toks):
+        start = pl.multiple_of(jnp.bitwise_xor(t, r) * rows, rows)
+        d_res[pl.ds(start, rows), :] = d_res_parts[r][...]
+    narrow[...] = mm(d_res[...], att[...], TN)
+    cut = narrow.shape[0] // copies
+    count = tile_count(cut, narrow.shape[1])
+    for side, out in ((core, kept), (1 - core, sent)):
+        for q in range(copies // 2):
+            first = pl.multiple_of((2 * q + side) * cut, 8)
+            put(out, q, count, narrow[pl.ds(first, cut), :].astype(bf16))
+
+
+def halve_kernel(mask, inner, ids, kept, got, kept_out, sent_out):
+    bit = low_bits(ids[1] // mask, 2)
     for q in range(kept_out.shape[0]):
-        for side, out, single in ((bit, kept_out, single_kept), (1 - bit, sent_out, single_sent)):
-            k = 2 * q + side
+        for side, out in ((bit, kept_out), (1 - bit, sent_out)):
+            k = q // inner * 2 * inner + side * inner + q % inner
             out[q] = (kept[k].astype(f32) + got[k].astype(f32)).astype(bf16)
-            for low in range(2):
-                start = pl.multiple_of((q * 4 + side * 2 + low) * cut, 8)
-                single[q, low] = total_ref[pl.ds(start, cut), :].astype(bf16)
-
-
-def last_first_kernel(toks, ids, kept, got, bias_kept, bias_got, moved, final, *rest):
+
+
+def last_bias_kernel(toks, ids, kept, got, *rest):
     pieces, blocks = rest[:toks], rest[toks]
-    moved[...] = (kept[0, 0].astype(f32) + got[0, 0].astype(f32)).astype(bf16)
-    final[...] = kept[0, 1].astype(f32) + got[0, 1].astype(f32)
-    total = bias_kept[0].astype(f32) + bias_got[0].astype(f32)
+    total = kept[0].astype(f32) + got[0].astype(f32)
     rows = blocks.shape[2]
     for a in range(toks):
         blocks[a] = total[:, a * rows : (a + 1) * rows].astype(bf16)
@@ -382,19 +383,37 @@
         pieces[r][...] = blocks[jnp.bitwise_xor(ids[0], r)]
 
 
-def last_second_kernel(ids, kept, got, single_kept, single_got, moved, kept_out, sent_out, halves):
-    moved[...] = (kept[0].astype(f32) + got[0].astype(f32)).astype(bf16)
-    halves[...] = (single_kept[0].astype(f32) + single_got[0].astype(f32)).astype(bf16)
-    core = low_bits(ids[1], 2)
-    kept_out[...] = halves[core]
-    sent_out[...] = halves[1 - core]
-
-
-def finish_kernel(moved_a, moved_b, kept_single, got_single, first, second, third, single):
-    first[...] = moved_b[0].astype(f32)
-    second[...] = moved_b[1].astype(f32)
-    third[...] = moved_a[...].astype(f32)
-    single[...] = kept_single[...].astype(f32) + got_single[...].astype(f32)
+def last_first_kernel(toks, ids, kept, got, moved, *rest):
+    pieces, blocks = rest[:toks], rest[toks]
+    total = kept[0].astype(f32) + got[0].astype(f32)
+    _, cut, own_width = moved.shape
+    count = tile_count(cut, own_width)
+    for k in range(2):
+        moved[k] = take(total, k * count, cut, own_width).astype(bf16)
+    rows = blocks.shape[2]
+    single = take(total, 2 * count, cut, rows * toks)
+    for a in range(toks):
+        blocks[a] = single[:, a * rows : (a + 1) * rows]
+    for r in range(toks):
+        pieces[r][...] = blocks[jnp.bitwise_xor(ids[0], r)].astype(bf16)
+
+
+def last_second_kernel(kept, got, moved, final):
+    total = kept[0].astype(f32) + got[0].astype(f32)
+    cut, own_width = moved.shape
+    moved[...] = take(total, 0, cut, own_width).astype(bf16)
+    final[...] = take(total, tile_count(cut, own_width), cut, own_width)
+
+
+def finish_kernel(moved_first, moved_second, *rest):
+    parts, (first, second, third, single) = rest[:-4], rest[-4:]
+    first[...] = moved_first[0].astype(f32)
+    second[...] = moved_first[1].astype(f32)
+    third[...] = moved_second[...].astype(f32)
+    total = parts[0][...].astype(f32)
+    for part in parts[1:]:
+        total = total + part[...].astype(f32)
+    single[...] = total
 
 
 def exit_kernel(toks, noisy, gain, d_res, d_own, *rest):
@@ -448,8 +467,8 @@
     return lax.ppermute(value, "tok", [(i, i ^ mask) for i in range(size)])
 
 
-def exchange(value, groups=None):
-    return lax.all_to_all(value, ("copy", "tok"), 0, 0, axis_index_groups=groups)
+def exchange(value):
+    return lax.all_to_all(value, ("copy", "tok"), 0, 0)
 
 
 def after(value, *earlier):
@@ -498,29 +517,26 @@
     pair_gain2 = pair_gain.reshape(1, channels)
     norm_gain2 = norm_gain.reshape(1, width)
 
-    (x_own,) = call(
-        enter_kernel,
+    entered = call(
+        functools.partial(enter_kernel, toks, cols),
         "enter",
-        [(array, "fetch") for array in (noisy2, single, restype.reshape(1, rows), restype_table)]
-        + [(norm_gain2, "fetch")],
-        [((rows, width), bf16)],
-        limit=60,
-    )
-    x_parts = [x_own] + [swap_tok(x_own, r) for r in range(1, toks)]
-    (bias_out,) = call(
-        functools.partial(bias_kernel, toks, cols),
-        "bias",
-        [(pair2, "fetch"), (pair_gain2, "fetch"), (w_pair.T, "fetch")],
-        [((devices // 2, own_heads * cols, rows), bf16)],
-        [VMEM((rows * cols, channels), f32)],
+        [where_am_i]
+        + [(array, "fetch") for array in (noisy2, single, restype.reshape(1, rows))]
+        + [(array, "fetch") for array in (restype_table, norm_gain, pair2, pair_gain2, w_pair.T)],
+        [((rows, width), bf16)] + [((own_heads * cols, rows), bf16)] * toks,
+        [VMEM((rows * cols, channels), f32), VMEM((heads * cols, rows), f32)],
         flops=2 * heads * cols * rows * channels * cols,
         limit=60,
     )
-    groups = [
-        [(2 * k + core) * toks + t for k in range(copies // 2) for t in range(toks)]
-        for core in range(2)
-    ]
-    bias_own = exchange(after(bias_out, *x_parts[1:]), groups)
+    x_own, bias_parts = entered[0], entered[1:]
+    bias_own = jnp.stack(
+        [bias_parts[0]] + [swap_tok(bias_parts[r], r) for r in range(1, toks)]
+    )
+    x_parts = [x_own] + [swap_tok(x_own, r) for r in range(1, toks)]
+    mask = copies // 2
+    while mask > 1:
+        bias_own = jnp.concatenate([bias_own, swap_copy(bias_own, mask)])
+        mask //= 2
     bias_other = swap_copy(bias_own, 1)
 
     weights3 = [w_query, w_key, w_value]
@@ -549,7 +565,7 @@
         [where_am_i, query, key, value, bias_own, bias_other, facts, chain_row],
         [((own_heads, tokens, tokens), bf16), ((tokens, own_width), bf16)]
         + [((rows, own_width), bf16)] * toks,
-        [VMEM((2, devices // 2, own_heads * cols, rows), bf16)],
+        [VMEM((2, copies // 2, toks, own_heads * cols, rows), bf16)],
         flops=4 * tokens * tokens * own_width,
         limit=32,
     )
@@ -569,14 +585,8 @@
         "hidden",
         [where_am_i, noisy3, upstream, d_hidden, trans_gain2]
         + att_parts
-        + [(w_out, ANY), (w_hidden_gate, ANY), (w_hidden_up, ANY)],
+        + [w_out, w_hidden_gate, w_hidden_up],
         [((rows, width), f32), ((rows, width), bf16)] + [((own_width, rows), bf16)] * toks,
-        [
-            VMEM((width, width), bf16),
-            VMEM((width, hidden), bf16),
-            VMEM((width, hidden), bf16),
-            pltpu.SemaphoreType.DMA((7,)),
-        ],
         flops=2 * rows * width * (2 * width + 4 * hidden),
     )
     d_res, d_res_b, d_att = results[0], results[1], results[2:]
@@ -596,12 +606,30 @@
     )
     bias_got = swap_copy(bias_sent, 1)
 
-    part_shape = (copies // 2, 2, cut, own_width)
-    kept, sent = call(
+    wide_tiles = tile_count(cut, own_width)
+    single_tiles = tile_count(cut, tokens)
+    found = call(
         functools.partial(first_kernel, copies, toks),
         "first",
+        [where_am_i, slices, x, d_query, d_key, d_value],
+        [((copies // 2, 2 * wide_tiles + single_tiles, 16, 128), bf16)] * 2
+        + [((width, rows), f32)]
+        + [((width, rows), bf16)] * (toks - 1),
+        [
+            VMEM((own_width, width), f32),
+            VMEM((toks, width, rows), f32),
+            VMEM((width, tokens), f32),
+        ],
+        flops=10 * tokens * width * own_width,
+    )
+    kept, sent, d_own = found[:3]
+    got = swap_copy(sent, 1)
+    d_others = [swap_tok(found[2 + r], r) for r in range(1, toks)]
+    kept_b, sent_b = call(
+        functools.partial(second_kernel, copies, toks),
+        "second",
         [where_am_i, x, att, d_value] + d_res_parts,
-        [(part_shape, bf16)] * 2,
+        [((copies // 2, 2 * wide_tiles, 16, 128), bf16)] * 2,
         [
             VMEM((tokens, width), bf16),
             VMEM((own_width, width), f32),
@@ -609,74 +637,48 @@
         ],
         flops=4 * tokens * width * own_width,
     )
-    got = swap_copy(sent, 1)
-
-    found = call(
-        functools.partial(second_kernel, copies, toks),
-        "second",
-        [where_am_i, slices, x, d_query, d_key, d_value],
-        [(part_shape, bf16)] * 2
-        + [((width, rows), f32)]
-        + [((width, rows), bf16)] * (toks - 1),
-        [VMEM((own_width, width), f32), VMEM((toks, width, rows), f32)],
-        flops=10 * tokens * width * own_width,
-    )
-    kept_b, sent_b, d_own = found[:3]
-    d_others = [swap_tok(found[2 + r], r) for r in range(1, toks)]
     got_b = swap_copy(sent_b, 1)
 
-    def halve(name, mask, pairs):
-        outs = []
-        for pair_kept, _ in pairs:
-            outs += [((pair_kept.shape[0] // 2,) + pair_kept.shape[1:], bf16)] * 2
-        flat = [array for one in pairs for array in one]
-        results = call(
-            functools.partial(halve_kernel, mask, len(pairs)), name, [where_am_i] + flat, outs
+    def halve(name, mask, left, kept, got):
+        inner = 1 << sum(1 for other in left if other < mask)
+        left.remove(mask)
+        shape = (kept.shape[0] // 2,) + kept.shape[1:]
+        kept, sent = call(
+            functools.partial(halve_kernel, mask, inner),
+            "%s_%d" % (name, mask),
+            [where_am_i, kept, got],
+            [(shape, bf16)] * 2,
         )
-        return [
-            (results[2 * n], swap_copy(results[2 * n + 1], mask)) for n in range(len(pairs))
-        ]
-
-    chain_a = halve("halve_a2", 2, [(kept, got), (bias_kept, bias_got)])
-    part_shape = (copies // 4, 2, cut, own_width)
-    single_shape = (copies // 4, 2, cut, rows)
-    kept_b, sent_b, single_kept, single_sent = call(
-        functools.partial(halve_single_kernel, toks, copies),
-        "halve_b2",
-        [where_am_i, kept_b, got_b, d_own] + d_others,
-        [(part_shape, bf16)] * 2 + [(single_shape, bf16)] * 2,
-        [VMEM((width, rows), f32)],
-    )
-    chain_b = [(kept_b, swap_copy(sent_b, 2)), (single_kept, swap_copy(single_sent, 2))]
+        return kept, swap_copy(sent, mask)
+
+    masks = [1 << b for b in range(1, copies.bit_length() - 1)]
+    bias_left, first_left, second_left = list(masks), list(masks), list(masks)
+    first, second, bias_chain = (kept, got), (kept_b, got_b), (bias_kept, bias_got)
+    for mask, mask_b in zip(masks, masks[1:] + masks[:1]):
+        bias_chain = halve("bias", mask, bias_left, *bias_chain)
+        first = halve("first", mask, first_left, *first)
+        second = halve("second", mask_b, second_left, *second)
+
+    group = copies // toks
+    swaps = []
+    for c in range(copies):
+        for t in range(toks):
+            swaps.append((c * toks + t, (t * group + c % group) * toks + c // group))
+
+    bias_parts = call(
+        functools.partial(last_bias_kernel, toks),
+        "last_bias",
+        [where_am_i, *bias_chain],
+        [((own_heads * cols, rows), bf16)] * toks,
+        [VMEM((toks, own_heads * cols, rows), bf16)],
+    )
+    bias_parts = [bias_parts[0]] + [swap_tok(bias_parts[r], r) for r in range(1, toks)]
     (grad_noisy,) = call(
         functools.partial(exit_kernel, toks),
         "exit",
         [noisy3, norm_gain2, d_res, d_own] + d_others,
         [((rows, width), bf16)],
     )
-    mask = 4
-    while mask < copies:
-        chain_a = halve("halve_a%d" % mask, mask, chain_a)
-        chain_b = halve("halve_b%d" % mask, mask, chain_b)
-        mask *= 2
-
-    group = copies // toks
-    swaps = []
-    for c in range(copies):
-        for t in range(toks):
-            swaps.append((c * toks + t, (t * group + c % group) * toks + c // group))
-
-    done = call(
-        functools.partial(last_first_kernel, toks),
-        "last_a",
-        [where_am_i] + [array for one in chain_a for array in one],
-        [((cut, own_width), bf16), ((cut, own_width), f32)]
-        + [((own_heads * cols, rows), bf16)] * toks,
-        [VMEM((toks, own_heads * cols, rows), bf16)],
-    )
-    moved_a, grad_out, bias_parts = done[0], done[1], done[2:]
-    bias_parts = [bias_parts[0]] + [swap_tok(bias_parts[r], r) for r in range(1, toks)]
-    moved_a = lax.ppermute(moved_a, ("copy", "tok"), swaps)
     grad_pair, weight_grad = call(
         functools.partial(pair_kernel, toks, cols),
         "pair",
@@ -687,19 +689,27 @@
     )
     weight_grad = jnp.sum(exchange(weight_grad), axis=0)
 
-    moved_b, last_kept, last_sent = call(
+    moved_second, grad_out = call(
         last_second_kernel,
-        "last_b",
-        [where_am_i] + [array for one in chain_b for array in one],
-        [((2, cut, own_width), bf16)] + [((cut, rows), bf16)] * 2,
-        [VMEM((2, cut, rows), bf16)],
-    )
-    last_got = swap_copy(last_sent, 1)
-    moved_b = lax.ppermute(moved_b, ("copy", "tok"), swaps)
+        "last_second",
+        [*second],
+        [((cut, own_width), bf16), ((cut, own_width), f32)],
+    )
+    moved_second = lax.ppermute(moved_second, ("copy", "tok"), swaps)
+    done = call(
+        functools.partial(last_first_kernel, toks),
+        "last_first",
+        [where_am_i, *first],
+        [((2, cut, own_width), bf16)] + [((cut, rows), bf16)] * toks,
+        [VMEM((toks, cut, rows), f32)],
+    )
+    moved_first, singles = done[0], done[1:]
+    moved_first = lax.ppermute(moved_first, ("copy", "tok"), swaps)
+    singles = [singles[0]] + [swap_tok(singles[r], r) for r in range(1, toks)]
     grad_query, grad_key, grad_value, grad_single = call(
         finish_kernel,
         "finish",
-        [moved_a, moved_b, last_kept, last_got],
+        [moved_first, moved_second] + singles,
         [((cut, own_width), f32)] * 3 + [((cut, rows), f32)],
     )
     return (

time: 127 us -> 130 us (1.024)
  blocking collectives: 15.3 us -> 0 us
  waiting for transfers between devices: 41.1 us -> 49.6 us
  starting transfers between devices: 31.3 us -> 38.5 us
  other arithmetic: 0.7 us -> 3.39 us
    all_to_all x1 -> x0, blocking collectives: 15.3 us -> none  [exchange(): lax.all_to_all(value, ('copy', 'tok'), 0, 0, axis_index_groups=groups)]
    ppermute x17 -> x16, starting transfers between devices: 15.1 us -> 22.3 us  [swap_copy(): return lax.ppermute(value, 'copy', [(i, i ^ mask) for i in range(size)])]
    ppermute x17 -> x16, waiting for transfers between devices: 19.2 us -> 25.3 us  [swap_copy(): return lax.ppermute(value, 'copy', [(i, i ^ mask) for i in range(size)])]
    ppermute x6 -> x8, waiting for transfers between devices: 20.7 us -> 24.3 us  [swap_tok(): return lax.ppermute(value, 'tok', [(i, i ^ mask) for i in range(size)])]
    ppermute x6 -> x8, starting transfers between devices: 5.47 us -> 1.92 us  [swap_tok(): return lax.ppermute(value, 'tok', [(i, i ^ mask) for i in range(size)])]
    all_to_all x1, starting transfers between devices: 3.12 us -> 6.62 us  [exchange(): return lax.all_to_all(value, ('copy', 'tok'), 0, 0)]
    concatenate x0 -> x2, other arithmetic: none -> 1.46 us  [per_device(): bias_own = jnp.concatenate([bias_own, swap_copy(bias_own, mask)])]
    reshape x1, local copies, waits for them, and re-layouts: 1.36 us -> 0.01 us  [per_device(): norm_gain2 = norm_gain.reshape(1, width)]
  transfers between devices with their start and end apart: 26 -> 27, of which waited for: 14 -> 14; matrix products, arithmetic and copies ran while one was open for 0% -> 1% of each run, Pallas kernels for 17% -> 13%
where the time goes in v5:
time: 130 us; the launch traced here: 128 us
  waiting for transfers between devices  49.6 us (38%)
  starting transfers between devices  38.5 us (30%)
  Pallas kernels  32 us (25%)
  local copies, waits for them, and re-layouts  3.39 us (3%)
  other arithmetic  3.39 us (3%)
    pallas_call x24, Pallas kernels, call(): pl.pallas_call(whole, name=name, out_shape=[jax.ShapeDtypeStruct(shape, k...  32 us
    ppermute x16, waiting for transfers between devices, swap_copy(): return lax.ppermute(value, 'copy', [(i, i ^ mask) for i in range(size)])  25.3 us
    ppermute x8, waiting for transfers between devices, swap_tok(): return lax.ppermute(value, 'tok', [(i, i ^ mask) for i in range(size)])  24.3 us
    ppermute x16, starting transfers between devices, swap_copy(): return lax.ppermute(value, 'copy', [(i, i ^ mask) for i in range(size)])  22.3 us
    all_to_all x1, starting transfers between devices, exchange(): return lax.all_to_all(value, ('copy', 'tok'), 0, 0)  6.62 us
    ppermute x1, starting transfers between devices, per_device(): moved_second = lax.ppermute(moved_second, ('copy', 'tok'), swaps)  5.71 us
    unnamed x42, local copies, waits for them, and re-layouts  3.36 us
  transfers between devices with their start and end apart: 27, of which 14 were waited for; matrix products, arithmetic and copies ran while one was open for 1% of the time, Pallas kernels for 13%

profile of v5, /device:TPU:2, one launch (start us, length us, event | category | flops | bytes accessed | tf_op | source)
XLA Modules:
  0.0 127.9 jit_solution(6247922637866673869)
XLA Ops:
  0.7 0.6 pad_add_fusion.refs_0_
  1.3 4.1 %enter.1 = (bf16[128,768]{1,0:T(8,128)(2,1)}, bf16[64,128]{1,0:T(8,128)(2,1)}, bf16[64,128]{1,0:T(8,128)(2,1)}) custom-call(s32[2]{0:T(128)} %pad_add_fusion.refs_0_, bf16[128,768]{1,0:T(8,128)(2,1)} %bitcast.24, bf16[128,768]{1,0:T(8,128)(2,1)} %refs_2_.1, s32[1,128]{1,0:T(1,128)} %bitcast.41, bf16[32,768]{1,0:T(8,128)(2,1)} %refs_4_.3, f32[768]{0:T(1024)} %refs_5_.3, ...), custom_call_target="tpu_custom_call" | custom-call | flops 67108864 | bytes 1202184 | tf_op jit(solution)/shard_map/enter/pallas_call | solution.py:75
  5.4 3.9 %collective-permute-done.1 = bf16[64,128]{1,0:T(8,128)(2,1)S(1)} collective-permute-done((bf16[64,128]{1,0:T(8,128)(2,1)}, bf16[64,128]{1,0:T(8,128)(2,1)S(1)}, u32[]{:S(2)}, u32[]{:S(2)}) %collective-permute-start.1) | collective-permute-done | bytes 16416 | tf_op jit(solution)/shard_map/ppermute | solution.py:467
  9.4 0.7 pad_maximum_fusion.2
  10.1 2.6 %collective-permute-start.2 = (bf16[2,64,128]{2,1,0:T(8,128)(2,1)S(1)}, bf16[2,64,128]{2,1,0:T(8,128)(2,1)S(1)}, u32[]{:S(2)}, u32[]{:S(2)}) collective-permute-start(bf16[2,64,128]{2,1,0:T(8,128)(2,1)S(1)} %pad_maximum_fusion.2), channel_id=1, source_target_pairs={{0,16},{2,18},{4,20},{6,22},{8,24},{10,26},{12,28},{14,30},{16,0},... | collective-permute-start | bytes 98312 | tf_op jit(solution)/shard_map/ppermute | solution.py:462
  12.7 0.7 constant_dynamic-update-slice_fusion.4
  13.4 1.5 %collective-permute-done.2 = bf16[2,64,128]{2,1,0:T(8,128)(2,1)S(1)} collective-permute-done((bf16[2,64,128]{2,1,0:T(8,128)(2,1)S(1)}, bf16[2,64,128]{2,1,0:T(8,128)(2,1)S(1)}, u32[]{:S(2)}, u32[]{:S(2)}) %collective-permute-start.2) | collective-permute-done | bytes 32800 | tf_op jit(solution)/shard_map/ppermute | solution.py:462
  14.9 0.7 pad_maximum_fusion.1
  15.6 1.6 %collective-permute-start.3 = (bf16[4,64,128]{2,1,0:T(8,128)(2,1)S(1)}, bf16[4,64,128]{2,1,0:T(8,128)(2,1)S(1)}, u32[]{:S(2)}, u32[]{:S(2)}) collective-permute-start(bf16[4,64,128]{2,1,0:T(8,128)(2,1)S(1)} %pad_maximum_fusion.1), channel_id=1, source_target_pairs={{0,8},{2,10},{4,12},{6,14},{8,0},{10,2},{12,4},{14,6},{16,24},{18,... | collective-permute-start | bytes 196616 | tf_op jit(solution)/shard_map/ppermute | solution.py:462
  17.2 2.7 %collective-permute-done.3 = bf16[4,64,128]{2,1,0:T(8,128)(2,1)S(1)} collective-permute-done((bf16[4,64,128]{2,1,0:T(8,128)(2,1)S(1)}, bf16[4,64,128]{2,1,0:T(8,128)(2,1)S(1)}, u32[]{:S(2)}, u32[]{:S(2)}) %collective-permute-start.3) | collective-permute-done | bytes 65568 | tf_op jit(solution)/shard_map/ppermute | solution.py:462
  19.9 0.7 pad_maximum_fusion
  20.6 1.6 %collective-permute-start.4 = (bf16[8,64,128]{2,1,0:T(8,128)(2,1)S(1)}, bf16[8,64,128]{2,1,0:T(8,128)(2,1)S(1)}, u32[]{:S(2)}, u32[]{:S(2)}) collective-permute-start(bf16[8,64,128]{2,1,0:T(8,128)(2,1)S(1)} %pad_maximum_fusion), channel_id=1, source_target_pairs={{0,4},{2,6},{4,0},{6,2},{8,12},{10,14},{12,8},{14,10},{16,20},{18,... | collective-permute-start | bytes 393224 | tf_op jit(solution)/shard_map/ppermute | solution.py:462
  22.3 3.4 %collective-permute-done.4 = bf16[8,64,128]{2,1,0:T(8,128)(2,1)S(1)} collective-permute-done((bf16[8,64,128]{2,1,0:T(8,128)(2,1)S(1)}, bf16[8,64,128]{2,1,0:T(8,128)(2,1)S(1)}, u32[]{:S(2)}, u32[]{:S(2)}) %collective-permute-start.4) | collective-permute-done | bytes 131104 | tf_op jit(solution)/shard_map/ppermute | solution.py:462
  26.1 1.3 copy-done.5
  27.3 1.3 copy-done.6
  28.6 1.0 stage.1
  29.6 3.7 %collective-permute-done.refs_3_ = bf16[128,768]{1,0:T(8,128)(2,1)S(1)} collective-permute-done((bf16[128,768]{1,0:T(8,128)(2,1)}, bf16[128,768]{1,0:T(8,128)(2,1)S(1)}, u32[]{:S(2)}, u32[]{:S(2)}) %collective-permute-start) | collective-permute-done | bytes 196640 | tf_op jit(solution)/shard_map/ppermute | solution.py:467
  33.3 1.4 %project.1 = (bf16[256,768]{1,0:T(8,128)(2,1)S(1)}, bf16[384,256]{1,0:T(8,128)(2,1)S(1)}, bf16[384,256]{1,0:T(8,128)(2,1)S(1)}, bf16[384,256]{1,0:T(8,128)(2,1)S(1)}) custom-call(s32[2]{0:T(128)S(1)} %copy-done.11, bf16[3,768,384]{2,1,0:T(8,128)(2,1)S(1)} %get-tuple-element.77.refs_1_, bf16[128,768]{1,0:T(8,128)(2,1)S(1)} %copy-done.10, ...), custom_call_target="tpu_custom_call" | custom-call | flops 452984832 | bytes 3145736 | tf_op jit(solution)/shard_map/project/pallas_call | solution.py:75
  34.8 2.1 %attention.1 = (bf16[4,256,256]{2,1,0:T(8,128)(2,1)S(1)}, bf16[256,384]{1,0:T(8,128)(2,1)S(1)}, bf16[128,384]{1,0:T(8,128)(2,1)S(1)}, bf16[128,384]{1,0:T(8,128)(2,1)S(1)}) custom-call(s32[2]{0:T(128)S(1)} %copy-done.11, bf16[384,256]{1,0:T(8,128)(2,1)S(1)} %get-tuple-element.79.refs_1_, bf16[384,256]{1,0:T(8,128)(2,1)S(1)} %get-tuple-element.80.refs_2_, ...), custom_call_target="tpu_custom_call" | custom-call | flops 100663296 | bytes 2163720 | tf_op jit(solution)/shard_map/attention/pallas_call | solution.py:75
  36.9 0.3 collective-permute-start.6
  37.3 0.9 down.1
  38.2 3.4 %collective-permute-done.6.refs_6_ = bf16[128,384]{1,0:T(8,128)(2,1)S(1)} collective-permute-done((bf16[128,384]{1,0:T(8,128)(2,1)S(1)}, bf16[128,384]{1,0:T(8,128)(2,1)S(1)}, u32[]{:S(2)}, u32[]{:S(2)}) %collective-permute-start.6) | collective-permute-done | bytes 98336 | tf_op jit(solution)/shard_map/ppermute | solution.py:467
  41.6 4.3 %hidden.1 = (f32[128,768]{1,0:T(8,128)S(1)}, bf16[128,768]{1,0:T(8,128)(2,1)S(1)}, bf16[384,128]{1,0:T(8,128)(2,1)S(1)}, bf16[384,128]{1,0:T(8,128)(2,1)S(1)}) custom-call(s32[2]{0:T(128)S(1)} %copy-done.11, bf16[128,768]{1,0:T(8,128)(2,1)S(1)} %get-tuple-element.73.refs_1_.refs_0_, bf16[128,768]{1,0:T(8,128)(2,1)S(1)} %get-tuple-element.74.refs_2_, ...), custom_call_target="tpu_custom_call" | custom-call | flops 1509949440 | bytes 8064008 | tf_op jit(solution)/shard_map/hidden/pallas_call | solution.py:75
  46.2 4.4 %collective-permute-done.7.refs_6_ = bf16[384,128]{1,0:T(8,128)(2,1)S(1)} collective-permute-done((bf16[384,128]{1,0:T(8,128)(2,1)S(1)}, bf16[384,128]{1,0:T(8,128)(2,1)S(1)}, u32[]{:S(2)}, u32[]{:S(2)}) %collective-permute-start.7) | collective-permute-done | bytes 98336 | tf_op jit(solution)/shard_map/ppermute | solution.py:467
  50.6 2.0 %backward.1 = (bf16[384,256]{1,0:T(8,128)(2,1)S(1)}, bf16[384,256]{1,0:T(8,128)(2,1)S(1)}, bf16[384,256]{1,0:T(8,128)(2,1)S(1)}, bf16[8,64,256]{2,1,0:T(8,128)(2,1)S(1)}, bf16[8,64,256]{2,1,0:T(8,128)(2,1)S(1)}) custom-call(s32[2]{0:T(128)S(1)} %copy-done.11, bf16[384,256]{1,0:T(8,128)(2,1)S(1)} %get-tuple-element.79.refs_1_, ...), custom_call_target="tpu_custom_call" | custom-call | flops 201326592 | bytes 2424840 | tf_op jit(solution)/shard_map/backward/pallas_call | solution.py:75
  52.6 2.1 %first.1 = (bf16[8,24,16,128]{3,2,1,0:T(8,128)(2,1)S(1)}, bf16[8,24,16,128]{3,2,1,0:T(8,128)(2,1)S(1)}, f32[768,128]{1,0:T(8,128)S(1)}, bf16[768,128]{1,0:T(8,128)(2,1)S(1)}) custom-call(s32[2]{0:T(128)S(1)} %copy-done.11, bf16[3,768,384]{2,1,0:T(8,128)(2,1)S(1)} %get-tuple-element.77.refs_1_, bf16[256,768]{1,0:T(8,128)(2,1)S(1)} %get-tuple-element.89.refs_2_.refs_1_, ...), custom_call_target="tpu_custom_call" | custom-call | flops 754974720 | bytes 4915208 | tf_op jit(solution)/shard_map/first/pallas_call | solution.py:75
  54.8 0.3 collective-permute-start.14
  55.1 7.0 %collective-permute-done.14.refs_5_ = bf16[128,768]{1,0:T(8,128)(2,1)S(1)} collective-permute-done((bf16[128,768]{1,0:T(8,128)(2,1)S(1)}, bf16[128,768]{1,0:T(8,128)(2,1)S(1)}, u32[]{:S(2)}, u32[]{:S(2)}) %collective-permute-start.14) | collective-permute-done | bytes 196640 | tf_op jit(solution)/shard_map/ppermute | solution.py:467
  62.1 1.4 %second.1 = (bf16[8,18,16,128]{3,2,1,0:T(8,128)(2,1)S(1)}, bf16[8,18,16,128]{3,2,1,0:T(8,128)(2,1)S(1)}) custom-call(s32[2]{0:T(128)S(1)} %copy-done.11, bf16[256,768]{1,0:T(8,128)(2,1)S(1)} %get-tuple-element.89.refs_2_.refs_1_, bf16[256,384]{1,0:T(8,128)(2,1)S(1)} %get-tuple-element.107.refs_2_, bf16[384,256]{1,0:T(8,128)(2,1)S(1)} %get-tuple-element.95.refs_5_.refs_3_, ...), custom_call_target="tpu_custom_call" | custom-call | flops 301989888 | bytes 2359304 | tf_op jit(solution)/shard_map/second/pallas_call | solution.py:75
  63.6 0.5 collective-permute-start.21
  64.1 0.7 first_2.1
  64.8 1.6 %collective-permute-start.10 = (bf16[4,24,16,128]{3,2,1,0:T(8,128)(2,1)S(1)}, bf16[4,24,16,128]{3,2,1,0:T(8,128)(2,1)S(1)}, u32[]{:S(2)}, u32[]{:S(2)}) collective-permute-start(bf16[4,24,16,128]{3,2,1,0:T(8,128)(2,1)S(1)} %get-tuple-element.101), channel_id=1, source_target_pairs={{0,4},{2,6},{4,0},{6,2},{8,12},{10,14},{12,8},{14,10},{16,20},{18,... | collective-permute-start | bytes 1179656 | tf_op jit(solution)/shard_map/ppermute | solution.py:462
  66.4 0.7 second_4.1
  67.1 1.7 %collective-permute-start.16 = (bf16[4,18,16,128]{3,2,1,0:T(8,128)(2,1)S(1)}, bf16[4,18,16,128]{3,2,1,0:T(8,128)(2,1)S(1)}, u32[]{:S(2)}, u32[]{:S(2)}) collective-permute-start(bf16[4,18,16,128]{3,2,1,0:T(8,128)(2,1)S(1)} %get-tuple-element.113), channel_id=1, source_target_pairs={{0,8},{2,10},{4,12},{6,14},{8,0},{10,2},{12,4},{14,6},{16,24},{18,... | collective-permute-start | bytes 884744 | tf_op jit(solution)/shard_map/ppermute | solution.py:462
  68.7 0.6 bias_2.1
  69.4 0.7 collective-permute-start.22
  70.1 8.7 %collective-permute-done.22.refs_2_ = bf16[4,64,256]{2,1,0:T(8,128)(2,1)S(1)} collective-permute-done((bf16[4,64,256]{2,1,0:T(8,128)(2,1)S(1)}, bf16[4,64,256]{2,1,0:T(8,128)(2,1)S(1)}, u32[]{:S(2)}, u32[]{:S(2)}) %collective-permute-start.22) | collective-permute-done | bytes 131104 | tf_op jit(solution)/shard_map/ppermute | solution.py:462
  78.8 0.6 bias_4.1
  79.4 1.6 %collective-permute-start.23 = (bf16[2,64,256]{2,1,0:T(8,128)(2,1)S(1)}, bf16[2,64,256]{2,1,0:T(8,128)(2,1)S(1)}, u32[]{:S(2)}, u32[]{:S(2)}) collective-permute-start(bf16[2,64,256]{2,1,0:T(8,128)(2,1)S(1)} %get-tuple-element.127), channel_id=1, source_target_pairs={{0,8},{2,10},{4,12},{6,14},{8,0},{10,2},{12,4},{14,6},{16,24},{18,... | collective-permute-start | bytes 196616 | tf_op jit(solution)/shard_map/ppermute | solution.py:462
  81.0 0.6 first_4.1
  81.7 0.5 collective-permute-start.11
  82.2 1.9 %collective-permute-done.23.refs_2_ = bf16[2,64,256]{2,1,0:T(8,128)(2,1)S(1)} collective-permute-done((bf16[2,64,256]{2,1,0:T(8,128)(2,1)S(1)}, bf16[2,64,256]{2,1,0:T(8,128)(2,1)S(1)}, u32[]{:S(2)}, u32[]{:S(2)}) %collective-permute-start.23) | collective-permute-done | bytes 65568 | tf_op jit(solution)/shard_map/ppermute | solution.py:462
  84.1 0.6 bias_8.1
  84.7 2.5 %collective-permute-start.24 = (bf16[1,64,256]{2,1,0:T(8,128)(2,1)S(1)}, bf16[1,64,256]{2,1,0:T(8,128)(2,1)S(1)}, u32[]{:S(2)}, u32[]{:S(2)}) collective-permute-start(bf16[1,64,256]{2,1,0:T(8,128)(2,1)S(1)} %get-tuple-element.129), channel_id=1, source_target_pairs={{0,16},{2,18},{4,20},{6,22},{8,24},{10,26},{12,28},{14,30},{16,0},... | collective-permute-start | bytes 98312 | tf_op jit(solution)/shard_map/ppermute | solution.py:462
  87.2 2.4 %collective-permute-done.24.refs_2_ = bf16[1,64,256]{2,1,0:T(8,128)(2,1)S(1)} collective-permute-done((bf16[1,64,256]{2,1,0:T(8,128)(2,1)S(1)}, bf16[1,64,256]{2,1,0:T(8,128)(2,1)S(1)}, u32[]{:S(2)}, u32[]{:S(2)}) %collective-permute-start.24) | collective-permute-done | bytes 32800 | tf_op jit(solution)/shard_map/ppermute | solution.py:462
  89.6 0.6 last_bias.1
  90.4 0.6 second_8.1
  91.0 2.9 %collective-permute-start.17 = (bf16[2,18,16,128]{3,2,1,0:T(8,128)(2,1)S(1)}, bf16[2,18,16,128]{3,2,1,0:T(8,128)(2,1)S(1)}, u32[]{:S(2)}, u32[]{:S(2)}) collective-permute-start(bf16[2,18,16,128]{3,2,1,0:T(8,128)(2,1)S(1)} %get-tuple-element.115), channel_id=1, source_target_pairs={{0,16},{2,18},{4,20},{6,22},{8,24},{10,26},{12,28},{14,30},{16,0},... | collective-permute-start | bytes 442376 | tf_op jit(solution)/shard_map/ppermute | solution.py:462
  94.0 3.4 %pair.1 = (bf16[2048,128]{1,0:T(8,128)(2,1)}, f32[32,8,128]{2,1,0:T(8,128)}) custom-call(s32[2]{0:T(128)S(1)} %copy-done.11, bf16[2048,128]{1,0:T(8,128)(2,1)S(1)} %bitcast.23, f32[1,128]{1,0:T(1,128)S(1)} %bitcast.30, bf16[8,128]{1,0:T(8,128)(2,1)S(1)} %bitcast.28, bf16[64,128]{1,0:T(8,128)(2,1)S(1)} %get-tuple-element.130.refs_4_, ...), custom_call_target="tpu_custom_call" | custom-call | flops 134217728 | bytes 1214984 | tf_op jit(solution)/shard_map/pair/pallas_call | solution.py:75
  97.4 6.6 %all-to-all-start = ((f32[32,8,128]{2,1,0:T(8,128)}), f32[32,8,128]{2,1,0:T(8,128)S(1)}, u32[]{:S(2)}, u32[]{:S(2)}) async-start(f32[32,8,128]{2,1,0:T(8,128)} %get-tuple-element.137), calls=%async_computation | async-start | bytes 262144 | tf_op jit(solution)/shard_map/all_to_all | solution.py:471
  104.0 0.3 collective-permute-start.8
  104.4 0.6 first_8.1
  105.0 2.7 %collective-permute-start.12 = (bf16[1,24,16,128]{3,2,1,0:T(8,128)(2,1)S(1)}, bf16[1,24,16,128]{3,2,1,0:T(8,128)(2,1)S(1)}, u32[]{:S(2)}, u32[]{:S(2)}) collective-permute-start(bf16[1,24,16,128]{3,2,1,0:T(8,128)(2,1)S(1)} %get-tuple-element.105), channel_id=1, source_target_pairs={{0,16},{2,18},{4,20},{6,22},{8,24},{10,26},{12,28},{14,30},{16,0},... | collective-permute-start | bytes 294920 | tf_op jit(solution)/shard_map/ppermute | solution.py:462
  107.7 0.6 second_2.1
  108.3 1.5 %collective-permute-start.18 = (bf16[1,18,16,128]{3,2,1,0:T(8,128)(2,1)S(1)}, bf16[1,18,16,128]{3,2,1,0:T(8,128)(2,1)S(1)}, u32[]{:S(2)}, u32[]{:S(2)}) collective-permute-start(bf16[1,18,16,128]{3,2,1,0:T(8,128)(2,1)S(1)} %get-tuple-element.117), channel_id=1, source_target_pairs={{0,4},{2,6},{4,0},{6,2},{8,12},{10,14},{12,8},{14,10},{16,20},{18,... | collective-permute-start | bytes 221192 | tf_op jit(solution)/shard_map/ppermute | solution.py:462
  109.8 4.7 %collective-permute-done.12.refs_2_ = bf16[1,24,16,128]{3,2,1,0:T(8,128)(2,1)S(1)} collective-permute-done((bf16[1,24,16,128]{3,2,1,0:T(8,128)(2,1)S(1)}, bf16[1,24,16,128]{3,2,1,0:T(8,128)(2,1)S(1)}, u32[]{:S(2)}, u32[]{:S(2)}) %collective-permute-start.12) | collective-permute-done | bytes 98336 | tf_op jit(solution)/shard_map/ppermute | solution.py:462
  114.5 0.6 last_first.1
  115.1 1.9 %collective-permute-start.13 = (bf16[2,48,384]{2,1,0:T(8,128)(2,1)S(1)}, bf16[2,48,384]{2,1,0:T(8,128)(2,1)S(1)}, u32[]{:S(2)}, u32[]{:S(2)}) collective-permute-start(bf16[2,48,384]{2,1,0:T(8,128)(2,1)S(1)} %get-tuple-element.106), channel_id=1, source_target_pairs={{0,0},{1,16},{2,2},{3,18},{4,4},{5,20},{6,6},{7,22},{8,8},{9,24},{... | collective-permute-start | bytes 221192 | tf_op jit(solution)/shard_map/ppermute | solution.py:707
  117.0 0.6 last_second.1
  117.7 5.7 %collective-permute-start.19 = (bf16[48,384]{1,0:T(8,128)(2,1)S(1)}, bf16[48,384]{1,0:T(8,128)(2,1)S(1)}, u32[]{:S(2)}, u32[]{:S(2)}) collective-permute-start(bf16[48,384]{1,0:T(8,128)(2,1)S(1)} %get-tuple-element.118), channel_id=1, source_target_pairs={{0,0},{1,16},{2,2},{3,18},{4,4},{5,20},{6,6},{7,22},{8,8},{9,24},{... | collective-permute-start | bytes 110600 | tf_op jit(solution)/shard_map/ppermute | solution.py:698
  123.5 1.2 exit.1
  124.7 0.6 reduce_sum.9
  125.3 1.8 %collective-permute-done.20.refs_3_ = bf16[48,128]{1,0:T(8,128)(2,1)S(1)} collective-permute-done((bf16[48,128]{1,0:T(8,128)(2,1)S(1)}, bf16[48,128]{1,0:T(8,128)(2,1)S(1)}, u32[]{:S(2)}, u32[]{:S(2)}) %collective-permute-start.20) | collective-permute-done | bytes 12320 | tf_op jit(solution)/shard_map/ppermute | solution.py:467
  127.2 0.7 finish.1
  (64 shorter events, 1.4 us)
Async XLA Ops:
  0.6 25.4 %copy-start.15 = (s32[256]{0:T(256)S(1)}, s32[256]{0:T(256)}, u32[]{:S(2)}) copy-start(s32[256]{0:T(256)} %param.24) | copy-start | bytes 3076
  0.6 25.4 %copy-start.16 = (s32[256]{0:T(256)S(1)}, s32[256]{0:T(256)}, u32[]{:S(2)}) copy-start(s32[256]{0:T(256)} %param.25) | copy-start | bytes 3076
  0.7 25.4 %copy-start.4 = (bf16[768,768]{1,0:T(8,128)(2,1)S(1)}, bf16[768,768]{1,0:T(8,128)(2,1)}, u32[]{:S(2)}) copy-start(bf16[768,768]{1,0:T(8,128)(2,1)} %refs_4_.2) | copy-start | bytes 3538948
  0.7 25.4 %copy-start.13 = (f32[6,8]{1,0:T(8,128)S(1)}, f32[6,8]{1,0:T(8,128)}, u32[]{:S(2)}) copy-start(f32[6,8]{1,0:T(8,128)} %refs_3_.1) | copy-start | bytes 580
  1.3 24.8 %copy-start.11 = (s32[2]{0:T(128)S(1)}, s32[2]{0:T(128)}, u32[]{:S(2)}) copy-start(s32[2]{0:T(128)} %pad_add_fusion.refs_0_) | copy-start | bytes 28
  5.4 4.0 %collective-permute-start.1 = (bf16[64,128]{1,0:T(8,128)(2,1)}, bf16[64,128]{1,0:T(8,128)(2,1)S(1)}, u32[]{:S(2)}, u32[]{:S(2)}) collective-permute-start(bf16[64,128]{1,0:T(8,128)(2,1)} %get-tuple-element.83), channel_id=1, source_target_pairs={{0,1},{1,0},{2,3},{3,2},{4,5},{5,4},{6,7},{7,6},{8,9},{9,8},{10,11... | collective-permute-start | bytes 49160 | tf_op jit(solution)/shard_map/ppermute | solution.py:467
  10.1 4.8 %collective-permute-start.2 = (bf16[2,64,128]{2,1,0:T(8,128)(2,1)S(1)}, bf16[2,64,128]{2,1,0:T(8,128)(2,1)S(1)}, u32[]{:S(2)}, u32[]{:S(2)}) collective-permute-start(bf16[2,64,128]{2,1,0:T(8,128)(2,1)S(1)} %pad_maximum_fusion.2), channel_id=1, source_target_pairs={{0,16},{2,18},{4,20},{6,22},{8,24},{10,26},{12,28},{14,30},{16,0},... | collective-permute-start | bytes 98312 | tf_op jit(solution)/shard_map/ppermute | solution.py:462
  15.6 4.3 %collective-permute-start.3 = (bf16[4,64,128]{2,1,0:T(8,128)(2,1)S(1)}, bf16[4,64,128]{2,1,0:T(8,128)(2,1)S(1)}, u32[]{:S(2)}, u32[]{:S(2)}) collective-permute-start(bf16[4,64,128]{2,1,0:T(8,128)(2,1)S(1)} %pad_maximum_fusion.1), channel_id=1, source_target_pairs={{0,8},{2,10},{4,12},{6,14},{8,0},{10,2},{12,4},{14,6},{16,24},{18,... | collective-permute-start | bytes 196616 | tf_op jit(solution)/shard_map/ppermute | solution.py:462
  20.6 5.0 %collective-permute-start.4 = (bf16[8,64,128]{2,1,0:T(8,128)(2,1)S(1)}, bf16[8,64,128]{2,1,0:T(8,128)(2,1)S(1)}, u32[]{:S(2)}, u32[]{:S(2)}) collective-permute-start(bf16[8,64,128]{2,1,0:T(8,128)(2,1)S(1)} %pad_maximum_fusion), channel_id=1, source_target_pairs={{0,4},{2,6},{4,0},{6,2},{8,12},{10,14},{12,8},{14,10},{16,20},{18,... | collective-permute-start | bytes 393224 | tf_op jit(solution)/shard_map/ppermute | solution.py:462
  25.7 9.0 %collective-permute-start.5 = (bf16[16,64,128]{2,1,0:T(8,128)(2,1)S(1)}, bf16[16,64,128]{2,1,0:T(8,128)(2,1)S(1)}, u32[]{:S(2)}, u32[]{:S(2)}) collective-permute-start(bf16[16,64,128]{2,1,0:T(8,128)(2,1)S(1)} %constant_dynamic-update-slice_fusion.refs_4_), channel_id=1, source_target_pairs={{0,2},{2,0},{4,6},{6,4},{8,10},{10,8},{12,14},{14,12},{16,18},{18,... | collective-permute-start | bytes 786440 | tf_op jit(solution)/shard_map/ppermute | solution.py:462
  25.8 7.5 %collective-permute-start = (bf16[128,768]{1,0:T(8,128)(2,1)}, bf16[128,768]{1,0:T(8,128)(2,1)S(1)}, u32[]{:S(2)}, u32[]{:S(2)}) collective-permute-start(bf16[128,768]{1,0:T(8,128)(2,1)} %get-tuple-element.78.refs_2_), channel_id=1, source_target_pairs={{0,1},{1,0},{2,3},{3,2},{4,5},{5,4},{6,7},{7,6},{8,9},{9,8},{10,11... | collective-permute-start | bytes 589832 | tf_op jit(solution)/shard_map/ppermute | solution.py:467
  26.1 1.3 copy-start.5
  27.3 1.3 copy-start.6
  28.6 4.7 %copy-start.10 = (bf16[128,768]{1,0:T(8,128)(2,1)S(1)}, bf16[128,768]{1,0:T(8,128)(2,1)}, u32[]{:S(2)}) copy-start(bf16[128,768]{1,0:T(8,128)(2,1)} %get-tuple-element.78.refs_2_) | copy-start | bytes 589828
  28.6 8.6 %copy-start.2 = (bf16[1536,768]{1,0:T(8,128)(2,1)S(1)}, bf16[1536,768]{1,0:T(8,128)(2,1)}, u32[]{:S(2)}) copy-start(bf16[1536,768]{1,0:T(8,128)(2,1)} %refs_1_.1) | copy-start | bytes 7077892
  28.6 8.6 %copy-start.9 = (bf16[1,128,768]{2,1,0:T(8,128)(2,1)S(1)}, bf16[1,128,768]{2,1,0:T(8,128)(2,1)}, u32[]{:S(2)}) copy-start(bf16[1,128,768]{2,1,0:T(8,128)(2,1)} %param.39) | copy-start | bytes 589828
  29.6 7.6 %copy-start.18 = (f32[768]{0:T(1024)S(1)}, f32[768]{0:T(1024)}, u32[]{:S(2)}) copy-start(f32[768]{0:T(1024)} %param.29) | copy-start | bytes 9220
  29.6 7.6 %copy-start.8 = (bf16[1,128,768]{2,1,0:T(8,128)(2,1)S(1)}, bf16[1,128,768]{2,1,0:T(8,128)(2,1)}, u32[]{:S(2)}) copy-start(bf16[1,128,768]{2,1,0:T(8,128)(2,1)} %param.20) | copy-start | bytes 589828
  33.3 8.3 %copy-start.1 = (bf16[768,1536]{1,0:T(8,128)(2,1)S(1)}, bf16[768,1536]{1,0:T(8,128)(2,1)}, u32[]{:S(2)}) copy-start(bf16[768,1536]{1,0:T(8,128)(2,1)} %refs_9_.1) | copy-start | bytes 7077892
  34.7 6.9 %copy-start = (bf16[768,1536]{1,0:T(8,128)(2,1)S(1)}, bf16[768,1536]{1,0:T(8,128)(2,1)}, u32[]{:S(2)}) copy-start(bf16[768,1536]{1,0:T(8,128)(2,1)} %refs_8_.1) | copy-start | bytes 7077892
  34.7 6.9 %copy-start.7 = (bf16[768,768]{1,0:T(8,128)(2,1)S(1)}, bf16[768,768]{1,0:T(8,128)(2,1)}, u32[]{:S(2)}) copy-start(bf16[768,768]{1,0:T(8,128)(2,1)} %refs_7_.1) | copy-start | bytes 3538948
  36.9 4.7 %collective-permute-start.6 = (bf16[128,384]{1,0:T(8,128)(2,1)S(1)}, bf16[128,384]{1,0:T(8,128)(2,1)S(1)}, u32[]{:S(2)}, u32[]{:S(2)}) collective-permute-start(bf16[128,384]{1,0:T(8,128)(2,1)S(1)} %get-tuple-element.87), channel_id=1, source_target_pairs={{0,1},{1,0},{2,3},{3,2},{4,5},{5,4},{6,7},{7,6},{8,9},{9,8},{10,11... | collective-permute-start | bytes 294920 | tf_op jit(solution)/shard_map/ppermute | solution.py:467
  45.9 4.7 %collective-permute-start.7 = (bf16[384,128]{1,0:T(8,128)(2,1)S(1)}, bf16[384,128]{1,0:T(8,128)(2,1)S(1)}, u32[]{:S(2)}, u32[]{:S(2)}) collective-permute-start(bf16[384,128]{1,0:T(8,128)(2,1)S(1)} %get-tuple-element.92), channel_id=1, source_target_pairs={{0,1},{1,0},{2,3},{3,2},{4,5},{5,4},{6,7},{7,6},{8,9},{9,8},{10,11... | collective-permute-start | bytes 294920 | tf_op jit(solution)/shard_map/ppermute | solution.py:467
  54.7 9.3 %collective-permute-start.9 = (bf16[8,24,16,128]{3,2,1,0:T(8,128)(2,1)S(1)}, bf16[8,24,16,128]{3,2,1,0:T(8,128)(2,1)S(1)}, u32[]{:S(2)}, u32[]{:S(2)}) collective-permute-start(bf16[8,24,16,128]{3,2,1,0:T(8,128)(2,1)S(1)} %get-tuple-element.99), channel_id=1, source_target_pairs={{0,2},{2,0},{4,6},{6,4},{8,10},{10,8},{12,14},{14,12},{16,18},{18,... | collective-permute-start | bytes 2359304 | tf_op jit(solution)/shard_map/ppermute | solution.py:462
  54.8 7.3 %collective-permute-start.14 = (bf16[128,768]{1,0:T(8,128)(2,1)S(1)}, bf16[128,768]{1,0:T(8,128)(2,1)S(1)}, u32[]{:S(2)}, u32[]{:S(2)}) collective-permute-start(bf16[128,768]{1,0:T(8,128)(2,1)S(1)} %get-tuple-element.109.refs_4_), channel_id=1, source_target_pairs={{0,1},{1,0},{2,3},{3,2},{4,5},{5,4},{6,7},{7,6},{8,9},{9,8},{10,11... | collective-permute-start | bytes 589832 | tf_op jit(solution)/shard_map/ppermute | solution.py:467
  63.5 2.9 %collective-permute-start.15 = (bf16[8,18,16,128]{3,2,1,0:T(8,128)(2,1)S(1)}, bf16[8,18,16,128]{3,2,1,0:T(8,128)(2,1)S(1)}, u32[]{:S(2)}, u32[]{:S(2)}) collective-permute-start(bf16[8,18,16,128]{3,2,1,0:T(8,128)(2,1)S(1)} %get-tuple-element.111), channel_id=1, source_target_pairs={{0,2},{2,0},{4,6},{6,4},{8,10},{10,8},{12,14},{14,12},{16,18},{18,... | collective-permute-start | bytes 1769480 | tf_op jit(solution)/shard_map/ppermute | solution.py:462
  63.6 5.2 %collective-permute-start.21 = (bf16[8,64,256]{2,1,0:T(8,128)(2,1)S(1)}, bf16[8,64,256]{2,1,0:T(8,128)(2,1)S(1)}, u32[]{:S(2)}, u32[]{:S(2)}) collective-permute-start(bf16[8,64,256]{2,1,0:T(8,128)(2,1)S(1)} %get-tuple-element.123), channel_id=1, source_target_pairs={{0,2},{2,0},{4,6},{6,4},{8,10},{10,8},{12,14},{14,12},{16,18},{18,... | collective-permute-start | bytes 786440 | tf_op jit(solution)/shard_map/ppermute | solution.py:462
  64.8 16.2 %collective-permute-start.10 = (bf16[4,24,16,128]{3,2,1,0:T(8,128)(2,1)S(1)}, bf16[4,24,16,128]{3,2,1,0:T(8,128)(2,1)S(1)}, u32[]{:S(2)}, u32[]{:S(2)}) collective-permute-start(bf16[4,24,16,128]{3,2,1,0:T(8,128)(2,1)S(1)} %get-tuple-element.101), channel_id=1, source_target_pairs={{0,4},{2,6},{4,0},{6,2},{8,12},{10,14},{12,8},{14,10},{16,20},{18,... | collective-permute-start | bytes 1179656 | tf_op jit(solution)/shard_map/ppermute | solution.py:462
  66.4 27.6 %copy-start.3 = (bf16[128,16,128]{2,1,0:T(8,128)(2,1)S(1)}, bf16[128,16,128]{2,1,0:T(8,128)(2,1)}, u32[]{:S(2)}) copy-start(bf16[128,16,128]{2,1,0:T(8,128)(2,1)} %param.22) | copy-start | bytes 1572868
  66.4 27.6 %copy-start.12 = (bf16[128,8]{0,1:T(8,128)(2,1)S(1)}, bf16[128,8]{0,1:T(8,128)(2,1)}, u32[]{:S(2)}) copy-start(bf16[128,8]{0,1:T(8,128)(2,1)} %param.34) | copy-start | bytes 6148
  66.4 27.6 %copy-start.14 = (f32[128]{0:T(128)S(1)}, f32[128]{0:T(128)}, u32[]{:S(2)}) copy-start(f32[128]{0:T(128)} %param.28) | copy-start | bytes 1540
  67.1 23.3 %collective-permute-start.16 = (bf16[4,18,16,128]{3,2,1,0:T(8,128)(2,1)S(1)}, bf16[4,18,16,128]{3,2,1,0:T(8,128)(2,1)S(1)}, u32[]{:S(2)}, u32[]{:S(2)}) collective-permute-start(bf16[4,18,16,128]{3,2,1,0:T(8,128)(2,1)S(1)} %get-tuple-element.113), channel_id=1, source_target_pairs={{0,8},{2,10},{4,12},{6,14},{8,0},{10,2},{12,4},{14,6},{16,24},{18,... | collective-permute-start | bytes 884744 | tf_op jit(solution)/shard_map/ppermute | solution.py:462
  69.4 9.4 %collective-permute-start.22 = (bf16[4,64,256]{2,1,0:T(8,128)(2,1)S(1)}, bf16[4,64,256]{2,1,0:T(8,128)(2,1)S(1)}, u32[]{:S(2)}, u32[]{:S(2)}) collective-permute-start(bf16[4,64,256]{2,1,0:T(8,128)(2,1)S(1)} %get-tuple-element.125), channel_id=1, source_target_pairs={{0,4},{2,6},{4,0},{6,2},{8,12},{10,14},{12,8},{14,10},{16,20},{18,... | collective-permute-start | bytes 393224 | tf_op jit(solution)/shard_map/ppermute | solution.py:462
  79.4 44.1 %copy-start.17 = (f32[768]{0:T(1024)S(1)}, f32[768]{0:T(1024)}, u32[]{:S(2)}) copy-start(f32[768]{0:T(1024)} %refs_5_.3) | copy-start | bytes 9220
  79.4 4.8 %collective-permute-start.23 = (bf16[2,64,256]{2,1,0:T(8,128)(2,1)S(1)}, bf16[2,64,256]{2,1,0:T(8,128)(2,1)S(1)}, u32[]{:S(2)}, u32[]{:S(2)}) collective-permute-start(bf16[2,64,256]{2,1,0:T(8,128)(2,1)S(1)} %get-tuple-element.127), channel_id=1, source_target_pairs={{0,8},{2,10},{4,12},{6,14},{8,0},{10,2},{12,4},{14,6},{16,24},{18,... | collective-permute-start | bytes 196616 | tf_op jit(solution)/shard_map/ppermute | solution.py:462
  81.7 22.7 %collective-permute-start.11 = (bf16[2,24,16,128]{3,2,1,0:T(8,128)(2,1)S(1)}, bf16[2,24,16,128]{3,2,1,0:T(8,128)(2,1)S(1)}, u32[]{:S(2)}, u32[]{:S(2)}) collective-permute-start(bf16[2,24,16,128]{3,2,1,0:T(8,128)(2,1)S(1)} %get-tuple-element.103), channel_id=1, source_target_pairs={{0,8},{2,10},{4,12},{6,14},{8,0},{10,2},{12,4},{14,6},{16,24},{18,... | collective-permute-start | bytes 589832 | tf_op jit(solution)/shard_map/ppermute | solution.py:462
  84.7 4.9 %collective-permute-start.24 = (bf16[1,64,256]{2,1,0:T(8,128)(2,1)S(1)}, bf16[1,64,256]{2,1,0:T(8,128)(2,1)S(1)}, u32[]{:S(2)}, u32[]{:S(2)}) collective-permute-start(bf16[1,64,256]{2,1,0:T(8,128)(2,1)S(1)} %get-tuple-element.129), channel_id=1, source_target_pairs={{0,16},{2,18},{4,20},{6,22},{8,24},{10,26},{12,28},{14,30},{16,0},... | collective-permute-start | bytes 98312 | tf_op jit(solution)/shard_map/ppermute | solution.py:462
  90.1 3.8 %collective-permute-start.25 = (bf16[64,128]{1,0:T(8,128)(2,1)S(1)}, bf16[64,128]{1,0:T(8,128)(2,1)S(1)}, u32[]{:S(2)}, u32[]{:S(2)}) collective-permute-start(bf16[64,128]{1,0:T(8,128)(2,1)S(1)} %get-tuple-element.131), channel_id=1, source_target_pairs={{0,1},{1,0},{2,3},{3,2},{4,5},{5,4},{6,7},{7,6},{8,9},{9,8},{10,11... | collective-permute-start | bytes 49160 | tf_op jit(solution)/shard_map/ppermute | solution.py:467
  91.0 16.7 %collective-permute-start.17 = (bf16[2,18,16,128]{3,2,1,0:T(8,128)(2,1)S(1)}, bf16[2,18,16,128]{3,2,1,0:T(8,128)(2,1)S(1)}, u32[]{:S(2)}, u32[]{:S(2)}) collective-permute-start(bf16[2,18,16,128]{3,2,1,0:T(8,128)(2,1)S(1)} %get-tuple-element.115), channel_id=1, source_target_pairs={{0,16},{2,18},{4,20},{6,22},{8,24},{10,26},{12,28},{14,30},{16,0},... | collective-permute-start | bytes 442376 | tf_op jit(solution)/shard_map/ppermute | solution.py:462
  97.4 27.3 %all-to-all-start = ((f32[32,8,128]{2,1,0:T(8,128)}), f32[32,8,128]{2,1,0:T(8,128)S(1)}, u32[]{:S(2)}, u32[]{:S(2)}) async-start(f32[32,8,128]{2,1,0:T(8,128)} %get-tuple-element.137), calls=%async_computation | async-start | bytes 262144 | tf_op jit(solution)/shard_map/all_to_all | solution.py:471
  104.0 19.5 %collective-permute-start.8 = (bf16[768,128]{1,0:T(8,128)(2,1)S(1)}, bf16[768,128]{1,0:T(8,128)(2,1)S(1)}, u32[]{:S(2)}, u32[]{:S(2)}) collective-permute-start(bf16[768,128]{1,0:T(8,128)(2,1)S(1)} %get-tuple-element.97), channel_id=1, source_target_pairs={{0,1},{1,0},{2,3},{3,2},{4,5},{5,4},{6,7},{7,6},{8,9},{9,8},{10,11... | collective-permute-start | bytes 589832 | tf_op jit(solution)/shard_map/ppermute | solution.py:467
  105.0 9.6 %collective-permute-start.12 = (bf16[1,24,16,128]{3,2,1,0:T(8,128)(2,1)S(1)}, bf16[1,24,16,128]{3,2,1,0:T(8,128)(2,1)S(1)}, u32[]{:S(2)}, u32[]{:S(2)}) collective-permute-start(bf16[1,24,16,128]{3,2,1,0:T(8,128)(2,1)S(1)} %get-tuple-element.105), channel_id=1, source_target_pairs={{0,16},{2,18},{4,20},{6,22},{8,24},{10,26},{12,28},{14,30},{16,0},... | collective-permute-start | bytes 294920 | tf_op jit(solution)/shard_map/ppermute | solution.py:462
  108.3 8.7 %collective-permute-start.18 = (bf16[1,18,16,128]{3,2,1,0:T(8,128)(2,1)S(1)}, bf16[1,18,16,128]{3,2,1,0:T(8,128)(2,1)S(1)}, u32[]{:S(2)}, u32[]{:S(2)}) collective-permute-start(bf16[1,18,16,128]{3,2,1,0:T(8,128)(2,1)S(1)} %get-tuple-element.117), channel_id=1, source_target_pairs={{0,4},{2,6},{4,0},{6,2},{8,12},{10,14},{12,8},{14,10},{16,20},{18,... | collective-permute-start | bytes 221192 | tf_op jit(solution)/shard_map/ppermute | solution.py:462
  115.1 12.1 %collective-permute-start.13 = (bf16[2,48,384]{2,1,0:T(8,128)(2,1)S(1)}, bf16[2,48,384]{2,1,0:T(8,128)(2,1)S(1)}, u32[]{:S(2)}, u32[]{:S(2)}) collective-permute-start(bf16[2,48,384]{2,1,0:T(8,128)(2,1)S(1)} %get-tuple-element.106), channel_id=1, source_target_pairs={{0,0},{1,16},{2,2},{3,18},{4,4},{5,20},{6,6},{7,22},{8,8},{9,24},{... | collective-permute-start | bytes 221192 | tf_op jit(solution)/shard_map/ppermute | solution.py:707
  117.7 7.6 %collective-permute-start.19 = (bf16[48,384]{1,0:T(8,128)(2,1)S(1)}, bf16[48,384]{1,0:T(8,128)(2,1)S(1)}, u32[]{:S(2)}, u32[]{:S(2)}) collective-permute-start(bf16[48,384]{1,0:T(8,128)(2,1)S(1)} %get-tuple-element.118), channel_id=1, source_target_pairs={{0,0},{1,16},{2,2},{3,18},{4,4},{5,20},{6,6},{7,22},{8,8},{9,24},{... | collective-permute-start | bytes 110600 | tf_op jit(solution)/shard_map/ppermute | solution.py:698
  123.4 3.8 %collective-permute-start.20 = (bf16[48,128]{1,0:T(8,128)(2,1)S(1)}, bf16[48,128]{1,0:T(8,128)(2,1)S(1)}, u32[]{:S(2)}, u32[]{:S(2)}) collective-permute-start(bf16[48,128]{1,0:T(8,128)(2,1)S(1)} %get-tuple-element.120), channel_id=1, source_target_pairs={{0,1},{1,0},{2,3},{3,2},{4,5},{5,4},{6,7},{7,6},{8,9},{9,8},{10,11... | collective-permute-start | bytes 36872 | tf_op jit(solution)/shard_map/ppermute | solution.py:467

commit v6 on v5

--- a/solution.py
+++ b/solution.py
@@ -38,7 +38,7 @@
     return lax.dot_general(left, right, (dims, ((), ())), preferred_element_type=f32)
 
 
-def call(body, name, inputs, outs, scratch=(), flops=0, limit=16):
+def call(body, name, inputs, outs, scratch=(), flops=0, limit=16, deps=()):
     arrays, specs, moved, fetched = [], [], 0, []
     for item in inputs:
         array, space = item if isinstance(item, tuple) else (item, VMEM)
@@ -53,12 +53,16 @@
         for extent in shape:
             size *= extent
         moved += size
+    read = len(arrays)
+    for array in deps:
+        arrays.append(array)
+        specs.append(pl.BlockSpec(memory_space=ANY))
     extra = [VMEM(arrays[k].shape, arrays[k].dtype) for k in fetched]
     if fetched:
         extra.append(pltpu.SemaphoreType.DMA((len(fetched),)))
 
     def whole(*refs):
-        refs = list(refs)
+        refs = list(refs[:read]) + list(refs[read + len(deps) :])
         if fetched:
             held, sem = refs[-1 - len(fetched) : -1], refs[-1]
             refs = refs[: -1 - len(fetched)]
@@ -170,21 +174,20 @@
         outs[k][...] = jnp.transpose(mm(x, slices[k])).astype(bf16)
 
 
-def attention_kernel(copies, toks, cols, head_width, ids, query, key, value, own, other, *rest):
-    facts, chain, weights_out, att_out = rest[:4]
-    pieces, bias = rest[4 : 4 + toks], rest[4 + toks]
-    t = ids[0]
-    core, pair_index = low_bits(ids[1], 2), ids[1] // 2
-    half = copies // 2
-    for p in range(half):
-        k = 0
-        for b in range(half.bit_length() - 1):
-            k += (p >> b & 1) * (half >> 1 >> b)
-        k = jnp.bitwise_xor(pair_index, k)
-        for r in range(toks):
-            a = jnp.bitwise_xor(t, r)
-            bias[core, k, a] = own[p * toks + r]
-            bias[1 - core, k, a] = other[p * toks + r]
+def join_kernel(*refs):
+    for n, ref in enumerate(refs[:-1]):
+        refs[-1][n] = ref[...]
+
+
+def attention_kernel(copies, toks, near, cols, head_width, ids, query, key, value, *rest):
+    biases, (facts, chain, weights_out, att_out) = rest[:near], rest[near : near + 4]
+    pieces, bias = rest[near + 4 : near + 4 + toks], rest[near + 4 + toks]
+    t, low, high = ids[0], low_bits(ids[1], near), ids[1] // near
+    for m in range(near):
+        for rz in range(copies // near):
+            c = jnp.bitwise_xor(high, rz) * near + jnp.bitwise_xor(low, m)
+            for r in range(toks):
+                bias[c, jnp.bitwise_xor(t, r)] = biases[m][rz * toks + r]
     own_heads = weights_out.shape[0]
     tokens = query.shape[1]
     rows = tokens // toks
@@ -199,7 +202,7 @@
         extra = jnp.concatenate(
             [
                 jnp.concatenate(
-                    [bias[c % 2, c // 2, a, line, :] for c in range(copies)], axis=0
+                    [bias[c, a, line, :] for c in range(copies)], axis=0
                 )
                 for a in range(toks)
             ],
@@ -261,13 +264,16 @@
 
 
 def backward_kernel(copies, toks, cols, head_width, ids, query, key, value, weights, *rest):
-    parts = rest[:toks]
-    d_query, d_key, d_value, bias_kept, bias_sent, blocks, d_logits = rest[toks:]
+    parts, d_res_b = rest[:toks], rest[toks]
+    d_query, d_key, d_value, bias_kept, bias_sent, d_res_out = rest[toks + 1 : toks + 7]
+    blocks, d_logits = rest[toks + 7 :]
+    d_res_out[...] = d_res_b[...]
     t = ids[0]
     core = low_bits(ids[1], 2)
     for r in range(toks):
         blocks[jnp.bitwise_xor(t, r)] = parts[r][...]
     d_att = jnp.concatenate([blocks[a] for a in range(toks)], axis=1)
+    count = tile_count(cols, query.shape[1])
     scale = head_width ** (-0.5)
     for h in range(weights.shape[0]):
         span = slice(h * head_width, (h + 1) * head_width)
@@ -281,7 +287,7 @@
         for q in range(copies // 2):
             for side, out in ((core, bias_kept), (1 - core, bias_sent)):
                 start = pl.multiple_of((2 * q + side) * cols, cols)
-                out[q, h * cols : (h + 1) * cols, :] = d_logits[pl.ds(start, cols), :]
+                put(out, q, h * count, d_logits[pl.ds(start, cols), :])
         d_query[span, :] = (mm(key[span, :], d_logits_b) * scale).astype(bf16)
         d_key[span, :] = (mm(query[span, :], d_logits_b, NT) * scale).astype(bf16)
         d_value[span, :] = mm(d_att_h, weights_b, NT).astype(bf16)
@@ -365,55 +371,62 @@
             put(out, q, count, narrow[pl.ds(first, cut), :].astype(bf16))
 
 
-def halve_kernel(mask, inner, ids, kept, got, kept_out, sent_out):
-    bit = low_bits(ids[1] // mask, 2)
-    for q in range(kept_out.shape[0]):
-        for side, out in ((bit, kept_out), (1 - bit, sent_out)):
-            k = q // inner * 2 * inner + side * inner + q % inner
-            out[q] = (kept[k].astype(f32) + got[k].astype(f32)).astype(bf16)
-
-
-def last_bias_kernel(toks, ids, kept, got, *rest):
+def step_kernel(segments, ids, *refs):
+    count = 1 + max(segment[0] for segment in segments)
+    ins, outs = refs[: 2 * count], refs[2 * count :]
+    for source, base, parts, tiles, mask, inner, target, start in segments:
+        kept, got = ins[2 * source : 2 * source + 2]
+        bit = low_bits(ids[1] // mask, 2)
+        for q in range(parts // 2):
+            for side, out in ((bit, outs[2 * target]), (1 - bit, outs[2 * target + 1])):
+                k = q // inner * 2 * inner + side * inner + q % inner
+                span = pl.ds(base + k * tiles, tiles)
+                out[start + q * tiles : start + (q + 1) * tiles] = (
+                    kept[span].astype(f32) + got[span].astype(f32)
+                ).astype(bf16)
+
+
+def last_bias_kernel(toks, base, count, cols, ids, kept, got, *rest):
     pieces, blocks = rest[:toks], rest[toks]
-    total = kept[0].astype(f32) + got[0].astype(f32)
-    rows = blocks.shape[2]
+    span = slice(base, base + count)
+    tiles = kept[span].astype(f32) + got[span].astype(f32)
+    part_rows, rows = pieces[0].shape
+    heads = part_rows // cols
+    total = jnp.concatenate(
+        [take(tiles, h * (count // heads), cols, rows * toks) for h in range(heads)], axis=0
+    )
     for a in range(toks):
         blocks[a] = total[:, a * rows : (a + 1) * rows].astype(bf16)
     for r in range(toks):
         pieces[r][...] = blocks[jnp.bitwise_xor(ids[0], r)]
 
 
-def last_first_kernel(toks, ids, kept, got, moved, *rest):
+def last_kernel(toks, ids, kept, got, kept_b, got_b, moved, final, *rest):
     pieces, blocks = rest[:toks], rest[toks]
-    total = kept[0].astype(f32) + got[0].astype(f32)
+    first = kept[...].astype(f32) + got[...].astype(f32)
+    second = kept_b[...].astype(f32) + got_b[...].astype(f32)
     _, cut, own_width = moved.shape
     count = tile_count(cut, own_width)
     for k in range(2):
-        moved[k] = take(total, k * count, cut, own_width).astype(bf16)
+        moved[k] = take(first, k * count, cut, own_width).astype(bf16)
+    moved[2] = take(second, 0, cut, own_width).astype(bf16)
+    final[...] = take(second, count, cut, own_width)
     rows = blocks.shape[2]
-    single = take(total, 2 * count, cut, rows * toks)
+    single = take(first, 2 * count, cut, rows * toks)
     for a in range(toks):
         blocks[a] = single[:, a * rows : (a + 1) * rows]
     for r in range(toks):
         pieces[r][...] = blocks[jnp.bitwise_xor(ids[0], r)].astype(bf16)
 
 
-def last_second_kernel(kept, got, moved, final):
-    total = kept[0].astype(f32) + got[0].astype(f32)
-    cut, own_width = moved.shape
-    moved[...] = take(total, 0, cut, own_width).astype(bf16)
-    final[...] = take(total, tile_count(cut, own_width), cut, own_width)
-
-
-def finish_kernel(moved_first, moved_second, *rest):
-    parts, (first, second, third, single) = rest[:-4], rest[-4:]
-    first[...] = moved_first[0].astype(f32)
-    second[...] = moved_first[1].astype(f32)
-    third[...] = moved_second[...].astype(f32)
+def finish_kernel(moved, *rest):
+    parts, outs = rest[:-4], rest[-4:]
+    for k in range(3):
+        outs[k][...] = moved[k].astype(f32)
     total = parts[0][...].astype(f32)
     for part in parts[1:]:
         total = total + part[...].astype(f32)
-    single[...] = total
+    outs[3][...] = total
 
 
 def exit_kernel(toks, noisy, gain, d_res, d_own, *rest):
@@ -469,10 +482,6 @@
 
 def exchange(value):
     return lax.all_to_all(value, ("copy", "tok"), 0, 0)
-
-
-def after(value, *earlier):
-    return lax.optimization_barrier((value,) + earlier)[0]
 
 
 def per_device(
@@ -529,16 +538,9 @@
         limit=60,
     )
     x_own, bias_parts = entered[0], entered[1:]
-    bias_own = jnp.stack(
-        [bias_parts[0]] + [swap_tok(bias_parts[r], r) for r in range(1, toks)]
-    )
     x_parts = [x_own] + [swap_tok(x_own, r) for r in range(1, toks)]
-    mask = copies // 2
-    while mask > 1:
-        bias_own = jnp.concatenate([bias_own, swap_copy(bias_own, mask)])
-        mask //= 2
-    bias_other = swap_copy(bias_own, 1)
-
+    near = 4
+    far = copies // near
     weights3 = [w_query, w_key, w_value]
     if own_width % 128:
         weights3 = [
@@ -552,6 +554,20 @@
         [((3, width, own_width), bf16), ((tokens, 128), f32), ((1, tokens), f32)],
         [pltpu.SemaphoreType.DMA((3,))],
     )
+    def join(name, parts, deps=()):
+        shape = (len(parts),) + parts[0].shape
+        return call(join_kernel, name, parts, [(shape, bf16)], deps=deps)[0]
+
+    mine = join(
+        "join_tok", [bias_parts[0]] + [swap_tok(bias_parts[r], r) for r in range(1, toks)]
+    )
+    lines = join(
+        "join_far",
+        [mine] + [swap_copy(mine, m * near) for m in range(1, far)],
+        deps=x_parts[1:] + [chain_row],
+    )
+    lines = lines.reshape((far * toks,) + lines.shape[2:])
+    biases = [lines] + [swap_copy(lines, m) for m in range(1, near)]
     x, query, key, value = call(
         functools.partial(project_kernel, toks),
         "project",
@@ -560,12 +576,12 @@
         flops=6 * tokens * width * own_width,
     )
     done = call(
-        functools.partial(attention_kernel, copies, toks, cols, head_width),
+        functools.partial(attention_kernel, copies, toks, near, cols, head_width),
         "attention",
-        [where_am_i, query, key, value, bias_own, bias_other, facts, chain_row],
+        [where_am_i, query, key, value] + biases + [facts, chain_row],
         [((own_heads, tokens, tokens), bf16), ((tokens, own_width), bf16)]
         + [((rows, own_width), bf16)] * toks,
-        [VMEM((2, copies // 2, toks, own_heads * cols, rows), bf16)],
+        [VMEM((copies, toks, own_heads * cols, rows), bf16)],
         flops=4 * tokens * tokens * own_width,
         limit=32,
     )
@@ -591,20 +607,21 @@
     )
     d_res, d_res_b, d_att = results[0], results[1], results[2:]
     d_att_parts = [d_att[0]] + [swap_tok(d_att[r], r) for r in range(1, toks)]
-    d_res_b = after(d_res_b, *d_att_parts[1:])
-    d_res_parts = [d_res_b] + [swap_tok(d_res_b, r) for r in range(1, toks)]
-
-    bias_shape = (copies // 2, own_heads * cols, tokens)
-    d_query, d_key, d_value, bias_kept, bias_sent = call(
+    bias_tiles = own_heads * tile_count(cols, tokens)
+    bias_shape = (copies // 2, bias_tiles, 16, 128)
+    d_query, d_key, d_value, bias_kept, bias_sent, d_res_b = call(
         functools.partial(backward_kernel, copies, toks, cols, head_width),
         "backward",
-        [where_am_i, query, key, value, weights] + d_att_parts,
-        [((own_width, tokens), bf16)] * 3 + [(bias_shape, bf16)] * 2,
+        [where_am_i, query, key, value, weights] + d_att_parts + [d_res_b],
+        [((own_width, tokens), bf16)] * 3 + [(bias_shape, bf16)] * 2 + [((rows, width), bf16)],
         [VMEM((toks, own_width, rows), bf16), VMEM((tokens, tokens), bf16)],
         flops=8 * tokens * tokens * own_width,
         limit=32,
     )
-    bias_got = swap_copy(bias_sent, 1)
+    d_res_parts = [d_res_b] + [swap_tok(d_res_b, r) for r in range(1, toks)]
+    bias_kept, bias_got = [
+        array.reshape((-1, 16, 128)) for array in (bias_kept, swap_copy(bias_sent, 1))
+    ]
 
     wide_tiles = tile_count(cut, own_width)
     single_tiles = tile_count(cut, tokens)
@@ -625,6 +642,38 @@
     kept, sent, d_own = found[:3]
     got = swap_copy(sent, 1)
     d_others = [swap_tok(found[2 + r], r) for r in range(1, toks)]
+
+    def step(name, pairs, segments, deps=()):
+        filled, full, masks_of = {}, [], {}
+        for source, base, parts, tiles, mask, left, target in segments:
+            inner = 1 << sum(1 for other in left if other < mask)
+            start = filled.get(target, 0)
+            full.append((source, base, parts, tiles, mask, inner, target, start))
+            filled[target] = start + parts // 2 * tiles
+            masks_of[target] = mask
+        outs = []
+        for target in range(len(filled)):
+            outs += [((filled[target], 16, 128), bf16)] * 2
+        results = call(
+            functools.partial(step_kernel, full),
+            name,
+            [where_am_i] + [array for one in pairs for array in one],
+            outs,
+            deps=deps,
+        )
+        return [
+            (results[2 * n], swap_copy(results[2 * n + 1], masks_of[n]))
+            for n in range(len(filled))
+        ]
+
+    masks = [1 << b for b in range(1, copies.bit_length() - 1)]
+    masks_b = masks[1:] + masks[:1]
+    bias_left, bias_parts = list(masks), copies // 2
+    (bias_pair,) = step(
+        "bias_first",
+        [(bias_kept, bias_got)],
+        [(0, 0, bias_parts, bias_tiles, masks[0], bias_left, 0)],
+    )
     kept_b, sent_b = call(
         functools.partial(second_kernel, copies, toks),
         "second",
@@ -636,28 +685,69 @@
             VMEM((width, own_width), f32),
         ],
         flops=4 * tokens * width * own_width,
+        deps=[bias_pair[0]],
     )
     got_b = swap_copy(sent_b, 1)
 
-    def halve(name, mask, left, kept, got):
-        inner = 1 << sum(1 for other in left if other < mask)
-        left.remove(mask)
-        shape = (kept.shape[0] // 2,) + kept.shape[1:]
-        kept, sent = call(
-            functools.partial(halve_kernel, mask, inner),
-            "%s_%d" % (name, mask),
-            [where_am_i, kept, got],
-            [(shape, bf16)] * 2,
+    (grad_noisy,) = call(
+        functools.partial(exit_kernel, toks),
+        "exit",
+        [noisy3, norm_gain2, d_res, d_own] + d_others,
+        [((rows, width), bf16)],
+    )
+    for mask in masks[:1:-1]:
+        bias_left = [other for other in bias_left if other != masks[0]]
+        bias_parts //= 2
+        (bias_pair,) = step(
+            "bias_%d" % mask,
+            [bias_pair],
+            [(0, 0, bias_parts, bias_tiles, mask, bias_left, 0)],
+            deps=[sent_b],
         )
-        return kept, swap_copy(sent, mask)
-
-    masks = [1 << b for b in range(1, copies.bit_length() - 1)]
-    bias_left, first_left, second_left = list(masks), list(masks), list(masks)
-    first, second, bias_chain = (kept, got), (kept_b, got_b), (bias_kept, bias_got)
-    for mask, mask_b in zip(masks, masks[1:] + masks[:1]):
-        bias_chain = halve("bias", mask, bias_left, *bias_chain)
-        first = halve("first", mask, first_left, *first)
-        second = halve("second", mask_b, second_left, *second)
+        bias_left = [other for other in bias_left if other != mask]
+    first_tiles, second_tiles = 2 * wide_tiles + single_tiles, 2 * wide_tiles
+    pairs = [
+        tuple(array.reshape((-1, 16, 128)) for array in one)
+        for one in ((kept, got), (kept_b, got_b))
+    ]
+    pairs.append(bias_pair)
+    parts = copies // 2
+    for n, (mask, mask_b) in enumerate(zip(masks, masks_b)):
+        segments = [
+            (0, 0, parts, first_tiles, mask, masks[n:], 0),
+            (1, 0, parts, second_tiles, mask_b, masks_b[n:], 1),
+        ]
+        deps = []
+        if n == 0:
+            segments.append((2, 0, 2, bias_tiles, mask_b, [mask_b], 1))
+        if n == 1:
+            bias_ready = pairs[1]
+            bias_base = parts * second_tiles
+            deps = [grad_noisy]
+        if n == 2:
+            deps = [weight_grad]
+        pairs = step("step_%d" % n, pairs, segments, deps=deps)
+        parts //= 2
+        if n == 1:
+            bias_pieces = call(
+                functools.partial(last_bias_kernel, toks, bias_base, bias_tiles, cols),
+                "last_bias",
+                [where_am_i, *bias_ready],
+                [((own_heads * cols, rows), bf16)] * toks,
+                [VMEM((toks, own_heads * cols, rows), bf16)],
+                deps=[pairs[0][0]],
+            )
+            bias_pieces = [bias_pieces[0]] + [
+                swap_tok(bias_pieces[r], r) for r in range(1, toks)
+            ]
+            grad_pair, weight_grad = call(
+                functools.partial(pair_kernel, toks, cols),
+                "pair",
+                [where_am_i, pair2, pair_gain2, w_pair.T] + bias_pieces,
+                [((rows * cols, channels), bf16), ((devices, heads, channels), f32)],
+                [VMEM((rows * cols, channels), f32)] * 2 + [VMEM((heads * cols, rows), f32)],
+                flops=4 * heads * cols * rows * channels * cols,
+            )
 
     group = copies // toks
     swaps = []
@@ -665,51 +755,22 @@
         for t in range(toks):
             swaps.append((c * toks + t, (t * group + c % group) * toks + c // group))
 
-    bias_parts = call(
-        functools.partial(last_bias_kernel, toks),
-        "last_bias",
-        [where_am_i, *bias_chain],
-        [((own_heads * cols, rows), bf16)] * toks,
-        [VMEM((toks, own_heads * cols, rows), bf16)],
-    )
-    bias_parts = [bias_parts[0]] + [swap_tok(bias_parts[r], r) for r in range(1, toks)]
-    (grad_noisy,) = call(
-        functools.partial(exit_kernel, toks),
-        "exit",
-        [noisy3, norm_gain2, d_res, d_own] + d_others,
-        [((rows, width), bf16)],
-    )
-    grad_pair, weight_grad = call(
-        functools.partial(pair_kernel, toks, cols),
-        "pair",
-        [where_am_i, pair2, pair_gain2, w_pair.T] + bias_parts,
-        [((rows * cols, channels), bf16), ((devices, heads, channels), f32)],
-        [VMEM((rows * cols, channels), f32)] * 2 + [VMEM((heads * cols, rows), f32)],
-        flops=4 * heads * cols * rows * channels * cols,
-    )
     weight_grad = jnp.sum(exchange(weight_grad), axis=0)
-
-    moved_second, grad_out = call(
-        last_second_kernel,
-        "last_second",
-        [*second],
-        [((cut, own_width), bf16), ((cut, own_width), f32)],
-    )
-    moved_second = lax.ppermute(moved_second, ("copy", "tok"), swaps)
-    done = call(
-        functools.partial(last_first_kernel, toks),
-        "last_first",
-        [where_am_i, *first],
-        [((2, cut, own_width), bf16)] + [((cut, rows), bf16)] * toks,
+    last = call(
+        functools.partial(last_kernel, toks),
+        "last",
+        [where_am_i, *pairs[0], *pairs[1]],
+        [((3, cut, own_width), bf16), ((cut, own_width), f32)] + [((cut, rows), bf16)] * toks,
         [VMEM((toks, cut, rows), f32)],
-    )
-    moved_first, singles = done[0], done[1:]
-    moved_first = lax.ppermute(moved_first, ("copy", "tok"), swaps)
+        deps=[weight_grad],
+    )
+    grad_out, singles = last[1], last[2:]
     singles = [singles[0]] + [swap_tok(singles[r], r) for r in range(1, toks)]
+    moved = lax.ppermute(last[0], ("copy", "tok"), swaps)
     grad_query, grad_key, grad_value, grad_single = call(
         finish_kernel,
         "finish",
-        [moved_first, moved_second] + singles,
+        [moved] + singles,
         [((cut, own_width), f32)] * 3 + [((cut, rows), f32)],
     )
     return (

time: 130 us -> 131 us (level)
  waiting for transfers between devices: 49.6 us -> 63.2 us
  starting transfers between devices: 38.5 us -> 27.5 us
  local copies, waits for them, and re-layouts: 3.39 us -> 8.22 us
  other arithmetic: 3.39 us -> 0.62 us
  Pallas kernels: 32 us -> 29.7 us
    ppermute x16 -> x17, starting transfers between devices: 22.3 us -> 15.6 us  [swap_copy(): return lax.ppermute(value, 'copy', [(i, i ^ mask) for i in range(size)])]
    ppermute x16 -> x17, waiting for transfers between devices: 25.3 us -> 30.9 us  [swap_copy(): return lax.ppermute(value, 'copy', [(i, i ^ mask) for i in range(size)])]
    ppermute x8, waiting for transfers between devices: 24.3 us -> 29.4 us  [swap_tok(): return lax.ppermute(value, 'tok', [(i, i ^ mask) for i in range(size)])]
    ppermute x2 -> x1, starting transfers between devices: 7.63 us -> 2.76 us  [per_device(): moved = lax.ppermute(last[0], ('copy', 'tok'), swaps)]
    unnamed x42 -> x46, local copies, waits for them, and re-layouts: 3.36 us -> 8.21 us
    ppermute x2 -> x1, waiting for transfers between devices: 0.01 us -> 2.92 us  [per_device(): moved = lax.ppermute(last[0], ('copy', 'tok'), swaps)]
    ppermute x8, starting transfers between devices: 1.92 us -> 4.37 us  [swap_tok(): return lax.ppermute(value, 'tok', [(i, i ^ mask) for i in range(size)])]
    pallas_call x24 -> x21, Pallas kernels: 32 us -> 29.7 us  [call(): pl.pallas_call(whole, name=name, out_shape=[jax.ShapeDtypeStruct(shape, k...]
  transfers between devices with their start and end apart: 27 -> 27, of which waited for: 14 -> 16; matrix products, arithmetic and copies ran while one was open for 1% -> 0% of each run, Pallas kernels for 13% -> 11%
where the time goes in v6:
time: 131 us; the launch traced here: 130 us
  waiting for transfers between devices  63.2 us (48%)
  Pallas kernels  29.7 us (23%)
  starting transfers between devices  27.5 us (21%)
  local copies, waits for them, and re-layouts  8.22 us (6%)
    ppermute x17, waiting for transfers between devices, swap_copy(): return lax.ppermute(value, 'copy', [(i, i ^ mask) for i in range(size)])  30.9 us
    pallas_call x21, Pallas kernels, call(): pl.pallas_call(whole, name=name, out_shape=[jax.ShapeDtypeStruct(shape, k...  29.7 us
    ppermute x8, waiting for transfers between devices, swap_tok(): return lax.ppermute(value, 'tok', [(i, i ^ mask) for i in range(size)])  29.4 us
    ppermute x17, starting transfers between devices, swap_copy(): return lax.ppermute(value, 'copy', [(i, i ^ mask) for i in range(size)])  15.6 us
    unnamed x46, local copies, waits for them, and re-layouts  8.21 us
    all_to_all x1, starting transfers between devices, exchange(): return lax.all_to_all(value, ('copy', 'tok'), 0, 0)  4.68 us
    ppermute x8, starting transfers between devices, swap_tok(): return lax.ppermute(value, 'tok', [(i, i ^ mask) for i in range(size)])  4.37 us
    ppermute x1, waiting for transfers between devices, per_device(): moved = lax.ppermute(last[0], ('copy', 'tok'), swaps)  2.92 us
  transfers between devices with their start and end apart: 27, of which 16 were waited for; matrix products, arithmetic and copies ran while one was open for 0% of the time, Pallas kernels for 11%

profile of v6, /device:TPU:2, one launch (start us, length us, event | category | flops | bytes accessed | tf_op | source)
XLA Modules:
  0.0 130.1 jit_solution(16264892219012274113)
XLA Ops:
  0.6 0.6 pad_add_fusion.refs_0_
  1.2 4.0 %enter.1 = (bf16[128,768]{1,0:T(8,128)(2,1)}, bf16[64,128]{1,0:T(8,128)(2,1)}, bf16[64,128]{1,0:T(8,128)(2,1)}) custom-call(s32[2]{0:T(128)} %pad_add_fusion.refs_0_, bf16[128,768]{1,0:T(8,128)(2,1)} %bitcast.28, bf16[128,768]{1,0:T(8,128)(2,1)} %refs_2_.1, s32[1,128]{1,0:T(1,128)} %bitcast.48, bf16[32,768]{1,0:T(8,128)(2,1)} %refs_4_.3, f32[768]{0:T(1024)} %refs_5_.3, ...), custom_call_target="tpu_custom_call" | custom-call | flops 67108864 | bytes 1202184 | tf_op jit(solution)/shard_map/enter/pallas_call | solution.py:79
  5.3 2.0 %collective-permute-start.1 = (bf16[64,128]{1,0:T(8,128)(2,1)}, bf16[64,128]{1,0:T(8,128)(2,1)S(1)}, u32[]{:S(2)}, u32[]{:S(2)}) collective-permute-start(bf16[64,128]{1,0:T(8,128)(2,1)} %get-tuple-element.80), channel_id=1, source_target_pairs={{0,1},{1,0},{2,3},{3,2},{4,5},{5,4},{6,7},{7,6},{8,9},{9,8},{10,11... | collective-permute-start | bytes 49160 | tf_op jit(solution)/shard_map/ppermute | solution.py:480
  7.3 5.2 %collective-permute-done.1.refs_1_ = bf16[64,128]{1,0:T(8,128)(2,1)S(1)} collective-permute-done((bf16[64,128]{1,0:T(8,128)(2,1)}, bf16[64,128]{1,0:T(8,128)(2,1)S(1)}, u32[]{:S(2)}, u32[]{:S(2)}) %collective-permute-start.1) | collective-permute-done | bytes 16416 | tf_op jit(solution)/shard_map/ppermute | solution.py:480
  12.5 0.7 copy-done.15
  13.2 3.6 %collective-permute-start.4 = (bf16[2,64,128]{2,1,0:T(8,128)(2,1)S(1)}, bf16[2,64,128]{2,1,0:T(8,128)(2,1)S(1)}, u32[]{:S(2)}, u32[]{:S(2)}) collective-permute-start(bf16[2,64,128]{2,1,0:T(8,128)(2,1)S(1)} %join_tok.1.refs_0_), channel_id=1, source_target_pairs={{0,24},{2,26},{4,28},{6,30},{8,16},{10,18},{12,20},{14,22},{16,8},... | collective-permute-start | bytes 98312 | tf_op jit(solution)/shard_map/ppermute | solution.py:475
  16.8 0.8 collective-permute-start.2
  17.6 1.3 copy-done.4
  18.8 1.3 copy-done.5
  20.1 1.3 copy-done.6
  21.4 0.7 copy-done.12
  22.0 0.7 copy-done.17
  22.7 0.7 copy-done.19
  23.4 0.7 copy-done.20
  24.1 1.0 stage.1
  25.3 1.6 %collective-permute-start.6 = (bf16[8,64,128]{2,1,0:T(8,128)(2,1)S(1)}, bf16[8,64,128]{2,1,0:T(8,128)(2,1)S(1)}, u32[]{:S(2)}, u32[]{:S(2)}) collective-permute-start(bf16[8,64,128]{2,1,0:T(8,128)(2,1)S(1)} %bitcast.35), channel_id=1, source_target_pairs={{0,4},{2,6},{4,0},{6,2},{8,12},{10,14},{12,8},{14,10},{16,20},{18,... | collective-permute-start | bytes 393224 | tf_op jit(solution)/shard_map/ppermute | solution.py:475
  26.8 0.3 collective-permute-start.5
  27.1 1.4 %project.1 = (bf16[256,768]{1,0:T(8,128)(2,1)S(1)}, bf16[384,256]{1,0:T(8,128)(2,1)S(1)}, bf16[384,256]{1,0:T(8,128)(2,1)S(1)}, bf16[384,256]{1,0:T(8,128)(2,1)S(1)}) custom-call(s32[2]{0:T(128)S(1)} %copy-done.13, bf16[3,768,384]{2,1,0:T(8,128)(2,1)S(1)} %get-tuple-element.74.refs_1_, bf16[128,768]{1,0:T(8,128)(2,1)S(1)} %copy-done.11, ...), custom_call_target="tpu_custom_call" | custom-call | flops 452984832 | bytes 3145736 | tf_op jit(solution)/shard_map/project/pallas_call | solution.py:79
  28.5 2.4 %collective-permute-done.7.refs_7_ = bf16[8,64,128]{2,1,0:T(8,128)(2,1)S(1)} collective-permute-done((bf16[8,64,128]{2,1,0:T(8,128)(2,1)S(1)}, bf16[8,64,128]{2,1,0:T(8,128)(2,1)S(1)}, u32[]{:S(2)}, u32[]{:S(2)}) %collective-permute-start.7) | collective-permute-done | bytes 131104 | tf_op jit(solution)/shard_map/ppermute | solution.py:475
  31.0 2.9 %collective-permute-done.6.refs_6_ = bf16[8,64,128]{2,1,0:T(8,128)(2,1)S(1)} collective-permute-done((bf16[8,64,128]{2,1,0:T(8,128)(2,1)S(1)}, bf16[8,64,128]{2,1,0:T(8,128)(2,1)S(1)}, u32[]{:S(2)}, u32[]{:S(2)}) %collective-permute-start.6) | collective-permute-done | bytes 131104 | tf_op jit(solution)/shard_map/ppermute | solution.py:475
  33.9 2.1 %attention.1 = (bf16[4,256,256]{2,1,0:T(8,128)(2,1)S(1)}, bf16[256,384]{1,0:T(8,128)(2,1)S(1)}, bf16[128,384]{1,0:T(8,128)(2,1)S(1)}, bf16[128,384]{1,0:T(8,128)(2,1)S(1)}) custom-call(s32[2]{0:T(128)S(1)} %copy-done.13, bf16[384,256]{1,0:T(8,128)(2,1)S(1)} %get-tuple-element.76.refs_1_, bf16[384,256]{1,0:T(8,128)(2,1)S(1)} %get-tuple-element.77.refs_2_, ...), custom_call_target="tpu_custom_call" | custom-call | flops 100663296 | bytes 2163720 | tf_op jit(solution)/shard_map/attention/pallas_call | solution.py:79
  36.0 0.4 collective-permute-start.8
  36.4 0.9 down.1
  37.3 3.5 %collective-permute-done.8.refs_6_ = bf16[128,384]{1,0:T(8,128)(2,1)S(1)} collective-permute-done((bf16[128,384]{1,0:T(8,128)(2,1)S(1)}, bf16[128,384]{1,0:T(8,128)(2,1)S(1)}, u32[]{:S(2)}, u32[]{:S(2)}) %collective-permute-start.8) | collective-permute-done | bytes 98336 | tf_op jit(solution)/shard_map/ppermute | solution.py:480
  40.8 4.3 %hidden.1 = (f32[128,768]{1,0:T(8,128)S(1)}, bf16[128,768]{1,0:T(8,128)(2,1)S(1)}, bf16[384,128]{1,0:T(8,128)(2,1)S(1)}, bf16[384,128]{1,0:T(8,128)(2,1)S(1)}) custom-call(s32[2]{0:T(128)S(1)} %copy-done.13, bf16[128,768]{1,0:T(8,128)(2,1)S(1)} %get-tuple-element.70.refs_1_.refs_0_, bf16[128,768]{1,0:T(8,128)(2,1)S(1)} %get-tuple-element.71.refs_2_, ...), custom_call_target="tpu_custom_call" | custom-call | flops 1509949440 | bytes 8064008 | tf_op jit(solution)/shard_map/hidden/pallas_call | solution.py:79
  45.1 0.3 collective-permute-start.9
  45.5 4.3 %collective-permute-done.9.refs_6_ = bf16[384,128]{1,0:T(8,128)(2,1)S(1)} collective-permute-done((bf16[384,128]{1,0:T(8,128)(2,1)S(1)}, bf16[384,128]{1,0:T(8,128)(2,1)S(1)}, u32[]{:S(2)}, u32[]{:S(2)}) %collective-permute-start.9) | collective-permute-done | bytes 98336 | tf_op jit(solution)/shard_map/ppermute | solution.py:480
  49.8 2.0 %backward.1 = (bf16[384,256]{1,0:T(8,128)(2,1)S(1)}, bf16[384,256]{1,0:T(8,128)(2,1)S(1)}, bf16[384,256]{1,0:T(8,128)(2,1)S(1)}, bf16[8,8,16,128]{3,2,1,0:T(8,12...) custom-call(s32[2]{0:T(128)S(1)} %copy-done.13, ...), custom_call_target="tpu_custom_call" | custom-call | flops 201326592 | bytes 2818056 | tf_op jit(solution)/shard_map/backward/pallas_call | solution.py:79
  51.9 0.3 collective-permute-start.12
  52.3 2.1 %first.1 = (bf16[8,24,16,128]{3,2,1,0:T(8,128)(2,1)S(1)}, bf16[8,24,16,128]{3,2,1,0:T(8,128)(2,1)S(1)}, f32[768,128]{1,0:T(8,128)S(1)}, bf16[768,128]{1,0:T(8,128)(2,1)S(1)}) custom-call(s32[2]{0:T(128)S(1)} %copy-done.13, bf16[3,768,384]{2,1,0:T(8,128)(2,1)S(1)} %get-tuple-element.74.refs_1_, bf16[256,768]{1,0:T(8,128)(2,1)S(1)} %get-tuple-element.86.refs_2_.refs_1_, ...), custom_call_target="tpu_custom_call" | custom-call | flops 754974720 | bytes 4915208 | tf_op jit(solution)/shard_map/first/pallas_call | solution.py:79
  54.4 0.2 collective-permute-start.11
  54.6 0.6 bias_first.1
  55.3 4.0 %collective-permute-done.12.refs_5_ = bf16[128,768]{1,0:T(8,128)(2,1)S(1)} collective-permute-done((bf16[128,768]{1,0:T(8,128)(2,1)S(1)}, bf16[128,768]{1,0:T(8,128)(2,1)S(1)}, u32[]{:S(2)}, u32[]{:S(2)}) %collective-permute-start.12) | collective-permute-done | bytes 196640 | tf_op jit(solution)/shard_map/ppermute | solution.py:480
  59.3 1.4 %second.1 = (bf16[8,18,16,128]{3,2,1,0:T(8,128)(2,1)S(1)}, bf16[8,18,16,128]{3,2,1,0:T(8,128)(2,1)S(1)}) custom-call(s32[2]{0:T(128)S(1)} %copy-done.13, bf16[256,768]{1,0:T(8,128)(2,1)S(1)} %get-tuple-element.86.refs_2_.refs_1_, bf16[256,384]{1,0:T(8,128)(2,1)S(1)} %get-tuple-element.98.refs_2_, bf16[384,256]{1,0:T(8,128)(2,1)S(1)} %get-tuple-element.93.refs_5_.refs_3_, ...), custom_call_target="tpu_custom_call" | custom-call | flops 301989888 | bytes 2359304 | tf_op jit(solution)/shard_map/second/pallas_call | solution.py:79
  60.7 0.4 collective-permute-start.15
  61.1 5.5 %collective-permute-done.15.refs_2_ = bf16[32,16,128]{2,1,0:T(8,128)(2,1)S(1)} collective-permute-done((bf16[32,16,128]{2,1,0:T(8,128)(2,1)S(1)}, bf16[32,16,128]{2,1,0:T(8,128)(2,1)S(1)}, u32[]{:S(2)}, u32[]{:S(2)}) %collective-permute-start.15) | collective-permute-done | bytes 131104 | tf_op jit(solution)/shard_map/ppermute | solution.py:475
  66.6 0.6 bias_8.1
  67.2 2.2 %collective-permute-start.16 = (bf16[16,16,128]{2,1,0:T(8,128)(2,1)S(1)}, bf16[16,16,128]{2,1,0:T(8,128)(2,1)S(1)}, u32[]{:S(2)}, u32[]{:S(2)}) collective-permute-start(bf16[16,16,128]{2,1,0:T(8,128)(2,1)S(1)} %get-tuple-element.107), channel_id=1, source_target_pairs={{0,16},{2,18},{4,20},{6,22},{8,24},{10,26},{12,28},{14,30},{16,0},... | collective-permute-start | bytes 196616 | tf_op jit(solution)/shard_map/ppermute | solution.py:475
  69.4 4.1 %collective-permute-done.16.refs_6_ = bf16[16,16,128]{2,1,0:T(8,128)(2,1)S(1)} collective-permute-done((bf16[16,16,128]{2,1,0:T(8,128)(2,1)S(1)}, bf16[16,16,128]{2,1,0:T(8,128)(2,1)S(1)}, u32[]{:S(2)}, u32[]{:S(2)}) %collective-permute-start.16) | collective-permute-done | bytes 65568 | tf_op jit(solution)/shard_map/ppermute | solution.py:475
  73.5 0.9 step_0.1
  74.4 0.4 collective-permute-start.17
  75.0 0.5 collective-permute-start.10
  75.5 5.1 %collective-permute-done.10.refs_4_ = bf16[768,128]{1,0:T(8,128)(2,1)S(1)} collective-permute-done((bf16[768,128]{1,0:T(8,128)(2,1)S(1)}, bf16[768,128]{1,0:T(8,128)(2,1)S(1)}, u32[]{:S(2)}, u32[]{:S(2)}) %collective-permute-start.10) | collective-permute-done | bytes 196640 | tf_op jit(solution)/shard_map/ppermute | solution.py:480
  80.7 1.2 exit.1.refs_5_
  81.9 1.0 collective-permute-done.17.refs_2_
  82.9 0.9 copy-done.8
  83.8 0.7 step_1.1
  84.6 1.6 %collective-permute-start.19 = (bf16[48,16,128]{2,1,0:T(8,128)(2,1)S(1)}, bf16[48,16,128]{2,1,0:T(8,128)(2,1)S(1)}, u32[]{:S(2)}, u32[]{:S(2)}) collective-permute-start(bf16[48,16,128]{2,1,0:T(8,128)(2,1)S(1)} %get-tuple-element.113), channel_id=1, source_target_pairs={{0,8},{2,10},{4,12},{6,14},{8,0},{10,2},{12,4},{14,6},{16,24},{18,... | collective-permute-start | bytes 589832 | tf_op jit(solution)/shard_map/ppermute | solution.py:475
  86.2 0.6 last_bias.1
  86.7 0.6 collective-permute-start.21
  87.4 3.2 %collective-permute-done.21.refs_5_ = bf16[64,128]{1,0:T(8,128)(2,1)S(1)} collective-permute-done((bf16[64,128]{1,0:T(8,128)(2,1)S(1)}, bf16[64,128]{1,0:T(8,128)(2,1)S(1)}, u32[]{:S(2)}, u32[]{:S(2)}) %collective-permute-start.21) | collective-permute-done | bytes 16416 | tf_op jit(solution)/shard_map/ppermute | solution.py:480
  90.6 3.4 %pair.1 = (bf16[2048,128]{1,0:T(8,128)(2,1)}, f32[32,8,128]{2,1,0:T(8,128)}) custom-call(s32[2]{0:T(128)S(1)} %copy-done.13, bf16[2048,128]{1,0:T(8,128)(2,1)S(1)} %bitcast.26, f32[1,128]{1,0:T(1,128)S(1)} %bitcast.45, bf16[8,128]{1,0:T(8,128)(2,1)S(1)} %bitcast.43, bf16[64,128]{1,0:T(8,128)(2,1)S(1)} %get-tuple-element.116.refs_4_, ...), custom_call_target="tpu_custom_call" | custom-call | flops 134217728 | bytes 1214984 | tf_op jit(solution)/shard_map/pair/pallas_call | solution.py:79
  94.0 4.7 %all-to-all-start = ((f32[32,8,128]{2,1,0:T(8,128)}), f32[32,8,128]{2,1,0:T(8,128)S(1)}, u32[]{:S(2)}, u32[]{:S(2)}) async-start(f32[32,8,128]{2,1,0:T(8,128)} %get-tuple-element.118.refs_5_), calls=%async_computation | async-start | bytes 262144 | tf_op jit(solution)/shard_map/all_to_all | solution.py:484
  98.7 2.4 %collective-permute-start.20 = (bf16[36,16,128]{2,1,0:T(8,128)(2,1)S(1)}, bf16[36,16,128]{2,1,0:T(8,128)(2,1)S(1)}, u32[]{:S(2)}, u32[]{:S(2)}) collective-permute-start(bf16[36,16,128]{2,1,0:T(8,128)(2,1)S(1)} %get-tuple-element.115), channel_id=1, source_target_pairs={{0,16},{2,18},{4,20},{6,22},{8,24},{10,26},{12,28},{14,30},{16,0},... | collective-permute-start | bytes 442376 | tf_op jit(solution)/shard_map/ppermute | solution.py:475
  101.1 10.2 %collective-permute-done.20.refs_4_ = bf16[36,16,128]{2,1,0:T(8,128)(2,1)S(1)} collective-permute-done((bf16[36,16,128]{2,1,0:T(8,128)(2,1)S(1)}, bf16[36,16,128]{2,1,0:T(8,128)(2,1)S(1)}, u32[]{:S(2)}, u32[]{:S(2)}) %collective-permute-start.20) | collective-permute-done | bytes 147488 | tf_op jit(solution)/shard_map/ppermute | solution.py:475
  111.3 0.6 step_2.1
  112.0 1.6 %collective-permute-start.23 = (bf16[18,16,128]{2,1,0:T(8,128)(2,1)S(1)}, bf16[18,16,128]{2,1,0:T(8,128)(2,1)S(1)}, u32[]{:S(2)}, u32[]{:S(2)}) collective-permute-start(bf16[18,16,128]{2,1,0:T(8,128)(2,1)S(1)} %get-tuple-element.122), channel_id=1, source_target_pairs={{0,4},{2,6},{4,0},{6,2},{8,12},{10,14},{12,8},{14,10},{16,20},{18,... | collective-permute-start | bytes 221192 | tf_op jit(solution)/shard_map/ppermute | solution.py:475
  113.6 2.8 %collective-permute-done.23.refs_4_ = bf16[18,16,128]{2,1,0:T(8,128)(2,1)S(1)} collective-permute-done((bf16[18,16,128]{2,1,0:T(8,128)(2,1)S(1)}, bf16[18,16,128]{2,1,0:T(8,128)(2,1)S(1)}, u32[]{:S(2)}, u32[]{:S(2)}) %collective-permute-start.23) | collective-permute-done | bytes 73760 | tf_op jit(solution)/shard_map/ppermute | solution.py:475
  116.4 2.0 %collective-permute-done.22.refs_2_ = bf16[24,16,128]{2,1,0:T(8,128)(2,1)S(1)} collective-permute-done((bf16[24,16,128]{2,1,0:T(8,128)(2,1)S(1)}, bf16[24,16,128]{2,1,0:T(8,128)(2,1)S(1)}, u32[]{:S(2)}, u32[]{:S(2)}) %collective-permute-start.22) | collective-permute-done | bytes 98336 | tf_op jit(solution)/shard_map/ppermute | solution.py:475
  118.4 1.2 last.1
  119.6 2.8 %collective-permute-start.24 = (bf16[3,48,384]{2,1,0:T(8,128)(2,1)S(1)}, bf16[3,48,384]{2,1,0:T(8,128)(2,1)S(1)}, u32[]{:S(2)}, u32[]{:S(2)}) collective-permute-start(bf16[3,48,384]{2,1,0:T(8,128)(2,1)S(1)} %get-tuple-element.123), channel_id=1, source_target_pairs={{0,0},{1,16},{2,2},{3,18},{4,4},{5,20},{6,6},{7,22},{8,8},{9,24},{... | collective-permute-start | bytes 331784 | tf_op jit(solution)/shard_map/ppermute | solution.py:769
  122.5 4.0 %collective-permute-done.25.refs_2_ = bf16[48,128]{1,0:T(8,128)(2,1)S(1)} collective-permute-done((bf16[48,128]{1,0:T(8,128)(2,1)S(1)}, bf16[48,128]{1,0:T(8,128)(2,1)S(1)}, u32[]{:S(2)}, u32[]{:S(2)}) %collective-permute-start.25) | collective-permute-done | bytes 12320 | tf_op jit(solution)/shard_map/ppermute | solution.py:480
  126.5 2.9 %collective-permute-done.24.refs_0_ = bf16[3,48,384]{2,1,0:T(8,128)(2,1)S(1)} collective-permute-done((bf16[3,48,384]{2,1,0:T(8,128)(2,1)S(1)}, bf16[3,48,384]{2,1,0:T(8,128)(2,1)S(1)}, u32[]{:S(2)}, u32[]{:S(2)}) %collective-permute-start.24) | collective-permute-done | bytes 110624 | tf_op jit(solution)/shard_map/ppermute | solution.py:769
  129.4 0.7 finish.1
  (61 shorter events, 0.8 us)
Async XLA Ops:
  5.2 19.9 %collective-permute-start = (bf16[128,768]{1,0:T(8,128)(2,1)}, bf16[128,768]{1,0:T(8,128)(2,1)S(1)}, u32[]{:S(2)}, u32[]{:S(2)}) collective-permute-start(bf16[128,768]{1,0:T(8,128)(2,1)} %get-tuple-element.75.refs_2_), channel_id=1, source_target_pairs={{0,1},{1,0},{2,3},{3,2},{4,5},{5,4},{6,7},{7,6},{8,9},{9,8},{10,11... | collective-permute-start | bytes 589832 | tf_op jit(solution)/shard_map/ppermute | solution.py:480
  5.3 7.2 %collective-permute-start.1 = (bf16[64,128]{1,0:T(8,128)(2,1)}, bf16[64,128]{1,0:T(8,128)(2,1)S(1)}, u32[]{:S(2)}, u32[]{:S(2)}) collective-permute-start(bf16[64,128]{1,0:T(8,128)(2,1)} %get-tuple-element.80), channel_id=1, source_target_pairs={{0,1},{1,0},{2,3},{3,2},{4,5},{5,4},{6,7},{7,6},{8,9},{9,8},{10,11... | collective-permute-start | bytes 49160 | tf_op jit(solution)/shard_map/ppermute | solution.py:480
  12.5 0.7 copy-start.15
  13.2 11.9 %collective-permute-start.4 = (bf16[2,64,128]{2,1,0:T(8,128)(2,1)S(1)}, bf16[2,64,128]{2,1,0:T(8,128)(2,1)S(1)}, u32[]{:S(2)}, u32[]{:S(2)}) collective-permute-start(bf16[2,64,128]{2,1,0:T(8,128)(2,1)S(1)} %join_tok.1.refs_0_), channel_id=1, source_target_pairs={{0,24},{2,26},{4,28},{6,30},{8,16},{10,18},{12,20},{14,22},{16,8},... | collective-permute-start | bytes 98312 | tf_op jit(solution)/shard_map/ppermute | solution.py:475
  16.8 8.3 %collective-permute-start.3 = (bf16[2,64,128]{2,1,0:T(8,128)(2,1)S(1)}, bf16[2,64,128]{2,1,0:T(8,128)(2,1)S(1)}, u32[]{:S(2)}, u32[]{:S(2)}) collective-permute-start(bf16[2,64,128]{2,1,0:T(8,128)(2,1)S(1)} %join_tok.1.refs_0_), channel_id=1, source_target_pairs={{0,16},{2,18},{4,20},{6,22},{8,24},{10,26},{12,28},{14,30},{16,0},... | collective-permute-start | bytes 98312 | tf_op jit(solution)/shard_map/ppermute | solution.py:475
  16.8 8.3 %collective-permute-start.2 = (bf16[2,64,128]{2,1,0:T(8,128)(2,1)S(1)}, bf16[2,64,128]{2,1,0:T(8,128)(2,1)S(1)}, u32[]{:S(2)}, u32[]{:S(2)}) collective-permute-start(bf16[2,64,128]{2,1,0:T(8,128)(2,1)S(1)} %join_tok.1.refs_0_), channel_id=1, source_target_pairs={{0,8},{2,10},{4,12},{6,14},{8,0},{10,2},{12,4},{14,6},{16,24},{18,... | collective-permute-start | bytes 98312 | tf_op jit(solution)/shard_map/ppermute | solution.py:475
  17.6 1.3 copy-start.4
  18.8 1.3 copy-start.5
  20.1 1.3 copy-start.6
  21.4 0.7 copy-start.12
  22.0 0.7 copy-start.17
  22.7 0.7 copy-start.19
  23.4 0.7 copy-start.20
  24.1 3.0 %copy-start.11 = (bf16[128,768]{1,0:T(8,128)(2,1)S(1)}, bf16[128,768]{1,0:T(8,128)(2,1)}, u32[]{:S(2)}) copy-start(bf16[128,768]{1,0:T(8,128)(2,1)} %get-tuple-element.75.refs_2_) | copy-start | bytes 589828
  24.1 3.0 %copy-start.13 = (s32[2]{0:T(128)S(1)}, s32[2]{0:T(128)}, u32[]{:S(2)}) copy-start(s32[2]{0:T(128)} %pad_add_fusion.refs_0_) | copy-start | bytes 28
  24.1 12.3 %copy-start.2 = (bf16[1536,768]{1,0:T(8,128)(2,1)S(1)}, bf16[1536,768]{1,0:T(8,128)(2,1)}, u32[]{:S(2)}) copy-start(bf16[1536,768]{1,0:T(8,128)(2,1)} %refs_1_.1) | copy-start | bytes 7077892
  25.1 11.3 %copy-start.10 = (bf16[1,128,768]{2,1,0:T(8,128)(2,1)S(1)}, bf16[1,128,768]{2,1,0:T(8,128)(2,1)}, u32[]{:S(2)}) copy-start(bf16[1,128,768]{2,1,0:T(8,128)(2,1)} %param.39) | copy-start | bytes 589828
  25.2 11.2 %copy-start.22 = (f32[768]{0:T(1024)S(1)}, f32[768]{0:T(1024)}, u32[]{:S(2)}) copy-start(f32[768]{0:T(1024)} %param.29) | copy-start | bytes 9220
  25.2 11.2 %copy-start.9 = (bf16[1,128,768]{2,1,0:T(8,128)(2,1)S(1)}, bf16[1,128,768]{2,1,0:T(8,128)(2,1)}, u32[]{:S(2)}) copy-start(bf16[1,128,768]{2,1,0:T(8,128)(2,1)} %param.20) | copy-start | bytes 589828
  25.2 5.8 %collective-permute-start.7 = (bf16[8,64,128]{2,1,0:T(8,128)(2,1)S(1)}, bf16[8,64,128]{2,1,0:T(8,128)(2,1)S(1)}, u32[]{:S(2)}, u32[]{:S(2)}) collective-permute-start(bf16[8,64,128]{2,1,0:T(8,128)(2,1)S(1)} %bitcast.34), channel_id=1, source_target_pairs={{0,6},{2,4},{4,2},{6,0},{8,14},{10,12},{12,10},{14,8},{16,22},{18,... | collective-permute-start | bytes 393224 | tf_op jit(solution)/shard_map/ppermute | solution.py:475
  25.3 8.6 %collective-permute-start.6 = (bf16[8,64,128]{2,1,0:T(8,128)(2,1)S(1)}, bf16[8,64,128]{2,1,0:T(8,128)(2,1)S(1)}, u32[]{:S(2)}, u32[]{:S(2)}) collective-permute-start(bf16[8,64,128]{2,1,0:T(8,128)(2,1)S(1)} %bitcast.35), channel_id=1, source_target_pairs={{0,4},{2,6},{4,0},{6,2},{8,12},{10,14},{12,8},{14,10},{16,20},{18,... | collective-permute-start | bytes 393224 | tf_op jit(solution)/shard_map/ppermute | solution.py:475
  26.8 7.0 %collective-permute-start.5 = (bf16[8,64,128]{2,1,0:T(8,128)(2,1)S(1)}, bf16[8,64,128]{2,1,0:T(8,128)(2,1)S(1)}, u32[]{:S(2)}, u32[]{:S(2)}) collective-permute-start(bf16[8,64,128]{2,1,0:T(8,128)(2,1)S(1)} %bitcast.36), channel_id=1, source_target_pairs={{0,2},{2,0},{4,6},{6,4},{8,10},{10,8},{12,14},{14,12},{16,18},{18,... | collective-permute-start | bytes 393224 | tf_op jit(solution)/shard_map/ppermute | solution.py:475
  27.1 13.7 %copy-start.1 = (bf16[768,1536]{1,0:T(8,128)(2,1)S(1)}, bf16[768,1536]{1,0:T(8,128)(2,1)}, u32[]{:S(2)}) copy-start(bf16[768,1536]{1,0:T(8,128)(2,1)} %refs_9_.1) | copy-start | bytes 7077892
  33.9 7.0 %copy-start = (bf16[768,1536]{1,0:T(8,128)(2,1)S(1)}, bf16[768,1536]{1,0:T(8,128)(2,1)}, u32[]{:S(2)}) copy-start(bf16[768,1536]{1,0:T(8,128)(2,1)} %refs_8_.1) | copy-start | bytes 7077892
  33.9 7.0 %copy-start.7 = (bf16[768,768]{1,0:T(8,128)(2,1)S(1)}, bf16[768,768]{1,0:T(8,128)(2,1)}, u32[]{:S(2)}) copy-start(bf16[768,768]{1,0:T(8,128)(2,1)} %refs_7_.1) | copy-start | bytes 3538948
  36.0 4.8 %collective-permute-start.8 = (bf16[128,384]{1,0:T(8,128)(2,1)S(1)}, bf16[128,384]{1,0:T(8,128)(2,1)S(1)}, u32[]{:S(2)}, u32[]{:S(2)}) collective-permute-start(bf16[128,384]{1,0:T(8,128)(2,1)S(1)} %get-tuple-element.84), channel_id=1, source_target_pairs={{0,1},{1,0},{2,3},{3,2},{4,5},{5,4},{6,7},{7,6},{8,9},{9,8},{10,11... | collective-permute-start | bytes 294920 | tf_op jit(solution)/shard_map/ppermute | solution.py:480
  45.1 4.7 %collective-permute-start.9 = (bf16[384,128]{1,0:T(8,128)(2,1)S(1)}, bf16[384,128]{1,0:T(8,128)(2,1)S(1)}, u32[]{:S(2)}, u32[]{:S(2)}) collective-permute-start(bf16[384,128]{1,0:T(8,128)(2,1)S(1)} %get-tuple-element.89), channel_id=1, source_target_pairs={{0,1},{1,0},{2,3},{3,2},{4,5},{5,4},{6,7},{7,6},{8,9},{9,8},{10,11... | collective-permute-start | bytes 294920 | tf_op jit(solution)/shard_map/ppermute | solution.py:480
  51.9 2.8 %collective-permute-start.13 = (bf16[8,8,16,128]{3,2,1,0:T(8,128)(2,1)S(1)}, bf16[8,8,16,128]{3,2,1,0:T(8,128)(2,1)S(1)}, u32[]{:S(2)}, u32[]{:S(2)}) collective-permute-start(bf16[8,8,16,128]{3,2,1,0:T(8,128)(2,1)S(1)} %get-tuple-element.101), channel_id=1, source_target_pairs={{0,2},{2,0},{4,6},{6,4},{8,10},{10,8},{12,14},{14,12},{16,18},{18,... | collective-permute-start | bytes 786440 | tf_op jit(solution)/shard_map/ppermute | solution.py:475
  51.9 7.3 %collective-permute-start.12 = (bf16[128,768]{1,0:T(8,128)(2,1)S(1)}, bf16[128,768]{1,0:T(8,128)(2,1)S(1)}, u32[]{:S(2)}, u32[]{:S(2)}) collective-permute-start(bf16[128,768]{1,0:T(8,128)(2,1)S(1)} %get-tuple-element.99.refs_4_), channel_id=1, source_target_pairs={{0,1},{1,0},{2,3},{3,2},{4,5},{5,4},{6,7},{7,6},{8,9},{9,8},{10,11... | collective-permute-start | bytes 589832 | tf_op jit(solution)/shard_map/ppermute | solution.py:480
  54.4 19.1 %collective-permute-start.11 = (bf16[8,24,16,128]{3,2,1,0:T(8,128)(2,1)S(1)}, bf16[8,24,16,128]{3,2,1,0:T(8,128)(2,1)S(1)}, u32[]{:S(2)}, u32[]{:S(2)}) collective-permute-start(bf16[8,24,16,128]{3,2,1,0:T(8,128)(2,1)S(1)} %get-tuple-element.97), channel_id=1, source_target_pairs={{0,2},{2,0},{4,6},{6,4},{8,10},{10,8},{12,14},{14,12},{16,18},{18,... | collective-permute-start | bytes 2359304 | tf_op jit(solution)/shard_map/ppermute | solution.py:475
  60.6 12.9 %collective-permute-start.14 = (bf16[8,18,16,128]{3,2,1,0:T(8,128)(2,1)S(1)}, bf16[8,18,16,128]{3,2,1,0:T(8,128)(2,1)S(1)}, u32[]{:S(2)}, u32[]{:S(2)}) collective-permute-start(bf16[8,18,16,128]{3,2,1,0:T(8,128)(2,1)S(1)} %get-tuple-element.104.refs_3_), channel_id=1, source_target_pairs={{0,2},{2,0},{4,6},{6,4},{8,10},{10,8},{12,14},{14,12},{16,18},{18,... | collective-permute-start | bytes 1769480 | tf_op jit(solution)/shard_map/ppermute | solution.py:475
  60.7 14.8 %copy-start.21 = (f32[768]{0:T(1024)S(1)}, f32[768]{0:T(1024)}, u32[]{:S(2)}) copy-start(f32[768]{0:T(1024)} %refs_5_.3) | copy-start | bytes 9220
  60.7 5.9 %collective-permute-start.15 = (bf16[32,16,128]{2,1,0:T(8,128)(2,1)S(1)}, bf16[32,16,128]{2,1,0:T(8,128)(2,1)S(1)}, u32[]{:S(2)}, u32[]{:S(2)}) collective-permute-start(bf16[32,16,128]{2,1,0:T(8,128)(2,1)S(1)} %get-tuple-element.105), channel_id=1, source_target_pairs={{0,4},{2,6},{4,0},{6,2},{8,12},{10,14},{12,8},{14,10},{16,20},{18,... | collective-permute-start | bytes 393224 | tf_op jit(solution)/shard_map/ppermute | solution.py:475
  67.2 6.3 %collective-permute-start.16 = (bf16[16,16,128]{2,1,0:T(8,128)(2,1)S(1)}, bf16[16,16,128]{2,1,0:T(8,128)(2,1)S(1)}, u32[]{:S(2)}, u32[]{:S(2)}) collective-permute-start(bf16[16,16,128]{2,1,0:T(8,128)(2,1)S(1)} %get-tuple-element.107), channel_id=1, source_target_pairs={{0,16},{2,18},{4,20},{6,22},{8,24},{10,26},{12,28},{14,30},{16,0},... | collective-permute-start | bytes 196616 | tf_op jit(solution)/shard_map/ppermute | solution.py:475
  74.4 8.5 %collective-permute-start.17 = (bf16[96,16,128]{2,1,0:T(8,128)(2,1)S(1)}, bf16[96,16,128]{2,1,0:T(8,128)(2,1)S(1)}, u32[]{:S(2)}, u32[]{:S(2)}) collective-permute-start(bf16[96,16,128]{2,1,0:T(8,128)(2,1)S(1)} %get-tuple-element.109), channel_id=1, source_target_pairs={{0,4},{2,6},{4,0},{6,2},{8,12},{10,14},{12,8},{14,10},{16,20},{18,... | collective-permute-start | bytes 1179656 | tf_op jit(solution)/shard_map/ppermute | solution.py:475
  74.8 7.1 %collective-permute-start.18 = (bf16[80,16,128]{2,1,0:T(8,128)(2,1)S(1)}, bf16[80,16,128]{2,1,0:T(8,128)(2,1)S(1)}, u32[]{:S(2)}, u32[]{:S(2)}) collective-permute-start(bf16[80,16,128]{2,1,0:T(8,128)(2,1)S(1)} %get-tuple-element.111), channel_id=1, source_target_pairs={{0,8},{2,10},{4,12},{6,14},{8,0},{10,2},{12,4},{14,6},{16,24},{18,... | collective-permute-start | bytes 983048 | tf_op jit(solution)/shard_map/ppermute | solution.py:475
  75.0 5.7 %collective-permute-start.10 = (bf16[768,128]{1,0:T(8,128)(2,1)S(1)}, bf16[768,128]{1,0:T(8,128)(2,1)S(1)}, u32[]{:S(2)}, u32[]{:S(2)}) collective-permute-start(bf16[768,128]{1,0:T(8,128)(2,1)S(1)} %get-tuple-element.95), channel_id=1, source_target_pairs={{0,1},{1,0},{2,3},{3,2},{4,5},{5,4},{6,7},{7,6},{8,9},{9,8},{10,11... | collective-permute-start | bytes 589832 | tf_op jit(solution)/shard_map/ppermute | solution.py:480
  80.7 9.9 %copy-start.3 = (bf16[128,16,128]{2,1,0:T(8,128)(2,1)S(1)}, bf16[128,16,128]{2,1,0:T(8,128)(2,1)}, u32[]{:S(2)}) copy-start(bf16[128,16,128]{2,1,0:T(8,128)(2,1)} %param.22) | copy-start | bytes 1572868
  80.7 9.9 %copy-start.16 = (bf16[128,8]{0,1:T(8,128)(2,1)S(1)}, bf16[128,8]{0,1:T(8,128)(2,1)}, u32[]{:S(2)}) copy-start(bf16[128,8]{0,1:T(8,128)(2,1)} %param.34) | copy-start | bytes 6148
  80.7 9.9 %copy-start.18 = (f32[128]{0:T(128)S(1)}, f32[128]{0:T(128)}, u32[]{:S(2)}) copy-start(f32[128]{0:T(128)} %param.28) | copy-start | bytes 1540
  82.9 0.9 copy-start.8
  84.6 26.7 %collective-permute-start.19 = (bf16[48,16,128]{2,1,0:T(8,128)(2,1)S(1)}, bf16[48,16,128]{2,1,0:T(8,128)(2,1)S(1)}, u32[]{:S(2)}, u32[]{:S(2)}) collective-permute-start(bf16[48,16,128]{2,1,0:T(8,128)(2,1)S(1)} %get-tuple-element.113), channel_id=1, source_target_pairs={{0,8},{2,10},{4,12},{6,14},{8,0},{10,2},{12,4},{14,6},{16,24},{18,... | collective-permute-start | bytes 589832 | tf_op jit(solution)/shard_map/ppermute | solution.py:475
  86.7 3.8 %collective-permute-start.21 = (bf16[64,128]{1,0:T(8,128)(2,1)S(1)}, bf16[64,128]{1,0:T(8,128)(2,1)S(1)}, u32[]{:S(2)}, u32[]{:S(2)}) collective-permute-start(bf16[64,128]{1,0:T(8,128)(2,1)S(1)} %get-tuple-element.117), channel_id=1, source_target_pairs={{0,1},{1,0},{2,3},{3,2},{4,5},{5,4},{6,7},{7,6},{8,9},{9,8},{10,11... | collective-permute-start | bytes 49160 | tf_op jit(solution)/shard_map/ppermute | solution.py:480
  94.0 19.6 %all-to-all-start = ((f32[32,8,128]{2,1,0:T(8,128)}), f32[32,8,128]{2,1,0:T(8,128)S(1)}, u32[]{:S(2)}, u32[]{:S(2)}) async-start(f32[32,8,128]{2,1,0:T(8,128)} %get-tuple-element.118.refs_5_), calls=%async_computation | async-start | bytes 262144 | tf_op jit(solution)/shard_map/all_to_all | solution.py:484
  98.7 12.6 %collective-permute-start.20 = (bf16[36,16,128]{2,1,0:T(8,128)(2,1)S(1)}, bf16[36,16,128]{2,1,0:T(8,128)(2,1)S(1)}, u32[]{:S(2)}, u32[]{:S(2)}) collective-permute-start(bf16[36,16,128]{2,1,0:T(8,128)(2,1)S(1)} %get-tuple-element.115), channel_id=1, source_target_pairs={{0,16},{2,18},{4,20},{6,22},{8,24},{10,26},{12,28},{14,30},{16,0},... | collective-permute-start | bytes 442376 | tf_op jit(solution)/shard_map/ppermute | solution.py:475
  111.9 6.5 %collective-permute-start.22 = (bf16[24,16,128]{2,1,0:T(8,128)(2,1)S(1)}, bf16[24,16,128]{2,1,0:T(8,128)(2,1)S(1)}, u32[]{:S(2)}, u32[]{:S(2)}) collective-permute-start(bf16[24,16,128]{2,1,0:T(8,128)(2,1)S(1)} %get-tuple-element.120), channel_id=1, source_target_pairs={{0,16},{2,18},{4,20},{6,22},{8,24},{10,26},{12,28},{14,30},{16,0},... | collective-permute-start | bytes 294920 | tf_op jit(solution)/shard_map/ppermute | solution.py:475
  112.0 4.4 %collective-permute-start.23 = (bf16[18,16,128]{2,1,0:T(8,128)(2,1)S(1)}, bf16[18,16,128]{2,1,0:T(8,128)(2,1)S(1)}, u32[]{:S(2)}, u32[]{:S(2)}) collective-permute-start(bf16[18,16,128]{2,1,0:T(8,128)(2,1)S(1)} %get-tuple-element.122), channel_id=1, source_target_pairs={{0,4},{2,6},{4,0},{6,2},{8,12},{10,14},{12,8},{14,10},{16,20},{18,... | collective-permute-start | bytes 221192 | tf_op jit(solution)/shard_map/ppermute | solution.py:475
  113.6 16.5 %copy-start.14 = (f32[8,128]{1,0:T(8,128)}, f32[8,128]{1,0:T(8,128)S(1)}, u32[]{:S(2)}) copy-start(f32[8,128]{1,0:T(8,128)S(1)} %reduce_sum.9.refs_5_) | copy-start | bytes 12292
  119.6 9.8 %collective-permute-start.24 = (bf16[3,48,384]{2,1,0:T(8,128)(2,1)S(1)}, bf16[3,48,384]{2,1,0:T(8,128)(2,1)S(1)}, u32[]{:S(2)}, u32[]{:S(2)}) collective-permute-start(bf16[3,48,384]{2,1,0:T(8,128)(2,1)S(1)} %get-tuple-element.123), channel_id=1, source_target_pairs={{0,0},{1,16},{2,2},{3,18},{4,4},{5,20},{6,6},{7,22},{8,8},{9,24},{... | collective-permute-start | bytes 331784 | tf_op jit(solution)/shard_map/ppermute | solution.py:769
  122.4 4.1 %collective-permute-start.25 = (bf16[48,128]{1,0:T(8,128)(2,1)S(1)}, bf16[48,128]{1,0:T(8,128)(2,1)S(1)}, u32[]{:S(2)}, u32[]{:S(2)}) collective-permute-start(bf16[48,128]{1,0:T(8,128)(2,1)S(1)} %get-tuple-element.125), channel_id=1, source_target_pairs={{0,1},{1,0},{2,3},{3,2},{4,5},{5,4},{6,7},{7,6},{8,9},{9,8},{10,11... | collective-permute-start | bytes 36872 | tf_op jit(solution)/shard_map/ppermute | solution.py:480

commit v7 on v6

--- a/solution.py
+++ b/solution.py
@@ -48,7 +48,7 @@
         arrays.append(array)
         specs.append(pl.BlockSpec(memory_space=space))
         moved += array.size * array.dtype.itemsize
-    for shape, kind in outs:
+    for shape, kind, *_ in outs:
         size = jnp.dtype(kind).itemsize
         for extent in shape:
             size *= extent
@@ -79,9 +79,9 @@
     return pl.pallas_call(
         whole,
         name=name,
-        out_shape=[jax.ShapeDtypeStruct(shape, kind) for shape, kind in outs],
+        out_shape=[jax.ShapeDtypeStruct(one[0], one[1]) for one in outs],
         in_specs=specs,
-        out_specs=[pl.BlockSpec(memory_space=VMEM)] * len(outs),
+        out_specs=[pl.BlockSpec(memory_space=(*one, VMEM)[2]) for one in outs],
         scratch_shapes=list(scratch) + extra,
         compiler_params=pltpu.CompilerParams(vmem_limit_bytes=limit * MIB),
         cost_estimate=pl.CostEstimate(flops=flops, bytes_accessed=moved, transcendentals=0),
@@ -104,9 +104,25 @@
     return spread, row_col
 
 
-def enter_kernel(toks, cols, ids, noisy, single, restype, table, gain, pair, pair_gain, *rest):
-    w_pair, x_out, bias_outs = rest[0], rest[1], rest[2 : 2 + toks]
-    rounded, bias = rest[2 + toks :]
+def own_slice(weight, t, own_width):
+    if weight.shape[1] == own_width:
+        return weight
+    return weight.at[:, pl.ds(pl.multiple_of(t * own_width, own_width), own_width)]
+
+
+def enter_kernel(toks, cols, ids, *rest):
+    noisy, single, restype, table, gain, pair, pair_gain, w_pair, chain, keymask = rest[:10]
+    chain_weight, weights = rest[10], rest[11:14]
+    x_out, columns, slices, facts_out, chain_out = rest[14:19]
+    bias_outs, (rounded, bias, sem) = rest[19 : 19 + toks], rest[19 + toks :]
+    t = ids[0]
+    transfers = []
+    for k in range(3):
+        transfer = pltpu.make_async_copy(
+            own_slice(weights[k], t, slices.shape[2]), slices.at[k], sem.at[k]
+        )
+        transfer.start()
+        transfers.append(transfer)
     rows = noisy.shape[0]
     pair_scaled, _, _ = layer_forward(pair[...].astype(f32), pair_gain[...])
     rounded[...] = pair_scaled.astype(bf16).astype(f32)
@@ -115,38 +131,21 @@
     total = jnp.zeros((head_count * cols, rows), f32)
     for j in range(cols):
         column = rounded[pl.ds(j, rows, stride=cols), :].astype(bf16)
+        columns[j] = column
         total = total + mm(jnp.where(row_col == j, spread, 0.0).astype(bf16), column, NT)
     bias[...] = total
     part = bias_outs[0].shape[0]
     for r in range(toks):
-        start = pl.multiple_of(jnp.bitwise_xor(ids[0], r) * part, part)
+        start = pl.multiple_of(jnp.bitwise_xor(t, r) * part, part)
         bias_outs[r][...] = bias[pl.ds(start, part), :].astype(bf16)
     normed_scaled, _, _ = layer_forward(noisy[...].astype(f32), gain[...])
     types = table.shape[0]
     onehot = (lax.broadcasted_iota(jnp.int32, (types, rows), 0) == restype[...]).astype(f32)
     condition = single[...].astype(f32) + mm(onehot.astype(bf16), table[...], TN)
     x_out[...] = (normed_scaled + condition).astype(bf16)
-
-
-def own_slice(weight, t, own_width):
-    if weight.shape[1] == own_width:
-        return weight
-    return weight.at[:, pl.ds(pl.multiple_of(t * own_width, own_width), own_width)]
-
-
-def stage_kernel(own_heads, ids, chain, keymask, chain_weight, *rest):
-    weights, (slices, facts_out, chain_out, sem) = rest[:3], rest[3:]
-    t = ids[0]
-    own_width = slices.shape[2]
-    transfers = []
-    for k in range(3):
-        transfer = pltpu.make_async_copy(
-            own_slice(weights[k], t, own_width), slices.at[k], sem.at[k]
-        )
-        transfer.start()
-        transfers.append(transfer)
     chain_row = chain[...]
     tokens = chain_row.shape[1]
+    own_heads = head_count // toks
     keep_row = keymask[...].astype(f32)
     line = lax.broadcasted_iota(jnp.int32, (128, tokens), 0)
     facts = jnp.where(line == 0, chain_row.astype(f32), 0.0) + jnp.where(line == 1, keep_row, 0.0)
@@ -177,6 +176,11 @@
 def join_kernel(*refs):
     for n, ref in enumerate(refs[:-1]):
         refs[-1][n] = ref[...]
+
+
+def join_tok_kernel(x, *refs):
+    refs[-1][...] = x[...]
+    join_kernel(*refs[:-1])
 
 
 def attention_kernel(copies, toks, near, cols, head_width, ids, query, key, value, *rest):
@@ -269,7 +273,8 @@
     blocks, d_logits = rest[toks + 7 :]
     d_res_out[...] = d_res_b[...]
     t = ids[0]
-    core = low_bits(ids[1], 2)
+    bit = low_bits(ids[1] // 2, 2)
+    heads = weights.shape[0]
     for r in range(toks):
         blocks[jnp.bitwise_xor(t, r)] = parts[r][...]
     d_att = jnp.concatenate([blocks[a] for a in range(toks)], axis=1)
@@ -284,10 +289,10 @@
         delta = jnp.sum(weights_f * d_weights, axis=0, keepdims=True)
         d_logits_b = (weights_f * (d_weights - delta)).astype(bf16)
         d_logits[...] = d_logits_b
-        for q in range(copies // 2):
-            for side, out in ((core, bias_kept), (1 - core, bias_sent)):
-                start = pl.multiple_of((2 * q + side) * cols, cols)
-                put(out, q, h * count, d_logits[pl.ds(start, cols), :])
+        for k in range(copies // 2):
+            for side, out in ((bit, bias_kept), (1 - bit, bias_sent)):
+                start = pl.multiple_of((k // 2 * 4 + side * 2 + k % 2) * cols, cols)
+                put(out, (k * heads + h) * count, d_logits[pl.ds(start, cols), :])
         d_query[span, :] = (mm(key[span, :], d_logits_b) * scale).astype(bf16)
         d_key[span, :] = (mm(query[span, :], d_logits_b, NT) * scale).astype(bf16)
         d_value[span, :] = mm(d_att_h, weights_b, NT).astype(bf16)
@@ -297,14 +302,14 @@
     return -(-rows // 16) * -(-lanes // 128)
 
 
-def put(out, q, base, value):
+def put(out, base, value):
     rows, lanes = value.shape
     for i in range(0, rows, 16):
         for j in range(0, lanes, 128):
             part = value[i : i + 16, j : j + 128]
             if part.shape != (16, 128):
-                out[q, base] = jnp.zeros((16, 128), out.dtype)
-            out[q, base, : part.shape[0], : part.shape[1]] = part
+                out[base] = jnp.zeros((16, 128), out.dtype)
+            out[base, : part.shape[0], : part.shape[1]] = part
             base += 1
 
 
@@ -318,7 +323,7 @@
     return whole[:rows, :lanes]
 
 
-def cut_wide(copies, toks, core, base, grad, kept, sent):
+def cut_wide(copies, toks, core, base, stride, grad, kept, sent):
     group = copies // toks
     cut, depth = grad.shape[1] // copies, grad.shape[1] // toks
     for side, out in ((core, kept), (1 - core, sent)):
@@ -326,7 +331,7 @@
             h = 2 * q // group
             first = pl.multiple_of((2 * q - h * group + side) * cut, 8)
             part = grad[pl.ds(first, cut), h * depth : (h + 1) * depth]
-            put(out, q, base, part.astype(bf16))
+            put(out, q * stride + base, part.astype(bf16))
 
 
 def first_kernel(copies, toks, ids, slices, x, d_query, d_key, d_value, *rest):
@@ -336,16 +341,17 @@
     rows = d_own.shape[1]
     cut = x.shape[1] // copies
     count = tile_count(cut, d_query.shape[0])
+    stride = 2 * count + tile_count(cut, rows * toks)
     for k, part in enumerate((d_query, d_key)):
         wide[...] = mm(part[...], x[...])
-        cut_wide(copies, toks, core, k * count, wide, kept, sent)
+        cut_wide(copies, toks, core, k * count, stride, wide, kept, sent)
     total = mm(slices[0], d_query[...]) + mm(slices[1], d_key[...])
     total = total + mm(slices[2], d_value[...])
     total_ref[...] = total
     for side, out in ((core, kept), (1 - core, sent)):
         for q in range(copies // 2):
             start = pl.multiple_of((2 * q + side) * cut, 8)
-            put(out, q, 2 * count, total_ref[pl.ds(start, cut), :].astype(bf16))
+            put(out, q * stride + 2 * count, total_ref[pl.ds(start, cut), :].astype(bf16))
     for a in range(toks):
         d_inputs[a] = total[:, a * rows : (a + 1) * rows]
     d_own[...] = d_inputs[t]
@@ -353,22 +359,29 @@
         d_others[r - 1][...] = d_inputs[jnp.bitwise_xor(t, r)].astype(bf16)
 
 
-def second_kernel(copies, toks, ids, x, att, d_value, *rest):
+def second_kernel(copies, toks, ids, x, att, d_value, bias_kept, bias_got, *rest):
     d_res_parts, (kept, sent, d_res, wide, narrow) = rest[:toks], rest[toks:]
     t, core = ids[0], low_bits(ids[1], 2)
     rows = d_res_parts[0].shape[0]
+    cut = narrow.shape[0] // copies
+    count = tile_count(cut, narrow.shape[1])
     wide[...] = mm(d_value[...], x[...])
-    cut_wide(copies, toks, core, 0, wide, kept, sent)
+    cut_wide(copies, toks, core, 0, 2 * count, wide, kept, sent)
     for r in range(toks):
         start = pl.multiple_of(jnp.bitwise_xor(t, r) * rows, rows)
         d_res[pl.ds(start, rows), :] = d_res_parts[r][...]
     narrow[...] = mm(d_res[...], att[...], TN)
-    cut = narrow.shape[0] // copies
-    count = tile_count(cut, narrow.shape[1])
+    base = copies * count
+    bias_count = bias_kept.shape[0] // (copies // 2)
     for side, out in ((core, kept), (1 - core, sent)):
         for q in range(copies // 2):
             first = pl.multiple_of((2 * q + side) * cut, 8)
-            put(out, q, count, narrow[pl.ds(first, cut), :].astype(bf16))
+            put(out, (2 * q + 1) * count, narrow[pl.ds(first, cut), :].astype(bf16))
+        for z in range(copies // 4):
+            span = pl.ds((2 * z + side) * bias_count, bias_count)
+            out[base + z * bias_count : base + (z + 1) * bias_count] = (
+                bias_kept[span].astype(f32) + bias_got[span].astype(f32)
+            ).astype(bf16)
 
 
 def step_kernel(segments, ids, *refs):
@@ -440,34 +453,42 @@
     ).astype(bf16)
 
 
-def pair_kernel(toks, cols, ids, pair, gain, w_pair, *rest):
-    parts, (grad_pair, weight_grad, rounded, spread_out, grads) = rest[:toks], rest[toks:]
-    head_count = w_pair.shape[0]
-    part_rows, rows = parts[0].shape
+def set_heads(toks, ids, parts, grads):
+    part_rows = parts[0].shape[0]
     for r in range(toks):
         start = pl.multiple_of(jnp.bitwise_xor(ids[0], r) * part_rows, part_rows)
         grads[pl.ds(start, part_rows), :] = parts[r][...].astype(f32)
-    grad = grads[...]
-    pair_scaled, pair_hat, pair_inverse = layer_forward(pair[...].astype(f32), gain[...])
-    rounded[...] = pair_scaled.astype(bf16).astype(f32)
-    spread, row_col = pair_weight_rows(w_pair[...], head_count, cols)
-    grad_b = grad.astype(bf16)
-    turned = jnp.transpose(grad).astype(bf16)
-    sums = jnp.zeros(spread.shape, f32)
+
+
+def pair_weight_kernel(toks, ids, columns, *rest):
+    parts, (weight_grad, grads) = rest[:toks], rest[toks:]
+    set_heads(toks, ids, parts, grads)
+    grad_b = grads[...].astype(bf16)
+    cols, _, channels = columns.shape
+    row_col = low_bits(lax.broadcasted_iota(jnp.int32, (grad_b.shape[0], channels), 0), cols)
+    sums = jnp.zeros((grad_b.shape[0], channels), f32)
     for j in range(cols):
-        here = row_col == j
-        column = rounded[pl.ds(j, rows, stride=cols), :].astype(bf16)
-        sums = sums + jnp.where(here, mm(grad_b, column), 0.0)
+        sums = sums + jnp.where(row_col == j, mm(grad_b, columns[j]), 0.0)
+    for h in range(weight_grad.shape[1]):
+        line = jnp.sum(sums[h * cols : (h + 1) * cols, :], axis=0, keepdims=True)
+        for n in range(weight_grad.shape[0]):
+            weight_grad[n, h : h + 1, :] = line
+
+
+def pair_kernel(toks, cols, ids, pair, gain, w_pair, *rest):
+    parts, (grad_pair, spread_out, grads) = rest[:toks], rest[toks:]
+    set_heads(toks, ids, parts, grads)
+    rows = parts[0].shape[1]
+    _, pair_hat, pair_inverse = layer_forward(pair[...].astype(f32), gain[...])
+    spread, row_col = pair_weight_rows(w_pair[...], w_pair.shape[0], cols)
+    turned = jnp.transpose(grads[...]).astype(bf16)
+    for j in range(cols):
         spread_out[pl.ds(j, rows, stride=cols), :] = mm(
-            turned, jnp.where(here, spread, 0.0).astype(bf16)
+            turned, jnp.where(row_col == j, spread, 0.0).astype(bf16)
         )
     grad_pair[...] = layer_backward(
         spread_out[...], gain[...], pair_hat, pair_inverse
     ).astype(bf16)
-    for h in range(head_count):
-        line = jnp.sum(sums[h * cols : (h + 1) * cols, :], axis=0, keepdims=True)
-        for n in range(weight_grad.shape[0]):
-            weight_grad[n, h : h + 1, :] = line
 
 
 def swap_copy(value, mask):
@@ -526,45 +547,48 @@
     pair_gain2 = pair_gain.reshape(1, channels)
     norm_gain2 = norm_gain.reshape(1, width)
 
-    entered = call(
-        functools.partial(enter_kernel, toks, cols),
-        "enter",
-        [where_am_i]
-        + [(array, "fetch") for array in (noisy2, single, restype.reshape(1, rows))]
-        + [(array, "fetch") for array in (restype_table, norm_gain, pair2, pair_gain2, w_pair.T)],
-        [((rows, width), bf16)] + [((own_heads * cols, rows), bf16)] * toks,
-        [VMEM((rows * cols, channels), f32), VMEM((heads * cols, rows), f32)],
-        flops=2 * heads * cols * rows * channels * cols,
-        limit=60,
-    )
-    x_own, bias_parts = entered[0], entered[1:]
-    x_parts = [x_own] + [swap_tok(x_own, r) for r in range(1, toks)]
-    near = 4
-    far = copies // near
     weights3 = [w_query, w_key, w_value]
     if own_width % 128:
         weights3 = [
             lax.dynamic_slice_in_dim(w, ids[0] * own_width, own_width, axis=1) for w in weights3
         ]
-    slices, facts, chain_row = call(
-        functools.partial(stage_kernel, own_heads),
-        "stage",
-        [where_am_i, chain.reshape(1, tokens), keymask.reshape(1, tokens), (chain_weight, SMEM)]
+    small = [noisy2, single, restype.reshape(1, rows), restype_table, norm_gain, pair2, pair_gain2]
+    small += [w_pair.T, chain.reshape(1, tokens), keymask.reshape(1, tokens)]
+    entered = call(
+        functools.partial(enter_kernel, toks, cols),
+        "enter",
+        [where_am_i]
+        + [(array, "fetch") for array in small]
+        + [(chain_weight, SMEM)]
         + [(w, ANY) for w in weights3],
-        [((3, width, own_width), bf16), ((tokens, 128), f32), ((1, tokens), f32)],
-        [pltpu.SemaphoreType.DMA((3,))],
-    )
-    def join(name, parts, deps=()):
-        shape = (len(parts),) + parts[0].shape
-        return call(join_kernel, name, parts, [(shape, bf16)], deps=deps)[0]
-
-    mine = join(
-        "join_tok", [bias_parts[0]] + [swap_tok(bias_parts[r], r) for r in range(1, toks)]
-    )
-    lines = join(
+        [((rows, width), bf16), ((cols, rows, channels), bf16)]
+        + [((3, width, own_width), bf16, ANY), ((tokens, 128), f32), ((1, tokens), f32)]
+        + [((own_heads * cols, rows), bf16)] * toks,
+        [VMEM((rows * cols, channels), f32), VMEM((heads * cols, rows), f32)]
+        + [pltpu.SemaphoreType.DMA((3,))],
+        flops=2 * heads * cols * rows * channels * cols,
+        limit=60,
+    )
+    x_own, columns, slices, facts, chain_row = entered[:5]
+    bias_parts = entered[5:]
+    near = 4
+    far = copies // near
+    part_shape = bias_parts[0].shape
+    bias_tok = [bias_parts[0]] + [swap_tok(bias_parts[r], r) for r in range(1, toks)]
+    mine, x_own = call(
+        join_tok_kernel,
+        "join_tok",
+        [(array, "fetch") for array in [x_own] + bias_tok],
+        [((toks,) + part_shape, bf16), ((rows, width), bf16)],
+        limit=60,
+    )
+    x_parts = [x_own] + [swap_tok(x_own, r) for r in range(1, toks)]
+    (lines,) = call(
+        join_kernel,
         "join_far",
         [mine] + [swap_copy(mine, m * near) for m in range(1, far)],
-        deps=x_parts[1:] + [chain_row],
+        [((far, toks) + part_shape, bf16)],
+        deps=x_parts[1:],
     )
     lines = lines.reshape((far * toks,) + lines.shape[2:])
     biases = [lines] + [swap_copy(lines, m) for m in range(1, near)]
@@ -608,7 +632,7 @@
     d_res, d_res_b, d_att = results[0], results[1], results[2:]
     d_att_parts = [d_att[0]] + [swap_tok(d_att[r], r) for r in range(1, toks)]
     bias_tiles = own_heads * tile_count(cols, tokens)
-    bias_shape = (copies // 2, bias_tiles, 16, 128)
+    bias_shape = (copies // 2 * bias_tiles, 16, 128)
     d_query, d_key, d_value, bias_kept, bias_sent, d_res_b = call(
         functools.partial(backward_kernel, copies, toks, cols, head_width),
         "backward",
@@ -619,17 +643,16 @@
         limit=32,
     )
     d_res_parts = [d_res_b] + [swap_tok(d_res_b, r) for r in range(1, toks)]
-    bias_kept, bias_got = [
-        array.reshape((-1, 16, 128)) for array in (bias_kept, swap_copy(bias_sent, 1))
-    ]
+    bias_got = swap_copy(bias_sent, 2)
 
     wide_tiles = tile_count(cut, own_width)
     single_tiles = tile_count(cut, tokens)
+    first_tiles, second_tiles = 2 * wide_tiles + single_tiles, 2 * wide_tiles
     found = call(
         functools.partial(first_kernel, copies, toks),
         "first",
         [where_am_i, slices, x, d_query, d_key, d_value],
-        [((copies // 2, 2 * wide_tiles + single_tiles, 16, 128), bf16)] * 2
+        [((copies // 2 * first_tiles, 16, 128), bf16)] * 2
         + [((width, rows), f32)]
         + [((width, rows), bf16)] * (toks - 1),
         [
@@ -668,24 +691,17 @@
 
     masks = [1 << b for b in range(1, copies.bit_length() - 1)]
     masks_b = masks[1:] + masks[:1]
-    bias_left, bias_parts = list(masks), copies // 2
-    (bias_pair,) = step(
-        "bias_first",
-        [(bias_kept, bias_got)],
-        [(0, 0, bias_parts, bias_tiles, masks[0], bias_left, 0)],
-    )
     kept_b, sent_b = call(
         functools.partial(second_kernel, copies, toks),
         "second",
-        [where_am_i, x, att, d_value] + d_res_parts,
-        [((copies // 2, 2 * wide_tiles, 16, 128), bf16)] * 2,
+        [where_am_i, x, att, d_value, bias_kept, bias_got] + d_res_parts,
+        [((copies // 2 * second_tiles + copies // 4 * bias_tiles, 16, 128), bf16)] * 2,
         [
             VMEM((tokens, width), bf16),
             VMEM((own_width, width), f32),
             VMEM((width, own_width), f32),
         ],
         flops=4 * tokens * width * own_width,
-        deps=[bias_pair[0]],
     )
     got_b = swap_copy(sent_b, 1)
 
@@ -695,59 +711,29 @@
         [noisy3, norm_gain2, d_res, d_own] + d_others,
         [((rows, width), bf16)],
     )
-    for mask in masks[:1:-1]:
-        bias_left = [other for other in bias_left if other != masks[0]]
-        bias_parts //= 2
-        (bias_pair,) = step(
-            "bias_%d" % mask,
-            [bias_pair],
-            [(0, 0, bias_parts, bias_tiles, mask, bias_left, 0)],
-            deps=[sent_b],
-        )
-        bias_left = [other for other in bias_left if other != mask]
-    first_tiles, second_tiles = 2 * wide_tiles + single_tiles, 2 * wide_tiles
-    pairs = [
-        tuple(array.reshape((-1, 16, 128)) for array in one)
-        for one in ((kept, got), (kept_b, got_b))
-    ]
-    pairs.append(bias_pair)
+    pairs = [(kept, got), (kept_b, got_b)]
     parts = copies // 2
     for n, (mask, mask_b) in enumerate(zip(masks, masks_b)):
         segments = [
             (0, 0, parts, first_tiles, mask, masks[n:], 0),
             (1, 0, parts, second_tiles, mask_b, masks_b[n:], 1),
         ]
-        deps = []
-        if n == 0:
-            segments.append((2, 0, 2, bias_tiles, mask_b, [mask_b], 1))
-        if n == 1:
+        bias_base = parts * second_tiles
+        if n + 1 < len(masks):
+            segments.append((1, bias_base, parts // 2, bias_tiles, mask_b, masks_b[n:-1], 1))
+        else:
             bias_ready = pairs[1]
-            bias_base = parts * second_tiles
-            deps = [grad_noisy]
-        if n == 2:
-            deps = [weight_grad]
-        pairs = step("step_%d" % n, pairs, segments, deps=deps)
+        pairs = step("step_%d" % n, pairs, segments, deps=[grad_noisy] if n == 1 else ())
         parts //= 2
-        if n == 1:
-            bias_pieces = call(
-                functools.partial(last_bias_kernel, toks, bias_base, bias_tiles, cols),
-                "last_bias",
-                [where_am_i, *bias_ready],
-                [((own_heads * cols, rows), bf16)] * toks,
-                [VMEM((toks, own_heads * cols, rows), bf16)],
-                deps=[pairs[0][0]],
-            )
-            bias_pieces = [bias_pieces[0]] + [
-                swap_tok(bias_pieces[r], r) for r in range(1, toks)
-            ]
-            grad_pair, weight_grad = call(
-                functools.partial(pair_kernel, toks, cols),
-                "pair",
-                [where_am_i, pair2, pair_gain2, w_pair.T] + bias_pieces,
-                [((rows * cols, channels), bf16), ((devices, heads, channels), f32)],
-                [VMEM((rows * cols, channels), f32)] * 2 + [VMEM((heads * cols, rows), f32)],
-                flops=4 * heads * cols * rows * channels * cols,
-            )
+    bias_pieces = call(
+        functools.partial(last_bias_kernel, toks, bias_base, bias_tiles, cols),
+        "last_bias",
+        [where_am_i, *bias_ready],
+        [((own_heads * cols, rows), bf16)] * toks,
+        [VMEM((toks, own_heads * cols, rows), bf16)],
+        deps=[pairs[0][0]],
+    )
+    bias_pieces = [bias_pieces[0]] + [swap_tok(bias_pieces[r], r) for r in range(1, toks)]
 
     group = copies // toks
     swaps = []
@@ -755,15 +741,33 @@
         for t in range(toks):
             swaps.append((c * toks + t, (t * group + c % group) * toks + c // group))
 
-    weight_grad = jnp.sum(exchange(weight_grad), axis=0)
     last = call(
         functools.partial(last_kernel, toks),
         "last",
         [where_am_i, *pairs[0], *pairs[1]],
         [((3, cut, own_width), bf16), ((cut, own_width), f32)] + [((cut, rows), bf16)] * toks,
         [VMEM((toks, cut, rows), f32)],
+        deps=bias_pieces[1:],
+    )
+    (weight_grad,) = call(
+        functools.partial(pair_weight_kernel, toks),
+        "pair_weight",
+        [where_am_i, columns] + bias_pieces,
+        [((devices, heads, channels), f32)],
+        [VMEM((heads * cols, rows), f32)],
+        flops=2 * heads * cols * rows * channels * cols,
+        deps=[last[0]],
+    )
+    (grad_pair,) = call(
+        functools.partial(pair_kernel, toks, cols),
+        "pair",
+        [where_am_i, pair2, pair_gain2, w_pair.T] + bias_pieces,
+        [((rows * cols, channels), bf16)],
+        [VMEM((rows * cols, channels), f32), VMEM((heads * cols, rows), f32)],
+        flops=2 * heads * cols * rows * channels * cols,
         deps=[weight_grad],
     )
+    weight_grad = jnp.sum(exchange(weight_grad), axis=0)
     grad_out, singles = last[1], last[2:]
     singles = [singles[0]] + [swap_tok(singles[r], r) for r in range(1, toks)]
     moved = lax.ppermute(last[0], ("copy", "tok"), swaps)

time: 131 us -> 164 us (1.25)
  Pallas kernels: 29.7 us -> 84.2 us
  waiting for transfers between devices: 63.2 us -> 42.3 us
  local copies, waits for them, and re-layouts: 8.22 us -> 4.77 us
  starting transfers between devices: 27.5 us -> 30.6 us
    pallas_call x21 -> x19, Pallas kernels: 29.7 us -> 84.2 us  [call(): pl.pallas_call(whole, name=name, out_shape=[jax.ShapeDtypeStruct(one[0],...]
    ppermute x17 -> x15, waiting for transfers between devices: 30.9 us -> 19.6 us  [swap_copy(): return lax.ppermute(value, 'copy', [(i, i ^ mask) for i in range(size)])]
    ppermute x8, waiting for transfers between devices: 29.4 us -> 19.5 us  [swap_tok(): return lax.ppermute(value, 'tok', [(i, i ^ mask) for i in range(size)])]
    ppermute x8, starting transfers between devices: 4.37 us -> 7.86 us  [swap_tok(): return lax.ppermute(value, 'tok', [(i, i ^ mask) for i in range(size)])]
    unnamed x46 -> x42, local copies, waits for them, and re-layouts: 8.21 us -> 4.76 us
    ppermute x17 -> x15, starting transfers between devices: 15.6 us -> 13.6 us  [swap_copy(): return lax.ppermute(value, 'copy', [(i, i ^ mask) for i in range(size)])]
  transfers between devices with their start and end apart: 27 -> 25, of which waited for: 16 -> 16; matrix products, arithmetic and copies ran while one was open for 0% -> 0% of each run, Pallas kernels for 11% -> 7%
where the time goes in v7:
time: 164 us
  Pallas kernels  84.2 us (51%)
  waiting for transfers between devices  42.3 us (26%)
  starting transfers between devices  30.6 us (19%)
  local copies, waits for them, and re-layouts  4.77 us (3%)
    pallas_call x19, Pallas kernels, call(): pl.pallas_call(whole, name=name, out_shape=[jax.ShapeDtypeStruct(one[0],...  84.2 us
    ppermute x15, waiting for transfers between devices, swap_copy(): return lax.ppermute(value, 'copy', [(i, i ^ mask) for i in range(size)])  19.6 us
    ppermute x8, waiting for transfers between devices, swap_tok(): return lax.ppermute(value, 'tok', [(i, i ^ mask) for i in range(size)])  19.5 us
    ppermute x15, starting transfers between devices, swap_copy(): return lax.ppermute(value, 'copy', [(i, i ^ mask) for i in range(size)])  13.6 us
    ppermute x8, starting transfers between devices, swap_tok(): return lax.ppermute(value, 'tok', [(i, i ^ mask) for i in range(size)])  7.86 us
    all_to_all x1, starting transfers between devices, exchange(): return lax.all_to_all(value, ('copy', 'tok'), 0, 0)  4.86 us
    unnamed x42, local copies, waits for them, and re-layouts  4.76 us
    ppermute x1, starting transfers between devices, per_device(): moved = lax.ppermute(last[0], ('copy', 'tok'), swaps)  4.28 us
  transfers between devices with their start and end apart: 25, of which 16 were waited for; matrix products, arithmetic and copies ran while one was open for 0% of the time, Pallas kernels for 7%

profile of v7, /device:TPU:2, one launch (start us, length us, event | category | flops | bytes accessed | tf_op | source)
XLA Modules:
  0.0 164.0 jit_solution(17951347496317325951)
XLA Ops:
  0.6 0.6 pad_add_fusion.refs_0_
  1.2 57.9 %enter.1 = (bf16[128,768]{1,0:T(8,128)(2,1)}, bf16[16,128,128]{2,1,0:T(8,128)(2,1)}, bf16[3,768,384]{2,1,0:T(8,128)(2,1)}, f32[256,128]{1,0:T(8,128)}, f32[1,256...) custom-call(s32[2]{0:T(128)} %pad_add_fusion.refs_0_, bf16[128,768]{1,0:T(8,128)(2,1)} %bitcast.21, ...), custom_call_target="tpu_custom_call" | custom-call | flops 67108864 | bytes 7169224 | tf_op jit(solution)/shard_map/enter/pallas_call | solution.py:79
  59.1 0.1 collective-permute-start
  59.2 3.9 %collective-permute-done.refs_2_ = bf16[64,128]{1,0:T(8,128)(2,1)S(1)} collective-permute-done((bf16[64,128]{1,0:T(8,128)(2,1)}, bf16[64,128]{1,0:T(8,128)(2,1)S(1)}, u32[]{:S(2)}, u32[]{:S(2)}) %collective-permute-start) | collective-permute-done | bytes 16416 | tf_op jit(solution)/shard_map/ppermute | solution.py:501
  63.2 0.6 copy-done.19
  63.8 1.6 %join_tok.1 = (bf16[2,64,128]{2,1,0:T(8,128)(2,1)}, bf16[128,768]{1,0:T(8,128)(2,1)}) custom-call(bf16[128,768]{1,0:T(8,128)(2,1)} %get-tuple-element.72.refs_0_, bf16[64,128]{1,0:T(8,128)(2,1)} %get-tuple-element.73.refs_1_, bf16[64,128]{1,0:T(8,128)(2,1)} %copy-done.19), custom_call_target="tpu_custom_call" | custom-call | bytes 458752 | tf_op jit(solution)/shard_map/join_tok/pallas_call | solution.py:79
  65.4 0.1 collective-permute-start.1
  65.5 4.1 %collective-permute-start.4 = (bf16[2,64,128]{2,1,0:T(8,128)(2,1)}, bf16[2,64,128]{2,1,0:T(8,128)(2,1)S(1)}, u32[]{:S(2)}, u32[]{:S(2)}) collective-permute-start(bf16[2,64,128]{2,1,0:T(8,128)(2,1)} %get-tuple-element.79.refs_0_), channel_id=1, source_target_pairs={{0,24},{2,26},{4,28},{6,30},{8,16},{10,18},{12,20},{14,22},{16,8},... | collective-permute-start | bytes 98312 | tf_op jit(solution)/shard_map/ppermute | solution.py:496
  69.6 0.6 collective-permute-start.2
  70.2 1.6 collective-permute-done.4.refs_3_
  71.8 2.9 %collective-permute-done.3.refs_2_ = bf16[2,64,128]{2,1,0:T(8,128)(2,1)S(1)} collective-permute-done((bf16[2,64,128]{2,1,0:T(8,128)(2,1)}, bf16[2,64,128]{2,1,0:T(8,128)(2,1)S(1)}, u32[]{:S(2)}, u32[]{:S(2)}) %collective-permute-start.3) | collective-permute-done | bytes 32800 | tf_op jit(solution)/shard_map/ppermute | solution.py:496
  74.7 0.8 copy-done.14
  75.4 0.1 collective-permute-start.7
  75.5 1.6 collective-permute-start.6
  77.1 0.3 collective-permute-start.5
  77.4 1.5 copy-done.4
  78.8 0.9 copy-done.11
  79.8 1.4 project.1
  81.2 2.9 %collective-permute-done.6.refs_6_ = bf16[8,64,128]{2,1,0:T(8,128)(2,1)S(1)} collective-permute-done((bf16[8,64,128]{2,1,0:T(8,128)(2,1)S(1)}, bf16[8,64,128]{2,1,0:T(8,128)(2,1)S(1)}, u32[]{:S(2)}, u32[]{:S(2)}) %collective-permute-start.6) | collective-permute-done | bytes 131104 | tf_op jit(solution)/shard_map/ppermute | solution.py:496
  84.1 2.1 %attention.1 = (bf16[4,256,256]{2,1,0:T(8,128)(2,1)S(1)}, bf16[256,384]{1,0:T(8,128)(2,1)S(1)}, bf16[128,384]{1,0:T(8,128)(2,1)S(1)}, bf16[128,384]{1,0:T(8,128)(2,1)S(1)}) custom-call(s32[2]{0:T(128)S(1)} %copy-done.13, bf16[384,256]{1,0:T(8,128)(2,1)S(1)} %get-tuple-element.76.refs_1_, bf16[384,256]{1,0:T(8,128)(2,1)S(1)} %get-tuple-element.77.refs_2_, ...), custom_call_target="tpu_custom_call" | custom-call | flops 100663296 | bytes 2163720 | tf_op jit(solution)/shard_map/attention/pallas_call | solution.py:79
  86.3 1.6 collective-permute-start.8
  87.9 0.9 down.1
  88.8 2.3 %collective-permute-done.8.refs_6_ = bf16[128,384]{1,0:T(8,128)(2,1)S(1)} collective-permute-done((bf16[128,384]{1,0:T(8,128)(2,1)S(1)}, bf16[128,384]{1,0:T(8,128)(2,1)S(1)}, u32[]{:S(2)}, u32[]{:S(2)}) %collective-permute-start.8) | collective-permute-done | bytes 98336 | tf_op jit(solution)/shard_map/ppermute | solution.py:501
  91.1 4.3 %hidden.1 = (f32[128,768]{1,0:T(8,128)S(1)}, bf16[128,768]{1,0:T(8,128)(2,1)S(1)}, bf16[384,128]{1,0:T(8,128)(2,1)S(1)}, bf16[384,128]{1,0:T(8,128)(2,1)S(1)}) custom-call(s32[2]{0:T(128)S(1)} %copy-done.13, bf16[128,768]{1,0:T(8,128)(2,1)S(1)} %get-tuple-element.67.refs_1_.refs_0_, bf16[128,768]{1,0:T(8,128)(2,1)S(1)} %get-tuple-element.68.refs_2_, ...), custom_call_target="tpu_custom_call" | custom-call | flops 1509949440 | bytes 8064008 | tf_op jit(solution)/shard_map/hidden/pallas_call | solution.py:79
  95.4 1.6 collective-permute-start.9
  97.0 3.1 %collective-permute-done.9.refs_6_ = bf16[384,128]{1,0:T(8,128)(2,1)S(1)} collective-permute-done((bf16[384,128]{1,0:T(8,128)(2,1)S(1)}, bf16[384,128]{1,0:T(8,128)(2,1)S(1)}, u32[]{:S(2)}, u32[]{:S(2)}) %collective-permute-start.9) | collective-permute-done | bytes 98336 | tf_op jit(solution)/shard_map/ppermute | solution.py:501
  100.1 2.0 %backward.1 = (bf16[384,256]{1,0:T(8,128)(2,1)S(1)}, bf16[384,256]{1,0:T(8,128)(2,1)S(1)}, bf16[384,256]{1,0:T(8,128)(2,1)S(1)}, bf16[64,16,128]{2,1,0:T(8,128)(...) custom-call(s32[2]{0:T(128)S(1)} %copy-done.13, ...), custom_call_target="tpu_custom_call" | custom-call | flops 201326592 | bytes 2818056 | tf_op jit(solution)/shard_map/backward/pallas_call | solution.py:79
  102.2 0.4 collective-permute-start.12
  102.6 1.5 collective-permute-start.13
  104.1 2.1 %first.1 = (bf16[192,16,128]{2,1,0:T(8,128)(2,1)S(1)}, bf16[192,16,128]{2,1,0:T(8,128)(2,1)S(1)}, f32[768,128]{1,0:T(8,128)S(1)}, bf16[768,128]{1,0:T(8,128)(2,1)S(1)}) custom-call(s32[2]{0:T(128)S(1)} %copy-done.13, bf16[3,768,384]{2,1,0:T(8,128)(2,1)S(1)} %copy-done.5, bf16[256,768]{1,0:T(8,128)(2,1)S(1)} %get-tuple-element.85.refs_2_.refs_1_, ...), custom_call_target="tpu_custom_call" | custom-call | flops 754974720 | bytes 4915208 | tf_op jit(solution)/shard_map/first/pallas_call | solution.py:79
  106.2 0.1 collective-permute-start.11
  106.3 2.0 %collective-permute-done.13.refs_7_ = bf16[128,768]{1,0:T(8,128)(2,1)S(1)} collective-permute-done((bf16[128,768]{1,0:T(8,128)(2,1)S(1)}, bf16[128,768]{1,0:T(8,128)(2,1)S(1)}, u32[]{:S(2)}, u32[]{:S(2)}) %collective-permute-start.13) | collective-permute-done | bytes 196640 | tf_op jit(solution)/shard_map/ppermute | solution.py:501
  108.2 0.3 collective-permute-done.12.refs_5_
  108.6 1.4 second.1
  110.0 0.1 collective-permute-start.14
  110.1 2.2 %collective-permute-done.14.refs_4_ = bf16[176,16,128]{2,1,0:T(8,128)(2,1)S(1)} collective-permute-done((bf16[176,16,128]{2,1,0:T(8,128)(2,1)S(1)}, bf16[176,16,128]{2,1,0:T(8,128)(2,1)S(1)}, u32[]{:S(2)}, u32[]{:S(2)}) %collective-permute-start.14) | collective-permute-done | bytes 720928 | tf_op jit(solution)/shard_map/ppermute | solution.py:496
  112.3 0.9 step_0.1
  113.2 1.4 collective-permute-start.15
  114.6 1.5 collective-permute-start.10
  116.0 5.2 %collective-permute-done.10.refs_4_ = bf16[768,128]{1,0:T(8,128)(2,1)S(1)} collective-permute-done((bf16[768,128]{1,0:T(8,128)(2,1)S(1)}, bf16[768,128]{1,0:T(8,128)(2,1)S(1)}, u32[]{:S(2)}, u32[]{:S(2)}) %collective-permute-start.10) | collective-permute-done | bytes 196640 | tf_op jit(solution)/shard_map/ppermute | solution.py:501
  121.2 1.2 exit.1.refs_5_
  122.4 2.3 %collective-permute-done.16.refs_4_ = bf16[88,16,128]{2,1,0:T(8,128)(2,1)S(1)} collective-permute-done((bf16[88,16,128]{2,1,0:T(8,128)(2,1)S(1)}, bf16[88,16,128]{2,1,0:T(8,128)(2,1)S(1)}, u32[]{:S(2)}, u32[]{:S(2)}) %collective-permute-start.16) | collective-permute-done | bytes 360480 | tf_op jit(solution)/shard_map/ppermute | solution.py:496
  124.7 0.9 copy-done.8
  125.7 0.7 step_1.1
  126.4 0.3 collective-permute-start.17
  126.7 2.0 %collective-permute-start.18 = (bf16[44,16,128]{2,1,0:T(8,128)(2,1)S(1)}, bf16[44,16,128]{2,1,0:T(8,128)(2,1)S(1)}, u32[]{:S(2)}, u32[]{:S(2)}) collective-permute-start(bf16[44,16,128]{2,1,0:T(8,128)(2,1)S(1)} %get-tuple-element.110), channel_id=1, source_target_pairs={{0,16},{2,18},{4,20},{6,22},{8,24},{10,26},{12,28},{14,30},{16,0},... | collective-permute-start | bytes 540680 | tf_op jit(solution)/shard_map/ppermute | solution.py:496
  128.8 5.9 %collective-permute-done.18.refs_4_.refs_2_ = bf16[44,16,128]{2,1,0:T(8,128)(2,1)S(1)} collective-permute-done((bf16[44,16,128]{2,1,0:T(8,128)(2,1)S(1)}, bf16[44,16,128]{2,1,0:T(8,128)(2,1)S(1)}, u32[]{:S(2)}, u32[]{:S(2)}) %collective-permute-start.18) | collective-permute-done | bytes 180256 | tf_op jit(solution)/shard_map/ppermute | solution.py:496
  134.7 1.4 collective-permute-done.17.refs_2_
  136.1 0.6 step_2.1
  136.8 1.7 %collective-permute-start.19 = (bf16[24,16,128]{2,1,0:T(8,128)(2,1)S(1)}, bf16[24,16,128]{2,1,0:T(8,128)(2,1)S(1)}, u32[]{:S(2)}, u32[]{:S(2)}) collective-permute-start(bf16[24,16,128]{2,1,0:T(8,128)(2,1)S(1)} %get-tuple-element.112), channel_id=1, source_target_pairs={{0,16},{2,18},{4,20},{6,22},{8,24},{10,26},{12,28},{14,30},{16,0},... | collective-permute-start | bytes 294920 | tf_op jit(solution)/shard_map/ppermute | solution.py:496
  138.4 1.0 collective-permute-start.20
  139.4 0.6 last_bias.1
  140.0 1.6 collective-permute-start.21
  141.5 2.2 %collective-permute-done.21.refs_5_.refs_3_ = bf16[64,128]{1,0:T(8,128)(2,1)S(1)} collective-permute-done((bf16[64,128]{1,0:T(8,128)(2,1)S(1)}, bf16[64,128]{1,0:T(8,128)(2,1)S(1)}, u32[]{:S(2)}, u32[]{:S(2)}) %collective-permute-start.21) | collective-permute-done | bytes 16416 | tf_op jit(solution)/shard_map/ppermute | solution.py:501
  143.8 1.2 last.1
  145.0 1.6 pair_weight.1.refs_6_
  146.6 4.9 %all-to-all-start = ((f32[32,8,128]{2,1,0:T(8,128)}), f32[32,8,128]{2,1,0:T(8,128)S(1)}, u32[]{:S(2)}, u32[]{:S(2)}) async-start(f32[32,8,128]{2,1,0:T(8,128)} %pair_weight.1.refs_6_), calls=%async_computation | async-start | bytes 262144 | tf_op jit(solution)/shard_map/all_to_all | solution.py:505
  151.4 4.3 %collective-permute-start.22 = (bf16[3,48,384]{2,1,0:T(8,128)(2,1)S(1)}, bf16[3,48,384]{2,1,0:T(8,128)(2,1)S(1)}, u32[]{:S(2)}, u32[]{:S(2)}) collective-permute-start(bf16[3,48,384]{2,1,0:T(8,128)(2,1)S(1)} %get-tuple-element.116.refs_4_), channel_id=1, source_target_pairs={{0,0},{1,16},{2,2},{3,18},{4,4},{5,20},{6,6},{7,22},{8,8},{9,24},{... | collective-permute-start | bytes 331784 | tf_op jit(solution)/shard_map/ppermute | solution.py:773
  155.7 0.1 collective-permute-start.23
  155.8 2.9 %pair.1 = bf16[2048,128]{1,0:T(8,128)(2,1)} custom-call(s32[2]{0:T(128)S(1)} %copy-done.13, bf16[2048,128]{1,0:T(8,128)(2,1)S(1)} %bitcast.20, f32[1,128]{1,0:T(1,128)S(1)} %bitcast.32, bf16[8,128]{1,0:T(8,128)(2,1)S(1)} %bitcast.30, bf16[64,128]{1,0:T(8,128)(2,1)S(1)} %get-tuple-element.120.refs_2_.refs_4_, ...), custom_call_target="tpu_custom_call" | custom-call | flops 67108864 | bytes 1083912 | tf_op jit(solution)/shard_map/pair/pallas_call | solution.py:79
  158.7 0.7 collective-permute-done.23.refs_2_
  159.5 3.2 %collective-permute-done.22.refs_0_ = bf16[3,48,384]{2,1,0:T(8,128)(2,1)S(1)} collective-permute-done((bf16[3,48,384]{2,1,0:T(8,128)(2,1)S(1)}, bf16[3,48,384]{2,1,0:T(8,128)(2,1)S(1)}, u32[]{:S(2)}, u32[]{:S(2)}) %collective-permute-start.22) | collective-permute-done | bytes 110624 | tf_op jit(solution)/shard_map/ppermute | solution.py:773
  162.7 0.7 finish.1
  163.4 0.6 reduce_sum.9
  (51 shorter events, 0.2 us)
Async XLA Ops:
  1.2 76.1 %copy-start.13 = (s32[2]{0:T(128)S(1)}, s32[2]{0:T(128)}, u32[]{:S(2)}) copy-start(s32[2]{0:T(128)} %pad_add_fusion.refs_0_) | copy-start | bytes 28
  1.2 86.6 %copy-start.2 = (bf16[1536,768]{1,0:T(8,128)(2,1)S(1)}, bf16[1536,768]{1,0:T(8,128)(2,1)}, u32[]{:S(2)}) copy-start(bf16[1536,768]{1,0:T(8,128)(2,1)} %refs_1_.1) | copy-start | bytes 7077892
  59.1 25.0 %copy-start.12 = (f32[256,128]{1,0:T(8,128)S(1)}, f32[256,128]{1,0:T(8,128)}, u32[]{:S(2)}) copy-start(f32[256,128]{1,0:T(8,128)} %get-tuple-element.80.refs_8_) | copy-start | bytes 393220
  59.1 25.0 %copy-start.17 = (f32[1,256]{1,0:T(1,128)S(1)}, f32[1,256]{1,0:T(1,128)}, u32[]{:S(2)}) copy-start(f32[1,256]{1,0:T(1,128)} %get-tuple-element.81.refs_9_) | copy-start | bytes 3076
  59.1 4.0 %collective-permute-start = (bf16[64,128]{1,0:T(8,128)(2,1)}, bf16[64,128]{1,0:T(8,128)(2,1)S(1)}, u32[]{:S(2)}, u32[]{:S(2)}) collective-permute-start(bf16[64,128]{1,0:T(8,128)(2,1)} %get-tuple-element.74), channel_id=1, source_target_pairs={{0,1},{1,0},{2,3},{3,2},{4,5},{5,4},{6,7},{7,6},{8,9},{9,8},{10,11... | collective-permute-start | bytes 49160 | tf_op jit(solution)/shard_map/ppermute | solution.py:501
  63.2 0.6 copy-start.19
  65.4 9.2 %collective-permute-start.1 = (bf16[128,768]{1,0:T(8,128)(2,1)}, bf16[128,768]{1,0:T(8,128)(2,1)S(1)}, u32[]{:S(2)}, u32[]{:S(2)}) collective-permute-start(bf16[128,768]{1,0:T(8,128)(2,1)} %get-tuple-element.75.refs_2_), channel_id=1, source_target_pairs={{0,1},{1,0},{2,3},{3,2},{4,5},{5,4},{6,7},{7,6},{8,9},{9,8},{10,11... | collective-permute-start | bytes 589832 | tf_op jit(solution)/shard_map/ppermute | solution.py:501
  65.5 6.3 %collective-permute-start.4 = (bf16[2,64,128]{2,1,0:T(8,128)(2,1)}, bf16[2,64,128]{2,1,0:T(8,128)(2,1)S(1)}, u32[]{:S(2)}, u32[]{:S(2)}) collective-permute-start(bf16[2,64,128]{2,1,0:T(8,128)(2,1)} %get-tuple-element.79.refs_0_), channel_id=1, source_target_pairs={{0,24},{2,26},{4,28},{6,30},{8,16},{10,18},{12,20},{14,22},{16,8},... | collective-permute-start | bytes 98312 | tf_op jit(solution)/shard_map/ppermute | solution.py:496
  69.6 5.0 %collective-permute-start.3 = (bf16[2,64,128]{2,1,0:T(8,128)(2,1)}, bf16[2,64,128]{2,1,0:T(8,128)(2,1)S(1)}, u32[]{:S(2)}, u32[]{:S(2)}) collective-permute-start(bf16[2,64,128]{2,1,0:T(8,128)(2,1)} %get-tuple-element.79.refs_0_), channel_id=1, source_target_pairs={{0,16},{2,18},{4,20},{6,22},{8,24},{10,26},{12,28},{14,30},{16,0},... | collective-permute-start | bytes 98312 | tf_op jit(solution)/shard_map/ppermute | solution.py:496
  69.6 5.0 %collective-permute-start.2 = (bf16[2,64,128]{2,1,0:T(8,128)(2,1)}, bf16[2,64,128]{2,1,0:T(8,128)(2,1)S(1)}, u32[]{:S(2)}, u32[]{:S(2)}) collective-permute-start(bf16[2,64,128]{2,1,0:T(8,128)(2,1)} %get-tuple-element.79.refs_0_), channel_id=1, source_target_pairs={{0,8},{2,10},{4,12},{6,14},{8,0},{10,2},{12,4},{14,6},{16,24},{18,... | collective-permute-start | bytes 98312 | tf_op jit(solution)/shard_map/ppermute | solution.py:496
  74.7 0.8 copy-start.14
  75.4 12.4 %copy-start.20 = (f32[768]{0:T(1024)S(1)}, f32[768]{0:T(1024)}, u32[]{:S(2)}) copy-start(f32[768]{0:T(1024)} %param.29) | copy-start | bytes 9220
  75.4 12.4 %copy-start.7 = (bf16[1,128,768]{2,1,0:T(8,128)(2,1)S(1)}, bf16[1,128,768]{2,1,0:T(8,128)(2,1)}, u32[]{:S(2)}) copy-start(bf16[1,128,768]{2,1,0:T(8,128)(2,1)} %param.20) | copy-start | bytes 589828
  75.4 12.5 %copy-start.10 = (bf16[1,128,768]{2,1,0:T(8,128)(2,1)S(1)}, bf16[1,128,768]{2,1,0:T(8,128)(2,1)}, u32[]{:S(2)}) copy-start(bf16[1,128,768]{2,1,0:T(8,128)(2,1)} %param.39) | copy-start | bytes 589828
  75.4 5.8 %collective-permute-start.7 = (bf16[8,64,128]{2,1,0:T(8,128)(2,1)S(1)}, bf16[8,64,128]{2,1,0:T(8,128)(2,1)S(1)}, u32[]{:S(2)}, u32[]{:S(2)}) collective-permute-start(bf16[8,64,128]{2,1,0:T(8,128)(2,1)S(1)} %bitcast.24), channel_id=1, source_target_pairs={{0,6},{2,4},{4,2},{6,0},{8,14},{10,12},{12,10},{14,8},{16,22},{18,... | collective-permute-start | bytes 393224 | tf_op jit(solution)/shard_map/ppermute | solution.py:496
  75.5 8.6 %collective-permute-start.6 = (bf16[8,64,128]{2,1,0:T(8,128)(2,1)S(1)}, bf16[8,64,128]{2,1,0:T(8,128)(2,1)S(1)}, u32[]{:S(2)}, u32[]{:S(2)}) collective-permute-start(bf16[8,64,128]{2,1,0:T(8,128)(2,1)S(1)} %bitcast.25), channel_id=1, source_target_pairs={{0,4},{2,6},{4,0},{6,2},{8,12},{10,14},{12,8},{14,10},{16,20},{18,... | collective-permute-start | bytes 393224 | tf_op jit(solution)/shard_map/ppermute | solution.py:496
  77.1 7.0 %collective-permute-start.5 = (bf16[8,64,128]{2,1,0:T(8,128)(2,1)S(1)}, bf16[8,64,128]{2,1,0:T(8,128)(2,1)S(1)}, u32[]{:S(2)}, u32[]{:S(2)}) collective-permute-start(bf16[8,64,128]{2,1,0:T(8,128)(2,1)S(1)} %bitcast.26), channel_id=1, source_target_pairs={{0,2},{2,0},{4,6},{6,4},{8,10},{10,8},{12,14},{14,12},{16,18},{18,... | collective-permute-start | bytes 393224 | tf_op jit(solution)/shard_map/ppermute | solution.py:496
  77.4 1.5 copy-start.4
  78.8 0.9 copy-start.11
  79.8 11.3 %copy-start.1 = (bf16[768,1536]{1,0:T(8,128)(2,1)S(1)}, bf16[768,1536]{1,0:T(8,128)(2,1)}, u32[]{:S(2)}) copy-start(bf16[768,1536]{1,0:T(8,128)(2,1)} %refs_9_.1) | copy-start | bytes 7077892
  84.1 7.0 %copy-start = (bf16[768,1536]{1,0:T(8,128)(2,1)S(1)}, bf16[768,1536]{1,0:T(8,128)(2,1)}, u32[]{:S(2)}) copy-start(bf16[768,1536]{1,0:T(8,128)(2,1)} %refs_8_.1) | copy-start | bytes 7077892
  84.1 7.0 %copy-start.6 = (bf16[768,768]{1,0:T(8,128)(2,1)S(1)}, bf16[768,768]{1,0:T(8,128)(2,1)}, u32[]{:S(2)}) copy-start(bf16[768,768]{1,0:T(8,128)(2,1)} %refs_7_.1) | copy-start | bytes 3538948
  86.3 4.8 %collective-permute-start.8 = (bf16[128,384]{1,0:T(8,128)(2,1)S(1)}, bf16[128,384]{1,0:T(8,128)(2,1)S(1)}, u32[]{:S(2)}, u32[]{:S(2)}) collective-permute-start(bf16[128,384]{1,0:T(8,128)(2,1)S(1)} %get-tuple-element.83), channel_id=1, source_target_pairs={{0,1},{1,0},{2,3},{3,2},{4,5},{5,4},{6,7},{7,6},{8,9},{9,8},{10,11... | collective-permute-start | bytes 294920 | tf_op jit(solution)/shard_map/ppermute | solution.py:501
  91.1 13.0 %copy-start.5 = (bf16[3,768,384]{2,1,0:T(8,128)(2,1)S(1)}, bf16[3,768,384]{2,1,0:T(8,128)(2,1)}, u32[]{:S(2)}) copy-start(bf16[3,768,384]{2,1,0:T(8,128)(2,1)} %get-tuple-element.71.refs_1_) | copy-start | bytes 5308420
  95.4 4.7 %collective-permute-start.9 = (bf16[384,128]{1,0:T(8,128)(2,1)S(1)}, bf16[384,128]{1,0:T(8,128)(2,1)S(1)}, u32[]{:S(2)}, u32[]{:S(2)}) collective-permute-start(bf16[384,128]{1,0:T(8,128)(2,1)S(1)} %get-tuple-element.88), channel_id=1, source_target_pairs={{0,1},{1,0},{2,3},{3,2},{4,5},{5,4},{6,7},{7,6},{8,9},{9,8},{10,11... | collective-permute-start | bytes 294920 | tf_op jit(solution)/shard_map/ppermute | solution.py:501
  102.2 6.4 %collective-permute-start.12 = (bf16[64,16,128]{2,1,0:T(8,128)(2,1)S(1)}, bf16[64,16,128]{2,1,0:T(8,128)(2,1)S(1)}, u32[]{:S(2)}, u32[]{:S(2)}) collective-permute-start(bf16[64,16,128]{2,1,0:T(8,128)(2,1)S(1)} %get-tuple-element.99), channel_id=1, source_target_pairs={{0,4},{2,6},{4,0},{6,2},{8,12},{10,14},{12,8},{14,10},{16,20},{18,... | collective-permute-start | bytes 786440 | tf_op jit(solution)/shard_map/ppermute | solution.py:496
  102.6 5.7 %collective-permute-start.13 = (bf16[128,768]{1,0:T(8,128)(2,1)S(1)}, bf16[128,768]{1,0:T(8,128)(2,1)S(1)}, u32[]{:S(2)}, u32[]{:S(2)}) collective-permute-start(bf16[128,768]{1,0:T(8,128)(2,1)S(1)} %get-tuple-element.100.refs_6_), channel_id=1, source_target_pairs={{0,1},{1,0},{2,3},{3,2},{4,5},{5,4},{6,7},{7,6},{8,9},{9,8},{10,11... | collective-permute-start | bytes 589832 | tf_op jit(solution)/shard_map/ppermute | solution.py:501
  106.2 3.9 %collective-permute-start.11 = (bf16[192,16,128]{2,1,0:T(8,128)(2,1)S(1)}, bf16[192,16,128]{2,1,0:T(8,128)(2,1)S(1)}, u32[]{:S(2)}, u32[]{:S(2)}) collective-permute-start(bf16[192,16,128]{2,1,0:T(8,128)(2,1)S(1)} %get-tuple-element.96), channel_id=1, source_target_pairs={{0,2},{2,0},{4,6},{6,4},{8,10},{10,8},{12,14},{14,12},{16,18},{18,... | collective-permute-start | bytes 2359304 | tf_op jit(solution)/shard_map/ppermute | solution.py:496
  110.0 6.1 %copy-start.18 = (f32[768]{0:T(1024)S(1)}, f32[768]{0:T(1024)}, u32[]{:S(2)}) copy-start(f32[768]{0:T(1024)} %refs_5_.1) | copy-start | bytes 9220
  110.0 2.3 %collective-permute-start.14 = (bf16[176,16,128]{2,1,0:T(8,128)(2,1)S(1)}, bf16[176,16,128]{2,1,0:T(8,128)(2,1)S(1)}, u32[]{:S(2)}, u32[]{:S(2)}) collective-permute-start(bf16[176,16,128]{2,1,0:T(8,128)(2,1)S(1)} %get-tuple-element.102), channel_id=1, source_target_pairs={{0,2},{2,0},{4,6},{6,4},{8,10},{10,8},{12,14},{14,12},{16,18},{18,... | collective-permute-start | bytes 2162696 | tf_op jit(solution)/shard_map/ppermute | solution.py:496
  113.2 11.6 %collective-permute-start.15 = (bf16[96,16,128]{2,1,0:T(8,128)(2,1)S(1)}, bf16[96,16,128]{2,1,0:T(8,128)(2,1)S(1)}, u32[]{:S(2)}, u32[]{:S(2)}) collective-permute-start(bf16[96,16,128]{2,1,0:T(8,128)(2,1)S(1)} %get-tuple-element.104), channel_id=1, source_target_pairs={{0,4},{2,6},{4,0},{6,2},{8,12},{10,14},{12,8},{14,10},{16,20},{18,... | collective-permute-start | bytes 1179656 | tf_op jit(solution)/shard_map/ppermute | solution.py:496
  114.6 10.2 %collective-permute-start.16 = (bf16[88,16,128]{2,1,0:T(8,128)(2,1)S(1)}, bf16[88,16,128]{2,1,0:T(8,128)(2,1)S(1)}, u32[]{:S(2)}, u32[]{:S(2)}) collective-permute-start(bf16[88,16,128]{2,1,0:T(8,128)(2,1)S(1)} %get-tuple-element.106), channel_id=1, source_target_pairs={{0,8},{2,10},{4,12},{6,14},{8,0},{10,2},{12,4},{14,6},{16,24},{18,... | collective-permute-start | bytes 1081352 | tf_op jit(solution)/shard_map/ppermute | solution.py:496
  114.6 6.7 %collective-permute-start.10 = (bf16[768,128]{1,0:T(8,128)(2,1)S(1)}, bf16[768,128]{1,0:T(8,128)(2,1)S(1)}, u32[]{:S(2)}, u32[]{:S(2)}) collective-permute-start(bf16[768,128]{1,0:T(8,128)(2,1)S(1)} %get-tuple-element.94), channel_id=1, source_target_pairs={{0,1},{1,0},{2,3},{3,2},{4,5},{5,4},{6,7},{7,6},{8,9},{9,8},{10,11... | collective-permute-start | bytes 589832 | tf_op jit(solution)/shard_map/ppermute | solution.py:501
  121.2 23.8 %copy-start.9 = (bf16[16,128,128]{2,1,0:T(8,128)(2,1)S(1)}, bf16[16,128,128]{2,1,0:T(8,128)(2,1)}, u32[]{:S(2)}) copy-start(bf16[16,128,128]{2,1,0:T(8,128)(2,1)} %get-tuple-element.121.refs_1_) | copy-start | bytes 1572868
  124.7 0.9 copy-start.8
  125.7 30.1 %copy-start.3 = (bf16[128,16,128]{2,1,0:T(8,128)(2,1)S(1)}, bf16[128,16,128]{2,1,0:T(8,128)(2,1)}, u32[]{:S(2)}) copy-start(bf16[128,16,128]{2,1,0:T(8,128)(2,1)} %param.22) | copy-start | bytes 1572868
  125.7 30.1 %copy-start.15 = (bf16[128,8]{0,1:T(8,128)(2,1)S(1)}, bf16[128,8]{0,1:T(8,128)(2,1)}, u32[]{:S(2)}) copy-start(bf16[128,8]{0,1:T(8,128)(2,1)} %param.34) | copy-start | bytes 6148
  125.7 30.1 %copy-start.16 = (f32[128]{0:T(128)S(1)}, f32[128]{0:T(128)}, u32[]{:S(2)}) copy-start(f32[128]{0:T(128)} %param.28) | copy-start | bytes 1540
  126.4 9.7 %collective-permute-start.17 = (bf16[48,16,128]{2,1,0:T(8,128)(2,1)S(1)}, bf16[48,16,128]{2,1,0:T(8,128)(2,1)S(1)}, u32[]{:S(2)}, u32[]{:S(2)}) collective-permute-start(bf16[48,16,128]{2,1,0:T(8,128)(2,1)S(1)} %get-tuple-element.108), channel_id=1, source_target_pairs={{0,8},{2,10},{4,12},{6,14},{8,0},{10,2},{12,4},{14,6},{16,24},{18,... | collective-permute-start | bytes 589832 | tf_op jit(solution)/shard_map/ppermute | solution.py:496
  126.7 7.9 %collective-permute-start.18 = (bf16[44,16,128]{2,1,0:T(8,128)(2,1)S(1)}, bf16[44,16,128]{2,1,0:T(8,128)(2,1)S(1)}, u32[]{:S(2)}, u32[]{:S(2)}) collective-permute-start(bf16[44,16,128]{2,1,0:T(8,128)(2,1)S(1)} %get-tuple-element.110), channel_id=1, source_target_pairs={{0,16},{2,18},{4,20},{6,22},{8,24},{10,26},{12,28},{14,30},{16,0},... | collective-permute-start | bytes 540680 | tf_op jit(solution)/shard_map/ppermute | solution.py:496
  136.8 7.0 %collective-permute-start.19 = (bf16[24,16,128]{2,1,0:T(8,128)(2,1)S(1)}, bf16[24,16,128]{2,1,0:T(8,128)(2,1)S(1)}, u32[]{:S(2)}, u32[]{:S(2)}) collective-permute-start(bf16[24,16,128]{2,1,0:T(8,128)(2,1)S(1)} %get-tuple-element.112), channel_id=1, source_target_pairs={{0,16},{2,18},{4,20},{6,22},{8,24},{10,26},{12,28},{14,30},{16,0},... | collective-permute-start | bytes 294920 | tf_op jit(solution)/shard_map/ppermute | solution.py:496
  138.4 5.3 %collective-permute-start.20 = (bf16[18,16,128]{2,1,0:T(8,128)(2,1)S(1)}, bf16[18,16,128]{2,1,0:T(8,128)(2,1)S(1)}, u32[]{:S(2)}, u32[]{:S(2)}) collective-permute-start(bf16[18,16,128]{2,1,0:T(8,128)(2,1)S(1)} %get-tuple-element.114), channel_id=1, source_target_pairs={{0,4},{2,6},{4,0},{6,2},{8,12},{10,14},{12,8},{14,10},{16,20},{18,... | collective-permute-start | bytes 221192 | tf_op jit(solution)/shard_map/ppermute | solution.py:496
  140.0 3.8 %collective-permute-start.21 = (bf16[64,128]{1,0:T(8,128)(2,1)S(1)}, bf16[64,128]{1,0:T(8,128)(2,1)S(1)}, u32[]{:S(2)}, u32[]{:S(2)}) collective-permute-start(bf16[64,128]{1,0:T(8,128)(2,1)S(1)} %get-tuple-element.115), channel_id=1, source_target_pairs={{0,1},{1,0},{2,3},{3,2},{4,5},{5,4},{6,7},{7,6},{8,9},{9,8},{10,11... | collective-permute-start | bytes 49160 | tf_op jit(solution)/shard_map/ppermute | solution.py:501
  146.6 16.8 %all-to-all-start = ((f32[32,8,128]{2,1,0:T(8,128)}), f32[32,8,128]{2,1,0:T(8,128)S(1)}, u32[]{:S(2)}, u32[]{:S(2)}) async-start(f32[32,8,128]{2,1,0:T(8,128)} %pair_weight.1.refs_6_), calls=%async_computation | async-start | bytes 262144 | tf_op jit(solution)/shard_map/all_to_all | solution.py:505
  151.4 11.3 %collective-permute-start.22 = (bf16[3,48,384]{2,1,0:T(8,128)(2,1)S(1)}, bf16[3,48,384]{2,1,0:T(8,128)(2,1)S(1)}, u32[]{:S(2)}, u32[]{:S(2)}) collective-permute-start(bf16[3,48,384]{2,1,0:T(8,128)(2,1)S(1)} %get-tuple-element.116.refs_4_), channel_id=1, source_target_pairs={{0,0},{1,16},{2,2},{3,18},{4,4},{5,20},{6,6},{7,22},{8,8},{9,24},{... | collective-permute-start | bytes 331784 | tf_op jit(solution)/shard_map/ppermute | solution.py:773
  155.7 3.8 %collective-permute-start.23 = (bf16[48,128]{1,0:T(8,128)(2,1)S(1)}, bf16[48,128]{1,0:T(8,128)(2,1)S(1)}, u32[]{:S(2)}, u32[]{:S(2)}) collective-permute-start(bf16[48,128]{1,0:T(8,128)(2,1)S(1)} %get-tuple-element.118), channel_id=1, source_target_pairs={{0,1},{1,0},{2,3},{3,2},{4,5},{5,4},{6,7},{7,6},{8,9},{9,8},{10,11... | collective-permute-start | bytes 36872 | tf_op jit(solution)/shard_map/ppermute | solution.py:501

commit v8 on v7

--- a/solution.py
+++ b/solution.py
@@ -112,17 +112,8 @@
 
 def enter_kernel(toks, cols, ids, *rest):
     noisy, single, restype, table, gain, pair, pair_gain, w_pair, chain, keymask = rest[:10]
-    chain_weight, weights = rest[10], rest[11:14]
-    x_out, columns, slices, facts_out, chain_out = rest[14:19]
-    bias_outs, (rounded, bias, sem) = rest[19 : 19 + toks], rest[19 + toks :]
+    chain_weight, x_out, columns, facts_out, chain_out, bias_out, rounded, bias = rest[10:]
     t = ids[0]
-    transfers = []
-    for k in range(3):
-        transfer = pltpu.make_async_copy(
-            own_slice(weights[k], t, slices.shape[2]), slices.at[k], sem.at[k]
-        )
-        transfer.start()
-        transfers.append(transfer)
     rows = noisy.shape[0]
     pair_scaled, _, _ = layer_forward(pair[...].astype(f32), pair_gain[...])
     rounded[...] = pair_scaled.astype(bf16).astype(f32)
@@ -134,10 +125,10 @@
         columns[j] = column
         total = total + mm(jnp.where(row_col == j, spread, 0.0).astype(bf16), column, NT)
     bias[...] = total
-    part = bias_outs[0].shape[0]
+    part = bias_out.shape[1]
     for r in range(toks):
         start = pl.multiple_of(jnp.bitwise_xor(t, r) * part, part)
-        bias_outs[r][...] = bias[pl.ds(start, part), :].astype(bf16)
+        bias_out[r] = bias[pl.ds(start, part), :].astype(bf16)
     normed_scaled, _, _ = layer_forward(noisy[...].astype(f32), gain[...])
     types = table.shape[0]
     onehot = (lax.broadcasted_iota(jnp.int32, (types, rows), 0) == restype[...]).astype(f32)
@@ -156,6 +147,17 @@
         facts = jnp.where(line == 2 + h, weight_row, facts)
     facts_out[...] = jnp.transpose(facts)
     chain_out[...] = chain_row.astype(f32)
+
+
+def stage_kernel(ids, *rest):
+    weights, (slices, sem) = rest[:3], rest[3:]
+    transfers = []
+    for k in range(3):
+        transfer = pltpu.make_async_copy(
+            own_slice(weights[k], ids[0], slices.shape[2]), slices.at[k], sem.at[k]
+        )
+        transfer.start()
+        transfers.append(transfer)
     for transfer in transfers:
         transfer.wait()
 
@@ -173,14 +175,15 @@
         outs[k][...] = jnp.transpose(mm(x, slices[k])).astype(bf16)
 
 
+def split_kernel(count, *refs):
+    for n in range(count):
+        for r, out in enumerate(refs[count:]):
+            out[n] = refs[n][r]
+
+
 def join_kernel(*refs):
     for n, ref in enumerate(refs[:-1]):
         refs[-1][n] = ref[...]
-
-
-def join_tok_kernel(x, *refs):
-    refs[-1][...] = x[...]
-    join_kernel(*refs[:-1])
 
 
 def attention_kernel(copies, toks, near, cols, head_width, ids, query, key, value, *rest):
@@ -191,7 +194,7 @@
         for rz in range(copies // near):
             c = jnp.bitwise_xor(high, rz) * near + jnp.bitwise_xor(low, m)
             for r in range(toks):
-                bias[c, jnp.bitwise_xor(t, r)] = biases[m][rz * toks + r]
+                bias[c, jnp.bitwise_xor(t, r)] = biases[m][r, rz]
     own_heads = weights_out.shape[0]
     tokens = query.shape[1]
     rows = tokens // toks
@@ -443,7 +446,8 @@
 
 
 def exit_kernel(toks, noisy, gain, d_res, d_own, *rest):
-    others, (grad_noisy,) = rest[: toks - 1], rest[toks - 1 :]
+    others, (grad_noisy, token) = rest[: toks - 1], rest[toks - 1 :]
+    token[...] = jnp.zeros(token.shape, f32)
     total = d_own[...]
     for part in others:
         total = total + part[...].astype(f32)
@@ -559,38 +563,38 @@
         "enter",
         [where_am_i]
         + [(array, "fetch") for array in small]
-        + [(chain_weight, SMEM)]
-        + [(w, ANY) for w in weights3],
+        + [(chain_weight, SMEM)],
         [((rows, width), bf16), ((cols, rows, channels), bf16)]
-        + [((3, width, own_width), bf16, ANY), ((tokens, 128), f32), ((1, tokens), f32)]
-        + [((own_heads * cols, rows), bf16)] * toks,
-        [VMEM((rows * cols, channels), f32), VMEM((heads * cols, rows), f32)]
-        + [pltpu.SemaphoreType.DMA((3,))],
+        + [((tokens, 128), f32), ((1, tokens), f32), ((toks, own_heads * cols, rows), bf16)],
+        [VMEM((rows * cols, channels), f32), VMEM((heads * cols, rows), f32)],
         flops=2 * heads * cols * rows * channels * cols,
         limit=60,
     )
-    x_own, columns, slices, facts, chain_row = entered[:5]
-    bias_parts = entered[5:]
+    x_own, columns, facts, chain_row, bias_mine = entered
     near = 4
     far = copies // near
-    part_shape = bias_parts[0].shape
-    bias_tok = [bias_parts[0]] + [swap_tok(bias_parts[r], r) for r in range(1, toks)]
-    mine, x_own = call(
-        join_tok_kernel,
-        "join_tok",
-        [(array, "fetch") for array in [x_own] + bias_tok],
-        [((toks,) + part_shape, bf16), ((rows, width), bf16)],
-        limit=60,
-    )
     x_parts = [x_own] + [swap_tok(x_own, r) for r in range(1, toks)]
+    (slices,) = call(
+        stage_kernel,
+        "stage",
+        [where_am_i] + [(w, ANY) for w in weights3],
+        [((3, width, own_width), bf16)],
+        [pltpu.SemaphoreType.DMA((3,))],
+        deps=[chain_row],
+    )
+    by_tok = call(
+        functools.partial(split_kernel, far),
+        "split_far",
+        [bias_mine] + [swap_copy(bias_mine, m * near) for m in range(1, far)],
+        [((far, own_heads * cols, rows), bf16)] * toks,
+        deps=[slices] + x_parts[1:],
+    )
     (lines,) = call(
         join_kernel,
-        "join_far",
-        [mine] + [swap_copy(mine, m * near) for m in range(1, far)],
-        [((far, toks) + part_shape, bf16)],
-        deps=x_parts[1:],
-    )
-    lines = lines.reshape((far * toks,) + lines.shape[2:])
+        "join_tok",
+        [by_tok[0]] + [swap_tok(by_tok[r], r) for r in range(1, toks)],
+        [((toks, far, own_heads * cols, rows), bf16)],
+    )
     biases = [lines] + [swap_copy(lines, m) for m in range(1, near)]
     x, query, key, value = call(
         functools.partial(project_kernel, toks),
@@ -705,11 +709,11 @@
     )
     got_b = swap_copy(sent_b, 1)
 
-    (grad_noisy,) = call(
+    grad_noisy, exited = call(
         functools.partial(exit_kernel, toks),
         "exit",
         [noisy3, norm_gain2, d_res, d_own] + d_others,
-        [((rows, width), bf16)],
+        [((rows, width), bf16), ((8, 128), f32)],
     )
     pairs = [(kept, got), (kept_b, got_b)]
     parts = copies // 2
@@ -723,7 +727,7 @@
             segments.append((1, bias_base, parts // 2, bias_tiles, mask_b, masks_b[n:-1], 1))
         else:
             bias_ready = pairs[1]
-        pairs = step("step_%d" % n, pairs, segments, deps=[grad_noisy] if n == 1 else ())
+        pairs = step("step_%d" % n, pairs, segments, deps=[exited] if n == 1 else ())
         parts //= 2
     bias_pieces = call(
         functools.partial(last_bias_kernel, toks, bias_base, bias_tiles, cols),
@@ -741,14 +745,6 @@
         for t in range(toks):
             swaps.append((c * toks + t, (t * group + c % group) * toks + c // group))
 
-    last = call(
-        functools.partial(last_kernel, toks),
-        "last",
-        [where_am_i, *pairs[0], *pairs[1]],
-        [((3, cut, own_width), bf16), ((cut, own_width), f32)] + [((cut, rows), bf16)] * toks,
-        [VMEM((toks, cut, rows), f32)],
-        deps=bias_pieces[1:],
-    )
     (weight_grad,) = call(
         functools.partial(pair_weight_kernel, toks),
         "pair_weight",
@@ -756,7 +752,14 @@
         [((devices, heads, channels), f32)],
         [VMEM((heads * cols, rows), f32)],
         flops=2 * heads * cols * rows * channels * cols,
-        deps=[last[0]],
+    )
+    last = call(
+        functools.partial(last_kernel, toks),
+        "last",
+        [where_am_i, *pairs[0], *pairs[1]],
+        [((3, cut, own_width), bf16), ((cut, own_width), f32)] + [((cut, rows), bf16)] * toks,
+        [VMEM((toks, cut, rows), f32)],
+        deps=[weight_grad],
     )
     (grad_pair,) = call(
         functools.partial(pair_kernel, toks, cols),
@@ -765,7 +768,7 @@
         [((rows * cols, channels), bf16)],
         [VMEM((rows * cols, channels), f32), VMEM((heads * cols, rows), f32)],
         flops=2 * heads * cols * rows * channels * cols,
-        deps=[weight_grad],
+        deps=[last[0]],
     )
     weight_grad = jnp.sum(exchange(weight_grad), axis=0)
     grad_out, singles = last[1], last[2:]

time: 164 us -> 116 us (0.71)
  Pallas kernels: 84.2 us -> 29.6 us
  starting transfers between devices: 30.6 us -> 37.4 us
    pallas_call x19 -> x20, Pallas kernels: 84.2 us -> 29.6 us  [call(): pl.pallas_call(whole, name=name, out_shape=[jax.ShapeDtypeStruct(one[0],...]
    ppermute x15, starting transfers between devices: 13.6 us -> 18.5 us  [swap_copy(): return lax.ppermute(value, 'copy', [(i, i ^ mask) for i in range(size)])]
    ppermute x8, starting transfers between devices: 7.86 us -> 10.2 us  [swap_tok(): return lax.ppermute(value, 'tok', [(i, i ^ mask) for i in range(size)])]
    ppermute x1, starting transfers between devices: 4.28 us -> 1.91 us  [per_device(): moved = lax.ppermute(last[0], ('copy', 'tok'), swaps)]
    ppermute x8, waiting for transfers between devices: 19.5 us -> 17.2 us  [swap_tok(): return lax.ppermute(value, 'tok', [(i, i ^ mask) for i in range(size)])]
    all_to_all x1, starting transfers between devices: 4.86 us -> 6.71 us  [exchange(): return lax.all_to_all(value, ('copy', 'tok'), 0, 0)]
    unnamed x42 -> x44, local copies, waits for them, and re-layouts: 4.76 us -> 5.23 us
  transfers between devices with their start and end apart: 25 -> 25, of which waited for: 16 -> 17; matrix products, arithmetic and copies ran while one was open for 0% -> 0% of each run, Pallas kernels for 7% -> 11%
where the time goes in v8:
time: 116 us
  waiting for transfers between devices  41.3 us (36%)
  starting transfers between devices  37.4 us (32%)
  Pallas kernels  29.6 us (26%)
  local copies, waits for them, and re-layouts  5.23 us (5%)
  other arithmetic  1.21 us (1%)
    pallas_call x20, Pallas kernels, call(): pl.pallas_call(whole, name=name, out_shape=[jax.ShapeDtypeStruct(one[0],...  29.6 us
    ppermute x15, waiting for transfers between devices, swap_copy(): return lax.ppermute(value, 'copy', [(i, i ^ mask) for i in range(size)])  20.9 us
    ppermute x15, starting transfers between devices, swap_copy(): return lax.ppermute(value, 'copy', [(i, i ^ mask) for i in range(size)])  18.5 us
    ppermute x8, waiting for transfers between devices, swap_tok(): return lax.ppermute(value, 'tok', [(i, i ^ mask) for i in range(size)])  17.2 us
    ppermute x8, starting transfers between devices, swap_tok(): return lax.ppermute(value, 'tok', [(i, i ^ mask) for i in range(size)])  10.2 us
    all_to_all x1, starting transfers between devices, exchange(): return lax.all_to_all(value, ('copy', 'tok'), 0, 0)  6.71 us
    unnamed x44, local copies, waits for them, and re-layouts  5.23 us
    ppermute x1, waiting for transfers between devices, per_device(): moved = lax.ppermute(last[0], ('copy', 'tok'), swaps)  3.31 us
  transfers between devices with their start and end apart: 25, of which 17 were waited for; matrix products, arithmetic and copies ran while one was open for 0% of the time, Pallas kernels for 11%

profile of v8, /device:TPU:2, one launch (start us, length us, event | category | flops | bytes accessed | tf_op | source)
XLA Modules:
  0.0 115.8 jit_solution(18321785704735453233)
XLA Ops:
  0.6 0.6 pad_add_fusion.refs_0_
  1.2 4.2 %enter.1 = (bf16[128,768]{1,0:T(8,128)(2,1)}, bf16[16,128,128]{2,1,0:T(8,128)(2,1)}, f32[256,128]{1,0:T(8,128)}, f32[1,256]{1,0:T(1,128)}, bf16[2,64,128]{2,1,0:T(8,128)(2,1)}) custom-call(s32[2]{0:T(128)} %pad_add_fusion.refs_0_, bf16[128,768]{1,0:T(8,128)(2,1)} %bitcast.20, bf16[128,768]{1,0:T(8,128)(2,1)} %refs_2_.2, s32[1,128]{1,0:T(1,128)} %bitcast.31, ...), custom_call_target="tpu_custom_call" | custom-call | flops 67108864 | bytes 1860808 | tf_op jit(solution)/shard_map/enter/pallas_call | solution.py:79
  5.5 4.1 %collective-permute-start.3 = (bf16[2,64,128]{2,1,0:T(8,128)(2,1)}, bf16[2,64,128]{2,1,0:T(8,128)(2,1)S(1)}, u32[]{:S(2)}, u32[]{:S(2)}) collective-permute-start(bf16[2,64,128]{2,1,0:T(8,128)(2,1)} %get-tuple-element.76.refs_0_), channel_id=1, source_target_pairs={{0,24},{2,26},{4,28},{6,30},{8,16},{10,18},{12,20},{14,22},{16,8},... | collective-permute-start | bytes 98312 | tf_op jit(solution)/shard_map/ppermute | solution.py:500
  9.6 0.6 collective-permute-start.1
  10.2 1.3 %copy-done.4 = bf16[768,768]{1,0:T(8,128)(2,1)S(1)} copy-done((bf16[768,768]{1,0:T(8,128)(2,1)S(1)}, bf16[768,768]{1,0:T(8,128)(2,1)}, u32[]{:S(2)}) %copy-start.4) | copy-done | bytes 1179672
  11.4 1.3 %copy-done.5 = bf16[768,768]{1,0:T(8,128)(2,1)S(1)} copy-done((bf16[768,768]{1,0:T(8,128)(2,1)S(1)}, bf16[768,768]{1,0:T(8,128)(2,1)}, u32[]{:S(2)}) %copy-start.5) | copy-done | bytes 1179672
  12.7 1.3 %copy-done.6 = bf16[768,768]{1,0:T(8,128)(2,1)S(1)} copy-done((bf16[768,768]{1,0:T(8,128)(2,1)S(1)}, bf16[768,768]{1,0:T(8,128)(2,1)}, u32[]{:S(2)}) %copy-start.6) | copy-done | bytes 1179672
  14.0 0.7 copy-done.13
  14.6 0.7 copy-done.17
  15.3 0.8 stage.1.refs_1_.refs_4_
  16.2 1.8 %collective-permute-start.4 = (bf16[4,64,128]{2,1,0:T(8,128)(2,1)S(1)}, bf16[4,64,128]{2,1,0:T(8,128)(2,1)S(1)}, u32[]{:S(2)}, u32[]{:S(2)}) collective-permute-start(bf16[4,64,128]{2,1,0:T(8,128)(2,1)S(1)} %get-tuple-element.78), channel_id=1, source_target_pairs={{0,1},{1,0},{2,3},{3,2},{4,5},{5,4},{6,7},{7,6},{8,9},{9,8},{10,11... | collective-permute-start | bytes 196616 | tf_op jit(solution)/shard_map/ppermute | solution.py:505
  18.0 2.6 %collective-permute-done.4.refs_1_ = bf16[4,64,128]{2,1,0:T(8,128)(2,1)S(1)} collective-permute-done((bf16[4,64,128]{2,1,0:T(8,128)(2,1)S(1)}, bf16[4,64,128]{2,1,0:T(8,128)(2,1)S(1)}, u32[]{:S(2)}, u32[]{:S(2)}) %collective-permute-start.4) | collective-permute-done | bytes 65568 | tf_op jit(solution)/shard_map/ppermute | solution.py:505
  20.6 0.1 collective-permute-start.7
  20.7 1.8 %collective-permute-start.6 = (bf16[2,4,64,128]{3,2,1,0:T(8,128)(2,1)S(1)}, bf16[2,4,64,128]{3,2,1,0:T(8,128)(2,1)S(1)}, u32[]{:S(2)}, u32[]{:S(2)}) collective-permute-start(bf16[2,4,64,128]{3,2,1,0:T(8,128)(2,1)S(1)} %join_tok.1.refs_4_), channel_id=1, source_target_pairs={{0,4},{2,6},{4,0},{6,2},{8,12},{10,14},{12,8},{14,10},{16,20},{18,... | collective-permute-start | bytes 393224 | tf_op jit(solution)/shard_map/ppermute | solution.py:500
  22.5 1.4 %project.1 = (bf16[256,768]{1,0:T(8,128)(2,1)S(1)}, bf16[384,256]{1,0:T(8,128)(2,1)S(1)}, bf16[384,256]{1,0:T(8,128)(2,1)S(1)}, bf16[384,256]{1,0:T(8,128)(2,1)S(1)}) custom-call(s32[2]{0:T(128)S(1)} %copy-done.14, bf16[3,768,384]{2,1,0:T(8,128)(2,1)S(1)} %stage.1.refs_1_.refs_4_, bf16[128,768]{1,0:T(8,128)(2,1)S(1)} %copy-done.11, ...), custom_call_target="tpu_custom_call" | custom-call | flops 452984832 | bytes 3145736 | tf_op jit(solution)/shard_map/project/pallas_call | solution.py:79
  23.9 2.2 %collective-permute-done.7.refs_7_ = bf16[2,4,64,128]{3,2,1,0:T(8,128)(2,1)S(1)} collective-permute-done((bf16[2,4,64,128]{3,2,1,0:T(8,128)(2,1)S(1)}, bf16[2,4,64,128]{3,2,1,0:T(8,128)(2,1)S(1)}, u32[]{:S(2)}, u32[]{:S(2)}) %collective-permute-start.7) | collective-permute-done | bytes 131104 | tf_op jit(solution)/shard_map/ppermute | solution.py:500
  26.1 3.1 %collective-permute-done.6.refs_6_ = bf16[2,4,64,128]{3,2,1,0:T(8,128)(2,1)S(1)} collective-permute-done((bf16[2,4,64,128]{3,2,1,0:T(8,128)(2,1)S(1)}, bf16[2,4,64,128]{3,2,1,0:T(8,128)(2,1)S(1)}, u32[]{:S(2)}, u32[]{:S(2)}) %collective-permute-start.6) | collective-permute-done | bytes 131104 | tf_op jit(solution)/shard_map/ppermute | solution.py:500
  29.3 2.1 %attention.1 = (bf16[4,256,256]{2,1,0:T(8,128)(2,1)S(1)}, bf16[256,384]{1,0:T(8,128)(2,1)S(1)}, bf16[128,384]{1,0:T(8,128)(2,1)S(1)}, bf16[128,384]{1,0:T(8,128)(2,1)S(1)}) custom-call(s32[2]{0:T(128)S(1)} %copy-done.14, bf16[384,256]{1,0:T(8,128)(2,1)S(1)} %get-tuple-element.73.refs_1_, bf16[384,256]{1,0:T(8,128)(2,1)S(1)} %get-tuple-element.74.refs_2_, ...), custom_call_target="tpu_custom_call" | custom-call | flops 100663296 | bytes 2163720 | tf_op jit(solution)/shard_map/attention/pallas_call | solution.py:79
  31.4 1.8 %collective-permute-start.8 = (bf16[128,384]{1,0:T(8,128)(2,1)S(1)}, bf16[128,384]{1,0:T(8,128)(2,1)S(1)}, u32[]{:S(2)}, u32[]{:S(2)}) collective-permute-start(bf16[128,384]{1,0:T(8,128)(2,1)S(1)} %get-tuple-element.81), channel_id=1, source_target_pairs={{0,1},{1,0},{2,3},{3,2},{4,5},{5,4},{6,7},{7,6},{8,9},{9,8},{10,11... | collective-permute-start | bytes 294920 | tf_op jit(solution)/shard_map/ppermute | solution.py:505
  33.2 0.9 down.1
  34.1 2.1 %collective-permute-done.8.refs_6_ = bf16[128,384]{1,0:T(8,128)(2,1)S(1)} collective-permute-done((bf16[128,384]{1,0:T(8,128)(2,1)S(1)}, bf16[128,384]{1,0:T(8,128)(2,1)S(1)}, u32[]{:S(2)}, u32[]{:S(2)}) %collective-permute-start.8) | collective-permute-done | bytes 98336 | tf_op jit(solution)/shard_map/ppermute | solution.py:505
  36.2 4.3 %hidden.1 = (f32[128,768]{1,0:T(8,128)S(1)}, bf16[128,768]{1,0:T(8,128)(2,1)S(1)}, bf16[384,128]{1,0:T(8,128)(2,1)S(1)}, bf16[384,128]{1,0:T(8,128)(2,1)S(1)}) custom-call(s32[2]{0:T(128)S(1)} %copy-done.14, bf16[128,768]{1,0:T(8,128)(2,1)S(1)} %get-tuple-element.67.refs_1_.refs_0_, bf16[128,768]{1,0:T(8,128)(2,1)S(1)} %get-tuple-element.68.refs_2_, ...), custom_call_target="tpu_custom_call" | custom-call | flops 1509949440 | bytes 8064008 | tf_op jit(solution)/shard_map/hidden/pallas_call | solution.py:79
  40.5 1.8 %collective-permute-start.9 = (bf16[384,128]{1,0:T(8,128)(2,1)S(1)}, bf16[384,128]{1,0:T(8,128)(2,1)S(1)}, u32[]{:S(2)}, u32[]{:S(2)}) collective-permute-start(bf16[384,128]{1,0:T(8,128)(2,1)S(1)} %get-tuple-element.86), channel_id=1, source_target_pairs={{0,1},{1,0},{2,3},{3,2},{4,5},{5,4},{6,7},{7,6},{8,9},{9,8},{10,11... | collective-permute-start | bytes 294920 | tf_op jit(solution)/shard_map/ppermute | solution.py:505
  42.3 2.9 %collective-permute-done.9.refs_6_ = bf16[384,128]{1,0:T(8,128)(2,1)S(1)} collective-permute-done((bf16[384,128]{1,0:T(8,128)(2,1)S(1)}, bf16[384,128]{1,0:T(8,128)(2,1)S(1)}, u32[]{:S(2)}, u32[]{:S(2)}) %collective-permute-start.9) | collective-permute-done | bytes 98336 | tf_op jit(solution)/shard_map/ppermute | solution.py:505
  45.2 2.0 %backward.1 = (bf16[384,256]{1,0:T(8,128)(2,1)S(1)}, bf16[384,256]{1,0:T(8,128)(2,1)S(1)}, bf16[384,256]{1,0:T(8,128)(2,1)S(1)}, bf16[64,16,128]{2,1,0:T(8,128)(...) custom-call(s32[2]{0:T(128)S(1)} %copy-done.14, ...), custom_call_target="tpu_custom_call" | custom-call | flops 201326592 | bytes 2818056 | tf_op jit(solution)/shard_map/backward/pallas_call | solution.py:79
  47.3 0.6 collective-permute-start.12
  47.8 1.6 %collective-permute-start.13 = (bf16[128,768]{1,0:T(8,128)(2,1)S(1)}, bf16[128,768]{1,0:T(8,128)(2,1)S(1)}, u32[]{:S(2)}, u32[]{:S(2)}) collective-permute-start(bf16[128,768]{1,0:T(8,128)(2,1)S(1)} %get-tuple-element.99.refs_6_), channel_id=1, source_target_pairs={{0,1},{1,0},{2,3},{3,2},{4,5},{5,4},{6,7},{7,6},{8,9},{9,8},{10,11... | collective-permute-start | bytes 589832 | tf_op jit(solution)/shard_map/ppermute | solution.py:505
  49.4 2.1 %first.1 = (bf16[192,16,128]{2,1,0:T(8,128)(2,1)S(1)}, bf16[192,16,128]{2,1,0:T(8,128)(2,1)S(1)}, f32[768,128]{1,0:T(8,128)S(1)}, bf16[768,128]{1,0:T(8,128)(2,1)S(1)}) custom-call(s32[2]{0:T(128)S(1)} %copy-done.14, bf16[3,768,384]{2,1,0:T(8,128)(2,1)S(1)} %stage.1.refs_1_.refs_4_, bf16[256,768]{1,0:T(8,128)(2,1)S(1)} %get-tuple-element.83.refs_2_.refs_1_, ...), custom_call_target="tpu_custom_call" | custom-call | flops 754974720 | bytes 4915208 | tf_op jit(solution)/shard_map/first/pallas_call | solution.py:79
  51.5 0.1 collective-permute-start.11
  51.6 1.9 %collective-permute-done.13.refs_7_ = bf16[128,768]{1,0:T(8,128)(2,1)S(1)} collective-permute-done((bf16[128,768]{1,0:T(8,128)(2,1)S(1)}, bf16[128,768]{1,0:T(8,128)(2,1)S(1)}, u32[]{:S(2)}, u32[]{:S(2)}) %collective-permute-start.13) | collective-permute-done | bytes 196640 | tf_op jit(solution)/shard_map/ppermute | solution.py:505
  53.5 0.2 collective-permute-done.12.refs_5_
  53.7 1.4 %second.1 = (bf16[176,16,128]{2,1,0:T(8,128)(2,1)S(1)}, bf16[176,16,128]{2,1,0:T(8,128)(2,1)S(1)}) custom-call(s32[2]{0:T(128)S(1)} %copy-done.14, bf16[256,768]{1,0:T(8,128)(2,1)S(1)} %get-tuple-element.83.refs_2_.refs_1_, bf16[256,384]{1,0:T(8,128)(2,1)S(1)} %get-tuple-element.96.refs_2_, bf16[384,256]{1,0:T(8,128)(2,1)S(1)} %get-tuple-element.90.refs_5_.refs_3_, ...), custom_call_target="tpu_custom_call" | custom-call | flops 301989888 | bytes 3145736 | tf_op jit(solution)/shard_map/second/pallas_call | solution.py:79
  55.1 0.1 collective-permute-start.14
  55.2 2.2 %collective-permute-done.14.refs_4_ = bf16[176,16,128]{2,1,0:T(8,128)(2,1)S(1)} collective-permute-done((bf16[176,16,128]{2,1,0:T(8,128)(2,1)S(1)}, bf16[176,16,128]{2,1,0:T(8,128)(2,1)S(1)}, u32[]{:S(2)}, u32[]{:S(2)}) %collective-permute-start.14) | collective-permute-done | bytes 720928 | tf_op jit(solution)/shard_map/ppermute | solution.py:500
  57.4 0.9 step_0.1
  58.3 1.6 %collective-permute-start.15 = (bf16[96,16,128]{2,1,0:T(8,128)(2,1)S(1)}, bf16[96,16,128]{2,1,0:T(8,128)(2,1)S(1)}, u32[]{:S(2)}, u32[]{:S(2)}) collective-permute-start(bf16[96,16,128]{2,1,0:T(8,128)(2,1)S(1)} %get-tuple-element.103), channel_id=1, source_target_pairs={{0,4},{2,6},{4,0},{6,2},{8,12},{10,14},{12,8},{14,10},{16,20},{18,... | collective-permute-start | bytes 1179656 | tf_op jit(solution)/shard_map/ppermute | solution.py:500
  59.8 1.3 %collective-permute-start.16 = (bf16[88,16,128]{2,1,0:T(8,128)(2,1)S(1)}, bf16[88,16,128]{2,1,0:T(8,128)(2,1)S(1)}, u32[]{:S(2)}, u32[]{:S(2)}) collective-permute-start(bf16[88,16,128]{2,1,0:T(8,128)(2,1)S(1)} %get-tuple-element.105), channel_id=1, source_target_pairs={{0,8},{2,10},{4,12},{6,14},{8,0},{10,2},{12,4},{14,6},{16,24},{18,... | collective-permute-start | bytes 1081352 | tf_op jit(solution)/shard_map/ppermute | solution.py:500
  61.2 1.5 %collective-permute-start.10 = (bf16[768,128]{1,0:T(8,128)(2,1)S(1)}, bf16[768,128]{1,0:T(8,128)(2,1)S(1)}, u32[]{:S(2)}, u32[]{:S(2)}) collective-permute-start(bf16[768,128]{1,0:T(8,128)(2,1)S(1)} %get-tuple-element.92), channel_id=1, source_target_pairs={{0,1},{1,0},{2,3},{3,2},{4,5},{5,4},{6,7},{7,6},{8,9},{9,8},{10,11... | collective-permute-start | bytes 589832 | tf_op jit(solution)/shard_map/ppermute | solution.py:505
  62.6 4.9 %collective-permute-done.10.refs_4_ = bf16[768,128]{1,0:T(8,128)(2,1)S(1)} collective-permute-done((bf16[768,128]{1,0:T(8,128)(2,1)S(1)}, bf16[768,128]{1,0:T(8,128)(2,1)S(1)}, u32[]{:S(2)}, u32[]{:S(2)}) %collective-permute-start.10) | collective-permute-done | bytes 196640 | tf_op jit(solution)/shard_map/ppermute | solution.py:505
  67.5 1.2 %exit.1 = (bf16[128,768]{1,0:T(8,128)(2,1)}, f32[8,128]{1,0:T(8,128)S(1)}) custom-call(bf16[128,768]{1,0:T(8,128)(2,1)S(1)} %get-tuple-element.67.refs_1_.refs_0_, f32[1,768]{1,0:T(1,128)S(1)} %reshape.49.refs_1_, f32[128,768]{1,0:T(8,128)S(1)} %get-tuple-element.82.refs_2_, f32[768,128]{1,0:T(8,128)S(1)} %get-tuple-element.91.refs_3_, ...), custom_call_target="tpu_custom_call" | custom-call | bytes 1383424 | tf_op jit(solution)/shard_map/exit/pallas_call | solution.py:79
  68.7 1.2 %collective-permute-done.16.refs_4_ = bf16[88,16,128]{2,1,0:T(8,128)(2,1)S(1)} collective-permute-done((bf16[88,16,128]{2,1,0:T(8,128)(2,1)S(1)}, bf16[88,16,128]{2,1,0:T(8,128)(2,1)S(1)}, u32[]{:S(2)}, u32[]{:S(2)}) %collective-permute-start.16) | collective-permute-done | bytes 360480 | tf_op jit(solution)/shard_map/ppermute | solution.py:500
  70.0 0.7 step_1.1
  70.7 1.4 %collective-permute-start.17 = (bf16[48,16,128]{2,1,0:T(8,128)(2,1)S(1)}, bf16[48,16,128]{2,1,0:T(8,128)(2,1)S(1)}, u32[]{:S(2)}, u32[]{:S(2)}) collective-permute-start(bf16[48,16,128]{2,1,0:T(8,128)(2,1)S(1)} %get-tuple-element.108), channel_id=1, source_target_pairs={{0,8},{2,10},{4,12},{6,14},{8,0},{10,2},{12,4},{14,6},{16,24},{18,... | collective-permute-start | bytes 589832 | tf_op jit(solution)/shard_map/ppermute | solution.py:500
  72.2 2.9 %collective-permute-start.18 = (bf16[44,16,128]{2,1,0:T(8,128)(2,1)S(1)}, bf16[44,16,128]{2,1,0:T(8,128)(2,1)S(1)}, u32[]{:S(2)}, u32[]{:S(2)}) collective-permute-start(bf16[44,16,128]{2,1,0:T(8,128)(2,1)S(1)} %get-tuple-element.110), channel_id=1, source_target_pairs={{0,16},{2,18},{4,20},{6,22},{8,24},{10,26},{12,28},{14,30},{16,0},... | collective-permute-start | bytes 540680 | tf_op jit(solution)/shard_map/ppermute | solution.py:500
  75.1 4.9 %collective-permute-done.18.refs_4_.refs_2_ = bf16[44,16,128]{2,1,0:T(8,128)(2,1)S(1)} collective-permute-done((bf16[44,16,128]{2,1,0:T(8,128)(2,1)S(1)}, bf16[44,16,128]{2,1,0:T(8,128)(2,1)S(1)}, u32[]{:S(2)}, u32[]{:S(2)}) %collective-permute-start.18) | collective-permute-done | bytes 180256 | tf_op jit(solution)/shard_map/ppermute | solution.py:500
  79.9 0.5 collective-permute-done.17.refs_2_
  80.5 0.6 step_2.1
  81.1 0.6 last_bias.1
  81.7 1.6 %collective-permute-start.21 = (bf16[64,128]{1,0:T(8,128)(2,1)S(1)}, bf16[64,128]{1,0:T(8,128)(2,1)S(1)}, u32[]{:S(2)}, u32[]{:S(2)}) collective-permute-start(bf16[64,128]{1,0:T(8,128)(2,1)S(1)} %get-tuple-element.117), channel_id=1, source_target_pairs={{0,1},{1,0},{2,3},{3,2},{4,5},{5,4},{6,7},{7,6},{8,9},{9,8},{10,11... | collective-permute-start | bytes 49160 | tf_op jit(solution)/shard_map/ppermute | solution.py:505
  83.3 2.2 %collective-permute-done.21.refs_3_.refs_5_ = bf16[64,128]{1,0:T(8,128)(2,1)S(1)} collective-permute-done((bf16[64,128]{1,0:T(8,128)(2,1)S(1)}, bf16[64,128]{1,0:T(8,128)(2,1)S(1)}, u32[]{:S(2)}, u32[]{:S(2)}) %collective-permute-start.21) | collective-permute-done | bytes 16416 | tf_op jit(solution)/shard_map/ppermute | solution.py:505
  85.5 1.6 %pair_weight.1.refs_5_ = f32[32,8,128]{2,1,0:T(8,128)} custom-call(s32[2]{0:T(128)S(1)} %copy-done.14, bf16[16,128,128]{2,1,0:T(8,128)(2,1)S(1)} %copy-done.9, bf16[64,128]{1,0:T(8,128)(2,1)S(1)} %get-tuple-element.116.refs_2_.refs_4_, bf16[64,128]{1,0:T(8,128)(2,1)S(1)} %collective-permute-done.21.refs_3_.refs_5_), custom_call_target="tpu_custom_call" | custom-call | flops 67108864 | bytes 688136 | tf_op jit(solution)/shard_map/pair_weight/pallas_call | solution.py:79
  87.0 6.7 %all-to-all-start = ((f32[32,8,128]{2,1,0:T(8,128)}), f32[32,8,128]{2,1,0:T(8,128)S(1)}, u32[]{:S(2)}, u32[]{:S(2)}) async-start(f32[32,8,128]{2,1,0:T(8,128)} %pair_weight.1.refs_5_), calls=%async_computation | async-start | bytes 262144 | tf_op jit(solution)/shard_map/all_to_all | solution.py:509
  93.7 2.4 %collective-permute-start.19 = (bf16[24,16,128]{2,1,0:T(8,128)(2,1)S(1)}, bf16[24,16,128]{2,1,0:T(8,128)(2,1)S(1)}, u32[]{:S(2)}, u32[]{:S(2)}) collective-permute-start(bf16[24,16,128]{2,1,0:T(8,128)(2,1)S(1)} %get-tuple-element.112), channel_id=1, source_target_pairs={{0,16},{2,18},{4,20},{6,22},{8,24},{10,26},{12,28},{14,30},{16,0},... | collective-permute-start | bytes 294920 | tf_op jit(solution)/shard_map/ppermute | solution.py:500
  96.2 1.5 %collective-permute-start.20 = (bf16[18,16,128]{2,1,0:T(8,128)(2,1)S(1)}, bf16[18,16,128]{2,1,0:T(8,128)(2,1)S(1)}, u32[]{:S(2)}, u32[]{:S(2)}) collective-permute-start(bf16[18,16,128]{2,1,0:T(8,128)(2,1)S(1)} %get-tuple-element.114), channel_id=1, source_target_pairs={{0,4},{2,6},{4,0},{6,2},{8,12},{10,14},{12,8},{14,10},{16,20},{18,... | collective-permute-start | bytes 221192 | tf_op jit(solution)/shard_map/ppermute | solution.py:500
  97.7 3.2 %collective-permute-done.20.refs_4_ = bf16[18,16,128]{2,1,0:T(8,128)(2,1)S(1)} collective-permute-done((bf16[18,16,128]{2,1,0:T(8,128)(2,1)S(1)}, bf16[18,16,128]{2,1,0:T(8,128)(2,1)S(1)}, u32[]{:S(2)}, u32[]{:S(2)}) %collective-permute-start.20) | collective-permute-done | bytes 73760 | tf_op jit(solution)/shard_map/ppermute | solution.py:500
  100.8 3.4 %collective-permute-done.19.refs_2_ = bf16[24,16,128]{2,1,0:T(8,128)(2,1)S(1)} collective-permute-done((bf16[24,16,128]{2,1,0:T(8,128)(2,1)S(1)}, bf16[24,16,128]{2,1,0:T(8,128)(2,1)S(1)}, u32[]{:S(2)}, u32[]{:S(2)}) %collective-permute-start.19) | collective-permute-done | bytes 98336 | tf_op jit(solution)/shard_map/ppermute | solution.py:500
  104.2 1.2 %last.1 = (bf16[3,48,384]{2,1,0:T(8,128)(2,1)S(1)}, f32[48,384]{1,0:T(8,128)}, bf16[48,128]{1,0:T(8,128)(2,1)S(1)}, bf16[48,128]{1,0:T(8,128)(2,1)S(1)}) custom-call(s32[2]{0:T(128)S(1)} %copy-done.14, bf16[24,16,128]{2,1,0:T(8,128)(2,1)S(1)} %get-tuple-element.111.refs_3_.refs_1_, bf16[24,16,128]{2,1,0:T(8,128)(2,1)S(1)} %collective-permute-done.19.refs_2_, ...), custom_call_target="tpu_custom_call" | custom-call | bytes 552968 | tf_op jit(solution)/shard_map/last/pallas_call | solution.py:79
  105.5 1.9 %collective-permute-start.22 = (bf16[3,48,384]{2,1,0:T(8,128)(2,1)S(1)}, bf16[3,48,384]{2,1,0:T(8,128)(2,1)S(1)}, u32[]{:S(2)}, u32[]{:S(2)}) collective-permute-start(bf16[3,48,384]{2,1,0:T(8,128)(2,1)S(1)} %get-tuple-element.118.refs_6_), channel_id=1, source_target_pairs={{0,0},{1,16},{2,2},{3,18},{4,4},{5,20},{6,6},{7,22},{8,8},{9,24},{... | collective-permute-start | bytes 331784 | tf_op jit(solution)/shard_map/ppermute | solution.py:776
  107.4 0.1 collective-permute-start.23
  107.5 2.9 %pair.1 = bf16[2048,128]{1,0:T(8,128)(2,1)} custom-call(s32[2]{0:T(128)S(1)} %copy-done.14, bf16[2048,128]{1,0:T(8,128)(2,1)S(1)} %bitcast.19, f32[1,128]{1,0:T(1,128)S(1)} %bitcast.26, bf16[8,128]{1,0:T(8,128)(2,1)S(1)} %bitcast.24, bf16[64,128]{1,0:T(8,128)(2,1)S(1)} %get-tuple-element.116.refs_2_.refs_4_, ...), custom_call_target="tpu_custom_call" | custom-call | flops 67108864 | bytes 1083912 | tf_op jit(solution)/shard_map/pair/pallas_call | solution.py:79
  110.4 0.7 collective-permute-done.23.refs_2_
  111.1 3.3 %collective-permute-done.22.refs_0_ = bf16[3,48,384]{2,1,0:T(8,128)(2,1)S(1)} collective-permute-done((bf16[3,48,384]{2,1,0:T(8,128)(2,1)S(1)}, bf16[3,48,384]{2,1,0:T(8,128)(2,1)S(1)}, u32[]{:S(2)}, u32[]{:S(2)}) %collective-permute-start.22) | collective-permute-done | bytes 110624 | tf_op jit(solution)/shard_map/ppermute | solution.py:776
  114.4 0.7 finish.1
  115.1 0.6 reduce_sum.9
  (54 shorter events, 0.3 us)
Async XLA Ops:
  5.4 10.8 %collective-permute-start = (bf16[128,768]{1,0:T(8,128)(2,1)}, bf16[128,768]{1,0:T(8,128)(2,1)S(1)}, u32[]{:S(2)}, u32[]{:S(2)}) collective-permute-start(bf16[128,768]{1,0:T(8,128)(2,1)} %get-tuple-element.72.refs_2_), channel_id=1, source_target_pairs={{0,1},{1,0},{2,3},{3,2},{4,5},{5,4},{6,7},{7,6},{8,9},{9,8},{10,11... | collective-permute-start | bytes 589832 | tf_op jit(solution)/shard_map/ppermute | solution.py:505
  5.5 10.7 %collective-permute-start.3 = (bf16[2,64,128]{2,1,0:T(8,128)(2,1)}, bf16[2,64,128]{2,1,0:T(8,128)(2,1)S(1)}, u32[]{:S(2)}, u32[]{:S(2)}) collective-permute-start(bf16[2,64,128]{2,1,0:T(8,128)(2,1)} %get-tuple-element.76.refs_0_), channel_id=1, source_target_pairs={{0,24},{2,26},{4,28},{6,30},{8,16},{10,18},{12,20},{14,22},{16,8},... | collective-permute-start | bytes 98312 | tf_op jit(solution)/shard_map/ppermute | solution.py:500
  9.6 6.5 %collective-permute-start.2 = (bf16[2,64,128]{2,1,0:T(8,128)(2,1)}, bf16[2,64,128]{2,1,0:T(8,128)(2,1)S(1)}, u32[]{:S(2)}, u32[]{:S(2)}) collective-permute-start(bf16[2,64,128]{2,1,0:T(8,128)(2,1)} %get-tuple-element.76.refs_0_), channel_id=1, source_target_pairs={{0,16},{2,18},{4,20},{6,22},{8,24},{10,26},{12,28},{14,30},{16,0},... | collective-permute-start | bytes 98312 | tf_op jit(solution)/shard_map/ppermute | solution.py:500
  9.6 6.6 %collective-permute-start.1 = (bf16[2,64,128]{2,1,0:T(8,128)(2,1)}, bf16[2,64,128]{2,1,0:T(8,128)(2,1)S(1)}, u32[]{:S(2)}, u32[]{:S(2)}) collective-permute-start(bf16[2,64,128]{2,1,0:T(8,128)(2,1)} %get-tuple-element.76.refs_0_), channel_id=1, source_target_pairs={{0,8},{2,10},{4,12},{6,14},{8,0},{10,2},{12,4},{14,6},{16,24},{18,... | collective-permute-start | bytes 98312 | tf_op jit(solution)/shard_map/ppermute | solution.py:500
  10.2 1.3 %copy-start.4 = (bf16[768,768]{1,0:T(8,128)(2,1)S(1)}, bf16[768,768]{1,0:T(8,128)(2,1)}, u32[]{:S(2)}) copy-start(bf16[768,768]{1,0:T(8,128)(2,1)} %refs_1_.3) | copy-start | bytes 3538948
  11.4 1.3 %copy-start.5 = (bf16[768,768]{1,0:T(8,128)(2,1)S(1)}, bf16[768,768]{1,0:T(8,128)(2,1)}, u32[]{:S(2)}) copy-start(bf16[768,768]{1,0:T(8,128)(2,1)} %refs_2_.3) | copy-start | bytes 3538948
  12.7 1.3 %copy-start.6 = (bf16[768,768]{1,0:T(8,128)(2,1)S(1)}, bf16[768,768]{1,0:T(8,128)(2,1)}, u32[]{:S(2)}) copy-start(bf16[768,768]{1,0:T(8,128)(2,1)} %refs_3_.1) | copy-start | bytes 3538948
  14.0 0.7 copy-start.13
  14.6 0.7 copy-start.17
  15.3 0.9 copy-start.15
  15.3 7.2 %copy-start.11 = (bf16[128,768]{1,0:T(8,128)(2,1)S(1)}, bf16[128,768]{1,0:T(8,128)(2,1)}, u32[]{:S(2)}) copy-start(bf16[128,768]{1,0:T(8,128)(2,1)} %get-tuple-element.72.refs_2_) | copy-start | bytes 589828
  15.3 13.9 %copy-start.12 = (f32[256,128]{1,0:T(8,128)S(1)}, f32[256,128]{1,0:T(8,128)}, u32[]{:S(2)}) copy-start(f32[256,128]{1,0:T(8,128)} %get-tuple-element.79.refs_8_) | copy-start | bytes 393220
  15.3 17.9 %copy-start.10 = (bf16[1,128,768]{2,1,0:T(8,128)(2,1)S(1)}, bf16[1,128,768]{2,1,0:T(8,128)(2,1)}, u32[]{:S(2)}) copy-start(bf16[1,128,768]{2,1,0:T(8,128)(2,1)} %param.39) | copy-start | bytes 589828
  16.1 6.4 %copy-start.14 = (s32[2]{0:T(128)S(1)}, s32[2]{0:T(128)}, u32[]{:S(2)}) copy-start(s32[2]{0:T(128)} %pad_add_fusion.refs_0_) | copy-start | bytes 28
  16.1 13.1 %copy-start.18 = (f32[1,256]{1,0:T(1,128)S(1)}, f32[1,256]{1,0:T(1,128)}, u32[]{:S(2)}) copy-start(f32[1,256]{1,0:T(1,128)} %get-tuple-element.71.refs_4_.refs_9_) | copy-start | bytes 3076
  16.2 17.0 %copy-start.2 = (bf16[1536,768]{1,0:T(8,128)(2,1)S(1)}, bf16[1536,768]{1,0:T(8,128)(2,1)}, u32[]{:S(2)}) copy-start(bf16[1536,768]{1,0:T(8,128)(2,1)} %refs_1_.2) | copy-start | bytes 7077892
  16.2 4.3 %collective-permute-start.4 = (bf16[4,64,128]{2,1,0:T(8,128)(2,1)S(1)}, bf16[4,64,128]{2,1,0:T(8,128)(2,1)S(1)}, u32[]{:S(2)}, u32[]{:S(2)}) collective-permute-start(bf16[4,64,128]{2,1,0:T(8,128)(2,1)S(1)} %get-tuple-element.78), channel_id=1, source_target_pairs={{0,1},{1,0},{2,3},{3,2},{4,5},{5,4},{6,7},{7,6},{8,9},{9,8},{10,11... | collective-permute-start | bytes 196616 | tf_op jit(solution)/shard_map/ppermute | solution.py:505
  20.5 12.7 %copy-start.21 = (f32[768]{0:T(1024)S(1)}, f32[768]{0:T(1024)}, u32[]{:S(2)}) copy-start(f32[768]{0:T(1024)} %param.29) | copy-start | bytes 9220
  20.6 12.7 %copy-start.8 = (bf16[1,128,768]{2,1,0:T(8,128)(2,1)S(1)}, bf16[1,128,768]{2,1,0:T(8,128)(2,1)}, u32[]{:S(2)}) copy-start(bf16[1,128,768]{2,1,0:T(8,128)(2,1)} %param.20) | copy-start | bytes 589828
  20.6 5.6 %collective-permute-start.7 = (bf16[2,4,64,128]{3,2,1,0:T(8,128)(2,1)S(1)}, bf16[2,4,64,128]{3,2,1,0:T(8,128)(2,1)S(1)}, u32[]{:S(2)}, u32[]{:S(2)}) collective-permute-start(bf16[2,4,64,128]{3,2,1,0:T(8,128)(2,1)S(1)} %join_tok.1.refs_4_), channel_id=1, source_target_pairs={{0,6},{2,4},{4,2},{6,0},{8,14},{10,12},{12,10},{14,8},{16,22},{18,... | collective-permute-start | bytes 393224 | tf_op jit(solution)/shard_map/ppermute | solution.py:500
  20.7 8.6 %collective-permute-start.6 = (bf16[2,4,64,128]{3,2,1,0:T(8,128)(2,1)S(1)}, bf16[2,4,64,128]{3,2,1,0:T(8,128)(2,1)S(1)}, u32[]{:S(2)}, u32[]{:S(2)}) collective-permute-start(bf16[2,4,64,128]{3,2,1,0:T(8,128)(2,1)S(1)} %join_tok.1.refs_4_), channel_id=1, source_target_pairs={{0,4},{2,6},{4,0},{6,2},{8,12},{10,14},{12,8},{14,10},{16,20},{18,... | collective-permute-start | bytes 393224 | tf_op jit(solution)/shard_map/ppermute | solution.py:500
  22.5 6.8 %collective-permute-start.5 = (bf16[2,4,64,128]{3,2,1,0:T(8,128)(2,1)S(1)}, bf16[2,4,64,128]{3,2,1,0:T(8,128)(2,1)S(1)}, u32[]{:S(2)}, u32[]{:S(2)}) collective-permute-start(bf16[2,4,64,128]{3,2,1,0:T(8,128)(2,1)S(1)} %join_tok.1.refs_4_), channel_id=1, source_target_pairs={{0,2},{2,0},{4,6},{6,4},{8,10},{10,8},{12,14},{14,12},{16,18},{18,... | collective-permute-start | bytes 393224 | tf_op jit(solution)/shard_map/ppermute | solution.py:500
  22.5 13.7 %copy-start.1 = (bf16[768,1536]{1,0:T(8,128)(2,1)S(1)}, bf16[768,1536]{1,0:T(8,128)(2,1)}, u32[]{:S(2)}) copy-start(bf16[768,1536]{1,0:T(8,128)(2,1)} %refs_9_.1) | copy-start | bytes 7077892
  29.3 6.9 %copy-start = (bf16[768,1536]{1,0:T(8,128)(2,1)S(1)}, bf16[768,1536]{1,0:T(8,128)(2,1)}, u32[]{:S(2)}) copy-start(bf16[768,1536]{1,0:T(8,128)(2,1)} %refs_8_.1) | copy-start | bytes 7077892
  29.3 6.9 %copy-start.7 = (bf16[768,768]{1,0:T(8,128)(2,1)S(1)}, bf16[768,768]{1,0:T(8,128)(2,1)}, u32[]{:S(2)}) copy-start(bf16[768,768]{1,0:T(8,128)(2,1)} %refs_7_.1) | copy-start | bytes 3538948
  31.4 4.8 %collective-permute-start.8 = (bf16[128,384]{1,0:T(8,128)(2,1)S(1)}, bf16[128,384]{1,0:T(8,128)(2,1)S(1)}, u32[]{:S(2)}, u32[]{:S(2)}) collective-permute-start(bf16[128,384]{1,0:T(8,128)(2,1)S(1)} %get-tuple-element.81), channel_id=1, source_target_pairs={{0,1},{1,0},{2,3},{3,2},{4,5},{5,4},{6,7},{7,6},{8,9},{9,8},{10,11... | collective-permute-start | bytes 294920 | tf_op jit(solution)/shard_map/ppermute | solution.py:505
  40.5 4.7 %collective-permute-start.9 = (bf16[384,128]{1,0:T(8,128)(2,1)S(1)}, bf16[384,128]{1,0:T(8,128)(2,1)S(1)}, u32[]{:S(2)}, u32[]{:S(2)}) collective-permute-start(bf16[384,128]{1,0:T(8,128)(2,1)S(1)} %get-tuple-element.86), channel_id=1, source_target_pairs={{0,1},{1,0},{2,3},{3,2},{4,5},{5,4},{6,7},{7,6},{8,9},{9,8},{10,11... | collective-permute-start | bytes 294920 | tf_op jit(solution)/shard_map/ppermute | solution.py:505
  47.3 6.4 %collective-permute-start.12 = (bf16[64,16,128]{2,1,0:T(8,128)(2,1)S(1)}, bf16[64,16,128]{2,1,0:T(8,128)(2,1)S(1)}, u32[]{:S(2)}, u32[]{:S(2)}) collective-permute-start(bf16[64,16,128]{2,1,0:T(8,128)(2,1)S(1)} %get-tuple-element.98), channel_id=1, source_target_pairs={{0,4},{2,6},{4,0},{6,2},{8,12},{10,14},{12,8},{14,10},{16,20},{18,... | collective-permute-start | bytes 786440 | tf_op jit(solution)/shard_map/ppermute | solution.py:500
  47.8 5.7 %collective-permute-start.13 = (bf16[128,768]{1,0:T(8,128)(2,1)S(1)}, bf16[128,768]{1,0:T(8,128)(2,1)S(1)}, u32[]{:S(2)}, u32[]{:S(2)}) collective-permute-start(bf16[128,768]{1,0:T(8,128)(2,1)S(1)} %get-tuple-element.99.refs_6_), channel_id=1, source_target_pairs={{0,1},{1,0},{2,3},{3,2},{4,5},{5,4},{6,7},{7,6},{8,9},{9,8},{10,11... | collective-permute-start | bytes 589832 | tf_op jit(solution)/shard_map/ppermute | solution.py:505
  51.5 3.6 %collective-permute-start.11 = (bf16[192,16,128]{2,1,0:T(8,128)(2,1)S(1)}, bf16[192,16,128]{2,1,0:T(8,128)(2,1)S(1)}, u32[]{:S(2)}, u32[]{:S(2)}) collective-permute-start(bf16[192,16,128]{2,1,0:T(8,128)(2,1)S(1)} %get-tuple-element.95), channel_id=1, source_target_pairs={{0,2},{2,0},{4,6},{6,4},{8,10},{10,8},{12,14},{14,12},{16,18},{18,... | collective-permute-start | bytes 2359304 | tf_op jit(solution)/shard_map/ppermute | solution.py:500
  55.1 7.6 %copy-start.20 = (f32[768]{0:T(1024)S(1)}, f32[768]{0:T(1024)}, u32[]{:S(2)}) copy-start(f32[768]{0:T(1024)} %refs_5_.1) | copy-start | bytes 9220
  55.1 2.3 %collective-permute-start.14 = (bf16[176,16,128]{2,1,0:T(8,128)(2,1)S(1)}, bf16[176,16,128]{2,1,0:T(8,128)(2,1)S(1)}, u32[]{:S(2)}, u32[]{:S(2)}) collective-permute-start(bf16[176,16,128]{2,1,0:T(8,128)(2,1)S(1)} %get-tuple-element.101), channel_id=1, source_target_pairs={{0,2},{2,0},{4,6},{6,4},{8,10},{10,8},{12,14},{14,12},{16,18},{18,... | collective-permute-start | bytes 2162696 | tf_op jit(solution)/shard_map/ppermute | solution.py:500
  58.3 11.7 %collective-permute-start.15 = (bf16[96,16,128]{2,1,0:T(8,128)(2,1)S(1)}, bf16[96,16,128]{2,1,0:T(8,128)(2,1)S(1)}, u32[]{:S(2)}, u32[]{:S(2)}) collective-permute-start(bf16[96,16,128]{2,1,0:T(8,128)(2,1)S(1)} %get-tuple-element.103), channel_id=1, source_target_pairs={{0,4},{2,6},{4,0},{6,2},{8,12},{10,14},{12,8},{14,10},{16,20},{18,... | collective-permute-start | bytes 1179656 | tf_op jit(solution)/shard_map/ppermute | solution.py:500
  59.8 10.2 %collective-permute-start.16 = (bf16[88,16,128]{2,1,0:T(8,128)(2,1)S(1)}, bf16[88,16,128]{2,1,0:T(8,128)(2,1)S(1)}, u32[]{:S(2)}, u32[]{:S(2)}) collective-permute-start(bf16[88,16,128]{2,1,0:T(8,128)(2,1)S(1)} %get-tuple-element.105), channel_id=1, source_target_pairs={{0,8},{2,10},{4,12},{6,14},{8,0},{10,2},{12,4},{14,6},{16,24},{18,... | collective-permute-start | bytes 1081352 | tf_op jit(solution)/shard_map/ppermute | solution.py:500
  61.2 6.4 %collective-permute-start.10 = (bf16[768,128]{1,0:T(8,128)(2,1)S(1)}, bf16[768,128]{1,0:T(8,128)(2,1)S(1)}, u32[]{:S(2)}, u32[]{:S(2)}) collective-permute-start(bf16[768,128]{1,0:T(8,128)(2,1)S(1)} %get-tuple-element.92), channel_id=1, source_target_pairs={{0,1},{1,0},{2,3},{3,2},{4,5},{5,4},{6,7},{7,6},{8,9},{9,8},{10,11... | collective-permute-start | bytes 589832 | tf_op jit(solution)/shard_map/ppermute | solution.py:505
  67.5 17.9 %copy-start.9 = (bf16[16,128,128]{2,1,0:T(8,128)(2,1)S(1)}, bf16[16,128,128]{2,1,0:T(8,128)(2,1)}, u32[]{:S(2)}) copy-start(bf16[16,128,128]{2,1,0:T(8,128)(2,1)} %get-tuple-element.115.refs_1_) | copy-start | bytes 1572868
  70.0 37.5 %copy-start.3 = (bf16[128,16,128]{2,1,0:T(8,128)(2,1)S(1)}, bf16[128,16,128]{2,1,0:T(8,128)(2,1)}, u32[]{:S(2)}) copy-start(bf16[128,16,128]{2,1,0:T(8,128)(2,1)} %param.22) | copy-start | bytes 1572868
  70.0 37.5 %copy-start.16 = (bf16[128,8]{0,1:T(8,128)(2,1)S(1)}, bf16[128,8]{0,1:T(8,128)(2,1)}, u32[]{:S(2)}) copy-start(bf16[128,8]{0,1:T(8,128)(2,1)} %param.34) | copy-start | bytes 6148
  70.0 37.5 %copy-start.19 = (f32[128]{0:T(128)S(1)}, f32[128]{0:T(128)}, u32[]{:S(2)}) copy-start(f32[128]{0:T(128)} %param.28) | copy-start | bytes 1540
  70.7 9.7 %collective-permute-start.17 = (bf16[48,16,128]{2,1,0:T(8,128)(2,1)S(1)}, bf16[48,16,128]{2,1,0:T(8,128)(2,1)S(1)}, u32[]{:S(2)}, u32[]{:S(2)}) collective-permute-start(bf16[48,16,128]{2,1,0:T(8,128)(2,1)S(1)} %get-tuple-element.108), channel_id=1, source_target_pairs={{0,8},{2,10},{4,12},{6,14},{8,0},{10,2},{12,4},{14,6},{16,24},{18,... | collective-permute-start | bytes 589832 | tf_op jit(solution)/shard_map/ppermute | solution.py:500
  72.2 7.8 %collective-permute-start.18 = (bf16[44,16,128]{2,1,0:T(8,128)(2,1)S(1)}, bf16[44,16,128]{2,1,0:T(8,128)(2,1)S(1)}, u32[]{:S(2)}, u32[]{:S(2)}) collective-permute-start(bf16[44,16,128]{2,1,0:T(8,128)(2,1)S(1)} %get-tuple-element.110), channel_id=1, source_target_pairs={{0,16},{2,18},{4,20},{6,22},{8,24},{10,26},{12,28},{14,30},{16,0},... | collective-permute-start | bytes 540680 | tf_op jit(solution)/shard_map/ppermute | solution.py:500
  81.7 3.8 %collective-permute-start.21 = (bf16[64,128]{1,0:T(8,128)(2,1)S(1)}, bf16[64,128]{1,0:T(8,128)(2,1)S(1)}, u32[]{:S(2)}, u32[]{:S(2)}) collective-permute-start(bf16[64,128]{1,0:T(8,128)(2,1)S(1)} %get-tuple-element.117), channel_id=1, source_target_pairs={{0,1},{1,0},{2,3},{3,2},{4,5},{5,4},{6,7},{7,6},{8,9},{9,8},{10,11... | collective-permute-start | bytes 49160 | tf_op jit(solution)/shard_map/ppermute | solution.py:505
  87.0 28.1 %all-to-all-start = ((f32[32,8,128]{2,1,0:T(8,128)}), f32[32,8,128]{2,1,0:T(8,128)S(1)}, u32[]{:S(2)}, u32[]{:S(2)}) async-start(f32[32,8,128]{2,1,0:T(8,128)} %pair_weight.1.refs_5_), calls=%async_computation | async-start | bytes 262144 | tf_op jit(solution)/shard_map/all_to_all | solution.py:509
  93.7 10.5 %collective-permute-start.19 = (bf16[24,16,128]{2,1,0:T(8,128)(2,1)S(1)}, bf16[24,16,128]{2,1,0:T(8,128)(2,1)S(1)}, u32[]{:S(2)}, u32[]{:S(2)}) collective-permute-start(bf16[24,16,128]{2,1,0:T(8,128)(2,1)S(1)} %get-tuple-element.112), channel_id=1, source_target_pairs={{0,16},{2,18},{4,20},{6,22},{8,24},{10,26},{12,28},{14,30},{16,0},... | collective-permute-start | bytes 294920 | tf_op jit(solution)/shard_map/ppermute | solution.py:500
  96.2 4.7 %collective-permute-start.20 = (bf16[18,16,128]{2,1,0:T(8,128)(2,1)S(1)}, bf16[18,16,128]{2,1,0:T(8,128)(2,1)S(1)}, u32[]{:S(2)}, u32[]{:S(2)}) collective-permute-start(bf16[18,16,128]{2,1,0:T(8,128)(2,1)S(1)} %get-tuple-element.114), channel_id=1, source_target_pairs={{0,4},{2,6},{4,0},{6,2},{8,12},{10,14},{12,8},{14,10},{16,20},{18,... | collective-permute-start | bytes 221192 | tf_op jit(solution)/shard_map/ppermute | solution.py:500
  105.5 9.0 %collective-permute-start.22 = (bf16[3,48,384]{2,1,0:T(8,128)(2,1)S(1)}, bf16[3,48,384]{2,1,0:T(8,128)(2,1)S(1)}, u32[]{:S(2)}, u32[]{:S(2)}) collective-permute-start(bf16[3,48,384]{2,1,0:T(8,128)(2,1)S(1)} %get-tuple-element.118.refs_6_), channel_id=1, source_target_pairs={{0,0},{1,16},{2,2},{3,18},{4,4},{5,20},{6,6},{7,22},{8,8},{9,24},{... | collective-permute-start | bytes 331784 | tf_op jit(solution)/shard_map/ppermute | solution.py:776
  107.4 3.8 %collective-permute-start.23 = (bf16[48,128]{1,0:T(8,128)(2,1)S(1)}, bf16[48,128]{1,0:T(8,128)(2,1)S(1)}, u32[]{:S(2)}, u32[]{:S(2)}) collective-permute-start(bf16[48,128]{1,0:T(8,128)(2,1)S(1)} %get-tuple-element.120), channel_id=1, source_target_pairs={{0,1},{1,0},{2,3},{3,2},{4,5},{5,4},{6,7},{7,6},{8,9},{9,8},{10,11... | collective-permute-start | bytes 36872 | tf_op jit(solution)/shard_map/ppermute | solution.py:505

commit v9 on v8

--- a/solution.py
+++ b/solution.py
@@ -187,14 +187,14 @@
 
 
 def attention_kernel(copies, toks, near, cols, head_width, ids, query, key, value, *rest):
-    biases, (facts, chain, weights_out, att_out) = rest[:near], rest[near : near + 4]
-    pieces, bias = rest[near + 4 : near + 4 + toks], rest[near + 4 + toks]
+    biases, (facts, chain, weights_out, att_out) = rest[:2], rest[2:6]
+    pieces, bias = rest[6 : 6 + toks], rest[6 + toks]
     t, low, high = ids[0], low_bits(ids[1], near), ids[1] // near
     for m in range(near):
         for rz in range(copies // near):
             c = jnp.bitwise_xor(high, rz) * near + jnp.bitwise_xor(low, m)
             for r in range(toks):
-                bias[c, jnp.bitwise_xor(t, r)] = biases[m][r, rz]
+                bias[c, jnp.bitwise_xor(t, r)] = biases[m % 2][m // 2, r, rz]
     own_heads = weights_out.shape[0]
     tokens = query.shape[1]
     rows = tokens // toks
@@ -574,28 +574,28 @@
     near = 4
     far = copies // near
     x_parts = [x_own] + [swap_tok(x_own, r) for r in range(1, toks)]
+    by_tok = call(
+        functools.partial(split_kernel, far),
+        "split_far",
+        [bias_mine] + [swap_copy(bias_mine, m * near) for m in range(1, far)],
+        [((far, own_heads * cols, rows), bf16)] * toks,
+        deps=x_parts[1:],
+    )
     (slices,) = call(
         stage_kernel,
         "stage",
         [where_am_i] + [(w, ANY) for w in weights3],
         [((3, width, own_width), bf16)],
         [pltpu.SemaphoreType.DMA((3,))],
-        deps=[chain_row],
-    )
-    by_tok = call(
-        functools.partial(split_kernel, far),
-        "split_far",
-        [bias_mine] + [swap_copy(bias_mine, m * near) for m in range(1, far)],
-        [((far, own_heads * cols, rows), bf16)] * toks,
-        deps=[slices] + x_parts[1:],
+        deps=[by_tok[0]],
     )
     (lines,) = call(
         join_kernel,
         "join_tok",
         [by_tok[0]] + [swap_tok(by_tok[r], r) for r in range(1, toks)],
         [((toks, far, own_heads * cols, rows), bf16)],
-    )
-    biases = [lines] + [swap_copy(lines, m) for m in range(1, near)]
+        deps=[slices],
+    )
     x, query, key, value = call(
         functools.partial(project_kernel, toks),
         "project",
@@ -603,6 +603,14 @@
         [((tokens, width), bf16)] + [((own_width, tokens), bf16)] * 3,
         flops=6 * tokens * width * own_width,
     )
+    (lines,) = call(
+        join_kernel,
+        "join_y",
+        [lines, swap_copy(lines, 2)],
+        [((2,) + lines.shape, bf16)],
+        deps=[value],
+    )
+    biases = [lines, swap_copy(lines, 1)]
     done = call(
         functools.partial(attention_kernel, copies, toks, near, cols, head_width),
         "attention",
@@ -752,6 +760,7 @@
         [((devices, heads, channels), f32)],
         [VMEM((heads * cols, rows), f32)],
         flops=2 * heads * cols * rows * channels * cols,
+        deps=[pairs[0][1], pairs[1][1]],
     )
     last = call(
         functools.partial(last_kernel, toks),

time: 116 us -> 108 us (0.931)
  starting transfers between devices: 37.4 us -> 27.3 us
  waiting for transfers between devices: 41.3 us -> 44.2 us
  local copies, waits for them, and re-layouts: 5.23 us -> 4.05 us
    ppermute x8, starting transfers between devices: 10.2 us -> 4.57 us  [swap_tok(): return lax.ppermute(value, 'tok', [(i, i ^ mask) for i in range(size)])]
    ppermute x15 -> x14, starting transfers between devices: 18.5 us -> 13.4 us  [swap_copy(): return lax.ppermute(value, 'copy', [(i, i ^ mask) for i in range(size)])]
    ppermute x8, waiting for transfers between devices: 17.2 us -> 20.5 us  [swap_tok(): return lax.ppermute(value, 'tok', [(i, i ^ mask) for i in range(size)])]
    ppermute x1, starting transfers between devices: 1.91 us -> 4.27 us  [per_device(): moved = lax.ppermute(last[0], ('copy', 'tok'), swaps)]
    all_to_all x1, starting transfers between devices: 6.71 us -> 5.09 us  [exchange(): return lax.all_to_all(value, ('copy', 'tok'), 0, 0)]
    unnamed x44 -> x42, local copies, waits for them, and re-layouts: 5.23 us -> 4.05 us
    ppermute x15 -> x14, waiting for transfers between devices: 20.9 us -> 20.7 us  [swap_copy(): return lax.ppermute(value, 'copy', [(i, i ^ mask) for i in range(size)])]
    pallas_call x20 -> x21, Pallas kernels: 29.6 us -> 29.6 us  [call(): pl.pallas_call(whole, name=name, out_shape=[jax.ShapeDtypeStruct(one[0],...]
  transfers between devices with their start and end apart: 25 -> 24, of which waited for: 17 -> 16; matrix products, arithmetic and copies ran while one was open for 0% -> 0% of each run, Pallas kernels for 11% -> 12%
where the time goes in v9:
time: 108 us; the launch traced here: 107 us
  waiting for transfers between devices  44.2 us (41%)
  Pallas kernels  29.6 us (27%)
  starting transfers between devices  27.3 us (25%)
  local copies, waits for them, and re-layouts  4.05 us (4%)
  other arithmetic  1.21 us (1%)
    pallas_call x21, Pallas kernels, call(): pl.pallas_call(whole, name=name, out_shape=[jax.ShapeDtypeStruct(one[0],...  29.6 us
    ppermute x14, waiting for transfers between devices, swap_copy(): return lax.ppermute(value, 'copy', [(i, i ^ mask) for i in range(size)])  20.7 us
    ppermute x8, waiting for transfers between devices, swap_tok(): return lax.ppermute(value, 'tok', [(i, i ^ mask) for i in range(size)])  20.5 us
    ppermute x14, starting transfers between devices, swap_copy(): return lax.ppermute(value, 'copy', [(i, i ^ mask) for i in range(size)])  13.4 us
    all_to_all x1, starting transfers between devices, exchange(): return lax.all_to_all(value, ('copy', 'tok'), 0, 0)  5.09 us
    ppermute x8, starting transfers between devices, swap_tok(): return lax.ppermute(value, 'tok', [(i, i ^ mask) for i in range(size)])  4.57 us
    ppermute x1, starting transfers between devices, per_device(): moved = lax.ppermute(last[0], ('copy', 'tok'), swaps)  4.27 us
    unnamed x42, local copies, waits for them, and re-layouts  4.05 us
  transfers between devices with their start and end apart: 24, of which 16 were waited for; matrix products, arithmetic and copies ran while one was open for 0% of the time, Pallas kernels for 12%

profile of v9, /device:TPU:2, one launch (start us, length us, event | category | flops | bytes accessed | tf_op | source)
XLA Modules:
  0.0 107.5 jit_solution(17104259154867775952)
XLA Ops:
  0.6 0.6 pad_add_fusion.refs_0_
  1.2 4.2 %enter.1 = (bf16[128,768]{1,0:T(8,128)(2,1)}, bf16[16,128,128]{2,1,0:T(8,128)(2,1)}, f32[256,128]{1,0:T(8,128)}, f32[1,256]{1,0:T(1,128)}, bf16[2,64,128]{2,1,0:T(8,128)(2,1)}) custom-call(s32[2]{0:T(128)} %pad_add_fusion.refs_0_, bf16[128,768]{1,0:T(8,128)(2,1)} %bitcast.20, bf16[128,768]{1,0:T(8,128)(2,1)} %refs_2_.2, s32[1,128]{1,0:T(1,128)} %bitcast.31, ...), custom_call_target="tpu_custom_call" | custom-call | flops 67108864 | bytes 1860808 | tf_op jit(solution)/shard_map/enter/pallas_call | solution.py:79
  5.4 0.1 collective-permute-start.3
  5.5 4.1 %collective-permute-start.2 = (bf16[2,64,128]{2,1,0:T(8,128)(2,1)}, bf16[2,64,128]{2,1,0:T(8,128)(2,1)S(1)}, u32[]{:S(2)}, u32[]{:S(2)}) collective-permute-start(bf16[2,64,128]{2,1,0:T(8,128)(2,1)} %get-tuple-element.71.refs_0_), channel_id=1, source_target_pairs={{0,24},{2,26},{4,28},{6,30},{8,16},{10,18},{12,20},{14,22},{16,8},... | collective-permute-start | bytes 98312 | tf_op jit(solution)/shard_map/ppermute | solution.py:500
  9.6 0.6 collective-permute-start
  10.2 1.7 %collective-permute-done.2.refs_3_ = bf16[2,64,128]{2,1,0:T(8,128)(2,1)S(1)} collective-permute-done((bf16[2,64,128]{2,1,0:T(8,128)(2,1)}, bf16[2,64,128]{2,1,0:T(8,128)(2,1)S(1)}, u32[]{:S(2)}, u32[]{:S(2)}) %collective-permute-start.2) | collective-permute-done | bytes 32800 | tf_op jit(solution)/shard_map/ppermute | solution.py:500
  11.8 2.8 %collective-permute-done.1.refs_2_ = bf16[2,64,128]{2,1,0:T(8,128)(2,1)S(1)} collective-permute-done((bf16[2,64,128]{2,1,0:T(8,128)(2,1)}, bf16[2,64,128]{2,1,0:T(8,128)(2,1)S(1)}, u32[]{:S(2)}, u32[]{:S(2)}) %collective-permute-start.1) | collective-permute-done | bytes 32800 | tf_op jit(solution)/shard_map/ppermute | solution.py:500
  14.6 0.8 copy-done.15
  15.4 1.6 %collective-permute-start.4 = (bf16[4,64,128]{2,1,0:T(8,128)(2,1)S(1)}, bf16[4,64,128]{2,1,0:T(8,128)(2,1)S(1)}, u32[]{:S(2)}, u32[]{:S(2)}) collective-permute-start(bf16[4,64,128]{2,1,0:T(8,128)(2,1)S(1)} %get-tuple-element.77), channel_id=1, source_target_pairs={{0,1},{1,0},{2,3},{3,2},{4,5},{5,4},{6,7},{7,6},{8,9},{9,8},{10,11... | collective-permute-start | bytes 196616 | tf_op jit(solution)/shard_map/ppermute | solution.py:505
  17.0 1.3 %copy-done.5 = bf16[768,768]{1,0:T(8,128)(2,1)S(1)} copy-done((bf16[768,768]{1,0:T(8,128)(2,1)S(1)}, bf16[768,768]{1,0:T(8,128)(2,1)}, u32[]{:S(2)}) %copy-start.5) | copy-done | bytes 1179672
  18.2 1.3 %copy-done.6 = bf16[768,768]{1,0:T(8,128)(2,1)S(1)} copy-done((bf16[768,768]{1,0:T(8,128)(2,1)S(1)}, bf16[768,768]{1,0:T(8,128)(2,1)}, u32[]{:S(2)}) %copy-start.6) | copy-done | bytes 1179672
  19.5 0.7 copy-done.13
  20.2 0.8 stage.1.refs_1_.refs_2_
  20.9 0.0 copy-start.11
  21.0 0.0 copy-start.14
  21.1 1.6 %collective-permute-start.5 = (bf16[2,4,64,128]{3,2,1,0:T(8,128)(2,1)S(1)}, bf16[2,4,64,128]{3,2,1,0:T(8,128)(2,1)S(1)}, u32[]{:S(2)}, u32[]{:S(2)}) collective-permute-start(bf16[2,4,64,128]{3,2,1,0:T(8,128)(2,1)S(1)} %join_tok.1.refs_0_), channel_id=1, source_target_pairs={{0,4},{2,6},{4,0},{6,2},{8,12},{10,14},{12,8},{14,10},{16,20},{18,... | collective-permute-start | bytes 393224 | tf_op jit(solution)/shard_map/ppermute | solution.py:500
  22.6 1.4 %project.1 = (bf16[256,768]{1,0:T(8,128)(2,1)S(1)}, bf16[384,256]{1,0:T(8,128)(2,1)S(1)}, bf16[384,256]{1,0:T(8,128)(2,1)S(1)}, bf16[384,256]{1,0:T(8,128)(2,1)S(1)}) custom-call(s32[2]{0:T(128)S(1)} %copy-done.13, bf16[3,768,384]{2,1,0:T(8,128)(2,1)S(1)} %stage.1.refs_1_.refs_2_, bf16[128,768]{1,0:T(8,128)(2,1)S(1)} %copy-done.11, ...), custom_call_target="tpu_custom_call" | custom-call | flops 452984832 | bytes 3145736 | tf_op jit(solution)/shard_map/project/pallas_call | solution.py:79
  24.0 2.0 %collective-permute-done.5.refs_1_ = bf16[2,4,64,128]{3,2,1,0:T(8,128)(2,1)S(1)} collective-permute-done((bf16[2,4,64,128]{3,2,1,0:T(8,128)(2,1)S(1)}, bf16[2,4,64,128]{3,2,1,0:T(8,128)(2,1)S(1)}, u32[]{:S(2)}, u32[]{:S(2)}) %collective-permute-start.5) | collective-permute-done | bytes 131104 | tf_op jit(solution)/shard_map/ppermute | solution.py:500
  26.1 0.1 collective-permute-start.6
  26.2 1.5 %collective-permute-done.6.refs_5_ = bf16[2,2,4,64,128]{4,3,2,1,0:T(8,128)(2,1)S(1)} collective-permute-done((bf16[2,2,4,64,128]{4,3,2,1,0:T(8,128)(2,1)S(1)}, bf16[2,2,4,64,128]{4,3,2,1,0:T(8,128)(2,1)S(1)}, u32[]{:S(2)}, u32[]{:S(2)}) %collective-permute-start.6) | collective-permute-done | bytes 262176 | tf_op jit(solution)/shard_map/ppermute | solution.py:500
  27.7 2.1 %attention.1 = (bf16[4,256,256]{2,1,0:T(8,128)(2,1)S(1)}, bf16[256,384]{1,0:T(8,128)(2,1)S(1)}, bf16[128,384]{1,0:T(8,128)(2,1)S(1)}, bf16[128,384]{1,0:T(8,128)(2,1)S(1)}) custom-call(s32[2]{0:T(128)S(1)} %copy-done.14, bf16[384,256]{1,0:T(8,128)(2,1)S(1)} %get-tuple-element.74.refs_1_, bf16[384,256]{1,0:T(8,128)(2,1)S(1)} %get-tuple-element.75.refs_2_, ...), custom_call_target="tpu_custom_call" | custom-call | flops 100663296 | bytes 2163720 | tf_op jit(solution)/shard_map/attention/pallas_call | solution.py:79
  29.9 0.6 collective-permute-start.7
  30.5 0.9 down.1
  31.4 3.4 %collective-permute-done.7.refs_6_ = bf16[128,384]{1,0:T(8,128)(2,1)S(1)} collective-permute-done((bf16[128,384]{1,0:T(8,128)(2,1)S(1)}, bf16[128,384]{1,0:T(8,128)(2,1)S(1)}, u32[]{:S(2)}, u32[]{:S(2)}) %collective-permute-start.7) | collective-permute-done | bytes 98336 | tf_op jit(solution)/shard_map/ppermute | solution.py:505
  34.8 4.3 %hidden.1 = (f32[128,768]{1,0:T(8,128)S(1)}, bf16[128,768]{1,0:T(8,128)(2,1)S(1)}, bf16[384,128]{1,0:T(8,128)(2,1)S(1)}, bf16[384,128]{1,0:T(8,128)(2,1)S(1)}) custom-call(s32[2]{0:T(128)S(1)} %copy-done.14, bf16[128,768]{1,0:T(8,128)(2,1)S(1)} %get-tuple-element.67.refs_1_.refs_0_, bf16[128,768]{1,0:T(8,128)(2,1)S(1)} %get-tuple-element.68.refs_2_, ...), custom_call_target="tpu_custom_call" | custom-call | flops 1509949440 | bytes 8064008 | tf_op jit(solution)/shard_map/hidden/pallas_call | solution.py:79
  39.1 0.6 collective-permute-start.8
  39.7 4.1 %collective-permute-done.8.refs_6_ = bf16[384,128]{1,0:T(8,128)(2,1)S(1)} collective-permute-done((bf16[384,128]{1,0:T(8,128)(2,1)S(1)}, bf16[384,128]{1,0:T(8,128)(2,1)S(1)}, u32[]{:S(2)}, u32[]{:S(2)}) %collective-permute-start.8) | collective-permute-done | bytes 98336 | tf_op jit(solution)/shard_map/ppermute | solution.py:505
  43.8 2.0 %backward.1 = (bf16[384,256]{1,0:T(8,128)(2,1)S(1)}, bf16[384,256]{1,0:T(8,128)(2,1)S(1)}, bf16[384,256]{1,0:T(8,128)(2,1)S(1)}, bf16[64,16,128]{2,1,0:T(8,128)(...) custom-call(s32[2]{0:T(128)S(1)} %copy-done.14, ...), custom_call_target="tpu_custom_call" | custom-call | flops 201326592 | bytes 2818056 | tf_op jit(solution)/shard_map/backward/pallas_call | solution.py:79
  45.8 1.6 %collective-permute-start.11 = (bf16[64,16,128]{2,1,0:T(8,128)(2,1)S(1)}, bf16[64,16,128]{2,1,0:T(8,128)(2,1)S(1)}, u32[]{:S(2)}, u32[]{:S(2)}) collective-permute-start(bf16[64,16,128]{2,1,0:T(8,128)(2,1)S(1)} %get-tuple-element.98), channel_id=1, source_target_pairs={{0,4},{2,6},{4,0},{6,2},{8,12},{10,14},{12,8},{14,10},{16,20},{18,... | collective-permute-start | bytes 786440 | tf_op jit(solution)/shard_map/ppermute | solution.py:500
  47.4 0.5 collective-permute-start.12
  48.0 2.1 %first.1 = (bf16[192,16,128]{2,1,0:T(8,128)(2,1)S(1)}, bf16[192,16,128]{2,1,0:T(8,128)(2,1)S(1)}, f32[768,128]{1,0:T(8,128)S(1)}, bf16[768,128]{1,0:T(8,128)(2,1)S(1)}) custom-call(s32[2]{0:T(128)S(1)} %copy-done.14, bf16[3,768,384]{2,1,0:T(8,128)(2,1)S(1)} %stage.1.refs_1_.refs_2_, bf16[256,768]{1,0:T(8,128)(2,1)S(1)} %get-tuple-element.83.refs_2_.refs_1_, ...), custom_call_target="tpu_custom_call" | custom-call | flops 754974720 | bytes 4915208 | tf_op jit(solution)/shard_map/first/pallas_call | solution.py:79
  50.1 0.1 collective-permute-start.10
  50.1 3.0 %collective-permute-done.12.refs_7_ = bf16[128,768]{1,0:T(8,128)(2,1)S(1)} collective-permute-done((bf16[128,768]{1,0:T(8,128)(2,1)S(1)}, bf16[128,768]{1,0:T(8,128)(2,1)S(1)}, u32[]{:S(2)}, u32[]{:S(2)}) %collective-permute-start.12) | collective-permute-done | bytes 196640 | tf_op jit(solution)/shard_map/ppermute | solution.py:505
  53.1 1.4 %second.1 = (bf16[176,16,128]{2,1,0:T(8,128)(2,1)S(1)}, bf16[176,16,128]{2,1,0:T(8,128)(2,1)S(1)}) custom-call(s32[2]{0:T(128)S(1)} %copy-done.14, bf16[256,768]{1,0:T(8,128)(2,1)S(1)} %get-tuple-element.83.refs_2_.refs_1_, bf16[256,384]{1,0:T(8,128)(2,1)S(1)} %get-tuple-element.96.refs_2_, bf16[384,256]{1,0:T(8,128)(2,1)S(1)} %get-tuple-element.90.refs_5_.refs_3_, ...), custom_call_target="tpu_custom_call" | custom-call | flops 301989888 | bytes 3145736 | tf_op jit(solution)/shard_map/second/pallas_call | solution.py:79
  54.5 0.1 collective-permute-start.13
  54.6 2.2 %collective-permute-done.13.refs_4_ = bf16[176,16,128]{2,1,0:T(8,128)(2,1)S(1)} collective-permute-done((bf16[176,16,128]{2,1,0:T(8,128)(2,1)S(1)}, bf16[176,16,128]{2,1,0:T(8,128)(2,1)S(1)}, u32[]{:S(2)}, u32[]{:S(2)}) %collective-permute-start.13) | collective-permute-done | bytes 720928 | tf_op jit(solution)/shard_map/ppermute | solution.py:500
  56.8 0.9 step_0.1
  57.7 0.8 collective-permute-start.14
  58.4 0.5 collective-permute-start.9
  59.0 6.1 %collective-permute-done.9.refs_4_ = bf16[768,128]{1,0:T(8,128)(2,1)S(1)} collective-permute-done((bf16[768,128]{1,0:T(8,128)(2,1)S(1)}, bf16[768,128]{1,0:T(8,128)(2,1)S(1)}, u32[]{:S(2)}, u32[]{:S(2)}) %collective-permute-start.9) | collective-permute-done | bytes 196640 | tf_op jit(solution)/shard_map/ppermute | solution.py:505
  65.1 1.2 %exit.1 = (bf16[128,768]{1,0:T(8,128)(2,1)}, f32[8,128]{1,0:T(8,128)S(1)}) custom-call(bf16[128,768]{1,0:T(8,128)(2,1)S(1)} %get-tuple-element.67.refs_1_.refs_0_, f32[1,768]{1,0:T(1,128)S(1)} %reshape.49.refs_1_, f32[128,768]{1,0:T(8,128)S(1)} %get-tuple-element.82.refs_2_, f32[768,128]{1,0:T(8,128)S(1)} %get-tuple-element.91.refs_3_, ...), custom_call_target="tpu_custom_call" | custom-call | bytes 1383424 | tf_op jit(solution)/shard_map/exit/pallas_call | solution.py:79
  66.3 2.3 %collective-permute-done.15.refs_4_ = bf16[88,16,128]{2,1,0:T(8,128)(2,1)S(1)} collective-permute-done((bf16[88,16,128]{2,1,0:T(8,128)(2,1)S(1)}, bf16[88,16,128]{2,1,0:T(8,128)(2,1)S(1)}, u32[]{:S(2)}, u32[]{:S(2)}) %collective-permute-start.15) | collective-permute-done | bytes 360480 | tf_op jit(solution)/shard_map/ppermute | solution.py:500
  68.6 0.3 collective-permute-done.14.refs_2_
  68.9 0.7 step_1.1
  69.6 0.1 collective-permute-start.16
  69.7 2.1 %collective-permute-start.17 = (bf16[44,16,128]{2,1,0:T(8,128)(2,1)S(1)}, bf16[44,16,128]{2,1,0:T(8,128)(2,1)S(1)}, u32[]{:S(2)}, u32[]{:S(2)}) collective-permute-start(bf16[44,16,128]{2,1,0:T(8,128)(2,1)S(1)} %get-tuple-element.110), channel_id=1, source_target_pairs={{0,16},{2,18},{4,20},{6,22},{8,24},{10,26},{12,28},{14,30},{16,0},... | collective-permute-start | bytes 540680 | tf_op jit(solution)/shard_map/ppermute | solution.py:500
  71.8 5.7 %collective-permute-done.17.refs_4_.refs_2_ = bf16[44,16,128]{2,1,0:T(8,128)(2,1)S(1)} collective-permute-done((bf16[44,16,128]{2,1,0:T(8,128)(2,1)S(1)}, bf16[44,16,128]{2,1,0:T(8,128)(2,1)S(1)}, u32[]{:S(2)}, u32[]{:S(2)}) %collective-permute-start.17) | collective-permute-done | bytes 180256 | tf_op jit(solution)/shard_map/ppermute | solution.py:500
  77.5 2.2 %collective-permute-done.16.refs_2_ = bf16[48,16,128]{2,1,0:T(8,128)(2,1)S(1)} collective-permute-done((bf16[48,16,128]{2,1,0:T(8,128)(2,1)S(1)}, bf16[48,16,128]{2,1,0:T(8,128)(2,1)S(1)}, u32[]{:S(2)}, u32[]{:S(2)}) %collective-permute-start.16) | collective-permute-done | bytes 196640 | tf_op jit(solution)/shard_map/ppermute | solution.py:500
  79.7 0.6 step_2.1
  80.3 1.4 %collective-permute-start.18 = (bf16[24,16,128]{2,1,0:T(8,128)(2,1)S(1)}, bf16[24,16,128]{2,1,0:T(8,128)(2,1)S(1)}, u32[]{:S(2)}, u32[]{:S(2)}) collective-permute-start(bf16[24,16,128]{2,1,0:T(8,128)(2,1)S(1)} %get-tuple-element.112), channel_id=1, source_target_pairs={{0,16},{2,18},{4,20},{6,22},{8,24},{10,26},{12,28},{14,30},{16,0},... | collective-permute-start | bytes 294920 | tf_op jit(solution)/shard_map/ppermute | solution.py:500
  81.7 1.0 collective-permute-start.19
  82.7 0.6 last_bias.1
  83.3 0.6 collective-permute-start.20
  83.9 3.2 %collective-permute-done.20.refs_3_.refs_5_ = bf16[64,128]{1,0:T(8,128)(2,1)S(1)} collective-permute-done((bf16[64,128]{1,0:T(8,128)(2,1)S(1)}, bf16[64,128]{1,0:T(8,128)(2,1)S(1)}, u32[]{:S(2)}, u32[]{:S(2)}) %collective-permute-start.20) | collective-permute-done | bytes 16416 | tf_op jit(solution)/shard_map/ppermute | solution.py:505
  87.1 1.6 %pair_weight.1.refs_5_ = f32[32,8,128]{2,1,0:T(8,128)} custom-call(s32[2]{0:T(128)S(1)} %copy-done.14, bf16[16,128,128]{2,1,0:T(8,128)(2,1)S(1)} %copy-done.9, bf16[64,128]{1,0:T(8,128)(2,1)S(1)} %get-tuple-element.116.refs_2_.refs_4_, bf16[64,128]{1,0:T(8,128)(2,1)S(1)} %collective-permute-done.20.refs_3_.refs_5_, ...), custom_call_target="tpu_custom_call" | custom-call | flops 67108864 | bytes 688136 | tf_op jit(solution)/shard_map/pair_weight/pallas_call | solution.py:79
  88.7 5.1 %all-to-all-start = ((f32[32,8,128]{2,1,0:T(8,128)}), f32[32,8,128]{2,1,0:T(8,128)S(1)}, u32[]{:S(2)}, u32[]{:S(2)}) async-start(f32[32,8,128]{2,1,0:T(8,128)} %pair_weight.1.refs_5_), calls=%async_computation | async-start | bytes 262144 | tf_op jit(solution)/shard_map/all_to_all | solution.py:509
  93.8 1.2 %last.1 = (bf16[3,48,384]{2,1,0:T(8,128)(2,1)S(1)}, f32[48,384]{1,0:T(8,128)}, bf16[48,128]{1,0:T(8,128)(2,1)S(1)}, bf16[48,128]{1,0:T(8,128)(2,1)S(1)}) custom-call(s32[2]{0:T(128)S(1)} %copy-done.14, bf16[24,16,128]{2,1,0:T(8,128)(2,1)S(1)} %get-tuple-element.111.refs_3_.refs_1_, bf16[24,16,128]{2,1,0:T(8,128)(2,1)S(1)} %collective-permute-done.18.refs_4_.refs_2_, ...), custom_call_target="tpu_custom_call" | custom-call | bytes 552968 | tf_op jit(solution)/shard_map/last/pallas_call | solution.py:79
  95.0 4.3 %collective-permute-start.21 = (bf16[3,48,384]{2,1,0:T(8,128)(2,1)S(1)}, bf16[3,48,384]{2,1,0:T(8,128)(2,1)S(1)}, u32[]{:S(2)}, u32[]{:S(2)}) collective-permute-start(bf16[3,48,384]{2,1,0:T(8,128)(2,1)S(1)} %get-tuple-element.118.refs_6_), channel_id=1, source_target_pairs={{0,0},{1,16},{2,2},{3,18},{4,4},{5,20},{6,6},{7,22},{8,8},{9,24},{... | collective-permute-start | bytes 331784 | tf_op jit(solution)/shard_map/ppermute | solution.py:785
  99.3 0.1 collective-permute-start.22
  99.4 2.9 %pair.1 = bf16[2048,128]{1,0:T(8,128)(2,1)} custom-call(s32[2]{0:T(128)S(1)} %copy-done.14, bf16[2048,128]{1,0:T(8,128)(2,1)S(1)} %bitcast.19, f32[1,128]{1,0:T(1,128)S(1)} %bitcast.26, bf16[8,128]{1,0:T(8,128)(2,1)S(1)} %bitcast.24, bf16[64,128]{1,0:T(8,128)(2,1)S(1)} %get-tuple-element.116.refs_2_.refs_4_, ...), custom_call_target="tpu_custom_call" | custom-call | flops 67108864 | bytes 1083912 | tf_op jit(solution)/shard_map/pair/pallas_call | solution.py:79
  102.3 0.7 collective-permute-done.22.refs_2_
  103.0 3.1 %collective-permute-done.21.refs_0_ = bf16[3,48,384]{2,1,0:T(8,128)(2,1)S(1)} collective-permute-done((bf16[3,48,384]{2,1,0:T(8,128)(2,1)S(1)}, bf16[3,48,384]{2,1,0:T(8,128)(2,1)S(1)}, u32[]{:S(2)}, u32[]{:S(2)}) %collective-permute-start.21) | collective-permute-done | bytes 110624 | tf_op jit(solution)/shard_map/ppermute | solution.py:785
  106.1 0.7 finish.1
  106.8 0.6 reduce_sum.9
  (51 shorter events, 0.2 us)
Async XLA Ops:
  0.6 16.3 %copy-start.4 = (bf16[768,768]{1,0:T(8,128)(2,1)S(1)}, bf16[768,768]{1,0:T(8,128)(2,1)}, u32[]{:S(2)}) copy-start(bf16[768,768]{1,0:T(8,128)(2,1)} %refs_1_.3) | copy-start | bytes 3538948
  5.4 9.2 %collective-permute-start.3 = (bf16[128,768]{1,0:T(8,128)(2,1)}, bf16[128,768]{1,0:T(8,128)(2,1)S(1)}, u32[]{:S(2)}, u32[]{:S(2)}) collective-permute-start(bf16[128,768]{1,0:T(8,128)(2,1)} %get-tuple-element.72.refs_2_), channel_id=1, source_target_pairs={{0,1},{1,0},{2,3},{3,2},{4,5},{5,4},{6,7},{7,6},{8,9},{9,8},{10,11... | collective-permute-start | bytes 589832 | tf_op jit(solution)/shard_map/ppermute | solution.py:505
  5.5 6.4 %collective-permute-start.2 = (bf16[2,64,128]{2,1,0:T(8,128)(2,1)}, bf16[2,64,128]{2,1,0:T(8,128)(2,1)S(1)}, u32[]{:S(2)}, u32[]{:S(2)}) collective-permute-start(bf16[2,64,128]{2,1,0:T(8,128)(2,1)} %get-tuple-element.71.refs_0_), channel_id=1, source_target_pairs={{0,24},{2,26},{4,28},{6,30},{8,16},{10,18},{12,20},{14,22},{16,8},... | collective-permute-start | bytes 98312 | tf_op jit(solution)/shard_map/ppermute | solution.py:500
  9.6 5.0 %collective-permute-start.1 = (bf16[2,64,128]{2,1,0:T(8,128)(2,1)}, bf16[2,64,128]{2,1,0:T(8,128)(2,1)S(1)}, u32[]{:S(2)}, u32[]{:S(2)}) collective-permute-start(bf16[2,64,128]{2,1,0:T(8,128)(2,1)} %get-tuple-element.71.refs_0_), channel_id=1, source_target_pairs={{0,16},{2,18},{4,20},{6,22},{8,24},{10,26},{12,28},{14,30},{16,0},... | collective-permute-start | bytes 98312 | tf_op jit(solution)/shard_map/ppermute | solution.py:500
  9.6 5.0 %collective-permute-start = (bf16[2,64,128]{2,1,0:T(8,128)(2,1)}, bf16[2,64,128]{2,1,0:T(8,128)(2,1)S(1)}, u32[]{:S(2)}, u32[]{:S(2)}) collective-permute-start(bf16[2,64,128]{2,1,0:T(8,128)(2,1)} %get-tuple-element.71.refs_0_), channel_id=1, source_target_pairs={{0,8},{2,10},{4,12},{6,14},{8,0},{10,2},{12,4},{14,6},{16,24},{18,... | collective-permute-start | bytes 98312 | tf_op jit(solution)/shard_map/ppermute | solution.py:500
  14.6 0.8 copy-start.15
  15.4 5.5 %collective-permute-start.4 = (bf16[4,64,128]{2,1,0:T(8,128)(2,1)S(1)}, bf16[4,64,128]{2,1,0:T(8,128)(2,1)S(1)}, u32[]{:S(2)}, u32[]{:S(2)}) collective-permute-start(bf16[4,64,128]{2,1,0:T(8,128)(2,1)S(1)} %get-tuple-element.77), channel_id=1, source_target_pairs={{0,1},{1,0},{2,3},{3,2},{4,5},{5,4},{6,7},{7,6},{8,9},{9,8},{10,11... | collective-permute-start | bytes 196616 | tf_op jit(solution)/shard_map/ppermute | solution.py:505
  17.0 1.3 %copy-start.5 = (bf16[768,768]{1,0:T(8,128)(2,1)S(1)}, bf16[768,768]{1,0:T(8,128)(2,1)}, u32[]{:S(2)}) copy-start(bf16[768,768]{1,0:T(8,128)(2,1)} %refs_2_.3) | copy-start | bytes 3538948
  18.2 1.3 %copy-start.6 = (bf16[768,768]{1,0:T(8,128)(2,1)S(1)}, bf16[768,768]{1,0:T(8,128)(2,1)}, u32[]{:S(2)}) copy-start(bf16[768,768]{1,0:T(8,128)(2,1)} %refs_3_.1) | copy-start | bytes 3538948
  19.5 0.7 copy-start.13
  20.2 7.6 %copy-start.12 = (f32[256,128]{1,0:T(8,128)S(1)}, f32[256,128]{1,0:T(8,128)}, u32[]{:S(2)}) copy-start(f32[256,128]{1,0:T(8,128)} %get-tuple-element.78.refs_6_) | copy-start | bytes 393220
  20.9 1.7 %copy-start.11 = (bf16[128,768]{1,0:T(8,128)(2,1)S(1)}, bf16[128,768]{1,0:T(8,128)(2,1)}, u32[]{:S(2)}) copy-start(bf16[128,768]{1,0:T(8,128)(2,1)} %get-tuple-element.72.refs_2_) | copy-start | bytes 589828
  21.0 9.5 %copy-start.2 = (bf16[1536,768]{1,0:T(8,128)(2,1)S(1)}, bf16[1536,768]{1,0:T(8,128)(2,1)}, u32[]{:S(2)}) copy-start(bf16[1536,768]{1,0:T(8,128)(2,1)} %refs_1_.2) | copy-start | bytes 7077892
  21.0 6.7 %copy-start.14 = (s32[2]{0:T(128)S(1)}, s32[2]{0:T(128)}, u32[]{:S(2)}) copy-start(s32[2]{0:T(128)} %pad_add_fusion.refs_0_) | copy-start | bytes 28
  21.0 6.7 %copy-start.18 = (f32[1,256]{1,0:T(1,128)S(1)}, f32[1,256]{1,0:T(1,128)}, u32[]{:S(2)}) copy-start(f32[1,256]{1,0:T(1,128)} %get-tuple-element.79.refs_7_) | copy-start | bytes 3076
  21.0 9.5 %copy-start.20 = (f32[768]{0:T(1024)S(1)}, f32[768]{0:T(1024)}, u32[]{:S(2)}) copy-start(f32[768]{0:T(1024)} %param.29) | copy-start | bytes 9220
  21.0 9.5 %copy-start.8 = (bf16[1,128,768]{2,1,0:T(8,128)(2,1)S(1)}, bf16[1,128,768]{2,1,0:T(8,128)(2,1)}, u32[]{:S(2)}) copy-start(bf16[1,128,768]{2,1,0:T(8,128)(2,1)} %param.20) | copy-start | bytes 589828
  21.0 9.5 %copy-start.10 = (bf16[1,128,768]{2,1,0:T(8,128)(2,1)S(1)}, bf16[1,128,768]{2,1,0:T(8,128)(2,1)}, u32[]{:S(2)}) copy-start(bf16[1,128,768]{2,1,0:T(8,128)(2,1)} %param.39) | copy-start | bytes 589828
  21.1 5.0 %collective-permute-start.5 = (bf16[2,4,64,128]{3,2,1,0:T(8,128)(2,1)S(1)}, bf16[2,4,64,128]{3,2,1,0:T(8,128)(2,1)S(1)}, u32[]{:S(2)}, u32[]{:S(2)}) collective-permute-start(bf16[2,4,64,128]{3,2,1,0:T(8,128)(2,1)S(1)} %join_tok.1.refs_0_), channel_id=1, source_target_pairs={{0,4},{2,6},{4,0},{6,2},{8,12},{10,14},{12,8},{14,10},{16,20},{18,... | collective-permute-start | bytes 393224 | tf_op jit(solution)/shard_map/ppermute | solution.py:500
  22.6 12.1 %copy-start.7 = (bf16[768,768]{1,0:T(8,128)(2,1)S(1)}, bf16[768,768]{1,0:T(8,128)(2,1)}, u32[]{:S(2)}) copy-start(bf16[768,768]{1,0:T(8,128)(2,1)} %refs_7_.1) | copy-start | bytes 3538948
  26.1 8.7 %copy-start.1 = (bf16[768,1536]{1,0:T(8,128)(2,1)S(1)}, bf16[768,1536]{1,0:T(8,128)(2,1)}, u32[]{:S(2)}) copy-start(bf16[768,1536]{1,0:T(8,128)(2,1)} %refs_9_.1) | copy-start | bytes 7077892
  26.1 1.6 %collective-permute-start.6 = (bf16[2,2,4,64,128]{4,3,2,1,0:T(8,128)(2,1)S(1)}, bf16[2,2,4,64,128]{4,3,2,1,0:T(8,128)(2,1)S(1)}, u32[]{:S(2)}, u32[]{:S(2)}) collective-permute-start(bf16[2,2,4,64,128]{4,3,2,1,0:T(8,128)(2,1)S(1)} %join_y.1.refs_4_), channel_id=1, source_target_pairs={{0,2},{2,0},{4,6},{6,4},{8,10},{10,8},{12,14},{14,12},{16,18},{18,... | collective-permute-start | bytes 786440 | tf_op jit(solution)/shard_map/ppermute | solution.py:500
  27.7 7.1 %copy-start = (bf16[768,1536]{1,0:T(8,128)(2,1)S(1)}, bf16[768,1536]{1,0:T(8,128)(2,1)}, u32[]{:S(2)}) copy-start(bf16[768,1536]{1,0:T(8,128)(2,1)} %refs_8_.1) | copy-start | bytes 7077892
  29.9 4.9 %collective-permute-start.7 = (bf16[128,384]{1,0:T(8,128)(2,1)S(1)}, bf16[128,384]{1,0:T(8,128)(2,1)S(1)}, u32[]{:S(2)}, u32[]{:S(2)}) collective-permute-start(bf16[128,384]{1,0:T(8,128)(2,1)S(1)} %get-tuple-element.81), channel_id=1, source_target_pairs={{0,1},{1,0},{2,3},{3,2},{4,5},{5,4},{6,7},{7,6},{8,9},{9,8},{10,11... | collective-permute-start | bytes 294920 | tf_op jit(solution)/shard_map/ppermute | solution.py:505
  39.1 4.7 %collective-permute-start.8 = (bf16[384,128]{1,0:T(8,128)(2,1)S(1)}, bf16[384,128]{1,0:T(8,128)(2,1)S(1)}, u32[]{:S(2)}, u32[]{:S(2)}) collective-permute-start(bf16[384,128]{1,0:T(8,128)(2,1)S(1)} %get-tuple-element.86), channel_id=1, source_target_pairs={{0,1},{1,0},{2,3},{3,2},{4,5},{5,4},{6,7},{7,6},{8,9},{9,8},{10,11... | collective-permute-start | bytes 294920 | tf_op jit(solution)/shard_map/ppermute | solution.py:505
  45.8 7.3 %collective-permute-start.11 = (bf16[64,16,128]{2,1,0:T(8,128)(2,1)S(1)}, bf16[64,16,128]{2,1,0:T(8,128)(2,1)S(1)}, u32[]{:S(2)}, u32[]{:S(2)}) collective-permute-start(bf16[64,16,128]{2,1,0:T(8,128)(2,1)S(1)} %get-tuple-element.98), channel_id=1, source_target_pairs={{0,4},{2,6},{4,0},{6,2},{8,12},{10,14},{12,8},{14,10},{16,20},{18,... | collective-permute-start | bytes 786440 | tf_op jit(solution)/shard_map/ppermute | solution.py:500
  47.4 5.7 %collective-permute-start.12 = (bf16[128,768]{1,0:T(8,128)(2,1)S(1)}, bf16[128,768]{1,0:T(8,128)(2,1)S(1)}, u32[]{:S(2)}, u32[]{:S(2)}) collective-permute-start(bf16[128,768]{1,0:T(8,128)(2,1)S(1)} %get-tuple-element.99.refs_6_), channel_id=1, source_target_pairs={{0,1},{1,0},{2,3},{3,2},{4,5},{5,4},{6,7},{7,6},{8,9},{9,8},{10,11... | collective-permute-start | bytes 589832 | tf_op jit(solution)/shard_map/ppermute | solution.py:505
  50.1 4.5 %collective-permute-start.10 = (bf16[192,16,128]{2,1,0:T(8,128)(2,1)S(1)}, bf16[192,16,128]{2,1,0:T(8,128)(2,1)S(1)}, u32[]{:S(2)}, u32[]{:S(2)}) collective-permute-start(bf16[192,16,128]{2,1,0:T(8,128)(2,1)S(1)} %get-tuple-element.95), channel_id=1, source_target_pairs={{0,2},{2,0},{4,6},{6,4},{8,10},{10,8},{12,14},{14,12},{16,18},{18,... | collective-permute-start | bytes 2359304 | tf_op jit(solution)/shard_map/ppermute | solution.py:500
  54.5 4.5 %copy-start.19 = (f32[768]{0:T(1024)S(1)}, f32[768]{0:T(1024)}, u32[]{:S(2)}) copy-start(f32[768]{0:T(1024)} %refs_5_.1) | copy-start | bytes 9220
  54.5 2.3 %collective-permute-start.13 = (bf16[176,16,128]{2,1,0:T(8,128)(2,1)S(1)}, bf16[176,16,128]{2,1,0:T(8,128)(2,1)S(1)}, u32[]{:S(2)}, u32[]{:S(2)}) collective-permute-start(bf16[176,16,128]{2,1,0:T(8,128)(2,1)S(1)} %get-tuple-element.101), channel_id=1, source_target_pairs={{0,2},{2,0},{4,6},{6,4},{8,10},{10,8},{12,14},{14,12},{16,18},{18,... | collective-permute-start | bytes 2162696 | tf_op jit(solution)/shard_map/ppermute | solution.py:500
  57.7 11.2 %collective-permute-start.14 = (bf16[96,16,128]{2,1,0:T(8,128)(2,1)S(1)}, bf16[96,16,128]{2,1,0:T(8,128)(2,1)S(1)}, u32[]{:S(2)}, u32[]{:S(2)}) collective-permute-start(bf16[96,16,128]{2,1,0:T(8,128)(2,1)S(1)} %get-tuple-element.103), channel_id=1, source_target_pairs={{0,4},{2,6},{4,0},{6,2},{8,12},{10,14},{12,8},{14,10},{16,20},{18,... | collective-permute-start | bytes 1179656 | tf_op jit(solution)/shard_map/ppermute | solution.py:500
  58.4 10.2 %collective-permute-start.15 = (bf16[88,16,128]{2,1,0:T(8,128)(2,1)S(1)}, bf16[88,16,128]{2,1,0:T(8,128)(2,1)S(1)}, u32[]{:S(2)}, u32[]{:S(2)}) collective-permute-start(bf16[88,16,128]{2,1,0:T(8,128)(2,1)S(1)} %get-tuple-element.105), channel_id=1, source_target_pairs={{0,8},{2,10},{4,12},{6,14},{8,0},{10,2},{12,4},{14,6},{16,24},{18,... | collective-permute-start | bytes 1081352 | tf_op jit(solution)/shard_map/ppermute | solution.py:500
  58.4 6.7 %collective-permute-start.9 = (bf16[768,128]{1,0:T(8,128)(2,1)S(1)}, bf16[768,128]{1,0:T(8,128)(2,1)S(1)}, u32[]{:S(2)}, u32[]{:S(2)}) collective-permute-start(bf16[768,128]{1,0:T(8,128)(2,1)S(1)} %get-tuple-element.92), channel_id=1, source_target_pairs={{0,1},{1,0},{2,3},{3,2},{4,5},{5,4},{6,7},{7,6},{8,9},{9,8},{10,11... | collective-permute-start | bytes 589832 | tf_op jit(solution)/shard_map/ppermute | solution.py:505
  65.1 22.0 %copy-start.9 = (bf16[16,128,128]{2,1,0:T(8,128)(2,1)S(1)}, bf16[16,128,128]{2,1,0:T(8,128)(2,1)}, u32[]{:S(2)}) copy-start(bf16[16,128,128]{2,1,0:T(8,128)(2,1)} %get-tuple-element.115.refs_1_) | copy-start | bytes 1572868
  69.6 29.7 %copy-start.3 = (bf16[128,16,128]{2,1,0:T(8,128)(2,1)S(1)}, bf16[128,16,128]{2,1,0:T(8,128)(2,1)}, u32[]{:S(2)}) copy-start(bf16[128,16,128]{2,1,0:T(8,128)(2,1)} %param.22) | copy-start | bytes 1572868
  69.6 29.7 %copy-start.16 = (bf16[128,8]{0,1:T(8,128)(2,1)S(1)}, bf16[128,8]{0,1:T(8,128)(2,1)}, u32[]{:S(2)}) copy-start(bf16[128,8]{0,1:T(8,128)(2,1)} %param.34) | copy-start | bytes 6148
  69.6 29.7 %copy-start.17 = (f32[128]{0:T(128)S(1)}, f32[128]{0:T(128)}, u32[]{:S(2)}) copy-start(f32[128]{0:T(128)} %param.28) | copy-start | bytes 1540
  69.6 10.0 %collective-permute-start.16 = (bf16[48,16,128]{2,1,0:T(8,128)(2,1)S(1)}, bf16[48,16,128]{2,1,0:T(8,128)(2,1)S(1)}, u32[]{:S(2)}, u32[]{:S(2)}) collective-permute-start(bf16[48,16,128]{2,1,0:T(8,128)(2,1)S(1)} %get-tuple-element.108), channel_id=1, source_target_pairs={{0,8},{2,10},{4,12},{6,14},{8,0},{10,2},{12,4},{14,6},{16,24},{18,... | collective-permute-start | bytes 589832 | tf_op jit(solution)/shard_map/ppermute | solution.py:500
  69.7 7.8 %collective-permute-start.17 = (bf16[44,16,128]{2,1,0:T(8,128)(2,1)S(1)}, bf16[44,16,128]{2,1,0:T(8,128)(2,1)S(1)}, u32[]{:S(2)}, u32[]{:S(2)}) collective-permute-start(bf16[44,16,128]{2,1,0:T(8,128)(2,1)S(1)} %get-tuple-element.110), channel_id=1, source_target_pairs={{0,16},{2,18},{4,20},{6,22},{8,24},{10,26},{12,28},{14,30},{16,0},... | collective-permute-start | bytes 540680 | tf_op jit(solution)/shard_map/ppermute | solution.py:500
  80.3 6.8 %collective-permute-start.18 = (bf16[24,16,128]{2,1,0:T(8,128)(2,1)S(1)}, bf16[24,16,128]{2,1,0:T(8,128)(2,1)S(1)}, u32[]{:S(2)}, u32[]{:S(2)}) collective-permute-start(bf16[24,16,128]{2,1,0:T(8,128)(2,1)S(1)} %get-tuple-element.112), channel_id=1, source_target_pairs={{0,16},{2,18},{4,20},{6,22},{8,24},{10,26},{12,28},{14,30},{16,0},... | collective-permute-start | bytes 294920 | tf_op jit(solution)/shard_map/ppermute | solution.py:500
  81.7 5.4 %collective-permute-start.19 = (bf16[18,16,128]{2,1,0:T(8,128)(2,1)S(1)}, bf16[18,16,128]{2,1,0:T(8,128)(2,1)S(1)}, u32[]{:S(2)}, u32[]{:S(2)}) collective-permute-start(bf16[18,16,128]{2,1,0:T(8,128)(2,1)S(1)} %get-tuple-element.114), channel_id=1, source_target_pairs={{0,4},{2,6},{4,0},{6,2},{8,12},{10,14},{12,8},{14,10},{16,20},{18,... | collective-permute-start | bytes 221192 | tf_op jit(solution)/shard_map/ppermute | solution.py:500
  83.3 3.8 %collective-permute-start.20 = (bf16[64,128]{1,0:T(8,128)(2,1)S(1)}, bf16[64,128]{1,0:T(8,128)(2,1)S(1)}, u32[]{:S(2)}, u32[]{:S(2)}) collective-permute-start(bf16[64,128]{1,0:T(8,128)(2,1)S(1)} %get-tuple-element.117), channel_id=1, source_target_pairs={{0,1},{1,0},{2,3},{3,2},{4,5},{5,4},{6,7},{7,6},{8,9},{9,8},{10,11... | collective-permute-start | bytes 49160 | tf_op jit(solution)/shard_map/ppermute | solution.py:505
  88.7 18.2 %all-to-all-start = ((f32[32,8,128]{2,1,0:T(8,128)}), f32[32,8,128]{2,1,0:T(8,128)S(1)}, u32[]{:S(2)}, u32[]{:S(2)}) async-start(f32[32,8,128]{2,1,0:T(8,128)} %pair_weight.1.refs_5_), calls=%async_computation | async-start | bytes 262144 | tf_op jit(solution)/shard_map/all_to_all | solution.py:509
  95.0 11.2 %collective-permute-start.21 = (bf16[3,48,384]{2,1,0:T(8,128)(2,1)S(1)}, bf16[3,48,384]{2,1,0:T(8,128)(2,1)S(1)}, u32[]{:S(2)}, u32[]{:S(2)}) collective-permute-start(bf16[3,48,384]{2,1,0:T(8,128)(2,1)S(1)} %get-tuple-element.118.refs_6_), channel_id=1, source_target_pairs={{0,0},{1,16},{2,2},{3,18},{4,4},{5,20},{6,6},{7,22},{8,8},{9,24},{... | collective-permute-start | bytes 331784 | tf_op jit(solution)/shard_map/ppermute | solution.py:785
  99.3 3.8 %collective-permute-start.22 = (bf16[48,128]{1,0:T(8,128)(2,1)S(1)}, bf16[48,128]{1,0:T(8,128)(2,1)S(1)}, u32[]{:S(2)}, u32[]{:S(2)}) collective-permute-start(bf16[48,128]{1,0:T(8,128)(2,1)S(1)} %get-tuple-element.120), channel_id=1, source_target_pairs={{0,1},{1,0},{2,3},{3,2},{4,5},{5,4},{6,7},{7,6},{8,9},{9,8},{10,11... | collective-permute-start | bytes 36872 | tf_op jit(solution)/shard_map/ppermute | solution.py:505

commit v10 on v9

--- a/solution.py
+++ b/solution.py
@@ -435,14 +435,16 @@
         pieces[r][...] = blocks[jnp.bitwise_xor(ids[0], r)].astype(bf16)
 
 
-def finish_kernel(moved, *rest):
-    parts, outs = rest[:-4], rest[-4:]
+def finish_kernel(group, ids, own, moved, terms, *rest):
+    parts, outs = rest[:-5], rest[-5:]
+    stays = jnp.where(ids[1] // group == ids[0], 1.0, 0.0).astype(f32)
     for k in range(3):
-        outs[k][...] = moved[k].astype(f32)
+        outs[k][...] = own[k].astype(f32) * stays + moved[k].astype(f32) * (1.0 - stays)
     total = parts[0][...].astype(f32)
     for part in parts[1:]:
         total = total + part[...].astype(f32)
     outs[3][...] = total
+    outs[4][...] = jnp.sum(terms[...], axis=0)
 
 
 def exit_kernel(toks, noisy, gain, d_res, d_own, *rest):
@@ -703,6 +705,11 @@
 
     masks = [1 << b for b in range(1, copies.bit_length() - 1)]
     masks_b = masks[1:] + masks[:1]
+    (ahead,) = step(
+        "step_ahead",
+        [(kept, got)],
+        [(0, 0, copies // 2, first_tiles, masks[0], masks, 0)],
+    )
     kept_b, sent_b = call(
         functools.partial(second_kernel, copies, toks),
         "second",
@@ -714,6 +721,7 @@
             VMEM((width, own_width), f32),
         ],
         flops=4 * tokens * width * own_width,
+        deps=[ahead[0]],
     )
     got_b = swap_copy(sent_b, 1)
 
@@ -723,19 +731,25 @@
         [noisy3, norm_gain2, d_res, d_own] + d_others,
         [((rows, width), bf16), ((8, 128), f32)],
     )
-    pairs = [(kept, got), (kept_b, got_b)]
+    pairs = [ahead, (kept_b, got_b)]
     parts = copies // 2
     for n, (mask, mask_b) in enumerate(zip(masks, masks_b)):
-        segments = [
-            (0, 0, parts, first_tiles, mask, masks[n:], 0),
-            (1, 0, parts, second_tiles, mask_b, masks_b[n:], 1),
-        ]
+        segments = []
+        if n > 0:
+            segments.append((0, 0, parts, first_tiles, mask, masks[n:], 0))
+        target = len(segments)
+        segments.append((target, 0, parts, second_tiles, mask_b, masks_b[n:], target))
         bias_base = parts * second_tiles
         if n + 1 < len(masks):
-            segments.append((1, bias_base, parts // 2, bias_tiles, mask_b, masks_b[n:-1], 1))
+            segments.append(
+                (target, bias_base, parts // 2, bias_tiles, mask_b, masks_b[n:-1], target)
+            )
         else:
             bias_ready = pairs[1]
-        pairs = step("step_%d" % n, pairs, segments, deps=[exited] if n == 1 else ())
+        if n == 0:
+            pairs = [ahead] + step("step_0", pairs[1:], segments)
+        else:
+            pairs = step("step_%d" % n, pairs, segments, deps=[exited] if n == 1 else ())
         parts //= 2
     bias_pieces = call(
         functools.partial(last_bias_kernel, toks, bias_base, bias_tiles, cols),
@@ -751,7 +765,8 @@
     swaps = []
     for c in range(copies):
         for t in range(toks):
-            swaps.append((c * toks + t, (t * group + c % group) * toks + c // group))
+            if c // group != t:
+                swaps.append((c * toks + t, (t * group + c % group) * toks + c // group))
 
     (weight_grad,) = call(
         functools.partial(pair_weight_kernel, toks),
@@ -779,15 +794,15 @@
         flops=2 * heads * cols * rows * channels * cols,
         deps=[last[0]],
     )
-    weight_grad = jnp.sum(exchange(weight_grad), axis=0)
+    weight_terms = exchange(weight_grad)
     grad_out, singles = last[1], last[2:]
     singles = [singles[0]] + [swap_tok(singles[r], r) for r in range(1, toks)]
     moved = lax.ppermute(last[0], ("copy", "tok"), swaps)
-    grad_query, grad_key, grad_value, grad_single = call(
-        finish_kernel,
+    grad_query, grad_key, grad_value, grad_single, weight_grad = call(
+        functools.partial(finish_kernel, group),
         "finish",
-        [moved] + singles,
-        [((cut, own_width), f32)] * 3 + [((cut, rows), f32)],
+        [where_am_i, last[0], moved, weight_terms] + singles,
+        [((cut, own_width), f32)] * 3 + [((cut, rows), f32), ((heads, channels), f32)],
     )
     return (
         grad_noisy[None],

time: 108 us -> 111 us (1.028)
  waiting for transfers between devices: 44.2 us -> 49 us
  starting transfers between devices: 27.3 us -> 25.7 us
    ppermute x8, waiting for transfers between devices: 20.5 us -> 23.3 us  [swap_tok(): return lax.ppermute(value, 'tok', [(i, i ^ mask) for i in range(size)])]
    ppermute x14, waiting for transfers between devices: 20.7 us -> 22.5 us  [swap_copy(): return lax.ppermute(value, 'copy', [(i, i ^ mask) for i in range(size)])]
    all_to_all x1, starting transfers between devices: 5.09 us -> 3.86 us  [exchange(): return lax.all_to_all(value, ('copy', 'tok'), 0, 0)]
    pallas_call x21 -> x22, Pallas kernels: 29.6 us -> 30.7 us  [call(): pl.pallas_call(whole, name=name, out_shape=[jax.ShapeDtypeStruct(one[0],...]
  transfers between devices with their start and end apart: 24 -> 24, of which waited for: 16 -> 17; matrix products, arithmetic and copies ran while one was open for 0% -> 0% of each run, Pallas kernels for 12% -> 9%
where the time goes in v10:
time: 111 us
  waiting for transfers between devices  49 us (44%)
  Pallas kernels  30.7 us (28%)
  starting transfers between devices  25.7 us (23%)
  local copies, waits for them, and re-layouts  4.05 us (4%)
    pallas_call x22, Pallas kernels, call(): pl.pallas_call(whole, name=name, out_shape=[jax.ShapeDtypeStruct(one[0],...  30.7 us
    ppermute x8, waiting for transfers between devices, swap_tok(): return lax.ppermute(value, 'tok', [(i, i ^ mask) for i in range(size)])  23.3 us
    ppermute x14, waiting for transfers between devices, swap_copy(): return lax.ppermute(value, 'copy', [(i, i ^ mask) for i in range(size)])  22.5 us
    ppermute x14, starting transfers between devices, swap_copy(): return lax.ppermute(value, 'copy', [(i, i ^ mask) for i in range(size)])  13 us
    ppermute x8, starting transfers between devices, swap_tok(): return lax.ppermute(value, 'tok', [(i, i ^ mask) for i in range(size)])  4.64 us
    ppermute x1, starting transfers between devices, per_device(): moved = lax.ppermute(last[0], ('copy', 'tok'), swaps)  4.27 us
    unnamed x42, local copies, waits for them, and re-layouts  4.05 us
    all_to_all x1, starting transfers between devices, exchange(): return lax.all_to_all(value, ('copy', 'tok'), 0, 0)  3.86 us
  transfers between devices with their start and end apart: 24, of which 17 were waited for; matrix products, arithmetic and copies ran while one was open for 0% of the time, Pallas kernels for 9%

profile of v10, /device:TPU:2, one launch (start us, length us, event | category | flops | bytes accessed | tf_op | source)
XLA Modules:
  0.0 111.1 jit_solution(12733319979894163817)
XLA Ops:
  0.6 0.6 pad_add_fusion.refs_0_
  1.2 4.2 %enter.1 = (bf16[128,768]{1,0:T(8,128)(2,1)}, bf16[16,128,128]{2,1,0:T(8,128)(2,1)}, f32[256,128]{1,0:T(8,128)}, f32[1,256]{1,0:T(1,128)}, bf16[2,64,128]{2,1,0:T(8,128)(2,1)}) custom-call(s32[2]{0:T(128)} %pad_add_fusion.refs_0_, bf16[128,768]{1,0:T(8,128)(2,1)} %bitcast.20, bf16[128,768]{1,0:T(8,128)(2,1)} %refs_2_.2, s32[1,128]{1,0:T(1,128)} %bitcast.30, ...), custom_call_target="tpu_custom_call" | custom-call | flops 67108864 | bytes 1860808 | tf_op jit(solution)/shard_map/enter/pallas_call | solution.py:79
  5.4 0.1 collective-permute-start.3
  5.5 2.1 %collective-permute-start = (bf16[2,64,128]{2,1,0:T(8,128)(2,1)}, bf16[2,64,128]{2,1,0:T(8,128)(2,1)S(1)}, u32[]{:S(2)}, u32[]{:S(2)}) collective-permute-start(bf16[2,64,128]{2,1,0:T(8,128)(2,1)} %get-tuple-element.72.refs_0_), channel_id=1, source_target_pairs={{0,8},{2,10},{4,12},{6,14},{8,0},{10,2},{12,4},{14,6},{16,24},{18,... | collective-permute-start | bytes 98312 | tf_op jit(solution)/shard_map/ppermute | solution.py:502
  7.6 2.6 %collective-permute-start.1 = (bf16[2,64,128]{2,1,0:T(8,128)(2,1)}, bf16[2,64,128]{2,1,0:T(8,128)(2,1)S(1)}, u32[]{:S(2)}, u32[]{:S(2)}) collective-permute-start(bf16[2,64,128]{2,1,0:T(8,128)(2,1)} %get-tuple-element.72.refs_0_), channel_id=1, source_target_pairs={{0,16},{2,18},{4,20},{6,22},{8,24},{10,26},{12,28},{14,30},{16,0},... | collective-permute-start | bytes 98312 | tf_op jit(solution)/shard_map/ppermute | solution.py:502
  10.2 2.7 %collective-permute-done.1.refs_2_ = bf16[2,64,128]{2,1,0:T(8,128)(2,1)S(1)} collective-permute-done((bf16[2,64,128]{2,1,0:T(8,128)(2,1)}, bf16[2,64,128]{2,1,0:T(8,128)(2,1)S(1)}, u32[]{:S(2)}, u32[]{:S(2)}) %collective-permute-start.1) | collective-permute-done | bytes 32800 | tf_op jit(solution)/shard_map/ppermute | solution.py:502
  12.9 3.2 %collective-permute-done.2.refs_3_ = bf16[2,64,128]{2,1,0:T(8,128)(2,1)S(1)} collective-permute-done((bf16[2,64,128]{2,1,0:T(8,128)(2,1)}, bf16[2,64,128]{2,1,0:T(8,128)(2,1)S(1)}, u32[]{:S(2)}, u32[]{:S(2)}) %collective-permute-start.2) | collective-permute-done | bytes 32800 | tf_op jit(solution)/shard_map/ppermute | solution.py:502
  16.1 0.8 copy-done.15
  16.9 1.6 %collective-permute-start.4 = (bf16[4,64,128]{2,1,0:T(8,128)(2,1)S(1)}, bf16[4,64,128]{2,1,0:T(8,128)(2,1)S(1)}, u32[]{:S(2)}, u32[]{:S(2)}) collective-permute-start(bf16[4,64,128]{2,1,0:T(8,128)(2,1)S(1)} %get-tuple-element.78), channel_id=1, source_target_pairs={{0,1},{1,0},{2,3},{3,2},{4,5},{5,4},{6,7},{7,6},{8,9},{9,8},{10,11... | collective-permute-start | bytes 196616 | tf_op jit(solution)/shard_map/ppermute | solution.py:507
  18.4 1.3 %copy-done.5 = bf16[768,768]{1,0:T(8,128)(2,1)S(1)} copy-done((bf16[768,768]{1,0:T(8,128)(2,1)S(1)}, bf16[768,768]{1,0:T(8,128)(2,1)}, u32[]{:S(2)}) %copy-start.5) | copy-done | bytes 1179672
  19.7 1.3 %copy-done.6 = bf16[768,768]{1,0:T(8,128)(2,1)S(1)} copy-done((bf16[768,768]{1,0:T(8,128)(2,1)S(1)}, bf16[768,768]{1,0:T(8,128)(2,1)}, u32[]{:S(2)}) %copy-start.6) | copy-done | bytes 1179672
  21.0 0.7 copy-done.13
  21.6 0.8 stage.1.refs_1_.refs_2_
  22.5 1.6 %collective-permute-start.5 = (bf16[2,4,64,128]{3,2,1,0:T(8,128)(2,1)S(1)}, bf16[2,4,64,128]{3,2,1,0:T(8,128)(2,1)S(1)}, u32[]{:S(2)}, u32[]{:S(2)}) collective-permute-start(bf16[2,4,64,128]{3,2,1,0:T(8,128)(2,1)S(1)} %join_tok.1.refs_0_), channel_id=1, source_target_pairs={{0,4},{2,6},{4,0},{6,2},{8,12},{10,14},{12,8},{14,10},{16,20},{18,... | collective-permute-start | bytes 393224 | tf_op jit(solution)/shard_map/ppermute | solution.py:502
  24.1 1.4 %project.1 = (bf16[256,768]{1,0:T(8,128)(2,1)S(1)}, bf16[384,256]{1,0:T(8,128)(2,1)S(1)}, bf16[384,256]{1,0:T(8,128)(2,1)S(1)}, bf16[384,256]{1,0:T(8,128)(2,1)S(1)}) custom-call(s32[2]{0:T(128)S(1)} %copy-done.13, bf16[3,768,384]{2,1,0:T(8,128)(2,1)S(1)} %stage.1.refs_1_.refs_2_, bf16[128,768]{1,0:T(8,128)(2,1)S(1)} %copy-done.11, ...), custom_call_target="tpu_custom_call" | custom-call | flops 452984832 | bytes 3145736 | tf_op jit(solution)/shard_map/project/pallas_call | solution.py:79
  25.5 2.0 %collective-permute-done.5.refs_1_ = bf16[2,4,64,128]{3,2,1,0:T(8,128)(2,1)S(1)} collective-permute-done((bf16[2,4,64,128]{3,2,1,0:T(8,128)(2,1)S(1)}, bf16[2,4,64,128]{3,2,1,0:T(8,128)(2,1)S(1)}, u32[]{:S(2)}, u32[]{:S(2)}) %collective-permute-start.5) | collective-permute-done | bytes 131104 | tf_op jit(solution)/shard_map/ppermute | solution.py:502
  27.6 0.1 collective-permute-start.6
  27.6 1.5 %collective-permute-done.6.refs_5_ = bf16[2,2,4,64,128]{4,3,2,1,0:T(8,128)(2,1)S(1)} collective-permute-done((bf16[2,2,4,64,128]{4,3,2,1,0:T(8,128)(2,1)S(1)}, bf16[2,2,4,64,128]{4,3,2,1,0:T(8,128)(2,1)S(1)}, u32[]{:S(2)}, u32[]{:S(2)}) %collective-permute-start.6) | collective-permute-done | bytes 262176 | tf_op jit(solution)/shard_map/ppermute | solution.py:502
  29.2 2.1 %attention.1 = (bf16[4,256,256]{2,1,0:T(8,128)(2,1)S(1)}, bf16[256,384]{1,0:T(8,128)(2,1)S(1)}, bf16[128,384]{1,0:T(8,128)(2,1)S(1)}, bf16[128,384]{1,0:T(8,128)(2,1)S(1)}) custom-call(s32[2]{0:T(128)S(1)} %copy-done.14, bf16[384,256]{1,0:T(8,128)(2,1)S(1)} %get-tuple-element.75.refs_1_, bf16[384,256]{1,0:T(8,128)(2,1)S(1)} %get-tuple-element.76.refs_2_, ...), custom_call_target="tpu_custom_call" | custom-call | flops 100663296 | bytes 2163720 | tf_op jit(solution)/shard_map/attention/pallas_call | solution.py:79
  31.3 0.6 collective-permute-start.7
  32.0 0.9 down.1
  32.9 3.4 %collective-permute-done.7.refs_6_ = bf16[128,384]{1,0:T(8,128)(2,1)S(1)} collective-permute-done((bf16[128,384]{1,0:T(8,128)(2,1)S(1)}, bf16[128,384]{1,0:T(8,128)(2,1)S(1)}, u32[]{:S(2)}, u32[]{:S(2)}) %collective-permute-start.7) | collective-permute-done | bytes 98336 | tf_op jit(solution)/shard_map/ppermute | solution.py:507
  36.2 4.3 %hidden.1 = (f32[128,768]{1,0:T(8,128)S(1)}, bf16[128,768]{1,0:T(8,128)(2,1)S(1)}, bf16[384,128]{1,0:T(8,128)(2,1)S(1)}, bf16[384,128]{1,0:T(8,128)(2,1)S(1)}) custom-call(s32[2]{0:T(128)S(1)} %copy-done.14, bf16[128,768]{1,0:T(8,128)(2,1)S(1)} %get-tuple-element.68.refs_1_.refs_0_, bf16[128,768]{1,0:T(8,128)(2,1)S(1)} %get-tuple-element.69.refs_2_, ...), custom_call_target="tpu_custom_call" | custom-call | flops 1509949440 | bytes 8064008 | tf_op jit(solution)/shard_map/hidden/pallas_call | solution.py:79
  40.6 0.6 collective-permute-start.8
  41.2 4.1 %collective-permute-done.8.refs_6_ = bf16[384,128]{1,0:T(8,128)(2,1)S(1)} collective-permute-done((bf16[384,128]{1,0:T(8,128)(2,1)S(1)}, bf16[384,128]{1,0:T(8,128)(2,1)S(1)}, u32[]{:S(2)}, u32[]{:S(2)}) %collective-permute-start.8) | collective-permute-done | bytes 98336 | tf_op jit(solution)/shard_map/ppermute | solution.py:507
  45.3 2.0 %backward.1 = (bf16[384,256]{1,0:T(8,128)(2,1)S(1)}, bf16[384,256]{1,0:T(8,128)(2,1)S(1)}, bf16[384,256]{1,0:T(8,128)(2,1)S(1)}, bf16[64,16,128]{2,1,0:T(8,128)(...) custom-call(s32[2]{0:T(128)S(1)} %copy-done.14, ...), custom_call_target="tpu_custom_call" | custom-call | flops 201326592 | bytes 2818056 | tf_op jit(solution)/shard_map/backward/pallas_call | solution.py:79
  47.3 2.1 %first.1 = (bf16[192,16,128]{2,1,0:T(8,128)(2,1)S(1)}, bf16[192,16,128]{2,1,0:T(8,128)(2,1)S(1)}, f32[768,128]{1,0:T(8,128)S(1)}, bf16[768,128]{1,0:T(8,128)(2,1)S(1)}) custom-call(s32[2]{0:T(128)S(1)} %copy-done.14, bf16[3,768,384]{2,1,0:T(8,128)(2,1)S(1)} %stage.1.refs_1_.refs_2_, bf16[256,768]{1,0:T(8,128)(2,1)S(1)} %get-tuple-element.84.refs_2_.refs_1_, ...), custom_call_target="tpu_custom_call" | custom-call | flops 754974720 | bytes 4915208 | tf_op jit(solution)/shard_map/first/pallas_call | solution.py:79
  49.4 0.1 collective-permute-start.10
  49.5 1.6 %collective-permute-start.12 = (bf16[64,16,128]{2,1,0:T(8,128)(2,1)S(1)}, bf16[64,16,128]{2,1,0:T(8,128)(2,1)S(1)}, u32[]{:S(2)}, u32[]{:S(2)}) collective-permute-start(bf16[64,16,128]{2,1,0:T(8,128)(2,1)S(1)} %get-tuple-element.101), channel_id=1, source_target_pairs={{0,4},{2,6},{4,0},{6,2},{8,12},{10,14},{12,8},{14,10},{16,20},{18,... | collective-permute-start | bytes 786440 | tf_op jit(solution)/shard_map/ppermute | solution.py:502
  51.1 0.5 collective-permute-start.13
  51.6 0.1 collective-permute-done.10.refs_2_
  51.7 0.7 step_ahead.1
  52.5 5.6 %collective-permute-done.13.refs_7_ = bf16[128,768]{1,0:T(8,128)(2,1)S(1)} collective-permute-done((bf16[128,768]{1,0:T(8,128)(2,1)S(1)}, bf16[128,768]{1,0:T(8,128)(2,1)S(1)}, u32[]{:S(2)}, u32[]{:S(2)}) %collective-permute-start.13) | collective-permute-done | bytes 196640 | tf_op jit(solution)/shard_map/ppermute | solution.py:507
  58.0 0.2 collective-permute-done.12.refs_5_
  58.2 1.4 %second.1 = (bf16[176,16,128]{2,1,0:T(8,128)(2,1)S(1)}, bf16[176,16,128]{2,1,0:T(8,128)(2,1)S(1)}) custom-call(s32[2]{0:T(128)S(1)} %copy-done.14, bf16[256,768]{1,0:T(8,128)(2,1)S(1)} %get-tuple-element.84.refs_2_.refs_1_, bf16[256,384]{1,0:T(8,128)(2,1)S(1)} %get-tuple-element.99.refs_2_, bf16[384,256]{1,0:T(8,128)(2,1)S(1)} %get-tuple-element.91.refs_5_.refs_3_, ...), custom_call_target="tpu_custom_call" | custom-call | flops 301989888 | bytes 3145736 | tf_op jit(solution)/shard_map/second/pallas_call | solution.py:79
  59.6 0.1 collective-permute-start.14
  59.7 1.6 %collective-permute-start.11 = (bf16[96,16,128]{2,1,0:T(8,128)(2,1)S(1)}, bf16[96,16,128]{2,1,0:T(8,128)(2,1)S(1)}, u32[]{:S(2)}, u32[]{:S(2)}) collective-permute-start(bf16[96,16,128]{2,1,0:T(8,128)(2,1)S(1)} %get-tuple-element.98), channel_id=1, source_target_pairs={{0,4},{2,6},{4,0},{6,2},{8,12},{10,14},{12,8},{14,10},{16,20},{18,... | collective-permute-start | bytes 1179656 | tf_op jit(solution)/shard_map/ppermute | solution.py:502
  61.3 0.6 collective-permute-done.14.refs_2_
  61.8 0.7 step_0.1
  62.6 0.1 collective-permute-start.15
  62.6 0.6 collective-permute-start.9
  63.3 6.4 %collective-permute-done.9.refs_4_ = bf16[768,128]{1,0:T(8,128)(2,1)S(1)} collective-permute-done((bf16[768,128]{1,0:T(8,128)(2,1)S(1)}, bf16[768,128]{1,0:T(8,128)(2,1)S(1)}, u32[]{:S(2)}, u32[]{:S(2)}) %collective-permute-start.9) | collective-permute-done | bytes 196640 | tf_op jit(solution)/shard_map/ppermute | solution.py:507
  69.7 1.2 %exit.1 = (bf16[128,768]{1,0:T(8,128)(2,1)}, f32[8,128]{1,0:T(8,128)S(1)}) custom-call(bf16[128,768]{1,0:T(8,128)(2,1)S(1)} %get-tuple-element.68.refs_1_.refs_0_, f32[1,768]{1,0:T(1,128)S(1)} %reshape.49.refs_1_, f32[128,768]{1,0:T(8,128)S(1)} %get-tuple-element.83.refs_2_, f32[768,128]{1,0:T(8,128)S(1)} %get-tuple-element.92.refs_3_, ...), custom_call_target="tpu_custom_call" | custom-call | bytes 1383424 | tf_op jit(solution)/shard_map/exit/pallas_call | solution.py:79
  70.9 0.3 collective-permute-done.11.refs_2_
  71.2 1.9 %collective-permute-done.15.refs_4_ = bf16[88,16,128]{2,1,0:T(8,128)(2,1)S(1)} collective-permute-done((bf16[88,16,128]{2,1,0:T(8,128)(2,1)S(1)}, bf16[88,16,128]{2,1,0:T(8,128)(2,1)S(1)}, u32[]{:S(2)}, u32[]{:S(2)}) %collective-permute-start.15) | collective-permute-done | bytes 360480 | tf_op jit(solution)/shard_map/ppermute | solution.py:502
  73.1 0.7 step_1.1
  73.9 0.4 collective-permute-start.16
  74.2 0.6 collective-permute-start.17
  74.9 9.9 %collective-permute-done.17.refs_4_.refs_2_ = bf16[44,16,128]{2,1,0:T(8,128)(2,1)S(1)} collective-permute-done((bf16[44,16,128]{2,1,0:T(8,128)(2,1)S(1)}, bf16[44,16,128]{2,1,0:T(8,128)(2,1)S(1)}, u32[]{:S(2)}, u32[]{:S(2)}) %collective-permute-start.17) | collective-permute-done | bytes 180256 | tf_op jit(solution)/shard_map/ppermute | solution.py:502
  84.8 0.6 step_2.1
  85.4 0.7 collective-permute-start.18
  86.1 1.5 %collective-permute-start.19 = (bf16[18,16,128]{2,1,0:T(8,128)(2,1)S(1)}, bf16[18,16,128]{2,1,0:T(8,128)(2,1)S(1)}, u32[]{:S(2)}, u32[]{:S(2)}) collective-permute-start(bf16[18,16,128]{2,1,0:T(8,128)(2,1)S(1)} %get-tuple-element.115), channel_id=1, source_target_pairs={{0,4},{2,6},{4,0},{6,2},{8,12},{10,14},{12,8},{14,10},{16,20},{18,... | collective-permute-start | bytes 221192 | tf_op jit(solution)/shard_map/ppermute | solution.py:502
  87.7 0.6 last_bias.1
  88.2 0.6 collective-permute-start.20
  88.8 3.2 %collective-permute-done.20.refs_3_.refs_5_ = bf16[64,128]{1,0:T(8,128)(2,1)S(1)} collective-permute-done((bf16[64,128]{1,0:T(8,128)(2,1)S(1)}, bf16[64,128]{1,0:T(8,128)(2,1)S(1)}, u32[]{:S(2)}, u32[]{:S(2)}) %collective-permute-start.20) | collective-permute-done | bytes 16416 | tf_op jit(solution)/shard_map/ppermute | solution.py:507
  92.0 1.5 %pair_weight.1.refs_5_ = f32[32,8,128]{2,1,0:T(8,128)} custom-call(s32[2]{0:T(128)S(1)} %copy-done.14, bf16[16,128,128]{2,1,0:T(8,128)(2,1)S(1)} %copy-done.9, bf16[64,128]{1,0:T(8,128)(2,1)S(1)} %get-tuple-element.117.refs_2_.refs_4_, bf16[64,128]{1,0:T(8,128)(2,1)S(1)} %collective-permute-done.20.refs_3_.refs_5_, ...), custom_call_target="tpu_custom_call" | custom-call | flops 67108864 | bytes 688136 | tf_op jit(solution)/shard_map/pair_weight/pallas_call | solution.py:79
  93.6 3.9 %all-to-all-start = ((f32[32,8,128]{2,1,0:T(8,128)}), f32[32,8,128]{2,1,0:T(8,128)S(1)}, u32[]{:S(2)}, u32[]{:S(2)}) async-start(f32[32,8,128]{2,1,0:T(8,128)} %pair_weight.1.refs_5_), calls=%async_computation | async-start | bytes 262144 | tf_op jit(solution)/shard_map/all_to_all | solution.py:511
  97.5 1.2 %last.1 = (bf16[3,48,384]{2,1,0:T(8,128)(2,1)S(1)}, f32[48,384]{1,0:T(8,128)}, bf16[48,128]{1,0:T(8,128)(2,1)S(1)}, bf16[48,128]{1,0:T(8,128)(2,1)S(1)}) custom-call(s32[2]{0:T(128)S(1)} %copy-done.14, bf16[24,16,128]{2,1,0:T(8,128)(2,1)S(1)} %get-tuple-element.112.refs_3_.refs_1_, bf16[24,16,128]{2,1,0:T(8,128)(2,1)S(1)} %collective-permute-done.18.refs_4_.refs_2_, ...), custom_call_target="tpu_custom_call" | custom-call | bytes 552968 | tf_op jit(solution)/shard_map/last/pallas_call | solution.py:79
  98.7 4.3 %collective-permute-start.21 = (bf16[3,48,384]{2,1,0:T(8,128)(2,1)S(1)}, bf16[3,48,384]{2,1,0:T(8,128)(2,1)S(1)}, u32[]{:S(2)}, u32[]{:S(2)}) collective-permute-start(bf16[3,48,384]{2,1,0:T(8,128)(2,1)S(1)} %get-tuple-element.119.refs_1_.refs_6_), channel_id=1, source_target_pairs={{1,16},{3,18},{5,20},{7,22},{9,24},{11,26},{13,28},{15,30},{16,1},... | collective-permute-start | bytes 331784 | tf_op jit(solution)/shard_map/ppermute | solution.py:800
  103.0 0.1 collective-permute-start.22
  103.1 2.9 %pair.1 = bf16[2048,128]{1,0:T(8,128)(2,1)} custom-call(s32[2]{0:T(128)S(1)} %copy-done.14, bf16[2048,128]{1,0:T(8,128)(2,1)S(1)} %bitcast.19, f32[1,128]{1,0:T(1,128)S(1)} %bitcast.26, bf16[8,128]{1,0:T(8,128)(2,1)S(1)} %bitcast.24, bf16[64,128]{1,0:T(8,128)(2,1)S(1)} %get-tuple-element.117.refs_2_.refs_4_, ...), custom_call_target="tpu_custom_call" | custom-call | flops 67108864 | bytes 1083912 | tf_op jit(solution)/shard_map/pair/pallas_call | solution.py:79
  106.0 0.7 collective-permute-done.22.refs_5_
  106.7 3.1 %collective-permute-done.21.refs_2_ = bf16[3,48,384]{2,1,0:T(8,128)(2,1)S(1)} collective-permute-done((bf16[3,48,384]{2,1,0:T(8,128)(2,1)S(1)}, bf16[3,48,384]{2,1,0:T(8,128)(2,1)S(1)}, u32[]{:S(2)}, u32[]{:S(2)}) %collective-permute-start.21) | collective-permute-done | bytes 110624 | tf_op jit(solution)/shard_map/ppermute | solution.py:800
  109.8 1.2 %finish.1 = (f32[48,384]{1,0:T(8,128)}, f32[48,384]{1,0:T(8,128)}, f32[48,384]{1,0:T(8,128)}, f32[48,128]{1,0:T(8,128)}, f32[8,128]{1,0:T(8,128)}) custom-call(s32[2]{0:T(128)S(1)} %copy-done.14, bf16[3,48,384]{2,1,0:T(8,128)(2,1)S(1)} %get-tuple-element.119.refs_1_.refs_6_, bf16[3,48,384]{2,1,0:T(8,128)(2,1)S(1)} %collective-permute-done.21.refs_2_, ...), custom_call_target="tpu_custom_call" | custom-call | bytes 626696 | tf_op jit(solution)/shard_map/finish/pallas_call | solution.py:79
  (51 shorter events, 0.2 us)
Async XLA Ops:
  0.6 17.8 %copy-start.4 = (bf16[768,768]{1,0:T(8,128)(2,1)S(1)}, bf16[768,768]{1,0:T(8,128)(2,1)}, u32[]{:S(2)}) copy-start(bf16[768,768]{1,0:T(8,128)(2,1)} %refs_1_.3) | copy-start | bytes 3538948
  5.4 10.7 %collective-permute-start.3 = (bf16[128,768]{1,0:T(8,128)(2,1)}, bf16[128,768]{1,0:T(8,128)(2,1)S(1)}, u32[]{:S(2)}, u32[]{:S(2)}) collective-permute-start(bf16[128,768]{1,0:T(8,128)(2,1)} %get-tuple-element.73.refs_2_), channel_id=1, source_target_pairs={{0,1},{1,0},{2,3},{3,2},{4,5},{5,4},{6,7},{7,6},{8,9},{9,8},{10,11... | collective-permute-start | bytes 589832 | tf_op jit(solution)/shard_map/ppermute | solution.py:507
  5.5 4.7 %collective-permute-start = (bf16[2,64,128]{2,1,0:T(8,128)(2,1)}, bf16[2,64,128]{2,1,0:T(8,128)(2,1)S(1)}, u32[]{:S(2)}, u32[]{:S(2)}) collective-permute-start(bf16[2,64,128]{2,1,0:T(8,128)(2,1)} %get-tuple-element.72.refs_0_), channel_id=1, source_target_pairs={{0,8},{2,10},{4,12},{6,14},{8,0},{10,2},{12,4},{14,6},{16,24},{18,... | collective-permute-start | bytes 98312 | tf_op jit(solution)/shard_map/ppermute | solution.py:502
  7.6 5.3 %collective-permute-start.1 = (bf16[2,64,128]{2,1,0:T(8,128)(2,1)}, bf16[2,64,128]{2,1,0:T(8,128)(2,1)S(1)}, u32[]{:S(2)}, u32[]{:S(2)}) collective-permute-start(bf16[2,64,128]{2,1,0:T(8,128)(2,1)} %get-tuple-element.72.refs_0_), channel_id=1, source_target_pairs={{0,16},{2,18},{4,20},{6,22},{8,24},{10,26},{12,28},{14,30},{16,0},... | collective-permute-start | bytes 98312 | tf_op jit(solution)/shard_map/ppermute | solution.py:502
  10.2 5.9 %collective-permute-start.2 = (bf16[2,64,128]{2,1,0:T(8,128)(2,1)}, bf16[2,64,128]{2,1,0:T(8,128)(2,1)S(1)}, u32[]{:S(2)}, u32[]{:S(2)}) collective-permute-start(bf16[2,64,128]{2,1,0:T(8,128)(2,1)} %get-tuple-element.72.refs_0_), channel_id=1, source_target_pairs={{0,24},{2,26},{4,28},{6,30},{8,16},{10,18},{12,20},{14,22},{16,8},... | collective-permute-start | bytes 98312 | tf_op jit(solution)/shard_map/ppermute | solution.py:502
  16.1 0.8 copy-start.15
  16.9 5.5 %collective-permute-start.4 = (bf16[4,64,128]{2,1,0:T(8,128)(2,1)S(1)}, bf16[4,64,128]{2,1,0:T(8,128)(2,1)S(1)}, u32[]{:S(2)}, u32[]{:S(2)}) collective-permute-start(bf16[4,64,128]{2,1,0:T(8,128)(2,1)S(1)} %get-tuple-element.78), channel_id=1, source_target_pairs={{0,1},{1,0},{2,3},{3,2},{4,5},{5,4},{6,7},{7,6},{8,9},{9,8},{10,11... | collective-permute-start | bytes 196616 | tf_op jit(solution)/shard_map/ppermute | solution.py:507
  18.4 1.3 %copy-start.5 = (bf16[768,768]{1,0:T(8,128)(2,1)S(1)}, bf16[768,768]{1,0:T(8,128)(2,1)}, u32[]{:S(2)}) copy-start(bf16[768,768]{1,0:T(8,128)(2,1)} %refs_2_.3) | copy-start | bytes 3538948
  19.7 1.3 %copy-start.6 = (bf16[768,768]{1,0:T(8,128)(2,1)S(1)}, bf16[768,768]{1,0:T(8,128)(2,1)}, u32[]{:S(2)}) copy-start(bf16[768,768]{1,0:T(8,128)(2,1)} %refs_3_.1) | copy-start | bytes 3538948
  21.0 0.7 copy-start.13
  21.6 7.6 %copy-start.12 = (f32[256,128]{1,0:T(8,128)S(1)}, f32[256,128]{1,0:T(8,128)}, u32[]{:S(2)}) copy-start(f32[256,128]{1,0:T(8,128)} %get-tuple-element.79.refs_6_) | copy-start | bytes 393220
  22.4 1.7 %copy-start.11 = (bf16[128,768]{1,0:T(8,128)(2,1)S(1)}, bf16[128,768]{1,0:T(8,128)(2,1)}, u32[]{:S(2)}) copy-start(bf16[128,768]{1,0:T(8,128)(2,1)} %get-tuple-element.73.refs_2_) | copy-start | bytes 589828
  22.4 9.5 %copy-start.2 = (bf16[1536,768]{1,0:T(8,128)(2,1)S(1)}, bf16[1536,768]{1,0:T(8,128)(2,1)}, u32[]{:S(2)}) copy-start(bf16[1536,768]{1,0:T(8,128)(2,1)} %refs_1_.2) | copy-start | bytes 7077892
  22.4 6.7 %copy-start.14 = (s32[2]{0:T(128)S(1)}, s32[2]{0:T(128)}, u32[]{:S(2)}) copy-start(s32[2]{0:T(128)} %pad_add_fusion.refs_0_) | copy-start | bytes 28
  22.5 6.7 %copy-start.18 = (f32[1,256]{1,0:T(1,128)S(1)}, f32[1,256]{1,0:T(1,128)}, u32[]{:S(2)}) copy-start(f32[1,256]{1,0:T(1,128)} %get-tuple-element.80.refs_7_) | copy-start | bytes 3076
  22.5 9.5 %copy-start.20 = (f32[768]{0:T(1024)S(1)}, f32[768]{0:T(1024)}, u32[]{:S(2)}) copy-start(f32[768]{0:T(1024)} %param.29) | copy-start | bytes 9220
  22.5 9.5 %copy-start.8 = (bf16[1,128,768]{2,1,0:T(8,128)(2,1)S(1)}, bf16[1,128,768]{2,1,0:T(8,128)(2,1)}, u32[]{:S(2)}) copy-start(bf16[1,128,768]{2,1,0:T(8,128)(2,1)} %param.20) | copy-start | bytes 589828
  22.5 9.5 %copy-start.10 = (bf16[1,128,768]{2,1,0:T(8,128)(2,1)S(1)}, bf16[1,128,768]{2,1,0:T(8,128)(2,1)}, u32[]{:S(2)}) copy-start(bf16[1,128,768]{2,1,0:T(8,128)(2,1)} %param.39) | copy-start | bytes 589828
  22.5 5.0 %collective-permute-start.5 = (bf16[2,4,64,128]{3,2,1,0:T(8,128)(2,1)S(1)}, bf16[2,4,64,128]{3,2,1,0:T(8,128)(2,1)S(1)}, u32[]{:S(2)}, u32[]{:S(2)}) collective-permute-start(bf16[2,4,64,128]{3,2,1,0:T(8,128)(2,1)S(1)} %join_tok.1.refs_0_), channel_id=1, source_target_pairs={{0,4},{2,6},{4,0},{6,2},{8,12},{10,14},{12,8},{14,10},{16,20},{18,... | collective-permute-start | bytes 393224 | tf_op jit(solution)/shard_map/ppermute | solution.py:502
  24.1 12.1 %copy-start.7 = (bf16[768,768]{1,0:T(8,128)(2,1)S(1)}, bf16[768,768]{1,0:T(8,128)(2,1)}, u32[]{:S(2)}) copy-start(bf16[768,768]{1,0:T(8,128)(2,1)} %refs_7_.1) | copy-start | bytes 3538948
  27.5 8.7 %copy-start.1 = (bf16[768,1536]{1,0:T(8,128)(2,1)S(1)}, bf16[768,1536]{1,0:T(8,128)(2,1)}, u32[]{:S(2)}) copy-start(bf16[768,1536]{1,0:T(8,128)(2,1)} %refs_9_.1) | copy-start | bytes 7077892
  27.6 1.6 %collective-permute-start.6 = (bf16[2,2,4,64,128]{4,3,2,1,0:T(8,128)(2,1)S(1)}, bf16[2,2,4,64,128]{4,3,2,1,0:T(8,128)(2,1)S(1)}, u32[]{:S(2)}, u32[]{:S(2)}) collective-permute-start(bf16[2,2,4,64,128]{4,3,2,1,0:T(8,128)(2,1)S(1)} %join_y.1.refs_4_), channel_id=1, source_target_pairs={{0,2},{2,0},{4,6},{6,4},{8,10},{10,8},{12,14},{14,12},{16,18},{18,... | collective-permute-start | bytes 786440 | tf_op jit(solution)/shard_map/ppermute | solution.py:502
  29.2 7.1 %copy-start = (bf16[768,1536]{1,0:T(8,128)(2,1)S(1)}, bf16[768,1536]{1,0:T(8,128)(2,1)}, u32[]{:S(2)}) copy-start(bf16[768,1536]{1,0:T(8,128)(2,1)} %refs_8_.1) | copy-start | bytes 7077892
  31.3 4.9 %collective-permute-start.7 = (bf16[128,384]{1,0:T(8,128)(2,1)S(1)}, bf16[128,384]{1,0:T(8,128)(2,1)S(1)}, u32[]{:S(2)}, u32[]{:S(2)}) collective-permute-start(bf16[128,384]{1,0:T(8,128)(2,1)S(1)} %get-tuple-element.82), channel_id=1, source_target_pairs={{0,1},{1,0},{2,3},{3,2},{4,5},{5,4},{6,7},{7,6},{8,9},{9,8},{10,11... | collective-permute-start | bytes 294920 | tf_op jit(solution)/shard_map/ppermute | solution.py:507
  40.6 4.7 %collective-permute-start.8 = (bf16[384,128]{1,0:T(8,128)(2,1)S(1)}, bf16[384,128]{1,0:T(8,128)(2,1)S(1)}, u32[]{:S(2)}, u32[]{:S(2)}) collective-permute-start(bf16[384,128]{1,0:T(8,128)(2,1)S(1)} %get-tuple-element.87), channel_id=1, source_target_pairs={{0,1},{1,0},{2,3},{3,2},{4,5},{5,4},{6,7},{7,6},{8,9},{9,8},{10,11... | collective-permute-start | bytes 294920 | tf_op jit(solution)/shard_map/ppermute | solution.py:507
  49.4 2.4 %collective-permute-start.10 = (bf16[192,16,128]{2,1,0:T(8,128)(2,1)S(1)}, bf16[192,16,128]{2,1,0:T(8,128)(2,1)S(1)}, u32[]{:S(2)}, u32[]{:S(2)}) collective-permute-start(bf16[192,16,128]{2,1,0:T(8,128)(2,1)S(1)} %get-tuple-element.96), channel_id=1, source_target_pairs={{0,2},{2,0},{4,6},{6,4},{8,10},{10,8},{12,14},{14,12},{16,18},{18,... | collective-permute-start | bytes 2359304 | tf_op jit(solution)/shard_map/ppermute | solution.py:502
  49.5 8.7 %collective-permute-start.12 = (bf16[64,16,128]{2,1,0:T(8,128)(2,1)S(1)}, bf16[64,16,128]{2,1,0:T(8,128)(2,1)S(1)}, u32[]{:S(2)}, u32[]{:S(2)}) collective-permute-start(bf16[64,16,128]{2,1,0:T(8,128)(2,1)S(1)} %get-tuple-element.101), channel_id=1, source_target_pairs={{0,4},{2,6},{4,0},{6,2},{8,12},{10,14},{12,8},{14,10},{16,20},{18,... | collective-permute-start | bytes 786440 | tf_op jit(solution)/shard_map/ppermute | solution.py:502
  51.1 7.0 %collective-permute-start.13 = (bf16[128,768]{1,0:T(8,128)(2,1)S(1)}, bf16[128,768]{1,0:T(8,128)(2,1)S(1)}, u32[]{:S(2)}, u32[]{:S(2)}) collective-permute-start(bf16[128,768]{1,0:T(8,128)(2,1)S(1)} %get-tuple-element.102.refs_6_), channel_id=1, source_target_pairs={{0,1},{1,0},{2,3},{3,2},{4,5},{5,4},{6,7},{7,6},{8,9},{9,8},{10,11... | collective-permute-start | bytes 589832 | tf_op jit(solution)/shard_map/ppermute | solution.py:507
  58.2 5.1 %copy-start.19 = (f32[768]{0:T(1024)S(1)}, f32[768]{0:T(1024)}, u32[]{:S(2)}) copy-start(f32[768]{0:T(1024)} %refs_5_.1) | copy-start | bytes 9220
  59.6 2.3 %collective-permute-start.14 = (bf16[176,16,128]{2,1,0:T(8,128)(2,1)S(1)}, bf16[176,16,128]{2,1,0:T(8,128)(2,1)S(1)}, u32[]{:S(2)}, u32[]{:S(2)}) collective-permute-start(bf16[176,16,128]{2,1,0:T(8,128)(2,1)S(1)} %get-tuple-element.104), channel_id=1, source_target_pairs={{0,2},{2,0},{4,6},{6,4},{8,10},{10,8},{12,14},{14,12},{16,18},{18,... | collective-permute-start | bytes 2162696 | tf_op jit(solution)/shard_map/ppermute | solution.py:502
  59.7 11.5 %collective-permute-start.11 = (bf16[96,16,128]{2,1,0:T(8,128)(2,1)S(1)}, bf16[96,16,128]{2,1,0:T(8,128)(2,1)S(1)}, u32[]{:S(2)}, u32[]{:S(2)}) collective-permute-start(bf16[96,16,128]{2,1,0:T(8,128)(2,1)S(1)} %get-tuple-element.98), channel_id=1, source_target_pairs={{0,4},{2,6},{4,0},{6,2},{8,12},{10,14},{12,8},{14,10},{16,20},{18,... | collective-permute-start | bytes 1179656 | tf_op jit(solution)/shard_map/ppermute | solution.py:502
  62.6 10.5 %collective-permute-start.15 = (bf16[88,16,128]{2,1,0:T(8,128)(2,1)S(1)}, bf16[88,16,128]{2,1,0:T(8,128)(2,1)S(1)}, u32[]{:S(2)}, u32[]{:S(2)}) collective-permute-start(bf16[88,16,128]{2,1,0:T(8,128)(2,1)S(1)} %get-tuple-element.106), channel_id=1, source_target_pairs={{0,8},{2,10},{4,12},{6,14},{8,0},{10,2},{12,4},{14,6},{16,24},{18,... | collective-permute-start | bytes 1081352 | tf_op jit(solution)/shard_map/ppermute | solution.py:502
  62.6 7.0 %collective-permute-start.9 = (bf16[768,128]{1,0:T(8,128)(2,1)S(1)}, bf16[768,128]{1,0:T(8,128)(2,1)S(1)}, u32[]{:S(2)}, u32[]{:S(2)}) collective-permute-start(bf16[768,128]{1,0:T(8,128)(2,1)S(1)} %get-tuple-element.93), channel_id=1, source_target_pairs={{0,1},{1,0},{2,3},{3,2},{4,5},{5,4},{6,7},{7,6},{8,9},{9,8},{10,11... | collective-permute-start | bytes 589832 | tf_op jit(solution)/shard_map/ppermute | solution.py:507
  69.7 22.4 %copy-start.9 = (bf16[16,128,128]{2,1,0:T(8,128)(2,1)S(1)}, bf16[16,128,128]{2,1,0:T(8,128)(2,1)}, u32[]{:S(2)}) copy-start(bf16[16,128,128]{2,1,0:T(8,128)(2,1)} %get-tuple-element.116.refs_1_) | copy-start | bytes 1572868
  73.8 29.2 %copy-start.3 = (bf16[128,16,128]{2,1,0:T(8,128)(2,1)S(1)}, bf16[128,16,128]{2,1,0:T(8,128)(2,1)}, u32[]{:S(2)}) copy-start(bf16[128,16,128]{2,1,0:T(8,128)(2,1)} %param.22) | copy-start | bytes 1572868
  73.9 29.2 %copy-start.16 = (bf16[128,8]{0,1:T(8,128)(2,1)S(1)}, bf16[128,8]{0,1:T(8,128)(2,1)}, u32[]{:S(2)}) copy-start(bf16[128,8]{0,1:T(8,128)(2,1)} %param.34) | copy-start | bytes 6148
  73.9 29.2 %copy-start.17 = (f32[128]{0:T(128)S(1)}, f32[128]{0:T(128)}, u32[]{:S(2)}) copy-start(f32[128]{0:T(128)} %param.28) | copy-start | bytes 1540
  73.9 10.9 %collective-permute-start.16 = (bf16[48,16,128]{2,1,0:T(8,128)(2,1)S(1)}, bf16[48,16,128]{2,1,0:T(8,128)(2,1)S(1)}, u32[]{:S(2)}, u32[]{:S(2)}) collective-permute-start(bf16[48,16,128]{2,1,0:T(8,128)(2,1)S(1)} %get-tuple-element.109), channel_id=1, source_target_pairs={{0,8},{2,10},{4,12},{6,14},{8,0},{10,2},{12,4},{14,6},{16,24},{18,... | collective-permute-start | bytes 589832 | tf_op jit(solution)/shard_map/ppermute | solution.py:502
  74.2 10.6 %collective-permute-start.17 = (bf16[44,16,128]{2,1,0:T(8,128)(2,1)S(1)}, bf16[44,16,128]{2,1,0:T(8,128)(2,1)S(1)}, u32[]{:S(2)}, u32[]{:S(2)}) collective-permute-start(bf16[44,16,128]{2,1,0:T(8,128)(2,1)S(1)} %get-tuple-element.111), channel_id=1, source_target_pairs={{0,16},{2,18},{4,20},{6,22},{8,24},{10,26},{12,28},{14,30},{16,0},... | collective-permute-start | bytes 540680 | tf_op jit(solution)/shard_map/ppermute | solution.py:502
  85.4 6.6 %collective-permute-start.18 = (bf16[24,16,128]{2,1,0:T(8,128)(2,1)S(1)}, bf16[24,16,128]{2,1,0:T(8,128)(2,1)S(1)}, u32[]{:S(2)}, u32[]{:S(2)}) collective-permute-start(bf16[24,16,128]{2,1,0:T(8,128)(2,1)S(1)} %get-tuple-element.113), channel_id=1, source_target_pairs={{0,16},{2,18},{4,20},{6,22},{8,24},{10,26},{12,28},{14,30},{16,0},... | collective-permute-start | bytes 294920 | tf_op jit(solution)/shard_map/ppermute | solution.py:502
  86.1 5.9 %collective-permute-start.19 = (bf16[18,16,128]{2,1,0:T(8,128)(2,1)S(1)}, bf16[18,16,128]{2,1,0:T(8,128)(2,1)S(1)}, u32[]{:S(2)}, u32[]{:S(2)}) collective-permute-start(bf16[18,16,128]{2,1,0:T(8,128)(2,1)S(1)} %get-tuple-element.115), channel_id=1, source_target_pairs={{0,4},{2,6},{4,0},{6,2},{8,12},{10,14},{12,8},{14,10},{16,20},{18,... | collective-permute-start | bytes 221192 | tf_op jit(solution)/shard_map/ppermute | solution.py:502
  88.2 3.8 %collective-permute-start.20 = (bf16[64,128]{1,0:T(8,128)(2,1)S(1)}, bf16[64,128]{1,0:T(8,128)(2,1)S(1)}, u32[]{:S(2)}, u32[]{:S(2)}) collective-permute-start(bf16[64,128]{1,0:T(8,128)(2,1)S(1)} %get-tuple-element.118), channel_id=1, source_target_pairs={{0,1},{1,0},{2,3},{3,2},{4,5},{5,4},{6,7},{7,6},{8,9},{9,8},{10,11... | collective-permute-start | bytes 49160 | tf_op jit(solution)/shard_map/ppermute | solution.py:507
  93.6 16.3 %all-to-all-start = ((f32[32,8,128]{2,1,0:T(8,128)}), f32[32,8,128]{2,1,0:T(8,128)S(1)}, u32[]{:S(2)}, u32[]{:S(2)}) async-start(f32[32,8,128]{2,1,0:T(8,128)} %pair_weight.1.refs_5_), calls=%async_computation | async-start | bytes 262144 | tf_op jit(solution)/shard_map/all_to_all | solution.py:511
  98.7 11.2 %collective-permute-start.21 = (bf16[3,48,384]{2,1,0:T(8,128)(2,1)S(1)}, bf16[3,48,384]{2,1,0:T(8,128)(2,1)S(1)}, u32[]{:S(2)}, u32[]{:S(2)}) collective-permute-start(bf16[3,48,384]{2,1,0:T(8,128)(2,1)S(1)} %get-tuple-element.119.refs_1_.refs_6_), channel_id=1, source_target_pairs={{1,16},{3,18},{5,20},{7,22},{9,24},{11,26},{13,28},{15,30},{16,1},... | collective-permute-start | bytes 331784 | tf_op jit(solution)/shard_map/ppermute | solution.py:800
  103.0 3.8 %collective-permute-start.22 = (bf16[48,128]{1,0:T(8,128)(2,1)S(1)}, bf16[48,128]{1,0:T(8,128)(2,1)S(1)}, u32[]{:S(2)}, u32[]{:S(2)}) collective-permute-start(bf16[48,128]{1,0:T(8,128)(2,1)S(1)} %get-tuple-element.121), channel_id=1, source_target_pairs={{0,1},{1,0},{2,3},{3,2},{4,5},{5,4},{6,7},{7,6},{8,9},{9,8},{10,11... | collective-permute-start | bytes 36872 | tf_op jit(solution)/shard_map/ppermute | solution.py:507

commit v11 on v9

--- a/solution.py
+++ b/solution.py
@@ -435,14 +435,16 @@
         pieces[r][...] = blocks[jnp.bitwise_xor(ids[0], r)].astype(bf16)
 
 
-def finish_kernel(moved, *rest):
-    parts, outs = rest[:-4], rest[-4:]
+def finish_kernel(group, ids, own, moved, terms, *rest):
+    parts, outs = rest[:-5], rest[-5:]
+    stays = jnp.where(ids[1] // group == ids[0], 1.0, 0.0).astype(f32)
     for k in range(3):
-        outs[k][...] = moved[k].astype(f32)
+        outs[k][...] = own[k].astype(f32) * stays + moved[k].astype(f32) * (1.0 - stays)
     total = parts[0][...].astype(f32)
     for part in parts[1:]:
         total = total + part[...].astype(f32)
     outs[3][...] = total
+    outs[4][...] = jnp.sum(terms[...], axis=0)
 
 
 def exit_kernel(toks, noisy, gain, d_res, d_own, *rest):
@@ -473,10 +475,9 @@
     sums = jnp.zeros((grad_b.shape[0], channels), f32)
     for j in range(cols):
         sums = sums + jnp.where(row_col == j, mm(grad_b, columns[j]), 0.0)
-    for h in range(weight_grad.shape[1]):
+    for h in range(weight_grad.shape[0]):
         line = jnp.sum(sums[h * cols : (h + 1) * cols, :], axis=0, keepdims=True)
-        for n in range(weight_grad.shape[0]):
-            weight_grad[n, h : h + 1, :] = line
+        weight_grad[h : h + 1, :] = line
 
 
 def pair_kernel(toks, cols, ids, pair, gain, w_pair, *rest):
@@ -503,10 +504,6 @@
 def swap_tok(value, mask):
     size = lax.axis_size("tok")
     return lax.ppermute(value, "tok", [(i, i ^ mask) for i in range(size)])
-
-
-def exchange(value):
-    return lax.all_to_all(value, ("copy", "tok"), 0, 0)
 
 
 def per_device(
@@ -543,7 +540,6 @@
     tokens = rows * toks
     hidden = w_down.shape[0]
     cut = width // copies
-    devices = copies * toks
     ids = jnp.stack([lax.axis_index("tok"), lax.axis_index("copy")]).astype(jnp.int32)
     where_am_i = (ids, SMEM)
     noisy2 = noisy.reshape(rows, width)
@@ -581,21 +577,28 @@
         [((far, own_heads * cols, rows), bf16)] * toks,
         deps=x_parts[1:],
     )
+    (lines,) = call(
+        join_kernel,
+        "join_tok",
+        [by_tok[0]] + [swap_tok(by_tok[r], r) for r in range(1, toks)],
+        [((toks, far, own_heads * cols, rows), bf16)],
+    )
     (slices,) = call(
         stage_kernel,
         "stage",
         [where_am_i] + [(w, ANY) for w in weights3],
         [((3, width, own_width), bf16)],
         [pltpu.SemaphoreType.DMA((3,))],
-        deps=[by_tok[0]],
+        deps=[lines],
     )
     (lines,) = call(
         join_kernel,
-        "join_tok",
-        [by_tok[0]] + [swap_tok(by_tok[r], r) for r in range(1, toks)],
-        [((toks, far, own_heads * cols, rows), bf16)],
+        "join_y",
+        [lines, swap_copy(lines, 2)],
+        [((2,) + lines.shape, bf16)],
         deps=[slices],
     )
+    biases = [lines, swap_copy(lines, 1)]
     x, query, key, value = call(
         functools.partial(project_kernel, toks),
         "project",
@@ -603,14 +606,6 @@
         [((tokens, width), bf16)] + [((own_width, tokens), bf16)] * 3,
         flops=6 * tokens * width * own_width,
     )
-    (lines,) = call(
-        join_kernel,
-        "join_y",
-        [lines, swap_copy(lines, 2)],
-        [((2,) + lines.shape, bf16)],
-        deps=[value],
-    )
-    biases = [lines, swap_copy(lines, 1)]
     done = call(
         functools.partial(attention_kernel, copies, toks, near, cols, head_width),
         "attention",
@@ -751,13 +746,14 @@
     swaps = []
     for c in range(copies):
         for t in range(toks):
-            swaps.append((c * toks + t, (t * group + c % group) * toks + c // group))
+            if c // group != t:
+                swaps.append((c * toks + t, (t * group + c % group) * toks + c // group))
 
     (weight_grad,) = call(
         functools.partial(pair_weight_kernel, toks),
         "pair_weight",
         [where_am_i, columns] + bias_pieces,
-        [((devices, heads, channels), f32)],
+        [((heads, channels), f32)],
         [VMEM((heads * cols, rows), f32)],
         flops=2 * heads * cols * rows * channels * cols,
         deps=[pairs[0][1], pairs[1][1]],
@@ -779,15 +775,15 @@
         flops=2 * heads * cols * rows * channels * cols,
         deps=[last[0]],
     )
-    weight_grad = jnp.sum(exchange(weight_grad), axis=0)
+    weight_terms = lax.all_gather(weight_grad, ("copy", "tok"))
     grad_out, singles = last[1], last[2:]
     singles = [singles[0]] + [swap_tok(singles[r], r) for r in range(1, toks)]
     moved = lax.ppermute(last[0], ("copy", "tok"), swaps)
-    grad_query, grad_key, grad_value, grad_single = call(
-        finish_kernel,
+    grad_query, grad_key, grad_value, grad_single, weight_grad = call(
+        functools.partial(finish_kernel, group),
         "finish",
-        [moved] + singles,
-        [((cut, own_width), f32)] * 3 + [((cut, rows), f32)],
+        [where_am_i, last[0], moved, weight_terms] + singles,
+        [((cut, own_width), f32)] * 3 + [((cut, rows), f32), ((heads, channels), f32)],
     )
     return (
         grad_noisy[None],

time: 108 us -> 165 us (1.53)
  blocking collectives: 0 us -> 66.3 us
  waiting for transfers between devices: 44.2 us -> 34.8 us
    all_gather x0 -> x1, blocking collectives: none -> 66.3 us  [per_device(): weight_terms = lax.all_gather(weight_grad, ('copy', 'tok'))]
    all_to_all x1 -> x0, starting transfers between devices: 5.09 us -> none  [exchange(): return lax.all_to_all(value, ('copy', 'tok'), 0, 0)]
    ppermute x8, starting transfers between devices: 4.57 us -> 9.35 us  [swap_tok(): return lax.ppermute(value, 'tok', [(i, i ^ mask) for i in range(size)])]
    ppermute x14, waiting for transfers between devices: 20.7 us -> 16.8 us  [swap_copy(): return lax.ppermute(value, 'copy', [(i, i ^ mask) for i in range(size)])]
    ppermute x1, waiting for transfers between devices: 3.13 us -> 0.01 us  [per_device(): moved = lax.ppermute(last[0], ('copy', 'tok'), swaps)]
    ppermute x8, waiting for transfers between devices: 20.5 us -> 18 us  [swap_tok(): return lax.ppermute(value, 'tok', [(i, i ^ mask) for i in range(size)])]
  transfers between devices with their start and end apart: 24 -> 23, of which waited for: 16 -> 14; matrix products, arithmetic and copies ran while one was open for 0% -> 0% of each run, Pallas kernels for 12% -> 7%
where the time goes in v11:
time: 165 us; the launch traced here: 163 us
  blocking collectives  66.3 us (40%)
  waiting for transfers between devices  34.8 us (21%)
  Pallas kernels  29.5 us (18%)
  starting transfers between devices  27.1 us (16%)
  local copies, waits for them, and re-layouts  4.05 us (2%)
    all_gather x1, blocking collectives, per_device(): weight_terms = lax.all_gather(weight_grad, ('copy', 'tok'))  66.3 us
    pallas_call x21, Pallas kernels, call(): pl.pallas_call(whole, name=name, out_shape=[jax.ShapeDtypeStruct(one[0],...  29.5 us
    ppermute x8, waiting for transfers between devices, swap_tok(): return lax.ppermute(value, 'tok', [(i, i ^ mask) for i in range(size)])  18 us
    ppermute x14, waiting for transfers between devices, swap_copy(): return lax.ppermute(value, 'copy', [(i, i ^ mask) for i in range(size)])  16.8 us
    ppermute x14, starting transfers between devices, swap_copy(): return lax.ppermute(value, 'copy', [(i, i ^ mask) for i in range(size)])  13.3 us
    ppermute x8, starting transfers between devices, swap_tok(): return lax.ppermute(value, 'tok', [(i, i ^ mask) for i in range(size)])  9.35 us
    ppermute x1, starting transfers between devices, per_device(): moved = lax.ppermute(last[0], ('copy', 'tok'), swaps)  4.41 us
    unnamed x42, local copies, waits for them, and re-layouts  4.04 us
  transfers between devices with their start and end apart: 23, of which 14 were waited for; matrix products, arithmetic and copies ran while one was open for 0% of the time, Pallas kernels for 7%

profile of v11, /device:TPU:2, one launch (start us, length us, event | category | flops | bytes accessed | tf_op | source)
XLA Modules:
  0.0 163.3 jit_solution(4221227069927161372)
XLA Ops:
  0.6 0.6 pad_add_fusion.refs_0_
  1.2 4.2 %enter.1 = (bf16[128,768]{1,0:T(8,128)(2,1)}, bf16[16,128,128]{2,1,0:T(8,128)(2,1)}, f32[256,128]{1,0:T(8,128)}, f32[1,256]{1,0:T(1,128)}, bf16[2,64,128]{2,1,0:T(8,128)(2,1)}) custom-call(s32[2]{0:T(128)} %pad_add_fusion.refs_0_, bf16[128,768]{1,0:T(8,128)(2,1)} %bitcast.21, bf16[128,768]{1,0:T(8,128)(2,1)} %refs_2_.2, s32[1,128]{1,0:T(1,128)} %bitcast.32, ...), custom_call_target="tpu_custom_call" | custom-call | flops 67108864 | bytes 1860808 | tf_op jit(solution)/shard_map/enter/pallas_call | solution.py:79
  5.4 0.1 collective-permute-start.3
  5.5 4.1 %collective-permute-start.2 = (bf16[2,64,128]{2,1,0:T(8,128)(2,1)}, bf16[2,64,128]{2,1,0:T(8,128)(2,1)S(1)}, u32[]{:S(2)}, u32[]{:S(2)}) collective-permute-start(bf16[2,64,128]{2,1,0:T(8,128)(2,1)} %get-tuple-element.72.refs_0_), channel_id=1, source_target_pairs={{0,24},{2,26},{4,28},{6,30},{8,16},{10,18},{12,20},{14,22},{16,8},... | collective-permute-start | bytes 98312 | tf_op jit(solution)/shard_map/ppermute | solution.py:501
  9.6 0.6 collective-permute-start
  10.2 1.7 %collective-permute-done.2.refs_3_ = bf16[2,64,128]{2,1,0:T(8,128)(2,1)S(1)} collective-permute-done((bf16[2,64,128]{2,1,0:T(8,128)(2,1)}, bf16[2,64,128]{2,1,0:T(8,128)(2,1)S(1)}, u32[]{:S(2)}, u32[]{:S(2)}) %collective-permute-start.2) | collective-permute-done | bytes 32800 | tf_op jit(solution)/shard_map/ppermute | solution.py:501
  11.8 2.8 %collective-permute-done.1.refs_2_ = bf16[2,64,128]{2,1,0:T(8,128)(2,1)S(1)} collective-permute-done((bf16[2,64,128]{2,1,0:T(8,128)(2,1)}, bf16[2,64,128]{2,1,0:T(8,128)(2,1)S(1)}, u32[]{:S(2)}, u32[]{:S(2)}) %collective-permute-start.1) | collective-permute-done | bytes 32800 | tf_op jit(solution)/shard_map/ppermute | solution.py:501
  14.6 0.8 copy-done.15
  15.4 1.6 collective-permute-start.4
  17.0 2.8 %collective-permute-done.4.refs_1_ = bf16[4,64,128]{2,1,0:T(8,128)(2,1)S(1)} collective-permute-done((bf16[4,64,128]{2,1,0:T(8,128)(2,1)S(1)}, bf16[4,64,128]{2,1,0:T(8,128)(2,1)S(1)}, u32[]{:S(2)}, u32[]{:S(2)}) %collective-permute-start.4) | collective-permute-done | bytes 65568 | tf_op jit(solution)/shard_map/ppermute | solution.py:506
  19.7 1.6 collective-permute-start.5
  21.3 1.3 copy-done.5
  22.6 1.3 copy-done.6
  23.9 0.7 copy-done.13
  24.5 0.8 stage.1.refs_1_.refs_2_
  25.3 0.0 copy-start.14
  25.3 0.0 copy-start.18
  25.4 0.0 copy-start.2
  25.4 0.0 copy-start.8
  25.4 0.1 collective-permute-start.6
  25.5 1.4 project.1
  26.9 0.1 collective-permute-done.6.refs_5_
  27.1 2.1 %attention.1 = (bf16[4,256,256]{2,1,0:T(8,128)(2,1)S(1)}, bf16[256,384]{1,0:T(8,128)(2,1)S(1)}, bf16[128,384]{1,0:T(8,128)(2,1)S(1)}, bf16[128,384]{1,0:T(8,128)(2,1)S(1)}) custom-call(s32[2]{0:T(128)S(1)} %copy-done.14, bf16[384,256]{1,0:T(8,128)(2,1)S(1)} %get-tuple-element.76.refs_1_, bf16[384,256]{1,0:T(8,128)(2,1)S(1)} %get-tuple-element.77.refs_2_, ...), custom_call_target="tpu_custom_call" | custom-call | flops 100663296 | bytes 2163720 | tf_op jit(solution)/shard_map/attention/pallas_call | solution.py:79
  29.2 1.6 collective-permute-start.7
  30.8 0.9 down.1
  31.7 2.7 %collective-permute-done.7.refs_6_ = bf16[128,384]{1,0:T(8,128)(2,1)S(1)} collective-permute-done((bf16[128,384]{1,0:T(8,128)(2,1)S(1)}, bf16[128,384]{1,0:T(8,128)(2,1)S(1)}, u32[]{:S(2)}, u32[]{:S(2)}) %collective-permute-start.7) | collective-permute-done | bytes 98336 | tf_op jit(solution)/shard_map/ppermute | solution.py:506
  34.4 4.3 %hidden.1 = (f32[128,768]{1,0:T(8,128)S(1)}, bf16[128,768]{1,0:T(8,128)(2,1)S(1)}, bf16[384,128]{1,0:T(8,128)(2,1)S(1)}, bf16[384,128]{1,0:T(8,128)(2,1)S(1)}) custom-call(s32[2]{0:T(128)S(1)} %copy-done.14, bf16[128,768]{1,0:T(8,128)(2,1)S(1)} %get-tuple-element.68.refs_1_.refs_0_, bf16[128,768]{1,0:T(8,128)(2,1)S(1)} %get-tuple-element.69.refs_2_, ...), custom_call_target="tpu_custom_call" | custom-call | flops 1509949440 | bytes 8064008 | tf_op jit(solution)/shard_map/hidden/pallas_call | solution.py:79
  38.7 1.6 collective-permute-start.8
  40.3 3.1 %collective-permute-done.8.refs_6_ = bf16[384,128]{1,0:T(8,128)(2,1)S(1)} collective-permute-done((bf16[384,128]{1,0:T(8,128)(2,1)S(1)}, bf16[384,128]{1,0:T(8,128)(2,1)S(1)}, u32[]{:S(2)}, u32[]{:S(2)}) %collective-permute-start.8) | collective-permute-done | bytes 98336 | tf_op jit(solution)/shard_map/ppermute | solution.py:506
  43.4 2.0 %backward.1 = (bf16[384,256]{1,0:T(8,128)(2,1)S(1)}, bf16[384,256]{1,0:T(8,128)(2,1)S(1)}, bf16[384,256]{1,0:T(8,128)(2,1)S(1)}, bf16[64,16,128]{2,1,0:T(8,128)(...) custom-call(s32[2]{0:T(128)S(1)} %copy-done.14, ...), custom_call_target="tpu_custom_call" | custom-call | flops 201326592 | bytes 2818056 | tf_op jit(solution)/shard_map/backward/pallas_call | solution.py:79
  45.5 1.0 collective-permute-start.11
  46.5 1.5 collective-permute-start.12
  48.0 2.1 %first.1 = (bf16[192,16,128]{2,1,0:T(8,128)(2,1)S(1)}, bf16[192,16,128]{2,1,0:T(8,128)(2,1)S(1)}, f32[768,128]{1,0:T(8,128)S(1)}, bf16[768,128]{1,0:T(8,128)(2,1)S(1)}) custom-call(s32[2]{0:T(128)S(1)} %copy-done.14, bf16[3,768,384]{2,1,0:T(8,128)(2,1)S(1)} %stage.1.refs_1_.refs_2_, bf16[256,768]{1,0:T(8,128)(2,1)S(1)} %get-tuple-element.84.refs_2_.refs_1_, ...), custom_call_target="tpu_custom_call" | custom-call | flops 754974720 | bytes 4915208 | tf_op jit(solution)/shard_map/first/pallas_call | solution.py:79
  50.0 0.1 collective-permute-start.10
  50.1 2.0 %collective-permute-done.12.refs_7_ = bf16[128,768]{1,0:T(8,128)(2,1)S(1)} collective-permute-done((bf16[128,768]{1,0:T(8,128)(2,1)S(1)}, bf16[128,768]{1,0:T(8,128)(2,1)S(1)}, u32[]{:S(2)}, u32[]{:S(2)}) %collective-permute-start.12) | collective-permute-done | bytes 196640 | tf_op jit(solution)/shard_map/ppermute | solution.py:506
  52.1 0.1 collective-permute-done.11.refs_5_
  52.2 1.4 second.1
  53.6 0.0 copy-start.19
  53.6 0.1 collective-permute-start.13
  53.7 2.2 %collective-permute-done.13.refs_4_ = bf16[176,16,128]{2,1,0:T(8,128)(2,1)S(1)} collective-permute-done((bf16[176,16,128]{2,1,0:T(8,128)(2,1)S(1)}, bf16[176,16,128]{2,1,0:T(8,128)(2,1)S(1)}, u32[]{:S(2)}, u32[]{:S(2)}) %collective-permute-start.13) | collective-permute-done | bytes 720928 | tf_op jit(solution)/shard_map/ppermute | solution.py:501
  55.9 0.9 step_0.1
  56.8 1.1 collective-permute-start.14
  57.9 1.5 collective-permute-start.9
  59.4 5.2 %collective-permute-done.9.refs_4_ = bf16[768,128]{1,0:T(8,128)(2,1)S(1)} collective-permute-done((bf16[768,128]{1,0:T(8,128)(2,1)S(1)}, bf16[768,128]{1,0:T(8,128)(2,1)S(1)}, u32[]{:S(2)}, u32[]{:S(2)}) %collective-permute-start.9) | collective-permute-done | bytes 196640 | tf_op jit(solution)/shard_map/ppermute | solution.py:506
  64.5 1.2 exit.1
  65.7 2.3 %collective-permute-done.15.refs_4_ = bf16[88,16,128]{2,1,0:T(8,128)(2,1)S(1)} collective-permute-done((bf16[88,16,128]{2,1,0:T(8,128)(2,1)S(1)}, bf16[88,16,128]{2,1,0:T(8,128)(2,1)S(1)}, u32[]{:S(2)}, u32[]{:S(2)}) %collective-permute-start.15) | collective-permute-done | bytes 360480 | tf_op jit(solution)/shard_map/ppermute | solution.py:501
  68.0 0.7 step_1.1
  68.8 0.3 collective-permute-start.16
  69.1 2.0 %collective-permute-start.17 = (bf16[44,16,128]{2,1,0:T(8,128)(2,1)S(1)}, bf16[44,16,128]{2,1,0:T(8,128)(2,1)S(1)}, u32[]{:S(2)}, u32[]{:S(2)}) collective-permute-start(bf16[44,16,128]{2,1,0:T(8,128)(2,1)S(1)} %get-tuple-element.111), channel_id=1, source_target_pairs={{0,16},{2,18},{4,20},{6,22},{8,24},{10,26},{12,28},{14,30},{16,0},... | collective-permute-start | bytes 540680 | tf_op jit(solution)/shard_map/ppermute | solution.py:501
  71.2 5.5 %collective-permute-done.17.refs_4_.refs_2_ = bf16[44,16,128]{2,1,0:T(8,128)(2,1)S(1)} collective-permute-done((bf16[44,16,128]{2,1,0:T(8,128)(2,1)S(1)}, bf16[44,16,128]{2,1,0:T(8,128)(2,1)S(1)}, u32[]{:S(2)}, u32[]{:S(2)}) %collective-permute-start.17) | collective-permute-done | bytes 180256 | tf_op jit(solution)/shard_map/ppermute | solution.py:501
  76.7 2.1 %collective-permute-done.16.refs_2_ = bf16[48,16,128]{2,1,0:T(8,128)(2,1)S(1)} collective-permute-done((bf16[48,16,128]{2,1,0:T(8,128)(2,1)S(1)}, bf16[48,16,128]{2,1,0:T(8,128)(2,1)S(1)}, u32[]{:S(2)}, u32[]{:S(2)}) %collective-permute-start.16) | collective-permute-done | bytes 196640 | tf_op jit(solution)/shard_map/ppermute | solution.py:501
  78.8 0.6 step_2.1
  79.4 1.4 collective-permute-start.18
  80.8 1.0 collective-permute-start.19
  81.9 0.6 last_bias.1
  82.4 1.6 collective-permute-start.20
  84.0 2.3 %collective-permute-done.20.refs_3_.refs_5_ = bf16[64,128]{1,0:T(8,128)(2,1)S(1)} collective-permute-done((bf16[64,128]{1,0:T(8,128)(2,1)S(1)}, bf16[64,128]{1,0:T(8,128)(2,1)S(1)}, u32[]{:S(2)}, u32[]{:S(2)}) %collective-permute-start.20) | collective-permute-done | bytes 16416 | tf_op jit(solution)/shard_map/ppermute | solution.py:506
  86.2 0.8 pair_weight.1.refs_5_
  87.1 1.2 last.1
  88.3 4.4 %collective-permute-start.21 = (bf16[3,48,384]{2,1,0:T(8,128)(2,1)S(1)}, bf16[3,48,384]{2,1,0:T(8,128)(2,1)S(1)}, u32[]{:S(2)}, u32[]{:S(2)}) collective-permute-start(bf16[3,48,384]{2,1,0:T(8,128)(2,1)S(1)} %get-tuple-element.119.refs_1_.refs_6_), channel_id=1, source_target_pairs={{1,16},{3,18},{5,20},{7,22},{9,24},{11,26},{13,28},{15,30},{16,1},... | collective-permute-start | bytes 331784 | tf_op jit(solution)/shard_map/ppermute | solution.py:781
  92.7 0.1 collective-permute-start.22
  92.8 66.3 %all-gather = f32[256,128]{1,0:T(8,128)S(1)} all-gather(f32[8,128]{1,0:T(8,128)S(1)} %pair_weight.1.refs_5_), channel_id=2, replica_groups=mesh['copy'=16,'tok'=2] {'copy','tok'}, dimensions={0}, use_global_device_ids=true | all-gather | bytes 135168 | tf_op jit(solution)/shard_map/all_gather | solution.py:778
  159.1 2.9 %pair.1 = bf16[2048,128]{1,0:T(8,128)(2,1)} custom-call(s32[2]{0:T(128)S(1)} %copy-done.14, bf16[2048,128]{1,0:T(8,128)(2,1)S(1)} %bitcast.20, f32[1,128]{1,0:T(1,128)S(1)} %bitcast.28, bf16[8,128]{1,0:T(8,128)(2,1)S(1)} %bitcast.26, bf16[64,128]{1,0:T(8,128)(2,1)S(1)} %get-tuple-element.117.refs_2_.refs_4_, ...), custom_call_target="tpu_custom_call" | custom-call | flops 67108864 | bytes 1083912 | tf_op jit(solution)/shard_map/pair/pallas_call | solution.py:79
  162.0 1.2 finish.1
  (49 shorter events, 0.1 us)
Async XLA Ops:
  0.6 20.7 %copy-start.4 = (bf16[768,768]{1,0:T(8,128)(2,1)S(1)}, bf16[768,768]{1,0:T(8,128)(2,1)}, u32[]{:S(2)}) copy-start(bf16[768,768]{1,0:T(8,128)(2,1)} %refs_1_.3) | copy-start | bytes 3538948
  5.4 9.2 %collective-permute-start.3 = (bf16[128,768]{1,0:T(8,128)(2,1)}, bf16[128,768]{1,0:T(8,128)(2,1)S(1)}, u32[]{:S(2)}, u32[]{:S(2)}) collective-permute-start(bf16[128,768]{1,0:T(8,128)(2,1)} %get-tuple-element.73.refs_2_), channel_id=1, source_target_pairs={{0,1},{1,0},{2,3},{3,2},{4,5},{5,4},{6,7},{7,6},{8,9},{9,8},{10,11... | collective-permute-start | bytes 589832 | tf_op jit(solution)/shard_map/ppermute | solution.py:506
  5.5 6.4 %collective-permute-start.2 = (bf16[2,64,128]{2,1,0:T(8,128)(2,1)}, bf16[2,64,128]{2,1,0:T(8,128)(2,1)S(1)}, u32[]{:S(2)}, u32[]{:S(2)}) collective-permute-start(bf16[2,64,128]{2,1,0:T(8,128)(2,1)} %get-tuple-element.72.refs_0_), channel_id=1, source_target_pairs={{0,24},{2,26},{4,28},{6,30},{8,16},{10,18},{12,20},{14,22},{16,8},... | collective-permute-start | bytes 98312 | tf_op jit(solution)/shard_map/ppermute | solution.py:501
  9.6 5.0 %collective-permute-start.1 = (bf16[2,64,128]{2,1,0:T(8,128)(2,1)}, bf16[2,64,128]{2,1,0:T(8,128)(2,1)S(1)}, u32[]{:S(2)}, u32[]{:S(2)}) collective-permute-start(bf16[2,64,128]{2,1,0:T(8,128)(2,1)} %get-tuple-element.72.refs_0_), channel_id=1, source_target_pairs={{0,16},{2,18},{4,20},{6,22},{8,24},{10,26},{12,28},{14,30},{16,0},... | collective-permute-start | bytes 98312 | tf_op jit(solution)/shard_map/ppermute | solution.py:501
  9.6 5.0 %collective-permute-start = (bf16[2,64,128]{2,1,0:T(8,128)(2,1)}, bf16[2,64,128]{2,1,0:T(8,128)(2,1)S(1)}, u32[]{:S(2)}, u32[]{:S(2)}) collective-permute-start(bf16[2,64,128]{2,1,0:T(8,128)(2,1)} %get-tuple-element.72.refs_0_), channel_id=1, source_target_pairs={{0,8},{2,10},{4,12},{6,14},{8,0},{10,2},{12,4},{14,6},{16,24},{18,... | collective-permute-start | bytes 98312 | tf_op jit(solution)/shard_map/ppermute | solution.py:501
  14.6 0.8 copy-start.15
  15.4 4.3 %collective-permute-start.4 = (bf16[4,64,128]{2,1,0:T(8,128)(2,1)S(1)}, bf16[4,64,128]{2,1,0:T(8,128)(2,1)S(1)}, u32[]{:S(2)}, u32[]{:S(2)}) collective-permute-start(bf16[4,64,128]{2,1,0:T(8,128)(2,1)S(1)} %get-tuple-element.75), channel_id=1, source_target_pairs={{0,1},{1,0},{2,3},{3,2},{4,5},{5,4},{6,7},{7,6},{8,9},{9,8},{10,11... | collective-permute-start | bytes 196616 | tf_op jit(solution)/shard_map/ppermute | solution.py:506
  19.7 5.6 %collective-permute-start.5 = (bf16[2,4,64,128]{3,2,1,0:T(8,128)(2,1)S(1)}, bf16[2,4,64,128]{3,2,1,0:T(8,128)(2,1)S(1)}, u32[]{:S(2)}, u32[]{:S(2)}) collective-permute-start(bf16[2,4,64,128]{3,2,1,0:T(8,128)(2,1)S(1)} %join_tok.1.refs_4_.refs_0_), channel_id=1, source_target_pairs={{0,4},{2,6},{4,0},{6,2},{8,12},{10,14},{12,8},{14,10},{16,20},{18,... | collective-permute-start | bytes 393224 | tf_op jit(solution)/shard_map/ppermute | solution.py:501
  21.3 1.3 copy-start.5
  22.6 1.3 copy-start.6
  23.9 0.7 copy-start.13
  24.5 1.0 copy-start.11
  24.5 2.5 %copy-start.12 = (f32[256,128]{1,0:T(8,128)S(1)}, f32[256,128]{1,0:T(8,128)}, u32[]{:S(2)}) copy-start(f32[256,128]{1,0:T(8,128)} %get-tuple-element.79.refs_6_) | copy-start | bytes 393220
  24.5 6.2 %copy-start.10 = (bf16[1,128,768]{2,1,0:T(8,128)(2,1)S(1)}, bf16[1,128,768]{2,1,0:T(8,128)(2,1)}, u32[]{:S(2)}) copy-start(bf16[1,128,768]{2,1,0:T(8,128)(2,1)} %param.39) | copy-start | bytes 589828
  25.3 1.7 %copy-start.14 = (s32[2]{0:T(128)S(1)}, s32[2]{0:T(128)}, u32[]{:S(2)}) copy-start(s32[2]{0:T(128)} %pad_add_fusion.refs_0_) | copy-start | bytes 28
  25.3 1.7 %copy-start.18 = (f32[1,256]{1,0:T(1,128)S(1)}, f32[1,256]{1,0:T(1,128)}, u32[]{:S(2)}) copy-start(f32[1,256]{1,0:T(1,128)} %get-tuple-element.80.refs_7_) | copy-start | bytes 3076
  25.4 5.4 %copy-start.2 = (bf16[1536,768]{1,0:T(8,128)(2,1)S(1)}, bf16[1536,768]{1,0:T(8,128)(2,1)}, u32[]{:S(2)}) copy-start(bf16[1536,768]{1,0:T(8,128)(2,1)} %refs_1_.2) | copy-start | bytes 7077892
  25.4 5.4 %copy-start.20 = (f32[768]{0:T(1024)S(1)}, f32[768]{0:T(1024)}, u32[]{:S(2)}) copy-start(f32[768]{0:T(1024)} %param.29) | copy-start | bytes 9220
  25.4 5.4 %copy-start.8 = (bf16[1,128,768]{2,1,0:T(8,128)(2,1)S(1)}, bf16[1,128,768]{2,1,0:T(8,128)(2,1)}, u32[]{:S(2)}) copy-start(bf16[1,128,768]{2,1,0:T(8,128)(2,1)} %param.20) | copy-start | bytes 589828
  25.4 1.6 collective-permute-start.6
  25.5 8.9 %copy-start.1 = (bf16[768,1536]{1,0:T(8,128)(2,1)S(1)}, bf16[768,1536]{1,0:T(8,128)(2,1)}, u32[]{:S(2)}) copy-start(bf16[768,1536]{1,0:T(8,128)(2,1)} %refs_9_.1) | copy-start | bytes 7077892
  27.0 7.4 %copy-start = (bf16[768,1536]{1,0:T(8,128)(2,1)S(1)}, bf16[768,1536]{1,0:T(8,128)(2,1)}, u32[]{:S(2)}) copy-start(bf16[768,1536]{1,0:T(8,128)(2,1)} %refs_8_.1) | copy-start | bytes 7077892
  27.0 7.4 %copy-start.7 = (bf16[768,768]{1,0:T(8,128)(2,1)S(1)}, bf16[768,768]{1,0:T(8,128)(2,1)}, u32[]{:S(2)}) copy-start(bf16[768,768]{1,0:T(8,128)(2,1)} %refs_7_.1) | copy-start | bytes 3538948
  29.2 5.2 %collective-permute-start.7 = (bf16[128,384]{1,0:T(8,128)(2,1)S(1)}, bf16[128,384]{1,0:T(8,128)(2,1)S(1)}, u32[]{:S(2)}, u32[]{:S(2)}) collective-permute-start(bf16[128,384]{1,0:T(8,128)(2,1)S(1)} %get-tuple-element.82), channel_id=1, source_target_pairs={{0,1},{1,0},{2,3},{3,2},{4,5},{5,4},{6,7},{7,6},{8,9},{9,8},{10,11... | collective-permute-start | bytes 294920 | tf_op jit(solution)/shard_map/ppermute | solution.py:506
  38.7 4.7 %collective-permute-start.8 = (bf16[384,128]{1,0:T(8,128)(2,1)S(1)}, bf16[384,128]{1,0:T(8,128)(2,1)S(1)}, u32[]{:S(2)}, u32[]{:S(2)}) collective-permute-start(bf16[384,128]{1,0:T(8,128)(2,1)S(1)} %get-tuple-element.87), channel_id=1, source_target_pairs={{0,1},{1,0},{2,3},{3,2},{4,5},{5,4},{6,7},{7,6},{8,9},{9,8},{10,11... | collective-permute-start | bytes 294920 | tf_op jit(solution)/shard_map/ppermute | solution.py:506
  45.5 6.8 %collective-permute-start.11 = (bf16[64,16,128]{2,1,0:T(8,128)(2,1)S(1)}, bf16[64,16,128]{2,1,0:T(8,128)(2,1)S(1)}, u32[]{:S(2)}, u32[]{:S(2)}) collective-permute-start(bf16[64,16,128]{2,1,0:T(8,128)(2,1)S(1)} %get-tuple-element.99), channel_id=1, source_target_pairs={{0,4},{2,6},{4,0},{6,2},{8,12},{10,14},{12,8},{14,10},{16,20},{18,... | collective-permute-start | bytes 786440 | tf_op jit(solution)/shard_map/ppermute | solution.py:501
  46.5 5.7 %collective-permute-start.12 = (bf16[128,768]{1,0:T(8,128)(2,1)S(1)}, bf16[128,768]{1,0:T(8,128)(2,1)S(1)}, u32[]{:S(2)}, u32[]{:S(2)}) collective-permute-start(bf16[128,768]{1,0:T(8,128)(2,1)S(1)} %get-tuple-element.100.refs_6_), channel_id=1, source_target_pairs={{0,1},{1,0},{2,3},{3,2},{4,5},{5,4},{6,7},{7,6},{8,9},{9,8},{10,11... | collective-permute-start | bytes 589832 | tf_op jit(solution)/shard_map/ppermute | solution.py:506
  50.0 3.7 %collective-permute-start.10 = (bf16[192,16,128]{2,1,0:T(8,128)(2,1)S(1)}, bf16[192,16,128]{2,1,0:T(8,128)(2,1)S(1)}, u32[]{:S(2)}, u32[]{:S(2)}) collective-permute-start(bf16[192,16,128]{2,1,0:T(8,128)(2,1)S(1)} %get-tuple-element.96), channel_id=1, source_target_pairs={{0,2},{2,0},{4,6},{6,4},{8,10},{10,8},{12,14},{14,12},{16,18},{18,... | collective-permute-start | bytes 2359304 | tf_op jit(solution)/shard_map/ppermute | solution.py:501
  53.6 5.7 %copy-start.19 = (f32[768]{0:T(1024)S(1)}, f32[768]{0:T(1024)}, u32[]{:S(2)}) copy-start(f32[768]{0:T(1024)} %refs_5_.1) | copy-start | bytes 9220
  53.6 2.3 %collective-permute-start.13 = (bf16[176,16,128]{2,1,0:T(8,128)(2,1)S(1)}, bf16[176,16,128]{2,1,0:T(8,128)(2,1)S(1)}, u32[]{:S(2)}, u32[]{:S(2)}) collective-permute-start(bf16[176,16,128]{2,1,0:T(8,128)(2,1)S(1)} %get-tuple-element.102), channel_id=1, source_target_pairs={{0,2},{2,0},{4,6},{6,4},{8,10},{10,8},{12,14},{14,12},{16,18},{18,... | collective-permute-start | bytes 2162696 | tf_op jit(solution)/shard_map/ppermute | solution.py:501
  56.8 11.2 %collective-permute-start.14 = (bf16[96,16,128]{2,1,0:T(8,128)(2,1)S(1)}, bf16[96,16,128]{2,1,0:T(8,128)(2,1)S(1)}, u32[]{:S(2)}, u32[]{:S(2)}) collective-permute-start(bf16[96,16,128]{2,1,0:T(8,128)(2,1)S(1)} %get-tuple-element.104), channel_id=1, source_target_pairs={{0,4},{2,6},{4,0},{6,2},{8,12},{10,14},{12,8},{14,10},{16,20},{18,... | collective-permute-start | bytes 1179656 | tf_op jit(solution)/shard_map/ppermute | solution.py:501
  57.9 10.2 %collective-permute-start.15 = (bf16[88,16,128]{2,1,0:T(8,128)(2,1)S(1)}, bf16[88,16,128]{2,1,0:T(8,128)(2,1)S(1)}, u32[]{:S(2)}, u32[]{:S(2)}) collective-permute-start(bf16[88,16,128]{2,1,0:T(8,128)(2,1)S(1)} %get-tuple-element.106), channel_id=1, source_target_pairs={{0,8},{2,10},{4,12},{6,14},{8,0},{10,2},{12,4},{14,6},{16,24},{18,... | collective-permute-start | bytes 1081352 | tf_op jit(solution)/shard_map/ppermute | solution.py:501
  57.9 6.7 %collective-permute-start.9 = (bf16[768,128]{1,0:T(8,128)(2,1)S(1)}, bf16[768,128]{1,0:T(8,128)(2,1)S(1)}, u32[]{:S(2)}, u32[]{:S(2)}) collective-permute-start(bf16[768,128]{1,0:T(8,128)(2,1)S(1)} %get-tuple-element.93), channel_id=1, source_target_pairs={{0,1},{1,0},{2,3},{3,2},{4,5},{5,4},{6,7},{7,6},{8,9},{9,8},{10,11... | collective-permute-start | bytes 589832 | tf_op jit(solution)/shard_map/ppermute | solution.py:506
  64.5 21.7 %copy-start.9 = (bf16[16,128,128]{2,1,0:T(8,128)(2,1)S(1)}, bf16[16,128,128]{2,1,0:T(8,128)(2,1)}, u32[]{:S(2)}) copy-start(bf16[16,128,128]{2,1,0:T(8,128)(2,1)} %get-tuple-element.116.refs_1_) | copy-start | bytes 1572868
  68.0 91.0 %copy-start.3 = (bf16[128,16,128]{2,1,0:T(8,128)(2,1)S(1)}, bf16[128,16,128]{2,1,0:T(8,128)(2,1)}, u32[]{:S(2)}) copy-start(bf16[128,16,128]{2,1,0:T(8,128)(2,1)} %param.22) | copy-start | bytes 1572868
  68.0 91.0 %copy-start.16 = (bf16[128,8]{0,1:T(8,128)(2,1)S(1)}, bf16[128,8]{0,1:T(8,128)(2,1)}, u32[]{:S(2)}) copy-start(bf16[128,8]{0,1:T(8,128)(2,1)} %param.34) | copy-start | bytes 6148
  68.0 91.0 %copy-start.17 = (f32[128]{0:T(128)S(1)}, f32[128]{0:T(128)}, u32[]{:S(2)}) copy-start(f32[128]{0:T(128)} %param.28) | copy-start | bytes 1540
  68.8 10.0 %collective-permute-start.16 = (bf16[48,16,128]{2,1,0:T(8,128)(2,1)S(1)}, bf16[48,16,128]{2,1,0:T(8,128)(2,1)S(1)}, u32[]{:S(2)}, u32[]{:S(2)}) collective-permute-start(bf16[48,16,128]{2,1,0:T(8,128)(2,1)S(1)} %get-tuple-element.109), channel_id=1, source_target_pairs={{0,8},{2,10},{4,12},{6,14},{8,0},{10,2},{12,4},{14,6},{16,24},{18,... | collective-permute-start | bytes 589832 | tf_op jit(solution)/shard_map/ppermute | solution.py:501
  69.1 7.5 %collective-permute-start.17 = (bf16[44,16,128]{2,1,0:T(8,128)(2,1)S(1)}, bf16[44,16,128]{2,1,0:T(8,128)(2,1)S(1)}, u32[]{:S(2)}, u32[]{:S(2)}) collective-permute-start(bf16[44,16,128]{2,1,0:T(8,128)(2,1)S(1)} %get-tuple-element.111), channel_id=1, source_target_pairs={{0,16},{2,18},{4,20},{6,22},{8,24},{10,26},{12,28},{14,30},{16,0},... | collective-permute-start | bytes 540680 | tf_op jit(solution)/shard_map/ppermute | solution.py:501
  79.4 6.8 %collective-permute-start.18 = (bf16[24,16,128]{2,1,0:T(8,128)(2,1)S(1)}, bf16[24,16,128]{2,1,0:T(8,128)(2,1)S(1)}, u32[]{:S(2)}, u32[]{:S(2)}) collective-permute-start(bf16[24,16,128]{2,1,0:T(8,128)(2,1)S(1)} %get-tuple-element.113), channel_id=1, source_target_pairs={{0,16},{2,18},{4,20},{6,22},{8,24},{10,26},{12,28},{14,30},{16,0},... | collective-permute-start | bytes 294920 | tf_op jit(solution)/shard_map/ppermute | solution.py:501
  80.8 5.4 %collective-permute-start.19 = (bf16[18,16,128]{2,1,0:T(8,128)(2,1)S(1)}, bf16[18,16,128]{2,1,0:T(8,128)(2,1)S(1)}, u32[]{:S(2)}, u32[]{:S(2)}) collective-permute-start(bf16[18,16,128]{2,1,0:T(8,128)(2,1)S(1)} %get-tuple-element.115), channel_id=1, source_target_pairs={{0,4},{2,6},{4,0},{6,2},{8,12},{10,14},{12,8},{14,10},{16,20},{18,... | collective-permute-start | bytes 221192 | tf_op jit(solution)/shard_map/ppermute | solution.py:501
  82.4 3.8 %collective-permute-start.20 = (bf16[64,128]{1,0:T(8,128)(2,1)S(1)}, bf16[64,128]{1,0:T(8,128)(2,1)S(1)}, u32[]{:S(2)}, u32[]{:S(2)}) collective-permute-start(bf16[64,128]{1,0:T(8,128)(2,1)S(1)} %get-tuple-element.118), channel_id=1, source_target_pairs={{0,1},{1,0},{2,3},{3,2},{4,5},{5,4},{6,7},{7,6},{8,9},{9,8},{10,11... | collective-permute-start | bytes 49160 | tf_op jit(solution)/shard_map/ppermute | solution.py:506
  88.3 73.7 %collective-permute-start.21 = (bf16[3,48,384]{2,1,0:T(8,128)(2,1)S(1)}, bf16[3,48,384]{2,1,0:T(8,128)(2,1)S(1)}, u32[]{:S(2)}, u32[]{:S(2)}) collective-permute-start(bf16[3,48,384]{2,1,0:T(8,128)(2,1)S(1)} %get-tuple-element.119.refs_1_.refs_6_), channel_id=1, source_target_pairs={{1,16},{3,18},{5,20},{7,22},{9,24},{11,26},{13,28},{15,30},{16,1},... | collective-permute-start | bytes 331784 | tf_op jit(solution)/shard_map/ppermute | solution.py:781
  92.7 69.3 %collective-permute-start.22 = (bf16[48,128]{1,0:T(8,128)(2,1)S(1)}, bf16[48,128]{1,0:T(8,128)(2,1)S(1)}, u32[]{:S(2)}, u32[]{:S(2)}) collective-permute-start(bf16[48,128]{1,0:T(8,128)(2,1)S(1)} %get-tuple-element.121), channel_id=1, source_target_pairs={{0,1},{1,0},{2,3},{3,2},{4,5},{5,4},{6,7},{7,6},{8,9},{9,8},{10,11... | collective-permute-start | bytes 36872 | tf_op jit(solution)/shard_map/ppermute | solution.py:506

commit v12 on v9

--- a/solution.py
+++ b/solution.py
@@ -344,8 +344,8 @@
     rows = d_own.shape[1]
     cut = x.shape[1] // copies
     count = tile_count(cut, d_query.shape[0])
-    stride = 2 * count + tile_count(cut, rows * toks)
-    for k, part in enumerate((d_query, d_key)):
+    stride = 3 * count + tile_count(cut, rows * toks)
+    for k, part in enumerate((d_query, d_key, d_value)):
         wide[...] = mm(part[...], x[...])
         cut_wide(copies, toks, core, k * count, stride, wide, kept, sent)
     total = mm(slices[0], d_query[...]) + mm(slices[1], d_key[...])
@@ -354,7 +354,7 @@
     for side, out in ((core, kept), (1 - core, sent)):
         for q in range(copies // 2):
             start = pl.multiple_of((2 * q + side) * cut, 8)
-            put(out, q * stride + 2 * count, total_ref[pl.ds(start, cut), :].astype(bf16))
+            put(out, q * stride + 3 * count, total_ref[pl.ds(start, cut), :].astype(bf16))
     for a in range(toks):
         d_inputs[a] = total[:, a * rows : (a + 1) * rows]
     d_own[...] = d_inputs[t]
@@ -362,24 +362,22 @@
         d_others[r - 1][...] = d_inputs[jnp.bitwise_xor(t, r)].astype(bf16)
 
 
-def second_kernel(copies, toks, ids, x, att, d_value, bias_kept, bias_got, *rest):
-    d_res_parts, (kept, sent, d_res, wide, narrow) = rest[:toks], rest[toks:]
+def second_kernel(copies, toks, ids, att, bias_kept, bias_got, *rest):
+    d_res_parts, (kept, sent, d_res, narrow) = rest[:toks], rest[toks:]
     t, core = ids[0], low_bits(ids[1], 2)
     rows = d_res_parts[0].shape[0]
     cut = narrow.shape[0] // copies
     count = tile_count(cut, narrow.shape[1])
-    wide[...] = mm(d_value[...], x[...])
-    cut_wide(copies, toks, core, 0, 2 * count, wide, kept, sent)
     for r in range(toks):
         start = pl.multiple_of(jnp.bitwise_xor(t, r) * rows, rows)
         d_res[pl.ds(start, rows), :] = d_res_parts[r][...]
     narrow[...] = mm(d_res[...], att[...], TN)
-    base = copies * count
+    base = copies // 2 * count
     bias_count = bias_kept.shape[0] // (copies // 2)
     for side, out in ((core, kept), (1 - core, sent)):
         for q in range(copies // 2):
             first = pl.multiple_of((2 * q + side) * cut, 8)
-            put(out, (2 * q + 1) * count, narrow[pl.ds(first, cut), :].astype(bf16))
+            put(out, q * count, narrow[pl.ds(first, cut), :].astype(bf16))
         for z in range(copies // 4):
             span = pl.ds((2 * z + side) * bias_count, bias_count)
             out[base + z * bias_count : base + (z + 1) * bias_count] = (
@@ -417,18 +415,53 @@
         pieces[r][...] = blocks[jnp.bitwise_xor(ids[0], r)]
 
 
+def across_kernel(wide, lines, segment, ids, kept, got, kept_b, got_b, *outs):
+    t = ids[0]
+    stride = kept.shape[0] // 2
+    step_kernel([(0, 0) + segment], ids, kept_b, got_b, *outs[2:])
+    for side, out in ((t, outs[0]), (1 - t, outs[1])):
+        span = pl.ds(side * stride, wide)
+        out[:wide] = (kept[span].astype(f32) + got[span].astype(f32)).astype(bf16)
+        for a in range(2):
+            for i in range(lines):
+                k = a * stride + wide + 2 * i + side
+                out[wide + a * lines + i] = (
+                    kept[k].astype(f32) + got[k].astype(f32)
+                ).astype(bf16)
+
+
+def far_kernel(wide, lines, half, ids, kept, got, kept_out, sent_out, groups):
+    t, a = ids[0], ids[1] // half
+    groups[t] = kept[:wide]
+    groups[1 - t] = got[:wide]
+    for side, out in ((a, kept_out), (1 - a, sent_out)):
+        out[:wide] = groups[side]
+        span = pl.ds(wide + side * lines, lines)
+        out[wide:] = (kept[span].astype(f32) + got[span].astype(f32)).astype(bf16)
+
+
+def close_kernel(kept, got, kept_b, got_b, terms, *outs):
+    total = kept[...].astype(f32) + got[...].astype(f32)
+    cut, own_width = outs[0].shape
+    count = tile_count(cut, own_width)
+    for k in range(3):
+        outs[k][...] = take(total, k * count, cut, own_width)
+    outs[3][...] = take(kept_b[...].astype(f32) + got_b[...].astype(f32), 0, cut, own_width)
+    outs[4][...] = take(total, 3 * count, cut, outs[4].shape[1])
+    outs[5][...] = jnp.sum(terms[...], axis=0)
+
+
 def last_kernel(toks, ids, kept, got, kept_b, got_b, moved, final, *rest):
     pieces, blocks = rest[:toks], rest[toks]
     first = kept[...].astype(f32) + got[...].astype(f32)
     second = kept_b[...].astype(f32) + got_b[...].astype(f32)
     _, cut, own_width = moved.shape
     count = tile_count(cut, own_width)
-    for k in range(2):
+    for k in range(3):
         moved[k] = take(first, k * count, cut, own_width).astype(bf16)
-    moved[2] = take(second, 0, cut, own_width).astype(bf16)
-    final[...] = take(second, count, cut, own_width)
+    final[...] = take(second, 0, cut, own_width)
     rows = blocks.shape[2]
-    single = take(first, 2 * count, cut, rows * toks)
+    single = take(first, 3 * count, cut, rows * toks)
     for a in range(toks):
         blocks[a] = single[:, a * rows : (a + 1) * rows]
     for r in range(toks):
@@ -659,7 +692,7 @@
 
     wide_tiles = tile_count(cut, own_width)
     single_tiles = tile_count(cut, tokens)
-    first_tiles, second_tiles = 2 * wide_tiles + single_tiles, 2 * wide_tiles
+    first_tiles, second_tiles = 3 * wide_tiles + single_tiles, wide_tiles
     found = call(
         functools.partial(first_kernel, copies, toks),
         "first",
@@ -672,7 +705,7 @@
             VMEM((toks, width, rows), f32),
             VMEM((width, tokens), f32),
         ],
-        flops=10 * tokens * width * own_width,
+        flops=12 * tokens * width * own_width,
     )
     kept, sent, d_own = found[:3]
     got = swap_copy(sent, 1)
@@ -706,14 +739,10 @@
     kept_b, sent_b = call(
         functools.partial(second_kernel, copies, toks),
         "second",
-        [where_am_i, x, att, d_value, bias_kept, bias_got] + d_res_parts,
+        [where_am_i, att, bias_kept, bias_got] + d_res_parts,
         [((copies // 2 * second_tiles + copies // 4 * bias_tiles, 16, 128), bf16)] * 2,
-        [
-            VMEM((tokens, width), bf16),
-            VMEM((own_width, width), f32),
-            VMEM((width, own_width), f32),
-        ],
-        flops=4 * tokens * width * own_width,
+        [VMEM((tokens, width), bf16), VMEM((width, own_width), f32)],
+        flops=2 * tokens * width * own_width,
     )
     got_b = swap_copy(sent_b, 1)
 
@@ -735,8 +764,21 @@
             segments.append((1, bias_base, parts // 2, bias_tiles, mask_b, masks_b[n:-1], 1))
         else:
             bias_ready = pairs[1]
+            if toks == 2:
+                break
         pairs = step("step_%d" % n, pairs, segments, deps=[exited] if n == 1 else ())
         parts //= 2
+    if toks == 2:
+        wide, lines = 3 * wide_tiles, single_tiles // 2
+        kept, sent, kept_b, sent_b = call(
+            functools.partial(
+                across_kernel, wide, lines, (2, second_tiles, masks_b[-1], 1, 0, 0)
+            ),
+            "across",
+            [where_am_i] + [array for one in pairs for array in one],
+            [((wide + 2 * lines, 16, 128), bf16)] * 2 + [((second_tiles, 16, 128), bf16)] * 2,
+        )
+        pairs = [(kept, swap_tok(sent, 1)), (kept_b, swap_copy(sent_b, masks_b[-1]))]
     bias_pieces = call(
         functools.partial(last_bias_kernel, toks, bias_base, bias_tiles, cols),
         "last_bias",
@@ -746,6 +788,18 @@
         deps=[pairs[0][0]],
     )
     bias_pieces = [bias_pieces[0]] + [swap_tok(bias_pieces[r], r) for r in range(1, toks)]
+    ready = [pairs[0][1], pairs[1][1]]
+    if toks == 2:
+        kept, sent = call(
+            functools.partial(far_kernel, wide, lines, copies // 2),
+            "far",
+            [where_am_i, *pairs[0]],
+            [((wide + lines, 16, 128), bf16)] * 2,
+            [VMEM((2, wide, 16, 128), bf16)],
+            deps=[pairs[1][1]] + bias_pieces[1:],
+        )
+        pairs[0] = (kept, swap_copy(sent, copies // 2))
+        ready = [kept]
 
     group = copies // toks
     swaps = []
@@ -760,15 +814,7 @@
         [((devices, heads, channels), f32)],
         [VMEM((heads * cols, rows), f32)],
         flops=2 * heads * cols * rows * channels * cols,
-        deps=[pairs[0][1], pairs[1][1]],
-    )
-    last = call(
-        functools.partial(last_kernel, toks),
-        "last",
-        [where_am_i, *pairs[0], *pairs[1]],
-        [((3, cut, own_width), bf16), ((cut, own_width), f32)] + [((cut, rows), bf16)] * toks,
-        [VMEM((toks, cut, rows), f32)],
-        deps=[weight_grad],
+        deps=ready,
     )
     (grad_pair,) = call(
         functools.partial(pair_kernel, toks, cols),
@@ -777,18 +823,33 @@
         [((rows * cols, channels), bf16)],
         [VMEM((rows * cols, channels), f32), VMEM((heads * cols, rows), f32)],
         flops=2 * heads * cols * rows * channels * cols,
-        deps=[last[0]],
-    )
-    weight_grad = jnp.sum(exchange(weight_grad), axis=0)
-    grad_out, singles = last[1], last[2:]
-    singles = [singles[0]] + [swap_tok(singles[r], r) for r in range(1, toks)]
-    moved = lax.ppermute(last[0], ("copy", "tok"), swaps)
-    grad_query, grad_key, grad_value, grad_single = call(
-        finish_kernel,
-        "finish",
-        [moved] + singles,
-        [((cut, own_width), f32)] * 3 + [((cut, rows), f32)],
-    )
+    )
+    weight_terms = exchange(weight_grad)
+    if toks == 2:
+        grad_query, grad_key, grad_value, grad_out, grad_single, weight_grad = call(
+            close_kernel,
+            "close",
+            [*pairs[0], *pairs[1], weight_terms],
+            [((cut, own_width), f32)] * 4 + [((cut, rows), f32), ((heads, channels), f32)],
+        )
+    else:
+        last = call(
+            functools.partial(last_kernel, toks),
+            "last",
+            [where_am_i, *pairs[0], *pairs[1]],
+            [((3, cut, own_width), bf16), ((cut, own_width), f32)] + [((cut, rows), bf16)] * toks,
+            [VMEM((toks, cut, rows), f32)],
+        )
+        weight_grad = jnp.sum(weight_terms, axis=0)
+        grad_out, singles = last[1], last[2:]
+        singles = [singles[0]] + [swap_tok(singles[r], r) for r in range(1, toks)]
+        moved = lax.ppermute(last[0], ("copy", "tok"), swaps)
+        grad_query, grad_key, grad_value, grad_single = call(
+            finish_kernel,
+            "finish",
+            [moved] + singles,
+            [((cut, own_width), f32)] * 3 + [((cut, rows), f32)],
+        )
     return (
         grad_noisy[None],
         grad_single.T,

time: 108 us -> 114 us (1.056); the launches traced: 107 us -> 112 us
  waiting for transfers between devices: 44.2 us -> 52.7 us
  starting transfers between devices: 27.3 us -> 25.5 us
    ppermute x14, waiting for transfers between devices: 20.7 us -> 31.6 us  [swap_copy(): return lax.ppermute(value, 'copy', [(i, i ^ mask) for i in range(size)])]
    ppermute x1 -> x0, starting transfers between devices: 4.27 us -> none  [per_device(): moved = lax.ppermute(last[0], ('copy', 'tok'), swaps)]
    ppermute x1 -> x0, waiting for transfers between devices: 3.13 us -> none  [per_device(): moved = lax.ppermute(last[0], ('copy', 'tok'), swaps)]
    ppermute x8, starting transfers between devices: 4.57 us -> 7.48 us  [swap_tok(): return lax.ppermute(value, 'tok', [(i, i ^ mask) for i in range(size)])]
    all_to_all x1, starting transfers between devices: 5.09 us -> 3.3 us  [exchange(): return lax.all_to_all(value, ('copy', 'tok'), 0, 0)]
    ppermute x14, starting transfers between devices: 13.4 us -> 14.7 us  [swap_copy(): return lax.ppermute(value, 'copy', [(i, i ^ mask) for i in range(size)])]
    unnamed x42 -> x40, local copies, waits for them, and re-layouts: 4.05 us -> 3.38 us
  transfers between devices with their start and end apart: 24 -> 23, of which waited for: 16 -> 15; matrix products, arithmetic and copies ran while one was open for 0% -> 0% of each run, Pallas kernels for 12% -> 8%
where the time goes in v12:
time: 114 us; the launch traced here: 112 us
  waiting for transfers between devices  52.7 us (46%)
  Pallas kernels  29.1 us (26%)
  starting transfers between devices  25.5 us (22%)
  local copies, waits for them, and re-layouts  3.38 us (3%)
    ppermute x14, waiting for transfers between devices, swap_copy(): return lax.ppermute(value, 'copy', [(i, i ^ mask) for i in range(size)])  31.6 us
    pallas_call x21, Pallas kernels, call(): pl.pallas_call(whole, name=name, out_shape=[jax.ShapeDtypeStruct(one[0],...  29.1 us
    ppermute x8, waiting for transfers between devices, swap_tok(): return lax.ppermute(value, 'tok', [(i, i ^ mask) for i in range(size)])  21.2 us
    ppermute x14, starting transfers between devices, swap_copy(): return lax.ppermute(value, 'copy', [(i, i ^ mask) for i in range(size)])  14.7 us
    ppermute x8, starting transfers between devices, swap_tok(): return lax.ppermute(value, 'tok', [(i, i ^ mask) for i in range(size)])  7.48 us
    unnamed x40, local copies, waits for them, and re-layouts  3.38 us
    all_to_all x1, starting transfers between devices, exchange(): return lax.all_to_all(value, ('copy', 'tok'), 0, 0)  3.3 us
  transfers between devices with their start and end apart: 23, of which 15 were waited for; matrix products, arithmetic and copies ran while one was open for 0% of the time, Pallas kernels for 8%

profile of v12, /device:TPU:2, one launch (start us, length us, event | category | flops | bytes accessed | tf_op | source)
XLA Modules:
  0.0 112.2 jit_solution(857754983289404347)
XLA Ops:
  0.6 0.6 pad_add_fusion.refs_0_
  1.2 4.3 %enter.1 = (bf16[128,768]{1,0:T(8,128)(2,1)}, bf16[16,128,128]{2,1,0:T(8,128)(2,1)}, f32[256,128]{1,0:T(8,128)}, f32[1,256]{1,0:T(1,128)}, bf16[2,64,128]{2,1,0:T(8,128)(2,1)}) custom-call(s32[2]{0:T(128)} %pad_add_fusion.refs_0_, bf16[128,768]{1,0:T(8,128)(2,1)} %bitcast.20, bf16[128,768]{1,0:T(8,128)(2,1)} %refs_2_.2, s32[1,128]{1,0:T(1,128)} %bitcast.30, ...), custom_call_target="tpu_custom_call" | custom-call | flops 67108864 | bytes 1860808 | tf_op jit(solution)/shard_map/enter/pallas_call | solution.py:79
  5.5 0.1 collective-permute-start.3
  5.6 2.1 %collective-permute-start = (bf16[2,64,128]{2,1,0:T(8,128)(2,1)}, bf16[2,64,128]{2,1,0:T(8,128)(2,1)S(1)}, u32[]{:S(2)}, u32[]{:S(2)}) collective-permute-start(bf16[2,64,128]{2,1,0:T(8,128)(2,1)} %get-tuple-element.71.refs_0_), channel_id=1, source_target_pairs={{0,8},{2,10},{4,12},{6,14},{8,0},{10,2},{12,4},{14,6},{16,24},{18,... | collective-permute-start | bytes 98312 | tf_op jit(solution)/shard_map/ppermute | solution.py:533
  7.7 2.6 %collective-permute-start.1 = (bf16[2,64,128]{2,1,0:T(8,128)(2,1)}, bf16[2,64,128]{2,1,0:T(8,128)(2,1)S(1)}, u32[]{:S(2)}, u32[]{:S(2)}) collective-permute-start(bf16[2,64,128]{2,1,0:T(8,128)(2,1)} %get-tuple-element.71.refs_0_), channel_id=1, source_target_pairs={{0,16},{2,18},{4,20},{6,22},{8,24},{10,26},{12,28},{14,30},{16,0},... | collective-permute-start | bytes 98312 | tf_op jit(solution)/shard_map/ppermute | solution.py:533
  10.3 2.7 %collective-permute-done.1.refs_2_ = bf16[2,64,128]{2,1,0:T(8,128)(2,1)S(1)} collective-permute-done((bf16[2,64,128]{2,1,0:T(8,128)(2,1)}, bf16[2,64,128]{2,1,0:T(8,128)(2,1)S(1)}, u32[]{:S(2)}, u32[]{:S(2)}) %collective-permute-start.1) | collective-permute-done | bytes 32800 | tf_op jit(solution)/shard_map/ppermute | solution.py:533
  13.0 3.2 %collective-permute-done.2.refs_3_ = bf16[2,64,128]{2,1,0:T(8,128)(2,1)S(1)} collective-permute-done((bf16[2,64,128]{2,1,0:T(8,128)(2,1)}, bf16[2,64,128]{2,1,0:T(8,128)(2,1)S(1)}, u32[]{:S(2)}, u32[]{:S(2)}) %collective-permute-start.2) | collective-permute-done | bytes 32800 | tf_op jit(solution)/shard_map/ppermute | solution.py:533
  16.2 0.8 copy-done.14
  17.0 1.6 %collective-permute-start.4 = (bf16[4,64,128]{2,1,0:T(8,128)(2,1)S(1)}, bf16[4,64,128]{2,1,0:T(8,128)(2,1)S(1)}, u32[]{:S(2)}, u32[]{:S(2)}) collective-permute-start(bf16[4,64,128]{2,1,0:T(8,128)(2,1)S(1)} %get-tuple-element.77), channel_id=1, source_target_pairs={{0,1},{1,0},{2,3},{3,2},{4,5},{5,4},{6,7},{7,6},{8,9},{9,8},{10,11... | collective-permute-start | bytes 196616 | tf_op jit(solution)/shard_map/ppermute | solution.py:538
  18.6 1.3 %copy-done.5 = bf16[768,768]{1,0:T(8,128)(2,1)S(1)} copy-done((bf16[768,768]{1,0:T(8,128)(2,1)S(1)}, bf16[768,768]{1,0:T(8,128)(2,1)}, u32[]{:S(2)}) %copy-start.5) | copy-done | bytes 1179672
  19.8 1.3 %copy-done.6 = bf16[768,768]{1,0:T(8,128)(2,1)S(1)} copy-done((bf16[768,768]{1,0:T(8,128)(2,1)S(1)}, bf16[768,768]{1,0:T(8,128)(2,1)}, u32[]{:S(2)}) %copy-start.6) | copy-done | bytes 1179672
  21.1 0.8 stage.1.refs_1_.refs_2_
  21.9 0.0 copy-start.11
  21.9 0.0 collective-permute-done.4.refs_1_
  21.9 0.0 copy-start.2
  21.9 0.0 copy-start.17
  21.9 1.6 %collective-permute-start.5 = (bf16[2,4,64,128]{3,2,1,0:T(8,128)(2,1)S(1)}, bf16[2,4,64,128]{3,2,1,0:T(8,128)(2,1)S(1)}, u32[]{:S(2)}, u32[]{:S(2)}) collective-permute-start(bf16[2,4,64,128]{3,2,1,0:T(8,128)(2,1)S(1)} %join_tok.1.refs_0_), channel_id=1, source_target_pairs={{0,4},{2,6},{4,0},{6,2},{8,12},{10,14},{12,8},{14,10},{16,20},{18,... | collective-permute-start | bytes 393224 | tf_op jit(solution)/shard_map/ppermute | solution.py:533
  23.5 1.4 %project.1 = (bf16[256,768]{1,0:T(8,128)(2,1)S(1)}, bf16[384,256]{1,0:T(8,128)(2,1)S(1)}, bf16[384,256]{1,0:T(8,128)(2,1)S(1)}, bf16[384,256]{1,0:T(8,128)(2,1)S(1)}) custom-call(s32[2]{0:T(128)S(1)} %copy-done.13, bf16[3,768,384]{2,1,0:T(8,128)(2,1)S(1)} %stage.1.refs_1_.refs_2_, bf16[128,768]{1,0:T(8,128)(2,1)S(1)} %copy-done.11, ...), custom_call_target="tpu_custom_call" | custom-call | flops 452984832 | bytes 3145736 | tf_op jit(solution)/shard_map/project/pallas_call | solution.py:79
  24.9 0.0 copy-start.19
  25.0 2.0 %collective-permute-done.5.refs_1_ = bf16[2,4,64,128]{3,2,1,0:T(8,128)(2,1)S(1)} collective-permute-done((bf16[2,4,64,128]{3,2,1,0:T(8,128)(2,1)S(1)}, bf16[2,4,64,128]{3,2,1,0:T(8,128)(2,1)S(1)}, u32[]{:S(2)}, u32[]{:S(2)}) %collective-permute-start.5) | collective-permute-done | bytes 131104 | tf_op jit(solution)/shard_map/ppermute | solution.py:533
  27.0 0.1 collective-permute-start.6
  27.1 1.5 %collective-permute-done.6.refs_5_ = bf16[2,2,4,64,128]{4,3,2,1,0:T(8,128)(2,1)S(1)} collective-permute-done((bf16[2,2,4,64,128]{4,3,2,1,0:T(8,128)(2,1)S(1)}, bf16[2,2,4,64,128]{4,3,2,1,0:T(8,128)(2,1)S(1)}, u32[]{:S(2)}, u32[]{:S(2)}) %collective-permute-start.6) | collective-permute-done | bytes 262176 | tf_op jit(solution)/shard_map/ppermute | solution.py:533
  28.6 2.1 %attention.1 = (bf16[4,256,256]{2,1,0:T(8,128)(2,1)S(1)}, bf16[256,384]{1,0:T(8,128)(2,1)S(1)}, bf16[128,384]{1,0:T(8,128)(2,1)S(1)}, bf16[128,384]{1,0:T(8,128)(2,1)S(1)}) custom-call(s32[2]{0:T(128)S(1)} %copy-done.13, bf16[384,256]{1,0:T(8,128)(2,1)S(1)} %get-tuple-element.74.refs_1_, bf16[384,256]{1,0:T(8,128)(2,1)S(1)} %get-tuple-element.75.refs_2_, ...), custom_call_target="tpu_custom_call" | custom-call | flops 100663296 | bytes 2163720 | tf_op jit(solution)/shard_map/attention/pallas_call | solution.py:79
  30.8 1.0 collective-permute-start.7
  31.8 0.0 copy-start
  31.8 0.9 down.1
  32.7 3.0 %collective-permute-done.7.refs_6_ = bf16[128,384]{1,0:T(8,128)(2,1)S(1)} collective-permute-done((bf16[128,384]{1,0:T(8,128)(2,1)S(1)}, bf16[128,384]{1,0:T(8,128)(2,1)S(1)}, u32[]{:S(2)}, u32[]{:S(2)}) %collective-permute-start.7) | collective-permute-done | bytes 98336 | tf_op jit(solution)/shard_map/ppermute | solution.py:538
  35.7 4.3 %hidden.1 = (f32[128,768]{1,0:T(8,128)S(1)}, bf16[128,768]{1,0:T(8,128)(2,1)S(1)}, bf16[384,128]{1,0:T(8,128)(2,1)S(1)}, bf16[384,128]{1,0:T(8,128)(2,1)S(1)}) custom-call(s32[2]{0:T(128)S(1)} %copy-done.13, bf16[128,768]{1,0:T(8,128)(2,1)S(1)} %get-tuple-element.67.refs_1_.refs_0_, bf16[128,768]{1,0:T(8,128)(2,1)S(1)} %get-tuple-element.68.refs_2_, ...), custom_call_target="tpu_custom_call" | custom-call | flops 1509949440 | bytes 8064008 | tf_op jit(solution)/shard_map/hidden/pallas_call | solution.py:79
  40.0 0.9 collective-permute-start.8
  40.9 3.7 %collective-permute-done.8.refs_6_ = bf16[384,128]{1,0:T(8,128)(2,1)S(1)} collective-permute-done((bf16[384,128]{1,0:T(8,128)(2,1)S(1)}, bf16[384,128]{1,0:T(8,128)(2,1)S(1)}, u32[]{:S(2)}, u32[]{:S(2)}) %collective-permute-start.8) | collective-permute-done | bytes 98336 | tf_op jit(solution)/shard_map/ppermute | solution.py:538
  44.7 2.0 %backward.1 = (bf16[384,256]{1,0:T(8,128)(2,1)S(1)}, bf16[384,256]{1,0:T(8,128)(2,1)S(1)}, bf16[384,256]{1,0:T(8,128)(2,1)S(1)}, bf16[64,16,128]{2,1,0:T(8,128)(...) custom-call(s32[2]{0:T(128)S(1)} %copy-done.13, ...), custom_call_target="tpu_custom_call" | custom-call | flops 201326592 | bytes 2818056 | tf_op jit(solution)/shard_map/backward/pallas_call | solution.py:79
  46.7 2.4 %first.1 = (bf16[264,16,128]{2,1,0:T(8,128)(2,1)S(1)}, bf16[264,16,128]{2,1,0:T(8,128)(2,1)S(1)}, f32[768,128]{1,0:T(8,128)S(1)}, bf16[768,128]{1,0:T(8,128)(2,1)S(1)}) custom-call(s32[2]{0:T(128)S(1)} %copy-done.13, bf16[3,768,384]{2,1,0:T(8,128)(2,1)S(1)} %stage.1.refs_1_.refs_2_, bf16[256,768]{1,0:T(8,128)(2,1)S(1)} %get-tuple-element.83.refs_2_, ...), custom_call_target="tpu_custom_call" | custom-call | flops 905969664 | bytes 5505032 | tf_op jit(solution)/shard_map/first/pallas_call | solution.py:79
  49.1 0.1 collective-permute-start.10
  49.2 1.6 %collective-permute-start.11 = (bf16[64,16,128]{2,1,0:T(8,128)(2,1)S(1)}, bf16[64,16,128]{2,1,0:T(8,128)(2,1)S(1)}, u32[]{:S(2)}, u32[]{:S(2)}) collective-permute-start(bf16[64,16,128]{2,1,0:T(8,128)(2,1)S(1)} %get-tuple-element.98), channel_id=1, source_target_pairs={{0,4},{2,6},{4,0},{6,2},{8,12},{10,14},{12,8},{14,10},{16,20},{18,... | collective-permute-start | bytes 786440 | tf_op jit(solution)/shard_map/ppermute | solution.py:533
  50.8 0.9 collective-permute-start.12
  51.7 6.1 %collective-permute-done.12.refs_5_ = bf16[128,768]{1,0:T(8,128)(2,1)S(1)} collective-permute-done((bf16[128,768]{1,0:T(8,128)(2,1)S(1)}, bf16[128,768]{1,0:T(8,128)(2,1)S(1)}, u32[]{:S(2)}, u32[]{:S(2)}) %collective-permute-start.12) | collective-permute-done | bytes 196640 | tf_op jit(solution)/shard_map/ppermute | solution.py:538
  57.7 0.2 collective-permute-done.11.refs_3_
  57.9 1.1 second.1
  59.0 0.1 collective-permute-start.13
  59.0 1.8 %collective-permute-done.13.refs_4_ = bf16[104,16,128]{2,1,0:T(8,128)(2,1)S(1)} collective-permute-done((bf16[104,16,128]{2,1,0:T(8,128)(2,1)S(1)}, bf16[104,16,128]{2,1,0:T(8,128)(2,1)S(1)}, u32[]{:S(2)}, u32[]{:S(2)}) %collective-permute-start.13) | collective-permute-done | bytes 426016 | tf_op jit(solution)/shard_map/ppermute | solution.py:533
  60.8 0.9 step_0.1
  61.7 1.6 %collective-permute-start.14 = (bf16[132,16,128]{2,1,0:T(8,128)(2,1)S(1)}, bf16[132,16,128]{2,1,0:T(8,128)(2,1)S(1)}, u32[]{:S(2)}, u32[]{:S(2)}) collective-permute-start(bf16[132,16,128]{2,1,0:T(8,128)(2,1)S(1)} %get-tuple-element.103), channel_id=1, source_target_pairs={{0,4},{2,6},{4,0},{6,2},{8,12},{10,14},{12,8},{14,10},{16,20},{18,... | collective-permute-start | bytes 1622024 | tf_op jit(solution)/shard_map/ppermute | solution.py:533
  63.3 0.9 collective-permute-start.9
  64.2 5.8 %collective-permute-done.9.refs_4_ = bf16[768,128]{1,0:T(8,128)(2,1)S(1)} collective-permute-done((bf16[768,128]{1,0:T(8,128)(2,1)S(1)}, bf16[768,128]{1,0:T(8,128)(2,1)S(1)}, u32[]{:S(2)}, u32[]{:S(2)}) %collective-permute-start.9) | collective-permute-done | bytes 196640 | tf_op jit(solution)/shard_map/ppermute | solution.py:538
  69.9 1.2 %exit.1 = (bf16[128,768]{1,0:T(8,128)(2,1)}, f32[8,128]{1,0:T(8,128)S(1)}) custom-call(bf16[128,768]{1,0:T(8,128)(2,1)S(1)} %get-tuple-element.67.refs_1_.refs_0_, f32[1,768]{1,0:T(1,128)S(1)} %reshape.49.refs_1_, f32[128,768]{1,0:T(8,128)S(1)} %get-tuple-element.82.refs_2_, f32[768,128]{1,0:T(8,128)S(1)} %get-tuple-element.91.refs_3_, ...), custom_call_target="tpu_custom_call" | custom-call | bytes 1383424 | tf_op jit(solution)/shard_map/exit/pallas_call | solution.py:79
  71.2 4.9 %collective-permute-done.14.refs_2_ = bf16[132,16,128]{2,1,0:T(8,128)(2,1)S(1)} collective-permute-done((bf16[132,16,128]{2,1,0:T(8,128)(2,1)S(1)}, bf16[132,16,128]{2,1,0:T(8,128)(2,1)S(1)}, u32[]{:S(2)}, u32[]{:S(2)}) %collective-permute-start.14) | collective-permute-done | bytes 540704 | tf_op jit(solution)/shard_map/ppermute | solution.py:533
  76.1 0.7 step_1.1
  76.8 0.1 collective-permute-start.16
  76.9 0.9 collective-permute-start.17
  77.8 6.9 %collective-permute-done.17.refs_4_.refs_2_ = bf16[26,16,128]{2,1,0:T(8,128)(2,1)S(1)} collective-permute-done((bf16[26,16,128]{2,1,0:T(8,128)(2,1)S(1)}, bf16[26,16,128]{2,1,0:T(8,128)(2,1)S(1)}, u32[]{:S(2)}, u32[]{:S(2)}) %collective-permute-start.17) | collective-permute-done | bytes 106528 | tf_op jit(solution)/shard_map/ppermute | solution.py:533
  84.7 2.2 %collective-permute-done.16.refs_2_ = bf16[66,16,128]{2,1,0:T(8,128)(2,1)S(1)} collective-permute-done((bf16[66,16,128]{2,1,0:T(8,128)(2,1)S(1)}, bf16[66,16,128]{2,1,0:T(8,128)(2,1)S(1)}, u32[]{:S(2)}, u32[]{:S(2)}) %collective-permute-start.16) | collective-permute-done | bytes 270368 | tf_op jit(solution)/shard_map/ppermute | solution.py:533
  86.9 0.6 across.1
  87.5 0.9 collective-permute-start.18
  88.5 1.5 %collective-permute-start.19 = (bf16[9,16,128]{2,1,0:T(8,128)(2,1)S(1)}, bf16[9,16,128]{2,1,0:T(8,128)(2,1)S(1)}, u32[]{:S(2)}, u32[]{:S(2)}) collective-permute-start(bf16[9,16,128]{2,1,0:T(8,128)(2,1)S(1)} %get-tuple-element.113), channel_id=1, source_target_pairs={{0,4},{2,6},{4,0},{6,2},{8,12},{10,14},{12,8},{14,10},{16,20},{18,... | collective-permute-start | bytes 110600 | tf_op jit(solution)/shard_map/ppermute | solution.py:533
  90.0 0.6 last_bias.1
  90.6 1.2 %collective-permute-start.20 = (bf16[64,128]{1,0:T(8,128)(2,1)S(1)}, bf16[64,128]{1,0:T(8,128)(2,1)S(1)}, u32[]{:S(2)}, u32[]{:S(2)}) collective-permute-start(bf16[64,128]{1,0:T(8,128)(2,1)S(1)} %get-tuple-element.114), channel_id=1, source_target_pairs={{0,1},{1,0},{2,3},{3,2},{4,5},{5,4},{6,7},{7,6},{8,9},{9,8},{10,11... | collective-permute-start | bytes 49160 | tf_op jit(solution)/shard_map/ppermute | solution.py:538
  91.8 2.6 %collective-permute-done.20.refs_4_.refs_3_.refs_5_ = bf16[64,128]{1,0:T(8,128)(2,1)S(1)} collective-permute-done((bf16[64,128]{1,0:T(8,128)(2,1)S(1)}, bf16[64,128]{1,0:T(8,128)(2,1)S(1)}, u32[]{:S(2)}, u32[]{:S(2)}) %collective-permute-start.20) | collective-permute-done | bytes 16416 | tf_op jit(solution)/shard_map/ppermute | solution.py:538
  94.4 0.6 far.1
  95.0 1.6 %pair_weight.1 = f32[32,8,128]{2,1,0:T(8,128)} custom-call(s32[2]{0:T(128)S(1)} %copy-done.13, bf16[16,128,128]{2,1,0:T(8,128)(2,1)S(1)} %copy-done.9, bf16[64,128]{1,0:T(8,128)(2,1)S(1)} %get-tuple-element.119.refs_2_.refs_4_, bf16[64,128]{1,0:T(8,128)(2,1)S(1)} %collective-permute-done.20.refs_4_.refs_3_.refs_5_, ...), custom_call_target="tpu_custom_call" | custom-call | flops 67108864 | bytes 688136 | tf_op jit(solution)/shard_map/pair_weight/pallas_call | solution.py:79
  96.5 3.3 %all-to-all-start = ((f32[32,8,128]{2,1,0:T(8,128)}), f32[32,8,128]{2,1,0:T(8,128)S(1)}, u32[]{:S(2)}, u32[]{:S(2)}) async-start(f32[32,8,128]{2,1,0:T(8,128)} %pair_weight.1), calls=%async_computation | async-start | bytes 262144 | tf_op jit(solution)/shard_map/all_to_all | solution.py:542
  99.8 2.6 %collective-permute-start.21 = (bf16[30,16,128]{2,1,0:T(8,128)(2,1)S(1)}, bf16[30,16,128]{2,1,0:T(8,128)(2,1)S(1)}, u32[]{:S(2)}, u32[]{:S(2)}) collective-permute-start(bf16[30,16,128]{2,1,0:T(8,128)(2,1)S(1)} %get-tuple-element.116), channel_id=1, source_target_pairs={{0,16},{2,18},{4,20},{6,22},{8,24},{10,26},{12,28},{14,30},{16,0},... | collective-permute-start | bytes 368648 | tf_op jit(solution)/shard_map/ppermute | solution.py:533
  102.4 2.9 %pair.1 = bf16[2048,128]{1,0:T(8,128)(2,1)} custom-call(s32[2]{0:T(128)S(1)} %copy-done.13, bf16[2048,128]{1,0:T(8,128)(2,1)S(1)} %bitcast.19, f32[1,128]{1,0:T(1,128)S(1)} %bitcast.26, bf16[8,128]{1,0:T(8,128)(2,1)S(1)} %bitcast.24, bf16[64,128]{1,0:T(8,128)(2,1)S(1)} %get-tuple-element.119.refs_2_.refs_4_, ...), custom_call_target="tpu_custom_call" | custom-call | flops 67108864 | bytes 1083912 | tf_op jit(solution)/shard_map/pair/pallas_call | solution.py:79
  105.3 6.2 %collective-permute-done.21.refs_1_ = bf16[30,16,128]{2,1,0:T(8,128)(2,1)S(1)} collective-permute-done((bf16[30,16,128]{2,1,0:T(8,128)(2,1)S(1)}, bf16[30,16,128]{2,1,0:T(8,128)(2,1)S(1)}, u32[]{:S(2)}, u32[]{:S(2)}) %collective-permute-start.21) | collective-permute-done | bytes 122912 | tf_op jit(solution)/shard_map/ppermute | solution.py:533
  111.5 0.7 close.1
  (46 shorter events, 0.1 us)
Async XLA Ops:
  0.6 17.9 %copy-start.4 = (bf16[768,768]{1,0:T(8,128)(2,1)S(1)}, bf16[768,768]{1,0:T(8,128)(2,1)}, u32[]{:S(2)}) copy-start(bf16[768,768]{1,0:T(8,128)(2,1)} %refs_1_.3) | copy-start | bytes 3538948
  1.2 17.3 %copy-start.13 = (s32[2]{0:T(128)S(1)}, s32[2]{0:T(128)}, u32[]{:S(2)}) copy-start(s32[2]{0:T(128)} %pad_add_fusion.refs_0_) | copy-start | bytes 28
  5.5 10.7 %collective-permute-start.3 = (bf16[128,768]{1,0:T(8,128)(2,1)}, bf16[128,768]{1,0:T(8,128)(2,1)S(1)}, u32[]{:S(2)}, u32[]{:S(2)}) collective-permute-start(bf16[128,768]{1,0:T(8,128)(2,1)} %get-tuple-element.72.refs_2_), channel_id=1, source_target_pairs={{0,1},{1,0},{2,3},{3,2},{4,5},{5,4},{6,7},{7,6},{8,9},{9,8},{10,11... | collective-permute-start | bytes 589832 | tf_op jit(solution)/shard_map/ppermute | solution.py:538
  5.6 4.7 %collective-permute-start = (bf16[2,64,128]{2,1,0:T(8,128)(2,1)}, bf16[2,64,128]{2,1,0:T(8,128)(2,1)S(1)}, u32[]{:S(2)}, u32[]{:S(2)}) collective-permute-start(bf16[2,64,128]{2,1,0:T(8,128)(2,1)} %get-tuple-element.71.refs_0_), channel_id=1, source_target_pairs={{0,8},{2,10},{4,12},{6,14},{8,0},{10,2},{12,4},{14,6},{16,24},{18,... | collective-permute-start | bytes 98312 | tf_op jit(solution)/shard_map/ppermute | solution.py:533
  7.7 5.3 %collective-permute-start.1 = (bf16[2,64,128]{2,1,0:T(8,128)(2,1)}, bf16[2,64,128]{2,1,0:T(8,128)(2,1)S(1)}, u32[]{:S(2)}, u32[]{:S(2)}) collective-permute-start(bf16[2,64,128]{2,1,0:T(8,128)(2,1)} %get-tuple-element.71.refs_0_), channel_id=1, source_target_pairs={{0,16},{2,18},{4,20},{6,22},{8,24},{10,26},{12,28},{14,30},{16,0},... | collective-permute-start | bytes 98312 | tf_op jit(solution)/shard_map/ppermute | solution.py:533
  10.3 5.9 %collective-permute-start.2 = (bf16[2,64,128]{2,1,0:T(8,128)(2,1)}, bf16[2,64,128]{2,1,0:T(8,128)(2,1)S(1)}, u32[]{:S(2)}, u32[]{:S(2)}) collective-permute-start(bf16[2,64,128]{2,1,0:T(8,128)(2,1)} %get-tuple-element.71.refs_0_), channel_id=1, source_target_pairs={{0,24},{2,26},{4,28},{6,30},{8,16},{10,18},{12,20},{14,22},{16,8},... | collective-permute-start | bytes 98312 | tf_op jit(solution)/shard_map/ppermute | solution.py:533
  16.2 0.8 copy-start.14
  17.0 4.9 %collective-permute-start.4 = (bf16[4,64,128]{2,1,0:T(8,128)(2,1)S(1)}, bf16[4,64,128]{2,1,0:T(8,128)(2,1)S(1)}, u32[]{:S(2)}, u32[]{:S(2)}) collective-permute-start(bf16[4,64,128]{2,1,0:T(8,128)(2,1)S(1)} %get-tuple-element.77), channel_id=1, source_target_pairs={{0,1},{1,0},{2,3},{3,2},{4,5},{5,4},{6,7},{7,6},{8,9},{9,8},{10,11... | collective-permute-start | bytes 196616 | tf_op jit(solution)/shard_map/ppermute | solution.py:538
  18.6 1.3 %copy-start.5 = (bf16[768,768]{1,0:T(8,128)(2,1)S(1)}, bf16[768,768]{1,0:T(8,128)(2,1)}, u32[]{:S(2)}) copy-start(bf16[768,768]{1,0:T(8,128)(2,1)} %refs_2_.3) | copy-start | bytes 3538948
  19.8 1.3 %copy-start.6 = (bf16[768,768]{1,0:T(8,128)(2,1)S(1)}, bf16[768,768]{1,0:T(8,128)(2,1)}, u32[]{:S(2)}) copy-start(bf16[768,768]{1,0:T(8,128)(2,1)} %refs_3_.1) | copy-start | bytes 3538948
  21.1 7.5 %copy-start.12 = (f32[256,128]{1,0:T(8,128)S(1)}, f32[256,128]{1,0:T(8,128)}, u32[]{:S(2)}) copy-start(f32[256,128]{1,0:T(8,128)} %get-tuple-element.78.refs_6_) | copy-start | bytes 393220
  21.9 1.6 %copy-start.11 = (bf16[128,768]{1,0:T(8,128)(2,1)S(1)}, bf16[128,768]{1,0:T(8,128)(2,1)}, u32[]{:S(2)}) copy-start(bf16[128,768]{1,0:T(8,128)(2,1)} %get-tuple-element.72.refs_2_) | copy-start | bytes 589828
  21.9 9.8 %copy-start.2 = (bf16[1536,768]{1,0:T(8,128)(2,1)S(1)}, bf16[1536,768]{1,0:T(8,128)(2,1)}, u32[]{:S(2)}) copy-start(bf16[1536,768]{1,0:T(8,128)(2,1)} %refs_1_.2) | copy-start | bytes 7077892
  21.9 6.7 %copy-start.17 = (f32[1,256]{1,0:T(1,128)S(1)}, f32[1,256]{1,0:T(1,128)}, u32[]{:S(2)}) copy-start(f32[1,256]{1,0:T(1,128)} %get-tuple-element.79.refs_7_) | copy-start | bytes 3076
  21.9 5.0 %collective-permute-start.5 = (bf16[2,4,64,128]{3,2,1,0:T(8,128)(2,1)S(1)}, bf16[2,4,64,128]{3,2,1,0:T(8,128)(2,1)S(1)}, u32[]{:S(2)}, u32[]{:S(2)}) collective-permute-start(bf16[2,4,64,128]{3,2,1,0:T(8,128)(2,1)S(1)} %join_tok.1.refs_0_), channel_id=1, source_target_pairs={{0,4},{2,6},{4,0},{6,2},{8,12},{10,14},{12,8},{14,10},{16,20},{18,... | collective-permute-start | bytes 393224 | tf_op jit(solution)/shard_map/ppermute | solution.py:533
  23.5 8.2 %copy-start.8 = (bf16[1,128,768]{2,1,0:T(8,128)(2,1)S(1)}, bf16[1,128,768]{2,1,0:T(8,128)(2,1)}, u32[]{:S(2)}) copy-start(bf16[1,128,768]{2,1,0:T(8,128)(2,1)} %param.20) | copy-start | bytes 589828
  23.5 8.2 %copy-start.10 = (bf16[1,128,768]{2,1,0:T(8,128)(2,1)S(1)}, bf16[1,128,768]{2,1,0:T(8,128)(2,1)}, u32[]{:S(2)}) copy-start(bf16[1,128,768]{2,1,0:T(8,128)(2,1)} %param.39) | copy-start | bytes 589828
  23.5 12.1 %copy-start.7 = (bf16[768,768]{1,0:T(8,128)(2,1)S(1)}, bf16[768,768]{1,0:T(8,128)(2,1)}, u32[]{:S(2)}) copy-start(bf16[768,768]{1,0:T(8,128)(2,1)} %refs_7_.1) | copy-start | bytes 3538948
  24.9 6.8 %copy-start.19 = (f32[768]{0:T(1024)S(1)}, f32[768]{0:T(1024)}, u32[]{:S(2)}) copy-start(f32[768]{0:T(1024)} %param.29) | copy-start | bytes 9220
  27.0 8.7 %copy-start.1 = (bf16[768,1536]{1,0:T(8,128)(2,1)S(1)}, bf16[768,1536]{1,0:T(8,128)(2,1)}, u32[]{:S(2)}) copy-start(bf16[768,1536]{1,0:T(8,128)(2,1)} %refs_9_.1) | copy-start | bytes 7077892
  27.0 1.6 %collective-permute-start.6 = (bf16[2,2,4,64,128]{4,3,2,1,0:T(8,128)(2,1)S(1)}, bf16[2,2,4,64,128]{4,3,2,1,0:T(8,128)(2,1)S(1)}, u32[]{:S(2)}, u32[]{:S(2)}) collective-permute-start(bf16[2,2,4,64,128]{4,3,2,1,0:T(8,128)(2,1)S(1)} %join_y.1.refs_4_), channel_id=1, source_target_pairs={{0,2},{2,0},{4,6},{6,4},{8,10},{10,8},{12,14},{14,12},{16,18},{18,... | collective-permute-start | bytes 786440 | tf_op jit(solution)/shard_map/ppermute | solution.py:533
  30.8 4.9 %collective-permute-start.7 = (bf16[128,384]{1,0:T(8,128)(2,1)S(1)}, bf16[128,384]{1,0:T(8,128)(2,1)S(1)}, u32[]{:S(2)}, u32[]{:S(2)}) collective-permute-start(bf16[128,384]{1,0:T(8,128)(2,1)S(1)} %get-tuple-element.81), channel_id=1, source_target_pairs={{0,1},{1,0},{2,3},{3,2},{4,5},{5,4},{6,7},{7,6},{8,9},{9,8},{10,11... | collective-permute-start | bytes 294920 | tf_op jit(solution)/shard_map/ppermute | solution.py:538
  31.8 3.9 %copy-start = (bf16[768,1536]{1,0:T(8,128)(2,1)S(1)}, bf16[768,1536]{1,0:T(8,128)(2,1)}, u32[]{:S(2)}) copy-start(bf16[768,1536]{1,0:T(8,128)(2,1)} %refs_8_.1) | copy-start | bytes 7077892
  40.0 4.7 %collective-permute-start.8 = (bf16[384,128]{1,0:T(8,128)(2,1)S(1)}, bf16[384,128]{1,0:T(8,128)(2,1)S(1)}, u32[]{:S(2)}, u32[]{:S(2)}) collective-permute-start(bf16[384,128]{1,0:T(8,128)(2,1)S(1)} %get-tuple-element.86), channel_id=1, source_target_pairs={{0,1},{1,0},{2,3},{3,2},{4,5},{5,4},{6,7},{7,6},{8,9},{9,8},{10,11... | collective-permute-start | bytes 294920 | tf_op jit(solution)/shard_map/ppermute | solution.py:538
  49.1 11.7 %collective-permute-start.10 = (bf16[264,16,128]{2,1,0:T(8,128)(2,1)S(1)}, bf16[264,16,128]{2,1,0:T(8,128)(2,1)S(1)}, u32[]{:S(2)}, u32[]{:S(2)}) collective-permute-start(bf16[264,16,128]{2,1,0:T(8,128)(2,1)S(1)} %get-tuple-element.95), channel_id=1, source_target_pairs={{0,2},{2,0},{4,6},{6,4},{8,10},{10,8},{12,14},{14,12},{16,18},{18,... | collective-permute-start | bytes 3244040 | tf_op jit(solution)/shard_map/ppermute | solution.py:533
  49.2 8.7 %collective-permute-start.11 = (bf16[64,16,128]{2,1,0:T(8,128)(2,1)S(1)}, bf16[64,16,128]{2,1,0:T(8,128)(2,1)S(1)}, u32[]{:S(2)}, u32[]{:S(2)}) collective-permute-start(bf16[64,16,128]{2,1,0:T(8,128)(2,1)S(1)} %get-tuple-element.98), channel_id=1, source_target_pairs={{0,4},{2,6},{4,0},{6,2},{8,12},{10,14},{12,8},{14,10},{16,20},{18,... | collective-permute-start | bytes 786440 | tf_op jit(solution)/shard_map/ppermute | solution.py:533
  50.8 7.0 %collective-permute-start.12 = (bf16[128,768]{1,0:T(8,128)(2,1)S(1)}, bf16[128,768]{1,0:T(8,128)(2,1)S(1)}, u32[]{:S(2)}, u32[]{:S(2)}) collective-permute-start(bf16[128,768]{1,0:T(8,128)(2,1)S(1)} %get-tuple-element.99.refs_4_), channel_id=1, source_target_pairs={{0,1},{1,0},{2,3},{3,2},{4,5},{5,4},{6,7},{7,6},{8,9},{9,8},{10,11... | collective-permute-start | bytes 589832 | tf_op jit(solution)/shard_map/ppermute | solution.py:538
  59.0 1.8 %collective-permute-start.13 = (bf16[104,16,128]{2,1,0:T(8,128)(2,1)S(1)}, bf16[104,16,128]{2,1,0:T(8,128)(2,1)S(1)}, u32[]{:S(2)}, u32[]{:S(2)}) collective-permute-start(bf16[104,16,128]{2,1,0:T(8,128)(2,1)S(1)} %get-tuple-element.101), channel_id=1, source_target_pairs={{0,2},{2,0},{4,6},{6,4},{8,10},{10,8},{12,14},{14,12},{16,18},{18,... | collective-permute-start | bytes 1277960 | tf_op jit(solution)/shard_map/ppermute | solution.py:533
  60.8 3.4 %copy-start.18 = (f32[768]{0:T(1024)S(1)}, f32[768]{0:T(1024)}, u32[]{:S(2)}) copy-start(f32[768]{0:T(1024)} %refs_5_.1) | copy-start | bytes 9220
  61.7 14.4 %collective-permute-start.14 = (bf16[132,16,128]{2,1,0:T(8,128)(2,1)S(1)}, bf16[132,16,128]{2,1,0:T(8,128)(2,1)S(1)}, u32[]{:S(2)}, u32[]{:S(2)}) collective-permute-start(bf16[132,16,128]{2,1,0:T(8,128)(2,1)S(1)} %get-tuple-element.103), channel_id=1, source_target_pairs={{0,4},{2,6},{4,0},{6,2},{8,12},{10,14},{12,8},{14,10},{16,20},{18,... | collective-permute-start | bytes 1622024 | tf_op jit(solution)/shard_map/ppermute | solution.py:533
  63.3 7.9 %collective-permute-start.15 = (bf16[52,16,128]{2,1,0:T(8,128)(2,1)S(1)}, bf16[52,16,128]{2,1,0:T(8,128)(2,1)S(1)}, u32[]{:S(2)}, u32[]{:S(2)}) collective-permute-start(bf16[52,16,128]{2,1,0:T(8,128)(2,1)S(1)} %get-tuple-element.105), channel_id=1, source_target_pairs={{0,8},{2,10},{4,12},{6,14},{8,0},{10,2},{12,4},{14,6},{16,24},{18,... | collective-permute-start | bytes 638984 | tf_op jit(solution)/shard_map/ppermute | solution.py:533
  63.3 6.7 %collective-permute-start.9 = (bf16[768,128]{1,0:T(8,128)(2,1)S(1)}, bf16[768,128]{1,0:T(8,128)(2,1)S(1)}, u32[]{:S(2)}, u32[]{:S(2)}) collective-permute-start(bf16[768,128]{1,0:T(8,128)(2,1)S(1)} %get-tuple-element.92), channel_id=1, source_target_pairs={{0,1},{1,0},{2,3},{3,2},{4,5},{5,4},{6,7},{7,6},{8,9},{9,8},{10,11... | collective-permute-start | bytes 589832 | tf_op jit(solution)/shard_map/ppermute | solution.py:538
  76.1 18.9 %copy-start.9 = (bf16[16,128,128]{2,1,0:T(8,128)(2,1)S(1)}, bf16[16,128,128]{2,1,0:T(8,128)(2,1)}, u32[]{:S(2)}) copy-start(bf16[16,128,128]{2,1,0:T(8,128)(2,1)} %get-tuple-element.118.refs_1_) | copy-start | bytes 1572868
  76.8 10.0 %collective-permute-start.16 = (bf16[66,16,128]{2,1,0:T(8,128)(2,1)S(1)}, bf16[66,16,128]{2,1,0:T(8,128)(2,1)S(1)}, u32[]{:S(2)}, u32[]{:S(2)}) collective-permute-start(bf16[66,16,128]{2,1,0:T(8,128)(2,1)S(1)} %get-tuple-element.108), channel_id=1, source_target_pairs={{0,8},{2,10},{4,12},{6,14},{8,0},{10,2},{12,4},{14,6},{16,24},{18,... | collective-permute-start | bytes 811016 | tf_op jit(solution)/shard_map/ppermute | solution.py:533
  76.9 7.8 %collective-permute-start.17 = (bf16[26,16,128]{2,1,0:T(8,128)(2,1)S(1)}, bf16[26,16,128]{2,1,0:T(8,128)(2,1)S(1)}, u32[]{:S(2)}, u32[]{:S(2)}) collective-permute-start(bf16[26,16,128]{2,1,0:T(8,128)(2,1)S(1)} %get-tuple-element.110), channel_id=1, source_target_pairs={{0,16},{2,18},{4,20},{6,22},{8,24},{10,26},{12,28},{14,30},{16,0},... | collective-permute-start | bytes 319496 | tf_op jit(solution)/shard_map/ppermute | solution.py:533
  86.9 15.5 %copy-start.3 = (bf16[128,16,128]{2,1,0:T(8,128)(2,1)S(1)}, bf16[128,16,128]{2,1,0:T(8,128)(2,1)}, u32[]{:S(2)}) copy-start(bf16[128,16,128]{2,1,0:T(8,128)(2,1)} %param.22) | copy-start | bytes 1572868
  86.9 15.5 %copy-start.15 = (bf16[128,8]{0,1:T(8,128)(2,1)S(1)}, bf16[128,8]{0,1:T(8,128)(2,1)}, u32[]{:S(2)}) copy-start(bf16[128,8]{0,1:T(8,128)(2,1)} %param.34) | copy-start | bytes 6148
  86.9 15.5 %copy-start.16 = (f32[128]{0:T(128)S(1)}, f32[128]{0:T(128)}, u32[]{:S(2)}) copy-start(f32[128]{0:T(128)} %param.28) | copy-start | bytes 1540
  87.5 6.9 %collective-permute-start.18 = (bf16[33,16,128]{2,1,0:T(8,128)(2,1)S(1)}, bf16[33,16,128]{2,1,0:T(8,128)(2,1)S(1)}, u32[]{:S(2)}, u32[]{:S(2)}) collective-permute-start(bf16[33,16,128]{2,1,0:T(8,128)(2,1)S(1)} %get-tuple-element.112), channel_id=1, source_target_pairs={{0,1},{1,0},{2,3},{3,2},{4,5},{5,4},{6,7},{7,6},{8,9},{9,8},{10,11... | collective-permute-start | bytes 405512 | tf_op jit(solution)/shard_map/ppermute | solution.py:538
  88.5 5.9 %collective-permute-start.19 = (bf16[9,16,128]{2,1,0:T(8,128)(2,1)S(1)}, bf16[9,16,128]{2,1,0:T(8,128)(2,1)S(1)}, u32[]{:S(2)}, u32[]{:S(2)}) collective-permute-start(bf16[9,16,128]{2,1,0:T(8,128)(2,1)S(1)} %get-tuple-element.113), channel_id=1, source_target_pairs={{0,4},{2,6},{4,0},{6,2},{8,12},{10,14},{12,8},{14,10},{16,20},{18,... | collective-permute-start | bytes 110600 | tf_op jit(solution)/shard_map/ppermute | solution.py:533
  90.6 3.8 %collective-permute-start.20 = (bf16[64,128]{1,0:T(8,128)(2,1)S(1)}, bf16[64,128]{1,0:T(8,128)(2,1)S(1)}, u32[]{:S(2)}, u32[]{:S(2)}) collective-permute-start(bf16[64,128]{1,0:T(8,128)(2,1)S(1)} %get-tuple-element.114), channel_id=1, source_target_pairs={{0,1},{1,0},{2,3},{3,2},{4,5},{5,4},{6,7},{7,6},{8,9},{9,8},{10,11... | collective-permute-start | bytes 49160 | tf_op jit(solution)/shard_map/ppermute | solution.py:538
  96.5 15.0 %all-to-all-start = ((f32[32,8,128]{2,1,0:T(8,128)}), f32[32,8,128]{2,1,0:T(8,128)S(1)}, u32[]{:S(2)}, u32[]{:S(2)}) async-start(f32[32,8,128]{2,1,0:T(8,128)} %pair_weight.1), calls=%async_computation | async-start | bytes 262144 | tf_op jit(solution)/shard_map/all_to_all | solution.py:542
  99.8 11.7 %collective-permute-start.21 = (bf16[30,16,128]{2,1,0:T(8,128)(2,1)S(1)}, bf16[30,16,128]{2,1,0:T(8,128)(2,1)S(1)}, u32[]{:S(2)}, u32[]{:S(2)}) collective-permute-start(bf16[30,16,128]{2,1,0:T(8,128)(2,1)S(1)} %get-tuple-element.116), channel_id=1, source_target_pairs={{0,16},{2,18},{4,20},{6,22},{8,24},{10,26},{12,28},{14,30},{16,0},... | collective-permute-start | bytes 368648 | tf_op jit(solution)/shard_map/ppermute | solution.py:533

commit v13 on v12

--- a/solution.py
+++ b/solution.py
@@ -338,23 +338,19 @@
 
 
 def first_kernel(copies, toks, ids, slices, x, d_query, d_key, d_value, *rest):
-    kept, sent, d_own = rest[:3]
-    d_others, (wide, d_inputs, total_ref) = rest[3 : 2 + toks], rest[2 + toks :]
+    kept, sent, d_own, single_all = rest[:4]
+    d_others, (wide, d_inputs) = rest[4 : 3 + toks], rest[3 + toks :]
     t, core = ids[0], low_bits(ids[1], 2)
     rows = d_own.shape[1]
     cut = x.shape[1] // copies
     count = tile_count(cut, d_query.shape[0])
-    stride = 3 * count + tile_count(cut, rows * toks)
+    stride = 3 * count
     for k, part in enumerate((d_query, d_key, d_value)):
         wide[...] = mm(part[...], x[...])
         cut_wide(copies, toks, core, k * count, stride, wide, kept, sent)
     total = mm(slices[0], d_query[...]) + mm(slices[1], d_key[...])
     total = total + mm(slices[2], d_value[...])
-    total_ref[...] = total
-    for side, out in ((core, kept), (1 - core, sent)):
-        for q in range(copies // 2):
-            start = pl.multiple_of((2 * q + side) * cut, 8)
-            put(out, q * stride + 3 * count, total_ref[pl.ds(start, cut), :].astype(bf16))
+    single_all[...] = total
     for a in range(toks):
         d_inputs[a] = total[:, a * rows : (a + 1) * rows]
     d_own[...] = d_inputs[t]
@@ -362,7 +358,7 @@
         d_others[r - 1][...] = d_inputs[jnp.bitwise_xor(t, r)].astype(bf16)
 
 
-def second_kernel(copies, toks, ids, att, bias_kept, bias_got, *rest):
+def second_kernel(copies, toks, ids, att, single_all, bias_kept, bias_got, *rest):
     d_res_parts, (kept, sent, d_res, narrow) = rest[:toks], rest[toks:]
     t, core = ids[0], low_bits(ids[1], 2)
     rows = d_res_parts[0].shape[0]
@@ -372,12 +368,14 @@
         start = pl.multiple_of(jnp.bitwise_xor(t, r) * rows, rows)
         d_res[pl.ds(start, rows), :] = d_res_parts[r][...]
     narrow[...] = mm(d_res[...], att[...], TN)
-    base = copies // 2 * count
+    stride = count + tile_count(cut, rows * toks)
+    base = copies // 2 * stride
     bias_count = bias_kept.shape[0] // (copies // 2)
     for side, out in ((core, kept), (1 - core, sent)):
         for q in range(copies // 2):
             first = pl.multiple_of((2 * q + side) * cut, 8)
-            put(out, q * count, narrow[pl.ds(first, cut), :].astype(bf16))
+            put(out, q * stride, narrow[pl.ds(first, cut), :].astype(bf16))
+            put(out, q * stride + count, single_all[pl.ds(first, cut), :].astype(bf16))
         for z in range(copies // 4):
             span = pl.ds((2 * z + side) * bias_count, bias_count)
             out[base + z * bias_count : base + (z + 1) * bias_count] = (
@@ -415,39 +413,42 @@
         pieces[r][...] = blocks[jnp.bitwise_xor(ids[0], r)]
 
 
-def across_kernel(wide, lines, segment, ids, kept, got, kept_b, got_b, *outs):
+def across_kernel(segment, ids, kept, got, kept_b, got_b, *outs):
     t = ids[0]
     stride = kept.shape[0] // 2
     step_kernel([(0, 0) + segment], ids, kept_b, got_b, *outs[2:])
     for side, out in ((t, outs[0]), (1 - t, outs[1])):
-        span = pl.ds(side * stride, wide)
-        out[:wide] = (kept[span].astype(f32) + got[span].astype(f32)).astype(bf16)
-        for a in range(2):
-            for i in range(lines):
-                k = a * stride + wide + 2 * i + side
-                out[wide + a * lines + i] = (
-                    kept[k].astype(f32) + got[k].astype(f32)
-                ).astype(bf16)
-
-
-def far_kernel(wide, lines, half, ids, kept, got, kept_out, sent_out, groups):
+        span = pl.ds(side * stride, stride)
+        out[...] = (kept[span].astype(f32) + got[span].astype(f32)).astype(bf16)
+
+
+def far_kernel(half, ids, kept, got, kept_b, got_b, kept_out, sent_out, single, other, *scratch):
+    groups, blocks = scratch
     t, a = ids[0], ids[1] // half
-    groups[t] = kept[:wide]
-    groups[1 - t] = got[:wide]
-    for side, out in ((a, kept_out), (1 - a, sent_out)):
-        out[:wide] = groups[side]
-        span = pl.ds(wide + side * lines, lines)
-        out[wide:] = (kept[span].astype(f32) + got[span].astype(f32)).astype(bf16)
-
-
-def close_kernel(kept, got, kept_b, got_b, terms, *outs):
+    groups[t] = kept[...]
+    groups[1 - t] = got[...]
+    kept_out[...] = groups[a]
+    sent_out[...] = groups[1 - a]
+    lines = single.shape[0]
+    base = kept_b.shape[0] - 2 * lines
+    for i in range(lines):
+        for j in range(2):
+            k = base + 2 * i + j
+            blocks[j, i] = (kept_b[k].astype(f32) + got_b[k].astype(f32)).astype(bf16)
+    single[...] = blocks[t]
+    other[...] = blocks[1 - t]
+
+
+def close_kernel(kept, got, kept_b, got_b, single, got_single, terms, *outs):
     total = kept[...].astype(f32) + got[...].astype(f32)
     cut, own_width = outs[0].shape
     count = tile_count(cut, own_width)
     for k in range(3):
         outs[k][...] = take(total, k * count, cut, own_width)
-    outs[3][...] = take(kept_b[...].astype(f32) + got_b[...].astype(f32), 0, cut, own_width)
-    outs[4][...] = take(total, 3 * count, cut, outs[4].shape[1])
+    total = kept_b[:count].astype(f32) + got_b[:count].astype(f32)
+    outs[3][...] = take(total, 0, cut, own_width)
+    total = single[...].astype(f32) + got_single[...].astype(f32)
+    outs[4][...] = take(total, 0, cut, outs[4].shape[1])
     outs[5][...] = jnp.sum(terms[...], axis=0)
 
 
@@ -461,7 +462,7 @@
         moved[k] = take(first, k * count, cut, own_width).astype(bf16)
     final[...] = take(second, 0, cut, own_width)
     rows = blocks.shape[2]
-    single = take(first, 3 * count, cut, rows * toks)
+    single = take(second, count, cut, rows * toks)
     for a in range(toks):
         blocks[a] = single[:, a * rows : (a + 1) * rows]
     for r in range(toks):
@@ -506,10 +507,13 @@
     sums = jnp.zeros((grad_b.shape[0], channels), f32)
     for j in range(cols):
         sums = sums + jnp.where(row_col == j, mm(grad_b, columns[j]), 0.0)
-    for h in range(weight_grad.shape[1]):
-        line = jnp.sum(sums[h * cols : (h + 1) * cols, :], axis=0, keepdims=True)
-        for n in range(weight_grad.shape[0]):
-            weight_grad[n, h : h + 1, :] = line
+    heads = weight_grad.shape[1]
+    lines = [
+        jnp.sum(sums[h * cols : (h + 1) * cols, :], axis=0, keepdims=True) for h in range(heads)
+    ]
+    whole = jnp.concatenate(lines, axis=0)
+    for n in range(weight_grad.shape[0]):
+        weight_grad[n] = whole
 
 
 def pair_kernel(toks, cols, ids, pair, gain, w_pair, *rest):
@@ -692,24 +696,20 @@
 
     wide_tiles = tile_count(cut, own_width)
     single_tiles = tile_count(cut, tokens)
-    first_tiles, second_tiles = 3 * wide_tiles + single_tiles, wide_tiles
+    first_tiles, second_tiles = 3 * wide_tiles, wide_tiles + single_tiles
     found = call(
         functools.partial(first_kernel, copies, toks),
         "first",
         [where_am_i, slices, x, d_query, d_key, d_value],
         [((copies // 2 * first_tiles, 16, 128), bf16)] * 2
-        + [((width, rows), f32)]
+        + [((width, rows), f32), ((width, tokens), f32)]
         + [((width, rows), bf16)] * (toks - 1),
-        [
-            VMEM((own_width, width), f32),
-            VMEM((toks, width, rows), f32),
-            VMEM((width, tokens), f32),
-        ],
+        [VMEM((own_width, width), f32), VMEM((toks, width, rows), f32)],
         flops=12 * tokens * width * own_width,
     )
-    kept, sent, d_own = found[:3]
+    kept, sent, d_own, single_all = found[:4]
     got = swap_copy(sent, 1)
-    d_others = [swap_tok(found[2 + r], r) for r in range(1, toks)]
+    d_others = [swap_tok(found[3 + r], r) for r in range(1, toks)]
 
     def step(name, pairs, segments, deps=()):
         filled, full, masks_of = {}, [], {}
@@ -739,10 +739,10 @@
     kept_b, sent_b = call(
         functools.partial(second_kernel, copies, toks),
         "second",
-        [where_am_i, att, bias_kept, bias_got] + d_res_parts,
+        [where_am_i, att, single_all, bias_kept, bias_got] + d_res_parts,
         [((copies // 2 * second_tiles + copies // 4 * bias_tiles, 16, 128), bf16)] * 2,
         [VMEM((tokens, width), bf16), VMEM((width, own_width), f32)],
-        flops=2 * tokens * width * own_width,
+        flops=20 * tokens * width * own_width,
     )
     got_b = swap_copy(sent_b, 1)
 
@@ -769,14 +769,11 @@
         pairs = step("step_%d" % n, pairs, segments, deps=[exited] if n == 1 else ())
         parts //= 2
     if toks == 2:
-        wide, lines = 3 * wide_tiles, single_tiles // 2
         kept, sent, kept_b, sent_b = call(
-            functools.partial(
-                across_kernel, wide, lines, (2, second_tiles, masks_b[-1], 1, 0, 0)
-            ),
+            functools.partial(across_kernel, (2, second_tiles, masks_b[-1], 1, 0, 0)),
             "across",
             [where_am_i] + [array for one in pairs for array in one],
-            [((wide + 2 * lines, 16, 128), bf16)] * 2 + [((second_tiles, 16, 128), bf16)] * 2,
+            [((first_tiles, 16, 128), bf16)] * 2 + [((second_tiles, 16, 128), bf16)] * 2,
         )
         pairs = [(kept, swap_tok(sent, 1)), (kept_b, swap_copy(sent_b, masks_b[-1]))]
     bias_pieces = call(
@@ -790,16 +787,18 @@
     bias_pieces = [bias_pieces[0]] + [swap_tok(bias_pieces[r], r) for r in range(1, toks)]
     ready = [pairs[0][1], pairs[1][1]]
     if toks == 2:
-        kept, sent = call(
-            functools.partial(far_kernel, wide, lines, copies // 2),
+        lines = single_tiles // 2
+        kept, sent, single_kept, single_sent = call(
+            functools.partial(far_kernel, copies // 2),
             "far",
-            [where_am_i, *pairs[0]],
-            [((wide + lines, 16, 128), bf16)] * 2,
-            [VMEM((2, wide, 16, 128), bf16)],
-            deps=[pairs[1][1]] + bias_pieces[1:],
+            [where_am_i, *pairs[0], *pairs[1]],
+            [((first_tiles, 16, 128), bf16)] * 2 + [((lines, 16, 128), bf16)] * 2,
+            [VMEM((2, first_tiles, 16, 128), bf16), VMEM((2, lines, 16, 128), bf16)],
+            deps=bias_pieces[1:],
         )
         pairs[0] = (kept, swap_copy(sent, copies // 2))
-        ready = [kept]
+        single_pair = (single_kept, swap_tok(single_sent, 1))
+        ready = []
 
     group = copies // toks
     swaps = []
@@ -829,7 +828,7 @@
         grad_query, grad_key, grad_value, grad_out, grad_single, weight_grad = call(
             close_kernel,
             "close",
-            [*pairs[0], *pairs[1], weight_terms],
+            [*pairs[0], *pairs[1], *single_pair, weight_terms],
             [((cut, own_width), f32)] * 4 + [((cut, rows), f32), ((heads, channels), f32)],
         )
     else:

time: 114 us -> 108 us (0.947)
  waiting for transfers between devices: 52.7 us -> 49.2 us
  starting transfers between devices: 25.5 us -> 22.6 us
    ppermute x14, waiting for transfers between devices: 31.6 us -> 28.5 us  [swap_copy(): return lax.ppermute(value, 'copy', [(i, i ^ mask) for i in range(size)])]
    ppermute x8 -> x9, starting transfers between devices: 7.48 us -> 5.86 us  [swap_tok(): return lax.ppermute(value, 'tok', [(i, i ^ mask) for i in range(size)])]
    unnamed x40 -> x42, local copies, waits for them, and re-layouts: 3.38 us -> 4.04 us
    ppermute x8 -> x9, waiting for transfers between devices: 21.2 us -> 20.8 us  [swap_tok(): return lax.ppermute(value, 'tok', [(i, i ^ mask) for i in range(size)])]
  transfers between devices with their start and end apart: 23 -> 24, of which waited for: 15 -> 17; matrix products, arithmetic and copies ran while one was open for 0% -> 0% of each run, Pallas kernels for 8% -> 10%
where the time goes in v13:
time: 108 us; the launch traced here: 106 us
  waiting for transfers between devices  49.2 us (46%)
  Pallas kernels  28.9 us (27%)
  starting transfers between devices  22.6 us (21%)
  local copies, waits for them, and re-layouts  4.05 us (4%)
    pallas_call x21, Pallas kernels, call(): pl.pallas_call(whole, name=name, out_shape=[jax.ShapeDtypeStruct(one[0],...  28.9 us
    ppermute x14, waiting for transfers between devices, swap_copy(): return lax.ppermute(value, 'copy', [(i, i ^ mask) for i in range(size)])  28.5 us
    ppermute x9, waiting for transfers between devices, swap_tok(): return lax.ppermute(value, 'tok', [(i, i ^ mask) for i in range(size)])  20.8 us
    ppermute x14, starting transfers between devices, swap_copy(): return lax.ppermute(value, 'copy', [(i, i ^ mask) for i in range(size)])  13.8 us
    ppermute x9, starting transfers between devices, swap_tok(): return lax.ppermute(value, 'tok', [(i, i ^ mask) for i in range(size)])  5.86 us
    unnamed x42, local copies, waits for them, and re-layouts  4.04 us
    all_to_all x1, starting transfers between devices, exchange(): return lax.all_to_all(value, ('copy', 'tok'), 0, 0)  2.89 us
  transfers between devices with their start and end apart: 24, of which 17 were waited for; matrix products, arithmetic and copies ran while one was open for 0% of the time, Pallas kernels for 10%

profile of v13, /device:TPU:2, one launch (start us, length us, event | category | flops | bytes accessed | tf_op | source)
XLA Modules:
  0.0 106.3 jit_solution(17331054625008861417)
XLA Ops:
  0.6 0.6 pad_add_fusion.refs_0_
  1.2 4.2 %enter.1 = (bf16[128,768]{1,0:T(8,128)(2,1)}, bf16[16,128,128]{2,1,0:T(8,128)(2,1)}, f32[256,128]{1,0:T(8,128)}, f32[1,256]{1,0:T(1,128)}, bf16[2,64,128]{2,1,0:T(8,128)(2,1)}) custom-call(s32[2]{0:T(128)} %pad_add_fusion.refs_0_, bf16[128,768]{1,0:T(8,128)(2,1)} %bitcast.20, bf16[128,768]{1,0:T(8,128)(2,1)} %refs_2_.2, s32[1,128]{1,0:T(1,128)} %bitcast.30, ...), custom_call_target="tpu_custom_call" | custom-call | flops 67108864 | bytes 1860808 | tf_op jit(solution)/shard_map/enter/pallas_call | solution.py:79
  5.4 0.1 collective-permute-start.3
  5.5 2.1 %collective-permute-start = (bf16[2,64,128]{2,1,0:T(8,128)(2,1)}, bf16[2,64,128]{2,1,0:T(8,128)(2,1)S(1)}, u32[]{:S(2)}, u32[]{:S(2)}) collective-permute-start(bf16[2,64,128]{2,1,0:T(8,128)(2,1)} %get-tuple-element.74.refs_0_), channel_id=1, source_target_pairs={{0,8},{2,10},{4,12},{6,14},{8,0},{10,2},{12,4},{14,6},{16,24},{18,... | collective-permute-start | bytes 98312 | tf_op jit(solution)/shard_map/ppermute | solution.py:537
  7.6 2.6 %collective-permute-start.1 = (bf16[2,64,128]{2,1,0:T(8,128)(2,1)}, bf16[2,64,128]{2,1,0:T(8,128)(2,1)S(1)}, u32[]{:S(2)}, u32[]{:S(2)}) collective-permute-start(bf16[2,64,128]{2,1,0:T(8,128)(2,1)} %get-tuple-element.74.refs_0_), channel_id=1, source_target_pairs={{0,16},{2,18},{4,20},{6,22},{8,24},{10,26},{12,28},{14,30},{16,0},... | collective-permute-start | bytes 98312 | tf_op jit(solution)/shard_map/ppermute | solution.py:537
  10.2 2.7 %collective-permute-done.1.refs_2_ = bf16[2,64,128]{2,1,0:T(8,128)(2,1)S(1)} collective-permute-done((bf16[2,64,128]{2,1,0:T(8,128)(2,1)}, bf16[2,64,128]{2,1,0:T(8,128)(2,1)S(1)}, u32[]{:S(2)}, u32[]{:S(2)}) %collective-permute-start.1) | collective-permute-done | bytes 32800 | tf_op jit(solution)/shard_map/ppermute | solution.py:537
  12.9 3.2 %collective-permute-done.2.refs_3_ = bf16[2,64,128]{2,1,0:T(8,128)(2,1)S(1)} collective-permute-done((bf16[2,64,128]{2,1,0:T(8,128)(2,1)}, bf16[2,64,128]{2,1,0:T(8,128)(2,1)S(1)}, u32[]{:S(2)}, u32[]{:S(2)}) %collective-permute-start.2) | collective-permute-done | bytes 32800 | tf_op jit(solution)/shard_map/ppermute | solution.py:537
  16.1 0.8 copy-done.15
  16.9 1.6 %collective-permute-start.4 = (bf16[4,64,128]{2,1,0:T(8,128)(2,1)S(1)}, bf16[4,64,128]{2,1,0:T(8,128)(2,1)S(1)}, u32[]{:S(2)}, u32[]{:S(2)}) collective-permute-start(bf16[4,64,128]{2,1,0:T(8,128)(2,1)S(1)} %get-tuple-element.80), channel_id=1, source_target_pairs={{0,1},{1,0},{2,3},{3,2},{4,5},{5,4},{6,7},{7,6},{8,9},{9,8},{10,11... | collective-permute-start | bytes 196616 | tf_op jit(solution)/shard_map/ppermute | solution.py:542
  18.4 1.3 %copy-done.5 = bf16[768,768]{1,0:T(8,128)(2,1)S(1)} copy-done((bf16[768,768]{1,0:T(8,128)(2,1)S(1)}, bf16[768,768]{1,0:T(8,128)(2,1)}, u32[]{:S(2)}) %copy-start.5) | copy-done | bytes 1179672
  19.7 1.3 %copy-done.6 = bf16[768,768]{1,0:T(8,128)(2,1)S(1)} copy-done((bf16[768,768]{1,0:T(8,128)(2,1)S(1)}, bf16[768,768]{1,0:T(8,128)(2,1)}, u32[]{:S(2)}) %copy-start.6) | copy-done | bytes 1179672
  21.0 0.7 copy-done.13
  21.6 0.8 stage.1.refs_1_.refs_2_
  22.4 0.0 copy-start.2
  22.4 0.0 copy-start.14
  22.5 1.6 %collective-permute-start.5 = (bf16[2,4,64,128]{3,2,1,0:T(8,128)(2,1)S(1)}, bf16[2,4,64,128]{3,2,1,0:T(8,128)(2,1)S(1)}, u32[]{:S(2)}, u32[]{:S(2)}) collective-permute-start(bf16[2,4,64,128]{3,2,1,0:T(8,128)(2,1)S(1)} %join_tok.1.refs_0_), channel_id=1, source_target_pairs={{0,4},{2,6},{4,0},{6,2},{8,12},{10,14},{12,8},{14,10},{16,20},{18,... | collective-permute-start | bytes 393224 | tf_op jit(solution)/shard_map/ppermute | solution.py:537
  24.1 1.4 %project.1 = (bf16[256,768]{1,0:T(8,128)(2,1)S(1)}, bf16[384,256]{1,0:T(8,128)(2,1)S(1)}, bf16[384,256]{1,0:T(8,128)(2,1)S(1)}, bf16[384,256]{1,0:T(8,128)(2,1)S(1)}) custom-call(s32[2]{0:T(128)S(1)} %copy-done.13, bf16[3,768,384]{2,1,0:T(8,128)(2,1)S(1)} %stage.1.refs_1_.refs_2_, bf16[128,768]{1,0:T(8,128)(2,1)S(1)} %copy-done.11, ...), custom_call_target="tpu_custom_call" | custom-call | flops 452984832 | bytes 3145736 | tf_op jit(solution)/shard_map/project/pallas_call | solution.py:79
  25.5 2.0 %collective-permute-done.5.refs_1_ = bf16[2,4,64,128]{3,2,1,0:T(8,128)(2,1)S(1)} collective-permute-done((bf16[2,4,64,128]{3,2,1,0:T(8,128)(2,1)S(1)}, bf16[2,4,64,128]{3,2,1,0:T(8,128)(2,1)S(1)}, u32[]{:S(2)}, u32[]{:S(2)}) %collective-permute-start.5) | collective-permute-done | bytes 131104 | tf_op jit(solution)/shard_map/ppermute | solution.py:537
  27.6 0.1 collective-permute-start.6
  27.6 1.5 %collective-permute-done.6.refs_5_ = bf16[2,2,4,64,128]{4,3,2,1,0:T(8,128)(2,1)S(1)} collective-permute-done((bf16[2,2,4,64,128]{4,3,2,1,0:T(8,128)(2,1)S(1)}, bf16[2,2,4,64,128]{4,3,2,1,0:T(8,128)(2,1)S(1)}, u32[]{:S(2)}, u32[]{:S(2)}) %collective-permute-start.6) | collective-permute-done | bytes 262176 | tf_op jit(solution)/shard_map/ppermute | solution.py:537
  29.2 2.1 %attention.1 = (bf16[4,256,256]{2,1,0:T(8,128)(2,1)S(1)}, bf16[256,384]{1,0:T(8,128)(2,1)S(1)}, bf16[128,384]{1,0:T(8,128)(2,1)S(1)}, bf16[128,384]{1,0:T(8,128)(2,1)S(1)}) custom-call(s32[2]{0:T(128)S(1)} %copy-done.14, bf16[384,256]{1,0:T(8,128)(2,1)S(1)} %get-tuple-element.77.refs_1_, bf16[384,256]{1,0:T(8,128)(2,1)S(1)} %get-tuple-element.78.refs_2_, ...), custom_call_target="tpu_custom_call" | custom-call | flops 100663296 | bytes 2163720 | tf_op jit(solution)/shard_map/attention/pallas_call | solution.py:79
  31.3 0.6 collective-permute-start.7
  32.0 0.9 down.1
  32.9 3.4 %collective-permute-done.7.refs_6_ = bf16[128,384]{1,0:T(8,128)(2,1)S(1)} collective-permute-done((bf16[128,384]{1,0:T(8,128)(2,1)S(1)}, bf16[128,384]{1,0:T(8,128)(2,1)S(1)}, u32[]{:S(2)}, u32[]{:S(2)}) %collective-permute-start.7) | collective-permute-done | bytes 98336 | tf_op jit(solution)/shard_map/ppermute | solution.py:542
  36.2 4.3 %hidden.1 = (f32[128,768]{1,0:T(8,128)S(1)}, bf16[128,768]{1,0:T(8,128)(2,1)S(1)}, bf16[384,128]{1,0:T(8,128)(2,1)S(1)}, bf16[384,128]{1,0:T(8,128)(2,1)S(1)}) custom-call(s32[2]{0:T(128)S(1)} %copy-done.14, bf16[128,768]{1,0:T(8,128)(2,1)S(1)} %get-tuple-element.70.refs_1_.refs_0_, bf16[128,768]{1,0:T(8,128)(2,1)S(1)} %get-tuple-element.71.refs_2_, ...), custom_call_target="tpu_custom_call" | custom-call | flops 1509949440 | bytes 8064008 | tf_op jit(solution)/shard_map/hidden/pallas_call | solution.py:79
  40.6 0.6 collective-permute-start.8
  41.2 4.1 %collective-permute-done.8.refs_6_ = bf16[384,128]{1,0:T(8,128)(2,1)S(1)} collective-permute-done((bf16[384,128]{1,0:T(8,128)(2,1)S(1)}, bf16[384,128]{1,0:T(8,128)(2,1)S(1)}, u32[]{:S(2)}, u32[]{:S(2)}) %collective-permute-start.8) | collective-permute-done | bytes 98336 | tf_op jit(solution)/shard_map/ppermute | solution.py:542
  45.3 2.0 %backward.1 = (bf16[384,256]{1,0:T(8,128)(2,1)S(1)}, bf16[384,256]{1,0:T(8,128)(2,1)S(1)}, bf16[384,256]{1,0:T(8,128)(2,1)S(1)}, bf16[64,16,128]{2,1,0:T(8,128)(...) custom-call(s32[2]{0:T(128)S(1)} %copy-done.14, ...), custom_call_target="tpu_custom_call" | custom-call | flops 201326592 | bytes 2818056 | tf_op jit(solution)/shard_map/backward/pallas_call | solution.py:79
  47.3 1.6 %collective-permute-start.11 = (bf16[64,16,128]{2,1,0:T(8,128)(2,1)S(1)}, bf16[64,16,128]{2,1,0:T(8,128)(2,1)S(1)}, u32[]{:S(2)}, u32[]{:S(2)}) collective-permute-start(bf16[64,16,128]{2,1,0:T(8,128)(2,1)S(1)} %get-tuple-element.102), channel_id=1, source_target_pairs={{0,4},{2,6},{4,0},{6,2},{8,12},{10,14},{12,8},{14,10},{16,20},{18,... | collective-permute-start | bytes 786440 | tf_op jit(solution)/shard_map/ppermute | solution.py:537
  48.9 0.5 collective-permute-start.12
  49.4 2.3 %first.1 = (bf16[216,16,128]{2,1,0:T(8,128)(2,1)S(1)}, bf16[216,16,128]{2,1,0:T(8,128)(2,1)S(1)}, f32[768,128]{1,0:T(8,128)S(1)}, f32[768,256]{1,0:T(8,128)S(1)}, bf16[768,128]{1,0:T(8,128)(2,1)S(1)}) custom-call(s32[2]{0:T(128)S(1)} %copy-done.14, bf16[3,768,384]{2,1,0:T(8,128)(2,1)S(1)} %stage.1.refs_1_.refs_2_, ...), custom_call_target="tpu_custom_call" | custom-call | flops 905969664 | bytes 5898248 | tf_op jit(solution)/shard_map/first/pallas_call | solution.py:79
  51.7 0.1 collective-permute-start.10
  51.8 2.8 %collective-permute-done.12.refs_6_ = bf16[128,768]{1,0:T(8,128)(2,1)S(1)} collective-permute-done((bf16[128,768]{1,0:T(8,128)(2,1)S(1)}, bf16[128,768]{1,0:T(8,128)(2,1)S(1)}, u32[]{:S(2)}, u32[]{:S(2)}) %collective-permute-start.12) | collective-permute-done | bytes 196640 | tf_op jit(solution)/shard_map/ppermute | solution.py:542
  54.6 1.1 %second.1 = (bf16[152,16,128]{2,1,0:T(8,128)(2,1)S(1)}, bf16[152,16,128]{2,1,0:T(8,128)(2,1)S(1)}) custom-call(s32[2]{0:T(128)S(1)} %copy-done.14, bf16[256,384]{1,0:T(8,128)(2,1)S(1)} %get-tuple-element.99.refs_1_, f32[768,256]{1,0:T(8,128)S(1)} %get-tuple-element.100.refs_2_, bf16[64,16,128]{2,1,0:T(8,128)(2,1)S(1)} %get-tuple-element.101.refs_3_, ...), custom_call_target="tpu_custom_call" | custom-call | flops 1509949440 | bytes 3145736 | tf_op jit(solution)/shard_map/second/pallas_call | solution.py:79
  55.7 0.1 collective-permute-start.13
  55.7 2.0 %collective-permute-done.13.refs_4_ = bf16[152,16,128]{2,1,0:T(8,128)(2,1)S(1)} collective-permute-done((bf16[152,16,128]{2,1,0:T(8,128)(2,1)S(1)}, bf16[152,16,128]{2,1,0:T(8,128)(2,1)S(1)}, u32[]{:S(2)}, u32[]{:S(2)}) %collective-permute-start.13) | collective-permute-done | bytes 622624 | tf_op jit(solution)/shard_map/ppermute | solution.py:537
  57.8 0.9 step_0.1
  58.7 0.8 collective-permute-start.14
  59.5 0.5 collective-permute-start.9
  60.0 6.1 %collective-permute-done.9.refs_4_ = bf16[768,128]{1,0:T(8,128)(2,1)S(1)} collective-permute-done((bf16[768,128]{1,0:T(8,128)(2,1)S(1)}, bf16[768,128]{1,0:T(8,128)(2,1)S(1)}, u32[]{:S(2)}, u32[]{:S(2)}) %collective-permute-start.9) | collective-permute-done | bytes 196640 | tf_op jit(solution)/shard_map/ppermute | solution.py:542
  66.1 1.2 %exit.1 = (bf16[128,768]{1,0:T(8,128)(2,1)}, f32[8,128]{1,0:T(8,128)S(1)}) custom-call(bf16[128,768]{1,0:T(8,128)(2,1)S(1)} %get-tuple-element.70.refs_1_.refs_0_, f32[1,768]{1,0:T(1,128)S(1)} %reshape.49.refs_1_, f32[128,768]{1,0:T(8,128)S(1)} %get-tuple-element.85.refs_2_, f32[768,128]{1,0:T(8,128)S(1)} %get-tuple-element.94.refs_3_, ...), custom_call_target="tpu_custom_call" | custom-call | bytes 1383424 | tf_op jit(solution)/shard_map/exit/pallas_call | solution.py:79
  67.3 1.3 %collective-permute-done.15.refs_4_ = bf16[76,16,128]{2,1,0:T(8,128)(2,1)S(1)} collective-permute-done((bf16[76,16,128]{2,1,0:T(8,128)(2,1)S(1)}, bf16[76,16,128]{2,1,0:T(8,128)(2,1)S(1)}, u32[]{:S(2)}, u32[]{:S(2)}) %collective-permute-start.15) | collective-permute-done | bytes 311328 | tf_op jit(solution)/shard_map/ppermute | solution.py:537
  68.6 2.4 %collective-permute-done.14.refs_2_ = bf16[108,16,128]{2,1,0:T(8,128)(2,1)S(1)} collective-permute-done((bf16[108,16,128]{2,1,0:T(8,128)(2,1)S(1)}, bf16[108,16,128]{2,1,0:T(8,128)(2,1)S(1)}, u32[]{:S(2)}, u32[]{:S(2)}) %collective-permute-start.14) | collective-permute-done | bytes 442400 | tf_op jit(solution)/shard_map/ppermute | solution.py:537
  71.0 0.7 step_1.1
  71.7 0.1 collective-permute-start.16
  71.8 0.9 collective-permute-start.17
  72.7 8.8 %collective-permute-done.17.refs_4_.refs_2_ = bf16[38,16,128]{2,1,0:T(8,128)(2,1)S(1)} collective-permute-done((bf16[38,16,128]{2,1,0:T(8,128)(2,1)S(1)}, bf16[38,16,128]{2,1,0:T(8,128)(2,1)S(1)}, u32[]{:S(2)}, u32[]{:S(2)}) %collective-permute-start.17) | collective-permute-done | bytes 155680 | tf_op jit(solution)/shard_map/ppermute | solution.py:537
  81.5 0.3 collective-permute-done.16.refs_2_
  81.8 0.6 across.1
  82.4 0.6 last_bias.1
  83.0 0.6 collective-permute-start.20
  83.6 3.2 %collective-permute-done.20.refs_5_.refs_3_ = bf16[64,128]{1,0:T(8,128)(2,1)S(1)} collective-permute-done((bf16[64,128]{1,0:T(8,128)(2,1)S(1)}, bf16[64,128]{1,0:T(8,128)(2,1)S(1)}, u32[]{:S(2)}, u32[]{:S(2)}) %collective-permute-start.20) | collective-permute-done | bytes 16416 | tf_op jit(solution)/shard_map/ppermute | solution.py:542
  86.8 1.5 %pair_weight.1 = f32[32,8,128]{2,1,0:T(8,128)} custom-call(s32[2]{0:T(128)S(1)} %copy-done.14, bf16[16,128,128]{2,1,0:T(8,128)(2,1)S(1)} %copy-done.9, bf16[64,128]{1,0:T(8,128)(2,1)S(1)} %get-tuple-element.125.refs_2_.refs_4_, bf16[64,128]{1,0:T(8,128)(2,1)S(1)} %collective-permute-done.20.refs_5_.refs_3_), custom_call_target="tpu_custom_call" | custom-call | flops 67108864 | bytes 688136 | tf_op jit(solution)/shard_map/pair_weight/pallas_call | solution.py:79
  88.3 2.9 %all-to-all-start = ((f32[32,8,128]{2,1,0:T(8,128)}), f32[32,8,128]{2,1,0:T(8,128)S(1)}, u32[]{:S(2)}, u32[]{:S(2)}) async-start(f32[32,8,128]{2,1,0:T(8,128)} %pair_weight.1), calls=%async_computation | async-start | bytes 262144 | tf_op jit(solution)/shard_map/all_to_all | solution.py:546
  91.2 0.3 collective-permute-start.18
  91.5 1.8 %collective-permute-start.19 = (bf16[15,16,128]{2,1,0:T(8,128)(2,1)S(1)}, bf16[15,16,128]{2,1,0:T(8,128)(2,1)S(1)}, u32[]{:S(2)}, u32[]{:S(2)}) collective-permute-start(bf16[15,16,128]{2,1,0:T(8,128)(2,1)S(1)} %get-tuple-element.118), channel_id=1, source_target_pairs={{0,4},{2,6},{4,0},{6,2},{8,12},{10,14},{12,8},{14,10},{16,20},{18,... | collective-permute-start | bytes 184328 | tf_op jit(solution)/shard_map/ppermute | solution.py:537
  93.3 2.7 %collective-permute-done.19.refs_4_.refs_3_ = bf16[15,16,128]{2,1,0:T(8,128)(2,1)S(1)} collective-permute-done((bf16[15,16,128]{2,1,0:T(8,128)(2,1)S(1)}, bf16[15,16,128]{2,1,0:T(8,128)(2,1)S(1)}, u32[]{:S(2)}, u32[]{:S(2)}) %collective-permute-start.19) | collective-permute-done | bytes 61472 | tf_op jit(solution)/shard_map/ppermute | solution.py:537
  96.0 1.2 %collective-permute-done.18.refs_2_ = bf16[27,16,128]{2,1,0:T(8,128)(2,1)S(1)} collective-permute-done((bf16[27,16,128]{2,1,0:T(8,128)(2,1)S(1)}, bf16[27,16,128]{2,1,0:T(8,128)(2,1)S(1)}, u32[]{:S(2)}, u32[]{:S(2)}) %collective-permute-start.18) | collective-permute-done | bytes 110624 | tf_op jit(solution)/shard_map/ppermute | solution.py:542
  97.2 0.6 far.1
  97.8 2.3 %collective-permute-start.21 = (bf16[27,16,128]{2,1,0:T(8,128)(2,1)S(1)}, bf16[27,16,128]{2,1,0:T(8,128)(2,1)S(1)}, u32[]{:S(2)}, u32[]{:S(2)}) collective-permute-start(bf16[27,16,128]{2,1,0:T(8,128)(2,1)S(1)} %get-tuple-element.121), channel_id=1, source_target_pairs={{0,16},{2,18},{4,20},{6,22},{8,24},{10,26},{12,28},{14,30},{16,0},... | collective-permute-start | bytes 331784 | tf_op jit(solution)/shard_map/ppermute | solution.py:537
  100.0 1.1 collective-permute-start.22
  101.1 2.9 %pair.1 = bf16[2048,128]{1,0:T(8,128)(2,1)} custom-call(s32[2]{0:T(128)S(1)} %copy-done.14, bf16[2048,128]{1,0:T(8,128)(2,1)S(1)} %bitcast.19, f32[1,128]{1,0:T(1,128)S(1)} %bitcast.26, bf16[8,128]{1,0:T(8,128)(2,1)S(1)} %bitcast.24, bf16[64,128]{1,0:T(8,128)(2,1)S(1)} %get-tuple-element.125.refs_2_.refs_4_, ...), custom_call_target="tpu_custom_call" | custom-call | flops 67108864 | bytes 1083912 | tf_op jit(solution)/shard_map/pair/pallas_call | solution.py:79
  104.0 1.5 %collective-permute-done.21.refs_1_ = bf16[27,16,128]{2,1,0:T(8,128)(2,1)S(1)} collective-permute-done((bf16[27,16,128]{2,1,0:T(8,128)(2,1)S(1)}, bf16[27,16,128]{2,1,0:T(8,128)(2,1)S(1)}, u32[]{:S(2)}, u32[]{:S(2)}) %collective-permute-start.21) | collective-permute-done | bytes 110624 | tf_op jit(solution)/shard_map/ppermute | solution.py:537
  105.5 0.7 close.1
  (50 shorter events, 0.2 us)
Async XLA Ops:
  0.6 17.8 %copy-start.4 = (bf16[768,768]{1,0:T(8,128)(2,1)S(1)}, bf16[768,768]{1,0:T(8,128)(2,1)}, u32[]{:S(2)}) copy-start(bf16[768,768]{1,0:T(8,128)(2,1)} %refs_1_.3) | copy-start | bytes 3538948
  5.4 10.7 %collective-permute-start.3 = (bf16[128,768]{1,0:T(8,128)(2,1)}, bf16[128,768]{1,0:T(8,128)(2,1)S(1)}, u32[]{:S(2)}, u32[]{:S(2)}) collective-permute-start(bf16[128,768]{1,0:T(8,128)(2,1)} %get-tuple-element.75.refs_2_), channel_id=1, source_target_pairs={{0,1},{1,0},{2,3},{3,2},{4,5},{5,4},{6,7},{7,6},{8,9},{9,8},{10,11... | collective-permute-start | bytes 589832 | tf_op jit(solution)/shard_map/ppermute | solution.py:542
  5.5 4.7 %collective-permute-start = (bf16[2,64,128]{2,1,0:T(8,128)(2,1)}, bf16[2,64,128]{2,1,0:T(8,128)(2,1)S(1)}, u32[]{:S(2)}, u32[]{:S(2)}) collective-permute-start(bf16[2,64,128]{2,1,0:T(8,128)(2,1)} %get-tuple-element.74.refs_0_), channel_id=1, source_target_pairs={{0,8},{2,10},{4,12},{6,14},{8,0},{10,2},{12,4},{14,6},{16,24},{18,... | collective-permute-start | bytes 98312 | tf_op jit(solution)/shard_map/ppermute | solution.py:537
  7.6 5.3 %collective-permute-start.1 = (bf16[2,64,128]{2,1,0:T(8,128)(2,1)}, bf16[2,64,128]{2,1,0:T(8,128)(2,1)S(1)}, u32[]{:S(2)}, u32[]{:S(2)}) collective-permute-start(bf16[2,64,128]{2,1,0:T(8,128)(2,1)} %get-tuple-element.74.refs_0_), channel_id=1, source_target_pairs={{0,16},{2,18},{4,20},{6,22},{8,24},{10,26},{12,28},{14,30},{16,0},... | collective-permute-start | bytes 98312 | tf_op jit(solution)/shard_map/ppermute | solution.py:537
  10.2 5.9 %collective-permute-start.2 = (bf16[2,64,128]{2,1,0:T(8,128)(2,1)}, bf16[2,64,128]{2,1,0:T(8,128)(2,1)S(1)}, u32[]{:S(2)}, u32[]{:S(2)}) collective-permute-start(bf16[2,64,128]{2,1,0:T(8,128)(2,1)} %get-tuple-element.74.refs_0_), channel_id=1, source_target_pairs={{0,24},{2,26},{4,28},{6,30},{8,16},{10,18},{12,20},{14,22},{16,8},... | collective-permute-start | bytes 98312 | tf_op jit(solution)/shard_map/ppermute | solution.py:537
  16.1 0.8 copy-start.15
  16.9 5.5 %collective-permute-start.4 = (bf16[4,64,128]{2,1,0:T(8,128)(2,1)S(1)}, bf16[4,64,128]{2,1,0:T(8,128)(2,1)S(1)}, u32[]{:S(2)}, u32[]{:S(2)}) collective-permute-start(bf16[4,64,128]{2,1,0:T(8,128)(2,1)S(1)} %get-tuple-element.80), channel_id=1, source_target_pairs={{0,1},{1,0},{2,3},{3,2},{4,5},{5,4},{6,7},{7,6},{8,9},{9,8},{10,11... | collective-permute-start | bytes 196616 | tf_op jit(solution)/shard_map/ppermute | solution.py:542
  18.4 1.3 %copy-start.5 = (bf16[768,768]{1,0:T(8,128)(2,1)S(1)}, bf16[768,768]{1,0:T(8,128)(2,1)}, u32[]{:S(2)}) copy-start(bf16[768,768]{1,0:T(8,128)(2,1)} %refs_2_.3) | copy-start | bytes 3538948
  19.7 1.3 %copy-start.6 = (bf16[768,768]{1,0:T(8,128)(2,1)S(1)}, bf16[768,768]{1,0:T(8,128)(2,1)}, u32[]{:S(2)}) copy-start(bf16[768,768]{1,0:T(8,128)(2,1)} %refs_3_.1) | copy-start | bytes 3538948
  21.0 0.7 copy-start.13
  21.6 7.6 %copy-start.12 = (f32[256,128]{1,0:T(8,128)S(1)}, f32[256,128]{1,0:T(8,128)}, u32[]{:S(2)}) copy-start(f32[256,128]{1,0:T(8,128)} %get-tuple-element.81.refs_6_) | copy-start | bytes 393220
  22.4 1.7 %copy-start.11 = (bf16[128,768]{1,0:T(8,128)(2,1)S(1)}, bf16[128,768]{1,0:T(8,128)(2,1)}, u32[]{:S(2)}) copy-start(bf16[128,768]{1,0:T(8,128)(2,1)} %get-tuple-element.75.refs_2_) | copy-start | bytes 589828
  22.4 9.5 %copy-start.2 = (bf16[1536,768]{1,0:T(8,128)(2,1)S(1)}, bf16[1536,768]{1,0:T(8,128)(2,1)}, u32[]{:S(2)}) copy-start(bf16[1536,768]{1,0:T(8,128)(2,1)} %refs_1_.2) | copy-start | bytes 7077892
  22.4 6.7 %copy-start.14 = (s32[2]{0:T(128)S(1)}, s32[2]{0:T(128)}, u32[]{:S(2)}) copy-start(s32[2]{0:T(128)} %pad_add_fusion.refs_0_) | copy-start | bytes 28
  22.5 6.7 %copy-start.18 = (f32[1,256]{1,0:T(1,128)S(1)}, f32[1,256]{1,0:T(1,128)}, u32[]{:S(2)}) copy-start(f32[1,256]{1,0:T(1,128)} %get-tuple-element.82.refs_7_) | copy-start | bytes 3076
  22.5 9.5 %copy-start.20 = (f32[768]{0:T(1024)S(1)}, f32[768]{0:T(1024)}, u32[]{:S(2)}) copy-start(f32[768]{0:T(1024)} %param.29) | copy-start | bytes 9220
  22.5 9.5 %copy-start.8 = (bf16[1,128,768]{2,1,0:T(8,128)(2,1)S(1)}, bf16[1,128,768]{2,1,0:T(8,128)(2,1)}, u32[]{:S(2)}) copy-start(bf16[1,128,768]{2,1,0:T(8,128)(2,1)} %param.20) | copy-start | bytes 589828
  22.5 9.5 %copy-start.10 = (bf16[1,128,768]{2,1,0:T(8,128)(2,1)S(1)}, bf16[1,128,768]{2,1,0:T(8,128)(2,1)}, u32[]{:S(2)}) copy-start(bf16[1,128,768]{2,1,0:T(8,128)(2,1)} %param.39) | copy-start | bytes 589828
  22.5 5.0 %collective-permute-start.5 = (bf16[2,4,64,128]{3,2,1,0:T(8,128)(2,1)S(1)}, bf16[2,4,64,128]{3,2,1,0:T(8,128)(2,1)S(1)}, u32[]{:S(2)}, u32[]{:S(2)}) collective-permute-start(bf16[2,4,64,128]{3,2,1,0:T(8,128)(2,1)S(1)} %join_tok.1.refs_0_), channel_id=1, source_target_pairs={{0,4},{2,6},{4,0},{6,2},{8,12},{10,14},{12,8},{14,10},{16,20},{18,... | collective-permute-start | bytes 393224 | tf_op jit(solution)/shard_map/ppermute | solution.py:537
  24.1 12.1 %copy-start.7 = (bf16[768,768]{1,0:T(8,128)(2,1)S(1)}, bf16[768,768]{1,0:T(8,128)(2,1)}, u32[]{:S(2)}) copy-start(bf16[768,768]{1,0:T(8,128)(2,1)} %refs_7_.1) | copy-start | bytes 3538948
  27.5 8.7 %copy-start.1 = (bf16[768,1536]{1,0:T(8,128)(2,1)S(1)}, bf16[768,1536]{1,0:T(8,128)(2,1)}, u32[]{:S(2)}) copy-start(bf16[768,1536]{1,0:T(8,128)(2,1)} %refs_9_.1) | copy-start | bytes 7077892
  27.6 1.6 %collective-permute-start.6 = (bf16[2,2,4,64,128]{4,3,2,1,0:T(8,128)(2,1)S(1)}, bf16[2,2,4,64,128]{4,3,2,1,0:T(8,128)(2,1)S(1)}, u32[]{:S(2)}, u32[]{:S(2)}) collective-permute-start(bf16[2,2,4,64,128]{4,3,2,1,0:T(8,128)(2,1)S(1)} %join_y.1.refs_4_), channel_id=1, source_target_pairs={{0,2},{2,0},{4,6},{6,4},{8,10},{10,8},{12,14},{14,12},{16,18},{18,... | collective-permute-start | bytes 786440 | tf_op jit(solution)/shard_map/ppermute | solution.py:537
  29.2 7.1 %copy-start = (bf16[768,1536]{1,0:T(8,128)(2,1)S(1)}, bf16[768,1536]{1,0:T(8,128)(2,1)}, u32[]{:S(2)}) copy-start(bf16[768,1536]{1,0:T(8,128)(2,1)} %refs_8_.1) | copy-start | bytes 7077892
  31.3 4.9 %collective-permute-start.7 = (bf16[128,384]{1,0:T(8,128)(2,1)S(1)}, bf16[128,384]{1,0:T(8,128)(2,1)S(1)}, u32[]{:S(2)}, u32[]{:S(2)}) collective-permute-start(bf16[128,384]{1,0:T(8,128)(2,1)S(1)} %get-tuple-element.84), channel_id=1, source_target_pairs={{0,1},{1,0},{2,3},{3,2},{4,5},{5,4},{6,7},{7,6},{8,9},{9,8},{10,11... | collective-permute-start | bytes 294920 | tf_op jit(solution)/shard_map/ppermute | solution.py:542
  40.6 4.7 %collective-permute-start.8 = (bf16[384,128]{1,0:T(8,128)(2,1)S(1)}, bf16[384,128]{1,0:T(8,128)(2,1)S(1)}, u32[]{:S(2)}, u32[]{:S(2)}) collective-permute-start(bf16[384,128]{1,0:T(8,128)(2,1)S(1)} %get-tuple-element.89), channel_id=1, source_target_pairs={{0,1},{1,0},{2,3},{3,2},{4,5},{5,4},{6,7},{7,6},{8,9},{9,8},{10,11... | collective-permute-start | bytes 294920 | tf_op jit(solution)/shard_map/ppermute | solution.py:542
  47.3 7.3 %collective-permute-start.11 = (bf16[64,16,128]{2,1,0:T(8,128)(2,1)S(1)}, bf16[64,16,128]{2,1,0:T(8,128)(2,1)S(1)}, u32[]{:S(2)}, u32[]{:S(2)}) collective-permute-start(bf16[64,16,128]{2,1,0:T(8,128)(2,1)S(1)} %get-tuple-element.102), channel_id=1, source_target_pairs={{0,4},{2,6},{4,0},{6,2},{8,12},{10,14},{12,8},{14,10},{16,20},{18,... | collective-permute-start | bytes 786440 | tf_op jit(solution)/shard_map/ppermute | solution.py:537
  48.9 5.7 %collective-permute-start.12 = (bf16[128,768]{1,0:T(8,128)(2,1)S(1)}, bf16[128,768]{1,0:T(8,128)(2,1)S(1)}, u32[]{:S(2)}, u32[]{:S(2)}) collective-permute-start(bf16[128,768]{1,0:T(8,128)(2,1)S(1)} %get-tuple-element.103.refs_5_), channel_id=1, source_target_pairs={{0,1},{1,0},{2,3},{3,2},{4,5},{5,4},{6,7},{7,6},{8,9},{9,8},{10,11... | collective-permute-start | bytes 589832 | tf_op jit(solution)/shard_map/ppermute | solution.py:542
  51.7 6.1 %collective-permute-start.10 = (bf16[216,16,128]{2,1,0:T(8,128)(2,1)S(1)}, bf16[216,16,128]{2,1,0:T(8,128)(2,1)S(1)}, u32[]{:S(2)}, u32[]{:S(2)}) collective-permute-start(bf16[216,16,128]{2,1,0:T(8,128)(2,1)S(1)} %get-tuple-element.98), channel_id=1, source_target_pairs={{0,2},{2,0},{4,6},{6,4},{8,10},{10,8},{12,14},{14,12},{16,18},{18,... | collective-permute-start | bytes 2654216 | tf_op jit(solution)/shard_map/ppermute | solution.py:537
  55.7 4.3 %copy-start.19 = (f32[768]{0:T(1024)S(1)}, f32[768]{0:T(1024)}, u32[]{:S(2)}) copy-start(f32[768]{0:T(1024)} %refs_5_.1) | copy-start | bytes 9220
  55.7 2.1 %collective-permute-start.13 = (bf16[152,16,128]{2,1,0:T(8,128)(2,1)S(1)}, bf16[152,16,128]{2,1,0:T(8,128)(2,1)S(1)}, u32[]{:S(2)}, u32[]{:S(2)}) collective-permute-start(bf16[152,16,128]{2,1,0:T(8,128)(2,1)S(1)} %get-tuple-element.105), channel_id=1, source_target_pairs={{0,2},{2,0},{4,6},{6,4},{8,10},{10,8},{12,14},{14,12},{16,18},{18,... | collective-permute-start | bytes 1867784 | tf_op jit(solution)/shard_map/ppermute | solution.py:537
  58.7 12.3 %collective-permute-start.14 = (bf16[108,16,128]{2,1,0:T(8,128)(2,1)S(1)}, bf16[108,16,128]{2,1,0:T(8,128)(2,1)S(1)}, u32[]{:S(2)}, u32[]{:S(2)}) collective-permute-start(bf16[108,16,128]{2,1,0:T(8,128)(2,1)S(1)} %get-tuple-element.107), channel_id=1, source_target_pairs={{0,4},{2,6},{4,0},{6,2},{8,12},{10,14},{12,8},{14,10},{16,20},{18,... | collective-permute-start | bytes 1327112 | tf_op jit(solution)/shard_map/ppermute | solution.py:537
  59.5 9.1 %collective-permute-start.15 = (bf16[76,16,128]{2,1,0:T(8,128)(2,1)S(1)}, bf16[76,16,128]{2,1,0:T(8,128)(2,1)S(1)}, u32[]{:S(2)}, u32[]{:S(2)}) collective-permute-start(bf16[76,16,128]{2,1,0:T(8,128)(2,1)S(1)} %get-tuple-element.109), channel_id=1, source_target_pairs={{0,8},{2,10},{4,12},{6,14},{8,0},{10,2},{12,4},{14,6},{16,24},{18,... | collective-permute-start | bytes 933896 | tf_op jit(solution)/shard_map/ppermute | solution.py:537
  59.5 6.7 %collective-permute-start.9 = (bf16[768,128]{1,0:T(8,128)(2,1)S(1)}, bf16[768,128]{1,0:T(8,128)(2,1)S(1)}, u32[]{:S(2)}, u32[]{:S(2)}) collective-permute-start(bf16[768,128]{1,0:T(8,128)(2,1)S(1)} %get-tuple-element.95), channel_id=1, source_target_pairs={{0,1},{1,0},{2,3},{3,2},{4,5},{5,4},{6,7},{7,6},{8,9},{9,8},{10,11... | collective-permute-start | bytes 589832 | tf_op jit(solution)/shard_map/ppermute | solution.py:542
  66.1 20.6 %copy-start.9 = (bf16[16,128,128]{2,1,0:T(8,128)(2,1)S(1)}, bf16[16,128,128]{2,1,0:T(8,128)(2,1)}, u32[]{:S(2)}) copy-start(bf16[16,128,128]{2,1,0:T(8,128)(2,1)} %get-tuple-element.124.refs_1_) | copy-start | bytes 1572868
  71.0 30.1 %copy-start.3 = (bf16[128,16,128]{2,1,0:T(8,128)(2,1)S(1)}, bf16[128,16,128]{2,1,0:T(8,128)(2,1)}, u32[]{:S(2)}) copy-start(bf16[128,16,128]{2,1,0:T(8,128)(2,1)} %param.22) | copy-start | bytes 1572868
  71.0 30.1 %copy-start.16 = (bf16[128,8]{0,1:T(8,128)(2,1)S(1)}, bf16[128,8]{0,1:T(8,128)(2,1)}, u32[]{:S(2)}) copy-start(bf16[128,8]{0,1:T(8,128)(2,1)} %param.34) | copy-start | bytes 6148
  71.0 30.1 %copy-start.17 = (f32[128]{0:T(128)S(1)}, f32[128]{0:T(128)}, u32[]{:S(2)}) copy-start(f32[128]{0:T(128)} %param.28) | copy-start | bytes 1540
  71.7 10.0 %collective-permute-start.16 = (bf16[54,16,128]{2,1,0:T(8,128)(2,1)S(1)}, bf16[54,16,128]{2,1,0:T(8,128)(2,1)S(1)}, u32[]{:S(2)}, u32[]{:S(2)}) collective-permute-start(bf16[54,16,128]{2,1,0:T(8,128)(2,1)S(1)} %get-tuple-element.112), channel_id=1, source_target_pairs={{0,8},{2,10},{4,12},{6,14},{8,0},{10,2},{12,4},{14,6},{16,24},{18,... | collective-permute-start | bytes 663560 | tf_op jit(solution)/shard_map/ppermute | solution.py:537
  71.8 9.7 %collective-permute-start.17 = (bf16[38,16,128]{2,1,0:T(8,128)(2,1)S(1)}, bf16[38,16,128]{2,1,0:T(8,128)(2,1)S(1)}, u32[]{:S(2)}, u32[]{:S(2)}) collective-permute-start(bf16[38,16,128]{2,1,0:T(8,128)(2,1)S(1)} %get-tuple-element.114), channel_id=1, source_target_pairs={{0,16},{2,18},{4,20},{6,22},{8,24},{10,26},{12,28},{14,30},{16,0},... | collective-permute-start | bytes 466952 | tf_op jit(solution)/shard_map/ppermute | solution.py:537
  83.0 3.8 %collective-permute-start.20 = (bf16[64,128]{1,0:T(8,128)(2,1)S(1)}, bf16[64,128]{1,0:T(8,128)(2,1)S(1)}, u32[]{:S(2)}, u32[]{:S(2)}) collective-permute-start(bf16[64,128]{1,0:T(8,128)(2,1)S(1)} %get-tuple-element.119), channel_id=1, source_target_pairs={{0,1},{1,0},{2,3},{3,2},{4,5},{5,4},{6,7},{7,6},{8,9},{9,8},{10,11... | collective-permute-start | bytes 49160 | tf_op jit(solution)/shard_map/ppermute | solution.py:542
  88.3 17.3 %all-to-all-start = ((f32[32,8,128]{2,1,0:T(8,128)}), f32[32,8,128]{2,1,0:T(8,128)S(1)}, u32[]{:S(2)}, u32[]{:S(2)}) async-start(f32[32,8,128]{2,1,0:T(8,128)} %pair_weight.1), calls=%async_computation | async-start | bytes 262144 | tf_op jit(solution)/shard_map/all_to_all | solution.py:546
  91.2 6.0 %collective-permute-start.18 = (bf16[27,16,128]{2,1,0:T(8,128)(2,1)S(1)}, bf16[27,16,128]{2,1,0:T(8,128)(2,1)S(1)}, u32[]{:S(2)}, u32[]{:S(2)}) collective-permute-start(bf16[27,16,128]{2,1,0:T(8,128)(2,1)S(1)} %get-tuple-element.116), channel_id=1, source_target_pairs={{0,1},{1,0},{2,3},{3,2},{4,5},{5,4},{6,7},{7,6},{8,9},{9,8},{10,11... | collective-permute-start | bytes 331784 | tf_op jit(solution)/shard_map/ppermute | solution.py:542
  91.5 4.5 %collective-permute-start.19 = (bf16[15,16,128]{2,1,0:T(8,128)(2,1)S(1)}, bf16[15,16,128]{2,1,0:T(8,128)(2,1)S(1)}, u32[]{:S(2)}, u32[]{:S(2)}) collective-permute-start(bf16[15,16,128]{2,1,0:T(8,128)(2,1)S(1)} %get-tuple-element.118), channel_id=1, source_target_pairs={{0,4},{2,6},{4,0},{6,2},{8,12},{10,14},{12,8},{14,10},{16,20},{18,... | collective-permute-start | bytes 184328 | tf_op jit(solution)/shard_map/ppermute | solution.py:537
  97.8 7.7 %collective-permute-start.21 = (bf16[27,16,128]{2,1,0:T(8,128)(2,1)S(1)}, bf16[27,16,128]{2,1,0:T(8,128)(2,1)S(1)}, u32[]{:S(2)}, u32[]{:S(2)}) collective-permute-start(bf16[27,16,128]{2,1,0:T(8,128)(2,1)S(1)} %get-tuple-element.121), channel_id=1, source_target_pairs={{0,16},{2,18},{4,20},{6,22},{8,24},{10,26},{12,28},{14,30},{16,0},... | collective-permute-start | bytes 331784 | tf_op jit(solution)/shard_map/ppermute | solution.py:537
  100.0 4.0 %collective-permute-start.22 = (bf16[3,16,128]{2,1,0:T(8,128)(2,1)S(1)}, bf16[3,16,128]{2,1,0:T(8,128)(2,1)S(1)}, u32[]{:S(2)}, u32[]{:S(2)}) collective-permute-start(bf16[3,16,128]{2,1,0:T(8,128)(2,1)S(1)} %get-tuple-element.123), channel_id=1, source_target_pairs={{0,1},{1,0},{2,3},{3,2},{4,5},{5,4},{6,7},{7,6},{8,9},{9,8},{10,11... | collective-permute-start | bytes 36872 | tf_op jit(solution)/shard_map/ppermute | solution.py:542

commit v14 on v13

--- a/solution.py
+++ b/solution.py
@@ -501,19 +501,14 @@
 def pair_weight_kernel(toks, ids, columns, *rest):
     parts, (weight_grad, grads) = rest[:toks], rest[toks:]
     set_heads(toks, ids, parts, grads)
-    grad_b = grads[...].astype(bf16)
     cols, _, channels = columns.shape
-    row_col = low_bits(lax.broadcasted_iota(jnp.int32, (grad_b.shape[0], channels), 0), cols)
-    sums = jnp.zeros((grad_b.shape[0], channels), f32)
+    heads = weight_grad.shape[1]
+    sums = jnp.zeros((heads, channels), f32)
     for j in range(cols):
-        sums = sums + jnp.where(row_col == j, mm(grad_b, columns[j]), 0.0)
-    heads = weight_grad.shape[1]
-    lines = [
-        jnp.sum(sums[h * cols : (h + 1) * cols, :], axis=0, keepdims=True) for h in range(heads)
-    ]
-    whole = jnp.concatenate(lines, axis=0)
+        lines = grads[pl.ds(j, heads, stride=cols), :].astype(bf16)
+        sums = sums + mm(lines, columns[j])
     for n in range(weight_grad.shape[0]):
-        weight_grad[n] = whole
+        weight_grad[n] = sums
 
 
 def pair_kernel(toks, cols, ids, pair, gain, w_pair, *rest):
@@ -766,7 +761,7 @@
             bias_ready = pairs[1]
             if toks == 2:
                 break
-        pairs = step("step_%d" % n, pairs, segments, deps=[exited] if n == 1 else ())
+        pairs = step("step_%d" % n, pairs, segments, deps=[exited] if n == 2 else ())
         parts //= 2
     if toks == 2:
         kept, sent, kept_b, sent_b = call(
@@ -774,6 +769,7 @@
             "across",
             [where_am_i] + [array for one in pairs for array in one],
             [((first_tiles, 16, 128), bf16)] * 2 + [((second_tiles, 16, 128), bf16)] * 2,
+            deps=[exited],
         )
         pairs = [(kept, swap_tok(sent, 1)), (kept_b, swap_copy(sent_b, masks_b[-1]))]
     bias_pieces = call(
@@ -798,7 +794,6 @@
         )
         pairs[0] = (kept, swap_copy(sent, copies // 2))
         single_pair = (single_kept, swap_tok(single_sent, 1))
-        ready = []
 
     group = copies // toks
     swaps = []

time: 108 us -> 108 us (level)
    ppermute x9, waiting for transfers between devices: 20.8 us -> 18.3 us  [swap_tok(): return lax.ppermute(value, 'tok', [(i, i ^ mask) for i in range(size)])]
    ppermute x14, waiting for transfers between devices: 28.5 us -> 29.9 us  [swap_copy(): return lax.ppermute(value, 'copy', [(i, i ^ mask) for i in range(size)])]
  transfers between devices with their start and end apart: 24 -> 24, of which waited for: 17 -> 15; matrix products, arithmetic and copies ran while one was open for 0% -> 0% of each run, Pallas kernels for 10% -> 11%
where the time goes in v14:
time: 108 us; the launch traced here: 106 us
  waiting for transfers between devices  48.2 us (45%)
  Pallas kernels  28.8 us (27%)
  starting transfers between devices  23.4 us (22%)
  local copies, waits for them, and re-layouts  4.04 us (4%)
    ppermute x14, waiting for transfers between devices, swap_copy(): return lax.ppermute(value, 'copy', [(i, i ^ mask) for i in range(size)])  29.9 us
    pallas_call x21, Pallas kernels, call(): pl.pallas_call(whole, name=name, out_shape=[jax.ShapeDtypeStruct(one[0],...  28.8 us
    ppermute x9, waiting for transfers between devices, swap_tok(): return lax.ppermute(value, 'tok', [(i, i ^ mask) for i in range(size)])  18.3 us
    ppermute x14, starting transfers between devices, swap_copy(): return lax.ppermute(value, 'copy', [(i, i ^ mask) for i in range(size)])  12.9 us
    ppermute x9, starting transfers between devices, swap_tok(): return lax.ppermute(value, 'tok', [(i, i ^ mask) for i in range(size)])  6.67 us
    unnamed x42, local copies, waits for them, and re-layouts  4.04 us
    all_to_all x1, starting transfers between devices, exchange(): return lax.all_to_all(value, ('copy', 'tok'), 0, 0)  3.88 us
  transfers between devices with their start and end apart: 24, of which 15 were waited for; matrix products, arithmetic and copies ran while one was open for 0% of the time, Pallas kernels for 11%

profile of v14, /device:TPU:2, one launch (start us, length us, event | category | flops | bytes accessed | tf_op | source)
XLA Modules:
  0.0 106.0 jit_solution(10082288807697587696)
XLA Ops:
  0.6 0.6 pad_add_fusion.refs_0_
  1.2 4.2 %enter.1 = (bf16[128,768]{1,0:T(8,128)(2,1)}, bf16[16,128,128]{2,1,0:T(8,128)(2,1)}, f32[256,128]{1,0:T(8,128)}, f32[1,256]{1,0:T(1,128)}, bf16[2,64,128]{2,1,0:T(8,128)(2,1)}) custom-call(s32[2]{0:T(128)} %pad_add_fusion.refs_0_, bf16[128,768]{1,0:T(8,128)(2,1)} %bitcast.20, bf16[128,768]{1,0:T(8,128)(2,1)} %refs_2_.2, s32[1,128]{1,0:T(1,128)} %bitcast.30, ...), custom_call_target="tpu_custom_call" | custom-call | flops 67108864 | bytes 1860808 | tf_op jit(solution)/shard_map/enter/pallas_call | solution.py:79
  5.4 0.1 collective-permute-start.3
  5.5 2.1 %collective-permute-start = (bf16[2,64,128]{2,1,0:T(8,128)(2,1)}, bf16[2,64,128]{2,1,0:T(8,128)(2,1)S(1)}, u32[]{:S(2)}, u32[]{:S(2)}) collective-permute-start(bf16[2,64,128]{2,1,0:T(8,128)(2,1)} %get-tuple-element.74.refs_0_), channel_id=1, source_target_pairs={{0,8},{2,10},{4,12},{6,14},{8,0},{10,2},{12,4},{14,6},{16,24},{18,... | collective-permute-start | bytes 98312 | tf_op jit(solution)/shard_map/ppermute | solution.py:532
  7.6 2.6 %collective-permute-start.1 = (bf16[2,64,128]{2,1,0:T(8,128)(2,1)}, bf16[2,64,128]{2,1,0:T(8,128)(2,1)S(1)}, u32[]{:S(2)}, u32[]{:S(2)}) collective-permute-start(bf16[2,64,128]{2,1,0:T(8,128)(2,1)} %get-tuple-element.74.refs_0_), channel_id=1, source_target_pairs={{0,16},{2,18},{4,20},{6,22},{8,24},{10,26},{12,28},{14,30},{16,0},... | collective-permute-start | bytes 98312 | tf_op jit(solution)/shard_map/ppermute | solution.py:532
  10.2 2.7 %collective-permute-done.1.refs_2_ = bf16[2,64,128]{2,1,0:T(8,128)(2,1)S(1)} collective-permute-done((bf16[2,64,128]{2,1,0:T(8,128)(2,1)}, bf16[2,64,128]{2,1,0:T(8,128)(2,1)S(1)}, u32[]{:S(2)}, u32[]{:S(2)}) %collective-permute-start.1) | collective-permute-done | bytes 32800 | tf_op jit(solution)/shard_map/ppermute | solution.py:532
  12.9 3.2 %collective-permute-done.2.refs_3_ = bf16[2,64,128]{2,1,0:T(8,128)(2,1)S(1)} collective-permute-done((bf16[2,64,128]{2,1,0:T(8,128)(2,1)}, bf16[2,64,128]{2,1,0:T(8,128)(2,1)S(1)}, u32[]{:S(2)}, u32[]{:S(2)}) %collective-permute-start.2) | collective-permute-done | bytes 32800 | tf_op jit(solution)/shard_map/ppermute | solution.py:532
  16.1 0.8 copy-done.15
  16.9 1.6 %collective-permute-start.4 = (bf16[4,64,128]{2,1,0:T(8,128)(2,1)S(1)}, bf16[4,64,128]{2,1,0:T(8,128)(2,1)S(1)}, u32[]{:S(2)}, u32[]{:S(2)}) collective-permute-start(bf16[4,64,128]{2,1,0:T(8,128)(2,1)S(1)} %get-tuple-element.80), channel_id=1, source_target_pairs={{0,1},{1,0},{2,3},{3,2},{4,5},{5,4},{6,7},{7,6},{8,9},{9,8},{10,11... | collective-permute-start | bytes 196616 | tf_op jit(solution)/shard_map/ppermute | solution.py:537
  18.4 1.3 %copy-done.5 = bf16[768,768]{1,0:T(8,128)(2,1)S(1)} copy-done((bf16[768,768]{1,0:T(8,128)(2,1)S(1)}, bf16[768,768]{1,0:T(8,128)(2,1)}, u32[]{:S(2)}) %copy-start.5) | copy-done | bytes 1179672
  19.7 1.3 %copy-done.6 = bf16[768,768]{1,0:T(8,128)(2,1)S(1)} copy-done((bf16[768,768]{1,0:T(8,128)(2,1)S(1)}, bf16[768,768]{1,0:T(8,128)(2,1)}, u32[]{:S(2)}) %copy-start.6) | copy-done | bytes 1179672
  21.0 0.7 copy-done.13
  21.6 0.8 stage.1.refs_1_.refs_2_
  22.4 0.0 copy-start.2
  22.5 0.0 copy-start.18
  22.5 0.0 copy-start.20
  22.5 1.6 %collective-permute-start.5 = (bf16[2,4,64,128]{3,2,1,0:T(8,128)(2,1)S(1)}, bf16[2,4,64,128]{3,2,1,0:T(8,128)(2,1)S(1)}, u32[]{:S(2)}, u32[]{:S(2)}) collective-permute-start(bf16[2,4,64,128]{3,2,1,0:T(8,128)(2,1)S(1)} %join_tok.1.refs_0_), channel_id=1, source_target_pairs={{0,4},{2,6},{4,0},{6,2},{8,12},{10,14},{12,8},{14,10},{16,20},{18,... | collective-permute-start | bytes 393224 | tf_op jit(solution)/shard_map/ppermute | solution.py:532
  24.1 1.4 %project.1 = (bf16[256,768]{1,0:T(8,128)(2,1)S(1)}, bf16[384,256]{1,0:T(8,128)(2,1)S(1)}, bf16[384,256]{1,0:T(8,128)(2,1)S(1)}, bf16[384,256]{1,0:T(8,128)(2,1)S(1)}) custom-call(s32[2]{0:T(128)S(1)} %copy-done.13, bf16[3,768,384]{2,1,0:T(8,128)(2,1)S(1)} %stage.1.refs_1_.refs_2_, bf16[128,768]{1,0:T(8,128)(2,1)S(1)} %copy-done.11, ...), custom_call_target="tpu_custom_call" | custom-call | flops 452984832 | bytes 3145736 | tf_op jit(solution)/shard_map/project/pallas_call | solution.py:79
  25.5 2.0 %collective-permute-done.5.refs_1_ = bf16[2,4,64,128]{3,2,1,0:T(8,128)(2,1)S(1)} collective-permute-done((bf16[2,4,64,128]{3,2,1,0:T(8,128)(2,1)S(1)}, bf16[2,4,64,128]{3,2,1,0:T(8,128)(2,1)S(1)}, u32[]{:S(2)}, u32[]{:S(2)}) %collective-permute-start.5) | collective-permute-done | bytes 131104 | tf_op jit(solution)/shard_map/ppermute | solution.py:532
  27.6 0.1 collective-permute-start.6
  27.6 1.5 %collective-permute-done.6.refs_5_ = bf16[2,2,4,64,128]{4,3,2,1,0:T(8,128)(2,1)S(1)} collective-permute-done((bf16[2,2,4,64,128]{4,3,2,1,0:T(8,128)(2,1)S(1)}, bf16[2,2,4,64,128]{4,3,2,1,0:T(8,128)(2,1)S(1)}, u32[]{:S(2)}, u32[]{:S(2)}) %collective-permute-start.6) | collective-permute-done | bytes 262176 | tf_op jit(solution)/shard_map/ppermute | solution.py:532
  29.2 2.1 %attention.1 = (bf16[4,256,256]{2,1,0:T(8,128)(2,1)S(1)}, bf16[256,384]{1,0:T(8,128)(2,1)S(1)}, bf16[128,384]{1,0:T(8,128)(2,1)S(1)}, bf16[128,384]{1,0:T(8,128)(2,1)S(1)}) custom-call(s32[2]{0:T(128)S(1)} %copy-done.14, bf16[384,256]{1,0:T(8,128)(2,1)S(1)} %get-tuple-element.77.refs_1_, bf16[384,256]{1,0:T(8,128)(2,1)S(1)} %get-tuple-element.78.refs_2_, ...), custom_call_target="tpu_custom_call" | custom-call | flops 100663296 | bytes 2163720 | tf_op jit(solution)/shard_map/attention/pallas_call | solution.py:79
  31.3 0.6 collective-permute-start.7
  32.0 0.9 down.1
  32.9 3.4 %collective-permute-done.7.refs_6_ = bf16[128,384]{1,0:T(8,128)(2,1)S(1)} collective-permute-done((bf16[128,384]{1,0:T(8,128)(2,1)S(1)}, bf16[128,384]{1,0:T(8,128)(2,1)S(1)}, u32[]{:S(2)}, u32[]{:S(2)}) %collective-permute-start.7) | collective-permute-done | bytes 98336 | tf_op jit(solution)/shard_map/ppermute | solution.py:537
  36.2 4.3 %hidden.1 = (f32[128,768]{1,0:T(8,128)S(1)}, bf16[128,768]{1,0:T(8,128)(2,1)S(1)}, bf16[384,128]{1,0:T(8,128)(2,1)S(1)}, bf16[384,128]{1,0:T(8,128)(2,1)S(1)}) custom-call(s32[2]{0:T(128)S(1)} %copy-done.14, bf16[128,768]{1,0:T(8,128)(2,1)S(1)} %get-tuple-element.70.refs_1_.refs_0_, bf16[128,768]{1,0:T(8,128)(2,1)S(1)} %get-tuple-element.71.refs_2_, ...), custom_call_target="tpu_custom_call" | custom-call | flops 1509949440 | bytes 8064008 | tf_op jit(solution)/shard_map/hidden/pallas_call | solution.py:79
  40.6 0.6 collective-permute-start.8
  41.2 4.1 %collective-permute-done.8.refs_6_ = bf16[384,128]{1,0:T(8,128)(2,1)S(1)} collective-permute-done((bf16[384,128]{1,0:T(8,128)(2,1)S(1)}, bf16[384,128]{1,0:T(8,128)(2,1)S(1)}, u32[]{:S(2)}, u32[]{:S(2)}) %collective-permute-start.8) | collective-permute-done | bytes 98336 | tf_op jit(solution)/shard_map/ppermute | solution.py:537
  45.3 2.0 %backward.1 = (bf16[384,256]{1,0:T(8,128)(2,1)S(1)}, bf16[384,256]{1,0:T(8,128)(2,1)S(1)}, bf16[384,256]{1,0:T(8,128)(2,1)S(1)}, bf16[64,16,128]{2,1,0:T(8,128)(...) custom-call(s32[2]{0:T(128)S(1)} %copy-done.14, ...), custom_call_target="tpu_custom_call" | custom-call | flops 201326592 | bytes 2818056 | tf_op jit(solution)/shard_map/backward/pallas_call | solution.py:79
  47.3 1.6 %collective-permute-start.11 = (bf16[64,16,128]{2,1,0:T(8,128)(2,1)S(1)}, bf16[64,16,128]{2,1,0:T(8,128)(2,1)S(1)}, u32[]{:S(2)}, u32[]{:S(2)}) collective-permute-start(bf16[64,16,128]{2,1,0:T(8,128)(2,1)S(1)} %get-tuple-element.102), channel_id=1, source_target_pairs={{0,4},{2,6},{4,0},{6,2},{8,12},{10,14},{12,8},{14,10},{16,20},{18,... | collective-permute-start | bytes 786440 | tf_op jit(solution)/shard_map/ppermute | solution.py:532
  48.9 0.5 collective-permute-start.12
  49.4 2.3 %first.1 = (bf16[216,16,128]{2,1,0:T(8,128)(2,1)S(1)}, bf16[216,16,128]{2,1,0:T(8,128)(2,1)S(1)}, f32[768,128]{1,0:T(8,128)S(1)}, f32[768,256]{1,0:T(8,128)S(1)}, bf16[768,128]{1,0:T(8,128)(2,1)S(1)}) custom-call(s32[2]{0:T(128)S(1)} %copy-done.14, bf16[3,768,384]{2,1,0:T(8,128)(2,1)S(1)} %stage.1.refs_1_.refs_2_, ...), custom_call_target="tpu_custom_call" | custom-call | flops 905969664 | bytes 5898248 | tf_op jit(solution)/shard_map/first/pallas_call | solution.py:79
  51.7 0.1 collective-permute-start.10
  51.8 2.8 %collective-permute-done.12.refs_6_ = bf16[128,768]{1,0:T(8,128)(2,1)S(1)} collective-permute-done((bf16[128,768]{1,0:T(8,128)(2,1)S(1)}, bf16[128,768]{1,0:T(8,128)(2,1)S(1)}, u32[]{:S(2)}, u32[]{:S(2)}) %collective-permute-start.12) | collective-permute-done | bytes 196640 | tf_op jit(solution)/shard_map/ppermute | solution.py:537
  54.6 1.1 %second.1 = (bf16[152,16,128]{2,1,0:T(8,128)(2,1)S(1)}, bf16[152,16,128]{2,1,0:T(8,128)(2,1)S(1)}) custom-call(s32[2]{0:T(128)S(1)} %copy-done.14, bf16[256,384]{1,0:T(8,128)(2,1)S(1)} %get-tuple-element.99.refs_1_, f32[768,256]{1,0:T(8,128)S(1)} %get-tuple-element.100.refs_2_, bf16[64,16,128]{2,1,0:T(8,128)(2,1)S(1)} %get-tuple-element.101.refs_3_, ...), custom_call_target="tpu_custom_call" | custom-call | flops 1509949440 | bytes 3145736 | tf_op jit(solution)/shard_map/second/pallas_call | solution.py:79
  55.7 0.1 collective-permute-start.13
  55.7 2.0 %collective-permute-done.13.refs_4_ = bf16[152,16,128]{2,1,0:T(8,128)(2,1)S(1)} collective-permute-done((bf16[152,16,128]{2,1,0:T(8,128)(2,1)S(1)}, bf16[152,16,128]{2,1,0:T(8,128)(2,1)S(1)}, u32[]{:S(2)}, u32[]{:S(2)}) %collective-permute-start.13) | collective-permute-done | bytes 622624 | tf_op jit(solution)/shard_map/ppermute | solution.py:532
  57.8 0.9 step_0.1
  58.7 0.8 collective-permute-start.14
  59.4 9.1 %collective-permute-done.15.refs_4_ = bf16[76,16,128]{2,1,0:T(8,128)(2,1)S(1)} collective-permute-done((bf16[76,16,128]{2,1,0:T(8,128)(2,1)S(1)}, bf16[76,16,128]{2,1,0:T(8,128)(2,1)S(1)}, u32[]{:S(2)}, u32[]{:S(2)}) %collective-permute-start.15) | collective-permute-done | bytes 311328 | tf_op jit(solution)/shard_map/ppermute | solution.py:532
  68.6 2.4 %collective-permute-done.14.refs_2_ = bf16[108,16,128]{2,1,0:T(8,128)(2,1)S(1)} collective-permute-done((bf16[108,16,128]{2,1,0:T(8,128)(2,1)S(1)}, bf16[108,16,128]{2,1,0:T(8,128)(2,1)S(1)}, u32[]{:S(2)}, u32[]{:S(2)}) %collective-permute-start.14) | collective-permute-done | bytes 442400 | tf_op jit(solution)/shard_map/ppermute | solution.py:532
  71.0 0.7 step_1.1
  71.7 0.1 collective-permute-start.16
  71.8 0.6 collective-permute-start.9
  72.4 0.8 collective-permute-start.17
  73.2 4.7 %collective-permute-done.9.refs_4_ = bf16[768,128]{1,0:T(8,128)(2,1)S(1)} collective-permute-done((bf16[768,128]{1,0:T(8,128)(2,1)S(1)}, bf16[768,128]{1,0:T(8,128)(2,1)S(1)}, u32[]{:S(2)}, u32[]{:S(2)}) %collective-permute-start.9) | collective-permute-done | bytes 196640 | tf_op jit(solution)/shard_map/ppermute | solution.py:537
  78.0 1.2 %exit.1 = (bf16[128,768]{1,0:T(8,128)(2,1)}, f32[8,128]{1,0:T(8,128)S(1)}) custom-call(bf16[128,768]{1,0:T(8,128)(2,1)S(1)} %get-tuple-element.70.refs_1_.refs_0_, f32[1,768]{1,0:T(1,128)S(1)} %reshape.49.refs_1_, f32[128,768]{1,0:T(8,128)S(1)} %get-tuple-element.85.refs_2_, f32[768,128]{1,0:T(8,128)S(1)} %get-tuple-element.94.refs_3_, ...), custom_call_target="tpu_custom_call" | custom-call | bytes 1383424 | tf_op jit(solution)/shard_map/exit/pallas_call | solution.py:79
  79.2 2.5 %collective-permute-done.17.refs_4_.refs_2_ = bf16[38,16,128]{2,1,0:T(8,128)(2,1)S(1)} collective-permute-done((bf16[38,16,128]{2,1,0:T(8,128)(2,1)S(1)}, bf16[38,16,128]{2,1,0:T(8,128)(2,1)S(1)}, u32[]{:S(2)}, u32[]{:S(2)}) %collective-permute-start.17) | collective-permute-done | bytes 155680 | tf_op jit(solution)/shard_map/ppermute | solution.py:532
  81.7 0.0 collective-permute-done.16.refs_2_
  81.7 0.6 across.1
  82.4 1.4 %collective-permute-start.18 = (bf16[27,16,128]{2,1,0:T(8,128)(2,1)S(1)}, bf16[27,16,128]{2,1,0:T(8,128)(2,1)S(1)}, u32[]{:S(2)}, u32[]{:S(2)}) collective-permute-start(bf16[27,16,128]{2,1,0:T(8,128)(2,1)S(1)} %get-tuple-element.116), channel_id=1, source_target_pairs={{0,1},{1,0},{2,3},{3,2},{4,5},{5,4},{6,7},{7,6},{8,9},{9,8},{10,11... | collective-permute-start | bytes 331784 | tf_op jit(solution)/shard_map/ppermute | solution.py:537
  83.8 0.7 collective-permute-start.19
  84.5 0.6 last_bias.1
  85.1 0.7 collective-permute-start.20
  85.8 3.1 %collective-permute-done.20.refs_5_.refs_3_ = bf16[64,128]{1,0:T(8,128)(2,1)S(1)} collective-permute-done((bf16[64,128]{1,0:T(8,128)(2,1)S(1)}, bf16[64,128]{1,0:T(8,128)(2,1)S(1)}, u32[]{:S(2)}, u32[]{:S(2)}) %collective-permute-start.20) | collective-permute-done | bytes 16416 | tf_op jit(solution)/shard_map/ppermute | solution.py:537
  88.9 1.5 %pair_weight.1 = f32[32,8,128]{2,1,0:T(8,128)} custom-call(s32[2]{0:T(128)S(1)} %copy-done.14, bf16[16,128,128]{2,1,0:T(8,128)(2,1)S(1)} %copy-done.9, bf16[64,128]{1,0:T(8,128)(2,1)S(1)} %get-tuple-element.125.refs_2_.refs_4_, bf16[64,128]{1,0:T(8,128)(2,1)S(1)} %collective-permute-done.20.refs_5_.refs_3_, ...), custom_call_target="tpu_custom_call" | custom-call | flops 67108864 | bytes 688136 | tf_op jit(solution)/shard_map/pair_weight/pallas_call | solution.py:79
  90.3 3.9 %all-to-all-start = ((f32[32,8,128]{2,1,0:T(8,128)}), f32[32,8,128]{2,1,0:T(8,128)S(1)}, u32[]{:S(2)}, u32[]{:S(2)}) async-start(f32[32,8,128]{2,1,0:T(8,128)} %pair_weight.1), calls=%async_computation | async-start | bytes 262144 | tf_op jit(solution)/shard_map/all_to_all | solution.py:541
  94.2 0.6 far.1
  94.8 2.4 %collective-permute-start.21 = (bf16[27,16,128]{2,1,0:T(8,128)(2,1)S(1)}, bf16[27,16,128]{2,1,0:T(8,128)(2,1)S(1)}, u32[]{:S(2)}, u32[]{:S(2)}) collective-permute-start(bf16[27,16,128]{2,1,0:T(8,128)(2,1)S(1)} %get-tuple-element.121), channel_id=1, source_target_pairs={{0,16},{2,18},{4,20},{6,22},{8,24},{10,26},{12,28},{14,30},{16,0},... | collective-permute-start | bytes 331784 | tf_op jit(solution)/shard_map/ppermute | solution.py:532
  97.3 0.6 collective-permute-start.22
  97.8 2.9 %pair.1 = bf16[2048,128]{1,0:T(8,128)(2,1)} custom-call(s32[2]{0:T(128)S(1)} %copy-done.14, bf16[2048,128]{1,0:T(8,128)(2,1)S(1)} %bitcast.19, f32[1,128]{1,0:T(1,128)S(1)} %bitcast.26, bf16[8,128]{1,0:T(8,128)(2,1)S(1)} %bitcast.24, bf16[64,128]{1,0:T(8,128)(2,1)S(1)} %get-tuple-element.125.refs_2_.refs_4_, ...), custom_call_target="tpu_custom_call" | custom-call | flops 67108864 | bytes 1083912 | tf_op jit(solution)/shard_map/pair/pallas_call | solution.py:79
  100.8 0.2 collective-permute-done.22.refs_5_
  101.0 4.3 %collective-permute-done.21.refs_1_ = bf16[27,16,128]{2,1,0:T(8,128)(2,1)S(1)} collective-permute-done((bf16[27,16,128]{2,1,0:T(8,128)(2,1)S(1)}, bf16[27,16,128]{2,1,0:T(8,128)(2,1)S(1)}, u32[]{:S(2)}, u32[]{:S(2)}) %collective-permute-start.21) | collective-permute-done | bytes 110624 | tf_op jit(solution)/shard_map/ppermute | solution.py:532
  105.2 0.7 close.1
  (50 shorter events, 0.1 us)
Async XLA Ops:
  0.6 17.8 %copy-start.4 = (bf16[768,768]{1,0:T(8,128)(2,1)S(1)}, bf16[768,768]{1,0:T(8,128)(2,1)}, u32[]{:S(2)}) copy-start(bf16[768,768]{1,0:T(8,128)(2,1)} %refs_1_.3) | copy-start | bytes 3538948
  5.4 10.7 %collective-permute-start.3 = (bf16[128,768]{1,0:T(8,128)(2,1)}, bf16[128,768]{1,0:T(8,128)(2,1)S(1)}, u32[]{:S(2)}, u32[]{:S(2)}) collective-permute-start(bf16[128,768]{1,0:T(8,128)(2,1)} %get-tuple-element.75.refs_2_), channel_id=1, source_target_pairs={{0,1},{1,0},{2,3},{3,2},{4,5},{5,4},{6,7},{7,6},{8,9},{9,8},{10,11... | collective-permute-start | bytes 589832 | tf_op jit(solution)/shard_map/ppermute | solution.py:537
  5.5 4.7 %collective-permute-start = (bf16[2,64,128]{2,1,0:T(8,128)(2,1)}, bf16[2,64,128]{2,1,0:T(8,128)(2,1)S(1)}, u32[]{:S(2)}, u32[]{:S(2)}) collective-permute-start(bf16[2,64,128]{2,1,0:T(8,128)(2,1)} %get-tuple-element.74.refs_0_), channel_id=1, source_target_pairs={{0,8},{2,10},{4,12},{6,14},{8,0},{10,2},{12,4},{14,6},{16,24},{18,... | collective-permute-start | bytes 98312 | tf_op jit(solution)/shard_map/ppermute | solution.py:532
  7.6 5.3 %collective-permute-start.1 = (bf16[2,64,128]{2,1,0:T(8,128)(2,1)}, bf16[2,64,128]{2,1,0:T(8,128)(2,1)S(1)}, u32[]{:S(2)}, u32[]{:S(2)}) collective-permute-start(bf16[2,64,128]{2,1,0:T(8,128)(2,1)} %get-tuple-element.74.refs_0_), channel_id=1, source_target_pairs={{0,16},{2,18},{4,20},{6,22},{8,24},{10,26},{12,28},{14,30},{16,0},... | collective-permute-start | bytes 98312 | tf_op jit(solution)/shard_map/ppermute | solution.py:532
  10.2 5.9 %collective-permute-start.2 = (bf16[2,64,128]{2,1,0:T(8,128)(2,1)}, bf16[2,64,128]{2,1,0:T(8,128)(2,1)S(1)}, u32[]{:S(2)}, u32[]{:S(2)}) collective-permute-start(bf16[2,64,128]{2,1,0:T(8,128)(2,1)} %get-tuple-element.74.refs_0_), channel_id=1, source_target_pairs={{0,24},{2,26},{4,28},{6,30},{8,16},{10,18},{12,20},{14,22},{16,8},... | collective-permute-start | bytes 98312 | tf_op jit(solution)/shard_map/ppermute | solution.py:532
  16.1 0.8 copy-start.15
  16.9 5.5 %collective-permute-start.4 = (bf16[4,64,128]{2,1,0:T(8,128)(2,1)S(1)}, bf16[4,64,128]{2,1,0:T(8,128)(2,1)S(1)}, u32[]{:S(2)}, u32[]{:S(2)}) collective-permute-start(bf16[4,64,128]{2,1,0:T(8,128)(2,1)S(1)} %get-tuple-element.80), channel_id=1, source_target_pairs={{0,1},{1,0},{2,3},{3,2},{4,5},{5,4},{6,7},{7,6},{8,9},{9,8},{10,11... | collective-permute-start | bytes 196616 | tf_op jit(solution)/shard_map/ppermute | solution.py:537
  18.4 1.3 %copy-start.5 = (bf16[768,768]{1,0:T(8,128)(2,1)S(1)}, bf16[768,768]{1,0:T(8,128)(2,1)}, u32[]{:S(2)}) copy-start(bf16[768,768]{1,0:T(8,128)(2,1)} %refs_2_.3) | copy-start | bytes 3538948
  19.7 1.3 %copy-start.6 = (bf16[768,768]{1,0:T(8,128)(2,1)S(1)}, bf16[768,768]{1,0:T(8,128)(2,1)}, u32[]{:S(2)}) copy-start(bf16[768,768]{1,0:T(8,128)(2,1)} %refs_3_.1) | copy-start | bytes 3538948
  21.0 0.7 copy-start.13
  21.6 7.6 %copy-start.12 = (f32[256,128]{1,0:T(8,128)S(1)}, f32[256,128]{1,0:T(8,128)}, u32[]{:S(2)}) copy-start(f32[256,128]{1,0:T(8,128)} %get-tuple-element.81.refs_6_) | copy-start | bytes 393220
  22.4 1.7 %copy-start.11 = (bf16[128,768]{1,0:T(8,128)(2,1)S(1)}, bf16[128,768]{1,0:T(8,128)(2,1)}, u32[]{:S(2)}) copy-start(bf16[128,768]{1,0:T(8,128)(2,1)} %get-tuple-element.75.refs_2_) | copy-start | bytes 589828
  22.4 9.5 %copy-start.2 = (bf16[1536,768]{1,0:T(8,128)(2,1)S(1)}, bf16[1536,768]{1,0:T(8,128)(2,1)}, u32[]{:S(2)}) copy-start(bf16[1536,768]{1,0:T(8,128)(2,1)} %refs_1_.2) | copy-start | bytes 7077892
  22.4 6.7 %copy-start.14 = (s32[2]{0:T(128)S(1)}, s32[2]{0:T(128)}, u32[]{:S(2)}) copy-start(s32[2]{0:T(128)} %pad_add_fusion.refs_0_) | copy-start | bytes 28
  22.5 6.7 %copy-start.18 = (f32[1,256]{1,0:T(1,128)S(1)}, f32[1,256]{1,0:T(1,128)}, u32[]{:S(2)}) copy-start(f32[1,256]{1,0:T(1,128)} %get-tuple-element.82.refs_7_) | copy-start | bytes 3076
  22.5 9.5 %copy-start.20 = (f32[768]{0:T(1024)S(1)}, f32[768]{0:T(1024)}, u32[]{:S(2)}) copy-start(f32[768]{0:T(1024)} %param.29) | copy-start | bytes 9220
  22.5 9.5 %copy-start.8 = (bf16[1,128,768]{2,1,0:T(8,128)(2,1)S(1)}, bf16[1,128,768]{2,1,0:T(8,128)(2,1)}, u32[]{:S(2)}) copy-start(bf16[1,128,768]{2,1,0:T(8,128)(2,1)} %param.20) | copy-start | bytes 589828
  22.5 9.5 %copy-start.10 = (bf16[1,128,768]{2,1,0:T(8,128)(2,1)S(1)}, bf16[1,128,768]{2,1,0:T(8,128)(2,1)}, u32[]{:S(2)}) copy-start(bf16[1,128,768]{2,1,0:T(8,128)(2,1)} %param.39) | copy-start | bytes 589828
  22.5 5.0 %collective-permute-start.5 = (bf16[2,4,64,128]{3,2,1,0:T(8,128)(2,1)S(1)}, bf16[2,4,64,128]{3,2,1,0:T(8,128)(2,1)S(1)}, u32[]{:S(2)}, u32[]{:S(2)}) collective-permute-start(bf16[2,4,64,128]{3,2,1,0:T(8,128)(2,1)S(1)} %join_tok.1.refs_0_), channel_id=1, source_target_pairs={{0,4},{2,6},{4,0},{6,2},{8,12},{10,14},{12,8},{14,10},{16,20},{18,... | collective-permute-start | bytes 393224 | tf_op jit(solution)/shard_map/ppermute | solution.py:532
  24.1 12.1 %copy-start.7 = (bf16[768,768]{1,0:T(8,128)(2,1)S(1)}, bf16[768,768]{1,0:T(8,128)(2,1)}, u32[]{:S(2)}) copy-start(bf16[768,768]{1,0:T(8,128)(2,1)} %refs_7_.1) | copy-start | bytes 3538948
  27.5 8.7 %copy-start.1 = (bf16[768,1536]{1,0:T(8,128)(2,1)S(1)}, bf16[768,1536]{1,0:T(8,128)(2,1)}, u32[]{:S(2)}) copy-start(bf16[768,1536]{1,0:T(8,128)(2,1)} %refs_9_.1) | copy-start | bytes 7077892
  27.6 1.6 %collective-permute-start.6 = (bf16[2,2,4,64,128]{4,3,2,1,0:T(8,128)(2,1)S(1)}, bf16[2,2,4,64,128]{4,3,2,1,0:T(8,128)(2,1)S(1)}, u32[]{:S(2)}, u32[]{:S(2)}) collective-permute-start(bf16[2,2,4,64,128]{4,3,2,1,0:T(8,128)(2,1)S(1)} %join_y.1.refs_4_), channel_id=1, source_target_pairs={{0,2},{2,0},{4,6},{6,4},{8,10},{10,8},{12,14},{14,12},{16,18},{18,... | collective-permute-start | bytes 786440 | tf_op jit(solution)/shard_map/ppermute | solution.py:532
  29.2 7.1 %copy-start = (bf16[768,1536]{1,0:T(8,128)(2,1)S(1)}, bf16[768,1536]{1,0:T(8,128)(2,1)}, u32[]{:S(2)}) copy-start(bf16[768,1536]{1,0:T(8,128)(2,1)} %refs_8_.1) | copy-start | bytes 7077892
  31.3 4.9 %collective-permute-start.7 = (bf16[128,384]{1,0:T(8,128)(2,1)S(1)}, bf16[128,384]{1,0:T(8,128)(2,1)S(1)}, u32[]{:S(2)}, u32[]{:S(2)}) collective-permute-start(bf16[128,384]{1,0:T(8,128)(2,1)S(1)} %get-tuple-element.84), channel_id=1, source_target_pairs={{0,1},{1,0},{2,3},{3,2},{4,5},{5,4},{6,7},{7,6},{8,9},{9,8},{10,11... | collective-permute-start | bytes 294920 | tf_op jit(solution)/shard_map/ppermute | solution.py:537
  40.6 4.7 %collective-permute-start.8 = (bf16[384,128]{1,0:T(8,128)(2,1)S(1)}, bf16[384,128]{1,0:T(8,128)(2,1)S(1)}, u32[]{:S(2)}, u32[]{:S(2)}) collective-permute-start(bf16[384,128]{1,0:T(8,128)(2,1)S(1)} %get-tuple-element.89), channel_id=1, source_target_pairs={{0,1},{1,0},{2,3},{3,2},{4,5},{5,4},{6,7},{7,6},{8,9},{9,8},{10,11... | collective-permute-start | bytes 294920 | tf_op jit(solution)/shard_map/ppermute | solution.py:537
  47.3 7.3 %collective-permute-start.11 = (bf16[64,16,128]{2,1,0:T(8,128)(2,1)S(1)}, bf16[64,16,128]{2,1,0:T(8,128)(2,1)S(1)}, u32[]{:S(2)}, u32[]{:S(2)}) collective-permute-start(bf16[64,16,128]{2,1,0:T(8,128)(2,1)S(1)} %get-tuple-element.102), channel_id=1, source_target_pairs={{0,4},{2,6},{4,0},{6,2},{8,12},{10,14},{12,8},{14,10},{16,20},{18,... | collective-permute-start | bytes 786440 | tf_op jit(solution)/shard_map/ppermute | solution.py:532
  48.9 5.7 %collective-permute-start.12 = (bf16[128,768]{1,0:T(8,128)(2,1)S(1)}, bf16[128,768]{1,0:T(8,128)(2,1)S(1)}, u32[]{:S(2)}, u32[]{:S(2)}) collective-permute-start(bf16[128,768]{1,0:T(8,128)(2,1)S(1)} %get-tuple-element.103.refs_5_), channel_id=1, source_target_pairs={{0,1},{1,0},{2,3},{3,2},{4,5},{5,4},{6,7},{7,6},{8,9},{9,8},{10,11... | collective-permute-start | bytes 589832 | tf_op jit(solution)/shard_map/ppermute | solution.py:537
  51.7 6.1 %collective-permute-start.10 = (bf16[216,16,128]{2,1,0:T(8,128)(2,1)S(1)}, bf16[216,16,128]{2,1,0:T(8,128)(2,1)S(1)}, u32[]{:S(2)}, u32[]{:S(2)}) collective-permute-start(bf16[216,16,128]{2,1,0:T(8,128)(2,1)S(1)} %get-tuple-element.98), channel_id=1, source_target_pairs={{0,2},{2,0},{4,6},{6,4},{8,10},{10,8},{12,14},{14,12},{16,18},{18,... | collective-permute-start | bytes 2654216 | tf_op jit(solution)/shard_map/ppermute | solution.py:532
  55.7 2.1 %collective-permute-start.13 = (bf16[152,16,128]{2,1,0:T(8,128)(2,1)S(1)}, bf16[152,16,128]{2,1,0:T(8,128)(2,1)S(1)}, u32[]{:S(2)}, u32[]{:S(2)}) collective-permute-start(bf16[152,16,128]{2,1,0:T(8,128)(2,1)S(1)} %get-tuple-element.105), channel_id=1, source_target_pairs={{0,2},{2,0},{4,6},{6,4},{8,10},{10,8},{12,14},{14,12},{16,18},{18,... | collective-permute-start | bytes 1867784 | tf_op jit(solution)/shard_map/ppermute | solution.py:532
  57.8 15.4 %copy-start.19 = (f32[768]{0:T(1024)S(1)}, f32[768]{0:T(1024)}, u32[]{:S(2)}) copy-start(f32[768]{0:T(1024)} %refs_5_.1) | copy-start | bytes 9220
  58.7 12.3 %collective-permute-start.14 = (bf16[108,16,128]{2,1,0:T(8,128)(2,1)S(1)}, bf16[108,16,128]{2,1,0:T(8,128)(2,1)S(1)}, u32[]{:S(2)}, u32[]{:S(2)}) collective-permute-start(bf16[108,16,128]{2,1,0:T(8,128)(2,1)S(1)} %get-tuple-element.107), channel_id=1, source_target_pairs={{0,4},{2,6},{4,0},{6,2},{8,12},{10,14},{12,8},{14,10},{16,20},{18,... | collective-permute-start | bytes 1327112 | tf_op jit(solution)/shard_map/ppermute | solution.py:532
  59.4 9.1 %collective-permute-start.15 = (bf16[76,16,128]{2,1,0:T(8,128)(2,1)S(1)}, bf16[76,16,128]{2,1,0:T(8,128)(2,1)S(1)}, u32[]{:S(2)}, u32[]{:S(2)}) collective-permute-start(bf16[76,16,128]{2,1,0:T(8,128)(2,1)S(1)} %get-tuple-element.109), channel_id=1, source_target_pairs={{0,8},{2,10},{4,12},{6,14},{8,0},{10,2},{12,4},{14,6},{16,24},{18,... | collective-permute-start | bytes 933896 | tf_op jit(solution)/shard_map/ppermute | solution.py:532
  71.0 17.9 %copy-start.9 = (bf16[16,128,128]{2,1,0:T(8,128)(2,1)S(1)}, bf16[16,128,128]{2,1,0:T(8,128)(2,1)}, u32[]{:S(2)}) copy-start(bf16[16,128,128]{2,1,0:T(8,128)(2,1)} %get-tuple-element.124.refs_1_) | copy-start | bytes 1572868
  71.7 10.0 %collective-permute-start.16 = (bf16[54,16,128]{2,1,0:T(8,128)(2,1)S(1)}, bf16[54,16,128]{2,1,0:T(8,128)(2,1)S(1)}, u32[]{:S(2)}, u32[]{:S(2)}) collective-permute-start(bf16[54,16,128]{2,1,0:T(8,128)(2,1)S(1)} %get-tuple-element.111), channel_id=1, source_target_pairs={{0,8},{2,10},{4,12},{6,14},{8,0},{10,2},{12,4},{14,6},{16,24},{18,... | collective-permute-start | bytes 663560 | tf_op jit(solution)/shard_map/ppermute | solution.py:532
  71.8 6.2 %collective-permute-start.9 = (bf16[768,128]{1,0:T(8,128)(2,1)S(1)}, bf16[768,128]{1,0:T(8,128)(2,1)S(1)}, u32[]{:S(2)}, u32[]{:S(2)}) collective-permute-start(bf16[768,128]{1,0:T(8,128)(2,1)S(1)} %get-tuple-element.95), channel_id=1, source_target_pairs={{0,1},{1,0},{2,3},{3,2},{4,5},{5,4},{6,7},{7,6},{8,9},{9,8},{10,11... | collective-permute-start | bytes 589832 | tf_op jit(solution)/shard_map/ppermute | solution.py:537
  72.4 9.3 %collective-permute-start.17 = (bf16[38,16,128]{2,1,0:T(8,128)(2,1)S(1)}, bf16[38,16,128]{2,1,0:T(8,128)(2,1)S(1)}, u32[]{:S(2)}, u32[]{:S(2)}) collective-permute-start(bf16[38,16,128]{2,1,0:T(8,128)(2,1)S(1)} %get-tuple-element.113), channel_id=1, source_target_pairs={{0,16},{2,18},{4,20},{6,22},{8,24},{10,26},{12,28},{14,30},{16,0},... | collective-permute-start | bytes 466952 | tf_op jit(solution)/shard_map/ppermute | solution.py:532
  77.9 19.9 %copy-start.3 = (bf16[128,16,128]{2,1,0:T(8,128)(2,1)S(1)}, bf16[128,16,128]{2,1,0:T(8,128)(2,1)}, u32[]{:S(2)}) copy-start(bf16[128,16,128]{2,1,0:T(8,128)(2,1)} %param.22) | copy-start | bytes 1572868
  78.0 19.9 %copy-start.16 = (bf16[128,8]{0,1:T(8,128)(2,1)S(1)}, bf16[128,8]{0,1:T(8,128)(2,1)}, u32[]{:S(2)}) copy-start(bf16[128,8]{0,1:T(8,128)(2,1)} %param.34) | copy-start | bytes 6148
  78.0 19.9 %copy-start.17 = (f32[128]{0:T(128)S(1)}, f32[128]{0:T(128)}, u32[]{:S(2)}) copy-start(f32[128]{0:T(128)} %param.28) | copy-start | bytes 1540
  82.4 6.5 %collective-permute-start.18 = (bf16[27,16,128]{2,1,0:T(8,128)(2,1)S(1)}, bf16[27,16,128]{2,1,0:T(8,128)(2,1)S(1)}, u32[]{:S(2)}, u32[]{:S(2)}) collective-permute-start(bf16[27,16,128]{2,1,0:T(8,128)(2,1)S(1)} %get-tuple-element.116), channel_id=1, source_target_pairs={{0,1},{1,0},{2,3},{3,2},{4,5},{5,4},{6,7},{7,6},{8,9},{9,8},{10,11... | collective-permute-start | bytes 331784 | tf_op jit(solution)/shard_map/ppermute | solution.py:537
  83.8 5.1 %collective-permute-start.19 = (bf16[15,16,128]{2,1,0:T(8,128)(2,1)S(1)}, bf16[15,16,128]{2,1,0:T(8,128)(2,1)S(1)}, u32[]{:S(2)}, u32[]{:S(2)}) collective-permute-start(bf16[15,16,128]{2,1,0:T(8,128)(2,1)S(1)} %get-tuple-element.118), channel_id=1, source_target_pairs={{0,4},{2,6},{4,0},{6,2},{8,12},{10,14},{12,8},{14,10},{16,20},{18,... | collective-permute-start | bytes 184328 | tf_op jit(solution)/shard_map/ppermute | solution.py:532
  85.1 3.8 %collective-permute-start.20 = (bf16[64,128]{1,0:T(8,128)(2,1)S(1)}, bf16[64,128]{1,0:T(8,128)(2,1)S(1)}, u32[]{:S(2)}, u32[]{:S(2)}) collective-permute-start(bf16[64,128]{1,0:T(8,128)(2,1)S(1)} %get-tuple-element.119), channel_id=1, source_target_pairs={{0,1},{1,0},{2,3},{3,2},{4,5},{5,4},{6,7},{7,6},{8,9},{9,8},{10,11... | collective-permute-start | bytes 49160 | tf_op jit(solution)/shard_map/ppermute | solution.py:537
  90.3 14.9 %all-to-all-start = ((f32[32,8,128]{2,1,0:T(8,128)}), f32[32,8,128]{2,1,0:T(8,128)S(1)}, u32[]{:S(2)}, u32[]{:S(2)}) async-start(f32[32,8,128]{2,1,0:T(8,128)} %pair_weight.1), calls=%async_computation | async-start | bytes 262144 | tf_op jit(solution)/shard_map/all_to_all | solution.py:541
  94.8 10.4 %collective-permute-start.21 = (bf16[27,16,128]{2,1,0:T(8,128)(2,1)S(1)}, bf16[27,16,128]{2,1,0:T(8,128)(2,1)S(1)}, u32[]{:S(2)}, u32[]{:S(2)}) collective-permute-start(bf16[27,16,128]{2,1,0:T(8,128)(2,1)S(1)} %get-tuple-element.121), channel_id=1, source_target_pairs={{0,16},{2,18},{4,20},{6,22},{8,24},{10,26},{12,28},{14,30},{16,0},... | collective-permute-start | bytes 331784 | tf_op jit(solution)/shard_map/ppermute | solution.py:532
  97.3 3.7 %collective-permute-start.22 = (bf16[3,16,128]{2,1,0:T(8,128)(2,1)S(1)}, bf16[3,16,128]{2,1,0:T(8,128)(2,1)S(1)}, u32[]{:S(2)}, u32[]{:S(2)}) collective-permute-start(bf16[3,16,128]{2,1,0:T(8,128)(2,1)S(1)} %get-tuple-element.123), channel_id=1, source_target_pairs={{0,1},{1,0},{2,3},{3,2},{4,5},{5,4},{6,7},{7,6},{8,9},{9,8},{10,11... | collective-permute-start | bytes 36872 | tf_op jit(solution)/shard_map/ppermute | solution.py:537

commit v15 on v14

--- a/solution.py
+++ b/solution.py
@@ -479,9 +479,10 @@
     outs[3][...] = total
 
 
-def exit_kernel(toks, noisy, gain, d_res, d_own, *rest):
-    others, (grad_noisy, token) = rest[: toks - 1], rest[toks - 1 :]
+def exit_kernel(toks, noisy, gain, d_res, d_own, columns, *rest):
+    others, (grad_noisy, token, columns_out) = rest[: toks - 1], rest[toks - 1 :]
     token[...] = jnp.zeros(token.shape, f32)
+    columns_out[...] = columns[...]
     total = d_own[...]
     for part in others:
         total = total + part[...].astype(f32)
@@ -741,11 +742,11 @@
     )
     got_b = swap_copy(sent_b, 1)
 
-    grad_noisy, exited = call(
+    grad_noisy, exited, columns = call(
         functools.partial(exit_kernel, toks),
         "exit",
-        [noisy3, norm_gain2, d_res, d_own] + d_others,
-        [((rows, width), bf16), ((8, 128), f32)],
+        [noisy3, norm_gain2, d_res, d_own, columns] + d_others,
+        [((rows, width), bf16), ((8, 128), f32), (columns.shape, bf16)],
     )
     pairs = [(kept, got), (kept_b, got_b)]
     parts = copies // 2
@@ -761,7 +762,7 @@
             bias_ready = pairs[1]
             if toks == 2:
                 break
-        pairs = step("step_%d" % n, pairs, segments, deps=[exited] if n == 2 else ())
+        pairs = step("step_%d" % n, pairs, segments, deps=[exited] if n == 1 else ())
         parts //= 2
     if toks == 2:
         kept, sent, kept_b, sent_b = call(
@@ -769,7 +770,6 @@
             "across",
             [where_am_i] + [array for one in pairs for array in one],
             [((first_tiles, 16, 128), bf16)] * 2 + [((second_tiles, 16, 128), bf16)] * 2,
-            deps=[exited],
         )
         pairs = [(kept, swap_tok(sent, 1)), (kept_b, swap_copy(sent_b, masks_b[-1]))]
     bias_pieces = call(
@@ -794,6 +794,7 @@
         )
         pairs[0] = (kept, swap_copy(sent, copies // 2))
         single_pair = (single_kept, swap_tok(single_sent, 1))
+        ready = [pairs[0][1], single_pair[1]]
 
     group = copies // toks
     swaps = []

time: 108 us -> 111 us (1.028)
  the two profiles are of different devices: /device:TPU:2 before, /device:TPU:0 now
where the time goes in v15:
time: 111 us; the launch traced here: 110 us
  waiting for transfers between devices  49.5 us (45%)
  Pallas kernels  28.8 us (26%)
  starting transfers between devices  26.4 us (24%)
  local copies, waits for them, and re-layouts  4.05 us (4%)
    pallas_call x21, Pallas kernels, call(): pl.pallas_call(whole, name=name, out_shape=[jax.ShapeDtypeStruct(one[0],...  28.8 us
    ppermute x14, waiting for transfers between devices, swap_copy(): return lax.ppermute(value, 'copy', [(i, i ^ mask) for i in range(size)])  24.9 us
    ppermute x9, waiting for transfers between devices, swap_tok(): return lax.ppermute(value, 'tok', [(i, i ^ mask) for i in range(size)])  18.9 us
    ppermute x9, starting transfers between devices, swap_tok(): return lax.ppermute(value, 'tok', [(i, i ^ mask) for i in range(size)])  12.4 us
    ppermute x14, starting transfers between devices, swap_copy(): return lax.ppermute(value, 'copy', [(i, i ^ mask) for i in range(size)])  11.5 us
    all_to_all x1, waiting for transfers between devices, exchange(): return lax.all_to_all(value, ('copy', 'tok'), 0, 0)  5.67 us
    unnamed x42, local copies, waits for them, and re-layouts  4.04 us
    all_to_all x1, starting transfers between devices, exchange(): return lax.all_to_all(value, ('copy', 'tok'), 0, 0)  2.57 us
  transfers between devices with their start and end apart: 24, of which 17 were waited for; matrix products, arithmetic and copies ran while one was open for 0% of the time, Pallas kernels for 10%

profile of v15, /device:TPU:0, one launch (start us, length us, event | category | flops | bytes accessed | tf_op | source)
XLA Modules:
  0.0 110.4 jit_solution(11976611887277498158)
XLA Ops:
  0.6 0.6 pad_add_fusion.refs_0_
  1.2 4.2 %enter.1 = (bf16[128,768]{1,0:T(8,128)(2,1)}, bf16[16,128,128]{2,1,0:T(8,128)(2,1)}, f32[256,128]{1,0:T(8,128)}, f32[1,256]{1,0:T(1,128)}, bf16[2,64,128]{2,1,0:T(8,128)(2,1)}) custom-call(s32[2]{0:T(128)} %pad_add_fusion.refs_0_, bf16[128,768]{1,0:T(8,128)(2,1)} %bitcast.20, bf16[128,768]{1,0:T(8,128)(2,1)} %refs_2_.2, s32[1,128]{1,0:T(1,128)} %bitcast.30, ...), custom_call_target="tpu_custom_call" | custom-call | flops 67108864 | bytes 1860808 | tf_op jit(solution)/shard_map/enter/pallas_call | solution.py:79
  5.4 3.0 %collective-permute-start.3 = (bf16[128,768]{1,0:T(8,128)(2,1)}, bf16[128,768]{1,0:T(8,128)(2,1)S(1)}, u32[]{:S(2)}, u32[]{:S(2)}) collective-permute-start(bf16[128,768]{1,0:T(8,128)(2,1)} %get-tuple-element.76.refs_2_), channel_id=1, source_target_pairs={{0,1},{1,0},{2,3},{3,2},{4,5},{5,4},{6,7},{7,6},{8,9},{9,8},{10,11... | collective-permute-start | bytes 589832 | tf_op jit(solution)/shard_map/ppermute | solution.py:538
  8.4 1.6 %collective-permute-start = (bf16[2,64,128]{2,1,0:T(8,128)(2,1)}, bf16[2,64,128]{2,1,0:T(8,128)(2,1)S(1)}, u32[]{:S(2)}, u32[]{:S(2)}) collective-permute-start(bf16[2,64,128]{2,1,0:T(8,128)(2,1)} %get-tuple-element.75.refs_0_), channel_id=1, source_target_pairs={{0,8},{2,10},{4,12},{6,14},{8,0},{10,2},{12,4},{14,6},{16,24},{18,... | collective-permute-start | bytes 98312 | tf_op jit(solution)/shard_map/ppermute | solution.py:533
  10.0 2.6 %collective-permute-start.1 = (bf16[2,64,128]{2,1,0:T(8,128)(2,1)}, bf16[2,64,128]{2,1,0:T(8,128)(2,1)S(1)}, u32[]{:S(2)}, u32[]{:S(2)}) collective-permute-start(bf16[2,64,128]{2,1,0:T(8,128)(2,1)} %get-tuple-element.75.refs_0_), channel_id=1, source_target_pairs={{0,16},{2,18},{4,20},{6,22},{8,24},{10,26},{12,28},{14,30},{16,0},... | collective-permute-start | bytes 98312 | tf_op jit(solution)/shard_map/ppermute | solution.py:533
  12.6 0.2 collective-permute-start.2
  12.8 2.5 %collective-permute-done.1.refs_2_ = bf16[2,64,128]{2,1,0:T(8,128)(2,1)S(1)} collective-permute-done((bf16[2,64,128]{2,1,0:T(8,128)(2,1)}, bf16[2,64,128]{2,1,0:T(8,128)(2,1)S(1)}, u32[]{:S(2)}, u32[]{:S(2)}) %collective-permute-start.1) | collective-permute-done | bytes 32800 | tf_op jit(solution)/shard_map/ppermute | solution.py:533
  15.3 3.2 %collective-permute-done.2.refs_3_ = bf16[2,64,128]{2,1,0:T(8,128)(2,1)S(1)} collective-permute-done((bf16[2,64,128]{2,1,0:T(8,128)(2,1)}, bf16[2,64,128]{2,1,0:T(8,128)(2,1)S(1)}, u32[]{:S(2)}, u32[]{:S(2)}) %collective-permute-start.2) | collective-permute-done | bytes 32800 | tf_op jit(solution)/shard_map/ppermute | solution.py:533
  18.5 0.8 copy-done.15
  19.3 0.6 collective-permute-start.4
  19.9 1.3 %copy-done.5 = bf16[768,768]{1,0:T(8,128)(2,1)S(1)} copy-done((bf16[768,768]{1,0:T(8,128)(2,1)S(1)}, bf16[768,768]{1,0:T(8,128)(2,1)}, u32[]{:S(2)}) %copy-start.5) | copy-done | bytes 1179672
  21.1 1.3 %copy-done.6 = bf16[768,768]{1,0:T(8,128)(2,1)S(1)} copy-done((bf16[768,768]{1,0:T(8,128)(2,1)S(1)}, bf16[768,768]{1,0:T(8,128)(2,1)}, u32[]{:S(2)}) %copy-start.6) | copy-done | bytes 1179672
  22.4 0.7 copy-done.13
  23.1 0.8 stage.1.refs_1_.refs_2_
  23.9 0.0 copy-start.2
  24.0 1.6 %collective-permute-start.5 = (bf16[2,4,64,128]{3,2,1,0:T(8,128)(2,1)S(1)}, bf16[2,4,64,128]{3,2,1,0:T(8,128)(2,1)S(1)}, u32[]{:S(2)}, u32[]{:S(2)}) collective-permute-start(bf16[2,4,64,128]{3,2,1,0:T(8,128)(2,1)S(1)} %join_tok.1.refs_0_), channel_id=1, source_target_pairs={{0,4},{2,6},{4,0},{6,2},{8,12},{10,14},{12,8},{14,10},{16,20},{18,... | collective-permute-start | bytes 393224 | tf_op jit(solution)/shard_map/ppermute | solution.py:533
  25.6 1.4 %project.1 = (bf16[256,768]{1,0:T(8,128)(2,1)S(1)}, bf16[384,256]{1,0:T(8,128)(2,1)S(1)}, bf16[384,256]{1,0:T(8,128)(2,1)S(1)}, bf16[384,256]{1,0:T(8,128)(2,1)S(1)}) custom-call(s32[2]{0:T(128)S(1)} %copy-done.13, bf16[3,768,384]{2,1,0:T(8,128)(2,1)S(1)} %stage.1.refs_1_.refs_2_, bf16[128,768]{1,0:T(8,128)(2,1)S(1)} %copy-done.11, ...), custom_call_target="tpu_custom_call" | custom-call | flops 452984832 | bytes 3145736 | tf_op jit(solution)/shard_map/project/pallas_call | solution.py:79
  27.0 2.0 %collective-permute-done.5.refs_1_ = bf16[2,4,64,128]{3,2,1,0:T(8,128)(2,1)S(1)} collective-permute-done((bf16[2,4,64,128]{3,2,1,0:T(8,128)(2,1)S(1)}, bf16[2,4,64,128]{3,2,1,0:T(8,128)(2,1)S(1)}, u32[]{:S(2)}, u32[]{:S(2)}) %collective-permute-start.5) | collective-permute-done | bytes 131104 | tf_op jit(solution)/shard_map/ppermute | solution.py:533
  29.0 0.1 collective-permute-start.6
  29.1 1.5 %collective-permute-done.6.refs_5_ = bf16[2,2,4,64,128]{4,3,2,1,0:T(8,128)(2,1)S(1)} collective-permute-done((bf16[2,2,4,64,128]{4,3,2,1,0:T(8,128)(2,1)S(1)}, bf16[2,2,4,64,128]{4,3,2,1,0:T(8,128)(2,1)S(1)}, u32[]{:S(2)}, u32[]{:S(2)}) %collective-permute-start.6) | collective-permute-done | bytes 262176 | tf_op jit(solution)/shard_map/ppermute | solution.py:533
  30.6 2.1 %attention.1 = (bf16[4,256,256]{2,1,0:T(8,128)(2,1)S(1)}, bf16[256,384]{1,0:T(8,128)(2,1)S(1)}, bf16[128,384]{1,0:T(8,128)(2,1)S(1)}, bf16[128,384]{1,0:T(8,128)(2,1)S(1)}) custom-call(s32[2]{0:T(128)S(1)} %copy-done.14, bf16[384,256]{1,0:T(8,128)(2,1)S(1)} %get-tuple-element.78.refs_1_, bf16[384,256]{1,0:T(8,128)(2,1)S(1)} %get-tuple-element.79.refs_2_, ...), custom_call_target="tpu_custom_call" | custom-call | flops 100663296 | bytes 2163720 | tf_op jit(solution)/shard_map/attention/pallas_call | solution.py:79
  32.8 1.6 %collective-permute-start.7 = (bf16[128,384]{1,0:T(8,128)(2,1)S(1)}, bf16[128,384]{1,0:T(8,128)(2,1)S(1)}, u32[]{:S(2)}, u32[]{:S(2)}) collective-permute-start(bf16[128,384]{1,0:T(8,128)(2,1)S(1)} %get-tuple-element.85), channel_id=1, source_target_pairs={{0,1},{1,0},{2,3},{3,2},{4,5},{5,4},{6,7},{7,6},{8,9},{9,8},{10,11... | collective-permute-start | bytes 294920 | tf_op jit(solution)/shard_map/ppermute | solution.py:538
  34.4 0.9 down.1
  35.3 2.4 %collective-permute-done.7.refs_6_ = bf16[128,384]{1,0:T(8,128)(2,1)S(1)} collective-permute-done((bf16[128,384]{1,0:T(8,128)(2,1)S(1)}, bf16[128,384]{1,0:T(8,128)(2,1)S(1)}, u32[]{:S(2)}, u32[]{:S(2)}) %collective-permute-start.7) | collective-permute-done | bytes 98336 | tf_op jit(solution)/shard_map/ppermute | solution.py:538
  37.7 4.3 %hidden.1 = (f32[128,768]{1,0:T(8,128)S(1)}, bf16[128,768]{1,0:T(8,128)(2,1)S(1)}, bf16[384,128]{1,0:T(8,128)(2,1)S(1)}, bf16[384,128]{1,0:T(8,128)(2,1)S(1)}) custom-call(s32[2]{0:T(128)S(1)} %copy-done.14, bf16[128,768]{1,0:T(8,128)(2,1)S(1)} %get-tuple-element.71.refs_1_.refs_0_, bf16[128,768]{1,0:T(8,128)(2,1)S(1)} %get-tuple-element.72.refs_2_, ...), custom_call_target="tpu_custom_call" | custom-call | flops 1509949440 | bytes 8064008 | tf_op jit(solution)/shard_map/hidden/pallas_call | solution.py:79
  42.0 1.6 %collective-permute-start.8 = (bf16[384,128]{1,0:T(8,128)(2,1)S(1)}, bf16[384,128]{1,0:T(8,128)(2,1)S(1)}, u32[]{:S(2)}, u32[]{:S(2)}) collective-permute-start(bf16[384,128]{1,0:T(8,128)(2,1)S(1)} %get-tuple-element.90), channel_id=1, source_target_pairs={{0,1},{1,0},{2,3},{3,2},{4,5},{5,4},{6,7},{7,6},{8,9},{9,8},{10,11... | collective-permute-start | bytes 294920 | tf_op jit(solution)/shard_map/ppermute | solution.py:538
  43.6 3.1 %collective-permute-done.8.refs_6_ = bf16[384,128]{1,0:T(8,128)(2,1)S(1)} collective-permute-done((bf16[384,128]{1,0:T(8,128)(2,1)S(1)}, bf16[384,128]{1,0:T(8,128)(2,1)S(1)}, u32[]{:S(2)}, u32[]{:S(2)}) %collective-permute-start.8) | collective-permute-done | bytes 98336 | tf_op jit(solution)/shard_map/ppermute | solution.py:538
  46.7 2.0 %backward.1 = (bf16[384,256]{1,0:T(8,128)(2,1)S(1)}, bf16[384,256]{1,0:T(8,128)(2,1)S(1)}, bf16[384,256]{1,0:T(8,128)(2,1)S(1)}, bf16[64,16,128]{2,1,0:T(8,128)(...) custom-call(s32[2]{0:T(128)S(1)} %copy-done.14, ...), custom_call_target="tpu_custom_call" | custom-call | flops 201326592 | bytes 2818056 | tf_op jit(solution)/shard_map/backward/pallas_call | solution.py:79
  48.7 1.6 %collective-permute-start.11 = (bf16[64,16,128]{2,1,0:T(8,128)(2,1)S(1)}, bf16[64,16,128]{2,1,0:T(8,128)(2,1)S(1)}, u32[]{:S(2)}, u32[]{:S(2)}) collective-permute-start(bf16[64,16,128]{2,1,0:T(8,128)(2,1)S(1)} %get-tuple-element.104), channel_id=1, source_target_pairs={{0,4},{2,6},{4,0},{6,2},{8,12},{10,14},{12,8},{14,10},{16,20},{18,... | collective-permute-start | bytes 786440 | tf_op jit(solution)/shard_map/ppermute | solution.py:533
  50.3 1.5 %collective-permute-start.12 = (bf16[128,768]{1,0:T(8,128)(2,1)S(1)}, bf16[128,768]{1,0:T(8,128)(2,1)S(1)}, u32[]{:S(2)}, u32[]{:S(2)}) collective-permute-start(bf16[128,768]{1,0:T(8,128)(2,1)S(1)} %get-tuple-element.105.refs_5_), channel_id=1, source_target_pairs={{0,1},{1,0},{2,3},{3,2},{4,5},{5,4},{6,7},{7,6},{8,9},{9,8},{10,11... | collective-permute-start | bytes 589832 | tf_op jit(solution)/shard_map/ppermute | solution.py:538
  51.8 2.3 %first.1 = (bf16[216,16,128]{2,1,0:T(8,128)(2,1)S(1)}, bf16[216,16,128]{2,1,0:T(8,128)(2,1)S(1)}, f32[768,128]{1,0:T(8,128)S(1)}, f32[768,256]{1,0:T(8,128)S(1)}, bf16[768,128]{1,0:T(8,128)(2,1)S(1)}) custom-call(s32[2]{0:T(128)S(1)} %copy-done.14, bf16[3,768,384]{2,1,0:T(8,128)(2,1)S(1)} %stage.1.refs_1_.refs_2_, ...), custom_call_target="tpu_custom_call" | custom-call | flops 905969664 | bytes 5898248 | tf_op jit(solution)/shard_map/first/pallas_call | solution.py:79
  54.1 0.1 collective-permute-start.10
  54.2 1.8 %collective-permute-done.12.refs_6_ = bf16[128,768]{1,0:T(8,128)(2,1)S(1)} collective-permute-done((bf16[128,768]{1,0:T(8,128)(2,1)S(1)}, bf16[128,768]{1,0:T(8,128)(2,1)S(1)}, u32[]{:S(2)}, u32[]{:S(2)}) %collective-permute-start.12) | collective-permute-done | bytes 196640 | tf_op jit(solution)/shard_map/ppermute | solution.py:538
  56.0 1.1 second.1
  57.1 0.1 collective-permute-start.13
  57.2 2.0 %collective-permute-done.13.refs_4_ = bf16[152,16,128]{2,1,0:T(8,128)(2,1)S(1)} collective-permute-done((bf16[152,16,128]{2,1,0:T(8,128)(2,1)S(1)}, bf16[152,16,128]{2,1,0:T(8,128)(2,1)S(1)}, u32[]{:S(2)}, u32[]{:S(2)}) %collective-permute-start.13) | collective-permute-done | bytes 622624 | tf_op jit(solution)/shard_map/ppermute | solution.py:533
  59.2 0.9 step_0.1
  60.1 0.8 collective-permute-start.14
  60.9 1.5 %collective-permute-start.9 = (bf16[768,128]{1,0:T(8,128)(2,1)S(1)}, bf16[768,128]{1,0:T(8,128)(2,1)S(1)}, u32[]{:S(2)}, u32[]{:S(2)}) collective-permute-start(bf16[768,128]{1,0:T(8,128)(2,1)S(1)} %get-tuple-element.97), channel_id=1, source_target_pairs={{0,1},{1,0},{2,3},{3,2},{4,5},{5,4},{6,7},{7,6},{8,9},{9,8},{10,11... | collective-permute-start | bytes 589832 | tf_op jit(solution)/shard_map/ppermute | solution.py:538
  62.4 5.2 %collective-permute-done.9.refs_5_ = bf16[768,128]{1,0:T(8,128)(2,1)S(1)} collective-permute-done((bf16[768,128]{1,0:T(8,128)(2,1)S(1)}, bf16[768,128]{1,0:T(8,128)(2,1)S(1)}, u32[]{:S(2)}, u32[]{:S(2)}) %collective-permute-start.9) | collective-permute-done | bytes 196640 | tf_op jit(solution)/shard_map/ppermute | solution.py:538
  67.6 1.2 %exit.1 = (bf16[128,768]{1,0:T(8,128)(2,1)}, f32[8,128]{1,0:T(8,128)S(1)}, bf16[16,128,128]{2,1,0:T(8,128)(2,1)S(1)}) custom-call(bf16[128,768]{1,0:T(8,128)(2,1)S(1)} %get-tuple-element.71.refs_1_.refs_0_, f32[1,768]{1,0:T(1,128)S(1)} %reshape.49.refs_1_, f32[128,768]{1,0:T(8,128)S(1)} %get-tuple-element.86.refs_2_, ...), custom_call_target="tpu_custom_call" | custom-call | bytes 2432000 | tf_op jit(solution)/shard_map/exit/pallas_call | solution.py:79
  68.8 1.2 %collective-permute-done.15.refs_4_ = bf16[76,16,128]{2,1,0:T(8,128)(2,1)S(1)} collective-permute-done((bf16[76,16,128]{2,1,0:T(8,128)(2,1)S(1)}, bf16[76,16,128]{2,1,0:T(8,128)(2,1)S(1)}, u32[]{:S(2)}, u32[]{:S(2)}) %collective-permute-start.15) | collective-permute-done | bytes 311328 | tf_op jit(solution)/shard_map/ppermute | solution.py:533
  70.0 2.4 %collective-permute-done.14.refs_2_ = bf16[108,16,128]{2,1,0:T(8,128)(2,1)S(1)} collective-permute-done((bf16[108,16,128]{2,1,0:T(8,128)(2,1)S(1)}, bf16[108,16,128]{2,1,0:T(8,128)(2,1)S(1)}, u32[]{:S(2)}, u32[]{:S(2)}) %collective-permute-start.14) | collective-permute-done | bytes 442400 | tf_op jit(solution)/shard_map/ppermute | solution.py:533
  72.4 0.7 step_1.1
  73.2 0.1 collective-permute-start.16
  73.3 0.9 collective-permute-start.17
  74.2 8.8 %collective-permute-done.17.refs_4_.refs_2_ = bf16[38,16,128]{2,1,0:T(8,128)(2,1)S(1)} collective-permute-done((bf16[38,16,128]{2,1,0:T(8,128)(2,1)S(1)}, bf16[38,16,128]{2,1,0:T(8,128)(2,1)S(1)}, u32[]{:S(2)}, u32[]{:S(2)}) %collective-permute-start.17) | collective-permute-done | bytes 155680 | tf_op jit(solution)/shard_map/ppermute | solution.py:533
  82.9 0.3 collective-permute-done.16.refs_2_
  83.2 0.6 across.1
  83.9 1.6 %collective-permute-start.18 = (bf16[27,16,128]{2,1,0:T(8,128)(2,1)S(1)}, bf16[27,16,128]{2,1,0:T(8,128)(2,1)S(1)}, u32[]{:S(2)}, u32[]{:S(2)}) collective-permute-start(bf16[27,16,128]{2,1,0:T(8,128)(2,1)S(1)} %get-tuple-element.118), channel_id=1, source_target_pairs={{0,1},{1,0},{2,3},{3,2},{4,5},{5,4},{6,7},{7,6},{8,9},{9,8},{10,11... | collective-permute-start | bytes 331784 | tf_op jit(solution)/shard_map/ppermute | solution.py:538
  85.4 0.7 collective-permute-start.19
  86.1 0.6 last_bias.1
  86.7 0.6 collective-permute-start.20
  87.3 3.2 %collective-permute-done.20.refs_5_.refs_3_ = bf16[64,128]{1,0:T(8,128)(2,1)S(1)} collective-permute-done((bf16[64,128]{1,0:T(8,128)(2,1)S(1)}, bf16[64,128]{1,0:T(8,128)(2,1)S(1)}, u32[]{:S(2)}, u32[]{:S(2)}) %collective-permute-start.20) | collective-permute-done | bytes 16416 | tf_op jit(solution)/shard_map/ppermute | solution.py:538
  90.5 0.6 far.1
  91.1 1.3 %collective-permute-start.21 = (bf16[27,16,128]{2,1,0:T(8,128)(2,1)S(1)}, bf16[27,16,128]{2,1,0:T(8,128)(2,1)S(1)}, u32[]{:S(2)}, u32[]{:S(2)}) collective-permute-start(bf16[27,16,128]{2,1,0:T(8,128)(2,1)S(1)} %get-tuple-element.123), channel_id=1, source_target_pairs={{0,16},{2,18},{4,20},{6,22},{8,24},{10,26},{12,28},{14,30},{16,0},... | collective-permute-start | bytes 331784 | tf_op jit(solution)/shard_map/ppermute | solution.py:533
  92.3 0.5 collective-permute-start.22
  92.9 3.2 %collective-permute-done.22.refs_5_ = bf16[3,16,128]{2,1,0:T(8,128)(2,1)S(1)} collective-permute-done((bf16[3,16,128]{2,1,0:T(8,128)(2,1)S(1)}, bf16[3,16,128]{2,1,0:T(8,128)(2,1)S(1)}, u32[]{:S(2)}, u32[]{:S(2)}) %collective-permute-start.22) | collective-permute-done | bytes 12320 | tf_op jit(solution)/shard_map/ppermute | solution.py:538
  96.0 1.0 collective-permute-done.21.refs_4_.refs_1_
  97.0 1.5 %pair_weight.1 = f32[32,8,128]{2,1,0:T(8,128)} custom-call(s32[2]{0:T(128)S(1)} %copy-done.14, bf16[16,128,128]{2,1,0:T(8,128)(2,1)S(1)} %get-tuple-element.126.refs_1_, bf16[64,128]{1,0:T(8,128)(2,1)S(1)} %get-tuple-element.127.refs_2_.refs_4_, bf16[64,128]{1,0:T(8,128)(2,1)S(1)} %collective-permute-done.20.refs_5_.refs_3_, ...), custom_call_target="tpu_custom_call" | custom-call | flops 67108864 | bytes 688136 | tf_op jit(solution)/shard_map/pair_weight/pallas_call | solution.py:79
  98.4 2.6 %all-to-all-start = ((f32[32,8,128]{2,1,0:T(8,128)}), f32[32,8,128]{2,1,0:T(8,128)S(1)}, u32[]{:S(2)}, u32[]{:S(2)}) async-start(f32[32,8,128]{2,1,0:T(8,128)} %pair_weight.1), calls=%async_computation | async-start | bytes 262144 | tf_op jit(solution)/shard_map/all_to_all | solution.py:542
  101.1 2.9 %pair.1 = bf16[2048,128]{1,0:T(8,128)(2,1)} custom-call(s32[2]{0:T(128)S(1)} %copy-done.14, bf16[2048,128]{1,0:T(8,128)(2,1)S(1)} %bitcast.19, f32[1,128]{1,0:T(1,128)S(1)} %bitcast.26, bf16[8,128]{1,0:T(8,128)(2,1)S(1)} %bitcast.24, bf16[64,128]{1,0:T(8,128)(2,1)S(1)} %get-tuple-element.127.refs_2_.refs_4_, ...), custom_call_target="tpu_custom_call" | custom-call | flops 67108864 | bytes 1083912 | tf_op jit(solution)/shard_map/pair/pallas_call | solution.py:79
  104.0 5.7 %all-to-all-done.refs_6_ = f32[32,8,128]{2,1,0:T(8,128)S(1)} async-done(((f32[32,8,128]{2,1,0:T(8,128)}), f32[32,8,128]{2,1,0:T(8,128)S(1)}, u32[]{:S(2)}, u32[]{:S(2)}) %all-to-all-start) | async-done | bytes 131104 | tf_op jit(solution)/shard_map/all_to_all | solution.py:542
  109.7 0.7 close.1
  (50 shorter events, 0.2 us)
Async XLA Ops:
  0.6 19.2 %copy-start.4 = (bf16[768,768]{1,0:T(8,128)(2,1)S(1)}, bf16[768,768]{1,0:T(8,128)(2,1)}, u32[]{:S(2)}) copy-start(bf16[768,768]{1,0:T(8,128)(2,1)} %refs_1_.3) | copy-start | bytes 3538948
  5.4 13.1 %collective-permute-start.3 = (bf16[128,768]{1,0:T(8,128)(2,1)}, bf16[128,768]{1,0:T(8,128)(2,1)S(1)}, u32[]{:S(2)}, u32[]{:S(2)}) collective-permute-start(bf16[128,768]{1,0:T(8,128)(2,1)} %get-tuple-element.76.refs_2_), channel_id=1, source_target_pairs={{0,1},{1,0},{2,3},{3,2},{4,5},{5,4},{6,7},{7,6},{8,9},{9,8},{10,11... | collective-permute-start | bytes 589832 | tf_op jit(solution)/shard_map/ppermute | solution.py:538
  8.4 4.4 %collective-permute-start = (bf16[2,64,128]{2,1,0:T(8,128)(2,1)}, bf16[2,64,128]{2,1,0:T(8,128)(2,1)S(1)}, u32[]{:S(2)}, u32[]{:S(2)}) collective-permute-start(bf16[2,64,128]{2,1,0:T(8,128)(2,1)} %get-tuple-element.75.refs_0_), channel_id=1, source_target_pairs={{0,8},{2,10},{4,12},{6,14},{8,0},{10,2},{12,4},{14,6},{16,24},{18,... | collective-permute-start | bytes 98312 | tf_op jit(solution)/shard_map/ppermute | solution.py:533
  10.0 5.3 %collective-permute-start.1 = (bf16[2,64,128]{2,1,0:T(8,128)(2,1)}, bf16[2,64,128]{2,1,0:T(8,128)(2,1)S(1)}, u32[]{:S(2)}, u32[]{:S(2)}) collective-permute-start(bf16[2,64,128]{2,1,0:T(8,128)(2,1)} %get-tuple-element.75.refs_0_), channel_id=1, source_target_pairs={{0,16},{2,18},{4,20},{6,22},{8,24},{10,26},{12,28},{14,30},{16,0},... | collective-permute-start | bytes 98312 | tf_op jit(solution)/shard_map/ppermute | solution.py:533
  12.6 5.9 %collective-permute-start.2 = (bf16[2,64,128]{2,1,0:T(8,128)(2,1)}, bf16[2,64,128]{2,1,0:T(8,128)(2,1)S(1)}, u32[]{:S(2)}, u32[]{:S(2)}) collective-permute-start(bf16[2,64,128]{2,1,0:T(8,128)(2,1)} %get-tuple-element.75.refs_0_), channel_id=1, source_target_pairs={{0,24},{2,26},{4,28},{6,30},{8,16},{10,18},{12,20},{14,22},{16,8},... | collective-permute-start | bytes 98312 | tf_op jit(solution)/shard_map/ppermute | solution.py:533
  18.5 0.8 copy-start.15
  19.3 4.6 %collective-permute-start.4 = (bf16[4,64,128]{2,1,0:T(8,128)(2,1)S(1)}, bf16[4,64,128]{2,1,0:T(8,128)(2,1)S(1)}, u32[]{:S(2)}, u32[]{:S(2)}) collective-permute-start(bf16[4,64,128]{2,1,0:T(8,128)(2,1)S(1)} %get-tuple-element.81), channel_id=1, source_target_pairs={{0,1},{1,0},{2,3},{3,2},{4,5},{5,4},{6,7},{7,6},{8,9},{9,8},{10,11... | collective-permute-start | bytes 196616 | tf_op jit(solution)/shard_map/ppermute | solution.py:538
  19.9 1.3 %copy-start.5 = (bf16[768,768]{1,0:T(8,128)(2,1)S(1)}, bf16[768,768]{1,0:T(8,128)(2,1)}, u32[]{:S(2)}) copy-start(bf16[768,768]{1,0:T(8,128)(2,1)} %refs_2_.3) | copy-start | bytes 3538948
  21.1 1.3 %copy-start.6 = (bf16[768,768]{1,0:T(8,128)(2,1)S(1)}, bf16[768,768]{1,0:T(8,128)(2,1)}, u32[]{:S(2)}) copy-start(bf16[768,768]{1,0:T(8,128)(2,1)} %refs_3_.1) | copy-start | bytes 3538948
  22.4 0.7 copy-start.13
  23.1 7.6 %copy-start.12 = (f32[256,128]{1,0:T(8,128)S(1)}, f32[256,128]{1,0:T(8,128)}, u32[]{:S(2)}) copy-start(f32[256,128]{1,0:T(8,128)} %get-tuple-element.82.refs_6_) | copy-start | bytes 393220
  23.8 1.7 %copy-start.11 = (bf16[128,768]{1,0:T(8,128)(2,1)S(1)}, bf16[128,768]{1,0:T(8,128)(2,1)}, u32[]{:S(2)}) copy-start(bf16[128,768]{1,0:T(8,128)(2,1)} %get-tuple-element.76.refs_2_) | copy-start | bytes 589828
  23.9 10.5 %copy-start.2 = (bf16[1536,768]{1,0:T(8,128)(2,1)S(1)}, bf16[1536,768]{1,0:T(8,128)(2,1)}, u32[]{:S(2)}) copy-start(bf16[1536,768]{1,0:T(8,128)(2,1)} %refs_1_.2) | copy-start | bytes 7077892
  23.9 6.7 %copy-start.14 = (s32[2]{0:T(128)S(1)}, s32[2]{0:T(128)}, u32[]{:S(2)}) copy-start(s32[2]{0:T(128)} %pad_add_fusion.refs_0_) | copy-start | bytes 28
  23.9 6.7 %copy-start.18 = (f32[1,256]{1,0:T(1,128)S(1)}, f32[1,256]{1,0:T(1,128)}, u32[]{:S(2)}) copy-start(f32[1,256]{1,0:T(1,128)} %get-tuple-element.83.refs_7_) | copy-start | bytes 3076
  23.9 10.4 %copy-start.20 = (f32[768]{0:T(1024)S(1)}, f32[768]{0:T(1024)}, u32[]{:S(2)}) copy-start(f32[768]{0:T(1024)} %param.29) | copy-start | bytes 9220
  23.9 10.4 %copy-start.8 = (bf16[1,128,768]{2,1,0:T(8,128)(2,1)S(1)}, bf16[1,128,768]{2,1,0:T(8,128)(2,1)}, u32[]{:S(2)}) copy-start(bf16[1,128,768]{2,1,0:T(8,128)(2,1)} %param.20) | copy-start | bytes 589828
  23.9 10.4 %copy-start.10 = (bf16[1,128,768]{2,1,0:T(8,128)(2,1)S(1)}, bf16[1,128,768]{2,1,0:T(8,128)(2,1)}, u32[]{:S(2)}) copy-start(bf16[1,128,768]{2,1,0:T(8,128)(2,1)} %param.39) | copy-start | bytes 589828
  24.0 5.0 %collective-permute-start.5 = (bf16[2,4,64,128]{3,2,1,0:T(8,128)(2,1)S(1)}, bf16[2,4,64,128]{3,2,1,0:T(8,128)(2,1)S(1)}, u32[]{:S(2)}, u32[]{:S(2)}) collective-permute-start(bf16[2,4,64,128]{3,2,1,0:T(8,128)(2,1)S(1)} %join_tok.1.refs_0_), channel_id=1, source_target_pairs={{0,4},{2,6},{4,0},{6,2},{8,12},{10,14},{12,8},{14,10},{16,20},{18,... | collective-permute-start | bytes 393224 | tf_op jit(solution)/shard_map/ppermute | solution.py:533
  25.6 12.1 %copy-start.7 = (bf16[768,768]{1,0:T(8,128)(2,1)S(1)}, bf16[768,768]{1,0:T(8,128)(2,1)}, u32[]{:S(2)}) copy-start(bf16[768,768]{1,0:T(8,128)(2,1)} %refs_7_.1) | copy-start | bytes 3538948
  29.0 8.7 %copy-start.1 = (bf16[768,1536]{1,0:T(8,128)(2,1)S(1)}, bf16[768,1536]{1,0:T(8,128)(2,1)}, u32[]{:S(2)}) copy-start(bf16[768,1536]{1,0:T(8,128)(2,1)} %refs_9_.1) | copy-start | bytes 7077892
  29.0 1.6 %collective-permute-start.6 = (bf16[2,2,4,64,128]{4,3,2,1,0:T(8,128)(2,1)S(1)}, bf16[2,2,4,64,128]{4,3,2,1,0:T(8,128)(2,1)S(1)}, u32[]{:S(2)}, u32[]{:S(2)}) collective-permute-start(bf16[2,2,4,64,128]{4,3,2,1,0:T(8,128)(2,1)S(1)} %join_y.1.refs_4_), channel_id=1, source_target_pairs={{0,2},{2,0},{4,6},{6,4},{8,10},{10,8},{12,14},{14,12},{16,18},{18,... | collective-permute-start | bytes 786440 | tf_op jit(solution)/shard_map/ppermute | solution.py:533
  30.6 7.1 %copy-start = (bf16[768,1536]{1,0:T(8,128)(2,1)S(1)}, bf16[768,1536]{1,0:T(8,128)(2,1)}, u32[]{:S(2)}) copy-start(bf16[768,1536]{1,0:T(8,128)(2,1)} %refs_8_.1) | copy-start | bytes 7077892
  32.8 4.9 %collective-permute-start.7 = (bf16[128,384]{1,0:T(8,128)(2,1)S(1)}, bf16[128,384]{1,0:T(8,128)(2,1)S(1)}, u32[]{:S(2)}, u32[]{:S(2)}) collective-permute-start(bf16[128,384]{1,0:T(8,128)(2,1)S(1)} %get-tuple-element.85), channel_id=1, source_target_pairs={{0,1},{1,0},{2,3},{3,2},{4,5},{5,4},{6,7},{7,6},{8,9},{9,8},{10,11... | collective-permute-start | bytes 294920 | tf_op jit(solution)/shard_map/ppermute | solution.py:538
  42.0 4.7 %collective-permute-start.8 = (bf16[384,128]{1,0:T(8,128)(2,1)S(1)}, bf16[384,128]{1,0:T(8,128)(2,1)S(1)}, u32[]{:S(2)}, u32[]{:S(2)}) collective-permute-start(bf16[384,128]{1,0:T(8,128)(2,1)S(1)} %get-tuple-element.90), channel_id=1, source_target_pairs={{0,1},{1,0},{2,3},{3,2},{4,5},{5,4},{6,7},{7,6},{8,9},{9,8},{10,11... | collective-permute-start | bytes 294920 | tf_op jit(solution)/shard_map/ppermute | solution.py:538
  48.7 7.3 %collective-permute-start.11 = (bf16[64,16,128]{2,1,0:T(8,128)(2,1)S(1)}, bf16[64,16,128]{2,1,0:T(8,128)(2,1)S(1)}, u32[]{:S(2)}, u32[]{:S(2)}) collective-permute-start(bf16[64,16,128]{2,1,0:T(8,128)(2,1)S(1)} %get-tuple-element.104), channel_id=1, source_target_pairs={{0,4},{2,6},{4,0},{6,2},{8,12},{10,14},{12,8},{14,10},{16,20},{18,... | collective-permute-start | bytes 786440 | tf_op jit(solution)/shard_map/ppermute | solution.py:533
  50.3 5.7 %collective-permute-start.12 = (bf16[128,768]{1,0:T(8,128)(2,1)S(1)}, bf16[128,768]{1,0:T(8,128)(2,1)S(1)}, u32[]{:S(2)}, u32[]{:S(2)}) collective-permute-start(bf16[128,768]{1,0:T(8,128)(2,1)S(1)} %get-tuple-element.105.refs_5_), channel_id=1, source_target_pairs={{0,1},{1,0},{2,3},{3,2},{4,5},{5,4},{6,7},{7,6},{8,9},{9,8},{10,11... | collective-permute-start | bytes 589832 | tf_op jit(solution)/shard_map/ppermute | solution.py:538
  54.1 5.1 %collective-permute-start.10 = (bf16[216,16,128]{2,1,0:T(8,128)(2,1)S(1)}, bf16[216,16,128]{2,1,0:T(8,128)(2,1)S(1)}, u32[]{:S(2)}, u32[]{:S(2)}) collective-permute-start(bf16[216,16,128]{2,1,0:T(8,128)(2,1)S(1)} %get-tuple-element.100), channel_id=1, source_target_pairs={{0,2},{2,0},{4,6},{6,4},{8,10},{10,8},{12,14},{14,12},{16,18},{18,... | collective-permute-start | bytes 2654216 | tf_op jit(solution)/shard_map/ppermute | solution.py:533
  57.1 5.3 %copy-start.19 = (f32[768]{0:T(1024)S(1)}, f32[768]{0:T(1024)}, u32[]{:S(2)}) copy-start(f32[768]{0:T(1024)} %refs_5_.1) | copy-start | bytes 9220
  57.1 10.5 %copy-start.9 = (bf16[16,128,128]{2,1,0:T(8,128)(2,1)S(1)}, bf16[16,128,128]{2,1,0:T(8,128)(2,1)}, u32[]{:S(2)}) copy-start(bf16[16,128,128]{2,1,0:T(8,128)(2,1)} %get-tuple-element.96.refs_4_) | copy-start | bytes 1572868
  57.1 2.1 %collective-permute-start.13 = (bf16[152,16,128]{2,1,0:T(8,128)(2,1)S(1)}, bf16[152,16,128]{2,1,0:T(8,128)(2,1)S(1)}, u32[]{:S(2)}, u32[]{:S(2)}) collective-permute-start(bf16[152,16,128]{2,1,0:T(8,128)(2,1)S(1)} %get-tuple-element.107), channel_id=1, source_target_pairs={{0,2},{2,0},{4,6},{6,4},{8,10},{10,8},{12,14},{14,12},{16,18},{18,... | collective-permute-start | bytes 1867784 | tf_op jit(solution)/shard_map/ppermute | solution.py:533
  60.1 12.3 %collective-permute-start.14 = (bf16[108,16,128]{2,1,0:T(8,128)(2,1)S(1)}, bf16[108,16,128]{2,1,0:T(8,128)(2,1)S(1)}, u32[]{:S(2)}, u32[]{:S(2)}) collective-permute-start(bf16[108,16,128]{2,1,0:T(8,128)(2,1)S(1)} %get-tuple-element.109), channel_id=1, source_target_pairs={{0,4},{2,6},{4,0},{6,2},{8,12},{10,14},{12,8},{14,10},{16,20},{18,... | collective-permute-start | bytes 1327112 | tf_op jit(solution)/shard_map/ppermute | solution.py:533
  60.9 9.1 %collective-permute-start.15 = (bf16[76,16,128]{2,1,0:T(8,128)(2,1)S(1)}, bf16[76,16,128]{2,1,0:T(8,128)(2,1)S(1)}, u32[]{:S(2)}, u32[]{:S(2)}) collective-permute-start(bf16[76,16,128]{2,1,0:T(8,128)(2,1)S(1)} %get-tuple-element.111), channel_id=1, source_target_pairs={{0,8},{2,10},{4,12},{6,14},{8,0},{10,2},{12,4},{14,6},{16,24},{18,... | collective-permute-start | bytes 933896 | tf_op jit(solution)/shard_map/ppermute | solution.py:533
  60.9 6.7 %collective-permute-start.9 = (bf16[768,128]{1,0:T(8,128)(2,1)S(1)}, bf16[768,128]{1,0:T(8,128)(2,1)S(1)}, u32[]{:S(2)}, u32[]{:S(2)}) collective-permute-start(bf16[768,128]{1,0:T(8,128)(2,1)S(1)} %get-tuple-element.97), channel_id=1, source_target_pairs={{0,1},{1,0},{2,3},{3,2},{4,5},{5,4},{6,7},{7,6},{8,9},{9,8},{10,11... | collective-permute-start | bytes 589832 | tf_op jit(solution)/shard_map/ppermute | solution.py:538
  72.4 28.6 %copy-start.3 = (bf16[128,16,128]{2,1,0:T(8,128)(2,1)S(1)}, bf16[128,16,128]{2,1,0:T(8,128)(2,1)}, u32[]{:S(2)}) copy-start(bf16[128,16,128]{2,1,0:T(8,128)(2,1)} %param.22) | copy-start | bytes 1572868
  72.4 28.6 %copy-start.16 = (bf16[128,8]{0,1:T(8,128)(2,1)S(1)}, bf16[128,8]{0,1:T(8,128)(2,1)}, u32[]{:S(2)}) copy-start(bf16[128,8]{0,1:T(8,128)(2,1)} %param.34) | copy-start | bytes 6148
  72.4 28.6 %copy-start.17 = (f32[128]{0:T(128)S(1)}, f32[128]{0:T(128)}, u32[]{:S(2)}) copy-start(f32[128]{0:T(128)} %param.28) | copy-start | bytes 1540
  73.2 10.0 %collective-permute-start.16 = (bf16[54,16,128]{2,1,0:T(8,128)(2,1)S(1)}, bf16[54,16,128]{2,1,0:T(8,128)(2,1)S(1)}, u32[]{:S(2)}, u32[]{:S(2)}) collective-permute-start(bf16[54,16,128]{2,1,0:T(8,128)(2,1)S(1)} %get-tuple-element.114), channel_id=1, source_target_pairs={{0,8},{2,10},{4,12},{6,14},{8,0},{10,2},{12,4},{14,6},{16,24},{18,... | collective-permute-start | bytes 663560 | tf_op jit(solution)/shard_map/ppermute | solution.py:533
  73.3 9.7 %collective-permute-start.17 = (bf16[38,16,128]{2,1,0:T(8,128)(2,1)S(1)}, bf16[38,16,128]{2,1,0:T(8,128)(2,1)S(1)}, u32[]{:S(2)}, u32[]{:S(2)}) collective-permute-start(bf16[38,16,128]{2,1,0:T(8,128)(2,1)S(1)} %get-tuple-element.116), channel_id=1, source_target_pairs={{0,16},{2,18},{4,20},{6,22},{8,24},{10,26},{12,28},{14,30},{16,0},... | collective-permute-start | bytes 466952 | tf_op jit(solution)/shard_map/ppermute | solution.py:533
  83.9 6.6 %collective-permute-start.18 = (bf16[27,16,128]{2,1,0:T(8,128)(2,1)S(1)}, bf16[27,16,128]{2,1,0:T(8,128)(2,1)S(1)}, u32[]{:S(2)}, u32[]{:S(2)}) collective-permute-start(bf16[27,16,128]{2,1,0:T(8,128)(2,1)S(1)} %get-tuple-element.118), channel_id=1, source_target_pairs={{0,1},{1,0},{2,3},{3,2},{4,5},{5,4},{6,7},{7,6},{8,9},{9,8},{10,11... | collective-permute-start | bytes 331784 | tf_op jit(solution)/shard_map/ppermute | solution.py:538
  85.4 5.1 %collective-permute-start.19 = (bf16[15,16,128]{2,1,0:T(8,128)(2,1)S(1)}, bf16[15,16,128]{2,1,0:T(8,128)(2,1)S(1)}, u32[]{:S(2)}, u32[]{:S(2)}) collective-permute-start(bf16[15,16,128]{2,1,0:T(8,128)(2,1)S(1)} %get-tuple-element.120), channel_id=1, source_target_pairs={{0,4},{2,6},{4,0},{6,2},{8,12},{10,14},{12,8},{14,10},{16,20},{18,... | collective-permute-start | bytes 184328 | tf_op jit(solution)/shard_map/ppermute | solution.py:533
  86.7 3.8 %collective-permute-start.20 = (bf16[64,128]{1,0:T(8,128)(2,1)S(1)}, bf16[64,128]{1,0:T(8,128)(2,1)S(1)}, u32[]{:S(2)}, u32[]{:S(2)}) collective-permute-start(bf16[64,128]{1,0:T(8,128)(2,1)S(1)} %get-tuple-element.121), channel_id=1, source_target_pairs={{0,1},{1,0},{2,3},{3,2},{4,5},{5,4},{6,7},{7,6},{8,9},{9,8},{10,11... | collective-permute-start | bytes 49160 | tf_op jit(solution)/shard_map/ppermute | solution.py:538
  91.1 5.9 %collective-permute-start.21 = (bf16[27,16,128]{2,1,0:T(8,128)(2,1)S(1)}, bf16[27,16,128]{2,1,0:T(8,128)(2,1)S(1)}, u32[]{:S(2)}, u32[]{:S(2)}) collective-permute-start(bf16[27,16,128]{2,1,0:T(8,128)(2,1)S(1)} %get-tuple-element.123), channel_id=1, source_target_pairs={{0,16},{2,18},{4,20},{6,22},{8,24},{10,26},{12,28},{14,30},{16,0},... | collective-permute-start | bytes 331784 | tf_op jit(solution)/shard_map/ppermute | solution.py:533
  92.3 3.7 %collective-permute-start.22 = (bf16[3,16,128]{2,1,0:T(8,128)(2,1)S(1)}, bf16[3,16,128]{2,1,0:T(8,128)(2,1)S(1)}, u32[]{:S(2)}, u32[]{:S(2)}) collective-permute-start(bf16[3,16,128]{2,1,0:T(8,128)(2,1)S(1)} %get-tuple-element.125), channel_id=1, source_target_pairs={{0,1},{1,0},{2,3},{3,2},{4,5},{5,4},{6,7},{7,6},{8,9},{9,8},{10,11... | collective-permute-start | bytes 36872 | tf_op jit(solution)/shard_map/ppermute | solution.py:538
  98.4 11.2 %all-to-all-start = ((f32[32,8,128]{2,1,0:T(8,128)}), f32[32,8,128]{2,1,0:T(8,128)S(1)}, u32[]{:S(2)}, u32[]{:S(2)}) async-start(f32[32,8,128]{2,1,0:T(8,128)} %pair_weight.1), calls=%async_computation | async-start | bytes 262144 | tf_op jit(solution)/shard_map/all_to_all | solution.py:542

commit v16 on v15

--- a/solution.py
+++ b/solution.py
@@ -502,12 +502,10 @@
 def pair_weight_kernel(toks, ids, columns, *rest):
     parts, (weight_grad, grads) = rest[:toks], rest[toks:]
     set_heads(toks, ids, parts, grads)
-    cols, _, channels = columns.shape
+    cols, rows, channels = columns.shape
     heads = weight_grad.shape[1]
-    sums = jnp.zeros((heads, channels), f32)
-    for j in range(cols):
-        lines = grads[pl.ds(j, heads, stride=cols), :].astype(bf16)
-        sums = sums + mm(lines, columns[j])
+    lines = [grads[pl.ds(j, heads, stride=cols), :].astype(bf16) for j in range(cols)]
+    sums = mm(jnp.concatenate(lines, axis=1), columns[...].reshape(cols * rows, channels))
     for n in range(weight_grad.shape[0]):
         weight_grad[n] = sums
 
@@ -794,7 +792,6 @@
         )
         pairs[0] = (kept, swap_copy(sent, copies // 2))
         single_pair = (single_kept, swap_tok(single_sent, 1))
-        ready = [pairs[0][1], single_pair[1]]
 
     group = copies // toks
     swaps = []

time: 111 us -> 107 us (0.964)
  the two profiles are of different devices: /device:TPU:0 before, /device:TPU:2 now
where the time goes in v16:
time: 107 us; the launch traced here: 105 us
  waiting for transfers between devices  47.3 us (44%)
  Pallas kernels  28.8 us (27%)
  starting transfers between devices  23.3 us (22%)
  local copies, waits for them, and re-layouts  4.05 us (4%)
    pallas_call x21, Pallas kernels, call(): pl.pallas_call(whole, name=name, out_shape=[jax.ShapeDtypeStruct(one[0],...  28.8 us
    ppermute x14, waiting for transfers between devices, swap_copy(): return lax.ppermute(value, 'copy', [(i, i ^ mask) for i in range(size)])  28.5 us
    ppermute x9, waiting for transfers between devices, swap_tok(): return lax.ppermute(value, 'tok', [(i, i ^ mask) for i in range(size)])  18.9 us
    ppermute x14, starting transfers between devices, swap_copy(): return lax.ppermute(value, 'copy', [(i, i ^ mask) for i in range(size)])  13.1 us
    ppermute x9, starting transfers between devices, swap_tok(): return lax.ppermute(value, 'tok', [(i, i ^ mask) for i in range(size)])  6.59 us
    unnamed x42, local copies, waits for them, and re-layouts  4.04 us
    all_to_all x1, starting transfers between devices, exchange(): return lax.all_to_all(value, ('copy', 'tok'), 0, 0)  3.68 us
  transfers between devices with their start and end apart: 24, of which 16 were waited for; matrix products, arithmetic and copies ran while one was open for 0% of the time, Pallas kernels for 11%

profile of v16, /device:TPU:2, one launch (start us, length us, event | category | flops | bytes accessed | tf_op | source)
XLA Modules:
  0.0 105.0 jit_solution(1366202192523247577)
XLA Ops:
  0.6 0.6 pad_add_fusion.refs_0_
  1.2 4.2 %enter.1 = (bf16[128,768]{1,0:T(8,128)(2,1)}, bf16[16,128,128]{2,1,0:T(8,128)(2,1)}, f32[256,128]{1,0:T(8,128)}, f32[1,256]{1,0:T(1,128)}, bf16[2,64,128]{2,1,0:T(8,128)(2,1)}) custom-call(s32[2]{0:T(128)} %pad_add_fusion.refs_0_, bf16[128,768]{1,0:T(8,128)(2,1)} %bitcast.20, bf16[128,768]{1,0:T(8,128)(2,1)} %refs_2_.2, s32[1,128]{1,0:T(1,128)} %bitcast.30, ...), custom_call_target="tpu_custom_call" | custom-call | flops 67108864 | bytes 1860808 | tf_op jit(solution)/shard_map/enter/pallas_call | solution.py:79
  5.4 0.1 collective-permute-start.3
  5.5 2.1 %collective-permute-start = (bf16[2,64,128]{2,1,0:T(8,128)(2,1)}, bf16[2,64,128]{2,1,0:T(8,128)(2,1)S(1)}, u32[]{:S(2)}, u32[]{:S(2)}) collective-permute-start(bf16[2,64,128]{2,1,0:T(8,128)(2,1)} %get-tuple-element.75.refs_0_), channel_id=1, source_target_pairs={{0,8},{2,10},{4,12},{6,14},{8,0},{10,2},{12,4},{14,6},{16,24},{18,... | collective-permute-start | bytes 98312 | tf_op jit(solution)/shard_map/ppermute | solution.py:531
  7.6 2.6 %collective-permute-start.1 = (bf16[2,64,128]{2,1,0:T(8,128)(2,1)}, bf16[2,64,128]{2,1,0:T(8,128)(2,1)S(1)}, u32[]{:S(2)}, u32[]{:S(2)}) collective-permute-start(bf16[2,64,128]{2,1,0:T(8,128)(2,1)} %get-tuple-element.75.refs_0_), channel_id=1, source_target_pairs={{0,16},{2,18},{4,20},{6,22},{8,24},{10,26},{12,28},{14,30},{16,0},... | collective-permute-start | bytes 98312 | tf_op jit(solution)/shard_map/ppermute | solution.py:531
  10.2 2.7 %collective-permute-done.1.refs_2_ = bf16[2,64,128]{2,1,0:T(8,128)(2,1)S(1)} collective-permute-done((bf16[2,64,128]{2,1,0:T(8,128)(2,1)}, bf16[2,64,128]{2,1,0:T(8,128)(2,1)S(1)}, u32[]{:S(2)}, u32[]{:S(2)}) %collective-permute-start.1) | collective-permute-done | bytes 32800 | tf_op jit(solution)/shard_map/ppermute | solution.py:531
  12.9 3.2 %collective-permute-done.2.refs_3_ = bf16[2,64,128]{2,1,0:T(8,128)(2,1)S(1)} collective-permute-done((bf16[2,64,128]{2,1,0:T(8,128)(2,1)}, bf16[2,64,128]{2,1,0:T(8,128)(2,1)S(1)}, u32[]{:S(2)}, u32[]{:S(2)}) %collective-permute-start.2) | collective-permute-done | bytes 32800 | tf_op jit(solution)/shard_map/ppermute | solution.py:531
  16.1 0.8 copy-done.15
  16.9 1.6 %collective-permute-start.4 = (bf16[4,64,128]{2,1,0:T(8,128)(2,1)S(1)}, bf16[4,64,128]{2,1,0:T(8,128)(2,1)S(1)}, u32[]{:S(2)}, u32[]{:S(2)}) collective-permute-start(bf16[4,64,128]{2,1,0:T(8,128)(2,1)S(1)} %get-tuple-element.81), channel_id=1, source_target_pairs={{0,1},{1,0},{2,3},{3,2},{4,5},{5,4},{6,7},{7,6},{8,9},{9,8},{10,11... | collective-permute-start | bytes 196616 | tf_op jit(solution)/shard_map/ppermute | solution.py:536
  18.4 1.3 %copy-done.5 = bf16[768,768]{1,0:T(8,128)(2,1)S(1)} copy-done((bf16[768,768]{1,0:T(8,128)(2,1)S(1)}, bf16[768,768]{1,0:T(8,128)(2,1)}, u32[]{:S(2)}) %copy-start.5) | copy-done | bytes 1179672
  19.7 1.3 %copy-done.6 = bf16[768,768]{1,0:T(8,128)(2,1)S(1)} copy-done((bf16[768,768]{1,0:T(8,128)(2,1)S(1)}, bf16[768,768]{1,0:T(8,128)(2,1)}, u32[]{:S(2)}) %copy-start.6) | copy-done | bytes 1179672
  21.0 0.7 copy-done.13
  21.6 0.8 stage.1.refs_1_.refs_2_
  22.4 0.0 copy-start.11
  22.5 0.0 copy-start.20
  22.5 0.0 copy-start.8
  22.5 1.6 %collective-permute-start.5 = (bf16[2,4,64,128]{3,2,1,0:T(8,128)(2,1)S(1)}, bf16[2,4,64,128]{3,2,1,0:T(8,128)(2,1)S(1)}, u32[]{:S(2)}, u32[]{:S(2)}) collective-permute-start(bf16[2,4,64,128]{3,2,1,0:T(8,128)(2,1)S(1)} %join_tok.1.refs_0_), channel_id=1, source_target_pairs={{0,4},{2,6},{4,0},{6,2},{8,12},{10,14},{12,8},{14,10},{16,20},{18,... | collective-permute-start | bytes 393224 | tf_op jit(solution)/shard_map/ppermute | solution.py:531
  24.1 1.4 %project.1 = (bf16[256,768]{1,0:T(8,128)(2,1)S(1)}, bf16[384,256]{1,0:T(8,128)(2,1)S(1)}, bf16[384,256]{1,0:T(8,128)(2,1)S(1)}, bf16[384,256]{1,0:T(8,128)(2,1)S(1)}) custom-call(s32[2]{0:T(128)S(1)} %copy-done.13, bf16[3,768,384]{2,1,0:T(8,128)(2,1)S(1)} %stage.1.refs_1_.refs_2_, bf16[128,768]{1,0:T(8,128)(2,1)S(1)} %copy-done.11, ...), custom_call_target="tpu_custom_call" | custom-call | flops 452984832 | bytes 3145736 | tf_op jit(solution)/shard_map/project/pallas_call | solution.py:79
  25.5 2.0 %collective-permute-done.5.refs_1_ = bf16[2,4,64,128]{3,2,1,0:T(8,128)(2,1)S(1)} collective-permute-done((bf16[2,4,64,128]{3,2,1,0:T(8,128)(2,1)S(1)}, bf16[2,4,64,128]{3,2,1,0:T(8,128)(2,1)S(1)}, u32[]{:S(2)}, u32[]{:S(2)}) %collective-permute-start.5) | collective-permute-done | bytes 131104 | tf_op jit(solution)/shard_map/ppermute | solution.py:531
  27.6 0.1 collective-permute-start.6
  27.6 1.5 %collective-permute-done.6.refs_5_ = bf16[2,2,4,64,128]{4,3,2,1,0:T(8,128)(2,1)S(1)} collective-permute-done((bf16[2,2,4,64,128]{4,3,2,1,0:T(8,128)(2,1)S(1)}, bf16[2,2,4,64,128]{4,3,2,1,0:T(8,128)(2,1)S(1)}, u32[]{:S(2)}, u32[]{:S(2)}) %collective-permute-start.6) | collective-permute-done | bytes 262176 | tf_op jit(solution)/shard_map/ppermute | solution.py:531
  29.2 2.1 %attention.1 = (bf16[4,256,256]{2,1,0:T(8,128)(2,1)S(1)}, bf16[256,384]{1,0:T(8,128)(2,1)S(1)}, bf16[128,384]{1,0:T(8,128)(2,1)S(1)}, bf16[128,384]{1,0:T(8,128)(2,1)S(1)}) custom-call(s32[2]{0:T(128)S(1)} %copy-done.14, bf16[384,256]{1,0:T(8,128)(2,1)S(1)} %get-tuple-element.78.refs_1_, bf16[384,256]{1,0:T(8,128)(2,1)S(1)} %get-tuple-element.79.refs_2_, ...), custom_call_target="tpu_custom_call" | custom-call | flops 100663296 | bytes 2163720 | tf_op jit(solution)/shard_map/attention/pallas_call | solution.py:79
  31.3 0.6 collective-permute-start.7
  32.0 0.9 down.1
  32.9 3.4 %collective-permute-done.7.refs_6_ = bf16[128,384]{1,0:T(8,128)(2,1)S(1)} collective-permute-done((bf16[128,384]{1,0:T(8,128)(2,1)S(1)}, bf16[128,384]{1,0:T(8,128)(2,1)S(1)}, u32[]{:S(2)}, u32[]{:S(2)}) %collective-permute-start.7) | collective-permute-done | bytes 98336 | tf_op jit(solution)/shard_map/ppermute | solution.py:536
  36.2 4.3 %hidden.1 = (f32[128,768]{1,0:T(8,128)S(1)}, bf16[128,768]{1,0:T(8,128)(2,1)S(1)}, bf16[384,128]{1,0:T(8,128)(2,1)S(1)}, bf16[384,128]{1,0:T(8,128)(2,1)S(1)}) custom-call(s32[2]{0:T(128)S(1)} %copy-done.14, bf16[128,768]{1,0:T(8,128)(2,1)S(1)} %get-tuple-element.71.refs_1_.refs_0_, bf16[128,768]{1,0:T(8,128)(2,1)S(1)} %get-tuple-element.72.refs_2_, ...), custom_call_target="tpu_custom_call" | custom-call | flops 1509949440 | bytes 8064008 | tf_op jit(solution)/shard_map/hidden/pallas_call | solution.py:79
  40.6 0.6 collective-permute-start.8
  41.2 4.1 %collective-permute-done.8.refs_6_ = bf16[384,128]{1,0:T(8,128)(2,1)S(1)} collective-permute-done((bf16[384,128]{1,0:T(8,128)(2,1)S(1)}, bf16[384,128]{1,0:T(8,128)(2,1)S(1)}, u32[]{:S(2)}, u32[]{:S(2)}) %collective-permute-start.8) | collective-permute-done | bytes 98336 | tf_op jit(solution)/shard_map/ppermute | solution.py:536
  45.3 2.0 %backward.1 = (bf16[384,256]{1,0:T(8,128)(2,1)S(1)}, bf16[384,256]{1,0:T(8,128)(2,1)S(1)}, bf16[384,256]{1,0:T(8,128)(2,1)S(1)}, bf16[64,16,128]{2,1,0:T(8,128)(...) custom-call(s32[2]{0:T(128)S(1)} %copy-done.14, ...), custom_call_target="tpu_custom_call" | custom-call | flops 201326592 | bytes 2818056 | tf_op jit(solution)/shard_map/backward/pallas_call | solution.py:79
  47.3 1.6 %collective-permute-start.11 = (bf16[64,16,128]{2,1,0:T(8,128)(2,1)S(1)}, bf16[64,16,128]{2,1,0:T(8,128)(2,1)S(1)}, u32[]{:S(2)}, u32[]{:S(2)}) collective-permute-start(bf16[64,16,128]{2,1,0:T(8,128)(2,1)S(1)} %get-tuple-element.104), channel_id=1, source_target_pairs={{0,4},{2,6},{4,0},{6,2},{8,12},{10,14},{12,8},{14,10},{16,20},{18,... | collective-permute-start | bytes 786440 | tf_op jit(solution)/shard_map/ppermute | solution.py:531
  48.9 0.5 collective-permute-start.12
  49.4 2.3 %first.1 = (bf16[216,16,128]{2,1,0:T(8,128)(2,1)S(1)}, bf16[216,16,128]{2,1,0:T(8,128)(2,1)S(1)}, f32[768,128]{1,0:T(8,128)S(1)}, f32[768,256]{1,0:T(8,128)S(1)}, bf16[768,128]{1,0:T(8,128)(2,1)S(1)}) custom-call(s32[2]{0:T(128)S(1)} %copy-done.14, bf16[3,768,384]{2,1,0:T(8,128)(2,1)S(1)} %stage.1.refs_1_.refs_2_, ...), custom_call_target="tpu_custom_call" | custom-call | flops 905969664 | bytes 5898248 | tf_op jit(solution)/shard_map/first/pallas_call | solution.py:79
  51.7 0.1 collective-permute-start.10
  51.8 2.8 %collective-permute-done.12.refs_6_ = bf16[128,768]{1,0:T(8,128)(2,1)S(1)} collective-permute-done((bf16[128,768]{1,0:T(8,128)(2,1)S(1)}, bf16[128,768]{1,0:T(8,128)(2,1)S(1)}, u32[]{:S(2)}, u32[]{:S(2)}) %collective-permute-start.12) | collective-permute-done | bytes 196640 | tf_op jit(solution)/shard_map/ppermute | solution.py:536
  54.6 1.1 %second.1 = (bf16[152,16,128]{2,1,0:T(8,128)(2,1)S(1)}, bf16[152,16,128]{2,1,0:T(8,128)(2,1)S(1)}) custom-call(s32[2]{0:T(128)S(1)} %copy-done.14, bf16[256,384]{1,0:T(8,128)(2,1)S(1)} %get-tuple-element.101.refs_1_, f32[768,256]{1,0:T(8,128)S(1)} %get-tuple-element.102.refs_2_, bf16[64,16,128]{2,1,0:T(8,128)(2,1)S(1)} %get-tuple-element.103.refs_3_, ...), custom_call_target="tpu_custom_call" | custom-call | flops 1509949440 | bytes 3145736 | tf_op jit(solution)/shard_map/second/pallas_call | solution.py:79
  55.7 0.1 collective-permute-start.13
  55.8 2.0 %collective-permute-done.13.refs_4_ = bf16[152,16,128]{2,1,0:T(8,128)(2,1)S(1)} collective-permute-done((bf16[152,16,128]{2,1,0:T(8,128)(2,1)S(1)}, bf16[152,16,128]{2,1,0:T(8,128)(2,1)S(1)}, u32[]{:S(2)}, u32[]{:S(2)}) %collective-permute-start.13) | collective-permute-done | bytes 622624 | tf_op jit(solution)/shard_map/ppermute | solution.py:531
  57.8 0.9 step_0.1
  58.7 0.8 collective-permute-start.14
  59.5 0.5 collective-permute-start.9
  60.0 6.1 %collective-permute-done.9.refs_5_ = bf16[768,128]{1,0:T(8,128)(2,1)S(1)} collective-permute-done((bf16[768,128]{1,0:T(8,128)(2,1)S(1)}, bf16[768,128]{1,0:T(8,128)(2,1)S(1)}, u32[]{:S(2)}, u32[]{:S(2)}) %collective-permute-start.9) | collective-permute-done | bytes 196640 | tf_op jit(solution)/shard_map/ppermute | solution.py:536
  66.1 1.2 %exit.1 = (bf16[128,768]{1,0:T(8,128)(2,1)}, f32[8,128]{1,0:T(8,128)S(1)}, bf16[16,128,128]{2,1,0:T(8,128)(2,1)S(1)}) custom-call(bf16[128,768]{1,0:T(8,128)(2,1)S(1)} %get-tuple-element.71.refs_1_.refs_0_, f32[1,768]{1,0:T(1,128)S(1)} %reshape.49.refs_1_, f32[128,768]{1,0:T(8,128)S(1)} %get-tuple-element.86.refs_2_, ...), custom_call_target="tpu_custom_call" | custom-call | bytes 2432000 | tf_op jit(solution)/shard_map/exit/pallas_call | solution.py:79
  67.4 1.2 %collective-permute-done.15.refs_4_ = bf16[76,16,128]{2,1,0:T(8,128)(2,1)S(1)} collective-permute-done((bf16[76,16,128]{2,1,0:T(8,128)(2,1)S(1)}, bf16[76,16,128]{2,1,0:T(8,128)(2,1)S(1)}, u32[]{:S(2)}, u32[]{:S(2)}) %collective-permute-start.15) | collective-permute-done | bytes 311328 | tf_op jit(solution)/shard_map/ppermute | solution.py:531
  68.6 2.4 %collective-permute-done.14.refs_2_ = bf16[108,16,128]{2,1,0:T(8,128)(2,1)S(1)} collective-permute-done((bf16[108,16,128]{2,1,0:T(8,128)(2,1)S(1)}, bf16[108,16,128]{2,1,0:T(8,128)(2,1)S(1)}, u32[]{:S(2)}, u32[]{:S(2)}) %collective-permute-start.14) | collective-permute-done | bytes 442400 | tf_op jit(solution)/shard_map/ppermute | solution.py:531
  71.0 0.7 step_1.1
  71.7 0.1 collective-permute-start.16
  71.8 0.9 collective-permute-start.17
  72.7 8.8 %collective-permute-done.17.refs_4_.refs_2_ = bf16[38,16,128]{2,1,0:T(8,128)(2,1)S(1)} collective-permute-done((bf16[38,16,128]{2,1,0:T(8,128)(2,1)S(1)}, bf16[38,16,128]{2,1,0:T(8,128)(2,1)S(1)}, u32[]{:S(2)}, u32[]{:S(2)}) %collective-permute-start.17) | collective-permute-done | bytes 155680 | tf_op jit(solution)/shard_map/ppermute | solution.py:531
  81.5 0.3 collective-permute-done.16.refs_2_
  81.8 0.6 across.1
  82.4 0.6 collective-permute-start.18
  83.0 0.7 collective-permute-start.19
  83.7 0.6 last_bias.1
  84.3 1.6 %collective-permute-start.20 = (bf16[64,128]{1,0:T(8,128)(2,1)S(1)}, bf16[64,128]{1,0:T(8,128)(2,1)S(1)}, u32[]{:S(2)}, u32[]{:S(2)}) collective-permute-start(bf16[64,128]{1,0:T(8,128)(2,1)S(1)} %get-tuple-element.121), channel_id=1, source_target_pairs={{0,1},{1,0},{2,3},{3,2},{4,5},{5,4},{6,7},{7,6},{8,9},{9,8},{10,11... | collective-permute-start | bytes 49160 | tf_op jit(solution)/shard_map/ppermute | solution.py:536
  85.8 2.2 %collective-permute-done.20.refs_5_.refs_3_ = bf16[64,128]{1,0:T(8,128)(2,1)S(1)} collective-permute-done((bf16[64,128]{1,0:T(8,128)(2,1)S(1)}, bf16[64,128]{1,0:T(8,128)(2,1)S(1)}, u32[]{:S(2)}, u32[]{:S(2)}) %collective-permute-start.20) | collective-permute-done | bytes 16416 | tf_op jit(solution)/shard_map/ppermute | solution.py:536
  88.1 1.4 %pair_weight.1 = f32[32,8,128]{2,1,0:T(8,128)} custom-call(s32[2]{0:T(128)S(1)} %copy-done.14, bf16[16,128,128]{2,1,0:T(8,128)(2,1)S(1)} %get-tuple-element.126.refs_1_, bf16[64,128]{1,0:T(8,128)(2,1)S(1)} %get-tuple-element.127.refs_2_.refs_4_, bf16[64,128]{1,0:T(8,128)(2,1)S(1)} %collective-permute-done.20.refs_5_.refs_3_, ...), custom_call_target="tpu_custom_call" | custom-call | flops 67108864 | bytes 688136 | tf_op jit(solution)/shard_map/pair_weight/pallas_call | solution.py:79
  89.5 3.7 %all-to-all-start = ((f32[32,8,128]{2,1,0:T(8,128)}), f32[32,8,128]{2,1,0:T(8,128)S(1)}, u32[]{:S(2)}, u32[]{:S(2)}) async-start(f32[32,8,128]{2,1,0:T(8,128)} %pair_weight.1), calls=%async_computation | async-start | bytes 262144 | tf_op jit(solution)/shard_map/all_to_all | solution.py:540
  93.2 0.6 far.1
  93.8 2.6 %collective-permute-start.21 = (bf16[27,16,128]{2,1,0:T(8,128)(2,1)S(1)}, bf16[27,16,128]{2,1,0:T(8,128)(2,1)S(1)}, u32[]{:S(2)}, u32[]{:S(2)}) collective-permute-start(bf16[27,16,128]{2,1,0:T(8,128)(2,1)S(1)} %get-tuple-element.123), channel_id=1, source_target_pairs={{0,16},{2,18},{4,20},{6,22},{8,24},{10,26},{12,28},{14,30},{16,0},... | collective-permute-start | bytes 331784 | tf_op jit(solution)/shard_map/ppermute | solution.py:531
  96.3 0.5 collective-permute-start.22
  96.9 2.9 %pair.1 = bf16[2048,128]{1,0:T(8,128)(2,1)} custom-call(s32[2]{0:T(128)S(1)} %copy-done.14, bf16[2048,128]{1,0:T(8,128)(2,1)S(1)} %bitcast.19, f32[1,128]{1,0:T(1,128)S(1)} %bitcast.26, bf16[8,128]{1,0:T(8,128)(2,1)S(1)} %bitcast.24, bf16[64,128]{1,0:T(8,128)(2,1)S(1)} %get-tuple-element.127.refs_2_.refs_4_, ...), custom_call_target="tpu_custom_call" | custom-call | flops 67108864 | bytes 1083912 | tf_op jit(solution)/shard_map/pair/pallas_call | solution.py:79
  99.8 0.2 collective-permute-done.22.refs_5_
  100.0 4.3 %collective-permute-done.21.refs_1_ = bf16[27,16,128]{2,1,0:T(8,128)(2,1)S(1)} collective-permute-done((bf16[27,16,128]{2,1,0:T(8,128)(2,1)S(1)}, bf16[27,16,128]{2,1,0:T(8,128)(2,1)S(1)}, u32[]{:S(2)}, u32[]{:S(2)}) %collective-permute-start.21) | collective-permute-done | bytes 110624 | tf_op jit(solution)/shard_map/ppermute | solution.py:531
  104.3 0.7 close.1
  (50 shorter events, 0.2 us)
Async XLA Ops:
  0.6 17.8 %copy-start.4 = (bf16[768,768]{1,0:T(8,128)(2,1)S(1)}, bf16[768,768]{1,0:T(8,128)(2,1)}, u32[]{:S(2)}) copy-start(bf16[768,768]{1,0:T(8,128)(2,1)} %refs_1_.3) | copy-start | bytes 3538948
  5.4 10.7 %collective-permute-start.3 = (bf16[128,768]{1,0:T(8,128)(2,1)}, bf16[128,768]{1,0:T(8,128)(2,1)S(1)}, u32[]{:S(2)}, u32[]{:S(2)}) collective-permute-start(bf16[128,768]{1,0:T(8,128)(2,1)} %get-tuple-element.76.refs_2_), channel_id=1, source_target_pairs={{0,1},{1,0},{2,3},{3,2},{4,5},{5,4},{6,7},{7,6},{8,9},{9,8},{10,11... | collective-permute-start | bytes 589832 | tf_op jit(solution)/shard_map/ppermute | solution.py:536
  5.5 4.7 %collective-permute-start = (bf16[2,64,128]{2,1,0:T(8,128)(2,1)}, bf16[2,64,128]{2,1,0:T(8,128)(2,1)S(1)}, u32[]{:S(2)}, u32[]{:S(2)}) collective-permute-start(bf16[2,64,128]{2,1,0:T(8,128)(2,1)} %get-tuple-element.75.refs_0_), channel_id=1, source_target_pairs={{0,8},{2,10},{4,12},{6,14},{8,0},{10,2},{12,4},{14,6},{16,24},{18,... | collective-permute-start | bytes 98312 | tf_op jit(solution)/shard_map/ppermute | solution.py:531
  7.6 5.3 %collective-permute-start.1 = (bf16[2,64,128]{2,1,0:T(8,128)(2,1)}, bf16[2,64,128]{2,1,0:T(8,128)(2,1)S(1)}, u32[]{:S(2)}, u32[]{:S(2)}) collective-permute-start(bf16[2,64,128]{2,1,0:T(8,128)(2,1)} %get-tuple-element.75.refs_0_), channel_id=1, source_target_pairs={{0,16},{2,18},{4,20},{6,22},{8,24},{10,26},{12,28},{14,30},{16,0},... | collective-permute-start | bytes 98312 | tf_op jit(solution)/shard_map/ppermute | solution.py:531
  10.2 5.9 %collective-permute-start.2 = (bf16[2,64,128]{2,1,0:T(8,128)(2,1)}, bf16[2,64,128]{2,1,0:T(8,128)(2,1)S(1)}, u32[]{:S(2)}, u32[]{:S(2)}) collective-permute-start(bf16[2,64,128]{2,1,0:T(8,128)(2,1)} %get-tuple-element.75.refs_0_), channel_id=1, source_target_pairs={{0,24},{2,26},{4,28},{6,30},{8,16},{10,18},{12,20},{14,22},{16,8},... | collective-permute-start | bytes 98312 | tf_op jit(solution)/shard_map/ppermute | solution.py:531
  16.1 0.8 copy-start.15
  16.9 5.5 %collective-permute-start.4 = (bf16[4,64,128]{2,1,0:T(8,128)(2,1)S(1)}, bf16[4,64,128]{2,1,0:T(8,128)(2,1)S(1)}, u32[]{:S(2)}, u32[]{:S(2)}) collective-permute-start(bf16[4,64,128]{2,1,0:T(8,128)(2,1)S(1)} %get-tuple-element.81), channel_id=1, source_target_pairs={{0,1},{1,0},{2,3},{3,2},{4,5},{5,4},{6,7},{7,6},{8,9},{9,8},{10,11... | collective-permute-start | bytes 196616 | tf_op jit(solution)/shard_map/ppermute | solution.py:536
  18.4 1.3 %copy-start.5 = (bf16[768,768]{1,0:T(8,128)(2,1)S(1)}, bf16[768,768]{1,0:T(8,128)(2,1)}, u32[]{:S(2)}) copy-start(bf16[768,768]{1,0:T(8,128)(2,1)} %refs_2_.3) | copy-start | bytes 3538948
  19.7 1.3 %copy-start.6 = (bf16[768,768]{1,0:T(8,128)(2,1)S(1)}, bf16[768,768]{1,0:T(8,128)(2,1)}, u32[]{:S(2)}) copy-start(bf16[768,768]{1,0:T(8,128)(2,1)} %refs_3_.1) | copy-start | bytes 3538948
  21.0 0.7 copy-start.13
  21.6 7.6 %copy-start.12 = (f32[256,128]{1,0:T(8,128)S(1)}, f32[256,128]{1,0:T(8,128)}, u32[]{:S(2)}) copy-start(f32[256,128]{1,0:T(8,128)} %get-tuple-element.82.refs_6_) | copy-start | bytes 393220
  22.4 1.7 %copy-start.11 = (bf16[128,768]{1,0:T(8,128)(2,1)S(1)}, bf16[128,768]{1,0:T(8,128)(2,1)}, u32[]{:S(2)}) copy-start(bf16[128,768]{1,0:T(8,128)(2,1)} %get-tuple-element.76.refs_2_) | copy-start | bytes 589828
  22.4 9.5 %copy-start.2 = (bf16[1536,768]{1,0:T(8,128)(2,1)S(1)}, bf16[1536,768]{1,0:T(8,128)(2,1)}, u32[]{:S(2)}) copy-start(bf16[1536,768]{1,0:T(8,128)(2,1)} %refs_1_.2) | copy-start | bytes 7077892
  22.4 6.7 %copy-start.14 = (s32[2]{0:T(128)S(1)}, s32[2]{0:T(128)}, u32[]{:S(2)}) copy-start(s32[2]{0:T(128)} %pad_add_fusion.refs_0_) | copy-start | bytes 28
  22.5 6.7 %copy-start.18 = (f32[1,256]{1,0:T(1,128)S(1)}, f32[1,256]{1,0:T(1,128)}, u32[]{:S(2)}) copy-start(f32[1,256]{1,0:T(1,128)} %get-tuple-element.83.refs_7_) | copy-start | bytes 3076
  22.5 9.5 %copy-start.20 = (f32[768]{0:T(1024)S(1)}, f32[768]{0:T(1024)}, u32[]{:S(2)}) copy-start(f32[768]{0:T(1024)} %param.29) | copy-start | bytes 9220
  22.5 9.5 %copy-start.8 = (bf16[1,128,768]{2,1,0:T(8,128)(2,1)S(1)}, bf16[1,128,768]{2,1,0:T(8,128)(2,1)}, u32[]{:S(2)}) copy-start(bf16[1,128,768]{2,1,0:T(8,128)(2,1)} %param.20) | copy-start | bytes 589828
  22.5 9.5 %copy-start.10 = (bf16[1,128,768]{2,1,0:T(8,128)(2,1)S(1)}, bf16[1,128,768]{2,1,0:T(8,128)(2,1)}, u32[]{:S(2)}) copy-start(bf16[1,128,768]{2,1,0:T(8,128)(2,1)} %param.39) | copy-start | bytes 589828
  22.5 5.0 %collective-permute-start.5 = (bf16[2,4,64,128]{3,2,1,0:T(8,128)(2,1)S(1)}, bf16[2,4,64,128]{3,2,1,0:T(8,128)(2,1)S(1)}, u32[]{:S(2)}, u32[]{:S(2)}) collective-permute-start(bf16[2,4,64,128]{3,2,1,0:T(8,128)(2,1)S(1)} %join_tok.1.refs_0_), channel_id=1, source_target_pairs={{0,4},{2,6},{4,0},{6,2},{8,12},{10,14},{12,8},{14,10},{16,20},{18,... | collective-permute-start | bytes 393224 | tf_op jit(solution)/shard_map/ppermute | solution.py:531
  24.1 12.1 %copy-start.7 = (bf16[768,768]{1,0:T(8,128)(2,1)S(1)}, bf16[768,768]{1,0:T(8,128)(2,1)}, u32[]{:S(2)}) copy-start(bf16[768,768]{1,0:T(8,128)(2,1)} %refs_7_.1) | copy-start | bytes 3538948
  27.5 8.7 %copy-start.1 = (bf16[768,1536]{1,0:T(8,128)(2,1)S(1)}, bf16[768,1536]{1,0:T(8,128)(2,1)}, u32[]{:S(2)}) copy-start(bf16[768,1536]{1,0:T(8,128)(2,1)} %refs_9_.1) | copy-start | bytes 7077892
  27.6 1.6 %collective-permute-start.6 = (bf16[2,2,4,64,128]{4,3,2,1,0:T(8,128)(2,1)S(1)}, bf16[2,2,4,64,128]{4,3,2,1,0:T(8,128)(2,1)S(1)}, u32[]{:S(2)}, u32[]{:S(2)}) collective-permute-start(bf16[2,2,4,64,128]{4,3,2,1,0:T(8,128)(2,1)S(1)} %join_y.1.refs_4_), channel_id=1, source_target_pairs={{0,2},{2,0},{4,6},{6,4},{8,10},{10,8},{12,14},{14,12},{16,18},{18,... | collective-permute-start | bytes 786440 | tf_op jit(solution)/shard_map/ppermute | solution.py:531
  29.2 7.1 %copy-start = (bf16[768,1536]{1,0:T(8,128)(2,1)S(1)}, bf16[768,1536]{1,0:T(8,128)(2,1)}, u32[]{:S(2)}) copy-start(bf16[768,1536]{1,0:T(8,128)(2,1)} %refs_8_.1) | copy-start | bytes 7077892
  31.3 4.9 %collective-permute-start.7 = (bf16[128,384]{1,0:T(8,128)(2,1)S(1)}, bf16[128,384]{1,0:T(8,128)(2,1)S(1)}, u32[]{:S(2)}, u32[]{:S(2)}) collective-permute-start(bf16[128,384]{1,0:T(8,128)(2,1)S(1)} %get-tuple-element.85), channel_id=1, source_target_pairs={{0,1},{1,0},{2,3},{3,2},{4,5},{5,4},{6,7},{7,6},{8,9},{9,8},{10,11... | collective-permute-start | bytes 294920 | tf_op jit(solution)/shard_map/ppermute | solution.py:536
  40.6 4.7 %collective-permute-start.8 = (bf16[384,128]{1,0:T(8,128)(2,1)S(1)}, bf16[384,128]{1,0:T(8,128)(2,1)S(1)}, u32[]{:S(2)}, u32[]{:S(2)}) collective-permute-start(bf16[384,128]{1,0:T(8,128)(2,1)S(1)} %get-tuple-element.90), channel_id=1, source_target_pairs={{0,1},{1,0},{2,3},{3,2},{4,5},{5,4},{6,7},{7,6},{8,9},{9,8},{10,11... | collective-permute-start | bytes 294920 | tf_op jit(solution)/shard_map/ppermute | solution.py:536
  47.3 7.3 %collective-permute-start.11 = (bf16[64,16,128]{2,1,0:T(8,128)(2,1)S(1)}, bf16[64,16,128]{2,1,0:T(8,128)(2,1)S(1)}, u32[]{:S(2)}, u32[]{:S(2)}) collective-permute-start(bf16[64,16,128]{2,1,0:T(8,128)(2,1)S(1)} %get-tuple-element.104), channel_id=1, source_target_pairs={{0,4},{2,6},{4,0},{6,2},{8,12},{10,14},{12,8},{14,10},{16,20},{18,... | collective-permute-start | bytes 786440 | tf_op jit(solution)/shard_map/ppermute | solution.py:531
  48.9 5.7 %collective-permute-start.12 = (bf16[128,768]{1,0:T(8,128)(2,1)S(1)}, bf16[128,768]{1,0:T(8,128)(2,1)S(1)}, u32[]{:S(2)}, u32[]{:S(2)}) collective-permute-start(bf16[128,768]{1,0:T(8,128)(2,1)S(1)} %get-tuple-element.105.refs_5_), channel_id=1, source_target_pairs={{0,1},{1,0},{2,3},{3,2},{4,5},{5,4},{6,7},{7,6},{8,9},{9,8},{10,11... | collective-permute-start | bytes 589832 | tf_op jit(solution)/shard_map/ppermute | solution.py:536
  51.7 6.1 %collective-permute-start.10 = (bf16[216,16,128]{2,1,0:T(8,128)(2,1)S(1)}, bf16[216,16,128]{2,1,0:T(8,128)(2,1)S(1)}, u32[]{:S(2)}, u32[]{:S(2)}) collective-permute-start(bf16[216,16,128]{2,1,0:T(8,128)(2,1)S(1)} %get-tuple-element.100), channel_id=1, source_target_pairs={{0,2},{2,0},{4,6},{6,4},{8,10},{10,8},{12,14},{14,12},{16,18},{18,... | collective-permute-start | bytes 2654216 | tf_op jit(solution)/shard_map/ppermute | solution.py:531
  55.7 4.3 %copy-start.19 = (f32[768]{0:T(1024)S(1)}, f32[768]{0:T(1024)}, u32[]{:S(2)}) copy-start(f32[768]{0:T(1024)} %refs_5_.1) | copy-start | bytes 9220
  55.7 10.5 %copy-start.9 = (bf16[16,128,128]{2,1,0:T(8,128)(2,1)S(1)}, bf16[16,128,128]{2,1,0:T(8,128)(2,1)}, u32[]{:S(2)}) copy-start(bf16[16,128,128]{2,1,0:T(8,128)(2,1)} %get-tuple-element.96.refs_4_) | copy-start | bytes 1572868
  55.7 2.1 %collective-permute-start.13 = (bf16[152,16,128]{2,1,0:T(8,128)(2,1)S(1)}, bf16[152,16,128]{2,1,0:T(8,128)(2,1)S(1)}, u32[]{:S(2)}, u32[]{:S(2)}) collective-permute-start(bf16[152,16,128]{2,1,0:T(8,128)(2,1)S(1)} %get-tuple-element.107), channel_id=1, source_target_pairs={{0,2},{2,0},{4,6},{6,4},{8,10},{10,8},{12,14},{14,12},{16,18},{18,... | collective-permute-start | bytes 1867784 | tf_op jit(solution)/shard_map/ppermute | solution.py:531
  58.7 12.3 %collective-permute-start.14 = (bf16[108,16,128]{2,1,0:T(8,128)(2,1)S(1)}, bf16[108,16,128]{2,1,0:T(8,128)(2,1)S(1)}, u32[]{:S(2)}, u32[]{:S(2)}) collective-permute-start(bf16[108,16,128]{2,1,0:T(8,128)(2,1)S(1)} %get-tuple-element.109), channel_id=1, source_target_pairs={{0,4},{2,6},{4,0},{6,2},{8,12},{10,14},{12,8},{14,10},{16,20},{18,... | collective-permute-start | bytes 1327112 | tf_op jit(solution)/shard_map/ppermute | solution.py:531
  59.5 9.1 %collective-permute-start.15 = (bf16[76,16,128]{2,1,0:T(8,128)(2,1)S(1)}, bf16[76,16,128]{2,1,0:T(8,128)(2,1)S(1)}, u32[]{:S(2)}, u32[]{:S(2)}) collective-permute-start(bf16[76,16,128]{2,1,0:T(8,128)(2,1)S(1)} %get-tuple-element.111), channel_id=1, source_target_pairs={{0,8},{2,10},{4,12},{6,14},{8,0},{10,2},{12,4},{14,6},{16,24},{18,... | collective-permute-start | bytes 933896 | tf_op jit(solution)/shard_map/ppermute | solution.py:531
  59.5 6.7 %collective-permute-start.9 = (bf16[768,128]{1,0:T(8,128)(2,1)S(1)}, bf16[768,128]{1,0:T(8,128)(2,1)S(1)}, u32[]{:S(2)}, u32[]{:S(2)}) collective-permute-start(bf16[768,128]{1,0:T(8,128)(2,1)S(1)} %get-tuple-element.97), channel_id=1, source_target_pairs={{0,1},{1,0},{2,3},{3,2},{4,5},{5,4},{6,7},{7,6},{8,9},{9,8},{10,11... | collective-permute-start | bytes 589832 | tf_op jit(solution)/shard_map/ppermute | solution.py:536
  71.0 25.9 %copy-start.3 = (bf16[128,16,128]{2,1,0:T(8,128)(2,1)S(1)}, bf16[128,16,128]{2,1,0:T(8,128)(2,1)}, u32[]{:S(2)}) copy-start(bf16[128,16,128]{2,1,0:T(8,128)(2,1)} %param.22) | copy-start | bytes 1572868
  71.0 25.9 %copy-start.16 = (bf16[128,8]{0,1:T(8,128)(2,1)S(1)}, bf16[128,8]{0,1:T(8,128)(2,1)}, u32[]{:S(2)}) copy-start(bf16[128,8]{0,1:T(8,128)(2,1)} %param.34) | copy-start | bytes 6148
  71.0 25.9 %copy-start.17 = (f32[128]{0:T(128)S(1)}, f32[128]{0:T(128)}, u32[]{:S(2)}) copy-start(f32[128]{0:T(128)} %param.28) | copy-start | bytes 1540
  71.7 10.0 %collective-permute-start.16 = (bf16[54,16,128]{2,1,0:T(8,128)(2,1)S(1)}, bf16[54,16,128]{2,1,0:T(8,128)(2,1)S(1)}, u32[]{:S(2)}, u32[]{:S(2)}) collective-permute-start(bf16[54,16,128]{2,1,0:T(8,128)(2,1)S(1)} %get-tuple-element.114), channel_id=1, source_target_pairs={{0,8},{2,10},{4,12},{6,14},{8,0},{10,2},{12,4},{14,6},{16,24},{18,... | collective-permute-start | bytes 663560 | tf_op jit(solution)/shard_map/ppermute | solution.py:531
  71.8 9.7 %collective-permute-start.17 = (bf16[38,16,128]{2,1,0:T(8,128)(2,1)S(1)}, bf16[38,16,128]{2,1,0:T(8,128)(2,1)S(1)}, u32[]{:S(2)}, u32[]{:S(2)}) collective-permute-start(bf16[38,16,128]{2,1,0:T(8,128)(2,1)S(1)} %get-tuple-element.116), channel_id=1, source_target_pairs={{0,16},{2,18},{4,20},{6,22},{8,24},{10,26},{12,28},{14,30},{16,0},... | collective-permute-start | bytes 466952 | tf_op jit(solution)/shard_map/ppermute | solution.py:531
  82.4 5.7 %collective-permute-start.18 = (bf16[27,16,128]{2,1,0:T(8,128)(2,1)S(1)}, bf16[27,16,128]{2,1,0:T(8,128)(2,1)S(1)}, u32[]{:S(2)}, u32[]{:S(2)}) collective-permute-start(bf16[27,16,128]{2,1,0:T(8,128)(2,1)S(1)} %get-tuple-element.118), channel_id=1, source_target_pairs={{0,1},{1,0},{2,3},{3,2},{4,5},{5,4},{6,7},{7,6},{8,9},{9,8},{10,11... | collective-permute-start | bytes 331784 | tf_op jit(solution)/shard_map/ppermute | solution.py:536
  83.0 5.1 %collective-permute-start.19 = (bf16[15,16,128]{2,1,0:T(8,128)(2,1)S(1)}, bf16[15,16,128]{2,1,0:T(8,128)(2,1)S(1)}, u32[]{:S(2)}, u32[]{:S(2)}) collective-permute-start(bf16[15,16,128]{2,1,0:T(8,128)(2,1)S(1)} %get-tuple-element.120), channel_id=1, source_target_pairs={{0,4},{2,6},{4,0},{6,2},{8,12},{10,14},{12,8},{14,10},{16,20},{18,... | collective-permute-start | bytes 184328 | tf_op jit(solution)/shard_map/ppermute | solution.py:531
  84.3 3.8 %collective-permute-start.20 = (bf16[64,128]{1,0:T(8,128)(2,1)S(1)}, bf16[64,128]{1,0:T(8,128)(2,1)S(1)}, u32[]{:S(2)}, u32[]{:S(2)}) collective-permute-start(bf16[64,128]{1,0:T(8,128)(2,1)S(1)} %get-tuple-element.121), channel_id=1, source_target_pairs={{0,1},{1,0},{2,3},{3,2},{4,5},{5,4},{6,7},{7,6},{8,9},{9,8},{10,11... | collective-permute-start | bytes 49160 | tf_op jit(solution)/shard_map/ppermute | solution.py:536
  89.5 14.8 %all-to-all-start = ((f32[32,8,128]{2,1,0:T(8,128)}), f32[32,8,128]{2,1,0:T(8,128)S(1)}, u32[]{:S(2)}, u32[]{:S(2)}) async-start(f32[32,8,128]{2,1,0:T(8,128)} %pair_weight.1), calls=%async_computation | async-start | bytes 262144 | tf_op jit(solution)/shard_map/all_to_all | solution.py:540
  93.8 10.5 %collective-permute-start.21 = (bf16[27,16,128]{2,1,0:T(8,128)(2,1)S(1)}, bf16[27,16,128]{2,1,0:T(8,128)(2,1)S(1)}, u32[]{:S(2)}, u32[]{:S(2)}) collective-permute-start(bf16[27,16,128]{2,1,0:T(8,128)(2,1)S(1)} %get-tuple-element.123), channel_id=1, source_target_pairs={{0,16},{2,18},{4,20},{6,22},{8,24},{10,26},{12,28},{14,30},{16,0},... | collective-permute-start | bytes 331784 | tf_op jit(solution)/shard_map/ppermute | solution.py:531
  96.3 3.7 %collective-permute-start.22 = (bf16[3,16,128]{2,1,0:T(8,128)(2,1)S(1)}, bf16[3,16,128]{2,1,0:T(8,128)(2,1)S(1)}, u32[]{:S(2)}, u32[]{:S(2)}) collective-permute-start(bf16[3,16,128]{2,1,0:T(8,128)(2,1)S(1)} %get-tuple-element.125), channel_id=1, source_target_pairs={{0,1},{1,0},{2,3},{3,2},{4,5},{5,4},{6,7},{7,6},{8,9},{9,8},{10,11... | collective-permute-start | bytes 36872 | tf_op jit(solution)/shard_map/ppermute | solution.py:536

commit v17 on v16

--- a/solution.py
+++ b/solution.py
@@ -449,7 +449,7 @@
     outs[3][...] = take(total, 0, cut, own_width)
     total = single[...].astype(f32) + got_single[...].astype(f32)
     outs[4][...] = take(total, 0, cut, outs[4].shape[1])
-    outs[5][...] = jnp.sum(terms[...], axis=0)
+    outs[5][...] = jnp.sum(terms[...].astype(f32), axis=0)
 
 
 def last_kernel(toks, ids, kept, got, kept_b, got_b, moved, final, *rest):
@@ -507,7 +507,7 @@
     lines = [grads[pl.ds(j, heads, stride=cols), :].astype(bf16) for j in range(cols)]
     sums = mm(jnp.concatenate(lines, axis=1), columns[...].reshape(cols * rows, channels))
     for n in range(weight_grad.shape[0]):
-        weight_grad[n] = sums
+        weight_grad[n] = sums.astype(weight_grad.dtype)
 
 
 def pair_kernel(toks, cols, ids, pair, gain, w_pair, *rest):
@@ -803,7 +803,7 @@
         functools.partial(pair_weight_kernel, toks),
         "pair_weight",
         [where_am_i, columns] + bias_pieces,
-        [((devices, heads, channels), f32)],
+        [((devices, heads, channels), bf16)],
         [VMEM((heads * cols, rows), f32)],
         flops=2 * heads * cols * rows * channels * cols,
         deps=ready,
@@ -832,7 +832,7 @@
             [((3, cut, own_width), bf16), ((cut, own_width), f32)] + [((cut, rows), bf16)] * toks,
             [VMEM((toks, cut, rows), f32)],
         )
-        weight_grad = jnp.sum(weight_terms, axis=0)
+        weight_grad = jnp.sum(weight_terms.astype(f32), axis=0)
         grad_out, singles = last[1], last[2:]
         singles = [singles[0]] + [swap_tok(singles[r], r) for r in range(1, toks)]
         moved = lax.ppermute(last[0], ("copy", "tok"), swaps)

time: 107 us -> 106 us (level)
  waiting for transfers between devices: 47.3 us -> 46.1 us
    ppermute x14, waiting for transfers between devices: 28.5 us -> 27.3 us  [swap_copy(): return lax.ppermute(value, 'copy', [(i, i ^ mask) for i in range(size)])]
where the time goes in v17:
time: 106 us; the launch traced here: 104 us
  waiting for transfers between devices  46.1 us (43%)
  Pallas kernels  28.8 us (27%)
  starting transfers between devices  23.3 us (22%)
  local copies, waits for them, and re-layouts  4.05 us (4%)
    pallas_call x21, Pallas kernels, call(): pl.pallas_call(whole, name=name, out_shape=[jax.ShapeDtypeStruct(one[0],...  28.8 us
    ppermute x14, waiting for transfers between devices, swap_copy(): return lax.ppermute(value, 'copy', [(i, i ^ mask) for i in range(size)])  27.3 us
    ppermute x9, waiting for transfers between devices, swap_tok(): return lax.ppermute(value, 'tok', [(i, i ^ mask) for i in range(size)])  18.8 us
    ppermute x14, starting transfers between devices, swap_copy(): return lax.ppermute(value, 'copy', [(i, i ^ mask) for i in range(size)])  13.1 us
    ppermute x9, starting transfers between devices, swap_tok(): return lax.ppermute(value, 'tok', [(i, i ^ mask) for i in range(size)])  6.59 us
    unnamed x42, local copies, waits for them, and re-layouts  4.04 us
    all_to_all x1, starting transfers between devices, exchange(): return lax.all_to_all(value, ('copy', 'tok'), 0, 0)  3.68 us
  transfers between devices with their start and end apart: 24, of which 16 were waited for; matrix products, arithmetic and copies ran while one was open for 0% of the time, Pallas kernels for 11%

profile of v17, /device:TPU:2, one launch (start us, length us, event | category | flops | bytes accessed | tf_op | source)
XLA Modules:
  0.0 103.8 jit_solution(16141722732550874021)
XLA Ops:
  0.6 0.6 pad_add_fusion.refs_0_
  1.2 4.2 %enter.1 = (bf16[128,768]{1,0:T(8,128)(2,1)}, bf16[16,128,128]{2,1,0:T(8,128)(2,1)}, f32[256,128]{1,0:T(8,128)}, f32[1,256]{1,0:T(1,128)}, bf16[2,64,128]{2,1,0:T(8,128)(2,1)}) custom-call(s32[2]{0:T(128)} %pad_add_fusion.refs_0_, bf16[128,768]{1,0:T(8,128)(2,1)} %bitcast.20, bf16[128,768]{1,0:T(8,128)(2,1)} %refs_2_.2, s32[1,128]{1,0:T(1,128)} %bitcast.30, ...), custom_call_target="tpu_custom_call" | custom-call | flops 67108864 | bytes 1860808 | tf_op jit(solution)/shard_map/enter/pallas_call | solution.py:79
  5.4 0.1 collective-permute-start.3
  5.5 2.1 %collective-permute-start = (bf16[2,64,128]{2,1,0:T(8,128)(2,1)}, bf16[2,64,128]{2,1,0:T(8,128)(2,1)S(1)}, u32[]{:S(2)}, u32[]{:S(2)}) collective-permute-start(bf16[2,64,128]{2,1,0:T(8,128)(2,1)} %get-tuple-element.75.refs_0_), channel_id=1, source_target_pairs={{0,8},{2,10},{4,12},{6,14},{8,0},{10,2},{12,4},{14,6},{16,24},{18,... | collective-permute-start | bytes 98312 | tf_op jit(solution)/shard_map/ppermute | solution.py:531
  7.6 2.6 %collective-permute-start.1 = (bf16[2,64,128]{2,1,0:T(8,128)(2,1)}, bf16[2,64,128]{2,1,0:T(8,128)(2,1)S(1)}, u32[]{:S(2)}, u32[]{:S(2)}) collective-permute-start(bf16[2,64,128]{2,1,0:T(8,128)(2,1)} %get-tuple-element.75.refs_0_), channel_id=1, source_target_pairs={{0,16},{2,18},{4,20},{6,22},{8,24},{10,26},{12,28},{14,30},{16,0},... | collective-permute-start | bytes 98312 | tf_op jit(solution)/shard_map/ppermute | solution.py:531
  10.2 2.7 %collective-permute-done.1.refs_2_ = bf16[2,64,128]{2,1,0:T(8,128)(2,1)S(1)} collective-permute-done((bf16[2,64,128]{2,1,0:T(8,128)(2,1)}, bf16[2,64,128]{2,1,0:T(8,128)(2,1)S(1)}, u32[]{:S(2)}, u32[]{:S(2)}) %collective-permute-start.1) | collective-permute-done | bytes 32800 | tf_op jit(solution)/shard_map/ppermute | solution.py:531
  12.9 3.2 %collective-permute-done.2.refs_3_ = bf16[2,64,128]{2,1,0:T(8,128)(2,1)S(1)} collective-permute-done((bf16[2,64,128]{2,1,0:T(8,128)(2,1)}, bf16[2,64,128]{2,1,0:T(8,128)(2,1)S(1)}, u32[]{:S(2)}, u32[]{:S(2)}) %collective-permute-start.2) | collective-permute-done | bytes 32800 | tf_op jit(solution)/shard_map/ppermute | solution.py:531
  16.1 0.8 copy-done.15
  16.9 1.6 %collective-permute-start.4 = (bf16[4,64,128]{2,1,0:T(8,128)(2,1)S(1)}, bf16[4,64,128]{2,1,0:T(8,128)(2,1)S(1)}, u32[]{:S(2)}, u32[]{:S(2)}) collective-permute-start(bf16[4,64,128]{2,1,0:T(8,128)(2,1)S(1)} %get-tuple-element.81), channel_id=1, source_target_pairs={{0,1},{1,0},{2,3},{3,2},{4,5},{5,4},{6,7},{7,6},{8,9},{9,8},{10,11... | collective-permute-start | bytes 196616 | tf_op jit(solution)/shard_map/ppermute | solution.py:536
  18.4 1.3 %copy-done.5 = bf16[768,768]{1,0:T(8,128)(2,1)S(1)} copy-done((bf16[768,768]{1,0:T(8,128)(2,1)S(1)}, bf16[768,768]{1,0:T(8,128)(2,1)}, u32[]{:S(2)}) %copy-start.5) | copy-done | bytes 1179672
  19.7 1.3 %copy-done.6 = bf16[768,768]{1,0:T(8,128)(2,1)S(1)} copy-done((bf16[768,768]{1,0:T(8,128)(2,1)S(1)}, bf16[768,768]{1,0:T(8,128)(2,1)}, u32[]{:S(2)}) %copy-start.6) | copy-done | bytes 1179672
  21.0 0.7 copy-done.13
  21.6 0.8 stage.1.refs_1_.refs_2_
  22.4 0.0 copy-start.2
  22.5 0.0 copy-start.18
  22.5 0.0 copy-start.20
  22.5 1.6 %collective-permute-start.5 = (bf16[2,4,64,128]{3,2,1,0:T(8,128)(2,1)S(1)}, bf16[2,4,64,128]{3,2,1,0:T(8,128)(2,1)S(1)}, u32[]{:S(2)}, u32[]{:S(2)}) collective-permute-start(bf16[2,4,64,128]{3,2,1,0:T(8,128)(2,1)S(1)} %join_tok.1.refs_0_), channel_id=1, source_target_pairs={{0,4},{2,6},{4,0},{6,2},{8,12},{10,14},{12,8},{14,10},{16,20},{18,... | collective-permute-start | bytes 393224 | tf_op jit(solution)/shard_map/ppermute | solution.py:531
  24.1 1.4 %project.1 = (bf16[256,768]{1,0:T(8,128)(2,1)S(1)}, bf16[384,256]{1,0:T(8,128)(2,1)S(1)}, bf16[384,256]{1,0:T(8,128)(2,1)S(1)}, bf16[384,256]{1,0:T(8,128)(2,1)S(1)}) custom-call(s32[2]{0:T(128)S(1)} %copy-done.13, bf16[3,768,384]{2,1,0:T(8,128)(2,1)S(1)} %stage.1.refs_1_.refs_2_, bf16[128,768]{1,0:T(8,128)(2,1)S(1)} %copy-done.11, ...), custom_call_target="tpu_custom_call" | custom-call | flops 452984832 | bytes 3145736 | tf_op jit(solution)/shard_map/project/pallas_call | solution.py:79
  25.5 2.0 %collective-permute-done.5.refs_1_ = bf16[2,4,64,128]{3,2,1,0:T(8,128)(2,1)S(1)} collective-permute-done((bf16[2,4,64,128]{3,2,1,0:T(8,128)(2,1)S(1)}, bf16[2,4,64,128]{3,2,1,0:T(8,128)(2,1)S(1)}, u32[]{:S(2)}, u32[]{:S(2)}) %collective-permute-start.5) | collective-permute-done | bytes 131104 | tf_op jit(solution)/shard_map/ppermute | solution.py:531
  27.6 0.1 collective-permute-start.6
  27.6 1.5 %collective-permute-done.6.refs_5_ = bf16[2,2,4,64,128]{4,3,2,1,0:T(8,128)(2,1)S(1)} collective-permute-done((bf16[2,2,4,64,128]{4,3,2,1,0:T(8,128)(2,1)S(1)}, bf16[2,2,4,64,128]{4,3,2,1,0:T(8,128)(2,1)S(1)}, u32[]{:S(2)}, u32[]{:S(2)}) %collective-permute-start.6) | collective-permute-done | bytes 262176 | tf_op jit(solution)/shard_map/ppermute | solution.py:531
  29.2 2.1 %attention.1 = (bf16[4,256,256]{2,1,0:T(8,128)(2,1)S(1)}, bf16[256,384]{1,0:T(8,128)(2,1)S(1)}, bf16[128,384]{1,0:T(8,128)(2,1)S(1)}, bf16[128,384]{1,0:T(8,128)(2,1)S(1)}) custom-call(s32[2]{0:T(128)S(1)} %copy-done.14, bf16[384,256]{1,0:T(8,128)(2,1)S(1)} %get-tuple-element.78.refs_1_, bf16[384,256]{1,0:T(8,128)(2,1)S(1)} %get-tuple-element.79.refs_2_, ...), custom_call_target="tpu_custom_call" | custom-call | flops 100663296 | bytes 2163720 | tf_op jit(solution)/shard_map/attention/pallas_call | solution.py:79
  31.3 0.6 collective-permute-start.7
  32.0 0.9 down.1
  32.9 3.4 %collective-permute-done.7.refs_6_ = bf16[128,384]{1,0:T(8,128)(2,1)S(1)} collective-permute-done((bf16[128,384]{1,0:T(8,128)(2,1)S(1)}, bf16[128,384]{1,0:T(8,128)(2,1)S(1)}, u32[]{:S(2)}, u32[]{:S(2)}) %collective-permute-start.7) | collective-permute-done | bytes 98336 | tf_op jit(solution)/shard_map/ppermute | solution.py:536
  36.2 4.3 %hidden.1 = (f32[128,768]{1,0:T(8,128)S(1)}, bf16[128,768]{1,0:T(8,128)(2,1)S(1)}, bf16[384,128]{1,0:T(8,128)(2,1)S(1)}, bf16[384,128]{1,0:T(8,128)(2,1)S(1)}) custom-call(s32[2]{0:T(128)S(1)} %copy-done.14, bf16[128,768]{1,0:T(8,128)(2,1)S(1)} %get-tuple-element.71.refs_1_.refs_0_, bf16[128,768]{1,0:T(8,128)(2,1)S(1)} %get-tuple-element.72.refs_2_, ...), custom_call_target="tpu_custom_call" | custom-call | flops 1509949440 | bytes 8064008 | tf_op jit(solution)/shard_map/hidden/pallas_call | solution.py:79
  40.6 0.6 collective-permute-start.8
  41.2 4.1 %collective-permute-done.8.refs_6_ = bf16[384,128]{1,0:T(8,128)(2,1)S(1)} collective-permute-done((bf16[384,128]{1,0:T(8,128)(2,1)S(1)}, bf16[384,128]{1,0:T(8,128)(2,1)S(1)}, u32[]{:S(2)}, u32[]{:S(2)}) %collective-permute-start.8) | collective-permute-done | bytes 98336 | tf_op jit(solution)/shard_map/ppermute | solution.py:536
  45.3 2.0 %backward.1 = (bf16[384,256]{1,0:T(8,128)(2,1)S(1)}, bf16[384,256]{1,0:T(8,128)(2,1)S(1)}, bf16[384,256]{1,0:T(8,128)(2,1)S(1)}, bf16[64,16,128]{2,1,0:T(8,128)(...) custom-call(s32[2]{0:T(128)S(1)} %copy-done.14, ...), custom_call_target="tpu_custom_call" | custom-call | flops 201326592 | bytes 2818056 | tf_op jit(solution)/shard_map/backward/pallas_call | solution.py:79
  47.3 1.6 %collective-permute-start.11 = (bf16[64,16,128]{2,1,0:T(8,128)(2,1)S(1)}, bf16[64,16,128]{2,1,0:T(8,128)(2,1)S(1)}, u32[]{:S(2)}, u32[]{:S(2)}) collective-permute-start(bf16[64,16,128]{2,1,0:T(8,128)(2,1)S(1)} %get-tuple-element.104), channel_id=1, source_target_pairs={{0,4},{2,6},{4,0},{6,2},{8,12},{10,14},{12,8},{14,10},{16,20},{18,... | collective-permute-start | bytes 786440 | tf_op jit(solution)/shard_map/ppermute | solution.py:531
  48.9 0.5 collective-permute-start.12
  49.4 2.3 %first.1 = (bf16[216,16,128]{2,1,0:T(8,128)(2,1)S(1)}, bf16[216,16,128]{2,1,0:T(8,128)(2,1)S(1)}, f32[768,128]{1,0:T(8,128)S(1)}, f32[768,256]{1,0:T(8,128)S(1)}, bf16[768,128]{1,0:T(8,128)(2,1)S(1)}) custom-call(s32[2]{0:T(128)S(1)} %copy-done.14, bf16[3,768,384]{2,1,0:T(8,128)(2,1)S(1)} %stage.1.refs_1_.refs_2_, ...), custom_call_target="tpu_custom_call" | custom-call | flops 905969664 | bytes 5898248 | tf_op jit(solution)/shard_map/first/pallas_call | solution.py:79
  51.7 0.1 collective-permute-start.10
  51.8 2.8 %collective-permute-done.12.refs_6_ = bf16[128,768]{1,0:T(8,128)(2,1)S(1)} collective-permute-done((bf16[128,768]{1,0:T(8,128)(2,1)S(1)}, bf16[128,768]{1,0:T(8,128)(2,1)S(1)}, u32[]{:S(2)}, u32[]{:S(2)}) %collective-permute-start.12) | collective-permute-done | bytes 196640 | tf_op jit(solution)/shard_map/ppermute | solution.py:536
  54.6 1.1 %second.1 = (bf16[152,16,128]{2,1,0:T(8,128)(2,1)S(1)}, bf16[152,16,128]{2,1,0:T(8,128)(2,1)S(1)}) custom-call(s32[2]{0:T(128)S(1)} %copy-done.14, bf16[256,384]{1,0:T(8,128)(2,1)S(1)} %get-tuple-element.101.refs_1_, f32[768,256]{1,0:T(8,128)S(1)} %get-tuple-element.102.refs_2_, bf16[64,16,128]{2,1,0:T(8,128)(2,1)S(1)} %get-tuple-element.103.refs_3_, ...), custom_call_target="tpu_custom_call" | custom-call | flops 1509949440 | bytes 3145736 | tf_op jit(solution)/shard_map/second/pallas_call | solution.py:79
  55.7 0.1 collective-permute-start.13
  55.8 2.0 %collective-permute-done.13.refs_4_ = bf16[152,16,128]{2,1,0:T(8,128)(2,1)S(1)} collective-permute-done((bf16[152,16,128]{2,1,0:T(8,128)(2,1)S(1)}, bf16[152,16,128]{2,1,0:T(8,128)(2,1)S(1)}, u32[]{:S(2)}, u32[]{:S(2)}) %collective-permute-start.13) | collective-permute-done | bytes 622624 | tf_op jit(solution)/shard_map/ppermute | solution.py:531
  57.8 0.9 step_0.1
  58.7 0.8 collective-permute-start.14
  59.5 0.5 collective-permute-start.9
  60.0 6.1 %collective-permute-done.9.refs_5_ = bf16[768,128]{1,0:T(8,128)(2,1)S(1)} collective-permute-done((bf16[768,128]{1,0:T(8,128)(2,1)S(1)}, bf16[768,128]{1,0:T(8,128)(2,1)S(1)}, u32[]{:S(2)}, u32[]{:S(2)}) %collective-permute-start.9) | collective-permute-done | bytes 196640 | tf_op jit(solution)/shard_map/ppermute | solution.py:536
  66.1 1.2 %exit.1 = (bf16[128,768]{1,0:T(8,128)(2,1)}, f32[8,128]{1,0:T(8,128)S(1)}, bf16[16,128,128]{2,1,0:T(8,128)(2,1)S(1)}) custom-call(bf16[128,768]{1,0:T(8,128)(2,1)S(1)} %get-tuple-element.71.refs_1_.refs_0_, f32[1,768]{1,0:T(1,128)S(1)} %reshape.49.refs_1_, f32[128,768]{1,0:T(8,128)S(1)} %get-tuple-element.86.refs_2_, ...), custom_call_target="tpu_custom_call" | custom-call | bytes 2432000 | tf_op jit(solution)/shard_map/exit/pallas_call | solution.py:79
  67.4 1.2 %collective-permute-done.15.refs_4_ = bf16[76,16,128]{2,1,0:T(8,128)(2,1)S(1)} collective-permute-done((bf16[76,16,128]{2,1,0:T(8,128)(2,1)S(1)}, bf16[76,16,128]{2,1,0:T(8,128)(2,1)S(1)}, u32[]{:S(2)}, u32[]{:S(2)}) %collective-permute-start.15) | collective-permute-done | bytes 311328 | tf_op jit(solution)/shard_map/ppermute | solution.py:531
  68.6 2.4 %collective-permute-done.14.refs_2_ = bf16[108,16,128]{2,1,0:T(8,128)(2,1)S(1)} collective-permute-done((bf16[108,16,128]{2,1,0:T(8,128)(2,1)S(1)}, bf16[108,16,128]{2,1,0:T(8,128)(2,1)S(1)}, u32[]{:S(2)}, u32[]{:S(2)}) %collective-permute-start.14) | collective-permute-done | bytes 442400 | tf_op jit(solution)/shard_map/ppermute | solution.py:531
  71.0 0.7 step_1.1
  71.7 0.1 collective-permute-start.16
  71.8 0.9 collective-permute-start.17
  72.7 8.8 %collective-permute-done.17.refs_4_.refs_2_ = bf16[38,16,128]{2,1,0:T(8,128)(2,1)S(1)} collective-permute-done((bf16[38,16,128]{2,1,0:T(8,128)(2,1)S(1)}, bf16[38,16,128]{2,1,0:T(8,128)(2,1)S(1)}, u32[]{:S(2)}, u32[]{:S(2)}) %collective-permute-start.17) | collective-permute-done | bytes 155680 | tf_op jit(solution)/shard_map/ppermute | solution.py:531
  81.5 0.3 collective-permute-done.16.refs_2_
  81.8 0.6 across.1
  82.4 0.6 collective-permute-start.18
  83.0 0.7 collective-permute-start.19
  83.7 0.6 last_bias.1
  84.3 1.6 %collective-permute-start.20 = (bf16[64,128]{1,0:T(8,128)(2,1)S(1)}, bf16[64,128]{1,0:T(8,128)(2,1)S(1)}, u32[]{:S(2)}, u32[]{:S(2)}) collective-permute-start(bf16[64,128]{1,0:T(8,128)(2,1)S(1)} %get-tuple-element.121), channel_id=1, source_target_pairs={{0,1},{1,0},{2,3},{3,2},{4,5},{5,4},{6,7},{7,6},{8,9},{9,8},{10,11... | collective-permute-start | bytes 49160 | tf_op jit(solution)/shard_map/ppermute | solution.py:536
  85.8 2.2 %collective-permute-done.20.refs_5_.refs_3_ = bf16[64,128]{1,0:T(8,128)(2,1)S(1)} collective-permute-done((bf16[64,128]{1,0:T(8,128)(2,1)S(1)}, bf16[64,128]{1,0:T(8,128)(2,1)S(1)}, u32[]{:S(2)}, u32[]{:S(2)}) %collective-permute-start.20) | collective-permute-done | bytes 16416 | tf_op jit(solution)/shard_map/ppermute | solution.py:536
  88.1 1.4 %pair_weight.1 = bf16[32,8,128]{2,1,0:T(8,128)(2,1)} custom-call(s32[2]{0:T(128)S(1)} %copy-done.14, bf16[16,128,128]{2,1,0:T(8,128)(2,1)S(1)} %get-tuple-element.126.refs_1_, bf16[64,128]{1,0:T(8,128)(2,1)S(1)} %get-tuple-element.127.refs_2_.refs_4_, bf16[64,128]{1,0:T(8,128)(2,1)S(1)} %collective-permute-done.20.refs_5_.refs_3_, ...), custom_call_target="tpu_custom_call" | custom-call | flops 67108864 | bytes 622600 | tf_op jit(solution)/shard_map/pair_weight/pallas_call | solution.py:79
  89.4 3.7 %all-to-all-start = ((bf16[32,8,128]{2,1,0:T(8,128)(2,1)}), bf16[32,8,128]{2,1,0:T(8,128)(2,1)S(1)}, u32[]{:S(2)}, u32[]{:S(2)}) async-start(bf16[32,8,128]{2,1,0:T(8,128)(2,1)} %pair_weight.1), calls=%async_computation | async-start | bytes 131072 | tf_op jit(solution)/shard_map/all_to_all | solution.py:540
  93.1 0.6 far.1
  93.7 2.6 %collective-permute-start.21 = (bf16[27,16,128]{2,1,0:T(8,128)(2,1)S(1)}, bf16[27,16,128]{2,1,0:T(8,128)(2,1)S(1)}, u32[]{:S(2)}, u32[]{:S(2)}) collective-permute-start(bf16[27,16,128]{2,1,0:T(8,128)(2,1)S(1)} %get-tuple-element.123), channel_id=1, source_target_pairs={{0,16},{2,18},{4,20},{6,22},{8,24},{10,26},{12,28},{14,30},{16,0},... | collective-permute-start | bytes 331784 | tf_op jit(solution)/shard_map/ppermute | solution.py:531
  96.3 0.5 collective-permute-start.22
  96.8 2.9 %pair.1 = bf16[2048,128]{1,0:T(8,128)(2,1)} custom-call(s32[2]{0:T(128)S(1)} %copy-done.14, bf16[2048,128]{1,0:T(8,128)(2,1)S(1)} %bitcast.19, f32[1,128]{1,0:T(1,128)S(1)} %bitcast.26, bf16[8,128]{1,0:T(8,128)(2,1)S(1)} %bitcast.24, bf16[64,128]{1,0:T(8,128)(2,1)S(1)} %get-tuple-element.127.refs_2_.refs_4_, ...), custom_call_target="tpu_custom_call" | custom-call | flops 67108864 | bytes 1083912 | tf_op jit(solution)/shard_map/pair/pallas_call | solution.py:79
  99.8 0.2 collective-permute-done.22.refs_5_
  100.0 3.1 %collective-permute-done.21.refs_1_ = bf16[27,16,128]{2,1,0:T(8,128)(2,1)S(1)} collective-permute-done((bf16[27,16,128]{2,1,0:T(8,128)(2,1)S(1)}, bf16[27,16,128]{2,1,0:T(8,128)(2,1)S(1)}, u32[]{:S(2)}, u32[]{:S(2)}) %collective-permute-start.21) | collective-permute-done | bytes 110624 | tf_op jit(solution)/shard_map/ppermute | solution.py:531
  103.1 0.7 close.1
  (50 shorter events, 0.2 us)
Async XLA Ops:
  0.6 17.8 %copy-start.4 = (bf16[768,768]{1,0:T(8,128)(2,1)S(1)}, bf16[768,768]{1,0:T(8,128)(2,1)}, u32[]{:S(2)}) copy-start(bf16[768,768]{1,0:T(8,128)(2,1)} %refs_1_.3) | copy-start | bytes 3538948
  5.4 10.7 %collective-permute-start.3 = (bf16[128,768]{1,0:T(8,128)(2,1)}, bf16[128,768]{1,0:T(8,128)(2,1)S(1)}, u32[]{:S(2)}, u32[]{:S(2)}) collective-permute-start(bf16[128,768]{1,0:T(8,128)(2,1)} %get-tuple-element.76.refs_2_), channel_id=1, source_target_pairs={{0,1},{1,0},{2,3},{3,2},{4,5},{5,4},{6,7},{7,6},{8,9},{9,8},{10,11... | collective-permute-start | bytes 589832 | tf_op jit(solution)/shard_map/ppermute | solution.py:536
  5.5 4.7 %collective-permute-start = (bf16[2,64,128]{2,1,0:T(8,128)(2,1)}, bf16[2,64,128]{2,1,0:T(8,128)(2,1)S(1)}, u32[]{:S(2)}, u32[]{:S(2)}) collective-permute-start(bf16[2,64,128]{2,1,0:T(8,128)(2,1)} %get-tuple-element.75.refs_0_), channel_id=1, source_target_pairs={{0,8},{2,10},{4,12},{6,14},{8,0},{10,2},{12,4},{14,6},{16,24},{18,... | collective-permute-start | bytes 98312 | tf_op jit(solution)/shard_map/ppermute | solution.py:531
  7.6 5.3 %collective-permute-start.1 = (bf16[2,64,128]{2,1,0:T(8,128)(2,1)}, bf16[2,64,128]{2,1,0:T(8,128)(2,1)S(1)}, u32[]{:S(2)}, u32[]{:S(2)}) collective-permute-start(bf16[2,64,128]{2,1,0:T(8,128)(2,1)} %get-tuple-element.75.refs_0_), channel_id=1, source_target_pairs={{0,16},{2,18},{4,20},{6,22},{8,24},{10,26},{12,28},{14,30},{16,0},... | collective-permute-start | bytes 98312 | tf_op jit(solution)/shard_map/ppermute | solution.py:531
  10.2 5.9 %collective-permute-start.2 = (bf16[2,64,128]{2,1,0:T(8,128)(2,1)}, bf16[2,64,128]{2,1,0:T(8,128)(2,1)S(1)}, u32[]{:S(2)}, u32[]{:S(2)}) collective-permute-start(bf16[2,64,128]{2,1,0:T(8,128)(2,1)} %get-tuple-element.75.refs_0_), channel_id=1, source_target_pairs={{0,24},{2,26},{4,28},{6,30},{8,16},{10,18},{12,20},{14,22},{16,8},... | collective-permute-start | bytes 98312 | tf_op jit(solution)/shard_map/ppermute | solution.py:531
  16.1 0.8 copy-start.15
  16.9 5.5 %collective-permute-start.4 = (bf16[4,64,128]{2,1,0:T(8,128)(2,1)S(1)}, bf16[4,64,128]{2,1,0:T(8,128)(2,1)S(1)}, u32[]{:S(2)}, u32[]{:S(2)}) collective-permute-start(bf16[4,64,128]{2,1,0:T(8,128)(2,1)S(1)} %get-tuple-element.81), channel_id=1, source_target_pairs={{0,1},{1,0},{2,3},{3,2},{4,5},{5,4},{6,7},{7,6},{8,9},{9,8},{10,11... | collective-permute-start | bytes 196616 | tf_op jit(solution)/shard_map/ppermute | solution.py:536
  18.4 1.3 %copy-start.5 = (bf16[768,768]{1,0:T(8,128)(2,1)S(1)}, bf16[768,768]{1,0:T(8,128)(2,1)}, u32[]{:S(2)}) copy-start(bf16[768,768]{1,0:T(8,128)(2,1)} %refs_2_.3) | copy-start | bytes 3538948
  19.7 1.3 %copy-start.6 = (bf16[768,768]{1,0:T(8,128)(2,1)S(1)}, bf16[768,768]{1,0:T(8,128)(2,1)}, u32[]{:S(2)}) copy-start(bf16[768,768]{1,0:T(8,128)(2,1)} %refs_3_.1) | copy-start | bytes 3538948
  21.0 0.7 copy-start.13
  21.6 7.6 %copy-start.12 = (f32[256,128]{1,0:T(8,128)S(1)}, f32[256,128]{1,0:T(8,128)}, u32[]{:S(2)}) copy-start(f32[256,128]{1,0:T(8,128)} %get-tuple-element.82.refs_6_) | copy-start | bytes 393220
  22.4 1.7 %copy-start.11 = (bf16[128,768]{1,0:T(8,128)(2,1)S(1)}, bf16[128,768]{1,0:T(8,128)(2,1)}, u32[]{:S(2)}) copy-start(bf16[128,768]{1,0:T(8,128)(2,1)} %get-tuple-element.76.refs_2_) | copy-start | bytes 589828
  22.4 9.5 %copy-start.2 = (bf16[1536,768]{1,0:T(8,128)(2,1)S(1)}, bf16[1536,768]{1,0:T(8,128)(2,1)}, u32[]{:S(2)}) copy-start(bf16[1536,768]{1,0:T(8,128)(2,1)} %refs_1_.2) | copy-start | bytes 7077892
  22.4 6.7 %copy-start.14 = (s32[2]{0:T(128)S(1)}, s32[2]{0:T(128)}, u32[]{:S(2)}) copy-start(s32[2]{0:T(128)} %pad_add_fusion.refs_0_) | copy-start | bytes 28
  22.5 6.7 %copy-start.18 = (f32[1,256]{1,0:T(1,128)S(1)}, f32[1,256]{1,0:T(1,128)}, u32[]{:S(2)}) copy-start(f32[1,256]{1,0:T(1,128)} %get-tuple-element.83.refs_7_) | copy-start | bytes 3076
  22.5 9.5 %copy-start.20 = (f32[768]{0:T(1024)S(1)}, f32[768]{0:T(1024)}, u32[]{:S(2)}) copy-start(f32[768]{0:T(1024)} %param.29) | copy-start | bytes 9220
  22.5 9.5 %copy-start.8 = (bf16[1,128,768]{2,1,0:T(8,128)(2,1)S(1)}, bf16[1,128,768]{2,1,0:T(8,128)(2,1)}, u32[]{:S(2)}) copy-start(bf16[1,128,768]{2,1,0:T(8,128)(2,1)} %param.20) | copy-start | bytes 589828
  22.5 9.5 %copy-start.10 = (bf16[1,128,768]{2,1,0:T(8,128)(2,1)S(1)}, bf16[1,128,768]{2,1,0:T(8,128)(2,1)}, u32[]{:S(2)}) copy-start(bf16[1,128,768]{2,1,0:T(8,128)(2,1)} %param.39) | copy-start | bytes 589828
  22.5 5.0 %collective-permute-start.5 = (bf16[2,4,64,128]{3,2,1,0:T(8,128)(2,1)S(1)}, bf16[2,4,64,128]{3,2,1,0:T(8,128)(2,1)S(1)}, u32[]{:S(2)}, u32[]{:S(2)}) collective-permute-start(bf16[2,4,64,128]{3,2,1,0:T(8,128)(2,1)S(1)} %join_tok.1.refs_0_), channel_id=1, source_target_pairs={{0,4},{2,6},{4,0},{6,2},{8,12},{10,14},{12,8},{14,10},{16,20},{18,... | collective-permute-start | bytes 393224 | tf_op jit(solution)/shard_map/ppermute | solution.py:531
  24.1 12.1 %copy-start.7 = (bf16[768,768]{1,0:T(8,128)(2,1)S(1)}, bf16[768,768]{1,0:T(8,128)(2,1)}, u32[]{:S(2)}) copy-start(bf16[768,768]{1,0:T(8,128)(2,1)} %refs_7_.1) | copy-start | bytes 3538948
  27.5 8.7 %copy-start.1 = (bf16[768,1536]{1,0:T(8,128)(2,1)S(1)}, bf16[768,1536]{1,0:T(8,128)(2,1)}, u32[]{:S(2)}) copy-start(bf16[768,1536]{1,0:T(8,128)(2,1)} %refs_9_.1) | copy-start | bytes 7077892
  27.6 1.6 %collective-permute-start.6 = (bf16[2,2,4,64,128]{4,3,2,1,0:T(8,128)(2,1)S(1)}, bf16[2,2,4,64,128]{4,3,2,1,0:T(8,128)(2,1)S(1)}, u32[]{:S(2)}, u32[]{:S(2)}) collective-permute-start(bf16[2,2,4,64,128]{4,3,2,1,0:T(8,128)(2,1)S(1)} %join_y.1.refs_4_), channel_id=1, source_target_pairs={{0,2},{2,0},{4,6},{6,4},{8,10},{10,8},{12,14},{14,12},{16,18},{18,... | collective-permute-start | bytes 786440 | tf_op jit(solution)/shard_map/ppermute | solution.py:531
  29.2 7.1 %copy-start = (bf16[768,1536]{1,0:T(8,128)(2,1)S(1)}, bf16[768,1536]{1,0:T(8,128)(2,1)}, u32[]{:S(2)}) copy-start(bf16[768,1536]{1,0:T(8,128)(2,1)} %refs_8_.1) | copy-start | bytes 7077892
  31.3 4.9 %collective-permute-start.7 = (bf16[128,384]{1,0:T(8,128)(2,1)S(1)}, bf16[128,384]{1,0:T(8,128)(2,1)S(1)}, u32[]{:S(2)}, u32[]{:S(2)}) collective-permute-start(bf16[128,384]{1,0:T(8,128)(2,1)S(1)} %get-tuple-element.85), channel_id=1, source_target_pairs={{0,1},{1,0},{2,3},{3,2},{4,5},{5,4},{6,7},{7,6},{8,9},{9,8},{10,11... | collective-permute-start | bytes 294920 | tf_op jit(solution)/shard_map/ppermute | solution.py:536
  40.6 4.7 %collective-permute-start.8 = (bf16[384,128]{1,0:T(8,128)(2,1)S(1)}, bf16[384,128]{1,0:T(8,128)(2,1)S(1)}, u32[]{:S(2)}, u32[]{:S(2)}) collective-permute-start(bf16[384,128]{1,0:T(8,128)(2,1)S(1)} %get-tuple-element.90), channel_id=1, source_target_pairs={{0,1},{1,0},{2,3},{3,2},{4,5},{5,4},{6,7},{7,6},{8,9},{9,8},{10,11... | collective-permute-start | bytes 294920 | tf_op jit(solution)/shard_map/ppermute | solution.py:536
  47.3 7.3 %collective-permute-start.11 = (bf16[64,16,128]{2,1,0:T(8,128)(2,1)S(1)}, bf16[64,16,128]{2,1,0:T(8,128)(2,1)S(1)}, u32[]{:S(2)}, u32[]{:S(2)}) collective-permute-start(bf16[64,16,128]{2,1,0:T(8,128)(2,1)S(1)} %get-tuple-element.104), channel_id=1, source_target_pairs={{0,4},{2,6},{4,0},{6,2},{8,12},{10,14},{12,8},{14,10},{16,20},{18,... | collective-permute-start | bytes 786440 | tf_op jit(solution)/shard_map/ppermute | solution.py:531
  48.9 5.7 %collective-permute-start.12 = (bf16[128,768]{1,0:T(8,128)(2,1)S(1)}, bf16[128,768]{1,0:T(8,128)(2,1)S(1)}, u32[]{:S(2)}, u32[]{:S(2)}) collective-permute-start(bf16[128,768]{1,0:T(8,128)(2,1)S(1)} %get-tuple-element.105.refs_5_), channel_id=1, source_target_pairs={{0,1},{1,0},{2,3},{3,2},{4,5},{5,4},{6,7},{7,6},{8,9},{9,8},{10,11... | collective-permute-start | bytes 589832 | tf_op jit(solution)/shard_map/ppermute | solution.py:536
  51.7 6.1 %collective-permute-start.10 = (bf16[216,16,128]{2,1,0:T(8,128)(2,1)S(1)}, bf16[216,16,128]{2,1,0:T(8,128)(2,1)S(1)}, u32[]{:S(2)}, u32[]{:S(2)}) collective-permute-start(bf16[216,16,128]{2,1,0:T(8,128)(2,1)S(1)} %get-tuple-element.100), channel_id=1, source_target_pairs={{0,2},{2,0},{4,6},{6,4},{8,10},{10,8},{12,14},{14,12},{16,18},{18,... | collective-permute-start | bytes 2654216 | tf_op jit(solution)/shard_map/ppermute | solution.py:531
  55.7 4.3 %copy-start.19 = (f32[768]{0:T(1024)S(1)}, f32[768]{0:T(1024)}, u32[]{:S(2)}) copy-start(f32[768]{0:T(1024)} %refs_5_.1) | copy-start | bytes 9220
  55.7 10.5 %copy-start.9 = (bf16[16,128,128]{2,1,0:T(8,128)(2,1)S(1)}, bf16[16,128,128]{2,1,0:T(8,128)(2,1)}, u32[]{:S(2)}) copy-start(bf16[16,128,128]{2,1,0:T(8,128)(2,1)} %get-tuple-element.96.refs_4_) | copy-start | bytes 1572868
  55.7 2.1 %collective-permute-start.13 = (bf16[152,16,128]{2,1,0:T(8,128)(2,1)S(1)}, bf16[152,16,128]{2,1,0:T(8,128)(2,1)S(1)}, u32[]{:S(2)}, u32[]{:S(2)}) collective-permute-start(bf16[152,16,128]{2,1,0:T(8,128)(2,1)S(1)} %get-tuple-element.107), channel_id=1, source_target_pairs={{0,2},{2,0},{4,6},{6,4},{8,10},{10,8},{12,14},{14,12},{16,18},{18,... | collective-permute-start | bytes 1867784 | tf_op jit(solution)/shard_map/ppermute | solution.py:531
  58.7 12.3 %collective-permute-start.14 = (bf16[108,16,128]{2,1,0:T(8,128)(2,1)S(1)}, bf16[108,16,128]{2,1,0:T(8,128)(2,1)S(1)}, u32[]{:S(2)}, u32[]{:S(2)}) collective-permute-start(bf16[108,16,128]{2,1,0:T(8,128)(2,1)S(1)} %get-tuple-element.109), channel_id=1, source_target_pairs={{0,4},{2,6},{4,0},{6,2},{8,12},{10,14},{12,8},{14,10},{16,20},{18,... | collective-permute-start | bytes 1327112 | tf_op jit(solution)/shard_map/ppermute | solution.py:531
  59.5 9.1 %collective-permute-start.15 = (bf16[76,16,128]{2,1,0:T(8,128)(2,1)S(1)}, bf16[76,16,128]{2,1,0:T(8,128)(2,1)S(1)}, u32[]{:S(2)}, u32[]{:S(2)}) collective-permute-start(bf16[76,16,128]{2,1,0:T(8,128)(2,1)S(1)} %get-tuple-element.111), channel_id=1, source_target_pairs={{0,8},{2,10},{4,12},{6,14},{8,0},{10,2},{12,4},{14,6},{16,24},{18,... | collective-permute-start | bytes 933896 | tf_op jit(solution)/shard_map/ppermute | solution.py:531
  59.5 6.7 %collective-permute-start.9 = (bf16[768,128]{1,0:T(8,128)(2,1)S(1)}, bf16[768,128]{1,0:T(8,128)(2,1)S(1)}, u32[]{:S(2)}, u32[]{:S(2)}) collective-permute-start(bf16[768,128]{1,0:T(8,128)(2,1)S(1)} %get-tuple-element.97), channel_id=1, source_target_pairs={{0,1},{1,0},{2,3},{3,2},{4,5},{5,4},{6,7},{7,6},{8,9},{9,8},{10,11... | collective-permute-start | bytes 589832 | tf_op jit(solution)/shard_map/ppermute | solution.py:536
  71.0 25.9 %copy-start.3 = (bf16[128,16,128]{2,1,0:T(8,128)(2,1)S(1)}, bf16[128,16,128]{2,1,0:T(8,128)(2,1)}, u32[]{:S(2)}) copy-start(bf16[128,16,128]{2,1,0:T(8,128)(2,1)} %param.22) | copy-start | bytes 1572868
  71.0 25.9 %copy-start.16 = (bf16[128,8]{0,1:T(8,128)(2,1)S(1)}, bf16[128,8]{0,1:T(8,128)(2,1)}, u32[]{:S(2)}) copy-start(bf16[128,8]{0,1:T(8,128)(2,1)} %param.34) | copy-start | bytes 6148
  71.0 25.9 %copy-start.17 = (f32[128]{0:T(128)S(1)}, f32[128]{0:T(128)}, u32[]{:S(2)}) copy-start(f32[128]{0:T(128)} %param.28) | copy-start | bytes 1540
  71.7 10.0 %collective-permute-start.16 = (bf16[54,16,128]{2,1,0:T(8,128)(2,1)S(1)}, bf16[54,16,128]{2,1,0:T(8,128)(2,1)S(1)}, u32[]{:S(2)}, u32[]{:S(2)}) collective-permute-start(bf16[54,16,128]{2,1,0:T(8,128)(2,1)S(1)} %get-tuple-element.114), channel_id=1, source_target_pairs={{0,8},{2,10},{4,12},{6,14},{8,0},{10,2},{12,4},{14,6},{16,24},{18,... | collective-permute-start | bytes 663560 | tf_op jit(solution)/shard_map/ppermute | solution.py:531
  71.8 9.7 %collective-permute-start.17 = (bf16[38,16,128]{2,1,0:T(8,128)(2,1)S(1)}, bf16[38,16,128]{2,1,0:T(8,128)(2,1)S(1)}, u32[]{:S(2)}, u32[]{:S(2)}) collective-permute-start(bf16[38,16,128]{2,1,0:T(8,128)(2,1)S(1)} %get-tuple-element.116), channel_id=1, source_target_pairs={{0,16},{2,18},{4,20},{6,22},{8,24},{10,26},{12,28},{14,30},{16,0},... | collective-permute-start | bytes 466952 | tf_op jit(solution)/shard_map/ppermute | solution.py:531
  82.4 5.7 %collective-permute-start.18 = (bf16[27,16,128]{2,1,0:T(8,128)(2,1)S(1)}, bf16[27,16,128]{2,1,0:T(8,128)(2,1)S(1)}, u32[]{:S(2)}, u32[]{:S(2)}) collective-permute-start(bf16[27,16,128]{2,1,0:T(8,128)(2,1)S(1)} %get-tuple-element.118), channel_id=1, source_target_pairs={{0,1},{1,0},{2,3},{3,2},{4,5},{5,4},{6,7},{7,6},{8,9},{9,8},{10,11... | collective-permute-start | bytes 331784 | tf_op jit(solution)/shard_map/ppermute | solution.py:536
  83.0 5.1 %collective-permute-start.19 = (bf16[15,16,128]{2,1,0:T(8,128)(2,1)S(1)}, bf16[15,16,128]{2,1,0:T(8,128)(2,1)S(1)}, u32[]{:S(2)}, u32[]{:S(2)}) collective-permute-start(bf16[15,16,128]{2,1,0:T(8,128)(2,1)S(1)} %get-tuple-element.120), channel_id=1, source_target_pairs={{0,4},{2,6},{4,0},{6,2},{8,12},{10,14},{12,8},{14,10},{16,20},{18,... | collective-permute-start | bytes 184328 | tf_op jit(solution)/shard_map/ppermute | solution.py:531
  84.3 3.8 %collective-permute-start.20 = (bf16[64,128]{1,0:T(8,128)(2,1)S(1)}, bf16[64,128]{1,0:T(8,128)(2,1)S(1)}, u32[]{:S(2)}, u32[]{:S(2)}) collective-permute-start(bf16[64,128]{1,0:T(8,128)(2,1)S(1)} %get-tuple-element.121), channel_id=1, source_target_pairs={{0,1},{1,0},{2,3},{3,2},{4,5},{5,4},{6,7},{7,6},{8,9},{9,8},{10,11... | collective-permute-start | bytes 49160 | tf_op jit(solution)/shard_map/ppermute | solution.py:536
  89.4 13.6 %all-to-all-start = ((bf16[32,8,128]{2,1,0:T(8,128)(2,1)}), bf16[32,8,128]{2,1,0:T(8,128)(2,1)S(1)}, u32[]{:S(2)}, u32[]{:S(2)}) async-start(bf16[32,8,128]{2,1,0:T(8,128)(2,1)} %pair_weight.1), calls=%async_computation | async-start | bytes 131072 | tf_op jit(solution)/shard_map/all_to_all | solution.py:540
  93.7 9.3 %collective-permute-start.21 = (bf16[27,16,128]{2,1,0:T(8,128)(2,1)S(1)}, bf16[27,16,128]{2,1,0:T(8,128)(2,1)S(1)}, u32[]{:S(2)}, u32[]{:S(2)}) collective-permute-start(bf16[27,16,128]{2,1,0:T(8,128)(2,1)S(1)} %get-tuple-element.123), channel_id=1, source_target_pairs={{0,16},{2,18},{4,20},{6,22},{8,24},{10,26},{12,28},{14,30},{16,0},... | collective-permute-start | bytes 331784 | tf_op jit(solution)/shard_map/ppermute | solution.py:531
  96.3 3.7 %collective-permute-start.22 = (bf16[3,16,128]{2,1,0:T(8,128)(2,1)S(1)}, bf16[3,16,128]{2,1,0:T(8,128)(2,1)S(1)}, u32[]{:S(2)}, u32[]{:S(2)}) collective-permute-start(bf16[3,16,128]{2,1,0:T(8,128)(2,1)S(1)} %get-tuple-element.125), channel_id=1, source_target_pairs={{0,1},{1,0},{2,3},{3,2},{4,5},{5,4},{6,7},{7,6},{8,9},{9,8},{10,11... | collective-permute-start | bytes 36872 | tf_op jit(solution)/shard_map/ppermute | solution.py:536
